TPU v7x, 32 devices: a whole 2x2x4 slice. The times are simulated.
32 devices in a mesh: lat: 4 (over y, x), lon: 8 (over z, core).
Axes of the slice: x: 2, y: 2, z: 4, core: 2. Of those that a mesh axis runs over, the one named last changes fastest.
Arguments:
- fields: bfloat16 [2, 24, 192, 512], P(None, 'lat', 'lon'), may hold values from -6 to 6
- cotangent: bfloat16 [2, 24, 192, 512], P(None, 'lat', 'lon'), may hold values from -6 to 6
- qkv_weight: bfloat16 [512, 1536], replicated, may hold values from -1 to 1, as said below
- proj_weight: bfloat16 [512, 512], replicated, may hold values from -0.25 to 0.25
Outputs:
- field_out: bfloat16 [2, 24, 192, 512], P(None, 'lat', 'lon')
- d_fields: bfloat16 [2, 24, 192, 512], P(None, 'lat', 'lon')
- qkv_grad: float32 [512, 1536], P('lon')
- proj_grad: float32 [512, 512], P(None, 'lon')
Inputs may be any that keep to these rules, and one draw needn't show every extreme that they name: `qkv_weight`: projection weights for inputs of 512 features; columns in the order queries, keys, values, head by head.
All inputs are finite; a program needn't handle non-finite values.
Results may differ from a plain program's by a relative error of at most 0.015.
Values may be sent and summed in bfloat16 or wider, within the bound.
No kernel may reach another device: no remote copies, remote signals or barrier semaphores. Data moves between devices by JAX's collectives and lax.ppermute only.
A program may use at most 64 MiB of HBM per device.

v0:
```python
import jax
import jax.numpy as jnp
from jax import lax
from jax.sharding import PartitionSpec as P

HEADS = 8
WIN_LAT = 6
WIN_LON = 12


epsilon = 1e-05


def passed_along(block, axis, distance):
    devices = range(lax.axis_size(axis))
    route = [((i - distance) % len(devices), i) for i in devices]
    return lax.ppermute(block, axis, route)


def to_windows(tokens):
    levels, row_count, col_count, feature = tokens.shape
    shaped = tokens.reshape(
        levels, row_count // WIN_LAT, WIN_LAT, col_count // WIN_LON, WIN_LON, feature
    )
    shaped = shaped.transpose(1, 3, 0, 2, 4, 5)
    return shaped.reshape(-1, levels * WIN_LAT * WIN_LON, feature)


def from_windows(windows, levels, row_count, col_count):
    feature = windows.shape[-1]
    shaped = windows.reshape(
        row_count // WIN_LAT, col_count // WIN_LON, levels, WIN_LAT, WIN_LON, feature
    )
    shaped = shaped.transpose(2, 0, 3, 1, 4, 5)
    return shaped.reshape(levels, row_count, col_count, feature)


def roll_in(stacked):
    half_lat = WIN_LAT // 2
    half_lon = WIN_LON // 2
    from_below = passed_along(stacked[:, :, :half_lat], "lat", -1)
    shifted = jnp.concatenate([stacked[:, :, half_lat:], from_below], axis=2)
    beside = passed_along(shifted[:, :, :, :half_lon], "lon", -1)
    return jnp.concatenate([shifted[:, :, :, half_lon:], beside], axis=3)


def roll_back_both(stacked):
    half_lat = WIN_LAT // 2
    half_lon = WIN_LON // 2
    from_above = passed_along(stacked[:, :, -half_lat:], "lat", 1)
    shifted = jnp.concatenate([from_above, stacked[:, :, :-half_lat]], axis=2)
    beside = passed_along(shifted[:, :, :, -half_lon:], "lon", 1)
    return jnp.concatenate([beside, shifted[:, :, :, :-half_lon]], axis=3)


def per_device(fields, cotangent, qkv_weight, proj_weight):
    levels, row_count, col_count, feature = fields.shape
    head_count = HEADS
    head_size = feature // head_count
    factor = head_size ** (-0.5)
    win_size = levels * WIN_LAT * WIN_LON
    stacked = roll_in(jnp.stack([fields, cotangent]))
    rolled = stacked[0]
    rolled_grad = stacked[1]
    total_lat = row_count * lax.axis_size("lat")
    row_ids = lax.axis_index("lat") * row_count + jnp.arange(row_count, dtype=jnp.int32)
    region = (row_ids >= total_lat - WIN_LAT // 2).astype(jnp.int32)
    region = jnp.broadcast_to(region[None, :, None, None], (levels, row_count, col_count, 1))
    region_w = to_windows(region)[..., 0]
    allowed = region_w[:, None, :, None] == region_w[:, None, None, :]
    inputs_f = rolled.astype(jnp.float32)
    token_mean = jnp.mean(inputs_f, -1, keepdims=True)
    centred = inputs_f - token_mean
    variance = jnp.mean(centred * centred, -1, keepdims=True)
    inv_std = lax.rsqrt(variance + epsilon)
    normed = centred * inv_std
    windows = to_windows(normed.astype(jnp.bfloat16))
    win_count = windows.shape[0]
    projected = jnp.einsum(
        "wtd,de->wte", windows, qkv_weight, preferred_element_type=jnp.float32
    ).astype(jnp.bfloat16)
    split_proj = projected.reshape(win_count, win_size, 3, head_count, head_size)
    queries = split_proj[:, :, 0]
    keys_all = split_proj[:, :, 1]
    values = split_proj[:, :, 2]
    scores = (
        jnp.einsum("wqhd,wkhd->whqk", queries, keys_all, preferred_element_type=jnp.float32)
        * factor
    )
    scores = jnp.where(allowed, scores, -1e30)
    row_peak = jnp.max(scores, -1, keepdims=True)
    exponent = jnp.exp(scores - row_peak)
    attn_probs = exponent / jnp.sum(exponent, -1, keepdims=True)
    probs_b = attn_probs.astype(jnp.bfloat16)
    mixed = jnp.einsum("whqk,wkhd->wqhd", probs_b, values, preferred_element_type=jnp.float32)
    mixed = mixed.astype(jnp.bfloat16).reshape(win_count, win_size, feature)
    attended = jnp.einsum("wtc,cd->wtd", mixed, proj_weight, preferred_element_type=jnp.float32)
    attended = from_windows(attended, levels, row_count, col_count)
    output = (inputs_f + attended).astype(jnp.bfloat16)
    grads_w = to_windows(rolled_grad)
    d_mixed = jnp.einsum(
        "wtd,cd->wtc", grads_w, proj_weight, preferred_element_type=jnp.float32
    ).astype(jnp.bfloat16)
    proj_term = jnp.einsum("wtd,wtc->dc", grads_w, mixed, preferred_element_type=jnp.float32)
    d_heads = d_mixed.reshape(win_count, win_size, head_count, head_size)
    d_probs = jnp.einsum("wqhd,wkhd->whqk", d_heads, values, preferred_element_type=jnp.float32)
    d_values = jnp.einsum(
        "whqk,wqhd->wkhd", probs_b, d_heads, preferred_element_type=jnp.float32
    ).astype(jnp.bfloat16)
    d_scores = (
        attn_probs * (d_probs - jnp.sum(d_probs * attn_probs, -1, keepdims=True)) * factor
    ).astype(jnp.bfloat16)
    d_queries = jnp.einsum(
        "whqk,wkhd->wqhd", d_scores, keys_all, preferred_element_type=jnp.float32
    ).astype(jnp.bfloat16)
    d_keys = jnp.einsum(
        "whqk,wqhd->wkhd", d_scores, queries, preferred_element_type=jnp.float32
    ).astype(jnp.bfloat16)
    d_projected = jnp.concatenate(
        [
            d_queries.reshape(win_count, win_size, feature),
            d_keys.reshape(win_count, win_size, feature),
            d_values.reshape(win_count, win_size, feature),
        ],
        -1,
    )
    qkv_term = jnp.einsum("wtd,wte->de", windows, d_projected, preferred_element_type=jnp.float32)
    d_normed = jnp.einsum(
        "wte,de->wtd", d_projected, qkv_weight, preferred_element_type=jnp.float32
    )
    d_normed = from_windows(d_normed, levels, row_count, col_count)
    d_inputs = rolled_grad.astype(jnp.float32) + inv_std * (
        d_normed
        - jnp.mean(d_normed, -1, keepdims=True)
        - normed * jnp.mean(d_normed * normed, -1, keepdims=True)
    )
    d_inputs = d_inputs.astype(jnp.bfloat16)
    qkv_share, proj_share = (
        lax.psum_scatter(
            qkv_term.astype(jnp.bfloat16), "lon", scatter_dimension=0, tiled=True
        ).astype(jnp.float32),
        lax.psum_scatter(
            proj_term.astype(jnp.bfloat16), "lon", scatter_dimension=0, tiled=True
        ).astype(jnp.float32),
    )
    qkv_share, proj_share = (
        lax.psum(qkv_share.astype(jnp.bfloat16), "lat").astype(jnp.float32),
        lax.psum(proj_share.astype(jnp.bfloat16), "lat").astype(jnp.float32),
    )
    moved = roll_back_both(jnp.stack([output, d_inputs]))
    field_out = moved[0]
    d_fields = moved[1]
    return (field_out, d_fields, qkv_share, jnp.transpose(proj_share))


def solution(mesh):
    placed = (P(None, "lat", "lon", None), P(None, "lat", "lon", None), P(), P())
    return jax.shard_map(
        per_device,
        mesh=mesh,
        in_specs=placed,
        out_specs=(
            P(None, "lat", "lon", None),
            P(None, "lat", "lon", None),
            P("lon", None),
            P(None, "lon"),
        ),
        check_vma=False,
    )
```

profile of v0, /device:TPU:0, one launch (start us, length us, event | category | flops | bytes accessed | tf_op | source)
XLA Modules:
  0.0 174.2 jit_solution(16806955941585279176)
XLA Ops:
  7.2 1.8 %copy_bitcast_fusion = (bf16[1,2,6,24,512]{4,1,3,2,0:T(2,128)(2,1)S(1)}, bf16[1,2,6,24,512]{4,1,3,2,0:T(2,128)(2,1)S(1)}) fusion(bf16[2,6,24,512]{3,2,1,0:T(8,128)(2,1)} %param.5, bf16[2,6,24,512]{3,2,1,0:T(8,128)(2,1)} %param.4), kind=kLoop, calls=%fused_computation.74 | loop fusion | bytes 1179648 | tf_op jit(solution)/shard_map/stack | solution.py:62
  9.0 0.9 fusion.48
  9.9 3.9 %collective-permute-start = (bf16[2,2,3,24,512]{4,1,3,2,0:T(2,128)(2,1)S(1)}, bf16[2,2,3,24,512]{4,1,3,2,0:T(2,128)(2,1)S(1)}, u32[]{:S(2)}, u32[]{:S(2)}) collective-permute-start(bf16[2,2,3,24,512]{4,1,3,2,0:T(2,128)(2,1)S(1)} %get-tuple-element.30), channel_id=1, source_target_pairs={{8,0},{16,8},{24,16},{0,24},{9,1},{17,9},{25,17},{1,25},{10,2},{18... | collective-permute-start | bytes 884744 | tf_op jit(solution)/shard_map/ppermute | solution.py:17
  14.0 6.1 %collective-permute-done = bf16[2,2,3,24,512]{4,1,3,2,0:T(2,128)(2,1)S(1)} collective-permute-done((bf16[2,2,3,24,512]{4,1,3,2,0:T(2,128)(2,1)S(1)}, bf16[2,2,3,24,512]{4,1,3,2,0:T(2,128)(2,1)S(1)}, u32[]{:S(2)}, u32[]{:S(2)}) %collective-permute-start) | collective-permute-done | bytes 294944 | tf_op jit(solution)/shard_map/ppermute | solution.py:17
  20.3 2.3 %collective-permute-start.1 = (bf16[2,2,6,6,512]{4,1,3,2,0:T(2,128)(2,1)S(1)}, bf16[2,2,6,6,512]{4,1,3,2,0:T(2,128)(2,1)S(1)}, u32[]{:S(2)}, u32[]{:S(2)}) collective-permute-start(bf16[2,2,6,6,512]{4,1,3,2,0:T(2,128)(2,1)S(1)} %pad_maximum_fusion.8), channel_id=1, source_target_pairs={{1,0},{2,1},{3,2},{4,3},{5,4},{6,5},{7,6},{0,7},{9,8},{10,9},{11,1... | collective-permute-start | bytes 442376 | tf_op jit(solution)/shard_map/ppermute | solution.py:17
  22.5 0.7 broadcast_compare_fusion
  23.3 0.6 fusion.44
  23.8 1.4 collective-permute-done.1
  25.6 0.7 copy-done.3
  26.6 0.7 copy-done.11
  27.6 1.0 copy.148
  29.1 0.6 fusion.31
  29.7 1.3 fusion.49
  31.3 0.7 copy-done.9
  32.0 1.6 convolution_convert_fusion
  33.6 2.6 %reshape.155 = bf16[2,144,3,8,64]{4,3,2,1,0:T(8,128)(2,1)S(1)} reshape(bf16[2,144,1536]{2,1,0:T(8,128)(2,1)} %convolution_convert_fusion) | data formatting | bytes 1769472 | tf_op jit(solution)/shard_map/reshape | solution.py:82
  36.1 1.3 fusion.75
  37.5 1.4 copy.151
  38.9 1.6 copy.150
  40.5 3.5 %fusion.76 = (f32[2,8,144]{2,1,0:T(8,128)S(1)}, f32[2,8,144,144]{2,3,1,0:T(8,128)}) fusion(pred[2,144,144]{1,2,0:T(8,128)(4,1)} %broadcast_compare_fusion, bf16[2,144,1,8,64]{1,4,3,0,2:T(8,128)(2,1)S(1)} %copy.151, bf16[2,144,1,8,64]{1,4,3,0,2:T(8,128)(2,1)S(1)} %copy.150), kind=kOutput, calls=%fused_computation.97 | convolution fusion | flops 43794576 | bytes 1967616 | tf_op jit(solution)/shard_map/sub | solution.py:92
  44.0 2.2 %convolution_convert_fusion.1 = bf16[2,8,64,144]{3,2,1,0:T(8,128)(2,1)S(1)} fusion(bf16[2,144,8,64]{1,3,2,0:T(8,128)(2,1)S(1)} %bitcast.120, f32[2,8,144,144]{2,3,1,0:T(8,128)} %get-tuple-element.34, f32[2,8,144]{2,1,0:T(8,128)S(1)} %get-tuple-element.33), kind=kOutput, calls=%fused_computation.21 | convolution fusion | flops 43278336 | bytes 1926144 | tf_op jit(solution)/shard_map/whqk,wqhd->wkhd/dot_general | solution.py:107
  46.3 0.9 copy.122
  47.6 2.0 %convolution_convert_fusion.2 = bf16[2,8,64,144]{3,2,1,0:T(8,128)(2,1)S(1)} fusion(bf16[2,144,1,8,64]{1,4,3,0,2:T(8,128)(2,1)S(1)} %copy.149, f32[2,8,144,144]{2,3,1,0:T(8,128)} %get-tuple-element.34, f32[2,8,144]{2,1,0:T(8,128)S(1)} %get-tuple-element.33), kind=kOutput, calls=%fused_computation.22 | convolution fusion | flops 43278336 | bytes 1926144 | tf_op jit(solution)/shard_map/whqk,wkhd->wqhd/dot_general | solution.py:95
  49.6 0.8 copy-done.17
  50.4 1.3 fusion.22
  52.0 1.9 %fusion.41 = f32[2,8,144,144]{2,3,1,0:T(8,128)} fusion(bf16[2,144,8,64]{1,3,2,0:T(8,128)(2,1)S(1)} %bitcast.121, bf16[2,144,1,8,64]{1,4,3,0,2:T(8,128)(2,1)S(1)} %copy.149), kind=kOutput, calls=%fused_computation.61 | convolution fusion | flops 42467328 | bytes 1916928 | tf_op jit(solution)/shard_map/wqhd,wkhd->whqk/dot_general | solution.py:106
  54.0 4.8 %fusion.19 = bf16[2,8,64,144]{3,2,1,0:T(8,128)(2,1)S(1)} fusion(f32[2,8,144,144]{2,3,1,0:T(8,128)} %fusion.41, bf16[2,144,1,8,64]{1,4,3,0,2:T(8,128)(2,1)} %copy-done.20, f32[2,8,144,144]{2,3,1,0:T(8,128)} %get-tuple-element.34, f32[2,8,144]{2,1,0:T(8,128)S(1)} %get-tuple-element.33), kind=kOutput, calls=%fused_computation.18 | convolution fusion | flops 44939664 | bytes 3253248 | tf_op jit(solution)/shard_map/whqk,wqhd->wkhd/dot_general | solution.py:116
  58.8 0.9 copy.121
  59.7 4.7 %fusion.16 = bf16[2,8,64,144]{3,2,1,0:T(8,128)(2,1)S(1)} fusion(f32[2,8,144,144]{2,3,1,0:T(8,128)} %fusion.41, bf16[2,144,1,8,64]{1,4,3,0,2:T(8,128)(2,1)S(1)} %copy-done.19, f32[2,8,144,144]{2,3,1,0:T(8,128)} %get-tuple-element.34, f32[2,8,144]{2,1,0:T(8,128)S(1)} %get-tuple-element.33), kind=kOutput, calls=%fused_computation.17 | convolution fusion | flops 44939664 | bytes 3253248 | tf_op jit(solution)/shard_map/whqk,wkhd->wqhd/dot_general | solution.py:113
  64.6 3.3 %fusion.2 = bf16[512,1536]{1,0:T(8,128)(2,1)} fusion(bf16[2,144,512]{2,1,0:T(8,128)(2,1)S(1)} %copy-done.21, bf16[2,144,512]{2,1,0:T(8,128)(2,1)} %copy.121, bf16[2,144,512]{2,1,0:T(8,128)(2,1)S(1)} %copy.120, bf16[2,144,512]{2,0,1:T(2,128)(2,1)S(1)} %bitcast.123), kind=kOutput, calls=%fused_computation.3 | convolution fusion | flops 456425472 | bytes 2752512 | tf_op jit(solution)/shard_map/wtd,wte->de/dot_general | solution.py:127
  68.0 1.8 %fusion.13 = f32[2,144,512]{2,1,0:T(8,128)S(1)} fusion(bf16[512,1536]{1,0:T(8,128)(2,1)S(1)} %copy-done, bf16[2,144,512]{2,1,0:T(8,128)(2,1)S(1)} %copy-done.21, bf16[2,144,512]{2,1,0:T(8,128)(2,1)} %copy.121, bf16[2,144,512]{2,1,0:T(8,128)(2,1)} %copy-done.22), kind=kOutput, calls=%fused_computation.13 | convolution fusion | flops 455639040 | bytes 3047424 | tf_op jit(solution)/shard_map/wte,de->wtd/dot_general | solution.py:128
  70.7 1.2 bitcast_reduce_fusion
  71.9 0.6 reshape.177
  72.5 0.6 reshape.178
  73.2 1.5 copy.142
  74.7 1.1 reshape.174
  75.8 1.6 convolution_bitcast_fusion.2
  77.9 1.1 add_convert_fusion
  79.4 2.4 %collective-permute-start.2 = (bf16[2,2,3,24,512]{4,1,3,2,0:T(2,128)(2,1)S(1)}, bf16[2,2,3,24,512]{4,1,3,2,0:T(2,128)(2,1)S(1)}, u32[]{:S(2)}, u32[]{:S(2)}) collective-permute-start(bf16[2,2,3,24,512]{4,1,3,2,0:T(2,128)(2,1)S(1)} %fusion.46), channel_id=1, source_target_pairs={{24,0},{0,8},{8,16},{16,24},{25,1},{1,9},{9,17},{17,25},{26,2},{2,... | collective-permute-start | bytes 884744 | tf_op jit(solution)/shard_map/ppermute | solution.py:17
  81.9 7.8 %collective-permute-done.2 = bf16[2,2,3,24,512]{4,1,3,2,0:T(2,128)(2,1)S(1)} collective-permute-done((bf16[2,2,3,24,512]{4,1,3,2,0:T(2,128)(2,1)S(1)}, bf16[2,2,3,24,512]{4,1,3,2,0:T(2,128)(2,1)S(1)}, u32[]{:S(2)}, u32[]{:S(2)}) %collective-permute-start.2) | collective-permute-done | bytes 294944 | tf_op jit(solution)/shard_map/ppermute | solution.py:17
  90.0 30.9 %reduce-scatter.3.cloned.1.call-done = bf16[64,1536]{1,0:T(8,128)(2,1)} async-done(((bf16[512,1536]{1,0:T(8,128)(2,1)}), bf16[64,1536]{1,0:T(8,128)(2,1)}) %reduce-scatter.3.cloned.1.call-update) | async-done | bytes 196624 | tf_op jit(solution)/shard_map/reduce_scatter | solution.py:139
  120.9 0.9 fusion.28
  121.8 0.5 slice_bitcast_fusion
  122.3 0.7 copy.134
  123.0 0.7 copy.135
  123.8 40.7 %all-reduce.3.cloned.1.call-done = (bf16[64,1536]{1,0:T(8,128)(2,1)}, bf16[512,64]{0,1:T(8,128)(2,1)}) async-done(((bf16[64,1536]{1,0:T(8,128)(2,1)}, bf16[512,64]{0,1:T(8,128)(2,1)}), (bf16[64,1536]{1,0:T(8,128)(2,1)}, bf16[512,64]{0,1:T(8,128)(2,1)})) %all-reduce.3.cloned.1.call-update) | async-done | bytes 262160 | tf_op jit(solution)/shard_map/psum | solution.py:147
  164.4 1.7 convert_element_type.125
  166.1 1.5 transpose.57
  (77 shorter events, 5.2 us)
Async XLA Ops:
  7.2 24.8 %copy-start = (bf16[512,1536]{1,0:T(8,128)(2,1)S(1)}, bf16[512,1536]{1,0:T(8,128)(2,1)}, u32[]{:S(2)}) copy-start(bf16[512,1536]{1,0:T(8,128)(2,1)} %param.6) | copy-start | bytes 4718596
  7.2 82.8 %reduce-scatter.5.cloned.1.call-start = ((), (), s32[]{:S(2)}) async-start(), calls=%async_computation.3 | async-start | bytes 589824 | tf_op jit(solution)/shard_map/reduce_scatter | solution.py:142
  9.0 18.3 %copy-start.7 = (bf16[512,512]{1,0:T(8,128)(2,1)S(1)}, bf16[512,512]{1,0:T(8,128)(2,1)}, u32[]{:S(2)}) copy-start(bf16[512,512]{1,0:T(8,128)(2,1)} %param.7) | copy-start | bytes 1572868
  9.9 10.2 %collective-permute-start = (bf16[2,2,3,24,512]{4,1,3,2,0:T(2,128)(2,1)S(1)}, bf16[2,2,3,24,512]{4,1,3,2,0:T(2,128)(2,1)S(1)}, u32[]{:S(2)}, u32[]{:S(2)}) collective-permute-start(bf16[2,2,3,24,512]{4,1,3,2,0:T(2,128)(2,1)S(1)} %get-tuple-element.30), channel_id=1, source_target_pairs={{8,0},{16,8},{24,16},{0,24},{9,1},{17,9},{25,17},{1,25},{10,2},{18... | collective-permute-start | bytes 884744 | tf_op jit(solution)/shard_map/ppermute | solution.py:17
  20.3 4.9 %collective-permute-start.1 = (bf16[2,2,6,6,512]{4,1,3,2,0:T(2,128)(2,1)S(1)}, bf16[2,2,6,6,512]{4,1,3,2,0:T(2,128)(2,1)S(1)}, u32[]{:S(2)}, u32[]{:S(2)}) collective-permute-start(bf16[2,2,6,6,512]{4,1,3,2,0:T(2,128)(2,1)S(1)} %pad_maximum_fusion.8), channel_id=1, source_target_pairs={{1,0},{2,1},{3,2},{4,3},{5,4},{6,5},{7,6},{0,7},{9,8},{10,9},{11,1... | collective-permute-start | bytes 442376 | tf_op jit(solution)/shard_map/ppermute | solution.py:17
  25.6 0.7 copy-start.3
  26.5 0.7 copy-start.11
  29.1 2.2 %copy-start.1 = (bf16[1,2,6,24,512]{4,1,3,2,0:T(2,128)(2,1)}, bf16[1,2,6,24,512]{4,1,3,2,0:T(2,128)(2,1)S(1)}, u32[]{:S(2)}) copy-start(bf16[1,2,6,24,512]{4,1,3,2,0:T(2,128)(2,1)S(1)} %get-tuple-element.23) | copy-start | bytes 884740
  29.7 1.6 copy-start.15
  29.7 1.6 copy-start.13
  31.3 0.7 copy-start.9
  38.9 5.1 %copy-start.18 = (bf16[2,144,1,8,64]{1,4,3,0,2:T(8,128)(2,1)}, bf16[2,144,1,8,64]{1,4,3,0,2:T(8,128)(2,1)S(1)}, u32[]{:S(2)}) copy-start(bf16[2,144,1,8,64]{1,4,3,0,2:T(8,128)(2,1)S(1)} %copy.151) | copy-start | bytes 884740
  40.5 3.5 %copy-start.20 = (bf16[2,144,1,8,64]{1,4,3,0,2:T(8,128)(2,1)}, bf16[2,144,1,8,64]{1,4,3,0,2:T(8,128)(2,1)S(1)}, u32[]{:S(2)}) copy-start(bf16[2,144,1,8,64]{1,4,3,0,2:T(8,128)(2,1)S(1)} %copy.150) | copy-start | bytes 884740
  40.5 3.5 %copy-start.8 = (bf16[2,144,512]{1,2,0:T(8,128)(2,1)S(1)}, bf16[2,144,512]{1,2,0:T(8,128)(2,1)}, u32[]{:S(2)}) copy-start(bf16[2,144,512]{1,2,0:T(8,128)(2,1)} %copy.148) | copy-start | bytes 884740
  44.0 3.2 %copy-start.5 = (bf16[2,144,1,8,64]{4,3,2,1,0:T(8,128)(2,1)S(1)}, bf16[2,144,1,8,64]{4,3,2,1,0:T(8,128)(2,1)}, u32[]{:S(2)}) copy-start(bf16[2,144,1,8,64]{4,3,2,1,0:T(8,128)(2,1)} %get-tuple-element.25) | copy-start | bytes 884740
  47.6 2.8 %copy-start.12 = (bf16[1,2,2,6,12,512]{5,1,4,3,2,0:T(2,128)(2,1)S(1)}, bf16[1,2,2,6,12,512]{5,1,4,3,2,0:T(2,128)(2,1)}, u32[]{:S(2)}) copy-start(bf16[1,2,2,6,12,512]{5,1,4,3,2,0:T(2,128)(2,1)} %copy-done.11) | copy-start | bytes 884740
  49.6 0.8 copy-start.17
  51.8 69.1 %reduce-scatter.3.cloned.1.call-start = ((), (), s32[]{:S(2)}) async-start(), calls=%async_computation.2 | async-start | bytes 1769472 | tf_op jit(solution)/shard_map/reduce_scatter | solution.py:139
  53.9 5.8 %copy-start.19 = (bf16[2,144,1,8,64]{1,4,3,0,2:T(8,128)(2,1)S(1)}, bf16[2,144,1,8,64]{1,4,3,0,2:T(8,128)(2,1)}, u32[]{:S(2)}) copy-start(bf16[2,144,1,8,64]{1,4,3,0,2:T(8,128)(2,1)} %copy-done.18) | copy-start | bytes 884740
  59.7 4.9 %copy-start.10 = (bf16[1,2,2,6,12,512]{5,1,4,3,2,0:T(2,128)(2,1)S(1)}, bf16[1,2,2,6,12,512]{5,1,4,3,2,0:T(2,128)(2,1)}, u32[]{:S(2)}) copy-start(bf16[1,2,2,6,12,512]{5,1,4,3,2,0:T(2,128)(2,1)} %copy-done.9) | copy-start | bytes 884740
  59.7 4.9 %copy-start.21 = (bf16[2,144,512]{2,1,0:T(8,128)(2,1)S(1)}, bf16[2,144,512]{2,1,0:T(8,128)(2,1)}, u32[]{:S(2)}) copy-start(bf16[2,144,512]{2,1,0:T(8,128)(2,1)} %copy.122) | copy-start | bytes 884740
  64.6 3.3 %copy-start.22 = (bf16[2,144,512]{2,1,0:T(8,128)(2,1)}, bf16[2,144,512]{2,1,0:T(8,128)(2,1)S(1)}, u32[]{:S(2)}) copy-start(bf16[2,144,512]{2,1,0:T(8,128)(2,1)S(1)} %copy.120) | copy-start | bytes 884740
  67.9 2.8 %copy-start.6 = (f32[2,1,6,2,12,512]{5,0,4,3,2,1:T(2,128)S(1)}, f32[2,1,6,2,12,512]{5,0,4,3,2,1:T(2,128)}, u32[]{:S(2)}) copy-start(f32[2,1,6,2,12,512]{5,0,4,3,2,1:T(2,128)} %get-tuple-element.21) | copy-start | bytes 1769476
  67.9 2.8 %copy-start.14 = (f32[2,6,2,12]{0,3,2,1:T(8,128)S(1)}, f32[2,6,2,12]{0,3,2,1:T(8,128)}, u32[]{:S(2)}) copy-start(f32[2,6,2,12]{0,3,2,1:T(8,128)} %copy-done.13) | copy-start | bytes 3460
  67.9 96.5 %all-reduce.3.cloned.1.call-start = ((), (), s32[]{:S(2)}) async-start(), calls=%async_computation.4 | async-start | bytes 524288 | tf_op jit(solution)/shard_map/psum | solution.py:147
  73.2 4.6 %copy-start.2 = (bf16[1,2,6,24,512]{4,1,3,2,0:T(2,128)(2,1)S(1)}, bf16[1,2,6,24,512]{4,1,3,2,0:T(2,128)(2,1)}, u32[]{:S(2)}) copy-start(bf16[1,2,6,24,512]{4,1,3,2,0:T(2,128)(2,1)} %copy-done.1) | copy-start | bytes 884740
  73.2 4.7 %copy-start.4 = (bf16[1,2,6,24,512]{4,1,3,2,0:T(2,128)(2,1)S(1)}, bf16[1,2,6,24,512]{4,1,3,2,0:T(2,128)(2,1)}, u32[]{:S(2)}) copy-start(bf16[1,2,6,24,512]{4,1,3,2,0:T(2,128)(2,1)} %copy-done.3) | copy-start | bytes 884740
  73.2 4.7 %copy-start.16 = (f32[2,6,24]{0,2,1:T(8,128)S(1)}, f32[2,6,24]{0,2,1:T(8,128)}, u32[]{:S(2)}) copy-start(f32[2,6,24]{0,2,1:T(8,128)} %copy-done.15) | copy-start | bytes 3460
  75.8 2.1 %copy-start.23 = (f32[2,6,24]{0,2,1:T(8,128)S(1)}, f32[2,6,24]{0,2,1:T(8,128)}, u32[]{:S(2)}) copy-start(f32[2,6,24]{0,2,1:T(8,128)} %reshape.177) | copy-start | bytes 3460
  75.8 2.1 %copy-start.24 = (f32[2,6,24]{0,2,1:T(8,128)S(1)}, f32[2,6,24]{0,2,1:T(8,128)}, u32[]{:S(2)}) copy-start(f32[2,6,24]{0,2,1:T(8,128)} %reshape.178) | copy-start | bytes 3460
  79.4 10.2 %collective-permute-start.2 = (bf16[2,2,3,24,512]{4,1,3,2,0:T(2,128)(2,1)S(1)}, bf16[2,2,3,24,512]{4,1,3,2,0:T(2,128)(2,1)S(1)}, u32[]{:S(2)}, u32[]{:S(2)}) collective-permute-start(bf16[2,2,3,24,512]{4,1,3,2,0:T(2,128)(2,1)S(1)} %fusion.46), channel_id=1, source_target_pairs={{24,0},{0,8},{8,16},{16,24},{25,1},{1,9},{9,17},{17,25},{26,2},{2,... | collective-permute-start | bytes 884744 | tf_op jit(solution)/shard_map/ppermute | solution.py:17
  89.9 31.0 %collective-permute-start.3 = (bf16[2,2,6,6,512]{4,1,3,2,0:T(2,128)(2,1)S(1)}, bf16[2,2,6,6,512]{4,1,3,2,0:T(2,128)(2,1)S(1)}, u32[]{:S(2)}, u32[]{:S(2)}) collective-permute-start(bf16[2,2,6,6,512]{4,1,3,2,0:T(2,128)(2,1)S(1)} %pad_maximum_fusion.7), channel_id=1, source_target_pairs={{7,0},{0,1},{1,2},{2,3},{3,4},{4,5},{5,6},{6,7},{15,8},{8,9},{9,10... | collective-permute-start | bytes 442376 | tf_op jit(solution)/shard_map/ppermute | solution.py:17
Sparse Core Ops, SparseCore 0:
  51.9 33.2 reduce-scatter.4
  87.6 33.1 reduce-scatter.2
  124.0 40.3 all-reduce.2
where the time goes:
time: 175 us; the launch traced here: 174 us
  waiting for transfers between devices  86.9 us (50%)
  matrix products  29 us (17%)
  local copies, waits for them, and re-layouts  22.9 us (13%)
  between operations  14.2 us (8%)
  other arithmetic  12.1 us (7%)
  starting transfers between devices  8.99 us (5%)
    psum x1, waiting for transfers between devices, per_device(): lax.psum(qkv_share.astype(jnp.bfloat16), 'lat').astype(jnp.float32)  40.7 us
    reduce_scatter x1, waiting for transfers between devices, per_device(): lax.psum_scatter(qkv_term.astype(jnp.bfloat16), 'lon', scatter_dimension=...  30.9 us
    ppermute x4, waiting for transfers between devices, passed_along(): return lax.ppermute(block, axis, route)  15.3 us
    ppermute x4, starting transfers between devices, passed_along(): return lax.ppermute(block, axis, route)  8.69 us
    unnamed x55, local copies, waits for them, and re-layouts  7.87 us
    dot_general x1, matrix products, per_device(): jnp.einsum('whqk,wqhd->wkhd', d_scores, queries, preferred_element_type=j...  4.85 us
    dot_general x1, matrix products, per_device(): jnp.einsum('whqk,wkhd->wqhd', d_scores, keys_all, preferred_element_type=...  4.7 us
  transfers between devices with their start and end apart: 7, of which 5 were waited for; matrix products, arithmetic and copies ran while one was open for 18% of the time, Pallas kernels for 0%

commit v1 on v0

v1 whole, which is shorter than its diff:
```python
import functools

import jax
import jax.numpy as jnp
from jax import lax
from jax.experimental import pallas as pl
from jax.experimental.pallas import tpu as pltpu
from jax.sharding import PartitionSpec as P

HEADS = 8
WIN_LAT = 6
WIN_LON = 12
LEVELS = 2
COLS = 24
HALF_LAT = WIN_LAT // 2
HALF_LON = WIN_LON // 2
INNER = COLS - HALF_LON
HALF = LEVELS * HALF_LAT * WIN_LON
WIN = 2 * HALF
TOKENS = 2 * WIN
LAT_ROWS = LEVELS * HALF_LAT * INNER
LON_ROWS = LEVELS * HALF_LAT * HALF_LON
LANES = 128

epsilon = 1e-05
BF = jnp.bfloat16
F32 = jnp.float32


def dot(a, b, dims):
    return lax.dot_general(a, b, (dims, ((), ())), preferred_element_type=F32)


NN = ((1,), (0,))
NT = ((1,), (1,))
TN = ((0,), (0,))


def div(x, by):
    return (x * ((65536 + by - 1) // by)) >> 16


def own_token(level, row, col):
    return level * (WIN_LAT * COLS) + row * COLS + col


def lat_piece_token(s, first):
    level = div(s, HALF_LAT * INNER)
    rest = s - level * (HALF_LAT * INNER)
    row = div(rest, INNER)
    return own_token(level, first + row, HALF_LON + rest - row * INNER)


def lon_piece_token(s, first):
    level = div(s, HALF_LAT * HALF_LON)
    rest = s - level * (HALF_LAT * HALF_LON)
    row = div(rest, HALF_LON)
    return own_token(level, first + row, rest - row * HALF_LON)


def window_sources(v):
    level = div(v, HALF_LAT * WIN_LON)
    rest = v - level * (HALF_LAT * WIN_LON)
    row = div(rest, WIN_LON)
    return level, row, rest - row * WIN_LON


def inner_window_own(v, kept):
    level, row, col = window_sources(v)
    return own_token(level, kept + row, HALF_LON + col)


def inner_window_lat(v):
    level, row, col = window_sources(v)
    return level * (HALF_LAT * INNER) + row * INNER + col


def outer_window_own(v, kept):
    level, row, col = window_sources(v)
    return jnp.where(col < HALF_LON, own_token(level, kept + row, HALF_LON + WIN_LON + col), -1)


def outer_window_lat(v):
    level, row, col = window_sources(v)
    return jnp.where(col < HALF_LON, level * (HALF_LAT * INNER) + row * INNER + WIN_LON + col, -1)


def outer_window_lon(v):
    level, row, col = window_sources(v)
    return jnp.where(col < HALF_LON, -1, level * (HALF_LAT * HALF_LON) + row * HALF_LON + col - HALF_LON)


def picks(source, rows, columns):
    index = source(lax.broadcasted_iota(jnp.int32, (rows, 1), 0))
    return (index == lax.broadcasted_iota(jnp.int32, (rows, columns), 1)).astype(BF)


def puts(source, rows, columns):
    index = source(lax.broadcasted_iota(jnp.int32, (1, columns), 1))
    return (lax.broadcasted_iota(jnp.int32, (rows, columns), 0) == index).astype(BF)


def pack_kernel(fields, cotangent, lat_out, lon_out, diag_out):
    even = lax.rem(lax.axis_index("lon"), 2) == 0
    sent = jnp.where(even, 0, HALF_LAT)
    kept = HALF_LAT - sent
    for out, pick in (
        (lat_out, picks(lambda s: lat_piece_token(s, sent), LAT_ROWS, TOKENS)),
        (lon_out, picks(lambda s: lon_piece_token(s, sent), LON_ROWS, TOKENS)),
        (diag_out, picks(lambda s: lon_piece_token(s, kept), LON_ROWS, TOKENS)),
    ):
        width = fields.shape[1]
        out[:, :width] = dot(pick, fields[...], NN).astype(BF)
        out[:, width:] = dot(pick, cotangent[...], NN).astype(BF)


def normalise(x):
    mean = jnp.mean(x, -1, keepdims=True)
    centred = x - mean
    variance = jnp.mean(centred * centred, -1, keepdims=True)
    inv_std = lax.rsqrt(variance + epsilon)
    return centred * inv_std, inv_std


def shares(transposed, lon_size, core):
    rows, tokens = transposed.shape
    by_core = transposed.reshape(lon_size // 2, 2, rows // lon_size, tokens)
    first = by_core[:, 0].reshape(rows // 2, tokens)
    second = by_core[:, 1].reshape(rows // 2, tokens)
    return jnp.where(core == 0, first, second), jnp.where(core == 0, second, first)


def transpose_bf16(block):
    return jnp.transpose(block.astype(F32)).astype(BF)


def put_split(out, lanes_from, block):
    width = out.shape[-1]
    for at in range(0, block.shape[1], width):
        out[(lanes_from + at) // width] = block[:, at : at + width].astype(out.dtype)


def attention_kernel(
    fields, cotangent, lat_in, lon_in, diag_in, qkv_weight, proj_weight,
    send_grad, windows_out, grads_out, normed_t_out, grads_t_out, d_projected, mixed,
):
    width = fields.shape[1]
    lat, lon = lax.axis_index("lat"), lax.axis_index("lon")
    lat_size, lon_size = lax.axis_size("lat"), lax.axis_size("lon")
    core = lax.rem(lon, 2)
    even = core == 0
    kept = jnp.where(even, HALF_LAT, 0)
    blocks = []
    for source, mine in ((0, fields), (1, cotangent)):
        lanes = slice(source * width, (source + 1) * width)
        blocks.append(
            jnp.concatenate(
                [
                    dot(picks(lambda v: inner_window_own(v, kept), HALF, TOKENS), mine[...], NN),
                    dot(picks(inner_window_lat, HALF, LAT_ROWS), lat_in[:, lanes], NN),
                    dot(picks(lambda v: outer_window_own(v, kept), HALF, TOKENS), mine[...], NN)
                    + dot(picks(outer_window_lon, HALF, LON_ROWS), lon_in[:, lanes], NN),
                    dot(picks(outer_window_lat, HALF, LAT_ROWS), lat_in[:, lanes], NN)
                    + dot(picks(outer_window_lon, HALF, LON_ROWS), diag_in[:, lanes], NN),
                ],
                axis=0,
            )
        )
    x = blocks[0]
    windows_out[...] = x.astype(BF)
    grads = blocks[1].astype(BF)
    grads_out[...] = grads
    normed, _ = normalise(x)
    normed_b = normed.astype(BF)
    projected = dot(normed_b, qkv_weight[...], NN).astype(BF)
    d_mixed = dot(grads, proj_weight[...], NT).astype(BF)

    head_size = width // HEADS
    factor = head_size ** (-0.5)
    apart = jnp.where(even, lat == lat_size - 1, lat == 0).astype(jnp.int32)
    half_b = (lax.broadcasted_iota(jnp.int32, (WIN, 2 * WIN), 0) >= HALF).astype(jnp.int32)
    at_a = lax.broadcasted_iota(jnp.int32, (WIN, 2 * WIN), 1)
    at_a = jnp.where(at_a >= WIN, at_a - WIN, at_a)
    half_a = (at_a >= HALF).astype(jnp.int32)
    allowed = ((half_a != half_b).astype(jnp.int32) * apart) == 0
    first_head = lax.broadcasted_iota(jnp.int32, (WIN, LANES), 1) < head_size
    zero = jnp.zeros((WIN, LANES), BF)

    def split_heads(block):
        return jnp.concatenate([jnp.where(first_head, block, zero), jnp.where(first_head, zero, block)], axis=0)

    def join_heads(block):
        return jnp.where(first_head, block[:WIN], block[WIN:]).astype(BF)

    for window in range(TOKENS // WIN):
        rows = slice(window * WIN, (window + 1) * WIN)
        for pair in range(width // LANES):
            at = pair * LANES
            q = projected[rows, at : at + LANES]
            k = projected[rows, width + at : width + at + LANES]
            v = projected[rows, 2 * width + at : 2 * width + at + LANES]
            dm = d_mixed[rows, at : at + LANES]
            q2, dm2 = split_heads(q), split_heads(dm)
            scores = dot(k, q2, NT) * factor
            scores = jnp.where(allowed, scores, -1e30)
            exponent = jnp.exp(scores - jnp.max(scores, 0, keepdims=True))
            probs = exponent * (1.0 / jnp.sum(exponent, 0, keepdims=True))
            probs_b = probs.astype(BF)
            mixed[rows, at : at + LANES] = join_heads(dot(probs_b, v, TN))
            d_probs = dot(v, dm2, NT)
            d_projected[rows, 2 * width + at : 2 * width + at + LANES] = dot(probs_b, dm2, NN).astype(BF)
            d_scores = probs * (d_probs - jnp.sum(d_probs * probs, 0, keepdims=True)) * factor
            d_scores = d_scores.astype(BF)
            d_projected[rows, at : at + LANES] = join_heads(dot(d_scores, k, TN))
            d_projected[rows, width + at : width + at + LANES] = dot(d_scores, q2, NN).astype(BF)

    normed_t = transpose_bf16(normed)
    grads_t = transpose_bf16(grads)
    normed_keep, normed_send = shares(normed_t, lon_size, core)
    grads_keep, grads_send = shares(grads_t, lon_size, core)
    normed_t_out[...] = normed_keep
    grads_t_out[...] = grads_keep
    put_split(send_grad, 0, dot(normed_send, d_projected[...], NN))
    put_split(send_grad, 3 * width, dot(grads_send, mixed[...], NN))


def output_kernel(
    windows, grads, normed_t, grads_t, d_projected, mixed, qkv_weight, proj_weight,
    keep_grad, results, lat_out, lon_out, diag_out,
):
    width = windows.shape[1]
    put_split(keep_grad, 0, dot(normed_t[...], d_projected[...], NN))
    put_split(keep_grad, 3 * width, dot(grads_t[...], mixed[...], NN))
    x = windows[...].astype(F32)
    normed, inv_std = normalise(x)
    output = (x + dot(mixed[...], proj_weight[...], NN)).astype(BF)
    d_normed = dot(d_projected[...], qkv_weight[...], NT)
    d_inputs = grads[...].astype(F32) + inv_std * (
        d_normed
        - jnp.mean(d_normed, -1, keepdims=True)
        - normed * jnp.mean(d_normed * normed, -1, keepdims=True)
    )
    results[:, :width] = output
    results[:, width:] = d_inputs.astype(BF)
    inner_y = slice(HALF, WIN)
    outer_x = slice(WIN, WIN + HALF)
    outer_y = slice(WIN + HALF, TOKENS)
    total = jnp.concatenate([output.astype(F32), d_inputs.astype(BF).astype(F32)], axis=1)
    y_inner = total[inner_y].astype(BF)
    y_outer = total[outer_y].astype(BF)
    x_outer = total[outer_x].astype(BF)
    lat_out[...] = (
        dot(puts(inner_window_lat, LAT_ROWS, HALF), y_inner, NN)
        + dot(puts(outer_window_lat, LAT_ROWS, HALF), y_outer, NN)
    ).astype(BF)
    lon_out[...] = dot(puts(outer_window_lon, LON_ROWS, HALF), x_outer, NN).astype(BF)
    diag_out[...] = dot(puts(outer_window_lon, LON_ROWS, HALF), y_outer, NN).astype(BF)


def place_kernel(results, lat_in, lon_in, diag_in, field_out, d_fields):
    width = field_out.shape[1]
    even = lax.rem(lax.axis_index("lon"), 2) == 0
    sent = jnp.where(even, 0, HALF_LAT)
    kept = HALF_LAT - sent
    put_lat = puts(lambda s: lat_piece_token(s, sent), TOKENS, LAT_ROWS)
    put_lon = puts(lambda s: lon_piece_token(s, sent), TOKENS, LON_ROWS)
    put_diag = puts(lambda s: lon_piece_token(s, kept), TOKENS, LON_ROWS)

    def own(t):
        window = (t >= WIN).astype(jnp.int32)
        u = t - window * WIN
        inner = inner_window_own(u, kept)
        outer = outer_window_own(u, kept)
        return jnp.where(u < HALF, jnp.where(window == 0, inner, outer), -1)

    put_own = puts(own, TOKENS, TOKENS)
    for index, out in ((0, field_out), (1, d_fields)):
        lanes = slice(index * width, (index + 1) * width)
        out[...] = (
            dot(put_own, results[:, lanes], NN)
            + dot(put_lat, lat_in[:, lanes], NN)
            + dot(put_lon, lon_in[:, lanes], NN)
            + dot(put_diag, diag_in[:, lanes], NN)
        ).astype(BF)


def add_kernel(a, b, out):
    out[...] = (a[...].astype(F32) + b[...].astype(F32)).astype(out.dtype)


def sum_kernel(parts, out):
    total = parts[0].astype(F32)
    for index in range(1, parts.shape[0]):
        total = total + parts[index].astype(F32)
    out[...] = total.astype(out.dtype)


def finish_kernel(parts, qkv_out, proj_out):
    width = proj_out.shape[0]
    total = jnp.concatenate([parts[i].astype(F32) for i in range(parts.shape[0])], axis=1)
    qkv_out[...] = total[:, : 3 * width]
    proj_out[...] = jnp.transpose(total[:, 3 * width :])


def call(kernel, outs, *args, name, flops=0, limit=32):
    vmem = pl.BlockSpec(memory_space=pltpu.VMEM)
    shapes = [jax.ShapeDtypeStruct(shape, dtype) for shape, dtype in outs]
    nbytes = sum(a.size * a.dtype.itemsize for a in (*args, *shapes))
    return pl.pallas_call(
        kernel,
        out_shape=shapes,
        in_specs=[vmem] * len(args),
        out_specs=[vmem] * len(shapes),
        compiler_params=pltpu.CompilerParams(vmem_limit_bytes=limit * 2**20),
        cost_estimate=pl.CostEstimate(flops=flops, bytes_accessed=nbytes, transcendentals=0),
        name=name,
    )(*args)


def routes(lat_size, lon_size):
    lat, lon, diag = [], [], []
    for i in range(lat_size):
        for j in range(lon_size):
            step = -1 if j % 2 == 0 else 1
            before = (j - 1) % lon_size
            me = i * lon_size + j
            lat.append((me, ((i + step) % lat_size) * lon_size + j))
            lon.append((me, i * lon_size + before))
            diag.append((me, ((i - step) % lat_size) * lon_size + before))
    return lat, lon, diag


def per_device(fields, cotangent, qkv_weight, proj_weight):
    levels, row_count, col_count, width = fields.shape
    lat_size, lon_size = lax.axis_size("lat"), lax.axis_size("lon")
    both = ("lat", "lon")
    lat_route, lon_route, diag_route = routes(lat_size, lon_size)

    def back(route):
        return [(target, source) for source, target in route]

    own_fields = fields.reshape(TOKENS, width)
    own_grads = cotangent.reshape(TOKENS, width)
    piece = [((LAT_ROWS, 2 * width), BF), ((LON_ROWS, 2 * width), BF), ((LON_ROWS, 2 * width), BF)]
    lat_piece, lon_piece, diag_piece = call(pack_kernel, piece, own_fields, own_grads, name="pack")
    lat_in = lax.ppermute(lat_piece, both, lat_route)
    diag_in = lax.ppermute(diag_piece, both, diag_route)
    lon_in = lax.ppermute(lon_piece, both, lon_route)

    split = (lat_size, width // 2, 4 * width // lat_size)
    send_grad, windows, grads, normed_t, grads_t, d_projected, mixed = call(
        attention_kernel,
        [
            (split, BF),
            ((TOKENS, width), BF),
            ((TOKENS, width), BF),
            ((width // 2, TOKENS), BF),
            ((width // 2, TOKENS), BF),
            ((TOKENS, 3 * width), BF),
            ((TOKENS, width), BF),
        ],
        own_fields, own_grads, lat_in, lon_in, diag_in, qkv_weight, proj_weight,
        name="attention", flops=2 * 10**9,
    )
    sibling = [(j, j ^ 1) for j in range(lon_size)]
    received = lax.ppermute(send_grad, "lon", sibling)
    keep_grad, results, lat_back, lon_back, diag_back = call(
        output_kernel,
        [(split, BF), ((TOKENS, 2 * width), BF), *piece],
        windows, grads, normed_t, grads_t, d_projected, mixed, qkv_weight, proj_weight,
        name="outputs", flops=10**9,
    )
    lat_home = lax.ppermute(lat_back, both, back(lat_route))
    diag_home = lax.ppermute(diag_back, both, back(diag_route))
    lon_home = lax.ppermute(lon_back, both, back(lon_route))

    (chip_sum,) = call(add_kernel, [(split, BF)], keep_grad, received, name="chip_sum")
    plane = lax.all_to_all(chip_sum, "lat", 0, 0)
    (plane_sum,) = call(sum_kernel, [(split[1:], BF)], plane, name="plane_sum")
    rows = width // lon_size
    by_chip = plane_sum.reshape(lon_size // 2, rows, split[2])
    groups = [list(range(core, lon_size, 2)) for core in range(2)]
    line = lax.all_to_all(by_chip, "lon", 0, 0, axis_index_groups=groups)
    (line_sum,) = call(sum_kernel, [((rows, split[2]), BF)], line, name="line_sum")
    shared = lax.all_to_all(jnp.broadcast_to(line_sum[None], (lat_size, rows, split[2])), "lat", 0, 0)
    field_out, d_fields = call(
        place_kernel,
        [((TOKENS, width), BF), ((TOKENS, width), BF)],
        results, lat_home, lon_home, diag_home,
        name="place",
    )
    qkv_grad, proj_grad = call(
        finish_kernel, [((rows, 3 * width), F32), ((width, rows), F32)], shared, name="finish"
    )
    return (field_out.reshape(fields.shape), d_fields.reshape(fields.shape), qkv_grad, proj_grad)


def solution(mesh):
    placed = (P(None, "lat", "lon", None), P(None, "lat", "lon", None), P(), P())
    return jax.shard_map(
        per_device,
        mesh=mesh,
        in_specs=placed,
        out_specs=(
            P(None, "lat", "lon", None),
            P(None, "lat", "lon", None),
            P("lon", None),
            P(None, "lon"),
        ),
        check_vma=False,
    )
```

time: 175 us -> 72.9 us (0.42)
  waiting for transfers between devices: 86.9 us -> 18.7 us
  matrix products: 29 us -> 0 us
  blocking collectives: 0 us -> 17.4 us
  local copies, waits for them, and re-layouts: 22.9 us -> 5.87 us
  between operations: 14.2 us -> 0.71 us
  other arithmetic: 12.1 us -> 0 us
  Pallas kernels: 0 us -> 11.7 us
  starting transfers between devices: 8.99 us -> 18.2 us
    psum x1 -> x0, waiting for transfers between devices: 40.7 us -> none  [per_device(): lax.psum(qkv_share.astype(jnp.bfloat16), 'lat').astype(jnp.float32)]
    reduce_scatter x2 -> x0, waiting for transfers between devices: 30.9 us -> none  [the longest x1 30.9 us: per_device(): lax.psum_scatter(qkv_term.astype(jnp.bfloat16), 'lon', scatter_dimension=...]
    dot_general x11 -> x0, matrix products: 25.6 us -> none  [the longest x1 4.85 us: per_device(): jnp.einsum('whqk,wqhd->wkhd', d_scores, queries, preferred_element_type=j...]
    all_to_all x0 -> x1, blocking collectives: none -> 17.4 us  [per_device(): plane = lax.all_to_all(chip_sum, 'lat', 0, 0)]
    pallas_call x0 -> x8, Pallas kernels: none -> 11.7 us  [call(): pl.pallas_call(kernel, out_shape=shapes, in_specs=[vmem] * len(args), out...]
    all_to_all x0 -> x2, starting transfers between devices: none -> 8.67 us  [the longest x1 5.27 us: per_device(): line = lax.all_to_all(by_chip, 'lon', 0, 0, axis_index_groups=groups)]
    all_to_all x0 -> x2, waiting for transfers between devices: none -> 7.27 us  [the longest x1 7.26 us: per_device(): line = lax.all_to_all(by_chip, 'lon', 0, 0, axis_index_groups=groups)]
    reshape x6 -> x0, local copies, waits for them, and re-layouts: 6.01 us -> none  [the longest x1 2.57 us: per_device(): projected.reshape(win_count, win_size, 3, head_count, head_size)]
  transfers between devices with their start and end apart: 7 -> 9, of which waited for: 5 -> 6; matrix products, arithmetic and copies ran while one was open for 18% -> 1% of each run, Pallas kernels for 0% -> 5%
where the time goes in v1:
time: 72.9 us; the launch traced here: 72.4 us
  waiting for transfers between devices  18.7 us (26%)
  starting transfers between devices  18.2 us (25%)
  blocking collectives  17.4 us (24%)
  Pallas kernels  11.7 us (16%)
  local copies, waits for them, and re-layouts  5.87 us (8%)
    all_to_all x1, blocking collectives, per_device(): plane = lax.all_to_all(chip_sum, 'lat', 0, 0)  17.4 us
    pallas_call x8, Pallas kernels, call(): pl.pallas_call(kernel, out_shape=shapes, in_specs=[vmem] * len(args), out...  11.7 us
    all_to_all x1, waiting for transfers between devices, per_device(): line = lax.all_to_all(by_chip, 'lon', 0, 0, axis_index_groups=groups)  7.26 us
    all_to_all x1, starting transfers between devices, per_device(): line = lax.all_to_all(by_chip, 'lon', 0, 0, axis_index_groups=groups)  5.27 us
    unnamed x13, local copies, waits for them, and re-layouts  5.14 us
    ppermute x1, starting transfers between devices, per_device(): lat_in = lax.ppermute(lat_piece, both, lat_route)  3.93 us
    ppermute x1, waiting for transfers between devices, per_device(): lon_home = lax.ppermute(lon_back, both, back(lon_route))  3.85 us
    all_to_all x1, starting transfers between devices, per_device(): lax.all_to_all(jnp.broadcast_to(line_sum[None], (lat_size, rows, split[2]...  3.41 us
  transfers between devices with their start and end apart: 9, of which 6 were waited for; matrix products, arithmetic and copies ran while one was open for 1% of the time, Pallas kernels for 5%

profile of v1, /device:TPU:0, one launch (start us, length us, event | category | flops | bytes accessed | tf_op | source)
XLA Modules:
  0.0 72.4 jit_solution(14072612564785745948)
XLA Ops:
  0.6 0.0 copy-start.4
  0.6 1.0 %copy-done.4 = bf16[2,6,24,512]{3,2,1,0:T(8,128)(2,1)S(1)} copy-done((bf16[2,6,24,512]{3,2,1,0:T(8,128)(2,1)S(1)}, bf16[2,6,24,512]{3,2,1,0:T(8,128)(2,1)}, u32[]{:S(2)}) %copy-start.4) | copy-done | bytes 294936
  1.6 0.0 copy-start.5
  1.6 1.0 %copy-done.5 = bf16[2,6,24,512]{3,2,1,0:T(8,128)(2,1)S(1)} copy-done((bf16[2,6,24,512]{3,2,1,0:T(8,128)(2,1)S(1)}, bf16[2,6,24,512]{3,2,1,0:T(8,128)(2,1)}, u32[]{:S(2)}) %copy-start.5) | copy-done | bytes 294936
  2.6 0.5 pack.1
  3.0 3.9 %collective-permute-start = (bf16[108,1024]{1,0:T(8,128)(2,1)S(1)}, bf16[108,1024]{1,0:T(8,128)(2,1)S(1)}, u32[]{:S(2)}, u32[]{:S(2)}) collective-permute-start(bf16[108,1024]{1,0:T(8,128)(2,1)S(1)} %get-tuple-element.23), channel_id=1, source_target_pairs={{0,24},{1,9},{2,26},{3,11},{4,28},{5,13},{6,30},{7,15},{8,0},{9,17... | collective-permute-start | bytes 663560 | tf_op jit(solution)/shard_map/ppermute | solution.py:346
  7.0 1.8 %collective-permute-start.1 = (bf16[36,1024]{1,0:T(8,128)(2,1)S(1)}, bf16[36,1024]{1,0:T(8,128)(2,1)S(1)}, u32[]{:S(2)}, u32[]{:S(2)}) collective-permute-start(bf16[36,1024]{1,0:T(8,128)(2,1)S(1)} %get-tuple-element.24), channel_id=1, source_target_pairs={{0,7},{1,0},{2,1},{3,2},{4,3},{5,4},{6,5},{7,6},{8,15},{9,8},{10,9... | collective-permute-start | bytes 221192 | tf_op jit(solution)/shard_map/ppermute | solution.py:348
  8.8 0.9 %collective-permute-start.2 = (bf16[36,1024]{1,0:T(8,128)(2,1)S(1)}, bf16[36,1024]{1,0:T(8,128)(2,1)S(1)}, u32[]{:S(2)}, u32[]{:S(2)}) collective-permute-start(bf16[36,1024]{1,0:T(8,128)(2,1)S(1)} %get-tuple-element.25), channel_id=1, source_target_pairs={{0,15},{1,24},{2,9},{3,26},{4,11},{5,28},{6,13},{7,30},{8,23},{9,0... | collective-permute-start | bytes 221192 | tf_op jit(solution)/shard_map/ppermute | solution.py:347
  9.7 1.1 %collective-permute-done.1.lon_in = bf16[36,1024]{1,0:T(8,128)(2,1)S(1)} collective-permute-done((bf16[36,1024]{1,0:T(8,128)(2,1)S(1)}, bf16[36,1024]{1,0:T(8,128)(2,1)S(1)}, u32[]{:S(2)}, u32[]{:S(2)}) %collective-permute-start.1) | collective-permute-done | bytes 73760 | tf_op jit(solution)/shard_map/ppermute | solution.py:348
  10.9 3.4 %collective-permute-done.2.diag_in = bf16[36,1024]{1,0:T(8,128)(2,1)S(1)} collective-permute-done((bf16[36,1024]{1,0:T(8,128)(2,1)S(1)}, bf16[36,1024]{1,0:T(8,128)(2,1)S(1)}, u32[]{:S(2)}, u32[]{:S(2)}) %collective-permute-start.2) | collective-permute-done | bytes 73760 | tf_op jit(solution)/shard_map/ppermute | solution.py:347
  14.2 0.0 collective-permute-done.lat_in
  14.2 0.0 copy-start
  14.2 1.4 %copy-done = bf16[512,1536]{1,0:T(8,128)(2,1)S(1)} copy-done((bf16[512,1536]{1,0:T(8,128)(2,1)S(1)}, bf16[512,1536]{1,0:T(8,128)(2,1)}, u32[]{:S(2)}) %copy-start) | copy-done | bytes 1572888
  15.6 0.0 copy-start.2
  15.7 1.0 %copy-done.2 = bf16[512,512]{1,0:T(8,128)(2,1)S(1)} copy-done((bf16[512,512]{1,0:T(8,128)(2,1)S(1)}, bf16[512,512]{1,0:T(8,128)(2,1)}, u32[]{:S(2)}) %copy-start.2) | copy-done | bytes 524312
  16.7 0.0 copy-start.1
  16.7 0.0 copy-start.3
  16.7 5.8 %attention.1 = (bf16[4,256,512]{2,1,0:T(8,128)(2,1)S(1)}, bf16[288,512]{1,0:T(8,128)(2,1)S(1)}, bf16[288,512]{1,0:T(8,128)(2,1)S(1)}, bf16[256,288]{1,0:T(8,128)...) custom-call(bf16[288,512]{1,0:T(8,128)(2,1)S(1)} %bitcast.6, ...), custom_call_target="tpu_custom_call" | custom-call | flops 2000000000 | bytes 6168576 | tf_op jit(solution)/shard_map/attention/pallas_call | solution.py:309
  22.5 0.1 collective-permute-start.6
  22.6 0.0 copy-done.1
  22.6 0.0 copy-done.3
  22.6 1.9 %outputs.1 = (bf16[4,256,512]{2,1,0:T(8,128)(2,1)S(1)}, bf16[288,1024]{1,0:T(8,128)(2,1)S(1)}, bf16[108,1024]{1,0:T(8,128)(2,1)S(1)}, bf16[36,1024]{1,0:T(8,128)(2,1)S(1)}, bf16[36,1024]{1,0:T(8,128)(2,1)S(1)}) custom-call(bf16[288,512]{1,0:T(8,128)(2,1)S(1)} %get-tuple-element.26.windows, bf16[288,512]{1,0:T(8,128)(2,1)S(1)} %get-tuple-element.27.grads, ...), custom_call_target="tpu_custom_call" | custom-call | flops 1000000000 | bytes 6168576 | tf_op jit(solution)/shard_map/outputs/pallas_call | solution.py:309
  24.5 0.8 %collective-permute-done.6.b = bf16[4,256,512]{2,1,0:T(8,128)(2,1)S(1)} collective-permute-done((bf16[4,256,512]{2,1,0:T(8,128)(2,1)S(1)}, bf16[4,256,512]{2,1,0:T(8,128)(2,1)S(1)}, u32[]{:S(2)}, u32[]{:S(2)}) %collective-permute-start.6) | collective-permute-done | bytes 1048608 | tf_op jit(solution)/shard_map/ppermute | solution.py:366
  25.2 0.2 chip_sum.1
  25.5 17.4 %all_to_all.15.parts = bf16[4,256,512]{2,1,0:T(8,128)(2,1)S(1)} all-to-all(bf16[4,256,512]{2,1,0:T(8,128)(2,1)S(1)} %chip_sum.1), channel_id=1, replica_groups=mesh['lat'=4,'lon'=8] {'lat'}, dimensions={0} | all-to-all | bytes 2097152 | tf_op jit(solution)/shard_map/all_to_all | solution.py:378
  42.8 0.8 %plane_sum.1 = bf16[256,512]{1,0:T(8,128)(2,1)} custom-call(bf16[4,256,512]{2,1,0:T(8,128)(2,1)S(1)} %all_to_all.15.parts), custom_call_target="tpu_custom_call" | custom-call | bytes 1310720 | tf_op jit(solution)/shard_map/plane_sum/pallas_call | solution.py:309
  43.7 5.3 %all-to-all-start.1 = ((bf16[4,64,512]{2,1,0:T(8,128)(2,1)}), bf16[4,64,512]{2,1,0:T(8,128)(2,1)S(1)}, u32[]{:S(2)}, u32[]{:S(2)}) async-start(bf16[4,64,512]{2,1,0:T(8,128)(2,1)} %bitcast.4), calls=%async_computation.1 | async-start | bytes 524288 | tf_op jit(solution)/shard_map/all_to_all | solution.py:383
  48.9 0.9 %collective-permute-start.3 = (bf16[108,1024]{1,0:T(8,128)(2,1)S(1)}, bf16[108,1024]{1,0:T(8,128)(2,1)S(1)}, u32[]{:S(2)}, u32[]{:S(2)}) collective-permute-start(bf16[108,1024]{1,0:T(8,128)(2,1)S(1)} %get-tuple-element.33), channel_id=1, source_target_pairs={{24,0},{9,1},{26,2},{11,3},{28,4},{13,5},{30,6},{15,7},{0,8},{17,9... | collective-permute-start | bytes 663560 | tf_op jit(solution)/shard_map/ppermute | solution.py:373
  49.9 7.3 %all-to-all-done.1.parts = bf16[4,64,512]{2,1,0:T(8,128)(2,1)S(1)} async-done(((bf16[4,64,512]{2,1,0:T(8,128)(2,1)}), bf16[4,64,512]{2,1,0:T(8,128)(2,1)S(1)}, u32[]{:S(2)}, u32[]{:S(2)}) %all-to-all-start.1) | async-done | bytes 262176 | tf_op jit(solution)/shard_map/all_to_all | solution.py:383
  57.2 0.7 broadcast_in_dim.2
  57.9 3.4 %all-to-all-start.2 = ((bf16[4,64,512]{2,1,0:T(8,128)(2,1)}), bf16[4,64,512]{2,1,0:T(8,128)(2,1)S(1)}, u32[]{:S(2)}, u32[]{:S(2)}) async-start(bf16[4,64,512]{2,1,0:T(8,128)(2,1)} %broadcast_in_dim.2), calls=%async_computation.2 | async-start | bytes 524288 | tf_op jit(solution)/shard_map/all_to_all | solution.py:385
  61.3 0.1 collective-permute-start.4
  61.4 1.8 %collective-permute-start.5 = (bf16[36,1024]{1,0:T(8,128)(2,1)S(1)}, bf16[36,1024]{1,0:T(8,128)(2,1)S(1)}, u32[]{:S(2)}, u32[]{:S(2)}) collective-permute-start(bf16[36,1024]{1,0:T(8,128)(2,1)S(1)} %get-tuple-element.35), channel_id=1, source_target_pairs={{15,0},{24,1},{9,2},{26,3},{11,4},{28,5},{13,6},{30,7},{23,8},{0,9... | collective-permute-start | bytes 221192 | tf_op jit(solution)/shard_map/ppermute | solution.py:374
  63.2 3.9 %collective-permute-done.4.lon_in = bf16[36,1024]{1,0:T(8,128)(2,1)S(1)} collective-permute-done((bf16[36,1024]{1,0:T(8,128)(2,1)S(1)}, bf16[36,1024]{1,0:T(8,128)(2,1)S(1)}, u32[]{:S(2)}, u32[]{:S(2)}) %collective-permute-start.4) | collective-permute-done | bytes 73760 | tf_op jit(solution)/shard_map/ppermute | solution.py:375
  67.0 2.2 %collective-permute-done.5.diag_in = bf16[36,1024]{1,0:T(8,128)(2,1)S(1)} collective-permute-done((bf16[36,1024]{1,0:T(8,128)(2,1)S(1)}, bf16[36,1024]{1,0:T(8,128)(2,1)S(1)}, u32[]{:S(2)}, u32[]{:S(2)}) %collective-permute-start.5) | collective-permute-done | bytes 73760 | tf_op jit(solution)/shard_map/ppermute | solution.py:374
  69.3 0.0 collective-permute-done.3.lat_in
  69.3 1.6 %place.1 = (bf16[288,512]{1,0:T(8,128)(2,1)}, bf16[288,512]{1,0:T(8,128)(2,1)}) custom-call(bf16[288,1024]{1,0:T(8,128)(2,1)S(1)} %get-tuple-element.32.results, bf16[108,1024]{1,0:T(8,128)(2,1)S(1)} %collective-permute-done.3.lat_in, bf16[36,1024]{1,0:T(8,128)(2,1)S(1)} %collective-permute-done.4.lon_in, bf16[36,1024]{1,0:T(8,128)(2,1)S(1)} %collective-permute-done.5.diag_in), custom_call_target="tpu_custom_call" | custom-call | bytes 1548288 | tf_op jit(solution)/shard_map/place/pallas_call | solution.py:309
  70.9 0.0 all-to-all-done.2.parts
  70.9 0.8 %finish.1 = (f32[64,1536]{1,0:T(8,128)}, f32[512,64]{1,0:T(8,128)S(1)}) custom-call(bf16[4,64,512]{2,1,0:T(8,128)(2,1)S(1)} %all-to-all-done.2.parts), custom_call_target="tpu_custom_call" | custom-call | bytes 786432 | tf_op jit(solution)/shard_map/finish/pallas_call | solution.py:309
  71.7 0.8 %copy.8 = f32[512,64]{0,1:T(8,128)} copy(f32[512,64]{1,0:T(8,128)S(1)} %get-tuple-element.45) | data formatting | bytes 262144
  (1 shorter events, 0.0 us)
Async XLA Ops:
  0.6 1.0 %copy-start.4 = (bf16[2,6,24,512]{3,2,1,0:T(8,128)(2,1)S(1)}, bf16[2,6,24,512]{3,2,1,0:T(8,128)(2,1)}, u32[]{:S(2)}) copy-start(bf16[2,6,24,512]{3,2,1,0:T(8,128)(2,1)} %param.4) | copy-start | bytes 884740
  1.6 1.0 %copy-start.5 = (bf16[2,6,24,512]{3,2,1,0:T(8,128)(2,1)S(1)}, bf16[2,6,24,512]{3,2,1,0:T(8,128)(2,1)}, u32[]{:S(2)}) copy-start(bf16[2,6,24,512]{3,2,1,0:T(8,128)(2,1)} %param.5) | copy-start | bytes 884740
  3.0 11.2 %collective-permute-start = (bf16[108,1024]{1,0:T(8,128)(2,1)S(1)}, bf16[108,1024]{1,0:T(8,128)(2,1)S(1)}, u32[]{:S(2)}, u32[]{:S(2)}) collective-permute-start(bf16[108,1024]{1,0:T(8,128)(2,1)S(1)} %get-tuple-element.23), channel_id=1, source_target_pairs={{0,24},{1,9},{2,26},{3,11},{4,28},{5,13},{6,30},{7,15},{8,0},{9,17... | collective-permute-start | bytes 663560 | tf_op jit(solution)/shard_map/ppermute | solution.py:346
  7.0 3.9 %collective-permute-start.1 = (bf16[36,1024]{1,0:T(8,128)(2,1)S(1)}, bf16[36,1024]{1,0:T(8,128)(2,1)S(1)}, u32[]{:S(2)}, u32[]{:S(2)}) collective-permute-start(bf16[36,1024]{1,0:T(8,128)(2,1)S(1)} %get-tuple-element.24), channel_id=1, source_target_pairs={{0,7},{1,0},{2,1},{3,2},{4,3},{5,4},{6,5},{7,6},{8,15},{9,8},{10,9... | collective-permute-start | bytes 221192 | tf_op jit(solution)/shard_map/ppermute | solution.py:348
  8.8 5.4 %collective-permute-start.2 = (bf16[36,1024]{1,0:T(8,128)(2,1)S(1)}, bf16[36,1024]{1,0:T(8,128)(2,1)S(1)}, u32[]{:S(2)}, u32[]{:S(2)}) collective-permute-start(bf16[36,1024]{1,0:T(8,128)(2,1)S(1)} %get-tuple-element.25), channel_id=1, source_target_pairs={{0,15},{1,24},{2,9},{3,26},{4,11},{5,28},{6,13},{7,30},{8,23},{9,0... | collective-permute-start | bytes 221192 | tf_op jit(solution)/shard_map/ppermute | solution.py:347
  14.2 1.4 %copy-start = (bf16[512,1536]{1,0:T(8,128)(2,1)S(1)}, bf16[512,1536]{1,0:T(8,128)(2,1)}, u32[]{:S(2)}) copy-start(bf16[512,1536]{1,0:T(8,128)(2,1)} %qkv_weight.3) | copy-start | bytes 4718596
  15.6 1.0 %copy-start.2 = (bf16[512,512]{1,0:T(8,128)(2,1)S(1)}, bf16[512,512]{1,0:T(8,128)(2,1)}, u32[]{:S(2)}) copy-start(bf16[512,512]{1,0:T(8,128)(2,1)} %proj_weight.3) | copy-start | bytes 1572868
  16.7 5.9 %copy-start.1 = (bf16[512,1536]{1,0:T(8,128)(2,1)S(1)}, bf16[512,1536]{1,0:T(8,128)(2,1)}, u32[]{:S(2)}) copy-start(bf16[512,1536]{1,0:T(8,128)(2,1)} %qkv_weight.3) | copy-start | bytes 4718596
  16.7 5.9 %copy-start.3 = (bf16[512,512]{1,0:T(8,128)(2,1)S(1)}, bf16[512,512]{1,0:T(8,128)(2,1)}, u32[]{:S(2)}) copy-start(bf16[512,512]{1,0:T(8,128)(2,1)} %proj_weight.3) | copy-start | bytes 1572868
  22.5 2.7 %collective-permute-start.6 = (bf16[4,256,512]{2,1,0:T(8,128)(2,1)S(1)}, bf16[4,256,512]{2,1,0:T(8,128)(2,1)S(1)}, u32[]{:S(2)}, u32[]{:S(2)}) collective-permute-start(bf16[4,256,512]{2,1,0:T(8,128)(2,1)S(1)} %get-tuple-element.39), channel_id=1, source_target_pairs={{0,1},{1,0},{2,3},{3,2},{4,5},{5,4},{6,7},{7,6},{8,9},{9,8},{10,11... | collective-permute-start | bytes 3145736 | tf_op jit(solution)/shard_map/ppermute | solution.py:366
  43.7 13.4 %all-to-all-start.1 = ((bf16[4,64,512]{2,1,0:T(8,128)(2,1)}), bf16[4,64,512]{2,1,0:T(8,128)(2,1)S(1)}, u32[]{:S(2)}, u32[]{:S(2)}) async-start(bf16[4,64,512]{2,1,0:T(8,128)(2,1)} %bitcast.4), calls=%async_computation.1 | async-start | bytes 524288 | tf_op jit(solution)/shard_map/all_to_all | solution.py:383
  48.9 20.3 %collective-permute-start.3 = (bf16[108,1024]{1,0:T(8,128)(2,1)S(1)}, bf16[108,1024]{1,0:T(8,128)(2,1)S(1)}, u32[]{:S(2)}, u32[]{:S(2)}) collective-permute-start(bf16[108,1024]{1,0:T(8,128)(2,1)S(1)} %get-tuple-element.33), channel_id=1, source_target_pairs={{24,0},{9,1},{26,2},{11,3},{28,4},{13,5},{30,6},{15,7},{0,8},{17,9... | collective-permute-start | bytes 663560 | tf_op jit(solution)/shard_map/ppermute | solution.py:373
  57.9 13.0 %all-to-all-start.2 = ((bf16[4,64,512]{2,1,0:T(8,128)(2,1)}), bf16[4,64,512]{2,1,0:T(8,128)(2,1)S(1)}, u32[]{:S(2)}, u32[]{:S(2)}) async-start(bf16[4,64,512]{2,1,0:T(8,128)(2,1)} %broadcast_in_dim.2), calls=%async_computation.2 | async-start | bytes 524288 | tf_op jit(solution)/shard_map/all_to_all | solution.py:385
  61.3 5.7 %collective-permute-start.4 = (bf16[36,1024]{1,0:T(8,128)(2,1)S(1)}, bf16[36,1024]{1,0:T(8,128)(2,1)S(1)}, u32[]{:S(2)}, u32[]{:S(2)}) collective-permute-start(bf16[36,1024]{1,0:T(8,128)(2,1)S(1)} %get-tuple-element.34), channel_id=1, source_target_pairs={{7,0},{0,1},{1,2},{2,3},{3,4},{4,5},{5,6},{6,7},{15,8},{8,9},{9,10... | collective-permute-start | bytes 221192 | tf_op jit(solution)/shard_map/ppermute | solution.py:375
  61.4 7.9 %collective-permute-start.5 = (bf16[36,1024]{1,0:T(8,128)(2,1)S(1)}, bf16[36,1024]{1,0:T(8,128)(2,1)S(1)}, u32[]{:S(2)}, u32[]{:S(2)}) collective-permute-start(bf16[36,1024]{1,0:T(8,128)(2,1)S(1)} %get-tuple-element.35), channel_id=1, source_target_pairs={{15,0},{24,1},{9,2},{26,3},{11,4},{28,5},{13,6},{30,7},{23,8},{0,9... | collective-permute-start | bytes 221192 | tf_op jit(solution)/shard_map/ppermute | solution.py:374

commit v2 on v1

--- a/solution.py
+++ b/solution.py
@@ -100,18 +100,41 @@
     return (lax.broadcasted_iota(jnp.int32, (rows, columns), 0) == index).astype(BF)
 
 
-def pack_kernel(fields, cotangent, lat_out, lon_out, diag_out):
+def pack_kernel(fields_hbm, cotangent_hbm, lat_out, lon_out, diag_out, own_out, fields, cotangent, arrived):
+    loads = [
+        pltpu.make_async_copy(fields_hbm, fields, arrived.at[0]),
+        pltpu.make_async_copy(cotangent_hbm, cotangent, arrived.at[1]),
+    ]
+    for load in loads:
+        load.start()
     even = lax.rem(lax.axis_index("lon"), 2) == 0
     sent = jnp.where(even, 0, HALF_LAT)
     kept = HALF_LAT - sent
-    for out, pick in (
-        (lat_out, picks(lambda s: lat_piece_token(s, sent), LAT_ROWS, TOKENS)),
-        (lon_out, picks(lambda s: lon_piece_token(s, sent), LON_ROWS, TOKENS)),
-        (diag_out, picks(lambda s: lon_piece_token(s, kept), LON_ROWS, TOKENS)),
-    ):
-        width = fields.shape[1]
-        out[:, :width] = dot(pick, fields[...], NN).astype(BF)
-        out[:, width:] = dot(pick, cotangent[...], NN).astype(BF)
+    width = fields.shape[1]
+    moves = (
+        (lat_out, 0, picks(lambda s: lat_piece_token(s, sent), LAT_ROWS, TOKENS)),
+        (lon_out, 0, picks(lambda s: lon_piece_token(s, sent), LON_ROWS, TOKENS)),
+        (diag_out, 0, picks(lambda s: lon_piece_token(s, kept), LON_ROWS, TOKENS)),
+        (own_out, 0, picks(lambda v: inner_window_own(v, kept), HALF, TOKENS)),
+        (own_out, 1, picks(lambda v: outer_window_own(v, kept), HALF, TOKENS)),
+    )
+    for load in loads:
+        load.wait()
+    for out, half, pick in moves:
+        rows = slice(half * HALF, half * HALF + pick.shape[0])
+        out[rows, :width] = dot(pick, fields[...], NN).astype(out.dtype)
+        out[rows, width:] = dot(pick, cotangent[...], NN).astype(out.dtype)
+
+
+def weights_kernel(_, qkv_hbm, proj_hbm, qkv_weight, proj_weight, arrived):
+    loads = [
+        pltpu.make_async_copy(qkv_hbm, qkv_weight, arrived.at[0]),
+        pltpu.make_async_copy(proj_hbm, proj_weight, arrived.at[1]),
+    ]
+    for load in loads:
+        load.start()
+    for load in loads:
+        load.wait()
 
 
 def normalise(x):
@@ -122,50 +145,51 @@
     return centred * inv_std, inv_std
 
 
-def shares(transposed, lon_size, core):
-    rows, tokens = transposed.shape
-    by_core = transposed.reshape(lon_size // 2, 2, rows // lon_size, tokens)
-    first = by_core[:, 0].reshape(rows // 2, tokens)
-    second = by_core[:, 1].reshape(rows // 2, tokens)
-    return jnp.where(core == 0, first, second), jnp.where(core == 0, second, first)
+def swap_bits(index, size, core):
+    bits = size.bit_length() - 1
+    turned = sum(((index >> b) & 1) << (bits - 1 - b) for b in range(bits))
+    return jnp.where(core == 0, index, turned)
+
+
+def shares(transposed, out, lon, core_of, lon_size):
+    rows = transposed.shape[0] // lon_size
+    chip = lon >> 1
+    for step in range(lon_size // 2):
+        start = pl.multiple_of(((chip ^ step) * 2 + core_of) * rows, rows)
+        out[step * rows : (step + 1) * rows, :] = transposed[pl.ds(start, rows), :]
 
 
 def transpose_bf16(block):
     return jnp.transpose(block.astype(F32)).astype(BF)
 
 
-def put_split(out, lanes_from, block):
-    width = out.shape[-1]
+def put_split(out, lanes_from, block, lat, core):
+    size, _, width = out.shape
     for at in range(0, block.shape[1], width):
-        out[(lanes_from + at) // width] = block[:, at : at + width].astype(out.dtype)
+        slot = swap_bits(lat ^ ((lanes_from + at) // width), size, core)
+        out[slot] = block[:, at : at + width].astype(out.dtype)
 
 
 def attention_kernel(
-    fields, cotangent, lat_in, lon_in, diag_in, qkv_weight, proj_weight,
-    send_grad, windows_out, grads_out, normed_t_out, grads_t_out, d_projected, mixed,
+    own, lat_in, lon_in, diag_in, qkv_weight, proj_weight,
+    send_grad, windows_out, grads_out, normed_t_out, grads_t_out, d_projected, mixed, normed_t, grads_t, send_rows,
 ):
-    width = fields.shape[1]
+    width = own.shape[1] // 2
     lat, lon = lax.axis_index("lat"), lax.axis_index("lon")
     lat_size, lon_size = lax.axis_size("lat"), lax.axis_size("lon")
     core = lax.rem(lon, 2)
     even = core == 0
-    kept = jnp.where(even, HALF_LAT, 0)
-    blocks = []
-    for source, mine in ((0, fields), (1, cotangent)):
-        lanes = slice(source * width, (source + 1) * width)
-        blocks.append(
-            jnp.concatenate(
-                [
-                    dot(picks(lambda v: inner_window_own(v, kept), HALF, TOKENS), mine[...], NN),
-                    dot(picks(inner_window_lat, HALF, LAT_ROWS), lat_in[:, lanes], NN),
-                    dot(picks(lambda v: outer_window_own(v, kept), HALF, TOKENS), mine[...], NN)
-                    + dot(picks(outer_window_lon, HALF, LON_ROWS), lon_in[:, lanes], NN),
-                    dot(picks(outer_window_lat, HALF, LAT_ROWS), lat_in[:, lanes], NN)
-                    + dot(picks(outer_window_lon, HALF, LON_ROWS), diag_in[:, lanes], NN),
-                ],
-                axis=0,
-            )
-        )
+    outer_lon = picks(outer_window_lon, HALF, LON_ROWS)
+    both = jnp.concatenate(
+        [
+            own[:HALF],
+            dot(picks(inner_window_lat, HALF, LAT_ROWS), lat_in[...], NN),
+            own[HALF:] + dot(outer_lon, lon_in[...], NN),
+            dot(picks(outer_window_lat, HALF, LAT_ROWS), lat_in[...], NN) + dot(outer_lon, diag_in[...], NN),
+        ],
+        axis=0,
+    )
+    blocks = both[:, :width], both[:, width:]
     x = blocks[0]
     windows_out[...] = x.astype(BF)
     grads = blocks[1].astype(BF)
@@ -214,23 +238,23 @@
             d_projected[rows, at : at + LANES] = join_heads(dot(d_scores, k, TN))
             d_projected[rows, width + at : width + at + LANES] = dot(d_scores, q2, NN).astype(BF)
 
-    normed_t = transpose_bf16(normed)
-    grads_t = transpose_bf16(grads)
-    normed_keep, normed_send = shares(normed_t, lon_size, core)
-    grads_keep, grads_send = shares(grads_t, lon_size, core)
-    normed_t_out[...] = normed_keep
-    grads_t_out[...] = grads_keep
-    put_split(send_grad, 0, dot(normed_send, d_projected[...], NN))
-    put_split(send_grad, 3 * width, dot(grads_send, mixed[...], NN))
+    normed_t[...] = transpose_bf16(normed)
+    grads_t[...] = transpose_bf16(grads)
+    shares(normed_t, send_rows, lon, 1 - core, lon_size)
+    put_split(send_grad, 0, dot(send_rows[...], d_projected[...], NN), lat, 1 - core)
+    shares(grads_t, send_rows, lon, 1 - core, lon_size)
+    put_split(send_grad, 3 * width, dot(send_rows[...], mixed[...], NN), lat, 1 - core)
+    shares(normed_t, normed_t_out, lon, core, lon_size)
+    shares(grads_t, grads_t_out, lon, core, lon_size)
 
 
 def output_kernel(
-    windows, grads, normed_t, grads_t, d_projected, mixed, qkv_weight, proj_weight,
-    keep_grad, results, lat_out, lon_out, diag_out,
+    windows, grads, normed_t, grads_t, d_projected, mixed, qkv_weight, proj_weight, keep_grad, results
 ):
     width = windows.shape[1]
-    put_split(keep_grad, 0, dot(normed_t[...], d_projected[...], NN))
-    put_split(keep_grad, 3 * width, dot(grads_t[...], mixed[...], NN))
+    lat, core = lax.axis_index("lat"), lax.rem(lax.axis_index("lon"), 2)
+    put_split(keep_grad, 0, dot(normed_t[...], d_projected[...], NN), lat, core)
+    put_split(keep_grad, 3 * width, dot(grads_t[...], mixed[...], NN), lat, core)
     x = windows[...].astype(F32)
     normed, inv_std = normalise(x)
     output = (x + dot(mixed[...], proj_weight[...], NN)).astype(BF)
@@ -242,19 +266,20 @@
     )
     results[:, :width] = output
     results[:, width:] = d_inputs.astype(BF)
-    inner_y = slice(HALF, WIN)
-    outer_x = slice(WIN, WIN + HALF)
-    outer_y = slice(WIN + HALF, TOKENS)
-    total = jnp.concatenate([output.astype(F32), d_inputs.astype(BF).astype(F32)], axis=1)
-    y_inner = total[inner_y].astype(BF)
-    y_outer = total[outer_y].astype(BF)
-    x_outer = total[outer_x].astype(BF)
+
+
+def pack_back_kernel(_, results, lat_out, lon_out, diag_out):
+    total = results[...].astype(F32)
+    y_inner = total[HALF:WIN].astype(BF)
+    x_outer = total[WIN : WIN + HALF].astype(BF)
+    y_outer = total[WIN + HALF :].astype(BF)
     lat_out[...] = (
         dot(puts(inner_window_lat, LAT_ROWS, HALF), y_inner, NN)
         + dot(puts(outer_window_lat, LAT_ROWS, HALF), y_outer, NN)
     ).astype(BF)
-    lon_out[...] = dot(puts(outer_window_lon, LON_ROWS, HALF), x_outer, NN).astype(BF)
-    diag_out[...] = dot(puts(outer_window_lon, LON_ROWS, HALF), y_outer, NN).astype(BF)
+    put_lon = puts(outer_window_lon, LON_ROWS, HALF)
+    lon_out[...] = dot(put_lon, x_outer, NN).astype(BF)
+    diag_out[...] = dot(put_lon, y_outer, NN).astype(BF)
 
 
 def place_kernel(results, lat_in, lon_in, diag_in, field_out, d_fields):
@@ -284,33 +309,50 @@
         ).astype(BF)
 
 
-def add_kernel(a, b, out):
-    out[...] = (a[...].astype(F32) + b[...].astype(F32)).astype(out.dtype)
-
-
-def sum_kernel(parts, out):
-    total = parts[0].astype(F32)
-    for index in range(1, parts.shape[0]):
-        total = total + parts[index].astype(F32)
+def halve_kernel(kept, received, send, keep):
+    for slot in range(send.shape[0]):
+        for out, source in ((send, 2 * slot + 1), (keep, 2 * slot)):
+            out[slot] = (kept[source].astype(F32) + received[source].astype(F32)).astype(BF)
+
+
+def line_parts_kernel(kept, received, keep, *sends):
+    rows = keep.shape[0]
+    for step, out in enumerate((keep, *sends)):
+        at = slice(step * rows, (step + 1) * rows)
+        out[...] = (kept[0, at].astype(F32) + received[0, at].astype(F32)).astype(out.dtype)
+
+
+def sum_kernel(*refs):
+    *parts, out = refs
+    total = parts[0][...].astype(F32)
+    for part in parts[1:]:
+        total = total + part[...].astype(F32)
     out[...] = total.astype(out.dtype)
 
 
-def finish_kernel(parts, qkv_out, proj_out):
-    width = proj_out.shape[0]
-    total = jnp.concatenate([parts[i].astype(F32) for i in range(parts.shape[0])], axis=1)
-    qkv_out[...] = total[:, : 3 * width]
-    proj_out[...] = jnp.transpose(total[:, 3 * width :])
-
-
-def call(kernel, outs, *args, name, flops=0, limit=32):
+def finish_kernel(*refs):
+    *parts, qkv_out, proj_out, shared = refs
+    lat = lax.axis_index("lat")
+    for step, part in enumerate(parts):
+        shared[lat ^ step] = part[...].astype(F32)
+    width = shared.shape[2]
+    for slot in range(shared.shape[0]):
+        at = slot * width
+        out, at = (qkv_out, at) if at < qkv_out.shape[1] else (proj_out, at - qkv_out.shape[1])
+        out[:, at : at + width] = shared[slot]
+
+
+def call(kernel, outs, *args, name, flops=0, limit=32, scratch=(), unread=()):
     vmem = pl.BlockSpec(memory_space=pltpu.VMEM)
+    anywhere = pl.BlockSpec(memory_space=pltpu.HBM)
     shapes = [jax.ShapeDtypeStruct(shape, dtype) for shape, dtype in outs]
     nbytes = sum(a.size * a.dtype.itemsize for a in (*args, *shapes))
     return pl.pallas_call(
         kernel,
         out_shape=shapes,
-        in_specs=[vmem] * len(args),
+        in_specs=[anywhere if i in unread else vmem for i in range(len(args))],
         out_specs=[vmem] * len(shapes),
+        scratch_shapes=scratch,
         compiler_params=pltpu.CompilerParams(vmem_limit_bytes=limit * 2**20),
         cost_estimate=pl.CostEstimate(flops=flops, bytes_accessed=nbytes, transcendentals=0),
         name=name,
@@ -342,10 +384,22 @@
     own_fields = fields.reshape(TOKENS, width)
     own_grads = cotangent.reshape(TOKENS, width)
     piece = [((LAT_ROWS, 2 * width), BF), ((LON_ROWS, 2 * width), BF), ((LON_ROWS, 2 * width), BF)]
-    lat_piece, lon_piece, diag_piece = call(pack_kernel, piece, own_fields, own_grads, name="pack")
+    lat_piece, lon_piece, diag_piece, own = call(
+        pack_kernel,
+        [*piece, ((WIN, 2 * width), F32)],
+        own_fields, own_grads,
+        name="pack", unread=(0, 1),
+        scratch=[pltpu.VMEM((TOKENS, width), BF)] * 2 + [pltpu.SemaphoreType.DMA((2,))],
+    )
     lat_in = lax.ppermute(lat_piece, both, lat_route)
     diag_in = lax.ppermute(diag_piece, both, diag_route)
     lon_in = lax.ppermute(lon_piece, both, lon_route)
+    qkv_here, proj_here = call(
+        weights_kernel,
+        [(qkv_weight.shape, BF), (proj_weight.shape, BF)],
+        lat_piece, qkv_weight, proj_weight,
+        name="weights", unread=(0, 1, 2), scratch=[pltpu.SemaphoreType.DMA((2,))],
+    )
 
     split = (lat_size, width // 2, 4 * width // lat_size)
     send_grad, windows, grads, normed_t, grads_t, d_projected, mixed = call(
@@ -359,30 +413,49 @@
             ((TOKENS, 3 * width), BF),
             ((TOKENS, width), BF),
         ],
-        own_fields, own_grads, lat_in, lon_in, diag_in, qkv_weight, proj_weight,
+        own, lat_in, lon_in, diag_in, qkv_here, proj_here,
         name="attention", flops=2 * 10**9,
+        scratch=[pltpu.VMEM((width, TOKENS), BF)] * 2 + [pltpu.VMEM((width // 2, TOKENS), BF)],
     )
     sibling = [(j, j ^ 1) for j in range(lon_size)]
     received = lax.ppermute(send_grad, "lon", sibling)
-    keep_grad, results, lat_back, lon_back, diag_back = call(
+    kept, results = call(
         output_kernel,
-        [(split, BF), ((TOKENS, 2 * width), BF), *piece],
-        windows, grads, normed_t, grads_t, d_projected, mixed, qkv_weight, proj_weight,
+        [(split, BF), ((TOKENS, 2 * width), BF)],
+        windows, grads, normed_t, grads_t, d_projected, mixed, qkv_here, proj_here,
         name="outputs", flops=10**9,
+    )
+
+    slots = lat_size
+    bits = lat_size.bit_length() - 1
+    for phase in range(bits):
+        slots //= 2
+        half = ((slots, *split[1:]), BF)
+        send, kept = call(halve_kernel, [half, half], kept, received, name=f"halve{slots}")
+        route = [
+            (i * lon_size + j, (i ^ (1 << (phase if j % 2 == 0 else bits - 1 - phase))) * lon_size + j)
+            for i in range(lat_size)
+            for j in range(lon_size)
+        ]
+        received = lax.ppermute(send, both, route)
+
+    rows = width // lon_size
+    share = ((rows, split[2]), BF)
+    parts = call(line_parts_kernel, [share] * (lon_size // 2), kept, received, name="line_parts")
+    arrived = [
+        lax.ppermute(parts[step], "lon", [(j, j ^ (2 * step)) for j in range(lon_size)])
+        for step in range(1, lon_size // 2)
+    ]
+    lat_back, lon_back, diag_back = call(
+        pack_back_kernel, piece, parts[-1], results, name="pack_back", unread=(0,)
     )
     lat_home = lax.ppermute(lat_back, both, back(lat_route))
     diag_home = lax.ppermute(diag_back, both, back(diag_route))
     lon_home = lax.ppermute(lon_back, both, back(lon_route))
-
-    (chip_sum,) = call(add_kernel, [(split, BF)], keep_grad, received, name="chip_sum")
-    plane = lax.all_to_all(chip_sum, "lat", 0, 0)
-    (plane_sum,) = call(sum_kernel, [(split[1:], BF)], plane, name="plane_sum")
-    rows = width // lon_size
-    by_chip = plane_sum.reshape(lon_size // 2, rows, split[2])
-    groups = [list(range(core, lon_size, 2)) for core in range(2)]
-    line = lax.all_to_all(by_chip, "lon", 0, 0, axis_index_groups=groups)
-    (line_sum,) = call(sum_kernel, [((rows, split[2]), BF)], line, name="line_sum")
-    shared = lax.all_to_all(jnp.broadcast_to(line_sum[None], (lat_size, rows, split[2])), "lat", 0, 0)
+    (line_sum,) = call(sum_kernel, [share], parts[0], *arrived, name="line_sum")
+    shared = [
+        lax.ppermute(line_sum, "lat", [(i, i ^ step) for i in range(lat_size)]) for step in range(1, lat_size)
+    ]
     field_out, d_fields = call(
         place_kernel,
         [((TOKENS, width), BF), ((TOKENS, width), BF)],
@@ -390,9 +463,12 @@
         name="place",
     )
     qkv_grad, proj_grad = call(
-        finish_kernel, [((rows, 3 * width), F32), ((width, rows), F32)], shared, name="finish"
-    )
-    return (field_out.reshape(fields.shape), d_fields.reshape(fields.shape), qkv_grad, proj_grad)
+        finish_kernel,
+        [((rows, 3 * width), F32), ((rows, width), F32)],
+        line_sum, *shared,
+        name="finish", scratch=[pltpu.VMEM((lat_size, *share[0]), F32)],
+    )
+    return (field_out.reshape(fields.shape), d_fields.reshape(fields.shape), qkv_grad, jnp.transpose(proj_grad))
 
 
 def solution(mesh):

time: 72.9 us -> 64.3 us (0.88)
  blocking collectives: 17.4 us -> 0 us
  waiting for transfers between devices: 18.7 us -> 28.5 us
  local copies, waits for them, and re-layouts: 5.87 us -> 4.36 us
    ppermute x0 -> x8, waiting for transfers between devices: none -> 25.4 us  [the longest x2 13 us: per_device(): received = lax.ppermute(send, both, route)]
    all_to_all x1 -> x0, blocking collectives: 17.4 us -> none  [per_device(): plane = lax.all_to_all(chip_sum, 'lat', 0, 0)]
    ppermute x0 -> x8, starting transfers between devices: none -> 10.1 us  [the longest x3 4.39 us: per_device(): lax.ppermute(parts[step], 'lon', [(j, j ^ 2 * step) for j in range(lon_si...]
    all_to_all x2 -> x0, starting transfers between devices: 8.67 us -> none  [the longest x1 5.27 us: per_device(): line = lax.all_to_all(by_chip, 'lon', 0, 0, axis_index_groups=groups)]
    all_to_all x2 -> x0, waiting for transfers between devices: 7.27 us -> none  [the longest x1 7.26 us: per_device(): line = lax.all_to_all(by_chip, 'lon', 0, 0, axis_index_groups=groups)]
    ppermute x1, waiting for transfers between devices: 3.85 us -> 0.01 us  [per_device(): lon_home = lax.ppermute(lon_back, both, back(lon_route))]
    ppermute x1, waiting for transfers between devices: 2.25 us -> 0.01 us  [per_device(): diag_home = lax.ppermute(diag_back, both, back(diag_route))]
    ppermute x1, starting transfers between devices: 1.8 us -> 0.01 us  [per_device(): diag_home = lax.ppermute(diag_back, both, back(diag_route))]
  transfers between devices with their start and end apart: 9 -> 15, of which waited for: 6 -> 9; matrix products, arithmetic and copies ran while one was open for 1% -> 0% of each run, Pallas kernels for 5% -> 4%
where the time goes in v2:
time: 64.3 us; the launch traced here: 64 us
  waiting for transfers between devices  28.5 us (44%)
  starting transfers between devices  18.7 us (29%)
  Pallas kernels  11.7 us (18%)
  local copies, waits for them, and re-layouts  4.36 us (7%)
  between operations  0.73 us (1%)
    ppermute x2, waiting for transfers between devices, per_device(): received = lax.ppermute(send, both, route)  13 us
    pallas_call x11, Pallas kernels, call(): pl.pallas_call(kernel, out_shape=shapes, in_specs=[anywhere if i in unrea...  11.7 us
    ppermute x3, waiting for transfers between devices, per_device(): lax.ppermute(line_sum, 'lat', [(i, i ^ step) for i in range(lat_size)])  6.54 us
    ppermute x3, waiting for transfers between devices, per_device(): lax.ppermute(parts[step], 'lon', [(j, j ^ 2 * step) for j in range(lon_si...  5.83 us
    ppermute x3, starting transfers between devices, per_device(): lax.ppermute(parts[step], 'lon', [(j, j ^ 2 * step) for j in range(lon_si...  4.39 us
    unnamed x8, local copies, waits for them, and re-layouts  4.36 us
    ppermute x1, starting transfers between devices, per_device(): lat_in = lax.ppermute(lat_piece, both, lat_route)  3.94 us
    ppermute x3, starting transfers between devices, per_device(): lax.ppermute(line_sum, 'lat', [(i, i ^ step) for i in range(lat_size)])  3.05 us
  transfers between devices with their start and end apart: 15, of which 9 were waited for; matrix products, arithmetic and copies ran while one was open for 0% of the time, Pallas kernels for 4%

profile of v2, /device:TPU:0, one launch (start us, length us, event | category | flops | bytes accessed | tf_op | source)
XLA Modules:
  0.0 64.0 jit_solution(9231016137632849506)
XLA Ops:
  0.6 0.0 copy-start.2
  0.6 1.0 %copy-done.2 = bf16[2,6,24,512]{3,2,1,0:T(8,128)(2,1)S(1)} copy-done((bf16[2,6,24,512]{3,2,1,0:T(8,128)(2,1)S(1)}, bf16[2,6,24,512]{3,2,1,0:T(8,128)(2,1)}, u32[]{:S(2)}) %copy-start.2) | copy-done | bytes 294936
  1.6 0.0 copy-start.3
  1.6 1.0 %copy-done.3 = bf16[2,6,24,512]{3,2,1,0:T(8,128)(2,1)S(1)} copy-done((bf16[2,6,24,512]{3,2,1,0:T(8,128)(2,1)S(1)}, bf16[2,6,24,512]{3,2,1,0:T(8,128)(2,1)}, u32[]{:S(2)}) %copy-start.3) | copy-done | bytes 294936
  2.6 1.0 %pack.1 = (bf16[108,1024]{1,0:T(8,128)(2,1)S(1)}, bf16[36,1024]{1,0:T(8,128)(2,1)S(1)}, bf16[36,1024]{1,0:T(8,128)(2,1)S(1)}, f32[144,1024]{1,0:T(8,128)S(1)}) custom-call(bf16[288,512]{1,0:T(8,128)(2,1)S(1)} %bitcast.5, bf16[288,512]{1,0:T(8,128)(2,1)S(1)} %bitcast.6), custom_call_target="tpu_custom_call" | custom-call | bytes 1548288 | tf_op jit(solution)/shard_map/pack/pallas_call | solution.py:350
  3.6 3.9 %collective-permute-start = (bf16[108,1024]{1,0:T(8,128)(2,1)S(1)}, bf16[108,1024]{1,0:T(8,128)(2,1)S(1)}, u32[]{:S(2)}, u32[]{:S(2)}) collective-permute-start(bf16[108,1024]{1,0:T(8,128)(2,1)S(1)} %get-tuple-element.35._), channel_id=1, source_target_pairs={{0,24},{1,9},{2,26},{3,11},{4,28},{5,13},{6,30},{7,15},{8,0},{9,17... | collective-permute-start | bytes 663560 | tf_op jit(solution)/shard_map/ppermute | solution.py:394
  7.5 1.8 %collective-permute-start.1 = (bf16[36,1024]{1,0:T(8,128)(2,1)S(1)}, bf16[36,1024]{1,0:T(8,128)(2,1)S(1)}, u32[]{:S(2)}, u32[]{:S(2)}) collective-permute-start(bf16[36,1024]{1,0:T(8,128)(2,1)S(1)} %get-tuple-element.36), channel_id=1, source_target_pairs={{0,7},{1,0},{2,1},{3,2},{4,3},{5,4},{6,5},{7,6},{8,15},{9,8},{10,9... | collective-permute-start | bytes 221192 | tf_op jit(solution)/shard_map/ppermute | solution.py:396
  9.4 0.9 %collective-permute-start.2 = (bf16[36,1024]{1,0:T(8,128)(2,1)S(1)}, bf16[36,1024]{1,0:T(8,128)(2,1)S(1)}, u32[]{:S(2)}, u32[]{:S(2)}) collective-permute-start(bf16[36,1024]{1,0:T(8,128)(2,1)S(1)} %get-tuple-element.37), channel_id=1, source_target_pairs={{0,15},{1,24},{2,9},{3,26},{4,11},{5,28},{6,13},{7,30},{8,23},{9,0... | collective-permute-start | bytes 221192 | tf_op jit(solution)/shard_map/ppermute | solution.py:395
  10.3 0.0 copy-start
  10.3 1.4 %copy-done = bf16[512,1536]{1,0:T(8,128)(2,1)S(1)} copy-done((bf16[512,1536]{1,0:T(8,128)(2,1)S(1)}, bf16[512,1536]{1,0:T(8,128)(2,1)}, u32[]{:S(2)}) %copy-start) | copy-done | bytes 1572888
  11.7 0.0 copy-start.1
  11.7 1.0 %copy-done.1 = bf16[512,512]{1,0:T(8,128)(2,1)S(1)} copy-done((bf16[512,512]{1,0:T(8,128)(2,1)S(1)}, bf16[512,512]{1,0:T(8,128)(2,1)}, u32[]{:S(2)}) %copy-start.1) | copy-done | bytes 524312
  12.7 0.2 weights.1
  12.9 0.0 collective-permute-done.1.lon_in
  12.9 1.9 %collective-permute-done.2.diag_in = bf16[36,1024]{1,0:T(8,128)(2,1)S(1)} collective-permute-done((bf16[36,1024]{1,0:T(8,128)(2,1)S(1)}, bf16[36,1024]{1,0:T(8,128)(2,1)S(1)}, u32[]{:S(2)}, u32[]{:S(2)}) %collective-permute-start.2) | collective-permute-done | bytes 73760 | tf_op jit(solution)/shard_map/ppermute | solution.py:395
  14.8 0.0 collective-permute-done.lat_in
  14.8 5.8 %attention.1 = (bf16[4,256,512]{2,1,0:T(8,128)(2,1)S(1)}, bf16[288,512]{1,0:T(8,128)(2,1)S(1)}, bf16[288,512]{1,0:T(8,128)(2,1)S(1)}, bf16[256,288]{1,0:T(8,128)...) custom-call(f32[144,1024]{1,0:T(8,128)S(1)} %get-tuple-element.34.own, ...), custom_call_target="tpu_custom_call" | custom-call | flops 2000000000 | bytes 6168576 | tf_op jit(solution)/shard_map/attention/pallas_call | solution.py:350
  20.6 0.1 collective-permute-start.3
  20.7 1.5 %outputs.1 = (bf16[4,256,512]{2,1,0:T(8,128)(2,1)S(1)}, bf16[288,1024]{1,0:T(8,128)(2,1)S(1)}) custom-call(bf16[288,512]{1,0:T(8,128)(2,1)S(1)} %get-tuple-element.40.windows, bf16[288,512]{1,0:T(8,128)(2,1)S(1)} %get-tuple-element.41.grads, bf16[256,288]{1,0:T(8,128)(2,1)S(1)} %get-tuple-element.42.normed_t, ...), custom_call_target="tpu_custom_call" | custom-call | flops 1000000000 | bytes 5799936 | tf_op jit(solution)/shard_map/outputs/pallas_call | solution.py:350
  22.1 1.2 %collective-permute-done.3.received = bf16[4,256,512]{2,1,0:T(8,128)(2,1)S(1)} collective-permute-done((bf16[4,256,512]{2,1,0:T(8,128)(2,1)S(1)}, bf16[4,256,512]{2,1,0:T(8,128)(2,1)S(1)}, u32[]{:S(2)}, u32[]{:S(2)}) %collective-permute-start.3) | collective-permute-done | bytes 1048608 | tf_op jit(solution)/shard_map/ppermute | solution.py:421
  23.3 0.2 halve2.1
  23.6 1.9 %collective-permute-start.4 = (bf16[2,256,512]{2,1,0:T(8,128)(2,1)S(1)}, bf16[2,256,512]{2,1,0:T(8,128)(2,1)S(1)}, u32[]{:S(2)}, u32[]{:S(2)}) collective-permute-start(bf16[2,256,512]{2,1,0:T(8,128)(2,1)S(1)} %get-tuple-element.50), channel_id=1, source_target_pairs={{0,8},{1,17},{2,10},{3,19},{4,12},{5,21},{6,14},{7,23},{8,0},{9,25... | collective-permute-start | bytes 1572872 | tf_op jit(solution)/shard_map/ppermute | solution.py:440
  25.5 7.3 %collective-permute-done.4.received = bf16[2,256,512]{2,1,0:T(8,128)(2,1)S(1)} collective-permute-done((bf16[2,256,512]{2,1,0:T(8,128)(2,1)S(1)}, bf16[2,256,512]{2,1,0:T(8,128)(2,1)S(1)}, u32[]{:S(2)}, u32[]{:S(2)}) %collective-permute-start.4) | collective-permute-done | bytes 524320 | tf_op jit(solution)/shard_map/ppermute | solution.py:440
  32.8 0.1 halve1.1
  32.9 0.7 %collective-permute-start.5 = (bf16[1,256,512]{2,1,0:T(8,128)(2,1)S(1)}, bf16[1,256,512]{2,1,0:T(8,128)(2,1)S(1)}, u32[]{:S(2)}, u32[]{:S(2)}) collective-permute-start(bf16[1,256,512]{2,1,0:T(8,128)(2,1)S(1)} %get-tuple-element.52), channel_id=1, source_target_pairs={{0,16},{1,9},{2,18},{3,11},{4,20},{5,13},{6,22},{7,15},{8,24},{9,1... | collective-permute-start | bytes 786440 | tf_op jit(solution)/shard_map/ppermute | solution.py:440
  33.7 5.7 %collective-permute-done.5.received = bf16[1,256,512]{2,1,0:T(8,128)(2,1)S(1)} collective-permute-done((bf16[1,256,512]{2,1,0:T(8,128)(2,1)S(1)}, bf16[1,256,512]{2,1,0:T(8,128)(2,1)S(1)}, u32[]{:S(2)}, u32[]{:S(2)}) %collective-permute-start.5) | collective-permute-done | bytes 262176 | tf_op jit(solution)/shard_map/ppermute | solution.py:440
  39.4 0.1 line_parts.1
  39.4 0.3 pack_back.1
  39.7 1.9 %collective-permute-start.6 = (bf16[108,1024]{1,0:T(8,128)(2,1)S(1)}, bf16[108,1024]{1,0:T(8,128)(2,1)S(1)}, u32[]{:S(2)}, u32[]{:S(2)}) collective-permute-start(bf16[108,1024]{1,0:T(8,128)(2,1)S(1)} %get-tuple-element.54), channel_id=1, source_target_pairs={{24,0},{9,1},{26,2},{11,3},{28,4},{13,5},{30,6},{15,7},{0,8},{17,9... | collective-permute-start | bytes 663560 | tf_op jit(solution)/shard_map/ppermute | solution.py:452
  41.6 1.6 %collective-permute-start.9 = (bf16[64,512]{1,0:T(8,128)(2,1)S(1)}, bf16[64,512]{1,0:T(8,128)(2,1)S(1)}, u32[]{:S(2)}, u32[]{:S(2)}) collective-permute-start(bf16[64,512]{1,0:T(8,128)(2,1)S(1)} %get-tuple-element.60), channel_id=1, source_target_pairs={{0,2},{1,3},{2,0},{3,1},{4,6},{5,7},{6,4},{7,5},{8,10},{9,11},{10,... | collective-permute-start | bytes 196616 | tf_op jit(solution)/shard_map/ppermute | solution.py:446
  43.2 2.6 %collective-permute-start.10 = (bf16[64,512]{1,0:T(8,128)(2,1)S(1)}, bf16[64,512]{1,0:T(8,128)(2,1)S(1)}, u32[]{:S(2)}, u32[]{:S(2)}) collective-permute-start(bf16[64,512]{1,0:T(8,128)(2,1)S(1)} %get-tuple-element.61), channel_id=1, source_target_pairs={{0,4},{1,5},{2,6},{3,7},{4,0},{5,1},{6,2},{7,3},{8,12},{9,13},{10,... | collective-permute-start | bytes 196616 | tf_op jit(solution)/shard_map/ppermute | solution.py:446
  45.8 0.2 collective-permute-start.11
  46.0 0.0 collective-permute-done.9.refs_1_
  46.0 3.8 %collective-permute-done.10.refs_2_ = bf16[64,512]{1,0:T(8,128)(2,1)S(1)} collective-permute-done((bf16[64,512]{1,0:T(8,128)(2,1)S(1)}, bf16[64,512]{1,0:T(8,128)(2,1)S(1)}, u32[]{:S(2)}, u32[]{:S(2)}) %collective-permute-start.10) | collective-permute-done | bytes 65568 | tf_op jit(solution)/shard_map/ppermute | solution.py:446
  49.8 2.1 %collective-permute-done.11.refs_3_ = bf16[64,512]{1,0:T(8,128)(2,1)S(1)} collective-permute-done((bf16[64,512]{1,0:T(8,128)(2,1)S(1)}, bf16[64,512]{1,0:T(8,128)(2,1)S(1)}, u32[]{:S(2)}, u32[]{:S(2)}) %collective-permute-start.11) | collective-permute-done | bytes 65568 | tf_op jit(solution)/shard_map/ppermute | solution.py:446
  51.9 1.5 %collective-permute-start.14 = (bf16[64,512]{1,0:T(8,128)(2,1)S(1)}, bf16[64,512]{1,0:T(8,128)(2,1)S(1)}, u32[]{:S(2)}, u32[]{:S(2)}) collective-permute-start(bf16[64,512]{1,0:T(8,128)(2,1)S(1)} %line_sum.1.refs_0_), channel_id=1, source_target_pairs={{0,24},{8,16},{16,8},{24,0},{1,25},{9,17},{17,9},{25,1},{2,26},{10... | collective-permute-start | bytes 196616 | tf_op jit(solution)/shard_map/ppermute | solution.py:457
  53.4 0.0 collective-permute-start.7
  53.4 0.0 collective-permute-start.8
  53.4 0.9 %collective-permute-start.13 = (bf16[64,512]{1,0:T(8,128)(2,1)S(1)}, bf16[64,512]{1,0:T(8,128)(2,1)S(1)}, u32[]{:S(2)}, u32[]{:S(2)}) collective-permute-start(bf16[64,512]{1,0:T(8,128)(2,1)S(1)} %line_sum.1.refs_0_), channel_id=1, source_target_pairs={{0,16},{8,24},{16,0},{24,8},{1,17},{9,25},{17,1},{25,9},{2,18},{10... | collective-permute-start | bytes 196616 | tf_op jit(solution)/shard_map/ppermute | solution.py:457
  54.4 2.9 %collective-permute-done.14.refs_3_ = bf16[64,512]{1,0:T(8,128)(2,1)S(1)} collective-permute-done((bf16[64,512]{1,0:T(8,128)(2,1)S(1)}, bf16[64,512]{1,0:T(8,128)(2,1)S(1)}, u32[]{:S(2)}, u32[]{:S(2)}) %collective-permute-start.14) | collective-permute-done | bytes 65568 | tf_op jit(solution)/shard_map/ppermute | solution.py:457
  57.2 0.6 collective-permute-start.12
  57.8 1.4 %collective-permute-done.13.refs_2_ = bf16[64,512]{1,0:T(8,128)(2,1)S(1)} collective-permute-done((bf16[64,512]{1,0:T(8,128)(2,1)S(1)}, bf16[64,512]{1,0:T(8,128)(2,1)S(1)}, u32[]{:S(2)}, u32[]{:S(2)}) %collective-permute-start.13) | collective-permute-done | bytes 65568 | tf_op jit(solution)/shard_map/ppermute | solution.py:457
  59.2 2.3 %collective-permute-done.12.refs_1_ = bf16[64,512]{1,0:T(8,128)(2,1)S(1)} collective-permute-done((bf16[64,512]{1,0:T(8,128)(2,1)S(1)}, bf16[64,512]{1,0:T(8,128)(2,1)S(1)}, u32[]{:S(2)}, u32[]{:S(2)}) %collective-permute-start.12) | collective-permute-done | bytes 65568 | tf_op jit(solution)/shard_map/ppermute | solution.py:457
  61.5 0.9 %finish.1 = (f32[64,1536]{1,0:T(8,128)}, f32[64,512]{1,0:T(8,128)}) custom-call(bf16[64,512]{1,0:T(8,128)(2,1)S(1)} %line_sum.1.refs_0_, bf16[64,512]{1,0:T(8,128)(2,1)S(1)} %collective-permute-done.12.refs_1_, bf16[64,512]{1,0:T(8,128)(2,1)S(1)} %collective-permute-done.13.refs_2_, bf16[64,512]{1,0:T(8,128)(2,1)S(1)} %collective-permute-done.14.refs_3_), custom_call_target="tpu_custom_call" | custom-call | bytes 786432 | tf_op jit(solution)/shard_map/finish/pallas_call | solution.py:350
  62.4 0.0 collective-permute-done.7.lon_in
  62.4 0.0 collective-permute-done.8.diag_in
  62.4 0.0 collective-permute-done.6.lat_in
  62.4 1.6 %place.1 = (bf16[288,512]{1,0:T(8,128)(2,1)}, bf16[288,512]{1,0:T(8,128)(2,1)}) custom-call(bf16[288,1024]{1,0:T(8,128)(2,1)S(1)} %get-tuple-element.46.results, bf16[108,1024]{1,0:T(8,128)(2,1)S(1)} %collective-permute-done.6.lat_in, bf16[36,1024]{1,0:T(8,128)(2,1)S(1)} %collective-permute-done.7.lon_in, bf16[36,1024]{1,0:T(8,128)(2,1)S(1)} %collective-permute-done.8.diag_in), custom_call_target="tpu_custom_call" | custom-call | bytes 1548288 | tf_op jit(solution)/shard_map/place/pallas_call | solution.py:350
  (1 shorter events, 0.0 us)
Async XLA Ops:
  0.6 1.0 %copy-start.2 = (bf16[2,6,24,512]{3,2,1,0:T(8,128)(2,1)S(1)}, bf16[2,6,24,512]{3,2,1,0:T(8,128)(2,1)}, u32[]{:S(2)}) copy-start(bf16[2,6,24,512]{3,2,1,0:T(8,128)(2,1)} %param.4) | copy-start | bytes 884740
  1.6 1.0 %copy-start.3 = (bf16[2,6,24,512]{3,2,1,0:T(8,128)(2,1)S(1)}, bf16[2,6,24,512]{3,2,1,0:T(8,128)(2,1)}, u32[]{:S(2)}) copy-start(bf16[2,6,24,512]{3,2,1,0:T(8,128)(2,1)} %param.5) | copy-start | bytes 884740
  3.6 11.2 %collective-permute-start = (bf16[108,1024]{1,0:T(8,128)(2,1)S(1)}, bf16[108,1024]{1,0:T(8,128)(2,1)S(1)}, u32[]{:S(2)}, u32[]{:S(2)}) collective-permute-start(bf16[108,1024]{1,0:T(8,128)(2,1)S(1)} %get-tuple-element.35._), channel_id=1, source_target_pairs={{0,24},{1,9},{2,26},{3,11},{4,28},{5,13},{6,30},{7,15},{8,0},{9,17... | collective-permute-start | bytes 663560 | tf_op jit(solution)/shard_map/ppermute | solution.py:394
  7.5 5.4 %collective-permute-start.1 = (bf16[36,1024]{1,0:T(8,128)(2,1)S(1)}, bf16[36,1024]{1,0:T(8,128)(2,1)S(1)}, u32[]{:S(2)}, u32[]{:S(2)}) collective-permute-start(bf16[36,1024]{1,0:T(8,128)(2,1)S(1)} %get-tuple-element.36), channel_id=1, source_target_pairs={{0,7},{1,0},{2,1},{3,2},{4,3},{5,4},{6,5},{7,6},{8,15},{9,8},{10,9... | collective-permute-start | bytes 221192 | tf_op jit(solution)/shard_map/ppermute | solution.py:396
  9.4 5.4 %collective-permute-start.2 = (bf16[36,1024]{1,0:T(8,128)(2,1)S(1)}, bf16[36,1024]{1,0:T(8,128)(2,1)S(1)}, u32[]{:S(2)}, u32[]{:S(2)}) collective-permute-start(bf16[36,1024]{1,0:T(8,128)(2,1)S(1)} %get-tuple-element.37), channel_id=1, source_target_pairs={{0,15},{1,24},{2,9},{3,26},{4,11},{5,28},{6,13},{7,30},{8,23},{9,0... | collective-permute-start | bytes 221192 | tf_op jit(solution)/shard_map/ppermute | solution.py:395
  10.3 1.4 %copy-start = (bf16[512,1536]{1,0:T(8,128)(2,1)S(1)}, bf16[512,1536]{1,0:T(8,128)(2,1)}, u32[]{:S(2)}) copy-start(bf16[512,1536]{1,0:T(8,128)(2,1)} %qkv_hbm.1) | copy-start | bytes 4718596
  11.7 1.0 %copy-start.1 = (bf16[512,512]{1,0:T(8,128)(2,1)S(1)}, bf16[512,512]{1,0:T(8,128)(2,1)}, u32[]{:S(2)}) copy-start(bf16[512,512]{1,0:T(8,128)(2,1)} %proj_hbm.1) | copy-start | bytes 1572868
  20.6 2.7 %collective-permute-start.3 = (bf16[4,256,512]{2,1,0:T(8,128)(2,1)S(1)}, bf16[4,256,512]{2,1,0:T(8,128)(2,1)S(1)}, u32[]{:S(2)}, u32[]{:S(2)}) collective-permute-start(bf16[4,256,512]{2,1,0:T(8,128)(2,1)S(1)} %get-tuple-element.48), channel_id=1, source_target_pairs={{0,1},{1,0},{2,3},{3,2},{4,5},{5,4},{6,7},{7,6},{8,9},{9,8},{10,11... | collective-permute-start | bytes 3145736 | tf_op jit(solution)/shard_map/ppermute | solution.py:421
  23.6 9.2 %collective-permute-start.4 = (bf16[2,256,512]{2,1,0:T(8,128)(2,1)S(1)}, bf16[2,256,512]{2,1,0:T(8,128)(2,1)S(1)}, u32[]{:S(2)}, u32[]{:S(2)}) collective-permute-start(bf16[2,256,512]{2,1,0:T(8,128)(2,1)S(1)} %get-tuple-element.50), channel_id=1, source_target_pairs={{0,8},{1,17},{2,10},{3,19},{4,12},{5,21},{6,14},{7,23},{8,0},{9,25... | collective-permute-start | bytes 1572872 | tf_op jit(solution)/shard_map/ppermute | solution.py:440
  32.9 6.4 %collective-permute-start.5 = (bf16[1,256,512]{2,1,0:T(8,128)(2,1)S(1)}, bf16[1,256,512]{2,1,0:T(8,128)(2,1)S(1)}, u32[]{:S(2)}, u32[]{:S(2)}) collective-permute-start(bf16[1,256,512]{2,1,0:T(8,128)(2,1)S(1)} %get-tuple-element.52), channel_id=1, source_target_pairs={{0,16},{1,9},{2,18},{3,11},{4,20},{5,13},{6,22},{7,15},{8,24},{9,1... | collective-permute-start | bytes 786440 | tf_op jit(solution)/shard_map/ppermute | solution.py:440
  39.7 22.6 %collective-permute-start.6 = (bf16[108,1024]{1,0:T(8,128)(2,1)S(1)}, bf16[108,1024]{1,0:T(8,128)(2,1)S(1)}, u32[]{:S(2)}, u32[]{:S(2)}) collective-permute-start(bf16[108,1024]{1,0:T(8,128)(2,1)S(1)} %get-tuple-element.54), channel_id=1, source_target_pairs={{24,0},{9,1},{26,2},{11,3},{28,4},{13,5},{30,6},{15,7},{0,8},{17,9... | collective-permute-start | bytes 663560 | tf_op jit(solution)/shard_map/ppermute | solution.py:452
  41.6 4.4 %collective-permute-start.9 = (bf16[64,512]{1,0:T(8,128)(2,1)S(1)}, bf16[64,512]{1,0:T(8,128)(2,1)S(1)}, u32[]{:S(2)}, u32[]{:S(2)}) collective-permute-start(bf16[64,512]{1,0:T(8,128)(2,1)S(1)} %get-tuple-element.60), channel_id=1, source_target_pairs={{0,2},{1,3},{2,0},{3,1},{4,6},{5,7},{6,4},{7,5},{8,10},{9,11},{10,... | collective-permute-start | bytes 196616 | tf_op jit(solution)/shard_map/ppermute | solution.py:446
  43.2 6.6 %collective-permute-start.10 = (bf16[64,512]{1,0:T(8,128)(2,1)S(1)}, bf16[64,512]{1,0:T(8,128)(2,1)S(1)}, u32[]{:S(2)}, u32[]{:S(2)}) collective-permute-start(bf16[64,512]{1,0:T(8,128)(2,1)S(1)} %get-tuple-element.61), channel_id=1, source_target_pairs={{0,4},{1,5},{2,6},{3,7},{4,0},{5,1},{6,2},{7,3},{8,12},{9,13},{10,... | collective-permute-start | bytes 196616 | tf_op jit(solution)/shard_map/ppermute | solution.py:446
  45.8 6.1 %collective-permute-start.11 = (bf16[64,512]{1,0:T(8,128)(2,1)S(1)}, bf16[64,512]{1,0:T(8,128)(2,1)S(1)}, u32[]{:S(2)}, u32[]{:S(2)}) collective-permute-start(bf16[64,512]{1,0:T(8,128)(2,1)S(1)} %get-tuple-element.53._), channel_id=1, source_target_pairs={{0,6},{1,7},{2,4},{3,5},{4,2},{5,3},{6,0},{7,1},{8,14},{9,15},{10,... | collective-permute-start | bytes 196616 | tf_op jit(solution)/shard_map/ppermute | solution.py:446
  51.9 5.3 %collective-permute-start.14 = (bf16[64,512]{1,0:T(8,128)(2,1)S(1)}, bf16[64,512]{1,0:T(8,128)(2,1)S(1)}, u32[]{:S(2)}, u32[]{:S(2)}) collective-permute-start(bf16[64,512]{1,0:T(8,128)(2,1)S(1)} %line_sum.1.refs_0_), channel_id=1, source_target_pairs={{0,24},{8,16},{16,8},{24,0},{1,25},{9,17},{17,9},{25,1},{2,26},{10... | collective-permute-start | bytes 196616 | tf_op jit(solution)/shard_map/ppermute | solution.py:457
  53.4 8.9 %collective-permute-start.7 = (bf16[36,1024]{1,0:T(8,128)(2,1)S(1)}, bf16[36,1024]{1,0:T(8,128)(2,1)S(1)}, u32[]{:S(2)}, u32[]{:S(2)}) collective-permute-start(bf16[36,1024]{1,0:T(8,128)(2,1)S(1)} %get-tuple-element.55), channel_id=1, source_target_pairs={{7,0},{0,1},{1,2},{2,3},{3,4},{4,5},{5,6},{6,7},{15,8},{8,9},{9,10... | collective-permute-start | bytes 221192 | tf_op jit(solution)/shard_map/ppermute | solution.py:454
  53.4 8.9 %collective-permute-start.8 = (bf16[36,1024]{1,0:T(8,128)(2,1)S(1)}, bf16[36,1024]{1,0:T(8,128)(2,1)S(1)}, u32[]{:S(2)}, u32[]{:S(2)}) collective-permute-start(bf16[36,1024]{1,0:T(8,128)(2,1)S(1)} %get-tuple-element.56), channel_id=1, source_target_pairs={{15,0},{24,1},{9,2},{26,3},{11,4},{28,5},{13,6},{30,7},{23,8},{0,9... | collective-permute-start | bytes 221192 | tf_op jit(solution)/shard_map/ppermute | solution.py:453
  53.4 5.8 %collective-permute-start.13 = (bf16[64,512]{1,0:T(8,128)(2,1)S(1)}, bf16[64,512]{1,0:T(8,128)(2,1)S(1)}, u32[]{:S(2)}, u32[]{:S(2)}) collective-permute-start(bf16[64,512]{1,0:T(8,128)(2,1)S(1)} %line_sum.1.refs_0_), channel_id=1, source_target_pairs={{0,16},{8,24},{16,0},{24,8},{1,17},{9,25},{17,1},{25,9},{2,18},{10... | collective-permute-start | bytes 196616 | tf_op jit(solution)/shard_map/ppermute | solution.py:457
  57.2 4.3 %collective-permute-start.12 = (bf16[64,512]{1,0:T(8,128)(2,1)S(1)}, bf16[64,512]{1,0:T(8,128)(2,1)S(1)}, u32[]{:S(2)}, u32[]{:S(2)}) collective-permute-start(bf16[64,512]{1,0:T(8,128)(2,1)S(1)} %line_sum.1.refs_0_), channel_id=1, source_target_pairs={{0,8},{8,0},{16,24},{24,16},{1,9},{9,1},{17,25},{25,17},{2,10},{10... | collective-permute-start | bytes 196616 | tf_op jit(solution)/shard_map/ppermute | solution.py:457

commit v3 on v2

v3 whole, which is shorter than its diff:
```python
import functools

import jax
import jax.numpy as jnp
from jax import lax
from jax.experimental import pallas as pl
from jax.experimental.pallas import tpu as pltpu
from jax.sharding import PartitionSpec as P

HEADS = 8
WIN_LAT = 6
WIN_LON = 12
LEVELS = 2
COLS = 24
HALF_LAT = WIN_LAT // 2
HALF_LON = WIN_LON // 2
HALF = LEVELS * HALF_LAT * WIN_LON
WIN = 2 * HALF
TOKENS = 2 * WIN
QUARTER = HALF // 2
LANES = 128

epsilon = 1e-05
LONG = 5 * 10**10
LOAD = 5 * 10**9
BF = jnp.bfloat16
F32 = jnp.float32


def dot(a, b, dims):
    return lax.dot_general(a, b, (dims, ((), ())), preferred_element_type=F32)


NN = ((1,), (0,))
NT = ((1,), (1,))
TN = ((0,), (0,))


def div(x, by):
    return (x * ((65536 + by - 1) // by)) >> 16


def own_token(level, row, col):
    return level * (WIN_LAT * COLS) + row * COLS + col


def inner_token(v, first):
    level = div(v, HALF_LAT * WIN_LON)
    rest = v - level * (HALF_LAT * WIN_LON)
    row = div(rest, WIN_LON)
    return own_token(level, first + row, HALF_LON + rest - row * WIN_LON)


def half_token(v, first, col):
    level = div(v, HALF_LAT * HALF_LON)
    rest = v - level * (HALF_LAT * HALF_LON)
    row = div(rest, HALF_LON)
    return jnp.where(v < QUARTER, own_token(level, first + row, col + rest - row * HALF_LON), -1)


def sources():
    even = lax.rem(lax.axis_index("lon"), 2) == 0
    sent = jnp.where(even, 0, HALF_LAT)
    kept = HALF_LAT - sent
    outer = HALF_LON + WIN_LON
    return (
        (lambda v: inner_token(v, sent), HALF),
        (lambda v: half_token(v, sent, outer), QUARTER),
        (lambda v: half_token(v, sent, 0), QUARTER),
        (lambda v: half_token(v, kept, 0), QUARTER),
        (lambda v: inner_token(v, kept), HALF),
        (lambda v: half_token(v, kept, outer), HALF),
    )


def picks(source, rows, columns):
    index = source(lax.broadcasted_iota(jnp.int32, (rows, 1), 0))
    return (index == lax.broadcasted_iota(jnp.int32, (rows, columns), 1)).astype(BF)


def puts(source, rows, columns):
    index = source(lax.broadcasted_iota(jnp.int32, (1, columns), 1))
    return (lax.broadcasted_iota(jnp.int32, (rows, columns), 0) == index).astype(BF)


def first_rows(v):
    return v


def last_rows(v):
    return v - QUARTER


def order_kernel(*outs):
    for out, (source, rows) in zip(outs, sources()):
        out[...] = picks(source, rows, TOKENS)


def pack_kernel(fields, cotangent, *refs):
    count = len(refs) // 2
    width = fields.shape[1]
    for pick, out in zip(refs[:count], refs[count:]):
        out[:, :width] = dot(pick[...], fields[...], NN).astype(out.dtype)
        out[:, width:] = dot(pick[...], cotangent[...], NN).astype(out.dtype)


def normalise(x):
    mean = jnp.mean(x, -1, keepdims=True)
    centred = x - mean
    variance = jnp.mean(centred * centred, -1, keepdims=True)
    inv_std = lax.rsqrt(variance + epsilon)
    return centred * inv_std, inv_std


def swap_bits(index, size, core):
    bits = size.bit_length() - 1
    turned = sum(((index >> b) & 1) << (bits - 1 - b) for b in range(bits))
    return jnp.where(core == 0, index, turned)


def shares(transposed, out, lon, core_of, lon_size):
    rows = transposed.shape[0] // lon_size
    chip = lon >> 1
    for step in range(lon_size // 2):
        start = pl.multiple_of(((chip ^ step) * 2 + core_of) * rows, rows)
        out[step * rows : (step + 1) * rows, :] = transposed[pl.ds(start, rows), :]


def transpose_bf16(block):
    return jnp.transpose(block.astype(F32)).astype(BF)


def put_split(out, lanes_from, block, lat, core, so_far=None):
    size, _, width = out.shape
    for at in range(0, block.shape[1], width):
        slot = swap_bits(lat ^ ((lanes_from + at) // width), size, core)
        part = block[:, at : at + width]
        if so_far is not None:
            part = part + so_far[slot]
        out[slot] = part.astype(out.dtype)


def inner_kernel(own, lat_in, qkv_weight, proj_weight, send_grad, *refs):
    both = jnp.concatenate([own[...], lat_in[...].astype(F32)], axis=0)
    one_window(both, qkv_weight, proj_weight, None, send_grad, *refs)


def outer_kernel(own, lat_in, lon_in, diag_in, qkv_weight, proj_weight, grad_so_far, send_grad, *refs):
    last = picks(last_rows, HALF, QUARTER)
    both = jnp.concatenate(
        [
            own[...] + dot(last, lon_in[...], NN),
            dot(picks(first_rows, HALF, QUARTER), lat_in[...], NN) + dot(last, diag_in[...], NN),
        ],
        axis=0,
    )
    one_window(both, qkv_weight, proj_weight, grad_so_far, send_grad, *refs)


def one_window(
    both, qkv_weight, proj_weight, grad_so_far,
    send_grad, windows_out, grads_out, normed_t_out, grads_t_out, d_projected, mixed, normed_t, grads_t, send_rows,
):
    width = both.shape[1] // 2
    lat, lon = lax.axis_index("lat"), lax.axis_index("lon")
    lat_size, lon_size = lax.axis_size("lat"), lax.axis_size("lon")
    core = lax.rem(lon, 2)
    even = core == 0
    blocks = both[:, :width], both[:, width:]
    x = blocks[0]
    windows_out[...] = x.astype(BF)
    grads = blocks[1].astype(BF)
    grads_out[...] = grads
    normed, _ = normalise(x)
    normed_b = normed.astype(BF)
    projected = dot(normed_b, qkv_weight[...], NN).astype(BF)
    d_mixed = dot(grads, proj_weight[...], NT).astype(BF)

    head_size = width // HEADS
    factor = head_size ** (-0.5)
    apart = jnp.where(even, lat == lat_size - 1, lat == 0).astype(jnp.int32)
    half_b = (lax.broadcasted_iota(jnp.int32, (WIN, 2 * WIN), 0) >= HALF).astype(jnp.int32)
    at_a = lax.broadcasted_iota(jnp.int32, (WIN, 2 * WIN), 1)
    at_a = jnp.where(at_a >= WIN, at_a - WIN, at_a)
    half_a = (at_a >= HALF).astype(jnp.int32)
    allowed = ((half_a != half_b).astype(jnp.int32) * apart) == 0
    first_head = lax.broadcasted_iota(jnp.int32, (WIN, LANES), 1) < head_size
    zero = jnp.zeros((WIN, LANES), BF)

    def split_heads(block):
        return jnp.concatenate([jnp.where(first_head, block, zero), jnp.where(first_head, zero, block)], axis=0)

    def join_heads(block):
        return jnp.where(first_head, block[:WIN], block[WIN:]).astype(BF)

    for pair in range(width // LANES):
        at = pair * LANES
        q = projected[:, at : at + LANES]
        k = projected[:, width + at : width + at + LANES]
        v = projected[:, 2 * width + at : 2 * width + at + LANES]
        dm = d_mixed[:, at : at + LANES]
        q2, dm2 = split_heads(q), split_heads(dm)
        scores = dot(k, q2, NT) * factor
        scores = jnp.where(allowed, scores, -1e30)
        exponent = jnp.exp(scores - jnp.max(scores, 0, keepdims=True))
        probs = exponent * (1.0 / jnp.sum(exponent, 0, keepdims=True))
        probs_b = probs.astype(BF)
        mixed[:, at : at + LANES] = join_heads(dot(probs_b, v, TN))
        d_probs = dot(v, dm2, NT)
        d_projected[:, 2 * width + at : 2 * width + at + LANES] = dot(probs_b, dm2, NN).astype(BF)
        d_scores = probs * (d_probs - jnp.sum(d_probs * probs, 0, keepdims=True)) * factor
        d_scores = d_scores.astype(BF)
        d_projected[:, at : at + LANES] = join_heads(dot(d_scores, k, TN))
        d_projected[:, width + at : width + at + LANES] = dot(d_scores, q2, NN).astype(BF)

    normed_t[...] = transpose_bf16(normed)
    grads_t[...] = transpose_bf16(grads)
    shares(normed_t, send_rows, lon, 1 - core, lon_size)
    put_split(send_grad, 0, dot(send_rows[...], d_projected[...], NN), lat, 1 - core, grad_so_far)
    shares(grads_t, send_rows, lon, 1 - core, lon_size)
    put_split(send_grad, 3 * width, dot(send_rows[...], mixed[...], NN), lat, 1 - core, grad_so_far)
    shares(normed_t, normed_t_out, lon, core, lon_size)
    shares(grads_t, grads_t_out, lon, core, lon_size)


def output_kernel(*refs):
    (*windows, qkv_weight, proj_weight, keep_grad, inner_results, outer_results) = refs
    per_window = windows[:6], windows[6:]
    lat, core = lax.axis_index("lat"), lax.rem(lax.axis_index("lon"), 2)
    width = proj_weight.shape[0]
    qkv_grad = sum(dot(w[2][...], w[4][...], NN) for w in per_window)
    proj_grad = sum(dot(w[3][...], w[5][...], NN) for w in per_window)
    put_split(keep_grad, 0, qkv_grad, lat, core)
    put_split(keep_grad, 3 * width, proj_grad, lat, core)
    x, grads, d_projected, mixed = (
        jnp.concatenate([w[i][...] for w in per_window], axis=0) for i in (0, 1, 4, 5)
    )
    x = x.astype(F32)
    normed, inv_std = normalise(x)
    output = (x + dot(mixed, proj_weight[...], NN)).astype(BF)
    d_normed = dot(d_projected, qkv_weight[...], NT)
    d_inputs = grads.astype(F32) + inv_std * (
        d_normed
        - jnp.mean(d_normed, -1, keepdims=True)
        - normed * jnp.mean(d_normed * normed, -1, keepdims=True)
    )
    d_inputs = d_inputs.astype(BF)
    for at, out in ((0, inner_results), (WIN, outer_results)):
        out[:, :width] = output[at : at + WIN]
        out[:, width:] = d_inputs[at : at + WIN]


def pack_back_kernel(_, inner_results, outer_results, lat_out, lon_out, diag_out):
    inner_y = inner_results[...].astype(F32)[HALF:]
    outer = outer_results[...].astype(F32)
    outer_x, outer_y = outer[:HALF].astype(BF), outer[HALF:].astype(BF)
    first, last = puts(first_rows, QUARTER, HALF), puts(last_rows, QUARTER, HALF)
    lat_out[...] = jnp.concatenate([inner_y, dot(first, outer_y, NN)], axis=0).astype(BF)
    lon_out[...] = dot(last, outer_x, NN).astype(BF)
    diag_out[...] = dot(last, outer_y, NN).astype(BF)


def place_kernel(inner_results, outer_results, lat_in, lon_in, diag_in, field_out, d_fields, placed):
    placed[...] = jnp.zeros_like(placed)
    width = field_out.shape[1]
    inner_lat, outer_lat, lon, diag, inner_own, outer_own = (source for source, _ in sources())

    def lat(v):
        return jnp.where(v < HALF, inner_lat(v), outer_lat(v - HALF))

    def only_first(source):
        return lambda v: jnp.where(v < HALF, source(v), -1)

    moves = (
        (puts(only_first(inner_own), TOKENS, WIN), inner_results),
        (puts(only_first(outer_own), TOKENS, WIN), outer_results),
        (puts(lat, TOKENS, HALF + QUARTER), lat_in),
        (puts(lon, TOKENS, QUARTER), lon_in),
        (puts(diag, TOKENS, QUARTER), diag_in),
    )
    for index, out in ((0, field_out), (1, d_fields)):
        lanes = slice(index * width, (index + 1) * width)
        out[...] = sum(dot(put, source[:, lanes], NN) for put, source in moves).astype(BF)


def halve_kernel(kept, received, send, keep):
    for slot in range(send.shape[0]):
        for out, source in ((send, 2 * slot + 1), (keep, 2 * slot)):
            out[slot] = (kept[source].astype(F32) + received[source].astype(F32)).astype(BF)


def line_parts_kernel(kept, received, keep, *sends):
    rows = keep.shape[0]
    for step, out in enumerate((keep, *sends)):
        at = slice(step * rows, (step + 1) * rows)
        out[...] = (kept[0, at].astype(F32) + received[0, at].astype(F32)).astype(out.dtype)


def sum_kernel(*refs):
    *parts, out = refs
    total = parts[0][...].astype(F32)
    for part in parts[1:]:
        total = total + part[...].astype(F32)
    out[...] = total.astype(out.dtype)


def finish_kernel(_, *refs):
    *parts, qkv_out, proj_out, shared = refs
    lat = lax.axis_index("lat")
    for step, part in enumerate(parts):
        shared[lat ^ step] = part[...].astype(F32)
    width = shared.shape[2]
    for slot in range(shared.shape[0]):
        at = slot * width
        out, at = (qkv_out, at) if at < qkv_out.shape[1] else (proj_out, at - qkv_out.shape[1])
        out[:, at : at + width] = shared[slot]


def call(kernel, outs, *args, name, flops=0, limit=32, scratch=(), unread=()):
    vmem = pl.BlockSpec(memory_space=pltpu.VMEM)
    anywhere = pl.BlockSpec(memory_space=pl.ANY)
    shapes = [jax.ShapeDtypeStruct(shape, dtype) for shape, dtype in outs]
    nbytes = sum(a.size * a.dtype.itemsize for a in (*args, *shapes))
    return pl.pallas_call(
        kernel,
        out_shape=shapes,
        in_specs=[anywhere if i in unread else vmem for i in range(len(args))],
        out_specs=[vmem] * len(shapes),
        scratch_shapes=scratch,
        compiler_params=pltpu.CompilerParams(vmem_limit_bytes=limit * 2**20),
        cost_estimate=pl.CostEstimate(flops=flops, bytes_accessed=nbytes, transcendentals=0),
        name=name,
    )(*args)


def routes(lat_size, lon_size):
    lat, lon, diag = [], [], []
    for i in range(lat_size):
        for j in range(lon_size):
            step = -1 if j % 2 == 0 else 1
            before = (j - 1) % lon_size
            me = i * lon_size + j
            lat.append((me, ((i + step) % lat_size) * lon_size + j))
            lon.append((me, i * lon_size + before))
            diag.append((me, ((i - step) % lat_size) * lon_size + before))
    return lat, lon, diag


def per_device(fields, cotangent, qkv_weight, proj_weight):
    levels, row_count, col_count, width = fields.shape
    lat_size, lon_size = lax.axis_size("lat"), lax.axis_size("lon")
    both = ("lat", "lon")
    lat_route, lon_route, diag_route = routes(lat_size, lon_size)

    def back(route):
        return [(target, source) for source, target in route]

    own_fields = fields.reshape(TOKENS, width)
    own_grads = cotangent.reshape(TOKENS, width)
    lengths = (HALF, QUARTER, QUARTER, QUARTER, HALF, HALF)
    picked = call(order_kernel, [((rows, TOKENS), BF) for rows in lengths], name="order", flops=LOAD)
    inner_lat, outer_lat, lon_piece, diag_piece, inner_own, outer_own = call(
        pack_kernel,
        [((rows, 2 * width), BF) for rows in lengths[:4]] + [((HALF, 2 * width), F32)] * 2,
        own_fields, own_grads, *picked,
        name="pack", flops=LOAD,
    )
    inner_in = lax.ppermute(inner_lat, both, lat_route)
    outer_in = lax.ppermute(outer_lat, both, lat_route)
    diag_in = lax.ppermute(diag_piece, both, diag_route)
    lon_in = lax.ppermute(lon_piece, both, lon_route)

    split = (lat_size, width // 2, 4 * width // lat_size)
    per_window = [
        ((WIN, width), BF),
        ((WIN, width), BF),
        ((width // 2, WIN), BF),
        ((width // 2, WIN), BF),
        ((WIN, 3 * width), BF),
        ((WIN, width), BF),
    ]
    scratch = [pltpu.VMEM((width, WIN), BF)] * 2 + [pltpu.VMEM((width // 2, WIN), BF)]
    grad_so_far, *inner = call(
        inner_kernel, [(split, F32), *per_window], inner_own, inner_in, qkv_weight, proj_weight,
        name="inner", flops=10**9, scratch=scratch,
    )
    send_grad, *outer = call(
        outer_kernel, [(split, BF), *per_window],
        outer_own, outer_in, lon_in, diag_in, qkv_weight, proj_weight, grad_so_far,
        name="outer", flops=10**9, scratch=scratch,
    )
    sibling = [(j, j ^ 1) for j in range(lon_size)]
    received = lax.ppermute(send_grad, "lon", sibling)
    kept, *results = call(
        output_kernel, [(split, BF), ((WIN, 2 * width), BF), ((WIN, 2 * width), BF)],
        *inner, *outer, qkv_weight, proj_weight,
        name="outputs", flops=10**9,
    )

    slots = lat_size
    bits = lat_size.bit_length() - 1
    for phase in range(bits):
        slots //= 2
        half = ((slots, *split[1:]), BF)
        send, kept = call(halve_kernel, [half, half], kept, received, name=f"halve{slots}")
        route = [
            (i * lon_size + j, (i ^ (1 << (phase if j % 2 == 0 else bits - 1 - phase))) * lon_size + j)
            for i in range(lat_size)
            for j in range(lon_size)
        ]
        received = lax.ppermute(send, both, route)

    rows = width // lon_size
    share = ((rows, split[2]), BF)
    parts = call(line_parts_kernel, [share] * (lon_size // 2), kept, received, name="line_parts")
    arrived = [
        lax.ppermute(parts[step], "lon", [(j, j ^ (2 * step)) for j in range(lon_size)])
        for step in range(1, lon_size // 2)
    ]
    lat_back, lon_back, diag_back = call(
        pack_back_kernel, [((rows, 2 * width), BF) for rows in (HALF + QUARTER, QUARTER, QUARTER)],
        parts[-1], *results,
        name="pack_back", unread=(0,),
    )
    lat_home = lax.ppermute(lat_back, both, back(lat_route))
    diag_home = lax.ppermute(diag_back, both, back(diag_route))
    lon_home = lax.ppermute(lon_back, both, back(lon_route))
    (line_sum,) = call(sum_kernel, [share], parts[0], *arrived, name="line_sum", flops=LONG)
    shared = [
        lax.ppermute(line_sum, "lat", [(i, i ^ step) for i in range(lat_size)]) for step in range(1, lat_size)
    ]
    field_out, d_fields, placed = call(
        place_kernel,
        [((TOKENS, width), BF), ((TOKENS, width), BF), ((8, LANES), F32)],
        *results, lat_home, lon_home, diag_home,
        name="place",
    )
    qkv_grad, proj_grad = call(
        finish_kernel,
        [((rows, 3 * width), F32), ((rows, width), F32)],
        placed, line_sum, *shared,
        name="finish", unread=(0,), scratch=[pltpu.VMEM((lat_size, *share[0]), F32)],
    )
    return (field_out.reshape(fields.shape), d_fields.reshape(fields.shape), qkv_grad, jnp.transpose(proj_grad))


def solution(mesh):
    placed = (P(None, "lat", "lon", None), P(None, "lat", "lon", None), P(), P())
    return jax.shard_map(
        per_device,
        mesh=mesh,
        in_specs=placed,
        out_specs=(
            P(None, "lat", "lon", None),
            P(None, "lat", "lon", None),
            P("lon", None),
            P(None, "lon"),
        ),
        check_vma=False,
    )
```

time: 64.3 us -> 57.3 us (0.89)
  waiting for transfers between devices: 28.5 us -> 21.6 us
  local copies, waits for them, and re-layouts: 4.36 us -> 0.94 us
  starting transfers between devices: 18.7 us -> 22 us
    ppermute x3, waiting for transfers between devices: 6.54 us -> 0.01 us  [per_device(): lax.ppermute(line_sum, 'lat', [(i, i ^ step) for i in range(lat_size)])]
    unnamed x8, local copies, waits for them, and re-layouts: 4.36 us -> 0.94 us
    ppermute x1, waiting for transfers between devices: 0.01 us -> 3.39 us  [per_device(): lat_home = lax.ppermute(lat_back, both, back(lat_route))]
    ppermute x1, starting transfers between devices: 0.01 us -> 2.73 us  [per_device(): diag_home = lax.ppermute(diag_back, both, back(diag_route))]
    ppermute x3, waiting for transfers between devices: 5.83 us -> 3.23 us  [per_device(): lax.ppermute(parts[step], 'lon', [(j, j ^ 2 * step) for j in range(lon_si...]
    ppermute x1, starting transfers between devices: 1.89 us -> 0.01 us  [per_device(): lat_home = lax.ppermute(lat_back, both, back(lat_route))]
    ppermute x1, waiting for transfers between devices: 1.88 us -> 0.01 us  [per_device(): diag_in = lax.ppermute(diag_piece, both, diag_route)]
    ppermute x1, starting transfers between devices: 0.93 us -> 2.17 us  [per_device(): diag_in = lax.ppermute(diag_piece, both, diag_route)]
  transfers between devices with their start and end apart: 15 -> 16, of which waited for: 9 -> 6; matrix products, arithmetic and copies ran while one was open for 0% -> 0% of each run, Pallas kernels for 4% -> 11%
where the time goes in v3:
time: 57.3 us; the launch traced here: 57.1 us
  starting transfers between devices  22 us (38%)
  waiting for transfers between devices  21.6 us (38%)
  Pallas kernels  11.9 us (21%)
  local copies, waits for them, and re-layouts  0.94 us (2%)
  between operations  0.76 us (1%)
    ppermute x2, waiting for transfers between devices, per_device(): received = lax.ppermute(send, both, route)  13.7 us
    pallas_call x12, Pallas kernels, call(): pl.pallas_call(kernel, out_shape=shapes, in_specs=[anywhere if i in unrea...  11.9 us
    ppermute x3, starting transfers between devices, per_device(): lax.ppermute(parts[step], 'lon', [(j, j ^ 2 * step) for j in range(lon_si...  4.47 us
    ppermute x1, starting transfers between devices, per_device(): inner_in = lax.ppermute(inner_lat, both, lat_route)  3.94 us
    ppermute x3, starting transfers between devices, per_device(): lax.ppermute(line_sum, 'lat', [(i, i ^ step) for i in range(lat_size)])  3.55 us
    ppermute x1, waiting for transfers between devices, per_device(): lat_home = lax.ppermute(lat_back, both, back(lat_route))  3.39 us
    ppermute x3, waiting for transfers between devices, per_device(): lax.ppermute(parts[step], 'lon', [(j, j ^ 2 * step) for j in range(lon_si...  3.23 us
    ppermute x1, starting transfers between devices, per_device(): diag_home = lax.ppermute(diag_back, both, back(diag_route))  2.73 us
  transfers between devices with their start and end apart: 16, of which 6 were waited for; matrix products, arithmetic and copies ran while one was open for 0% of the time, Pallas kernels for 11%

profile of v3, /device:TPU:0, one launch (start us, length us, event | category | flops | bytes accessed | tf_op | source)
XLA Modules:
  0.0 57.1 jit_solution(17243109303482467192)
XLA Ops:
  0.6 0.0 copy-start.3
  0.6 0.0 copy-start.2
  0.7 0.1 order.1
  0.8 0.8 %copy-done.3 = bf16[2,6,24,512]{3,2,1,0:T(8,128)(2,1)S(1)} copy-done((bf16[2,6,24,512]{3,2,1,0:T(8,128)(2,1)S(1)}, bf16[2,6,24,512]{3,2,1,0:T(8,128)(2,1)}, u32[]{:S(2)}) %copy-start.3) | copy-done | bytes 294936
  1.6 0.1 copy-done.2
  1.7 0.9 %pack.1 = (bf16[72,1024]{1,0:T(8,128)(2,1)S(1)}, bf16[36,1024]{1,0:T(8,128)(2,1)S(1)}, bf16[36,1024]{1,0:T(8,128)(2,1)S(1)}, bf16[36,1024]{1,0:T(8,128)(2,1)S(1)...) custom-call(bf16[288,512]{1,0:T(8,128)(2,1)S(1)} %bitcast.5, bf16[288,512]{1,0:T(8,128)(2,1)S(1)} %bitcast.6, ...), custom_call_target="tpu_custom_call" | custom-call | flops 5000000000 | bytes 1734912 | tf_op jit(solution)/shard_map/pack/pallas_call | solution.py:324
  2.6 3.9 %collective-permute-start = (bf16[72,1024]{1,0:T(8,128)(2,1)S(1)}, bf16[72,1024]{1,0:T(8,128)(2,1)S(1)}, u32[]{:S(2)}, u32[]{:S(2)}) collective-permute-start(bf16[72,1024]{1,0:T(8,128)(2,1)S(1)} %get-tuple-element.56), channel_id=1, source_target_pairs={{0,24},{1,9},{2,26},{3,11},{4,28},{5,13},{6,30},{7,15},{8,0},{9,17... | collective-permute-start | bytes 442376 | tf_op jit(solution)/shard_map/ppermute | solution.py:368
  6.5 0.5 collective-permute-start.1
  7.0 2.5 %collective-permute-start.2 = (bf16[36,1024]{1,0:T(8,128)(2,1)S(1)}, bf16[36,1024]{1,0:T(8,128)(2,1)S(1)}, u32[]{:S(2)}, u32[]{:S(2)}) collective-permute-start(bf16[36,1024]{1,0:T(8,128)(2,1)S(1)} %get-tuple-element.65), channel_id=1, source_target_pairs={{0,7},{1,0},{2,1},{3,2},{4,3},{5,4},{6,5},{7,6},{8,15},{9,8},{10,9... | collective-permute-start | bytes 221192 | tf_op jit(solution)/shard_map/ppermute | solution.py:371
  9.5 2.2 %collective-permute-start.3 = (bf16[36,1024]{1,0:T(8,128)(2,1)S(1)}, bf16[36,1024]{1,0:T(8,128)(2,1)S(1)}, u32[]{:S(2)}, u32[]{:S(2)}) collective-permute-start(bf16[36,1024]{1,0:T(8,128)(2,1)S(1)} %get-tuple-element.66), channel_id=1, source_target_pairs={{0,15},{1,24},{2,9},{3,26},{4,11},{5,28},{6,13},{7,30},{8,23},{9,0... | collective-permute-start | bytes 221192 | tf_op jit(solution)/shard_map/ppermute | solution.py:370
  11.7 0.0 collective-permute-done.lat_in
  11.7 0.0 copy-done.1
  11.7 3.1 %inner.1 = (f32[4,256,512]{2,1,0:T(8,128)S(1)}, bf16[144,512]{1,0:T(8,128)(2,1)S(1)}, bf16[144,512]{1,0:T(8,128)(2,1)S(1)}, bf16[256,144]{1,0:T(8,128)(2,1)S(1)}...) custom-call(f32[72,1024]{1,0:T(8,128)S(1)} %get-tuple-element.55.own, ...), custom_call_target="tpu_custom_call" | custom-call | flops 1000000000 | bytes 5668864 | tf_op jit(solution)/shard_map/inner/pallas_call | solution.py:324
  14.8 0.0 collective-permute-done.1.lat_in
  14.8 0.0 collective-permute-done.2.lon_in
  14.8 0.0 collective-permute-done.3.diag_in
  14.8 3.3 %outer.1 = (bf16[4,256,512]{2,1,0:T(8,128)(2,1)S(1)}, bf16[144,512]{1,0:T(8,128)(2,1)S(1)}, bf16[144,512]{1,0:T(8,128)(2,1)S(1)}, bf16[256,144]{1,0:T(8,128)(2,1...) custom-call(f32[72,1024]{1,0:T(8,128)S(1)} %get-tuple-element.63.own, ...), custom_call_target="tpu_custom_call" | custom-call | flops 1000000000 | bytes 6791168 | tf_op jit(solution)/shard_map/outer/pallas_call | solution.py:324
  18.1 0.1 collective-permute-start.4
  18.2 1.4 %outputs.1 = (bf16[4,256,512]{2,1,0:T(8,128)(2,1)S(1)}, bf16[144,1024]{1,0:T(8,128)(2,1)S(1)}, bf16[144,1024]{1,0:T(8,128)(2,1)S(1)}) custom-call(bf16[144,512]{1,0:T(8,128)(2,1)S(1)} %get-tuple-element.57.refs_0_, bf16[144,512]{1,0:T(8,128)(2,1)S(1)} %get-tuple-element.58.refs_1_, bf16[256,144]{1,0:T(8,128)(2,1)S(1)} %get-tuple-element.59.refs_2_, ...), custom_call_target="tpu_custom_call" | custom-call | flops 1000000000 | bytes 5799936 | tf_op jit(solution)/shard_map/outputs/pallas_call | solution.py:324
  19.6 1.2 %collective-permute-done.4.received = bf16[4,256,512]{2,1,0:T(8,128)(2,1)S(1)} collective-permute-done((bf16[4,256,512]{2,1,0:T(8,128)(2,1)S(1)}, bf16[4,256,512]{2,1,0:T(8,128)(2,1)S(1)}, u32[]{:S(2)}, u32[]{:S(2)}) %collective-permute-start.4) | collective-permute-done | bytes 1048608 | tf_op jit(solution)/shard_map/ppermute | solution.py:393
  20.8 0.2 halve2.1
  21.0 1.4 %collective-permute-start.5 = (bf16[2,256,512]{2,1,0:T(8,128)(2,1)S(1)}, bf16[2,256,512]{2,1,0:T(8,128)(2,1)S(1)}, u32[]{:S(2)}, u32[]{:S(2)}) collective-permute-start(bf16[2,256,512]{2,1,0:T(8,128)(2,1)S(1)} %get-tuple-element.79), channel_id=1, source_target_pairs={{0,8},{1,17},{2,10},{3,19},{4,12},{5,21},{6,14},{7,23},{8,0},{9,25... | collective-permute-start | bytes 1572872 | tf_op jit(solution)/shard_map/ppermute | solution.py:411
  22.4 7.9 %collective-permute-done.5.received = bf16[2,256,512]{2,1,0:T(8,128)(2,1)S(1)} collective-permute-done((bf16[2,256,512]{2,1,0:T(8,128)(2,1)S(1)}, bf16[2,256,512]{2,1,0:T(8,128)(2,1)S(1)}, u32[]{:S(2)}, u32[]{:S(2)}) %collective-permute-start.5) | collective-permute-done | bytes 524320 | tf_op jit(solution)/shard_map/ppermute | solution.py:411
  30.3 0.1 halve1.1
  30.4 0.6 %collective-permute-start.6 = (bf16[1,256,512]{2,1,0:T(8,128)(2,1)S(1)}, bf16[1,256,512]{2,1,0:T(8,128)(2,1)S(1)}, u32[]{:S(2)}, u32[]{:S(2)}) collective-permute-start(bf16[1,256,512]{2,1,0:T(8,128)(2,1)S(1)} %get-tuple-element.81), channel_id=1, source_target_pairs={{0,16},{1,9},{2,18},{3,11},{4,20},{5,13},{6,22},{7,15},{8,24},{9,1... | collective-permute-start | bytes 786440 | tf_op jit(solution)/shard_map/ppermute | solution.py:411
  31.0 5.8 %collective-permute-done.6.received = bf16[1,256,512]{2,1,0:T(8,128)(2,1)S(1)} collective-permute-done((bf16[1,256,512]{2,1,0:T(8,128)(2,1)S(1)}, bf16[1,256,512]{2,1,0:T(8,128)(2,1)S(1)}, u32[]{:S(2)}, u32[]{:S(2)}) %collective-permute-start.6) | collective-permute-done | bytes 262176 | tf_op jit(solution)/shard_map/ppermute | solution.py:411
  36.9 0.1 line_parts.1
  36.9 2.0 %collective-permute-start.10 = (bf16[64,512]{1,0:T(8,128)(2,1)S(1)}, bf16[64,512]{1,0:T(8,128)(2,1)S(1)}, u32[]{:S(2)}, u32[]{:S(2)}) collective-permute-start(bf16[64,512]{1,0:T(8,128)(2,1)S(1)} %get-tuple-element.90), channel_id=1, source_target_pairs={{0,2},{1,3},{2,0},{3,1},{4,6},{5,7},{6,4},{7,5},{8,10},{9,11},{10,... | collective-permute-start | bytes 196616 | tf_op jit(solution)/shard_map/ppermute | solution.py:417
  38.9 2.1 %collective-permute-start.11 = (bf16[64,512]{1,0:T(8,128)(2,1)S(1)}, bf16[64,512]{1,0:T(8,128)(2,1)S(1)}, u32[]{:S(2)}, u32[]{:S(2)}) collective-permute-start(bf16[64,512]{1,0:T(8,128)(2,1)S(1)} %get-tuple-element.91), channel_id=1, source_target_pairs={{0,4},{1,5},{2,6},{3,7},{4,0},{5,1},{6,2},{7,3},{8,12},{9,13},{10,... | collective-permute-start | bytes 196616 | tf_op jit(solution)/shard_map/ppermute | solution.py:417
  41.0 0.4 collective-permute-start.12
  41.4 0.2 pack_back.1
  41.6 0.1 collective-permute-start.8
  41.7 2.7 %collective-permute-start.9 = (bf16[36,1024]{1,0:T(8,128)(2,1)S(1)}, bf16[36,1024]{1,0:T(8,128)(2,1)S(1)}, u32[]{:S(2)}, u32[]{:S(2)}) collective-permute-start(bf16[36,1024]{1,0:T(8,128)(2,1)S(1)} %get-tuple-element.85), channel_id=1, source_target_pairs={{15,0},{24,1},{9,2},{26,3},{11,4},{28,5},{13,6},{30,7},{23,8},{0,9... | collective-permute-start | bytes 221192 | tf_op jit(solution)/shard_map/ppermute | solution.py:426
  44.4 0.0 collective-permute-done.10.refs_1_
  44.4 0.0 collective-permute-start.7
  44.4 1.1 %collective-permute-done.11.refs_2_ = bf16[64,512]{1,0:T(8,128)(2,1)S(1)} collective-permute-done((bf16[64,512]{1,0:T(8,128)(2,1)S(1)}, bf16[64,512]{1,0:T(8,128)(2,1)S(1)}, u32[]{:S(2)}, u32[]{:S(2)}) %collective-permute-start.11) | collective-permute-done | bytes 65568 | tf_op jit(solution)/shard_map/ppermute | solution.py:417
  45.5 2.2 %collective-permute-done.12.refs_3_ = bf16[64,512]{1,0:T(8,128)(2,1)S(1)} collective-permute-done((bf16[64,512]{1,0:T(8,128)(2,1)S(1)}, bf16[64,512]{1,0:T(8,128)(2,1)S(1)}, u32[]{:S(2)}, u32[]{:S(2)}) %collective-permute-start.12) | collective-permute-done | bytes 65568 | tf_op jit(solution)/shard_map/ppermute | solution.py:417
  47.7 2.0 %collective-permute-start.15 = (bf16[64,512]{1,0:T(8,128)(2,1)S(1)}, bf16[64,512]{1,0:T(8,128)(2,1)S(1)}, u32[]{:S(2)}, u32[]{:S(2)}) collective-permute-start(bf16[64,512]{1,0:T(8,128)(2,1)S(1)} %line_sum.1.refs_0_), channel_id=1, source_target_pairs={{0,24},{8,16},{16,8},{24,0},{1,25},{9,17},{17,9},{25,1},{2,26},{10... | collective-permute-start | bytes 196616 | tf_op jit(solution)/shard_map/ppermute | solution.py:430
  49.7 0.9 %collective-permute-start.14 = (bf16[64,512]{1,0:T(8,128)(2,1)S(1)}, bf16[64,512]{1,0:T(8,128)(2,1)S(1)}, u32[]{:S(2)}, u32[]{:S(2)}) collective-permute-start(bf16[64,512]{1,0:T(8,128)(2,1)S(1)} %line_sum.1.refs_0_), channel_id=1, source_target_pairs={{0,16},{8,24},{16,0},{24,8},{1,17},{9,25},{17,1},{25,9},{2,18},{10... | collective-permute-start | bytes 196616 | tf_op jit(solution)/shard_map/ppermute | solution.py:430
  50.6 0.0 collective-permute-done.8.lon_in
  50.6 0.7 %collective-permute-start.13 = (bf16[64,512]{1,0:T(8,128)(2,1)S(1)}, bf16[64,512]{1,0:T(8,128)(2,1)S(1)}, u32[]{:S(2)}, u32[]{:S(2)}) collective-permute-start(bf16[64,512]{1,0:T(8,128)(2,1)S(1)} %line_sum.1.refs_0_), channel_id=1, source_target_pairs={{0,8},{8,0},{16,24},{24,16},{1,9},{9,1},{17,25},{25,17},{2,10},{10... | collective-permute-start | bytes 196616 | tf_op jit(solution)/shard_map/ppermute | solution.py:430
  51.2 0.0 collective-permute-done.9.diag_in
  51.2 3.4 %collective-permute-done.7.lat_in = bf16[108,1024]{1,0:T(8,128)(2,1)S(1)} collective-permute-done((bf16[108,1024]{1,0:T(8,128)(2,1)S(1)}, bf16[108,1024]{1,0:T(8,128)(2,1)S(1)}, u32[]{:S(2)}, u32[]{:S(2)}) %collective-permute-start.7) | collective-permute-done | bytes 221216 | tf_op jit(solution)/shard_map/ppermute | solution.py:425
  54.6 1.6 %place.1 = (bf16[288,512]{1,0:T(8,128)(2,1)}, bf16[288,512]{1,0:T(8,128)(2,1)}, f32[8,128]{1,0:T(8,128)S(1)}) custom-call(bf16[144,1024]{1,0:T(8,128)(2,1)S(1)} %get-tuple-element.74.inner_results, bf16[144,1024]{1,0:T(8,128)(2,1)S(1)} %get-tuple-element.75.outer_results, bf16[108,1024]{1,0:T(8,128)(2,1)S(1)} %collective-permute-done.7.lat_in, ...), custom_call_target="tpu_custom_call" | custom-call | bytes 1552384 | tf_op jit(solution)/shard_map/place/pallas_call | solution.py:324
  56.3 0.0 collective-permute-done.15.refs_3_
  56.3 0.0 collective-permute-done.14.refs_2_
  56.3 0.0 collective-permute-done.13.refs_1_
  56.3 0.9 %finish.1 = (f32[64,1536]{1,0:T(8,128)}, f32[64,512]{1,0:T(8,128)}) custom-call(f32[8,128]{1,0:T(8,128)S(1)} %get-tuple-element.88._, bf16[64,512]{1,0:T(8,128)(2,1)S(1)} %line_sum.1.refs_0_, bf16[64,512]{1,0:T(8,128)(2,1)S(1)} %collective-permute-done.13.refs_1_, bf16[64,512]{1,0:T(8,128)(2,1)S(1)} %collective-permute-done.14.refs_2_, ...), custom_call_target="tpu_custom_call" | custom-call | bytes 790528 | tf_op jit(solution)/shard_map/finish/pallas_call | solution.py:324
  (4 shorter events, 0.0 us)
Async XLA Ops:
  0.6 1.0 %copy-start.3 = (bf16[2,6,24,512]{3,2,1,0:T(8,128)(2,1)S(1)}, bf16[2,6,24,512]{3,2,1,0:T(8,128)(2,1)}, u32[]{:S(2)}) copy-start(bf16[2,6,24,512]{3,2,1,0:T(8,128)(2,1)} %param.5) | copy-start | bytes 884740
  0.6 1.0 %copy-start.2 = (bf16[2,6,24,512]{3,2,1,0:T(8,128)(2,1)S(1)}, bf16[2,6,24,512]{3,2,1,0:T(8,128)(2,1)}, u32[]{:S(2)}) copy-start(bf16[2,6,24,512]{3,2,1,0:T(8,128)(2,1)} %param.4) | copy-start | bytes 884740
  1.7 10.0 %copy-start = (bf16[512,1536]{1,0:T(8,128)(2,1)S(1)}, bf16[512,1536]{1,0:T(8,128)(2,1)}, u32[]{:S(2)}) copy-start(bf16[512,1536]{1,0:T(8,128)(2,1)} %refs_12_.1) | copy-start | bytes 4718596
  1.7 10.0 %copy-start.1 = (bf16[512,512]{1,0:T(8,128)(2,1)S(1)}, bf16[512,512]{1,0:T(8,128)(2,1)}, u32[]{:S(2)}) copy-start(bf16[512,512]{1,0:T(8,128)(2,1)} %refs_13_.1) | copy-start | bytes 1572868
  2.6 9.1 %collective-permute-start = (bf16[72,1024]{1,0:T(8,128)(2,1)S(1)}, bf16[72,1024]{1,0:T(8,128)(2,1)S(1)}, u32[]{:S(2)}, u32[]{:S(2)}) collective-permute-start(bf16[72,1024]{1,0:T(8,128)(2,1)S(1)} %get-tuple-element.56), channel_id=1, source_target_pairs={{0,24},{1,9},{2,26},{3,11},{4,28},{5,13},{6,30},{7,15},{8,0},{9,17... | collective-permute-start | bytes 442376 | tf_op jit(solution)/shard_map/ppermute | solution.py:368
  6.5 8.3 %collective-permute-start.1 = (bf16[36,1024]{1,0:T(8,128)(2,1)S(1)}, bf16[36,1024]{1,0:T(8,128)(2,1)S(1)}, u32[]{:S(2)}, u32[]{:S(2)}) collective-permute-start(bf16[36,1024]{1,0:T(8,128)(2,1)S(1)} %get-tuple-element.64), channel_id=1, source_target_pairs={{0,24},{1,9},{2,26},{3,11},{4,28},{5,13},{6,30},{7,15},{8,0},{9,17... | collective-permute-start | bytes 221192 | tf_op jit(solution)/shard_map/ppermute | solution.py:369
  7.0 7.7 %collective-permute-start.2 = (bf16[36,1024]{1,0:T(8,128)(2,1)S(1)}, bf16[36,1024]{1,0:T(8,128)(2,1)S(1)}, u32[]{:S(2)}, u32[]{:S(2)}) collective-permute-start(bf16[36,1024]{1,0:T(8,128)(2,1)S(1)} %get-tuple-element.65), channel_id=1, source_target_pairs={{0,7},{1,0},{2,1},{3,2},{4,3},{5,4},{6,5},{7,6},{8,15},{9,8},{10,9... | collective-permute-start | bytes 221192 | tf_op jit(solution)/shard_map/ppermute | solution.py:371
  9.5 5.3 %collective-permute-start.3 = (bf16[36,1024]{1,0:T(8,128)(2,1)S(1)}, bf16[36,1024]{1,0:T(8,128)(2,1)S(1)}, u32[]{:S(2)}, u32[]{:S(2)}) collective-permute-start(bf16[36,1024]{1,0:T(8,128)(2,1)S(1)} %get-tuple-element.66), channel_id=1, source_target_pairs={{0,15},{1,24},{2,9},{3,26},{4,11},{5,28},{6,13},{7,30},{8,23},{9,0... | collective-permute-start | bytes 221192 | tf_op jit(solution)/shard_map/ppermute | solution.py:370
  18.1 2.7 %collective-permute-start.4 = (bf16[4,256,512]{2,1,0:T(8,128)(2,1)S(1)}, bf16[4,256,512]{2,1,0:T(8,128)(2,1)S(1)}, u32[]{:S(2)}, u32[]{:S(2)}) collective-permute-start(bf16[4,256,512]{2,1,0:T(8,128)(2,1)S(1)} %get-tuple-element.77), channel_id=1, source_target_pairs={{0,1},{1,0},{2,3},{3,2},{4,5},{5,4},{6,7},{7,6},{8,9},{9,8},{10,11... | collective-permute-start | bytes 3145736 | tf_op jit(solution)/shard_map/ppermute | solution.py:393
  21.0 9.2 %collective-permute-start.5 = (bf16[2,256,512]{2,1,0:T(8,128)(2,1)S(1)}, bf16[2,256,512]{2,1,0:T(8,128)(2,1)S(1)}, u32[]{:S(2)}, u32[]{:S(2)}) collective-permute-start(bf16[2,256,512]{2,1,0:T(8,128)(2,1)S(1)} %get-tuple-element.79), channel_id=1, source_target_pairs={{0,8},{1,17},{2,10},{3,19},{4,12},{5,21},{6,14},{7,23},{8,0},{9,25... | collective-permute-start | bytes 1572872 | tf_op jit(solution)/shard_map/ppermute | solution.py:411
  30.4 6.4 %collective-permute-start.6 = (bf16[1,256,512]{2,1,0:T(8,128)(2,1)S(1)}, bf16[1,256,512]{2,1,0:T(8,128)(2,1)S(1)}, u32[]{:S(2)}, u32[]{:S(2)}) collective-permute-start(bf16[1,256,512]{2,1,0:T(8,128)(2,1)S(1)} %get-tuple-element.81), channel_id=1, source_target_pairs={{0,16},{1,9},{2,18},{3,11},{4,20},{5,13},{6,22},{7,15},{8,24},{9,1... | collective-permute-start | bytes 786440 | tf_op jit(solution)/shard_map/ppermute | solution.py:411
  36.9 7.5 %collective-permute-start.10 = (bf16[64,512]{1,0:T(8,128)(2,1)S(1)}, bf16[64,512]{1,0:T(8,128)(2,1)S(1)}, u32[]{:S(2)}, u32[]{:S(2)}) collective-permute-start(bf16[64,512]{1,0:T(8,128)(2,1)S(1)} %get-tuple-element.90), channel_id=1, source_target_pairs={{0,2},{1,3},{2,0},{3,1},{4,6},{5,7},{6,4},{7,5},{8,10},{9,11},{10,... | collective-permute-start | bytes 196616 | tf_op jit(solution)/shard_map/ppermute | solution.py:417
  38.9 6.6 %collective-permute-start.11 = (bf16[64,512]{1,0:T(8,128)(2,1)S(1)}, bf16[64,512]{1,0:T(8,128)(2,1)S(1)}, u32[]{:S(2)}, u32[]{:S(2)}) collective-permute-start(bf16[64,512]{1,0:T(8,128)(2,1)S(1)} %get-tuple-element.91), channel_id=1, source_target_pairs={{0,4},{1,5},{2,6},{3,7},{4,0},{5,1},{6,2},{7,3},{8,12},{9,13},{10,... | collective-permute-start | bytes 196616 | tf_op jit(solution)/shard_map/ppermute | solution.py:417
  41.0 6.7 %collective-permute-start.12 = (bf16[64,512]{1,0:T(8,128)(2,1)S(1)}, bf16[64,512]{1,0:T(8,128)(2,1)S(1)}, u32[]{:S(2)}, u32[]{:S(2)}) collective-permute-start(bf16[64,512]{1,0:T(8,128)(2,1)S(1)} %get-tuple-element.82._), channel_id=1, source_target_pairs={{0,6},{1,7},{2,4},{3,5},{4,2},{5,3},{6,0},{7,1},{8,14},{9,15},{10,... | collective-permute-start | bytes 196616 | tf_op jit(solution)/shard_map/ppermute | solution.py:417
  41.6 9.0 %collective-permute-start.8 = (bf16[36,1024]{1,0:T(8,128)(2,1)S(1)}, bf16[36,1024]{1,0:T(8,128)(2,1)S(1)}, u32[]{:S(2)}, u32[]{:S(2)}) collective-permute-start(bf16[36,1024]{1,0:T(8,128)(2,1)S(1)} %get-tuple-element.84), channel_id=1, source_target_pairs={{7,0},{0,1},{1,2},{2,3},{3,4},{4,5},{5,6},{6,7},{15,8},{8,9},{9,10... | collective-permute-start | bytes 221192 | tf_op jit(solution)/shard_map/ppermute | solution.py:427
  41.7 9.6 %collective-permute-start.9 = (bf16[36,1024]{1,0:T(8,128)(2,1)S(1)}, bf16[36,1024]{1,0:T(8,128)(2,1)S(1)}, u32[]{:S(2)}, u32[]{:S(2)}) collective-permute-start(bf16[36,1024]{1,0:T(8,128)(2,1)S(1)} %get-tuple-element.85), channel_id=1, source_target_pairs={{15,0},{24,1},{9,2},{26,3},{11,4},{28,5},{13,6},{30,7},{23,8},{0,9... | collective-permute-start | bytes 221192 | tf_op jit(solution)/shard_map/ppermute | solution.py:426
  44.4 10.2 %collective-permute-start.7 = (bf16[108,1024]{1,0:T(8,128)(2,1)S(1)}, bf16[108,1024]{1,0:T(8,128)(2,1)S(1)}, u32[]{:S(2)}, u32[]{:S(2)}) collective-permute-start(bf16[108,1024]{1,0:T(8,128)(2,1)S(1)} %get-tuple-element.83), channel_id=1, source_target_pairs={{24,0},{9,1},{26,2},{11,3},{28,4},{13,5},{30,6},{15,7},{0,8},{17,9... | collective-permute-start | bytes 663560 | tf_op jit(solution)/shard_map/ppermute | solution.py:425
  47.7 8.6 %collective-permute-start.15 = (bf16[64,512]{1,0:T(8,128)(2,1)S(1)}, bf16[64,512]{1,0:T(8,128)(2,1)S(1)}, u32[]{:S(2)}, u32[]{:S(2)}) collective-permute-start(bf16[64,512]{1,0:T(8,128)(2,1)S(1)} %line_sum.1.refs_0_), channel_id=1, source_target_pairs={{0,24},{8,16},{16,8},{24,0},{1,25},{9,17},{17,9},{25,1},{2,26},{10... | collective-permute-start | bytes 196616 | tf_op jit(solution)/shard_map/ppermute | solution.py:430
  49.7 6.6 %collective-permute-start.14 = (bf16[64,512]{1,0:T(8,128)(2,1)S(1)}, bf16[64,512]{1,0:T(8,128)(2,1)S(1)}, u32[]{:S(2)}, u32[]{:S(2)}) collective-permute-start(bf16[64,512]{1,0:T(8,128)(2,1)S(1)} %line_sum.1.refs_0_), channel_id=1, source_target_pairs={{0,16},{8,24},{16,0},{24,8},{1,17},{9,25},{17,1},{25,9},{2,18},{10... | collective-permute-start | bytes 196616 | tf_op jit(solution)/shard_map/ppermute | solution.py:430
  50.6 5.7 %collective-permute-start.13 = (bf16[64,512]{1,0:T(8,128)(2,1)S(1)}, bf16[64,512]{1,0:T(8,128)(2,1)S(1)}, u32[]{:S(2)}, u32[]{:S(2)}) collective-permute-start(bf16[64,512]{1,0:T(8,128)(2,1)S(1)} %line_sum.1.refs_0_), channel_id=1, source_target_pairs={{0,8},{8,0},{16,24},{24,16},{1,9},{9,1},{17,25},{25,17},{2,10},{10... | collective-permute-start | bytes 196616 | tf_op jit(solution)/shard_map/ppermute | solution.py:430

commit v4 on v3

--- a/solution.py
+++ b/solution.py
@@ -145,7 +145,7 @@
     one_window(both, qkv_weight, proj_weight, None, send_grad, *refs)
 
 
-def outer_kernel(own, lat_in, lon_in, diag_in, qkv_weight, proj_weight, grad_so_far, send_grad, *refs):
+def outer_kernel(own, lon_in, lat_in, diag_in, qkv_weight, proj_weight, grad_so_far, send_grad, *refs):
     last = picks(last_rows, HALF, QUARTER)
     both = jnp.concatenate(
         [
@@ -296,7 +296,7 @@
         out[...] = (kept[0, at].astype(F32) + received[0, at].astype(F32)).astype(out.dtype)
 
 
-def sum_kernel(*refs):
+def sum_kernel(_, *refs):
     *parts, out = refs
     total = parts[0][...].astype(F32)
     for part in parts[1:]:
@@ -304,7 +304,7 @@
     out[...] = total.astype(out.dtype)
 
 
-def finish_kernel(_, *refs):
+def finish_kernel(*refs):
     *parts, qkv_out, proj_out, shared = refs
     lat = lax.axis_index("lat")
     for step, part in enumerate(parts):
@@ -366,9 +366,9 @@
         name="pack", flops=LOAD,
     )
     inner_in = lax.ppermute(inner_lat, both, lat_route)
+    lon_in = lax.ppermute(lon_piece, both, lon_route)
     outer_in = lax.ppermute(outer_lat, both, lat_route)
     diag_in = lax.ppermute(diag_piece, both, diag_route)
-    lon_in = lax.ppermute(lon_piece, both, lon_route)
 
     split = (lat_size, width // 2, 4 * width // lat_size)
     per_window = [
@@ -386,7 +386,7 @@
     )
     send_grad, *outer = call(
         outer_kernel, [(split, BF), *per_window],
-        outer_own, outer_in, lon_in, diag_in, qkv_weight, proj_weight, grad_so_far,
+        outer_own, lon_in, outer_in, diag_in, qkv_weight, proj_weight, grad_so_far,
         name="outer", flops=10**9, scratch=scratch,
     )
     sibling = [(j, j ^ 1) for j in range(lon_size)]
@@ -410,24 +410,21 @@
         ]
         received = lax.ppermute(send, both, route)
 
+    lat_back, lon_back, diag_back = call(
+        pack_back_kernel, [((rows, 2 * width), BF) for rows in (HALF + QUARTER, QUARTER, QUARTER)],
+        send, *results,
+        name="pack_back", unread=(0,),
+    )
+    lat_home = lax.ppermute(lat_back, both, back(lat_route))
+    diag_home = lax.ppermute(diag_back, both, back(diag_route))
+    lon_home = lax.ppermute(lon_back, both, back(lon_route))
+
     rows = width // lon_size
     share = ((rows, split[2]), BF)
-    parts = call(line_parts_kernel, [share] * (lon_size // 2), kept, received, name="line_parts")
+    parts = call(line_parts_kernel, [share] * (lon_size // 2), kept, received, name="line_parts", flops=LONG)
     arrived = [
         lax.ppermute(parts[step], "lon", [(j, j ^ (2 * step)) for j in range(lon_size)])
         for step in range(1, lon_size // 2)
-    ]
-    lat_back, lon_back, diag_back = call(
-        pack_back_kernel, [((rows, 2 * width), BF) for rows in (HALF + QUARTER, QUARTER, QUARTER)],
-        parts[-1], *results,
-        name="pack_back", unread=(0,),
-    )
-    lat_home = lax.ppermute(lat_back, both, back(lat_route))
-    diag_home = lax.ppermute(diag_back, both, back(diag_route))
-    lon_home = lax.ppermute(lon_back, both, back(lon_route))
-    (line_sum,) = call(sum_kernel, [share], parts[0], *arrived, name="line_sum", flops=LONG)
-    shared = [
-        lax.ppermute(line_sum, "lat", [(i, i ^ step) for i in range(lat_size)]) for step in range(1, lat_size)
     ]
     field_out, d_fields, placed = call(
         place_kernel,
@@ -435,11 +432,15 @@
         *results, lat_home, lon_home, diag_home,
         name="place",
     )
+    (line_sum,) = call(sum_kernel, [share], placed, parts[0], *arrived, name="line_sum", unread=(0,))
+    shared = [
+        lax.ppermute(line_sum, "lat", [(i, i ^ step) for i in range(lat_size)]) for step in range(1, lat_size)
+    ]
     qkv_grad, proj_grad = call(
         finish_kernel,
         [((rows, 3 * width), F32), ((rows, width), F32)],
-        placed, line_sum, *shared,
-        name="finish", unread=(0,), scratch=[pltpu.VMEM((lat_size, *share[0]), F32)],
+        line_sum, *shared,
+        name="finish", scratch=[pltpu.VMEM((lat_size, *share[0]), F32)],
     )
     return (field_out.reshape(fields.shape), d_fields.reshape(fields.shape), qkv_grad, jnp.transpose(proj_grad))
 

time: 57.3 us -> 57.3 us (level)
  waiting for transfers between devices: 21.6 us -> 16.4 us
  starting transfers between devices: 22 us -> 27.2 us
    ppermute x2, waiting for transfers between devices: 13.7 us -> 7.87 us  [per_device(): received = lax.ppermute(send, both, route)]
    ppermute x3, waiting for transfers between devices: 0.01 us -> 3.62 us  [per_device(): lax.ppermute(line_sum, 'lat', [(i, i ^ step) for i in range(lat_size)])]
    ppermute x3, waiting for transfers between devices: 3.23 us -> 0.09 us  [per_device(): lax.ppermute(parts[step], 'lon', [(j, j ^ 2 * step) for j in range(lon_si...]
    ppermute x3, starting transfers between devices: 3.55 us -> 5.91 us  [per_device(): lax.ppermute(line_sum, 'lat', [(i, i ^ step) for i in range(lat_size)])]
    ppermute x2, starting transfers between devices: 1.96 us -> 3.54 us  [per_device(): received = lax.ppermute(send, both, route)]
    ppermute x1, starting transfers between devices: 2.73 us -> 3.98 us  [per_device(): diag_home = lax.ppermute(diag_back, both, back(diag_route))]
    ppermute x1, starting transfers between devices: 0.54 us -> 1.44 us  [per_device(): outer_in = lax.ppermute(outer_lat, both, lat_route)]
    ppermute x1, starting transfers between devices: 2.48 us -> 1.8 us  [per_device(): lon_in = lax.ppermute(lon_piece, both, lon_route)]
  transfers between devices with their start and end apart: 16 -> 16, of which waited for: 6 -> 7; matrix products, arithmetic and copies ran while one was open for 0% -> 0% of each run, Pallas kernels for 11% -> 11%
where the time goes in v4:
time: 57.3 us; the launch traced here: 57.2 us
  starting transfers between devices  27.2 us (47%)
  waiting for transfers between devices  16.4 us (29%)
  Pallas kernels  11.9 us (21%)
  local copies, waits for them, and re-layouts  0.94 us (2%)
  between operations  0.75 us (1%)
    pallas_call x12, Pallas kernels, call(): pl.pallas_call(kernel, out_shape=shapes, in_specs=[anywhere if i in unrea...  11.9 us
    ppermute x2, waiting for transfers between devices, per_device(): received = lax.ppermute(send, both, route)  7.87 us
    ppermute x3, starting transfers between devices, per_device(): lax.ppermute(line_sum, 'lat', [(i, i ^ step) for i in range(lat_size)])  5.91 us
    ppermute x3, starting transfers between devices, per_device(): lax.ppermute(parts[step], 'lon', [(j, j ^ 2 * step) for j in range(lon_si...  4.75 us
    ppermute x1, starting transfers between devices, per_device(): diag_home = lax.ppermute(diag_back, both, back(diag_route))  3.98 us
    ppermute x1, starting transfers between devices, per_device(): inner_in = lax.ppermute(inner_lat, both, lat_route)  3.94 us
    ppermute x1, waiting for transfers between devices, per_device(): lat_home = lax.ppermute(lat_back, both, back(lat_route))  3.7 us
    ppermute x3, waiting for transfers between devices, per_device(): lax.ppermute(line_sum, 'lat', [(i, i ^ step) for i in range(lat_size)])  3.62 us
  transfers between devices with their start and end apart: 16, of which 7 were waited for; matrix products, arithmetic and copies ran while one was open for 0% of the time, Pallas kernels for 11%

profile of v4, /device:TPU:0, one launch (start us, length us, event | category | flops | bytes accessed | tf_op | source)
XLA Modules:
  0.0 57.2 jit_solution(12842006013621853020)
XLA Ops:
  0.6 0.0 copy-start.3
  0.6 0.0 copy-start.2
  0.7 0.1 order.1
  0.8 0.8 %copy-done.3 = bf16[2,6,24,512]{3,2,1,0:T(8,128)(2,1)S(1)} copy-done((bf16[2,6,24,512]{3,2,1,0:T(8,128)(2,1)S(1)}, bf16[2,6,24,512]{3,2,1,0:T(8,128)(2,1)}, u32[]{:S(2)}) %copy-start.3) | copy-done | bytes 294936
  1.6 0.1 copy-done.2
  1.7 0.9 %pack.1 = (bf16[72,1024]{1,0:T(8,128)(2,1)S(1)}, bf16[36,1024]{1,0:T(8,128)(2,1)S(1)}, bf16[36,1024]{1,0:T(8,128)(2,1)S(1)}, bf16[36,1024]{1,0:T(8,128)(2,1)S(1)...) custom-call(bf16[288,512]{1,0:T(8,128)(2,1)S(1)} %bitcast.5, bf16[288,512]{1,0:T(8,128)(2,1)S(1)} %bitcast.6, ...), custom_call_target="tpu_custom_call" | custom-call | flops 5000000000 | bytes 1734912 | tf_op jit(solution)/shard_map/pack/pallas_call | solution.py:324
  2.6 3.9 %collective-permute-start = (bf16[72,1024]{1,0:T(8,128)(2,1)S(1)}, bf16[72,1024]{1,0:T(8,128)(2,1)S(1)}, u32[]{:S(2)}, u32[]{:S(2)}) collective-permute-start(bf16[72,1024]{1,0:T(8,128)(2,1)S(1)} %get-tuple-element.56), channel_id=1, source_target_pairs={{0,24},{1,9},{2,26},{3,11},{4,28},{5,13},{6,30},{7,15},{8,0},{9,17... | collective-permute-start | bytes 442376 | tf_op jit(solution)/shard_map/ppermute | solution.py:368
  6.5 1.8 %collective-permute-start.1 = (bf16[36,1024]{1,0:T(8,128)(2,1)S(1)}, bf16[36,1024]{1,0:T(8,128)(2,1)S(1)}, u32[]{:S(2)}, u32[]{:S(2)}) collective-permute-start(bf16[36,1024]{1,0:T(8,128)(2,1)S(1)} %get-tuple-element.64), channel_id=1, source_target_pairs={{0,7},{1,0},{2,1},{3,2},{4,3},{5,4},{6,5},{7,6},{8,15},{9,8},{10,9... | collective-permute-start | bytes 221192 | tf_op jit(solution)/shard_map/ppermute | solution.py:369
  8.3 1.4 %collective-permute-start.2 = (bf16[36,1024]{1,0:T(8,128)(2,1)S(1)}, bf16[36,1024]{1,0:T(8,128)(2,1)S(1)}, u32[]{:S(2)}, u32[]{:S(2)}) collective-permute-start(bf16[36,1024]{1,0:T(8,128)(2,1)S(1)} %get-tuple-element.65), channel_id=1, source_target_pairs={{0,24},{1,9},{2,26},{3,11},{4,28},{5,13},{6,30},{7,15},{8,0},{9,17... | collective-permute-start | bytes 221192 | tf_op jit(solution)/shard_map/ppermute | solution.py:370
  9.7 1.6 %collective-permute-start.3 = (bf16[36,1024]{1,0:T(8,128)(2,1)S(1)}, bf16[36,1024]{1,0:T(8,128)(2,1)S(1)}, u32[]{:S(2)}, u32[]{:S(2)}) collective-permute-start(bf16[36,1024]{1,0:T(8,128)(2,1)S(1)} %get-tuple-element.66), channel_id=1, source_target_pairs={{0,15},{1,24},{2,9},{3,26},{4,11},{5,28},{6,13},{7,30},{8,23},{9,0... | collective-permute-start | bytes 221192 | tf_op jit(solution)/shard_map/ppermute | solution.py:371
  11.4 0.0 collective-permute-done.lat_in
  11.4 0.0 copy-done
  11.4 3.1 %inner.1 = (f32[4,256,512]{2,1,0:T(8,128)S(1)}, bf16[144,512]{1,0:T(8,128)(2,1)S(1)}, bf16[144,512]{1,0:T(8,128)(2,1)S(1)}, bf16[256,144]{1,0:T(8,128)(2,1)S(1)}...) custom-call(f32[72,1024]{1,0:T(8,128)S(1)} %get-tuple-element.55.own, ...), custom_call_target="tpu_custom_call" | custom-call | flops 1000000000 | bytes 5668864 | tf_op jit(solution)/shard_map/inner/pallas_call | solution.py:324
  14.4 0.0 collective-permute-done.1.lon_in
  14.4 0.0 collective-permute-done.2.lat_in
  14.5 0.0 collective-permute-done.3.diag_in
  14.5 3.3 %outer.1 = (bf16[4,256,512]{2,1,0:T(8,128)(2,1)S(1)}, bf16[144,512]{1,0:T(8,128)(2,1)S(1)}, bf16[144,512]{1,0:T(8,128)(2,1)S(1)}, bf16[256,144]{1,0:T(8,128)(2,1...) custom-call(f32[72,1024]{1,0:T(8,128)S(1)} %get-tuple-element.63.own, ...), custom_call_target="tpu_custom_call" | custom-call | flops 1000000000 | bytes 6791168 | tf_op jit(solution)/shard_map/outer/pallas_call | solution.py:324
  17.7 0.1 collective-permute-start.4
  17.9 1.4 %outputs.1 = (bf16[4,256,512]{2,1,0:T(8,128)(2,1)S(1)}, bf16[144,1024]{1,0:T(8,128)(2,1)S(1)}, bf16[144,1024]{1,0:T(8,128)(2,1)S(1)}) custom-call(bf16[144,512]{1,0:T(8,128)(2,1)S(1)} %get-tuple-element.57.refs_0_, bf16[144,512]{1,0:T(8,128)(2,1)S(1)} %get-tuple-element.58.refs_1_, bf16[256,144]{1,0:T(8,128)(2,1)S(1)} %get-tuple-element.59.refs_2_, ...), custom_call_target="tpu_custom_call" | custom-call | flops 1000000000 | bytes 5799936 | tf_op jit(solution)/shard_map/outputs/pallas_call | solution.py:324
  19.3 1.1 %collective-permute-done.4.received = bf16[4,256,512]{2,1,0:T(8,128)(2,1)S(1)} collective-permute-done((bf16[4,256,512]{2,1,0:T(8,128)(2,1)S(1)}, bf16[4,256,512]{2,1,0:T(8,128)(2,1)S(1)}, u32[]{:S(2)}, u32[]{:S(2)}) %collective-permute-start.4) | collective-permute-done | bytes 1048608 | tf_op jit(solution)/shard_map/ppermute | solution.py:393
  20.5 0.2 halve2.1
  20.7 2.0 %collective-permute-start.5 = (bf16[2,256,512]{2,1,0:T(8,128)(2,1)S(1)}, bf16[2,256,512]{2,1,0:T(8,128)(2,1)S(1)}, u32[]{:S(2)}, u32[]{:S(2)}) collective-permute-start(bf16[2,256,512]{2,1,0:T(8,128)(2,1)S(1)} %get-tuple-element.79), channel_id=1, source_target_pairs={{0,8},{1,17},{2,10},{3,19},{4,12},{5,21},{6,14},{7,23},{8,0},{9,25... | collective-permute-start | bytes 1572872 | tf_op jit(solution)/shard_map/ppermute | solution.py:411
  22.7 7.3 %collective-permute-done.5.received = bf16[2,256,512]{2,1,0:T(8,128)(2,1)S(1)} collective-permute-done((bf16[2,256,512]{2,1,0:T(8,128)(2,1)S(1)}, bf16[2,256,512]{2,1,0:T(8,128)(2,1)S(1)}, u32[]{:S(2)}, u32[]{:S(2)}) %collective-permute-start.5) | collective-permute-done | bytes 524320 | tf_op jit(solution)/shard_map/ppermute | solution.py:411
  30.0 0.1 halve1.1
  30.1 1.6 %collective-permute-start.9 = (bf16[1,256,512]{2,1,0:T(8,128)(2,1)S(1)}, bf16[1,256,512]{2,1,0:T(8,128)(2,1)S(1)}, u32[]{:S(2)}, u32[]{:S(2)}) collective-permute-start(bf16[1,256,512]{2,1,0:T(8,128)(2,1)S(1)} %get-tuple-element.80._), channel_id=1, source_target_pairs={{0,16},{1,9},{2,18},{3,11},{4,20},{5,13},{6,22},{7,15},{8,24},{9,1... | collective-permute-start | bytes 786440 | tf_op jit(solution)/shard_map/ppermute | solution.py:411
  31.7 0.2 pack_back.1
  31.9 0.1 collective-permute-start.7
  32.0 4.0 %collective-permute-start.8 = (bf16[36,1024]{1,0:T(8,128)(2,1)S(1)}, bf16[36,1024]{1,0:T(8,128)(2,1)S(1)}, u32[]{:S(2)}, u32[]{:S(2)}) collective-permute-start(bf16[36,1024]{1,0:T(8,128)(2,1)S(1)} %get-tuple-element.83), channel_id=1, source_target_pairs={{15,0},{24,1},{9,2},{26,3},{11,4},{28,5},{13,6},{30,7},{23,8},{0,9... | collective-permute-start | bytes 221192 | tf_op jit(solution)/shard_map/ppermute | solution.py:419
  35.9 0.0 collective-permute-start.6
  35.9 0.6 %collective-permute-done.9.received = bf16[1,256,512]{2,1,0:T(8,128)(2,1)S(1)} collective-permute-done((bf16[1,256,512]{2,1,0:T(8,128)(2,1)S(1)}, bf16[1,256,512]{2,1,0:T(8,128)(2,1)S(1)}, u32[]{:S(2)}, u32[]{:S(2)}) %collective-permute-start.9) | collective-permute-done | bytes 262176 | tf_op jit(solution)/shard_map/ppermute | solution.py:411
  36.5 0.1 line_parts.1
  36.6 2.3 %collective-permute-start.10 = (bf16[64,512]{1,0:T(8,128)(2,1)S(1)}, bf16[64,512]{1,0:T(8,128)(2,1)S(1)}, u32[]{:S(2)}, u32[]{:S(2)}) collective-permute-start(bf16[64,512]{1,0:T(8,128)(2,1)S(1)} %get-tuple-element.89), channel_id=1, source_target_pairs={{0,2},{1,3},{2,0},{3,1},{4,6},{5,7},{6,4},{7,5},{8,10},{9,11},{10,... | collective-permute-start | bytes 196616 | tf_op jit(solution)/shard_map/ppermute | solution.py:426
  38.9 1.8 %collective-permute-start.11 = (bf16[64,512]{1,0:T(8,128)(2,1)S(1)}, bf16[64,512]{1,0:T(8,128)(2,1)S(1)}, u32[]{:S(2)}, u32[]{:S(2)}) collective-permute-start(bf16[64,512]{1,0:T(8,128)(2,1)S(1)} %get-tuple-element.90), channel_id=1, source_target_pairs={{0,4},{1,5},{2,6},{3,7},{4,0},{5,1},{6,2},{7,3},{8,12},{9,13},{10,... | collective-permute-start | bytes 196616 | tf_op jit(solution)/shard_map/ppermute | solution.py:426
  40.6 0.0 collective-permute-done.7.lon_in
  40.6 0.7 %collective-permute-start.12 = (bf16[64,512]{1,0:T(8,128)(2,1)S(1)}, bf16[64,512]{1,0:T(8,128)(2,1)S(1)}, u32[]{:S(2)}, u32[]{:S(2)}) collective-permute-start(bf16[64,512]{1,0:T(8,128)(2,1)S(1)} %get-tuple-element.91), channel_id=1, source_target_pairs={{0,6},{1,7},{2,4},{3,5},{4,2},{5,3},{6,0},{7,1},{8,14},{9,15},{10,... | collective-permute-start | bytes 196616 | tf_op jit(solution)/shard_map/ppermute | solution.py:426
  41.3 0.0 collective-permute-done.8.diag_in
  41.3 3.7 %collective-permute-done.6.lat_in = bf16[108,1024]{1,0:T(8,128)(2,1)S(1)} collective-permute-done((bf16[108,1024]{1,0:T(8,128)(2,1)S(1)}, bf16[108,1024]{1,0:T(8,128)(2,1)S(1)}, u32[]{:S(2)}, u32[]{:S(2)}) %collective-permute-start.6) | collective-permute-done | bytes 221216 | tf_op jit(solution)/shard_map/ppermute | solution.py:418
  45.0 1.6 %place.1 = (bf16[288,512]{1,0:T(8,128)(2,1)}, bf16[288,512]{1,0:T(8,128)(2,1)}, f32[8,128]{1,0:T(8,128)S(1)}) custom-call(bf16[144,1024]{1,0:T(8,128)(2,1)S(1)} %get-tuple-element.74.inner_results, bf16[144,1024]{1,0:T(8,128)(2,1)S(1)} %get-tuple-element.75.outer_results, bf16[108,1024]{1,0:T(8,128)(2,1)S(1)} %collective-permute-done.6.lat_in, ...), custom_call_target="tpu_custom_call" | custom-call | bytes 1552384 | tf_op jit(solution)/shard_map/place/pallas_call | solution.py:324
  46.7 0.0 collective-permute-done.10.refs_1_
  46.7 0.0 collective-permute-done.11.refs_2_
  46.7 0.1 collective-permute-done.12.refs_3_
  46.8 5.3 %collective-permute-start.15 = (bf16[64,512]{1,0:T(8,128)(2,1)S(1)}, bf16[64,512]{1,0:T(8,128)(2,1)S(1)}, u32[]{:S(2)}, u32[]{:S(2)}) collective-permute-start(bf16[64,512]{1,0:T(8,128)(2,1)S(1)} %line_sum.1.refs_0_), channel_id=1, source_target_pairs={{0,24},{8,16},{16,8},{24,0},{1,25},{9,17},{17,9},{25,1},{2,26},{10... | collective-permute-start | bytes 196616 | tf_op jit(solution)/shard_map/ppermute | solution.py:437
  52.1 0.0 collective-permute-start.14
  52.1 0.6 %collective-permute-start.13 = (bf16[64,512]{1,0:T(8,128)(2,1)S(1)}, bf16[64,512]{1,0:T(8,128)(2,1)S(1)}, u32[]{:S(2)}, u32[]{:S(2)}) collective-permute-start(bf16[64,512]{1,0:T(8,128)(2,1)S(1)} %line_sum.1.refs_0_), channel_id=1, source_target_pairs={{0,8},{8,0},{16,24},{24,16},{1,9},{9,1},{17,25},{25,17},{2,10},{10... | collective-permute-start | bytes 196616 | tf_op jit(solution)/shard_map/ppermute | solution.py:437
  52.7 1.6 %collective-permute-done.15.refs_3_ = bf16[64,512]{1,0:T(8,128)(2,1)S(1)} collective-permute-done((bf16[64,512]{1,0:T(8,128)(2,1)S(1)}, bf16[64,512]{1,0:T(8,128)(2,1)S(1)}, u32[]{:S(2)}, u32[]{:S(2)}) %collective-permute-start.15) | collective-permute-done | bytes 65568 | tf_op jit(solution)/shard_map/ppermute | solution.py:437
  54.3 2.0 %collective-permute-done.14.refs_2_ = bf16[64,512]{1,0:T(8,128)(2,1)S(1)} collective-permute-done((bf16[64,512]{1,0:T(8,128)(2,1)S(1)}, bf16[64,512]{1,0:T(8,128)(2,1)S(1)}, u32[]{:S(2)}, u32[]{:S(2)}) %collective-permute-start.14) | collective-permute-done | bytes 65568 | tf_op jit(solution)/shard_map/ppermute | solution.py:437
  56.3 0.0 collective-permute-done.13.refs_1_
  56.3 0.9 %finish.1 = (f32[64,1536]{1,0:T(8,128)}, f32[64,512]{1,0:T(8,128)}) custom-call(bf16[64,512]{1,0:T(8,128)(2,1)S(1)} %line_sum.1.refs_0_, bf16[64,512]{1,0:T(8,128)(2,1)S(1)} %collective-permute-done.13.refs_1_, bf16[64,512]{1,0:T(8,128)(2,1)S(1)} %collective-permute-done.14.refs_2_, bf16[64,512]{1,0:T(8,128)(2,1)S(1)} %collective-permute-done.15.refs_3_), custom_call_target="tpu_custom_call" | custom-call | bytes 786432 | tf_op jit(solution)/shard_map/finish/pallas_call | solution.py:324
  (4 shorter events, 0.0 us)
Async XLA Ops:
  0.6 1.0 %copy-start.3 = (bf16[2,6,24,512]{3,2,1,0:T(8,128)(2,1)S(1)}, bf16[2,6,24,512]{3,2,1,0:T(8,128)(2,1)}, u32[]{:S(2)}) copy-start(bf16[2,6,24,512]{3,2,1,0:T(8,128)(2,1)} %param.5) | copy-start | bytes 884740
  0.6 1.0 %copy-start.2 = (bf16[2,6,24,512]{3,2,1,0:T(8,128)(2,1)S(1)}, bf16[2,6,24,512]{3,2,1,0:T(8,128)(2,1)}, u32[]{:S(2)}) copy-start(bf16[2,6,24,512]{3,2,1,0:T(8,128)(2,1)} %param.4) | copy-start | bytes 884740
  1.7 9.7 %copy-start = (bf16[512,1536]{1,0:T(8,128)(2,1)S(1)}, bf16[512,1536]{1,0:T(8,128)(2,1)}, u32[]{:S(2)}) copy-start(bf16[512,1536]{1,0:T(8,128)(2,1)} %refs_12_.1) | copy-start | bytes 4718596
  1.7 9.7 %copy-start.1 = (bf16[512,512]{1,0:T(8,128)(2,1)S(1)}, bf16[512,512]{1,0:T(8,128)(2,1)}, u32[]{:S(2)}) copy-start(bf16[512,512]{1,0:T(8,128)(2,1)} %refs_13_.1) | copy-start | bytes 1572868
  2.6 8.8 %collective-permute-start = (bf16[72,1024]{1,0:T(8,128)(2,1)S(1)}, bf16[72,1024]{1,0:T(8,128)(2,1)S(1)}, u32[]{:S(2)}, u32[]{:S(2)}) collective-permute-start(bf16[72,1024]{1,0:T(8,128)(2,1)S(1)} %get-tuple-element.56), channel_id=1, source_target_pairs={{0,24},{1,9},{2,26},{3,11},{4,28},{5,13},{6,30},{7,15},{8,0},{9,17... | collective-permute-start | bytes 442376 | tf_op jit(solution)/shard_map/ppermute | solution.py:368
  6.5 7.9 %collective-permute-start.1 = (bf16[36,1024]{1,0:T(8,128)(2,1)S(1)}, bf16[36,1024]{1,0:T(8,128)(2,1)S(1)}, u32[]{:S(2)}, u32[]{:S(2)}) collective-permute-start(bf16[36,1024]{1,0:T(8,128)(2,1)S(1)} %get-tuple-element.64), channel_id=1, source_target_pairs={{0,7},{1,0},{2,1},{3,2},{4,3},{5,4},{6,5},{7,6},{8,15},{9,8},{10,9... | collective-permute-start | bytes 221192 | tf_op jit(solution)/shard_map/ppermute | solution.py:369
  8.3 6.1 %collective-permute-start.2 = (bf16[36,1024]{1,0:T(8,128)(2,1)S(1)}, bf16[36,1024]{1,0:T(8,128)(2,1)S(1)}, u32[]{:S(2)}, u32[]{:S(2)}) collective-permute-start(bf16[36,1024]{1,0:T(8,128)(2,1)S(1)} %get-tuple-element.65), channel_id=1, source_target_pairs={{0,24},{1,9},{2,26},{3,11},{4,28},{5,13},{6,30},{7,15},{8,0},{9,17... | collective-permute-start | bytes 221192 | tf_op jit(solution)/shard_map/ppermute | solution.py:370
  9.7 4.7 %collective-permute-start.3 = (bf16[36,1024]{1,0:T(8,128)(2,1)S(1)}, bf16[36,1024]{1,0:T(8,128)(2,1)S(1)}, u32[]{:S(2)}, u32[]{:S(2)}) collective-permute-start(bf16[36,1024]{1,0:T(8,128)(2,1)S(1)} %get-tuple-element.66), channel_id=1, source_target_pairs={{0,15},{1,24},{2,9},{3,26},{4,11},{5,28},{6,13},{7,30},{8,23},{9,0... | collective-permute-start | bytes 221192 | tf_op jit(solution)/shard_map/ppermute | solution.py:371
  17.7 2.7 %collective-permute-start.4 = (bf16[4,256,512]{2,1,0:T(8,128)(2,1)S(1)}, bf16[4,256,512]{2,1,0:T(8,128)(2,1)S(1)}, u32[]{:S(2)}, u32[]{:S(2)}) collective-permute-start(bf16[4,256,512]{2,1,0:T(8,128)(2,1)S(1)} %get-tuple-element.77), channel_id=1, source_target_pairs={{0,1},{1,0},{2,3},{3,2},{4,5},{5,4},{6,7},{7,6},{8,9},{9,8},{10,11... | collective-permute-start | bytes 3145736 | tf_op jit(solution)/shard_map/ppermute | solution.py:393
  20.7 9.2 %collective-permute-start.5 = (bf16[2,256,512]{2,1,0:T(8,128)(2,1)S(1)}, bf16[2,256,512]{2,1,0:T(8,128)(2,1)S(1)}, u32[]{:S(2)}, u32[]{:S(2)}) collective-permute-start(bf16[2,256,512]{2,1,0:T(8,128)(2,1)S(1)} %get-tuple-element.79), channel_id=1, source_target_pairs={{0,8},{1,17},{2,10},{3,19},{4,12},{5,21},{6,14},{7,23},{8,0},{9,25... | collective-permute-start | bytes 1572872 | tf_op jit(solution)/shard_map/ppermute | solution.py:411
  30.1 6.4 %collective-permute-start.9 = (bf16[1,256,512]{2,1,0:T(8,128)(2,1)S(1)}, bf16[1,256,512]{2,1,0:T(8,128)(2,1)S(1)}, u32[]{:S(2)}, u32[]{:S(2)}) collective-permute-start(bf16[1,256,512]{2,1,0:T(8,128)(2,1)S(1)} %get-tuple-element.80._), channel_id=1, source_target_pairs={{0,16},{1,9},{2,18},{3,11},{4,20},{5,13},{6,22},{7,15},{8,24},{9,1... | collective-permute-start | bytes 786440 | tf_op jit(solution)/shard_map/ppermute | solution.py:411
  31.9 8.7 %collective-permute-start.7 = (bf16[36,1024]{1,0:T(8,128)(2,1)S(1)}, bf16[36,1024]{1,0:T(8,128)(2,1)S(1)}, u32[]{:S(2)}, u32[]{:S(2)}) collective-permute-start(bf16[36,1024]{1,0:T(8,128)(2,1)S(1)} %get-tuple-element.82), channel_id=1, source_target_pairs={{7,0},{0,1},{1,2},{2,3},{3,4},{4,5},{5,6},{6,7},{15,8},{8,9},{9,10... | collective-permute-start | bytes 221192 | tf_op jit(solution)/shard_map/ppermute | solution.py:420
  32.0 9.4 %collective-permute-start.8 = (bf16[36,1024]{1,0:T(8,128)(2,1)S(1)}, bf16[36,1024]{1,0:T(8,128)(2,1)S(1)}, u32[]{:S(2)}, u32[]{:S(2)}) collective-permute-start(bf16[36,1024]{1,0:T(8,128)(2,1)S(1)} %get-tuple-element.83), channel_id=1, source_target_pairs={{15,0},{24,1},{9,2},{26,3},{11,4},{28,5},{13,6},{30,7},{23,8},{0,9... | collective-permute-start | bytes 221192 | tf_op jit(solution)/shard_map/ppermute | solution.py:419
  35.9 9.1 %collective-permute-start.6 = (bf16[108,1024]{1,0:T(8,128)(2,1)S(1)}, bf16[108,1024]{1,0:T(8,128)(2,1)S(1)}, u32[]{:S(2)}, u32[]{:S(2)}) collective-permute-start(bf16[108,1024]{1,0:T(8,128)(2,1)S(1)} %get-tuple-element.81), channel_id=1, source_target_pairs={{24,0},{9,1},{26,2},{11,3},{28,4},{13,5},{30,6},{15,7},{0,8},{17,9... | collective-permute-start | bytes 663560 | tf_op jit(solution)/shard_map/ppermute | solution.py:418
  36.6 10.1 %collective-permute-start.10 = (bf16[64,512]{1,0:T(8,128)(2,1)S(1)}, bf16[64,512]{1,0:T(8,128)(2,1)S(1)}, u32[]{:S(2)}, u32[]{:S(2)}) collective-permute-start(bf16[64,512]{1,0:T(8,128)(2,1)S(1)} %get-tuple-element.89), channel_id=1, source_target_pairs={{0,2},{1,3},{2,0},{3,1},{4,6},{5,7},{6,4},{7,5},{8,10},{9,11},{10,... | collective-permute-start | bytes 196616 | tf_op jit(solution)/shard_map/ppermute | solution.py:426
  38.9 7.8 %collective-permute-start.11 = (bf16[64,512]{1,0:T(8,128)(2,1)S(1)}, bf16[64,512]{1,0:T(8,128)(2,1)S(1)}, u32[]{:S(2)}, u32[]{:S(2)}) collective-permute-start(bf16[64,512]{1,0:T(8,128)(2,1)S(1)} %get-tuple-element.90), channel_id=1, source_target_pairs={{0,4},{1,5},{2,6},{3,7},{4,0},{5,1},{6,2},{7,3},{8,12},{9,13},{10,... | collective-permute-start | bytes 196616 | tf_op jit(solution)/shard_map/ppermute | solution.py:426
  40.6 6.1 %collective-permute-start.12 = (bf16[64,512]{1,0:T(8,128)(2,1)S(1)}, bf16[64,512]{1,0:T(8,128)(2,1)S(1)}, u32[]{:S(2)}, u32[]{:S(2)}) collective-permute-start(bf16[64,512]{1,0:T(8,128)(2,1)S(1)} %get-tuple-element.91), channel_id=1, source_target_pairs={{0,6},{1,7},{2,4},{3,5},{4,2},{5,3},{6,0},{7,1},{8,14},{9,15},{10,... | collective-permute-start | bytes 196616 | tf_op jit(solution)/shard_map/ppermute | solution.py:426
  46.8 7.5 %collective-permute-start.15 = (bf16[64,512]{1,0:T(8,128)(2,1)S(1)}, bf16[64,512]{1,0:T(8,128)(2,1)S(1)}, u32[]{:S(2)}, u32[]{:S(2)}) collective-permute-start(bf16[64,512]{1,0:T(8,128)(2,1)S(1)} %line_sum.1.refs_0_), channel_id=1, source_target_pairs={{0,24},{8,16},{16,8},{24,0},{1,25},{9,17},{17,9},{25,1},{2,26},{10... | collective-permute-start | bytes 196616 | tf_op jit(solution)/shard_map/ppermute | solution.py:437
  52.1 4.3 %collective-permute-start.14 = (bf16[64,512]{1,0:T(8,128)(2,1)S(1)}, bf16[64,512]{1,0:T(8,128)(2,1)S(1)}, u32[]{:S(2)}, u32[]{:S(2)}) collective-permute-start(bf16[64,512]{1,0:T(8,128)(2,1)S(1)} %line_sum.1.refs_0_), channel_id=1, source_target_pairs={{0,16},{8,24},{16,0},{24,8},{1,17},{9,25},{17,1},{25,9},{2,18},{10... | collective-permute-start | bytes 196616 | tf_op jit(solution)/shard_map/ppermute | solution.py:437
  52.1 4.3 %collective-permute-start.13 = (bf16[64,512]{1,0:T(8,128)(2,1)S(1)}, bf16[64,512]{1,0:T(8,128)(2,1)S(1)}, u32[]{:S(2)}, u32[]{:S(2)}) collective-permute-start(bf16[64,512]{1,0:T(8,128)(2,1)S(1)} %line_sum.1.refs_0_), channel_id=1, source_target_pairs={{0,8},{8,0},{16,24},{24,16},{1,9},{9,1},{17,25},{25,17},{2,10},{10... | collective-permute-start | bytes 196616 | tf_op jit(solution)/shard_map/ppermute | solution.py:437

commit v5 on v3

--- a/solution.py
+++ b/solution.py
@@ -21,7 +21,7 @@
 LANES = 128
 
 epsilon = 1e-05
-LONG = 5 * 10**10
+LONG = 2 * 10**9
 LOAD = 5 * 10**9
 BF = jnp.bfloat16
 F32 = jnp.float32
@@ -145,7 +145,7 @@
     one_window(both, qkv_weight, proj_weight, None, send_grad, *refs)
 
 
-def outer_kernel(own, lat_in, lon_in, diag_in, qkv_weight, proj_weight, grad_so_far, send_grad, *refs):
+def outer_kernel(own, lon_in, lat_in, diag_in, qkv_weight, proj_weight, grad_so_far, send_grad, *refs):
     last = picks(last_rows, HALF, QUARTER)
     both = jnp.concatenate(
         [
@@ -260,10 +260,8 @@
     diag_out[...] = dot(last, outer_y, NN).astype(BF)
 
 
-def place_kernel(inner_results, outer_results, lat_in, lon_in, diag_in, field_out, d_fields, placed):
-    placed[...] = jnp.zeros_like(placed)
-    width = field_out.shape[1]
-    inner_lat, outer_lat, lon, diag, inner_own, outer_own = (source for source, _ in sources())
+def place_kernel(inner_results, outer_results, lat_in, placed):
+    inner_lat, outer_lat, _, _, inner_own, outer_own = (source for source, _ in sources())
 
     def lat(v):
         return jnp.where(v < HALF, inner_lat(v), outer_lat(v - HALF))
@@ -271,16 +269,24 @@
     def only_first(source):
         return lambda v: jnp.where(v < HALF, source(v), -1)
 
-    moves = (
-        (puts(only_first(inner_own), TOKENS, WIN), inner_results),
-        (puts(only_first(outer_own), TOKENS, WIN), outer_results),
-        (puts(lat, TOKENS, HALF + QUARTER), lat_in),
-        (puts(lon, TOKENS, QUARTER), lon_in),
-        (puts(diag, TOKENS, QUARTER), diag_in),
-    )
-    for index, out in ((0, field_out), (1, d_fields)):
-        lanes = slice(index * width, (index + 1) * width)
-        out[...] = sum(dot(put, source[:, lanes], NN) for put, source in moves).astype(BF)
+    placed[...] = (
+        dot(puts(only_first(inner_own), TOKENS, WIN), inner_results[...], NN)
+        + dot(puts(only_first(outer_own), TOKENS, WIN), outer_results[...], NN)
+        + dot(puts(lat, TOKENS, HALF + QUARTER), lat_in[...], NN)
+    )
+
+
+def place_rest_kernel(placed, lon_in, diag_in, field_out, d_fields, done):
+    done[...] = jnp.zeros_like(done)
+    width = field_out.shape[1]
+    _, _, lon, diag, _, _ = (source for source, _ in sources())
+    total = (
+        placed[...]
+        + dot(puts(lon, TOKENS, QUARTER), lon_in[...], NN)
+        + dot(puts(diag, TOKENS, QUARTER), diag_in[...], NN)
+    ).astype(BF)
+    field_out[...] = total[:, :width]
+    d_fields[...] = total[:, width:]
 
 
 def halve_kernel(kept, received, send, keep):
@@ -346,6 +352,10 @@
     return lat, lon, diag
 
 
+def line_order(chips):
+    return [*range(chips // 2, chips), *range(1, chips // 2)]
+
+
 def per_device(fields, cotangent, qkv_weight, proj_weight):
     levels, row_count, col_count, width = fields.shape
     lat_size, lon_size = lax.axis_size("lat"), lax.axis_size("lon")
@@ -366,9 +376,9 @@
         name="pack", flops=LOAD,
     )
     inner_in = lax.ppermute(inner_lat, both, lat_route)
+    lon_in = lax.ppermute(lon_piece, both, lon_route)
     outer_in = lax.ppermute(outer_lat, both, lat_route)
     diag_in = lax.ppermute(diag_piece, both, diag_route)
-    lon_in = lax.ppermute(lon_piece, both, lon_route)
 
     split = (lat_size, width // 2, 4 * width // lat_size)
     per_window = [
@@ -386,7 +396,7 @@
     )
     send_grad, *outer = call(
         outer_kernel, [(split, BF), *per_window],
-        outer_own, outer_in, lon_in, diag_in, qkv_weight, proj_weight, grad_so_far,
+        outer_own, lon_in, outer_in, diag_in, qkv_weight, proj_weight, grad_so_far,
         name="outer", flops=10**9, scratch=scratch,
     )
     sibling = [(j, j ^ 1) for j in range(lon_size)]
@@ -415,7 +425,7 @@
     parts = call(line_parts_kernel, [share] * (lon_size // 2), kept, received, name="line_parts")
     arrived = [
         lax.ppermute(parts[step], "lon", [(j, j ^ (2 * step)) for j in range(lon_size)])
-        for step in range(1, lon_size // 2)
+        for step in line_order(lon_size // 2)
     ]
     lat_back, lon_back, diag_back = call(
         pack_back_kernel, [((rows, 2 * width), BF) for rows in (HALF + QUARTER, QUARTER, QUARTER)],
@@ -429,16 +439,19 @@
     shared = [
         lax.ppermute(line_sum, "lat", [(i, i ^ step) for i in range(lat_size)]) for step in range(1, lat_size)
     ]
-    field_out, d_fields, placed = call(
-        place_kernel,
+    (placed,) = call(
+        place_kernel, [((TOKENS, 2 * width), F32)], *results, lat_home, name="place"
+    )
+    field_out, d_fields, done = call(
+        place_rest_kernel,
         [((TOKENS, width), BF), ((TOKENS, width), BF), ((8, LANES), F32)],
-        *results, lat_home, lon_home, diag_home,
-        name="place",
+        placed, lon_home, diag_home,
+        name="place_rest",
     )
     qkv_grad, proj_grad = call(
         finish_kernel,
         [((rows, 3 * width), F32), ((rows, width), F32)],
-        placed, line_sum, *shared,
+        done, line_sum, *shared,
         name="finish", unread=(0,), scratch=[pltpu.VMEM((lat_size, *share[0]), F32)],
     )
     return (field_out.reshape(fields.shape), d_fields.reshape(fields.shape), qkv_grad, jnp.transpose(proj_grad))

time: 57.3 us -> 55.5 us (0.969)
  waiting for transfers between devices: 21.6 us -> 16.9 us
  starting transfers between devices: 22 us -> 24.7 us
    ppermute x1, waiting for transfers between devices: 3.39 us -> 0.01 us  [per_device(): lat_home = lax.ppermute(lat_back, both, back(lat_route))]
    ppermute x3, waiting for transfers between devices: 0.01 us -> 2.29 us  [per_device(): lax.ppermute(line_sum, 'lat', [(i, i ^ step) for i in range(lat_size)])]
    ppermute x1, starting transfers between devices: 0.01 us -> 2 us  [per_device(): lat_home = lax.ppermute(lat_back, both, back(lat_route))]
    ppermute x3, waiting for transfers between devices: 3.23 us -> 1.32 us  [per_device(): lax.ppermute(parts[step], 'lon', [(j, j ^ 2 * step) for j in range(lon_si...]
    ppermute x2, starting transfers between devices: 1.96 us -> 3.54 us  [per_device(): received = lax.ppermute(send, both, route)]
    ppermute x2, waiting for transfers between devices: 13.7 us -> 12.1 us  [per_device(): received = lax.ppermute(send, both, route)]
    ppermute x1, starting transfers between devices: 0.54 us -> 1.44 us  [per_device(): outer_in = lax.ppermute(outer_lat, both, lat_route)]
    ppermute x1, starting transfers between devices: 2.48 us -> 1.8 us  [per_device(): lon_in = lax.ppermute(lon_piece, both, lon_route)]
  transfers between devices with their start and end apart: 16 -> 16, of which waited for: 6 -> 7; matrix products, arithmetic and copies ran while one was open for 0% -> 0% of each run, Pallas kernels for 11% -> 12%
where the time goes in v5:
time: 55.5 us; the launch traced here: 55.4 us
  starting transfers between devices  24.7 us (45%)
  waiting for transfers between devices  16.9 us (30%)
  Pallas kernels  12.1 us (22%)
  local copies, waits for them, and re-layouts  0.94 us (2%)
  between operations  0.76 us (1%)
    ppermute x2, waiting for transfers between devices, per_device(): received = lax.ppermute(send, both, route)  12.1 us
    pallas_call x13, Pallas kernels, call(): pl.pallas_call(kernel, out_shape=shapes, in_specs=[anywhere if i in unrea...  12.1 us
    ppermute x3, starting transfers between devices, per_device(): lax.ppermute(parts[step], 'lon', [(j, j ^ 2 * step) for j in range(lon_si...  4.45 us
    ppermute x1, starting transfers between devices, per_device(): inner_in = lax.ppermute(inner_lat, both, lat_route)  3.94 us
    ppermute x3, starting transfers between devices, per_device(): lax.ppermute(line_sum, 'lat', [(i, i ^ step) for i in range(lat_size)])  3.71 us
    ppermute x2, starting transfers between devices, per_device(): received = lax.ppermute(send, both, route)  3.54 us
    ppermute x3, waiting for transfers between devices, per_device(): lax.ppermute(line_sum, 'lat', [(i, i ^ step) for i in range(lat_size)])  2.29 us
    ppermute x1, starting transfers between devices, per_device(): diag_home = lax.ppermute(diag_back, both, back(diag_route))  2.11 us
  transfers between devices with their start and end apart: 16, of which 7 were waited for; matrix products, arithmetic and copies ran while one was open for 0% of the time, Pallas kernels for 12%

profile of v5, /device:TPU:0, one launch (start us, length us, event | category | flops | bytes accessed | tf_op | source)
XLA Modules:
  0.0 55.4 jit_solution(13303654735153313374)
XLA Ops:
  0.6 0.0 copy-start.3
  0.7 0.1 order.1
  0.8 0.8 %copy-done.3 = bf16[2,6,24,512]{3,2,1,0:T(8,128)(2,1)S(1)} copy-done((bf16[2,6,24,512]{3,2,1,0:T(8,128)(2,1)S(1)}, bf16[2,6,24,512]{3,2,1,0:T(8,128)(2,1)}, u32[]{:S(2)}) %copy-start.3) | copy-done | bytes 294936
  1.6 0.1 copy-done.2
  1.7 0.9 %pack.1 = (bf16[72,1024]{1,0:T(8,128)(2,1)S(1)}, bf16[36,1024]{1,0:T(8,128)(2,1)S(1)}, bf16[36,1024]{1,0:T(8,128)(2,1)S(1)}, bf16[36,1024]{1,0:T(8,128)(2,1)S(1)...) custom-call(bf16[288,512]{1,0:T(8,128)(2,1)S(1)} %bitcast.5, bf16[288,512]{1,0:T(8,128)(2,1)S(1)} %bitcast.6, ...), custom_call_target="tpu_custom_call" | custom-call | flops 5000000000 | bytes 1734912 | tf_op jit(solution)/shard_map/pack/pallas_call | solution.py:330
  2.6 3.9 %collective-permute-start = (bf16[72,1024]{1,0:T(8,128)(2,1)S(1)}, bf16[72,1024]{1,0:T(8,128)(2,1)S(1)}, u32[]{:S(2)}, u32[]{:S(2)}) collective-permute-start(bf16[72,1024]{1,0:T(8,128)(2,1)S(1)} %get-tuple-element.56), channel_id=1, source_target_pairs={{0,24},{1,9},{2,26},{3,11},{4,28},{5,13},{6,30},{7,15},{8,0},{9,17... | collective-permute-start | bytes 442376 | tf_op jit(solution)/shard_map/ppermute | solution.py:378
  6.5 1.8 %collective-permute-start.1 = (bf16[36,1024]{1,0:T(8,128)(2,1)S(1)}, bf16[36,1024]{1,0:T(8,128)(2,1)S(1)}, u32[]{:S(2)}, u32[]{:S(2)}) collective-permute-start(bf16[36,1024]{1,0:T(8,128)(2,1)S(1)} %get-tuple-element.64), channel_id=1, source_target_pairs={{0,7},{1,0},{2,1},{3,2},{4,3},{5,4},{6,5},{7,6},{8,15},{9,8},{10,9... | collective-permute-start | bytes 221192 | tf_op jit(solution)/shard_map/ppermute | solution.py:379
  8.3 1.4 %collective-permute-start.2 = (bf16[36,1024]{1,0:T(8,128)(2,1)S(1)}, bf16[36,1024]{1,0:T(8,128)(2,1)S(1)}, u32[]{:S(2)}, u32[]{:S(2)}) collective-permute-start(bf16[36,1024]{1,0:T(8,128)(2,1)S(1)} %get-tuple-element.65), channel_id=1, source_target_pairs={{0,24},{1,9},{2,26},{3,11},{4,28},{5,13},{6,30},{7,15},{8,0},{9,17... | collective-permute-start | bytes 221192 | tf_op jit(solution)/shard_map/ppermute | solution.py:380
  9.7 1.6 %collective-permute-start.3 = (bf16[36,1024]{1,0:T(8,128)(2,1)S(1)}, bf16[36,1024]{1,0:T(8,128)(2,1)S(1)}, u32[]{:S(2)}, u32[]{:S(2)}) collective-permute-start(bf16[36,1024]{1,0:T(8,128)(2,1)S(1)} %get-tuple-element.66), channel_id=1, source_target_pairs={{0,15},{1,24},{2,9},{3,26},{4,11},{5,28},{6,13},{7,30},{8,23},{9,0... | collective-permute-start | bytes 221192 | tf_op jit(solution)/shard_map/ppermute | solution.py:381
  11.4 0.0 collective-permute-done.lat_in
  11.4 0.0 copy-done.1
  11.4 3.1 %inner.1 = (f32[4,256,512]{2,1,0:T(8,128)S(1)}, bf16[144,512]{1,0:T(8,128)(2,1)S(1)}, bf16[144,512]{1,0:T(8,128)(2,1)S(1)}, bf16[256,144]{1,0:T(8,128)(2,1)S(1)}...) custom-call(f32[72,1024]{1,0:T(8,128)S(1)} %get-tuple-element.55.own, ...), custom_call_target="tpu_custom_call" | custom-call | flops 1000000000 | bytes 5668864 | tf_op jit(solution)/shard_map/inner/pallas_call | solution.py:330
  14.4 0.0 collective-permute-done.1.lon_in
  14.4 0.0 collective-permute-done.2.lat_in
  14.5 0.0 collective-permute-done.3.diag_in
  14.5 3.3 %outer.1 = (bf16[4,256,512]{2,1,0:T(8,128)(2,1)S(1)}, bf16[144,512]{1,0:T(8,128)(2,1)S(1)}, bf16[144,512]{1,0:T(8,128)(2,1)S(1)}, bf16[256,144]{1,0:T(8,128)(2,1...) custom-call(f32[72,1024]{1,0:T(8,128)S(1)} %get-tuple-element.63.own, ...), custom_call_target="tpu_custom_call" | custom-call | flops 1000000000 | bytes 6791168 | tf_op jit(solution)/shard_map/outer/pallas_call | solution.py:330
  17.7 0.1 collective-permute-start.4
  17.9 1.4 %outputs.1 = (bf16[4,256,512]{2,1,0:T(8,128)(2,1)S(1)}, bf16[144,1024]{1,0:T(8,128)(2,1)S(1)}, bf16[144,1024]{1,0:T(8,128)(2,1)S(1)}) custom-call(bf16[144,512]{1,0:T(8,128)(2,1)S(1)} %get-tuple-element.57.refs_0_, bf16[144,512]{1,0:T(8,128)(2,1)S(1)} %get-tuple-element.58.refs_1_, bf16[256,144]{1,0:T(8,128)(2,1)S(1)} %get-tuple-element.59.refs_2_, ...), custom_call_target="tpu_custom_call" | custom-call | flops 1000000000 | bytes 5799936 | tf_op jit(solution)/shard_map/outputs/pallas_call | solution.py:330
  19.3 1.1 %collective-permute-done.4.received = bf16[4,256,512]{2,1,0:T(8,128)(2,1)S(1)} collective-permute-done((bf16[4,256,512]{2,1,0:T(8,128)(2,1)S(1)}, bf16[4,256,512]{2,1,0:T(8,128)(2,1)S(1)}, u32[]{:S(2)}, u32[]{:S(2)}) %collective-permute-start.4) | collective-permute-done | bytes 1048608 | tf_op jit(solution)/shard_map/ppermute | solution.py:403
  20.5 0.2 halve2.1
  20.7 2.0 %collective-permute-start.5 = (bf16[2,256,512]{2,1,0:T(8,128)(2,1)S(1)}, bf16[2,256,512]{2,1,0:T(8,128)(2,1)S(1)}, u32[]{:S(2)}, u32[]{:S(2)}) collective-permute-start(bf16[2,256,512]{2,1,0:T(8,128)(2,1)S(1)} %get-tuple-element.79), channel_id=1, source_target_pairs={{0,8},{1,17},{2,10},{3,19},{4,12},{5,21},{6,14},{7,23},{8,0},{9,25... | collective-permute-start | bytes 1572872 | tf_op jit(solution)/shard_map/ppermute | solution.py:421
  22.7 7.3 %collective-permute-done.5.received = bf16[2,256,512]{2,1,0:T(8,128)(2,1)S(1)} collective-permute-done((bf16[2,256,512]{2,1,0:T(8,128)(2,1)S(1)}, bf16[2,256,512]{2,1,0:T(8,128)(2,1)S(1)}, u32[]{:S(2)}, u32[]{:S(2)}) %collective-permute-start.5) | collective-permute-done | bytes 524320 | tf_op jit(solution)/shard_map/ppermute | solution.py:421
  30.0 0.1 halve1.1
  30.1 1.6 %collective-permute-start.6 = (bf16[1,256,512]{2,1,0:T(8,128)(2,1)S(1)}, bf16[1,256,512]{2,1,0:T(8,128)(2,1)S(1)}, u32[]{:S(2)}, u32[]{:S(2)}) collective-permute-start(bf16[1,256,512]{2,1,0:T(8,128)(2,1)S(1)} %get-tuple-element.81), channel_id=1, source_target_pairs={{0,16},{1,9},{2,18},{3,11},{4,20},{5,13},{6,22},{7,15},{8,24},{9,1... | collective-permute-start | bytes 786440 | tf_op jit(solution)/shard_map/ppermute | solution.py:421
  31.7 4.9 %collective-permute-done.6.received = bf16[1,256,512]{2,1,0:T(8,128)(2,1)S(1)} collective-permute-done((bf16[1,256,512]{2,1,0:T(8,128)(2,1)S(1)}, bf16[1,256,512]{2,1,0:T(8,128)(2,1)S(1)}, u32[]{:S(2)}, u32[]{:S(2)}) %collective-permute-start.6) | collective-permute-done | bytes 262176 | tf_op jit(solution)/shard_map/ppermute | solution.py:421
  36.5 0.1 line_parts.1
  36.6 2.8 %collective-permute-start.10 = (bf16[64,512]{1,0:T(8,128)(2,1)S(1)}, bf16[64,512]{1,0:T(8,128)(2,1)S(1)}, u32[]{:S(2)}, u32[]{:S(2)}) collective-permute-start(bf16[64,512]{1,0:T(8,128)(2,1)S(1)} %get-tuple-element.90), channel_id=1, source_target_pairs={{0,4},{1,5},{2,6},{3,7},{4,0},{5,1},{6,2},{7,3},{8,12},{9,13},{10,... | collective-permute-start | bytes 196616 | tf_op jit(solution)/shard_map/ppermute | solution.py:427
  39.4 1.2 %collective-permute-start.12 = (bf16[64,512]{1,0:T(8,128)(2,1)S(1)}, bf16[64,512]{1,0:T(8,128)(2,1)S(1)}, u32[]{:S(2)}, u32[]{:S(2)}) collective-permute-start(bf16[64,512]{1,0:T(8,128)(2,1)S(1)} %get-tuple-element.91), channel_id=1, source_target_pairs={{0,2},{1,3},{2,0},{3,1},{4,6},{5,7},{6,4},{7,5},{8,10},{9,11},{10,... | collective-permute-start | bytes 196616 | tf_op jit(solution)/shard_map/ppermute | solution.py:427
  40.6 0.4 collective-permute-start.11
  41.0 0.2 pack_back.1
  41.3 2.0 %collective-permute-start.7 = (bf16[108,1024]{1,0:T(8,128)(2,1)S(1)}, bf16[108,1024]{1,0:T(8,128)(2,1)S(1)}, u32[]{:S(2)}, u32[]{:S(2)}) collective-permute-start(bf16[108,1024]{1,0:T(8,128)(2,1)S(1)} %get-tuple-element.83), channel_id=1, source_target_pairs={{24,0},{9,1},{26,2},{11,3},{28,4},{13,5},{30,6},{15,7},{0,8},{17,9... | collective-permute-start | bytes 663560 | tf_op jit(solution)/shard_map/ppermute | solution.py:435
  43.3 0.0 collective-permute-start.8
  43.3 0.0 collective-permute-done.10.refs_1_
  43.3 2.1 %collective-permute-start.9 = (bf16[36,1024]{1,0:T(8,128)(2,1)S(1)}, bf16[36,1024]{1,0:T(8,128)(2,1)S(1)}, u32[]{:S(2)}, u32[]{:S(2)}) collective-permute-start(bf16[36,1024]{1,0:T(8,128)(2,1)S(1)} %get-tuple-element.85), channel_id=1, source_target_pairs={{15,0},{24,1},{9,2},{26,3},{11,4},{28,5},{13,6},{30,7},{23,8},{0,9... | collective-permute-start | bytes 221192 | tf_op jit(solution)/shard_map/ppermute | solution.py:436
  45.4 0.0 collective-permute-done.12.refs_3_
  45.4 1.3 %collective-permute-done.11.refs_2_ = bf16[64,512]{1,0:T(8,128)(2,1)S(1)} collective-permute-done((bf16[64,512]{1,0:T(8,128)(2,1)S(1)}, bf16[64,512]{1,0:T(8,128)(2,1)S(1)}, u32[]{:S(2)}, u32[]{:S(2)}) %collective-permute-start.11) | collective-permute-done | bytes 65568 | tf_op jit(solution)/shard_map/ppermute | solution.py:427
  46.7 3.1 %collective-permute-start.15 = (bf16[64,512]{1,0:T(8,128)(2,1)S(1)}, bf16[64,512]{1,0:T(8,128)(2,1)S(1)}, u32[]{:S(2)}, u32[]{:S(2)}) collective-permute-start(bf16[64,512]{1,0:T(8,128)(2,1)S(1)} %line_sum.1.refs_0_), channel_id=1, source_target_pairs={{0,24},{8,16},{16,8},{24,0},{1,25},{9,17},{17,9},{25,1},{2,26},{10... | collective-permute-start | bytes 196616 | tf_op jit(solution)/shard_map/ppermute | solution.py:440
  49.8 0.5 collective-permute-start.14
  50.3 0.0 collective-permute-done.7.lat_in
  50.3 0.2 collective-permute-start.13
  50.4 0.6 %place.1.placed = f32[288,1024]{1,0:T(8,128)S(1)} custom-call(bf16[144,1024]{1,0:T(8,128)(2,1)S(1)} %get-tuple-element.74.inner_results, bf16[144,1024]{1,0:T(8,128)(2,1)S(1)} %get-tuple-element.75.outer_results, bf16[108,1024]{1,0:T(8,128)(2,1)S(1)} %collective-permute-done.7.lat_in), custom_call_target="tpu_custom_call" | custom-call | bytes 1990656 | tf_op jit(solution)/shard_map/place/pallas_call | solution.py:330
  51.0 0.0 collective-permute-done.8.lon_in
  51.1 0.0 collective-permute-done.9.diag_in
  51.1 1.2 %place_rest.1 = (bf16[288,512]{1,0:T(8,128)(2,1)}, bf16[288,512]{1,0:T(8,128)(2,1)}, f32[8,128]{1,0:T(8,128)S(1)}) custom-call(f32[288,1024]{1,0:T(8,128)S(1)} %place.1.placed, bf16[36,1024]{1,0:T(8,128)(2,1)S(1)} %collective-permute-done.8.lon_in, bf16[36,1024]{1,0:T(8,128)(2,1)S(1)} %collective-permute-done.9.diag_in), custom_call_target="tpu_custom_call" | custom-call | bytes 1921024 | tf_op jit(solution)/shard_map/place_rest/pallas_call | solution.py:330
  52.3 0.5 collective-permute-done.15.refs_3_
  52.7 1.3 %collective-permute-done.14.refs_2_ = bf16[64,512]{1,0:T(8,128)(2,1)S(1)} collective-permute-done((bf16[64,512]{1,0:T(8,128)(2,1)S(1)}, bf16[64,512]{1,0:T(8,128)(2,1)S(1)}, u32[]{:S(2)}, u32[]{:S(2)}) %collective-permute-start.14) | collective-permute-done | bytes 65568 | tf_op jit(solution)/shard_map/ppermute | solution.py:440
  54.1 0.5 collective-permute-done.13.refs_1_
  54.5 0.9 %finish.1 = (f32[64,1536]{1,0:T(8,128)}, f32[64,512]{1,0:T(8,128)}) custom-call(f32[8,128]{1,0:T(8,128)S(1)} %get-tuple-element.88._, bf16[64,512]{1,0:T(8,128)(2,1)S(1)} %line_sum.1.refs_0_, bf16[64,512]{1,0:T(8,128)(2,1)S(1)} %collective-permute-done.13.refs_1_, bf16[64,512]{1,0:T(8,128)(2,1)S(1)} %collective-permute-done.14.refs_2_, ...), custom_call_target="tpu_custom_call" | custom-call | bytes 790528 | tf_op jit(solution)/shard_map/finish/pallas_call | solution.py:330
  (5 shorter events, 0.0 us)
Async XLA Ops:
  0.6 1.0 %copy-start.3 = (bf16[2,6,24,512]{3,2,1,0:T(8,128)(2,1)S(1)}, bf16[2,6,24,512]{3,2,1,0:T(8,128)(2,1)}, u32[]{:S(2)}) copy-start(bf16[2,6,24,512]{3,2,1,0:T(8,128)(2,1)} %param.5) | copy-start | bytes 884740
  0.6 1.0 %copy-start.2 = (bf16[2,6,24,512]{3,2,1,0:T(8,128)(2,1)S(1)}, bf16[2,6,24,512]{3,2,1,0:T(8,128)(2,1)}, u32[]{:S(2)}) copy-start(bf16[2,6,24,512]{3,2,1,0:T(8,128)(2,1)} %param.4) | copy-start | bytes 884740
  1.7 9.7 %copy-start = (bf16[512,1536]{1,0:T(8,128)(2,1)S(1)}, bf16[512,1536]{1,0:T(8,128)(2,1)}, u32[]{:S(2)}) copy-start(bf16[512,1536]{1,0:T(8,128)(2,1)} %refs_12_.1) | copy-start | bytes 4718596
  1.7 9.7 %copy-start.1 = (bf16[512,512]{1,0:T(8,128)(2,1)S(1)}, bf16[512,512]{1,0:T(8,128)(2,1)}, u32[]{:S(2)}) copy-start(bf16[512,512]{1,0:T(8,128)(2,1)} %refs_13_.1) | copy-start | bytes 1572868
  2.6 8.8 %collective-permute-start = (bf16[72,1024]{1,0:T(8,128)(2,1)S(1)}, bf16[72,1024]{1,0:T(8,128)(2,1)S(1)}, u32[]{:S(2)}, u32[]{:S(2)}) collective-permute-start(bf16[72,1024]{1,0:T(8,128)(2,1)S(1)} %get-tuple-element.56), channel_id=1, source_target_pairs={{0,24},{1,9},{2,26},{3,11},{4,28},{5,13},{6,30},{7,15},{8,0},{9,17... | collective-permute-start | bytes 442376 | tf_op jit(solution)/shard_map/ppermute | solution.py:378
  6.5 7.9 %collective-permute-start.1 = (bf16[36,1024]{1,0:T(8,128)(2,1)S(1)}, bf16[36,1024]{1,0:T(8,128)(2,1)S(1)}, u32[]{:S(2)}, u32[]{:S(2)}) collective-permute-start(bf16[36,1024]{1,0:T(8,128)(2,1)S(1)} %get-tuple-element.64), channel_id=1, source_target_pairs={{0,7},{1,0},{2,1},{3,2},{4,3},{5,4},{6,5},{7,6},{8,15},{9,8},{10,9... | collective-permute-start | bytes 221192 | tf_op jit(solution)/shard_map/ppermute | solution.py:379
  8.3 6.1 %collective-permute-start.2 = (bf16[36,1024]{1,0:T(8,128)(2,1)S(1)}, bf16[36,1024]{1,0:T(8,128)(2,1)S(1)}, u32[]{:S(2)}, u32[]{:S(2)}) collective-permute-start(bf16[36,1024]{1,0:T(8,128)(2,1)S(1)} %get-tuple-element.65), channel_id=1, source_target_pairs={{0,24},{1,9},{2,26},{3,11},{4,28},{5,13},{6,30},{7,15},{8,0},{9,17... | collective-permute-start | bytes 221192 | tf_op jit(solution)/shard_map/ppermute | solution.py:380
  9.7 4.7 %collective-permute-start.3 = (bf16[36,1024]{1,0:T(8,128)(2,1)S(1)}, bf16[36,1024]{1,0:T(8,128)(2,1)S(1)}, u32[]{:S(2)}, u32[]{:S(2)}) collective-permute-start(bf16[36,1024]{1,0:T(8,128)(2,1)S(1)} %get-tuple-element.66), channel_id=1, source_target_pairs={{0,15},{1,24},{2,9},{3,26},{4,11},{5,28},{6,13},{7,30},{8,23},{9,0... | collective-permute-start | bytes 221192 | tf_op jit(solution)/shard_map/ppermute | solution.py:381
  17.7 2.7 %collective-permute-start.4 = (bf16[4,256,512]{2,1,0:T(8,128)(2,1)S(1)}, bf16[4,256,512]{2,1,0:T(8,128)(2,1)S(1)}, u32[]{:S(2)}, u32[]{:S(2)}) collective-permute-start(bf16[4,256,512]{2,1,0:T(8,128)(2,1)S(1)} %get-tuple-element.77), channel_id=1, source_target_pairs={{0,1},{1,0},{2,3},{3,2},{4,5},{5,4},{6,7},{7,6},{8,9},{9,8},{10,11... | collective-permute-start | bytes 3145736 | tf_op jit(solution)/shard_map/ppermute | solution.py:403
  20.7 9.2 %collective-permute-start.5 = (bf16[2,256,512]{2,1,0:T(8,128)(2,1)S(1)}, bf16[2,256,512]{2,1,0:T(8,128)(2,1)S(1)}, u32[]{:S(2)}, u32[]{:S(2)}) collective-permute-start(bf16[2,256,512]{2,1,0:T(8,128)(2,1)S(1)} %get-tuple-element.79), channel_id=1, source_target_pairs={{0,8},{1,17},{2,10},{3,19},{4,12},{5,21},{6,14},{7,23},{8,0},{9,25... | collective-permute-start | bytes 1572872 | tf_op jit(solution)/shard_map/ppermute | solution.py:421
  30.1 6.4 %collective-permute-start.6 = (bf16[1,256,512]{2,1,0:T(8,128)(2,1)S(1)}, bf16[1,256,512]{2,1,0:T(8,128)(2,1)S(1)}, u32[]{:S(2)}, u32[]{:S(2)}) collective-permute-start(bf16[1,256,512]{2,1,0:T(8,128)(2,1)S(1)} %get-tuple-element.81), channel_id=1, source_target_pairs={{0,16},{1,9},{2,18},{3,11},{4,20},{5,13},{6,22},{7,15},{8,24},{9,1... | collective-permute-start | bytes 786440 | tf_op jit(solution)/shard_map/ppermute | solution.py:421
  36.6 6.7 %collective-permute-start.10 = (bf16[64,512]{1,0:T(8,128)(2,1)S(1)}, bf16[64,512]{1,0:T(8,128)(2,1)S(1)}, u32[]{:S(2)}, u32[]{:S(2)}) collective-permute-start(bf16[64,512]{1,0:T(8,128)(2,1)S(1)} %get-tuple-element.90), channel_id=1, source_target_pairs={{0,4},{1,5},{2,6},{3,7},{4,0},{5,1},{6,2},{7,3},{8,12},{9,13},{10,... | collective-permute-start | bytes 196616 | tf_op jit(solution)/shard_map/ppermute | solution.py:427
  39.4 6.0 %collective-permute-start.12 = (bf16[64,512]{1,0:T(8,128)(2,1)S(1)}, bf16[64,512]{1,0:T(8,128)(2,1)S(1)}, u32[]{:S(2)}, u32[]{:S(2)}) collective-permute-start(bf16[64,512]{1,0:T(8,128)(2,1)S(1)} %get-tuple-element.91), channel_id=1, source_target_pairs={{0,2},{1,3},{2,0},{3,1},{4,6},{5,7},{6,4},{7,5},{8,10},{9,11},{10,... | collective-permute-start | bytes 196616 | tf_op jit(solution)/shard_map/ppermute | solution.py:427
  40.6 6.1 %collective-permute-start.11 = (bf16[64,512]{1,0:T(8,128)(2,1)S(1)}, bf16[64,512]{1,0:T(8,128)(2,1)S(1)}, u32[]{:S(2)}, u32[]{:S(2)}) collective-permute-start(bf16[64,512]{1,0:T(8,128)(2,1)S(1)} %get-tuple-element.82._), channel_id=1, source_target_pairs={{0,6},{1,7},{2,4},{3,5},{4,2},{5,3},{6,0},{7,1},{8,14},{9,15},{10,... | collective-permute-start | bytes 196616 | tf_op jit(solution)/shard_map/ppermute | solution.py:427
  41.3 9.0 %collective-permute-start.7 = (bf16[108,1024]{1,0:T(8,128)(2,1)S(1)}, bf16[108,1024]{1,0:T(8,128)(2,1)S(1)}, u32[]{:S(2)}, u32[]{:S(2)}) collective-permute-start(bf16[108,1024]{1,0:T(8,128)(2,1)S(1)} %get-tuple-element.83), channel_id=1, source_target_pairs={{24,0},{9,1},{26,2},{11,3},{28,4},{13,5},{30,6},{15,7},{0,8},{17,9... | collective-permute-start | bytes 663560 | tf_op jit(solution)/shard_map/ppermute | solution.py:435
  43.3 7.8 %collective-permute-start.8 = (bf16[36,1024]{1,0:T(8,128)(2,1)S(1)}, bf16[36,1024]{1,0:T(8,128)(2,1)S(1)}, u32[]{:S(2)}, u32[]{:S(2)}) collective-permute-start(bf16[36,1024]{1,0:T(8,128)(2,1)S(1)} %get-tuple-element.84), channel_id=1, source_target_pairs={{7,0},{0,1},{1,2},{2,3},{3,4},{4,5},{5,6},{6,7},{15,8},{8,9},{9,10... | collective-permute-start | bytes 221192 | tf_op jit(solution)/shard_map/ppermute | solution.py:437
  43.3 7.8 %collective-permute-start.9 = (bf16[36,1024]{1,0:T(8,128)(2,1)S(1)}, bf16[36,1024]{1,0:T(8,128)(2,1)S(1)}, u32[]{:S(2)}, u32[]{:S(2)}) collective-permute-start(bf16[36,1024]{1,0:T(8,128)(2,1)S(1)} %get-tuple-element.85), channel_id=1, source_target_pairs={{15,0},{24,1},{9,2},{26,3},{11,4},{28,5},{13,6},{30,7},{23,8},{0,9... | collective-permute-start | bytes 221192 | tf_op jit(solution)/shard_map/ppermute | solution.py:436
  46.7 6.0 %collective-permute-start.15 = (bf16[64,512]{1,0:T(8,128)(2,1)S(1)}, bf16[64,512]{1,0:T(8,128)(2,1)S(1)}, u32[]{:S(2)}, u32[]{:S(2)}) collective-permute-start(bf16[64,512]{1,0:T(8,128)(2,1)S(1)} %line_sum.1.refs_0_), channel_id=1, source_target_pairs={{0,24},{8,16},{16,8},{24,0},{1,25},{9,17},{17,9},{25,1},{2,26},{10... | collective-permute-start | bytes 196616 | tf_op jit(solution)/shard_map/ppermute | solution.py:440
  49.8 4.3 %collective-permute-start.14 = (bf16[64,512]{1,0:T(8,128)(2,1)S(1)}, bf16[64,512]{1,0:T(8,128)(2,1)S(1)}, u32[]{:S(2)}, u32[]{:S(2)}) collective-permute-start(bf16[64,512]{1,0:T(8,128)(2,1)S(1)} %line_sum.1.refs_0_), channel_id=1, source_target_pairs={{0,16},{8,24},{16,0},{24,8},{1,17},{9,25},{17,1},{25,9},{2,18},{10... | collective-permute-start | bytes 196616 | tf_op jit(solution)/shard_map/ppermute | solution.py:440
  50.3 4.3 %collective-permute-start.13 = (bf16[64,512]{1,0:T(8,128)(2,1)S(1)}, bf16[64,512]{1,0:T(8,128)(2,1)S(1)}, u32[]{:S(2)}, u32[]{:S(2)}) collective-permute-start(bf16[64,512]{1,0:T(8,128)(2,1)S(1)} %line_sum.1.refs_0_), channel_id=1, source_target_pairs={{0,8},{8,0},{16,24},{24,16},{1,9},{9,1},{17,25},{25,17},{2,10},{10... | collective-permute-start | bytes 196616 | tf_op jit(solution)/shard_map/ppermute | solution.py:440

commit v6 on v5

--- a/solution.py
+++ b/solution.py
@@ -104,14 +104,6 @@
         out[:, width:] = dot(pick[...], cotangent[...], NN).astype(out.dtype)
 
 
-def normalise(x):
-    mean = jnp.mean(x, -1, keepdims=True)
-    centred = x - mean
-    variance = jnp.mean(centred * centred, -1, keepdims=True)
-    inv_std = lax.rsqrt(variance + epsilon)
-    return centred * inv_std, inv_std
-
-
 def swap_bits(index, size, core):
     bits = size.bit_length() - 1
     turned = sum(((index >> b) & 1) << (bits - 1 - b) for b in range(bits))
@@ -140,9 +132,35 @@
         out[slot] = part.astype(out.dtype)
 
 
-def inner_kernel(own, lat_in, qkv_weight, proj_weight, send_grad, *refs):
-    both = jnp.concatenate([own[...], lat_in[...].astype(F32)], axis=0)
-    one_window(both, qkv_weight, proj_weight, None, send_grad, *refs)
+def normalise(x):
+    mean = jnp.mean(x, -1, keepdims=True)
+    centred = x - mean
+    variance = jnp.mean(centred * centred, -1, keepdims=True)
+    inv_std = lax.rsqrt(variance + epsilon)
+    return centred * inv_std, inv_std
+
+
+def project(both, qkv_weight, proj_weight):
+    width = both.shape[1] // 2
+    normed, _ = normalise(both[:, :width])
+    projected = dot(normed.astype(BF), qkv_weight[...], NN)
+    return normed, projected, dot(both[:, width:].astype(BF), proj_weight[...], NT)
+
+
+def own_kernel(
+    fields, cotangent, pick_lat, pick_diag, pick_own, inner_own, qkv_weight, proj_weight,
+    outer_lat, diag, outer_own, normed, projected, d_mixed,
+):
+    pack_kernel(fields, cotangent, pick_lat, pick_diag, pick_own, outer_lat, diag, outer_own)
+    normed[...], projected[...], d_mixed[...] = project(inner_own[...], qkv_weight, proj_weight)
+
+
+def inner_kernel(own, own_normed, own_projected, own_d_mixed, lat_in, qkv_weight, proj_weight, send_grad, *refs):
+    arrived = lat_in[...].astype(F32)
+    parts = project(arrived, qkv_weight, proj_weight)
+    both = jnp.concatenate([own[...], arrived], axis=0)
+    parts = [jnp.concatenate([mine[...], part], axis=0) for mine, part in zip((own_normed, own_projected, own_d_mixed), parts)]
+    one_window(both, *parts, None, send_grad, *refs)
 
 
 def outer_kernel(own, lon_in, lat_in, diag_in, qkv_weight, proj_weight, grad_so_far, send_grad, *refs):
@@ -154,11 +172,11 @@
         ],
         axis=0,
     )
-    one_window(both, qkv_weight, proj_weight, grad_so_far, send_grad, *refs)
+    one_window(both, *project(both, qkv_weight, proj_weight), grad_so_far, send_grad, *refs)
 
 
 def one_window(
-    both, qkv_weight, proj_weight, grad_so_far,
+    both, normed, projected, d_mixed, grad_so_far,
     send_grad, windows_out, grads_out, normed_t_out, grads_t_out, d_projected, mixed, normed_t, grads_t, send_rows,
 ):
     width = both.shape[1] // 2
@@ -171,10 +189,7 @@
     windows_out[...] = x.astype(BF)
     grads = blocks[1].astype(BF)
     grads_out[...] = grads
-    normed, _ = normalise(x)
-    normed_b = normed.astype(BF)
-    projected = dot(normed_b, qkv_weight[...], NN).astype(BF)
-    d_mixed = dot(grads, proj_weight[...], NT).astype(BF)
+    projected, d_mixed = projected.astype(BF), d_mixed.astype(BF)
 
     head_size = width // HEADS
     factor = head_size ** (-0.5)
@@ -193,25 +208,31 @@
     def join_heads(block):
         return jnp.where(first_head, block[:WIN], block[WIN:]).astype(BF)
 
-    for pair in range(width // LANES):
-        at = pair * LANES
-        q = projected[:, at : at + LANES]
-        k = projected[:, width + at : width + at + LANES]
-        v = projected[:, 2 * width + at : 2 * width + at + LANES]
-        dm = d_mixed[:, at : at + LANES]
-        q2, dm2 = split_heads(q), split_heads(dm)
-        scores = dot(k, q2, NT) * factor
-        scores = jnp.where(allowed, scores, -1e30)
-        exponent = jnp.exp(scores - jnp.max(scores, 0, keepdims=True))
-        probs = exponent * (1.0 / jnp.sum(exponent, 0, keepdims=True))
-        probs_b = probs.astype(BF)
-        mixed[:, at : at + LANES] = join_heads(dot(probs_b, v, TN))
-        d_probs = dot(v, dm2, NT)
-        d_projected[:, 2 * width + at : 2 * width + at + LANES] = dot(probs_b, dm2, NN).astype(BF)
-        d_scores = probs * (d_probs - jnp.sum(d_probs * probs, 0, keepdims=True)) * factor
-        d_scores = d_scores.astype(BF)
-        d_projected[:, at : at + LANES] = join_heads(dot(d_scores, k, TN))
-        d_projected[:, width + at : width + at + LANES] = dot(d_scores, q2, NN).astype(BF)
+    pairs = range(width // LANES)
+
+    def blocks_of(array, lanes_from):
+        return [array[:, lanes_from + pair * LANES : lanes_from + (pair + 1) * LANES] for pair in pairs]
+
+    def store(out, lanes_from, blocks):
+        for pair, block in zip(pairs, blocks):
+            out[:, lanes_from + pair * LANES : lanes_from + (pair + 1) * LANES] = block.astype(out.dtype)
+
+    k, v = blocks_of(projected, width), blocks_of(projected, 2 * width)
+    q2 = [split_heads(block) for block in blocks_of(projected, 0)]
+    dm2 = [split_heads(block) for block in blocks_of(d_mixed, 0)]
+    scores = [jnp.where(allowed, dot(k[p], q2[p], NT) * factor, -1e30) for p in pairs]
+    d_probs = [dot(v[p], dm2[p], NT) for p in pairs]
+    exponents = [jnp.exp(s - jnp.max(s, 0, keepdims=True)) for s in scores]
+    probs = [e * (1.0 / jnp.sum(e, 0, keepdims=True)) for e in exponents]
+    probs_b = [p.astype(BF) for p in probs]
+    store(mixed, 0, [join_heads(dot(probs_b[p], v[p], TN)) for p in pairs])
+    store(d_projected, 2 * width, [dot(probs_b[p], dm2[p], NN) for p in pairs])
+    d_scores = [
+        (probs[p] * (d_probs[p] - jnp.sum(d_probs[p] * probs[p], 0, keepdims=True)) * factor).astype(BF)
+        for p in pairs
+    ]
+    store(d_projected, 0, [join_heads(dot(d_scores[p], k[p], TN)) for p in pairs])
+    store(d_projected, width, [dot(d_scores[p], q2[p], NN) for p in pairs])
 
     normed_t[...] = transpose_bf16(normed)
     grads_t[...] = transpose_bf16(grads)
@@ -352,10 +373,6 @@
     return lat, lon, diag
 
 
-def line_order(chips):
-    return [*range(chips // 2, chips), *range(1, chips // 2)]
-
-
 def per_device(fields, cotangent, qkv_weight, proj_weight):
     levels, row_count, col_count, width = fields.shape
     lat_size, lon_size = lax.axis_size("lat"), lax.axis_size("lon")
@@ -369,11 +386,18 @@
     own_grads = cotangent.reshape(TOKENS, width)
     lengths = (HALF, QUARTER, QUARTER, QUARTER, HALF, HALF)
     picked = call(order_kernel, [((rows, TOKENS), BF) for rows in lengths], name="order", flops=LOAD)
-    inner_lat, outer_lat, lon_piece, diag_piece, inner_own, outer_own = call(
-        pack_kernel,
-        [((rows, 2 * width), BF) for rows in lengths[:4]] + [((HALF, 2 * width), F32)] * 2,
-        own_fields, own_grads, *picked,
+    pick_inner, pick_outer, pick_lon, pick_diag, pick_own, pick_outer_own = picked
+    whole, half = ((HALF, 2 * width), F32), ((HALF, 2 * width), BF)
+    quarter = ((QUARTER, 2 * width), BF)
+    inner_lat, lon_piece, inner_own = call(
+        pack_kernel, [half, quarter, whole], own_fields, own_grads, pick_inner, pick_lon, pick_own,
         name="pack", flops=LOAD,
+    )
+    outer_lat, diag_piece, outer_own, *own_parts = call(
+        own_kernel,
+        [quarter, quarter, whole, *(((HALF, lanes), F32) for lanes in (width, 3 * width, width))],
+        own_fields, own_grads, pick_outer, pick_diag, pick_outer_own, inner_own, qkv_weight, proj_weight,
+        name="own", flops=5 * 10**8,
     )
     inner_in = lax.ppermute(inner_lat, both, lat_route)
     lon_in = lax.ppermute(lon_piece, both, lon_route)
@@ -391,7 +415,7 @@
     ]
     scratch = [pltpu.VMEM((width, WIN), BF)] * 2 + [pltpu.VMEM((width // 2, WIN), BF)]
     grad_so_far, *inner = call(
-        inner_kernel, [(split, F32), *per_window], inner_own, inner_in, qkv_weight, proj_weight,
+        inner_kernel, [(split, F32), *per_window], inner_own, *own_parts, inner_in, qkv_weight, proj_weight,
         name="inner", flops=10**9, scratch=scratch,
     )
     send_grad, *outer = call(
@@ -425,7 +449,7 @@
     parts = call(line_parts_kernel, [share] * (lon_size // 2), kept, received, name="line_parts")
     arrived = [
         lax.ppermute(parts[step], "lon", [(j, j ^ (2 * step)) for j in range(lon_size)])
-        for step in line_order(lon_size // 2)
+        for step in range(lon_size // 2 - 1, 0, -1)
     ]
     lat_back, lon_back, diag_back = call(
         pack_back_kernel, [((rows, 2 * width), BF) for rows in (HALF + QUARTER, QUARTER, QUARTER)],

time: 55.5 us -> 53.9 us (0.971)
  starting transfers between devices: 24.7 us -> 22.6 us
  waiting for transfers between devices: 16.9 us -> 18.6 us
  Pallas kernels: 12.1 us -> 11 us
    ppermute x1, starting transfers between devices: 2.11 us -> 0.14 us  [per_device(): diag_home = lax.ppermute(diag_back, both, back(diag_route))]
    ppermute x3, waiting for transfers between devices: 1.32 us -> 3.2 us  [per_device(): lax.ppermute(parts[step], 'lon', [(j, j ^ 2 * step) for j in range(lon_si...]
    ppermute x3, waiting for transfers between devices: 2.29 us -> 1.15 us  [per_device(): lax.ppermute(line_sum, 'lat', [(i, i ^ step) for i in range(lat_size)])]
    pallas_call x13 -> x14, Pallas kernels: 12.1 us -> 11 us  [call(): pl.pallas_call(kernel, out_shape=shapes, in_specs=[anywhere if i in unrea...]
where the time goes in v6:
time: 53.9 us; the launch traced here: 53.8 us
  starting transfers between devices  22.6 us (42%)
  waiting for transfers between devices  18.6 us (35%)
  Pallas kernels  11 us (20%)
  local copies, waits for them, and re-layouts  0.94 us (2%)
  between operations  0.76 us (1%)
    ppermute x2, waiting for transfers between devices, per_device(): received = lax.ppermute(send, both, route)  12.6 us
    pallas_call x14, Pallas kernels, call(): pl.pallas_call(kernel, out_shape=shapes, in_specs=[anywhere if i in unrea...  11 us
    ppermute x3, starting transfers between devices, per_device(): lax.ppermute(parts[step], 'lon', [(j, j ^ 2 * step) for j in range(lon_si...  4.45 us
    ppermute x1, starting transfers between devices, per_device(): inner_in = lax.ppermute(inner_lat, both, lat_route)  3.94 us
    ppermute x3, starting transfers between devices, per_device(): lax.ppermute(line_sum, 'lat', [(i, i ^ step) for i in range(lat_size)])  3.55 us
    ppermute x2, starting transfers between devices, per_device(): received = lax.ppermute(send, both, route)  3.42 us
    ppermute x3, waiting for transfers between devices, per_device(): lax.ppermute(parts[step], 'lon', [(j, j ^ 2 * step) for j in range(lon_si...  3.2 us
    ppermute x1, starting transfers between devices, per_device(): lat_home = lax.ppermute(lat_back, both, back(lat_route))  2.07 us
  transfers between devices with their start and end apart: 16, of which 7 were waited for; matrix products, arithmetic and copies ran while one was open for 0% of the time, Pallas kernels for 12%

profile of v6, /device:TPU:0, one launch (start us, length us, event | category | flops | bytes accessed | tf_op | source)
XLA Modules:
  0.0 53.8 jit_solution(18399526587041946543)
XLA Ops:
  0.7 0.1 order.1
  0.8 0.8 %copy-done.3 = bf16[2,6,24,512]{3,2,1,0:T(8,128)(2,1)S(1)} copy-done((bf16[2,6,24,512]{3,2,1,0:T(8,128)(2,1)S(1)}, bf16[2,6,24,512]{3,2,1,0:T(8,128)(2,1)}, u32[]{:S(2)}) %copy-start.3) | copy-done | bytes 294936
  1.6 0.1 copy-done.2
  1.7 0.5 pack.1
  2.2 3.9 %collective-permute-start = (bf16[72,1024]{1,0:T(8,128)(2,1)S(1)}, bf16[72,1024]{1,0:T(8,128)(2,1)S(1)}, u32[]{:S(2)}, u32[]{:S(2)}) collective-permute-start(bf16[72,1024]{1,0:T(8,128)(2,1)S(1)} %get-tuple-element.62), channel_id=1, source_target_pairs={{0,24},{1,9},{2,26},{3,11},{4,28},{5,13},{6,30},{7,15},{8,0},{9,17... | collective-permute-start | bytes 442376 | tf_op jit(solution)/shard_map/ppermute | solution.py:402
  6.1 1.8 %collective-permute-start.1 = (bf16[36,1024]{1,0:T(8,128)(2,1)S(1)}, bf16[36,1024]{1,0:T(8,128)(2,1)S(1)}, u32[]{:S(2)}, u32[]{:S(2)}) collective-permute-start(bf16[36,1024]{1,0:T(8,128)(2,1)S(1)} %get-tuple-element.70), channel_id=1, source_target_pairs={{0,7},{1,0},{2,1},{3,2},{4,3},{5,4},{6,5},{7,6},{8,15},{9,8},{10,9... | collective-permute-start | bytes 221192 | tf_op jit(solution)/shard_map/ppermute | solution.py:403
  8.0 0.0 copy-done.1
  8.0 0.9 %own.1 = (bf16[36,1024]{1,0:T(8,128)(2,1)S(1)}, bf16[36,1024]{1,0:T(8,128)(2,1)S(1)}, f32[72,1024]{1,0:T(8,128)S(1)}, f32[72,512]{1,0:T(8,128)S(1)}, f32[72,1536]{1,0:T(8,128)S(1)}, /*index=5*/f32[72,512]{1,0:T(8,128)S(1)}) custom-call(bf16[288,512]{1,0:T(8,128)(2,1)S(1)} %bitcast.6, bf16[288,512]{1,0:T(8,128)(2,1)S(1)} %bitcast.8, ...), custom_call_target="tpu_custom_call" | custom-call | flops 500000000 | bytes 4244480 | tf_op jit(solution)/shard_map/own/pallas_call | solution.py:351
  8.9 1.5 %collective-permute-start.2 = (bf16[36,1024]{1,0:T(8,128)(2,1)S(1)}, bf16[36,1024]{1,0:T(8,128)(2,1)S(1)}, u32[]{:S(2)}, u32[]{:S(2)}) collective-permute-start(bf16[36,1024]{1,0:T(8,128)(2,1)S(1)} %get-tuple-element.71), channel_id=1, source_target_pairs={{0,24},{1,9},{2,26},{3,11},{4,28},{5,13},{6,30},{7,15},{8,0},{9,17... | collective-permute-start | bytes 221192 | tf_op jit(solution)/shard_map/ppermute | solution.py:404
  10.4 1.6 %collective-permute-start.3 = (bf16[36,1024]{1,0:T(8,128)(2,1)S(1)}, bf16[36,1024]{1,0:T(8,128)(2,1)S(1)}, u32[]{:S(2)}, u32[]{:S(2)}) collective-permute-start(bf16[36,1024]{1,0:T(8,128)(2,1)S(1)} %get-tuple-element.72), channel_id=1, source_target_pairs={{0,15},{1,24},{2,9},{3,26},{4,11},{5,28},{6,13},{7,30},{8,23},{9,0... | collective-permute-start | bytes 221192 | tf_op jit(solution)/shard_map/ppermute | solution.py:405
  12.0 0.0 collective-permute-done.lat_in
  12.0 2.2 %inner.1 = (f32[4,256,512]{2,1,0:T(8,128)S(1)}, bf16[144,512]{1,0:T(8,128)(2,1)S(1)}, bf16[144,512]{1,0:T(8,128)(2,1)S(1)}, bf16[256,144]{1,0:T(8,128)(2,1)S(1)}...) custom-call(f32[72,1024]{1,0:T(8,128)S(1)} %get-tuple-element.55.inner_own.own, ...), custom_call_target="tpu_custom_call" | custom-call | flops 1000000000 | bytes 6406144 | tf_op jit(solution)/shard_map/inner/pallas_call | solution.py:351
  14.2 0.0 collective-permute-done.1.lon_in
  14.2 0.0 collective-permute-done.2.lat_in
  14.2 0.4 collective-permute-done.3.diag_in
  14.6 2.4 %outer.1 = (bf16[4,256,512]{2,1,0:T(8,128)(2,1)S(1)}, bf16[144,512]{1,0:T(8,128)(2,1)S(1)}, bf16[144,512]{1,0:T(8,128)(2,1)S(1)}, bf16[256,144]{1,0:T(8,128)(2,1...) custom-call(f32[72,1024]{1,0:T(8,128)S(1)} %get-tuple-element.69.own, ...), custom_call_target="tpu_custom_call" | custom-call | flops 1000000000 | bytes 6791168 | tf_op jit(solution)/shard_map/outer/pallas_call | solution.py:351
  17.1 0.1 collective-permute-start.4
  17.1 1.4 %outputs.1 = (bf16[4,256,512]{2,1,0:T(8,128)(2,1)S(1)}, bf16[144,1024]{1,0:T(8,128)(2,1)S(1)}, bf16[144,1024]{1,0:T(8,128)(2,1)S(1)}) custom-call(bf16[144,512]{1,0:T(8,128)(2,1)S(1)} %get-tuple-element.63.refs_0_, bf16[144,512]{1,0:T(8,128)(2,1)S(1)} %get-tuple-element.64.refs_1_, bf16[256,144]{1,0:T(8,128)(2,1)S(1)} %get-tuple-element.65.refs_2_, ...), custom_call_target="tpu_custom_call" | custom-call | flops 1000000000 | bytes 5799936 | tf_op jit(solution)/shard_map/outputs/pallas_call | solution.py:351
  18.6 1.2 %collective-permute-done.4.received = bf16[4,256,512]{2,1,0:T(8,128)(2,1)S(1)} collective-permute-done((bf16[4,256,512]{2,1,0:T(8,128)(2,1)S(1)}, bf16[4,256,512]{2,1,0:T(8,128)(2,1)S(1)}, u32[]{:S(2)}, u32[]{:S(2)}) %collective-permute-start.4) | collective-permute-done | bytes 1048608 | tf_op jit(solution)/shard_map/ppermute | solution.py:427
  19.8 0.2 halve2.1
  20.0 2.5 %collective-permute-start.5 = (bf16[2,256,512]{2,1,0:T(8,128)(2,1)S(1)}, bf16[2,256,512]{2,1,0:T(8,128)(2,1)S(1)}, u32[]{:S(2)}, u32[]{:S(2)}) collective-permute-start(bf16[2,256,512]{2,1,0:T(8,128)(2,1)S(1)} %get-tuple-element.85), channel_id=1, source_target_pairs={{0,8},{1,17},{2,10},{3,19},{4,12},{5,21},{6,14},{7,23},{8,0},{9,25... | collective-permute-start | bytes 1572872 | tf_op jit(solution)/shard_map/ppermute | solution.py:445
  22.5 7.2 %collective-permute-done.5.received = bf16[2,256,512]{2,1,0:T(8,128)(2,1)S(1)} collective-permute-done((bf16[2,256,512]{2,1,0:T(8,128)(2,1)S(1)}, bf16[2,256,512]{2,1,0:T(8,128)(2,1)S(1)}, u32[]{:S(2)}, u32[]{:S(2)}) %collective-permute-start.5) | collective-permute-done | bytes 524320 | tf_op jit(solution)/shard_map/ppermute | solution.py:445
  29.6 0.1 halve1.1
  29.8 1.0 %collective-permute-start.6 = (bf16[1,256,512]{2,1,0:T(8,128)(2,1)S(1)}, bf16[1,256,512]{2,1,0:T(8,128)(2,1)S(1)}, u32[]{:S(2)}, u32[]{:S(2)}) collective-permute-start(bf16[1,256,512]{2,1,0:T(8,128)(2,1)S(1)} %get-tuple-element.87), channel_id=1, source_target_pairs={{0,16},{1,9},{2,18},{3,11},{4,20},{5,13},{6,22},{7,15},{8,24},{9,1... | collective-permute-start | bytes 786440 | tf_op jit(solution)/shard_map/ppermute | solution.py:445
  30.7 5.5 %collective-permute-done.6.received = bf16[1,256,512]{2,1,0:T(8,128)(2,1)S(1)} collective-permute-done((bf16[1,256,512]{2,1,0:T(8,128)(2,1)S(1)}, bf16[1,256,512]{2,1,0:T(8,128)(2,1)S(1)}, u32[]{:S(2)}, u32[]{:S(2)}) %collective-permute-start.6) | collective-permute-done | bytes 262176 | tf_op jit(solution)/shard_map/ppermute | solution.py:445
  36.2 0.1 line_parts.1
  36.3 1.4 %collective-permute-start.11 = (bf16[64,512]{1,0:T(8,128)(2,1)S(1)}, bf16[64,512]{1,0:T(8,128)(2,1)S(1)}, u32[]{:S(2)}, u32[]{:S(2)}) collective-permute-start(bf16[64,512]{1,0:T(8,128)(2,1)S(1)} %get-tuple-element.96), channel_id=1, source_target_pairs={{0,4},{1,5},{2,6},{3,7},{4,0},{5,1},{6,2},{7,3},{8,12},{9,13},{10,... | collective-permute-start | bytes 196616 | tf_op jit(solution)/shard_map/ppermute | solution.py:451
  37.7 2.6 %collective-permute-start.12 = (bf16[64,512]{1,0:T(8,128)(2,1)S(1)}, bf16[64,512]{1,0:T(8,128)(2,1)S(1)}, u32[]{:S(2)}, u32[]{:S(2)}) collective-permute-start(bf16[64,512]{1,0:T(8,128)(2,1)S(1)} %get-tuple-element.97), channel_id=1, source_target_pairs={{0,2},{1,3},{2,0},{3,1},{4,6},{5,7},{6,4},{7,5},{8,10},{9,11},{10,... | collective-permute-start | bytes 196616 | tf_op jit(solution)/shard_map/ppermute | solution.py:451
  40.3 0.4 collective-permute-start.10
  40.7 0.2 pack_back.1
  40.9 2.1 %collective-permute-start.7 = (bf16[108,1024]{1,0:T(8,128)(2,1)S(1)}, bf16[108,1024]{1,0:T(8,128)(2,1)S(1)}, u32[]{:S(2)}, u32[]{:S(2)}) collective-permute-start(bf16[108,1024]{1,0:T(8,128)(2,1)S(1)} %get-tuple-element.89), channel_id=1, source_target_pairs={{24,0},{9,1},{26,2},{11,3},{28,4},{13,5},{30,6},{15,7},{0,8},{17,9... | collective-permute-start | bytes 663560 | tf_op jit(solution)/shard_map/ppermute | solution.py:459
  43.0 0.0 collective-permute-start.8
  43.0 0.0 collective-permute-done.11.refs_2_
  43.0 0.1 collective-permute-start.9
  43.2 0.0 collective-permute-done.12.refs_3_
  43.2 3.2 %collective-permute-done.10.refs_1_ = bf16[64,512]{1,0:T(8,128)(2,1)S(1)} collective-permute-done((bf16[64,512]{1,0:T(8,128)(2,1)S(1)}, bf16[64,512]{1,0:T(8,128)(2,1)S(1)}, u32[]{:S(2)}, u32[]{:S(2)}) %collective-permute-start.10) | collective-permute-done | bytes 65568 | tf_op jit(solution)/shard_map/ppermute | solution.py:451
  46.4 1.8 %collective-permute-start.15 = (bf16[64,512]{1,0:T(8,128)(2,1)S(1)}, bf16[64,512]{1,0:T(8,128)(2,1)S(1)}, u32[]{:S(2)}, u32[]{:S(2)}) collective-permute-start(bf16[64,512]{1,0:T(8,128)(2,1)S(1)} %line_sum.1.refs_0_), channel_id=1, source_target_pairs={{0,24},{8,16},{16,8},{24,0},{1,25},{9,17},{17,9},{25,1},{2,26},{10... | collective-permute-start | bytes 196616 | tf_op jit(solution)/shard_map/ppermute | solution.py:464
  48.2 0.5 collective-permute-start.14
  48.7 0.0 collective-permute-done.7.lat_in
  48.7 1.3 %collective-permute-start.13 = (bf16[64,512]{1,0:T(8,128)(2,1)S(1)}, bf16[64,512]{1,0:T(8,128)(2,1)S(1)}, u32[]{:S(2)}, u32[]{:S(2)}) collective-permute-start(bf16[64,512]{1,0:T(8,128)(2,1)S(1)} %line_sum.1.refs_0_), channel_id=1, source_target_pairs={{0,8},{8,0},{16,24},{24,16},{1,9},{9,1},{17,25},{25,17},{2,10},{10... | collective-permute-start | bytes 196616 | tf_op jit(solution)/shard_map/ppermute | solution.py:464
  50.0 0.6 %place.1.placed = f32[288,1024]{1,0:T(8,128)S(1)} custom-call(bf16[144,1024]{1,0:T(8,128)(2,1)S(1)} %get-tuple-element.80.inner_results, bf16[144,1024]{1,0:T(8,128)(2,1)S(1)} %get-tuple-element.81.outer_results, bf16[108,1024]{1,0:T(8,128)(2,1)S(1)} %collective-permute-done.7.lat_in), custom_call_target="tpu_custom_call" | custom-call | bytes 1990656 | tf_op jit(solution)/shard_map/place/pallas_call | solution.py:351
  50.6 0.0 collective-permute-done.8.lon_in
  50.6 0.0 collective-permute-done.9.diag_in
  50.6 1.2 %place_rest.1 = (bf16[288,512]{1,0:T(8,128)(2,1)}, bf16[288,512]{1,0:T(8,128)(2,1)}, f32[8,128]{1,0:T(8,128)S(1)}) custom-call(f32[288,1024]{1,0:T(8,128)S(1)} %place.1.placed, bf16[36,1024]{1,0:T(8,128)(2,1)S(1)} %collective-permute-done.8.lon_in, bf16[36,1024]{1,0:T(8,128)(2,1)S(1)} %collective-permute-done.9.diag_in), custom_call_target="tpu_custom_call" | custom-call | bytes 1921024 | tf_op jit(solution)/shard_map/place_rest/pallas_call | solution.py:351
  51.8 0.0 collective-permute-done.15.refs_3_
  51.8 0.7 %collective-permute-done.14.refs_2_ = bf16[64,512]{1,0:T(8,128)(2,1)S(1)} collective-permute-done((bf16[64,512]{1,0:T(8,128)(2,1)S(1)}, bf16[64,512]{1,0:T(8,128)(2,1)S(1)}, u32[]{:S(2)}, u32[]{:S(2)}) %collective-permute-start.14) | collective-permute-done | bytes 65568 | tf_op jit(solution)/shard_map/ppermute | solution.py:464
  52.5 0.4 collective-permute-done.13.refs_1_
  52.9 0.9 %finish.1 = (f32[64,1536]{1,0:T(8,128)}, f32[64,512]{1,0:T(8,128)}) custom-call(f32[8,128]{1,0:T(8,128)S(1)} %get-tuple-element.94._, bf16[64,512]{1,0:T(8,128)(2,1)S(1)} %line_sum.1.refs_0_, bf16[64,512]{1,0:T(8,128)(2,1)S(1)} %collective-permute-done.13.refs_1_, bf16[64,512]{1,0:T(8,128)(2,1)S(1)} %collective-permute-done.14.refs_2_, ...), custom_call_target="tpu_custom_call" | custom-call | bytes 790528 | tf_op jit(solution)/shard_map/finish/pallas_call | solution.py:351
  (6 shorter events, 0.0 us)
Async XLA Ops:
  0.6 1.0 %copy-start.3 = (bf16[2,6,24,512]{3,2,1,0:T(8,128)(2,1)S(1)}, bf16[2,6,24,512]{3,2,1,0:T(8,128)(2,1)}, u32[]{:S(2)}) copy-start(bf16[2,6,24,512]{3,2,1,0:T(8,128)(2,1)} %param.5) | copy-start | bytes 884740
  0.6 1.0 %copy-start.2 = (bf16[2,6,24,512]{3,2,1,0:T(8,128)(2,1)S(1)}, bf16[2,6,24,512]{3,2,1,0:T(8,128)(2,1)}, u32[]{:S(2)}) copy-start(bf16[2,6,24,512]{3,2,1,0:T(8,128)(2,1)} %param.4) | copy-start | bytes 884740
  1.7 6.3 %copy-start = (bf16[512,1536]{1,0:T(8,128)(2,1)S(1)}, bf16[512,1536]{1,0:T(8,128)(2,1)}, u32[]{:S(2)}) copy-start(bf16[512,1536]{1,0:T(8,128)(2,1)} %refs_12_.1) | copy-start | bytes 4718596
  1.7 6.3 %copy-start.1 = (bf16[512,512]{1,0:T(8,128)(2,1)S(1)}, bf16[512,512]{1,0:T(8,128)(2,1)}, u32[]{:S(2)}) copy-start(bf16[512,512]{1,0:T(8,128)(2,1)} %refs_13_.1) | copy-start | bytes 1572868
  2.2 9.8 %collective-permute-start = (bf16[72,1024]{1,0:T(8,128)(2,1)S(1)}, bf16[72,1024]{1,0:T(8,128)(2,1)S(1)}, u32[]{:S(2)}, u32[]{:S(2)}) collective-permute-start(bf16[72,1024]{1,0:T(8,128)(2,1)S(1)} %get-tuple-element.62), channel_id=1, source_target_pairs={{0,24},{1,9},{2,26},{3,11},{4,28},{5,13},{6,30},{7,15},{8,0},{9,17... | collective-permute-start | bytes 442376 | tf_op jit(solution)/shard_map/ppermute | solution.py:402
  6.1 8.1 %collective-permute-start.1 = (bf16[36,1024]{1,0:T(8,128)(2,1)S(1)}, bf16[36,1024]{1,0:T(8,128)(2,1)S(1)}, u32[]{:S(2)}, u32[]{:S(2)}) collective-permute-start(bf16[36,1024]{1,0:T(8,128)(2,1)S(1)} %get-tuple-element.70), channel_id=1, source_target_pairs={{0,7},{1,0},{2,1},{3,2},{4,3},{5,4},{6,5},{7,6},{8,15},{9,8},{10,9... | collective-permute-start | bytes 221192 | tf_op jit(solution)/shard_map/ppermute | solution.py:403
  8.9 5.3 %collective-permute-start.2 = (bf16[36,1024]{1,0:T(8,128)(2,1)S(1)}, bf16[36,1024]{1,0:T(8,128)(2,1)S(1)}, u32[]{:S(2)}, u32[]{:S(2)}) collective-permute-start(bf16[36,1024]{1,0:T(8,128)(2,1)S(1)} %get-tuple-element.71), channel_id=1, source_target_pairs={{0,24},{1,9},{2,26},{3,11},{4,28},{5,13},{6,30},{7,15},{8,0},{9,17... | collective-permute-start | bytes 221192 | tf_op jit(solution)/shard_map/ppermute | solution.py:404
  10.4 4.2 %collective-permute-start.3 = (bf16[36,1024]{1,0:T(8,128)(2,1)S(1)}, bf16[36,1024]{1,0:T(8,128)(2,1)S(1)}, u32[]{:S(2)}, u32[]{:S(2)}) collective-permute-start(bf16[36,1024]{1,0:T(8,128)(2,1)S(1)} %get-tuple-element.72), channel_id=1, source_target_pairs={{0,15},{1,24},{2,9},{3,26},{4,11},{5,28},{6,13},{7,30},{8,23},{9,0... | collective-permute-start | bytes 221192 | tf_op jit(solution)/shard_map/ppermute | solution.py:405
  17.1 2.7 %collective-permute-start.4 = (bf16[4,256,512]{2,1,0:T(8,128)(2,1)S(1)}, bf16[4,256,512]{2,1,0:T(8,128)(2,1)S(1)}, u32[]{:S(2)}, u32[]{:S(2)}) collective-permute-start(bf16[4,256,512]{2,1,0:T(8,128)(2,1)S(1)} %get-tuple-element.83), channel_id=1, source_target_pairs={{0,1},{1,0},{2,3},{3,2},{4,5},{5,4},{6,7},{7,6},{8,9},{9,8},{10,11... | collective-permute-start | bytes 3145736 | tf_op jit(solution)/shard_map/ppermute | solution.py:427
  20.0 9.6 %collective-permute-start.5 = (bf16[2,256,512]{2,1,0:T(8,128)(2,1)S(1)}, bf16[2,256,512]{2,1,0:T(8,128)(2,1)S(1)}, u32[]{:S(2)}, u32[]{:S(2)}) collective-permute-start(bf16[2,256,512]{2,1,0:T(8,128)(2,1)S(1)} %get-tuple-element.85), channel_id=1, source_target_pairs={{0,8},{1,17},{2,10},{3,19},{4,12},{5,21},{6,14},{7,23},{8,0},{9,25... | collective-permute-start | bytes 1572872 | tf_op jit(solution)/shard_map/ppermute | solution.py:445
  29.8 6.4 %collective-permute-start.6 = (bf16[1,256,512]{2,1,0:T(8,128)(2,1)S(1)}, bf16[1,256,512]{2,1,0:T(8,128)(2,1)S(1)}, u32[]{:S(2)}, u32[]{:S(2)}) collective-permute-start(bf16[1,256,512]{2,1,0:T(8,128)(2,1)S(1)} %get-tuple-element.87), channel_id=1, source_target_pairs={{0,16},{1,9},{2,18},{3,11},{4,20},{5,13},{6,22},{7,15},{8,24},{9,1... | collective-permute-start | bytes 786440 | tf_op jit(solution)/shard_map/ppermute | solution.py:445
  36.3 6.8 %collective-permute-start.11 = (bf16[64,512]{1,0:T(8,128)(2,1)S(1)}, bf16[64,512]{1,0:T(8,128)(2,1)S(1)}, u32[]{:S(2)}, u32[]{:S(2)}) collective-permute-start(bf16[64,512]{1,0:T(8,128)(2,1)S(1)} %get-tuple-element.96), channel_id=1, source_target_pairs={{0,4},{1,5},{2,6},{3,7},{4,0},{5,1},{6,2},{7,3},{8,12},{9,13},{10,... | collective-permute-start | bytes 196616 | tf_op jit(solution)/shard_map/ppermute | solution.py:451
  37.7 5.5 %collective-permute-start.12 = (bf16[64,512]{1,0:T(8,128)(2,1)S(1)}, bf16[64,512]{1,0:T(8,128)(2,1)S(1)}, u32[]{:S(2)}, u32[]{:S(2)}) collective-permute-start(bf16[64,512]{1,0:T(8,128)(2,1)S(1)} %get-tuple-element.97), channel_id=1, source_target_pairs={{0,2},{1,3},{2,0},{3,1},{4,6},{5,7},{6,4},{7,5},{8,10},{9,11},{10,... | collective-permute-start | bytes 196616 | tf_op jit(solution)/shard_map/ppermute | solution.py:451
  40.3 6.1 %collective-permute-start.10 = (bf16[64,512]{1,0:T(8,128)(2,1)S(1)}, bf16[64,512]{1,0:T(8,128)(2,1)S(1)}, u32[]{:S(2)}, u32[]{:S(2)}) collective-permute-start(bf16[64,512]{1,0:T(8,128)(2,1)S(1)} %get-tuple-element.88._), channel_id=1, source_target_pairs={{0,6},{1,7},{2,4},{3,5},{4,2},{5,3},{6,0},{7,1},{8,14},{9,15},{10,... | collective-permute-start | bytes 196616 | tf_op jit(solution)/shard_map/ppermute | solution.py:451
  40.9 7.7 %collective-permute-start.7 = (bf16[108,1024]{1,0:T(8,128)(2,1)S(1)}, bf16[108,1024]{1,0:T(8,128)(2,1)S(1)}, u32[]{:S(2)}, u32[]{:S(2)}) collective-permute-start(bf16[108,1024]{1,0:T(8,128)(2,1)S(1)} %get-tuple-element.89), channel_id=1, source_target_pairs={{24,0},{9,1},{26,2},{11,3},{28,4},{13,5},{30,6},{15,7},{0,8},{17,9... | collective-permute-start | bytes 663560 | tf_op jit(solution)/shard_map/ppermute | solution.py:459
  43.0 7.6 %collective-permute-start.8 = (bf16[36,1024]{1,0:T(8,128)(2,1)S(1)}, bf16[36,1024]{1,0:T(8,128)(2,1)S(1)}, u32[]{:S(2)}, u32[]{:S(2)}) collective-permute-start(bf16[36,1024]{1,0:T(8,128)(2,1)S(1)} %get-tuple-element.90), channel_id=1, source_target_pairs={{7,0},{0,1},{1,2},{2,3},{3,4},{4,5},{5,6},{6,7},{15,8},{8,9},{9,10... | collective-permute-start | bytes 221192 | tf_op jit(solution)/shard_map/ppermute | solution.py:461
  43.0 7.6 %collective-permute-start.9 = (bf16[36,1024]{1,0:T(8,128)(2,1)S(1)}, bf16[36,1024]{1,0:T(8,128)(2,1)S(1)}, u32[]{:S(2)}, u32[]{:S(2)}) collective-permute-start(bf16[36,1024]{1,0:T(8,128)(2,1)S(1)} %get-tuple-element.91), channel_id=1, source_target_pairs={{15,0},{24,1},{9,2},{26,3},{11,4},{28,5},{13,6},{30,7},{23,8},{0,9... | collective-permute-start | bytes 221192 | tf_op jit(solution)/shard_map/ppermute | solution.py:460
  46.4 5.4 %collective-permute-start.15 = (bf16[64,512]{1,0:T(8,128)(2,1)S(1)}, bf16[64,512]{1,0:T(8,128)(2,1)S(1)}, u32[]{:S(2)}, u32[]{:S(2)}) collective-permute-start(bf16[64,512]{1,0:T(8,128)(2,1)S(1)} %line_sum.1.refs_0_), channel_id=1, source_target_pairs={{0,24},{8,16},{16,8},{24,0},{1,25},{9,17},{17,9},{25,1},{2,26},{10... | collective-permute-start | bytes 196616 | tf_op jit(solution)/shard_map/ppermute | solution.py:464
  48.2 4.3 %collective-permute-start.14 = (bf16[64,512]{1,0:T(8,128)(2,1)S(1)}, bf16[64,512]{1,0:T(8,128)(2,1)S(1)}, u32[]{:S(2)}, u32[]{:S(2)}) collective-permute-start(bf16[64,512]{1,0:T(8,128)(2,1)S(1)} %line_sum.1.refs_0_), channel_id=1, source_target_pairs={{0,16},{8,24},{16,0},{24,8},{1,17},{9,25},{17,1},{25,9},{2,18},{10... | collective-permute-start | bytes 196616 | tf_op jit(solution)/shard_map/ppermute | solution.py:464
  48.7 4.3 %collective-permute-start.13 = (bf16[64,512]{1,0:T(8,128)(2,1)S(1)}, bf16[64,512]{1,0:T(8,128)(2,1)S(1)}, u32[]{:S(2)}, u32[]{:S(2)}) collective-permute-start(bf16[64,512]{1,0:T(8,128)(2,1)S(1)} %line_sum.1.refs_0_), channel_id=1, source_target_pairs={{0,8},{8,0},{16,24},{24,16},{1,9},{9,1},{17,25},{25,17},{2,10},{10... | collective-permute-start | bytes 196616 | tf_op jit(solution)/shard_map/ppermute | solution.py:464

commit v7 on v6

--- a/solution.py
+++ b/solution.py
@@ -21,7 +21,7 @@
 LANES = 128
 
 epsilon = 1e-05
-LONG = 2 * 10**9
+LONG = 13 * 10**8
 LOAD = 5 * 10**9
 BF = jnp.bfloat16
 F32 = jnp.float32
@@ -122,14 +122,15 @@
     return jnp.transpose(block.astype(F32)).astype(BF)
 
 
-def put_split(out, lanes_from, block, lat, core, so_far=None):
-    size, _, width = out.shape
-    for at in range(0, block.shape[1], width):
-        slot = swap_bits(lat ^ ((lanes_from + at) // width), size, core)
-        part = block[:, at : at + width]
-        if so_far is not None:
-            part = part + so_far[slot]
-        out[slot] = part.astype(out.dtype)
+def slot_product(slot, size, lat, core, windows):
+    share = lat ^ swap_bits(slot, size, core)
+    total = None
+    for left, right in windows:
+        lanes = right.shape[1] // size
+        of_proj = (share >= 3 * size // 4).astype(jnp.int32)
+        part = dot(left[of_proj], right[:, pl.ds(pl.multiple_of(share * lanes, lanes), lanes)], NN)
+        total = part if total is None else total + part
+    return total
 
 
 def normalise(x):
@@ -159,11 +160,16 @@
     arrived = lat_in[...].astype(F32)
     parts = project(arrived, qkv_weight, proj_weight)
     both = jnp.concatenate([own[...], arrived], axis=0)
-    parts = [jnp.concatenate([mine[...], part], axis=0) for mine, part in zip((own_normed, own_projected, own_d_mixed), parts)]
-    one_window(both, *parts, None, send_grad, *refs)
-
-
-def outer_kernel(own, lon_in, lat_in, diag_in, qkv_weight, proj_weight, grad_so_far, send_grad, *refs):
+    mine = own_normed, own_projected, own_d_mixed
+    parts = [jnp.concatenate([first[...], second], axis=0) for first, second in zip(mine, parts)]
+    one_window(both, *parts, *refs)
+    *_, right, left, _, _ = refs
+    lat, core, size = place()
+    for slot in range(size):
+        send_grad[slot] = slot_product(slot, size, lat, 1 - core, [(left, right)])
+
+
+def outer_kernel(own, lon_in, lat_in, diag_in, qkv_weight, proj_weight, grad_so_far, send_first, send_rest, *refs):
     last = picks(last_rows, HALF, QUARTER)
     both = jnp.concatenate(
         [
@@ -172,17 +178,29 @@
         ],
         axis=0,
     )
-    one_window(both, *project(both, qkv_weight, proj_weight), grad_so_far, send_grad, *refs)
+    one_window(both, *project(both, qkv_weight, proj_weight), *refs)
+    *_, right, left, _, _ = refs
+    lat, core, size = place()
+    for slot in first_order(size):
+        total = grad_so_far[slot] + slot_product(slot, size, lat, 1 - core, [(left, right)])
+        (send_first if slot % 2 else send_rest)[slot // 2] = total.astype(BF)
+
+
+def place():
+    return lax.axis_index("lat"), lax.rem(lax.axis_index("lon"), 2), lax.axis_size("lat")
+
+
+def first_order(size):
+    return [*range(1, size, 2), *range(0, size, 2)]
 
 
 def one_window(
-    both, normed, projected, d_mixed, grad_so_far,
-    send_grad, windows_out, grads_out, normed_t_out, grads_t_out, d_projected, mixed, normed_t, grads_t, send_rows,
+    both, normed, projected, d_mixed,
+    windows_out, grads_out, left_keep, right, left_send, normed_t, grads_t,
 ):
     width = both.shape[1] // 2
-    lat, lon = lax.axis_index("lat"), lax.axis_index("lon")
-    lat_size, lon_size = lax.axis_size("lat"), lax.axis_size("lon")
-    core = lax.rem(lon, 2)
+    lat, core, lat_size = place()
+    lon, lon_size = lax.axis_index("lon"), lax.axis_size("lon")
     even = core == 0
     blocks = both[:, :width], both[:, width:]
     x = blocks[0]
@@ -225,37 +243,38 @@
     exponents = [jnp.exp(s - jnp.max(s, 0, keepdims=True)) for s in scores]
     probs = [e * (1.0 / jnp.sum(e, 0, keepdims=True)) for e in exponents]
     probs_b = [p.astype(BF) for p in probs]
-    store(mixed, 0, [join_heads(dot(probs_b[p], v[p], TN)) for p in pairs])
-    store(d_projected, 2 * width, [dot(probs_b[p], dm2[p], NN) for p in pairs])
+    store(right, 3 * width, [join_heads(dot(probs_b[p], v[p], TN)) for p in pairs])
+    store(right, 2 * width, [dot(probs_b[p], dm2[p], NN) for p in pairs])
     d_scores = [
         (probs[p] * (d_probs[p] - jnp.sum(d_probs[p] * probs[p], 0, keepdims=True)) * factor).astype(BF)
         for p in pairs
     ]
-    store(d_projected, 0, [join_heads(dot(d_scores[p], k[p], TN)) for p in pairs])
-    store(d_projected, width, [dot(d_scores[p], q2[p], NN) for p in pairs])
+    store(right, 0, [join_heads(dot(d_scores[p], k[p], TN)) for p in pairs])
+    store(right, width, [dot(d_scores[p], q2[p], NN) for p in pairs])
 
     normed_t[...] = transpose_bf16(normed)
     grads_t[...] = transpose_bf16(grads)
-    shares(normed_t, send_rows, lon, 1 - core, lon_size)
-    put_split(send_grad, 0, dot(send_rows[...], d_projected[...], NN), lat, 1 - core, grad_so_far)
-    shares(grads_t, send_rows, lon, 1 - core, lon_size)
-    put_split(send_grad, 3 * width, dot(send_rows[...], mixed[...], NN), lat, 1 - core, grad_so_far)
-    shares(normed_t, normed_t_out, lon, core, lon_size)
-    shares(grads_t, grads_t_out, lon, core, lon_size)
-
-
-def output_kernel(*refs):
-    (*windows, qkv_weight, proj_weight, keep_grad, inner_results, outer_results) = refs
-    per_window = windows[:6], windows[6:]
-    lat, core = lax.axis_index("lat"), lax.rem(lax.axis_index("lon"), 2)
+    for index, source in enumerate((normed_t, grads_t)):
+        shares(source, left_send.at[index], lon, 1 - core, lon_size)
+        shares(source, left_keep.at[index], lon, core, lon_size)
+
+
+def keep_kernel(inner_left, inner_right, outer_left, outer_right, keep_first):
+    lat, core, size = place()
+    windows = [(inner_left, inner_right), (outer_left, outer_right)]
+    for slot in range(1, size, 2):
+        keep_first[slot // 2] = slot_product(slot, size, lat, core, windows).astype(BF)
+
+
+def output_kernel(_, *refs):
+    (*windows, qkv_weight, proj_weight, keep_rest, inner_results, outer_results) = refs
+    per_window = windows[:4], windows[4:]
+    lat, core, size = place()
     width = proj_weight.shape[0]
-    qkv_grad = sum(dot(w[2][...], w[4][...], NN) for w in per_window)
-    proj_grad = sum(dot(w[3][...], w[5][...], NN) for w in per_window)
-    put_split(keep_grad, 0, qkv_grad, lat, core)
-    put_split(keep_grad, 3 * width, proj_grad, lat, core)
-    x, grads, d_projected, mixed = (
-        jnp.concatenate([w[i][...] for w in per_window], axis=0) for i in (0, 1, 4, 5)
-    )
+    for slot in range(0, size, 2):
+        keep_rest[slot // 2] = slot_product(slot, size, lat, core, [w[2:] for w in per_window]).astype(BF)
+    x, grads, right = (jnp.concatenate([w[i][...] for w in per_window], axis=0) for i in (0, 1, 3))
+    d_projected, mixed = right[:, : 3 * width], right[:, 3 * width :]
     x = x.astype(F32)
     normed, inv_std = normalise(x)
     output = (x + dot(mixed, proj_weight[...], NN)).astype(BF)
@@ -271,14 +290,16 @@
         out[:, width:] = d_inputs[at : at + WIN]
 
 
-def pack_back_kernel(_, inner_results, outer_results, lat_out, lon_out, diag_out):
+def pack_lon_kernel(outer_results, lon_out):
+    outer_x = outer_results[...].astype(F32)[:HALF].astype(BF)
+    lon_out[...] = dot(puts(last_rows, QUARTER, HALF), outer_x, NN).astype(BF)
+
+
+def pack_back_kernel(_, inner_results, outer_results, lat_out, diag_out):
     inner_y = inner_results[...].astype(F32)[HALF:]
-    outer = outer_results[...].astype(F32)
-    outer_x, outer_y = outer[:HALF].astype(BF), outer[HALF:].astype(BF)
-    first, last = puts(first_rows, QUARTER, HALF), puts(last_rows, QUARTER, HALF)
-    lat_out[...] = jnp.concatenate([inner_y, dot(first, outer_y, NN)], axis=0).astype(BF)
-    lon_out[...] = dot(last, outer_x, NN).astype(BF)
-    diag_out[...] = dot(last, outer_y, NN).astype(BF)
+    outer_y = outer_results[...].astype(F32)[HALF:].astype(BF)
+    lat_out[...] = jnp.concatenate([inner_y, dot(puts(first_rows, QUARTER, HALF), outer_y, NN)], axis=0).astype(BF)
+    diag_out[...] = dot(puts(last_rows, QUARTER, HALF), outer_y, NN).astype(BF)
 
 
 def place_kernel(inner_results, outer_results, lat_in, placed):
@@ -310,17 +331,19 @@
     d_fields[...] = total[:, width:]
 
 
-def halve_kernel(kept, received, send, keep):
+def halve_kernel(_, *refs):
+    *parts, send, keep = refs
     for slot in range(send.shape[0]):
         for out, source in ((send, 2 * slot + 1), (keep, 2 * slot)):
-            out[slot] = (kept[source].astype(F32) + received[source].astype(F32)).astype(BF)
-
-
-def line_parts_kernel(kept, received, keep, *sends):
+            out[slot] = sum(part[source].astype(F32) for part in parts).astype(BF)
+
+
+def line_parts_kernel(count, *refs):
+    parts, (keep, *sends) = refs[:count], refs[count:]
     rows = keep.shape[0]
     for step, out in enumerate((keep, *sends)):
         at = slice(step * rows, (step + 1) * rows)
-        out[...] = (kept[0, at].astype(F32) + received[0, at].astype(F32)).astype(out.dtype)
+        out[...] = sum(part[0, at].astype(F32) for part in parts).astype(out.dtype)
 
 
 def sum_kernel(*refs):
@@ -405,60 +428,70 @@
     diag_in = lax.ppermute(diag_piece, both, diag_route)
 
     split = (lat_size, width // 2, 4 * width // lat_size)
+    halves = ((lat_size // 2, *split[1:]), BF)
     per_window = [
         ((WIN, width), BF),
         ((WIN, width), BF),
-        ((width // 2, WIN), BF),
-        ((width // 2, WIN), BF),
-        ((WIN, 3 * width), BF),
-        ((WIN, width), BF),
+        ((2, width // 2, WIN), BF),
+        ((WIN, 4 * width), BF),
     ]
-    scratch = [pltpu.VMEM((width, WIN), BF)] * 2 + [pltpu.VMEM((width // 2, WIN), BF)]
+    scratch = [pltpu.VMEM((2, width // 2, WIN), BF)] + [pltpu.VMEM((width, WIN), BF)] * 2
     grad_so_far, *inner = call(
         inner_kernel, [(split, F32), *per_window], inner_own, *own_parts, inner_in, qkv_weight, proj_weight,
         name="inner", flops=10**9, scratch=scratch,
     )
-    send_grad, *outer = call(
-        outer_kernel, [(split, BF), *per_window],
+    send_first, send_rest, *outer = call(
+        outer_kernel, [halves, halves, *per_window],
         outer_own, lon_in, outer_in, diag_in, qkv_weight, proj_weight, grad_so_far,
         name="outer", flops=10**9, scratch=scratch,
     )
     sibling = [(j, j ^ 1) for j in range(lon_size)]
-    received = lax.ppermute(send_grad, "lon", sibling)
-    kept, *results = call(
-        output_kernel, [(split, BF), ((WIN, 2 * width), BF), ((WIN, 2 * width), BF)],
-        *inner, *outer, qkv_weight, proj_weight,
-        name="outputs", flops=10**9,
-    )
-
-    slots = lat_size
-    bits = lat_size.bit_length() - 1
-    for phase in range(bits):
-        slots //= 2
-        half = ((slots, *split[1:]), BF)
-        send, kept = call(halve_kernel, [half, half], kept, received, name=f"halve{slots}")
+    received_first = lax.ppermute(send_first, "lon", sibling)
+    received_rest = lax.ppermute(send_rest, "lon", sibling)
+    (keep_first,) = call(keep_kernel, [halves], *inner[2:], *outer[2:], name="keep", flops=10**9)
+
+    def halving(phase, send):
         route = [
             (i * lon_size + j, (i ^ (1 << (phase if j % 2 == 0 else bits - 1 - phase))) * lon_size + j)
             for i in range(lat_size)
             for j in range(lon_size)
         ]
-        received = lax.ppermute(send, both, route)
+        return lax.ppermute(send, both, route)
+
+    bits = lat_size.bit_length() - 1
+    (send,) = call(sum_kernel, [halves], keep_first, received_first, name="chip_sum")
+    received = halving(0, send)
+    keep_rest, *results = call(
+        output_kernel, [halves, ((WIN, 2 * width), BF), ((WIN, 2 * width), BF)],
+        send, *inner, *outer, qkv_weight, proj_weight,
+        name="outputs", flops=10**9, unread=(0,),
+    )
+    (lon_back,) = call(pack_lon_kernel, [quarter], results[1], name="pack_lon")
+    lon_home = lax.ppermute(lon_back, both, back(lon_route))
+    kept = [keep_rest, received_rest, received]
+    slots = lat_size // 2
+    for phase in range(1, bits):
+        slots //= 2
+        stay = ((slots, *split[1:]), BF)
+        send, keep = call(halve_kernel, [stay, stay], lon_home, *kept, name=f"halve{slots}", unread=(0,))
+        kept = [keep, halving(phase, send)]
 
     rows = width // lon_size
     share = ((rows, split[2]), BF)
-    parts = call(line_parts_kernel, [share] * (lon_size // 2), kept, received, name="line_parts")
+    parts = call(
+        functools.partial(line_parts_kernel, len(kept)), [share] * (lon_size // 2), *kept, name="line_parts"
+    )
     arrived = [
         lax.ppermute(parts[step], "lon", [(j, j ^ (2 * step)) for j in range(lon_size)])
         for step in range(lon_size // 2 - 1, 0, -1)
     ]
-    lat_back, lon_back, diag_back = call(
-        pack_back_kernel, [((rows, 2 * width), BF) for rows in (HALF + QUARTER, QUARTER, QUARTER)],
-        parts[-1], *results,
+    lat_back, diag_back = call(
+        pack_back_kernel, [((HALF + QUARTER, 2 * width), BF), quarter],
+        parts[1], *results,
         name="pack_back", unread=(0,),
     )
     lat_home = lax.ppermute(lat_back, both, back(lat_route))
     diag_home = lax.ppermute(diag_back, both, back(diag_route))
-    lon_home = lax.ppermute(lon_back, both, back(lon_route))
     (line_sum,) = call(sum_kernel, [share], parts[0], *arrived, name="line_sum", flops=LONG)
     shared = [
         lax.ppermute(line_sum, "lat", [(i, i ^ step) for i in range(lat_size)]) for step in range(1, lat_size)

time: 53.9 us -> 52.4 us (0.972)
  waiting for transfers between devices: 18.6 us -> 16.4 us
    ppermute x3 -> x4, waiting for transfers between devices: 13.8 us -> 6.56 us  [the longest x2 5.58 us: halving(): return lax.ppermute(send, both, route)]
    ppermute x1, waiting for transfers between devices: 0.01 us -> 5.64 us  [per_device(): lon_home = lax.ppermute(lon_back, both, back(lon_route))]
    ppermute x3, waiting for transfers between devices: 3.2 us -> 2.11 us  [per_device(): lax.ppermute(parts[step], 'lon', [(j, j ^ 2 * step) for j in range(lon_si...]
    ppermute x3 -> x4, starting transfers between devices: 3.5 us -> 3.99 us  [the longest x2 3.42 us: halving(): return lax.ppermute(send, both, route)]
    pallas_call x14 -> x16, Pallas kernels: 11 us -> 11.3 us  [call(): pl.pallas_call(kernel, out_shape=shapes, in_specs=[anywhere if i in unrea...]
  transfers between devices with their start and end apart: 16 -> 17, of which waited for: 7 -> 11; matrix products, arithmetic and copies ran while one was open for 0% -> 0% of each run, Pallas kernels for 12% -> 14%
where the time goes in v7:
time: 52.4 us; the launch traced here: 52.3 us
  starting transfers between devices  23 us (44%)
  waiting for transfers between devices  16.4 us (31%)
  Pallas kernels  11.3 us (22%)
  local copies, waits for them, and re-layouts  0.94 us (2%)
  between operations  0.77 us (1%)
    pallas_call x16, Pallas kernels, call(): pl.pallas_call(kernel, out_shape=shapes, in_specs=[anywhere if i in unrea...  11.3 us
    ppermute x1, waiting for transfers between devices, per_device(): lon_home = lax.ppermute(lon_back, both, back(lon_route))  5.64 us
    ppermute x2, waiting for transfers between devices, halving(): return lax.ppermute(send, both, route)  5.58 us
    ppermute x3, starting transfers between devices, per_device(): lax.ppermute(parts[step], 'lon', [(j, j ^ 2 * step) for j in range(lon_si...  4.45 us
    ppermute x1, starting transfers between devices, per_device(): inner_in = lax.ppermute(inner_lat, both, lat_route)  3.94 us
    ppermute x3, starting transfers between devices, per_device(): lax.ppermute(line_sum, 'lat', [(i, i ^ step) for i in range(lat_size)])  3.55 us
    ppermute x2, starting transfers between devices, halving(): return lax.ppermute(send, both, route)  3.42 us
    ppermute x3, waiting for transfers between devices, per_device(): lax.ppermute(parts[step], 'lon', [(j, j ^ 2 * step) for j in range(lon_si...  2.11 us
  transfers between devices with their start and end apart: 17, of which 11 were waited for; matrix products, arithmetic and copies ran while one was open for 0% of the time, Pallas kernels for 14%

profile of v7, /device:TPU:0, one launch (start us, length us, event | category | flops | bytes accessed | tf_op | source)
XLA Modules:
  0.0 52.3 jit_solution(4178338077015065913)
XLA Ops:
  0.7 0.1 order.1
  0.8 0.8 %copy-done.3 = bf16[2,6,24,512]{3,2,1,0:T(8,128)(2,1)S(1)} copy-done((bf16[2,6,24,512]{3,2,1,0:T(8,128)(2,1)S(1)}, bf16[2,6,24,512]{3,2,1,0:T(8,128)(2,1)}, u32[]{:S(2)}) %copy-start.3) | copy-done | bytes 294936
  1.6 0.1 copy-done.2
  1.7 0.5 pack.1
  2.2 3.9 %collective-permute-start = (bf16[72,1024]{1,0:T(8,128)(2,1)S(1)}, bf16[72,1024]{1,0:T(8,128)(2,1)S(1)}, u32[]{:S(2)}, u32[]{:S(2)}) collective-permute-start(bf16[72,1024]{1,0:T(8,128)(2,1)S(1)} %get-tuple-element.56), channel_id=1, source_target_pairs={{0,24},{1,9},{2,26},{3,11},{4,28},{5,13},{6,30},{7,15},{8,0},{9,17... | collective-permute-start | bytes 442376 | tf_op jit(solution)/shard_map/ppermute | solution.py:425
  6.1 1.8 %collective-permute-start.1 = (bf16[36,1024]{1,0:T(8,128)(2,1)S(1)}, bf16[36,1024]{1,0:T(8,128)(2,1)S(1)}, u32[]{:S(2)}, u32[]{:S(2)}) collective-permute-start(bf16[36,1024]{1,0:T(8,128)(2,1)S(1)} %get-tuple-element.60), channel_id=1, source_target_pairs={{0,7},{1,0},{2,1},{3,2},{4,3},{5,4},{6,5},{7,6},{8,15},{9,8},{10,9... | collective-permute-start | bytes 221192 | tf_op jit(solution)/shard_map/ppermute | solution.py:426
  8.0 0.9 %own.1 = (bf16[36,1024]{1,0:T(8,128)(2,1)S(1)}, bf16[36,1024]{1,0:T(8,128)(2,1)S(1)}, f32[72,1024]{1,0:T(8,128)S(1)}, f32[72,512]{1,0:T(8,128)S(1)}, f32[72,1536]{1,0:T(8,128)S(1)}, /*index=5*/f32[72,512]{1,0:T(8,128)S(1)}) custom-call(bf16[288,512]{1,0:T(8,128)(2,1)S(1)} %bitcast.6, bf16[288,512]{1,0:T(8,128)(2,1)S(1)} %bitcast.8, ...), custom_call_target="tpu_custom_call" | custom-call | flops 500000000 | bytes 4244480 | tf_op jit(solution)/shard_map/own/pallas_call | solution.py:374
  8.9 1.5 %collective-permute-start.2 = (bf16[36,1024]{1,0:T(8,128)(2,1)S(1)}, bf16[36,1024]{1,0:T(8,128)(2,1)S(1)}, u32[]{:S(2)}, u32[]{:S(2)}) collective-permute-start(bf16[36,1024]{1,0:T(8,128)(2,1)S(1)} %get-tuple-element.61), channel_id=1, source_target_pairs={{0,24},{1,9},{2,26},{3,11},{4,28},{5,13},{6,30},{7,15},{8,0},{9,17... | collective-permute-start | bytes 221192 | tf_op jit(solution)/shard_map/ppermute | solution.py:427
  10.4 1.6 %collective-permute-start.3 = (bf16[36,1024]{1,0:T(8,128)(2,1)S(1)}, bf16[36,1024]{1,0:T(8,128)(2,1)S(1)}, u32[]{:S(2)}, u32[]{:S(2)}) collective-permute-start(bf16[36,1024]{1,0:T(8,128)(2,1)S(1)} %get-tuple-element.62), channel_id=1, source_target_pairs={{0,15},{1,24},{2,9},{3,26},{4,11},{5,28},{6,13},{7,30},{8,23},{9,0... | collective-permute-start | bytes 221192 | tf_op jit(solution)/shard_map/ppermute | solution.py:428
  12.0 0.0 collective-permute-done.lat_in
  12.0 2.3 %inner.1 = (f32[4,256,512]{2,1,0:T(8,128)S(1)}, bf16[144,512]{1,0:T(8,128)(2,1)S(1)}, bf16[144,512]{1,0:T(8,128)(2,1)S(1)}, bf16[2,256,144]{2,1,0:T(8,128)(2,1)S(1)}, bf16[144,2048]{1,0:T(8,128)(2,1)S(1)}) custom-call(f32[72,1024]{1,0:T(8,128)S(1)} %get-tuple-element.49.inner_own.own, f32[72,512]{1,0:T(8,128)S(1)} %get-tuple-element.53.own_normed, ...), custom_call_target="tpu_custom_call" | custom-call | flops 1000000000 | bytes 6406144 | tf_op jit(solution)/shard_map/inner/pallas_call | solution.py:374
  14.2 0.0 collective-permute-done.1.lon_in
  14.3 0.0 collective-permute-done.2.lat_in
  14.3 0.3 collective-permute-done.3.diag_in
  14.6 2.5 %outer.1 = (bf16[2,256,512]{2,1,0:T(8,128)(2,1)S(1)}, bf16[2,256,512]{2,1,0:T(8,128)(2,1)S(1)}, bf16[144,512]{1,0:T(8,128)(2,1)S(1)}, bf16[144,512]{1,0:T(8,128)...) custom-call(f32[72,1024]{1,0:T(8,128)S(1)} %get-tuple-element.59.own, ...), custom_call_target="tpu_custom_call" | custom-call | flops 1000000000 | bytes 6791168 | tf_op jit(solution)/shard_map/outer/pallas_call | solution.py:374
  17.1 0.1 collective-permute-start.4
  17.2 0.5 collective-permute-start.6
  17.7 0.4 keep.1.refs_0_
  18.1 1.0 %collective-permute-done.4.refs_1_ = bf16[2,256,512]{2,1,0:T(8,128)(2,1)S(1)} collective-permute-done((bf16[2,256,512]{2,1,0:T(8,128)(2,1)S(1)}, bf16[2,256,512]{2,1,0:T(8,128)(2,1)S(1)}, u32[]{:S(2)}, u32[]{:S(2)}) %collective-permute-start.4) | collective-permute-done | bytes 524320 | tf_op jit(solution)/shard_map/ppermute | solution.py:449
  19.1 0.1 chip_sum.1._
  19.2 2.5 %collective-permute-start.7 = (bf16[2,256,512]{2,1,0:T(8,128)(2,1)S(1)}, bf16[2,256,512]{2,1,0:T(8,128)(2,1)S(1)}, u32[]{:S(2)}, u32[]{:S(2)}) collective-permute-start(bf16[2,256,512]{2,1,0:T(8,128)(2,1)S(1)} %chip_sum.1._), channel_id=1, source_target_pairs={{0,8},{1,17},{2,10},{3,19},{4,12},{5,21},{6,14},{7,23},{8,0},{9,25... | collective-permute-start | bytes 1572872 | tf_op jit(solution)/shard_map/ppermute | solution.py:459
  21.6 1.2 %outputs.1 = (bf16[2,256,512]{2,1,0:T(8,128)(2,1)S(1)}, bf16[144,1024]{1,0:T(8,128)(2,1)S(1)}, bf16[144,1024]{1,0:T(8,128)(2,1)S(1)}) custom-call(bf16[2,256,512]{2,1,0:T(8,128)(2,1)S(1)} %chip_sum.1._, bf16[144,512]{1,0:T(8,128)(2,1)S(1)} %get-tuple-element.67.refs_0_, bf16[144,512]{1,0:T(8,128)(2,1)S(1)} %get-tuple-element.68.refs_1_, ...), custom_call_target="tpu_custom_call" | custom-call | flops 1000000000 | bytes 5799936 | tf_op jit(solution)/shard_map/outputs/pallas_call | solution.py:374
  22.8 0.2 pack_lon.1
  23.0 0.1 collective-permute-start.5
  23.0 5.6 %collective-permute-done.5._.lon_in = bf16[36,1024]{1,0:T(8,128)(2,1)S(1)} collective-permute-done((bf16[36,1024]{1,0:T(8,128)(2,1)S(1)}, bf16[36,1024]{1,0:T(8,128)(2,1)S(1)}, u32[]{:S(2)}, u32[]{:S(2)}) %collective-permute-start.5) | collective-permute-done | bytes 73760 | tf_op jit(solution)/shard_map/ppermute | solution.py:470
  28.7 0.1 collective-permute-done.7.refs_2_
  28.8 0.2 halve1.1
  29.0 1.0 %collective-permute-start.8 = (bf16[1,256,512]{2,1,0:T(8,128)(2,1)S(1)}, bf16[1,256,512]{2,1,0:T(8,128)(2,1)S(1)}, u32[]{:S(2)}, u32[]{:S(2)}) collective-permute-start(bf16[1,256,512]{2,1,0:T(8,128)(2,1)S(1)} %get-tuple-element.76), channel_id=1, source_target_pairs={{0,16},{1,9},{2,18},{3,11},{4,20},{5,13},{6,22},{7,15},{8,24},{9,1... | collective-permute-start | bytes 786440 | tf_op jit(solution)/shard_map/ppermute | solution.py:459
  30.0 5.5 %collective-permute-done.8.refs_1_ = bf16[1,256,512]{2,1,0:T(8,128)(2,1)S(1)} collective-permute-done((bf16[1,256,512]{2,1,0:T(8,128)(2,1)S(1)}, bf16[1,256,512]{2,1,0:T(8,128)(2,1)S(1)}, u32[]{:S(2)}, u32[]{:S(2)}) %collective-permute-start.8) | collective-permute-done | bytes 262176 | tf_op jit(solution)/shard_map/ppermute | solution.py:459
  35.4 0.1 line_parts.1
  35.5 3.5 %collective-permute-start.11 = (bf16[64,512]{1,0:T(8,128)(2,1)S(1)}, bf16[64,512]{1,0:T(8,128)(2,1)S(1)}, u32[]{:S(2)}, u32[]{:S(2)}) collective-permute-start(bf16[64,512]{1,0:T(8,128)(2,1)S(1)} %get-tuple-element.84), channel_id=1, source_target_pairs={{0,6},{1,7},{2,4},{3,5},{4,2},{5,3},{6,0},{7,1},{8,14},{9,15},{10,... | collective-permute-start | bytes 196616 | tf_op jit(solution)/shard_map/ppermute | solution.py:485
  39.0 0.9 %collective-permute-start.13 = (bf16[64,512]{1,0:T(8,128)(2,1)S(1)}, bf16[64,512]{1,0:T(8,128)(2,1)S(1)}, u32[]{:S(2)}, u32[]{:S(2)}) collective-permute-start(bf16[64,512]{1,0:T(8,128)(2,1)S(1)} %get-tuple-element.77._), channel_id=1, source_target_pairs={{0,2},{1,3},{2,0},{3,1},{4,6},{5,7},{6,4},{7,5},{8,10},{9,11},{10,... | collective-permute-start | bytes 196616 | tf_op jit(solution)/shard_map/ppermute | solution.py:485
  40.0 0.2 pack_back.1
  40.1 2.1 %collective-permute-start.9 = (bf16[108,1024]{1,0:T(8,128)(2,1)S(1)}, bf16[108,1024]{1,0:T(8,128)(2,1)S(1)}, u32[]{:S(2)}, u32[]{:S(2)}) collective-permute-start(bf16[108,1024]{1,0:T(8,128)(2,1)S(1)} %get-tuple-element.78), channel_id=1, source_target_pairs={{24,0},{9,1},{26,2},{11,3},{28,4},{13,5},{30,6},{15,7},{0,8},{17,9... | collective-permute-start | bytes 663560 | tf_op jit(solution)/shard_map/ppermute | solution.py:493
  42.2 0.0 collective-permute-start.10
  42.2 0.0 collective-permute-done.11.refs_1_
  42.2 2.0 %collective-permute-done.12.refs_2_ = bf16[64,512]{1,0:T(8,128)(2,1)S(1)} collective-permute-done((bf16[64,512]{1,0:T(8,128)(2,1)S(1)}, bf16[64,512]{1,0:T(8,128)(2,1)S(1)}, u32[]{:S(2)}, u32[]{:S(2)}) %collective-permute-start.12) | collective-permute-done | bytes 65568 | tf_op jit(solution)/shard_map/ppermute | solution.py:485
  44.2 0.1 collective-permute-done.13.refs_3_
  44.4 1.6 %collective-permute-start.16 = (bf16[64,512]{1,0:T(8,128)(2,1)S(1)}, bf16[64,512]{1,0:T(8,128)(2,1)S(1)}, u32[]{:S(2)}, u32[]{:S(2)}) collective-permute-start(bf16[64,512]{1,0:T(8,128)(2,1)S(1)} %line_sum.1.refs_0_), channel_id=1, source_target_pairs={{0,24},{8,16},{16,8},{24,0},{1,25},{9,17},{17,9},{25,1},{2,26},{10... | collective-permute-start | bytes 196616 | tf_op jit(solution)/shard_map/ppermute | solution.py:497
  45.9 1.2 %collective-permute-start.15 = (bf16[64,512]{1,0:T(8,128)(2,1)S(1)}, bf16[64,512]{1,0:T(8,128)(2,1)S(1)}, u32[]{:S(2)}, u32[]{:S(2)}) collective-permute-start(bf16[64,512]{1,0:T(8,128)(2,1)S(1)} %line_sum.1.refs_0_), channel_id=1, source_target_pairs={{0,16},{8,24},{16,0},{24,8},{1,17},{9,25},{17,1},{25,9},{2,18},{10... | collective-permute-start | bytes 196616 | tf_op jit(solution)/shard_map/ppermute | solution.py:497
  47.2 0.8 %collective-permute-start.14 = (bf16[64,512]{1,0:T(8,128)(2,1)S(1)}, bf16[64,512]{1,0:T(8,128)(2,1)S(1)}, u32[]{:S(2)}, u32[]{:S(2)}) collective-permute-start(bf16[64,512]{1,0:T(8,128)(2,1)S(1)} %line_sum.1.refs_0_), channel_id=1, source_target_pairs={{0,8},{8,0},{16,24},{24,16},{1,9},{9,1},{17,25},{25,17},{2,10},{10... | collective-permute-start | bytes 196616 | tf_op jit(solution)/shard_map/ppermute | solution.py:497
  47.9 0.6 %place.1.placed = f32[288,1024]{1,0:T(8,128)S(1)} custom-call(bf16[144,1024]{1,0:T(8,128)(2,1)S(1)} %get-tuple-element.71.inner_results, bf16[144,1024]{1,0:T(8,128)(2,1)S(1)} %get-tuple-element.72.outer_results, bf16[108,1024]{1,0:T(8,128)(2,1)S(1)} %collective-permute-done.9.lat_in), custom_call_target="tpu_custom_call" | custom-call | bytes 1990656 | tf_op jit(solution)/shard_map/place/pallas_call | solution.py:374
  48.5 0.4 collective-permute-done.10.diag_in
  48.9 1.2 %place_rest.1 = (bf16[288,512]{1,0:T(8,128)(2,1)}, bf16[288,512]{1,0:T(8,128)(2,1)}, f32[8,128]{1,0:T(8,128)S(1)}) custom-call(f32[288,1024]{1,0:T(8,128)S(1)} %place.1.placed, bf16[36,1024]{1,0:T(8,128)(2,1)S(1)} %collective-permute-done.5._.lon_in, bf16[36,1024]{1,0:T(8,128)(2,1)S(1)} %collective-permute-done.10.diag_in), custom_call_target="tpu_custom_call" | custom-call | bytes 1921024 | tf_op jit(solution)/shard_map/place_rest/pallas_call | solution.py:374
  50.1 0.7 %collective-permute-done.16.refs_3_ = bf16[64,512]{1,0:T(8,128)(2,1)S(1)} collective-permute-done((bf16[64,512]{1,0:T(8,128)(2,1)S(1)}, bf16[64,512]{1,0:T(8,128)(2,1)S(1)}, u32[]{:S(2)}, u32[]{:S(2)}) %collective-permute-start.16) | collective-permute-done | bytes 65568 | tf_op jit(solution)/shard_map/ppermute | solution.py:497
  50.8 0.1 collective-permute-done.15.refs_2_
  51.0 0.5 collective-permute-done.14.refs_1_
  51.4 0.9 %finish.1 = (f32[64,1536]{1,0:T(8,128)}, f32[64,512]{1,0:T(8,128)}) custom-call(f32[8,128]{1,0:T(8,128)S(1)} %get-tuple-element.82._, bf16[64,512]{1,0:T(8,128)(2,1)S(1)} %line_sum.1.refs_0_, bf16[64,512]{1,0:T(8,128)(2,1)S(1)} %collective-permute-done.14.refs_1_, bf16[64,512]{1,0:T(8,128)(2,1)S(1)} %collective-permute-done.15.refs_2_, ...), custom_call_target="tpu_custom_call" | custom-call | bytes 790528 | tf_op jit(solution)/shard_map/finish/pallas_call | solution.py:374
  (10 shorter events, 0.1 us)
Async XLA Ops:
  0.6 1.0 %copy-start.3 = (bf16[2,6,24,512]{3,2,1,0:T(8,128)(2,1)S(1)}, bf16[2,6,24,512]{3,2,1,0:T(8,128)(2,1)}, u32[]{:S(2)}) copy-start(bf16[2,6,24,512]{3,2,1,0:T(8,128)(2,1)} %param.5) | copy-start | bytes 884740
  0.6 1.0 %copy-start.2 = (bf16[2,6,24,512]{3,2,1,0:T(8,128)(2,1)S(1)}, bf16[2,6,24,512]{3,2,1,0:T(8,128)(2,1)}, u32[]{:S(2)}) copy-start(bf16[2,6,24,512]{3,2,1,0:T(8,128)(2,1)} %param.4) | copy-start | bytes 884740
  1.7 6.3 %copy-start = (bf16[512,1536]{1,0:T(8,128)(2,1)S(1)}, bf16[512,1536]{1,0:T(8,128)(2,1)}, u32[]{:S(2)}) copy-start(bf16[512,1536]{1,0:T(8,128)(2,1)} %refs_8_.1) | copy-start | bytes 4718596
  1.7 6.3 %copy-start.1 = (bf16[512,512]{1,0:T(8,128)(2,1)S(1)}, bf16[512,512]{1,0:T(8,128)(2,1)}, u32[]{:S(2)}) copy-start(bf16[512,512]{1,0:T(8,128)(2,1)} %refs_9_.1) | copy-start | bytes 1572868
  2.2 9.8 %collective-permute-start = (bf16[72,1024]{1,0:T(8,128)(2,1)S(1)}, bf16[72,1024]{1,0:T(8,128)(2,1)S(1)}, u32[]{:S(2)}, u32[]{:S(2)}) collective-permute-start(bf16[72,1024]{1,0:T(8,128)(2,1)S(1)} %get-tuple-element.56), channel_id=1, source_target_pairs={{0,24},{1,9},{2,26},{3,11},{4,28},{5,13},{6,30},{7,15},{8,0},{9,17... | collective-permute-start | bytes 442376 | tf_op jit(solution)/shard_map/ppermute | solution.py:425
  6.1 8.1 %collective-permute-start.1 = (bf16[36,1024]{1,0:T(8,128)(2,1)S(1)}, bf16[36,1024]{1,0:T(8,128)(2,1)S(1)}, u32[]{:S(2)}, u32[]{:S(2)}) collective-permute-start(bf16[36,1024]{1,0:T(8,128)(2,1)S(1)} %get-tuple-element.60), channel_id=1, source_target_pairs={{0,7},{1,0},{2,1},{3,2},{4,3},{5,4},{6,5},{7,6},{8,15},{9,8},{10,9... | collective-permute-start | bytes 221192 | tf_op jit(solution)/shard_map/ppermute | solution.py:426
  8.9 5.4 %collective-permute-start.2 = (bf16[36,1024]{1,0:T(8,128)(2,1)S(1)}, bf16[36,1024]{1,0:T(8,128)(2,1)S(1)}, u32[]{:S(2)}, u32[]{:S(2)}) collective-permute-start(bf16[36,1024]{1,0:T(8,128)(2,1)S(1)} %get-tuple-element.61), channel_id=1, source_target_pairs={{0,24},{1,9},{2,26},{3,11},{4,28},{5,13},{6,30},{7,15},{8,0},{9,17... | collective-permute-start | bytes 221192 | tf_op jit(solution)/shard_map/ppermute | solution.py:427
  10.4 4.2 %collective-permute-start.3 = (bf16[36,1024]{1,0:T(8,128)(2,1)S(1)}, bf16[36,1024]{1,0:T(8,128)(2,1)S(1)}, u32[]{:S(2)}, u32[]{:S(2)}) collective-permute-start(bf16[36,1024]{1,0:T(8,128)(2,1)S(1)} %get-tuple-element.62), channel_id=1, source_target_pairs={{0,15},{1,24},{2,9},{3,26},{4,11},{5,28},{6,13},{7,30},{8,23},{9,0... | collective-permute-start | bytes 221192 | tf_op jit(solution)/shard_map/ppermute | solution.py:428
  17.1 2.0 %collective-permute-start.4 = (bf16[2,256,512]{2,1,0:T(8,128)(2,1)S(1)}, bf16[2,256,512]{2,1,0:T(8,128)(2,1)S(1)}, u32[]{:S(2)}, u32[]{:S(2)}) collective-permute-start(bf16[2,256,512]{2,1,0:T(8,128)(2,1)S(1)} %get-tuple-element.66), channel_id=1, source_target_pairs={{0,1},{1,0},{2,3},{3,2},{4,5},{5,4},{6,7},{7,6},{8,9},{9,8},{10,11... | collective-permute-start | bytes 1572872 | tf_op jit(solution)/shard_map/ppermute | solution.py:449
  17.2 5.9 %collective-permute-start.6 = (bf16[2,256,512]{2,1,0:T(8,128)(2,1)S(1)}, bf16[2,256,512]{2,1,0:T(8,128)(2,1)S(1)}, u32[]{:S(2)}, u32[]{:S(2)}) collective-permute-start(bf16[2,256,512]{2,1,0:T(8,128)(2,1)S(1)} %get-tuple-element.74), channel_id=1, source_target_pairs={{0,1},{1,0},{2,3},{3,2},{4,5},{5,4},{6,7},{7,6},{8,9},{9,8},{10,11... | collective-permute-start | bytes 1572872 | tf_op jit(solution)/shard_map/ppermute | solution.py:450
  19.2 9.6 %collective-permute-start.7 = (bf16[2,256,512]{2,1,0:T(8,128)(2,1)S(1)}, bf16[2,256,512]{2,1,0:T(8,128)(2,1)S(1)}, u32[]{:S(2)}, u32[]{:S(2)}) collective-permute-start(bf16[2,256,512]{2,1,0:T(8,128)(2,1)S(1)} %chip_sum.1._), channel_id=1, source_target_pairs={{0,8},{1,17},{2,10},{3,19},{4,12},{5,21},{6,14},{7,23},{8,0},{9,25... | collective-permute-start | bytes 1572872 | tf_op jit(solution)/shard_map/ppermute | solution.py:459
  23.0 5.7 %collective-permute-start.5 = (bf16[36,1024]{1,0:T(8,128)(2,1)S(1)}, bf16[36,1024]{1,0:T(8,128)(2,1)S(1)}, u32[]{:S(2)}, u32[]{:S(2)}) collective-permute-start(bf16[36,1024]{1,0:T(8,128)(2,1)S(1)} %pack_lon.1), channel_id=1, source_target_pairs={{7,0},{0,1},{1,2},{2,3},{3,4},{4,5},{5,6},{6,7},{15,8},{8,9},{9,10... | collective-permute-start | bytes 221192 | tf_op jit(solution)/shard_map/ppermute | solution.py:470
  29.0 6.4 %collective-permute-start.8 = (bf16[1,256,512]{2,1,0:T(8,128)(2,1)S(1)}, bf16[1,256,512]{2,1,0:T(8,128)(2,1)S(1)}, u32[]{:S(2)}, u32[]{:S(2)}) collective-permute-start(bf16[1,256,512]{2,1,0:T(8,128)(2,1)S(1)} %get-tuple-element.76), channel_id=1, source_target_pairs={{0,16},{1,9},{2,18},{3,11},{4,20},{5,13},{6,22},{7,15},{8,24},{9,1... | collective-permute-start | bytes 786440 | tf_op jit(solution)/shard_map/ppermute | solution.py:459
  35.5 6.7 %collective-permute-start.11 = (bf16[64,512]{1,0:T(8,128)(2,1)S(1)}, bf16[64,512]{1,0:T(8,128)(2,1)S(1)}, u32[]{:S(2)}, u32[]{:S(2)}) collective-permute-start(bf16[64,512]{1,0:T(8,128)(2,1)S(1)} %get-tuple-element.84), channel_id=1, source_target_pairs={{0,6},{1,7},{2,4},{3,5},{4,2},{5,3},{6,0},{7,1},{8,14},{9,15},{10,... | collective-permute-start | bytes 196616 | tf_op jit(solution)/shard_map/ppermute | solution.py:485
  39.0 5.2 %collective-permute-start.12 = (bf16[64,512]{1,0:T(8,128)(2,1)S(1)}, bf16[64,512]{1,0:T(8,128)(2,1)S(1)}, u32[]{:S(2)}, u32[]{:S(2)}) collective-permute-start(bf16[64,512]{1,0:T(8,128)(2,1)S(1)} %get-tuple-element.85), channel_id=1, source_target_pairs={{0,4},{1,5},{2,6},{3,7},{4,0},{5,1},{6,2},{7,3},{8,12},{9,13},{10,... | collective-permute-start | bytes 196616 | tf_op jit(solution)/shard_map/ppermute | solution.py:485
  39.0 5.3 %collective-permute-start.13 = (bf16[64,512]{1,0:T(8,128)(2,1)S(1)}, bf16[64,512]{1,0:T(8,128)(2,1)S(1)}, u32[]{:S(2)}, u32[]{:S(2)}) collective-permute-start(bf16[64,512]{1,0:T(8,128)(2,1)S(1)} %get-tuple-element.77._), channel_id=1, source_target_pairs={{0,2},{1,3},{2,0},{3,1},{4,6},{5,7},{6,4},{7,5},{8,10},{9,11},{10,... | collective-permute-start | bytes 196616 | tf_op jit(solution)/shard_map/ppermute | solution.py:485
  40.1 7.8 %collective-permute-start.9 = (bf16[108,1024]{1,0:T(8,128)(2,1)S(1)}, bf16[108,1024]{1,0:T(8,128)(2,1)S(1)}, u32[]{:S(2)}, u32[]{:S(2)}) collective-permute-start(bf16[108,1024]{1,0:T(8,128)(2,1)S(1)} %get-tuple-element.78), channel_id=1, source_target_pairs={{24,0},{9,1},{26,2},{11,3},{28,4},{13,5},{30,6},{15,7},{0,8},{17,9... | collective-permute-start | bytes 663560 | tf_op jit(solution)/shard_map/ppermute | solution.py:493
  42.2 6.7 %collective-permute-start.10 = (bf16[36,1024]{1,0:T(8,128)(2,1)S(1)}, bf16[36,1024]{1,0:T(8,128)(2,1)S(1)}, u32[]{:S(2)}, u32[]{:S(2)}) collective-permute-start(bf16[36,1024]{1,0:T(8,128)(2,1)S(1)} %get-tuple-element.79), channel_id=1, source_target_pairs={{15,0},{24,1},{9,2},{26,3},{11,4},{28,5},{13,6},{30,7},{23,8},{0,9... | collective-permute-start | bytes 221192 | tf_op jit(solution)/shard_map/ppermute | solution.py:494
  44.4 6.5 %collective-permute-start.16 = (bf16[64,512]{1,0:T(8,128)(2,1)S(1)}, bf16[64,512]{1,0:T(8,128)(2,1)S(1)}, u32[]{:S(2)}, u32[]{:S(2)}) collective-permute-start(bf16[64,512]{1,0:T(8,128)(2,1)S(1)} %line_sum.1.refs_0_), channel_id=1, source_target_pairs={{0,24},{8,16},{16,8},{24,0},{1,25},{9,17},{17,9},{25,1},{2,26},{10... | collective-permute-start | bytes 196616 | tf_op jit(solution)/shard_map/ppermute | solution.py:497
  45.9 5.0 %collective-permute-start.15 = (bf16[64,512]{1,0:T(8,128)(2,1)S(1)}, bf16[64,512]{1,0:T(8,128)(2,1)S(1)}, u32[]{:S(2)}, u32[]{:S(2)}) collective-permute-start(bf16[64,512]{1,0:T(8,128)(2,1)S(1)} %line_sum.1.refs_0_), channel_id=1, source_target_pairs={{0,16},{8,24},{16,0},{24,8},{1,17},{9,25},{17,1},{25,9},{2,18},{10... | collective-permute-start | bytes 196616 | tf_op jit(solution)/shard_map/ppermute | solution.py:497
  47.2 4.3 %collective-permute-start.14 = (bf16[64,512]{1,0:T(8,128)(2,1)S(1)}, bf16[64,512]{1,0:T(8,128)(2,1)S(1)}, u32[]{:S(2)}, u32[]{:S(2)}) collective-permute-start(bf16[64,512]{1,0:T(8,128)(2,1)S(1)} %line_sum.1.refs_0_), channel_id=1, source_target_pairs={{0,8},{8,0},{16,24},{24,16},{1,9},{9,1},{17,25},{25,17},{2,10},{10... | collective-permute-start | bytes 196616 | tf_op jit(solution)/shard_map/ppermute | solution.py:497

commit v8 on v7

--- a/solution.py
+++ b/solution.py
@@ -149,10 +149,11 @@
 
 
 def own_kernel(
-    fields, cotangent, pick_lat, pick_diag, pick_own, inner_own, qkv_weight, proj_weight,
-    outer_lat, diag, outer_own, normed, projected, d_mixed,
+    _, fields, cotangent, pick_lat, pick_diag, pick_outer, pick_inner, qkv_weight, proj_weight,
+    outer_lat, diag, outer_own, inner_own, normed, projected, d_mixed,
 ):
-    pack_kernel(fields, cotangent, pick_lat, pick_diag, pick_own, outer_lat, diag, outer_own)
+    picked = pick_lat, pick_diag, pick_outer, pick_inner
+    pack_kernel(fields, cotangent, *picked, outer_lat, diag, outer_own, inner_own)
     normed[...], projected[...], d_mixed[...] = project(inner_own[...], qkv_weight, proj_weight)
 
 
@@ -165,11 +166,11 @@
     one_window(both, *parts, *refs)
     *_, right, left, _, _ = refs
     lat, core, size = place()
-    for slot in range(size):
-        send_grad[slot] = slot_product(slot, size, lat, 1 - core, [(left, right)])
-
-
-def outer_kernel(own, lon_in, lat_in, diag_in, qkv_weight, proj_weight, grad_so_far, send_first, send_rest, *refs):
+    for slot in range(1, size, 2):
+        send_grad[slot // 2] = slot_product(slot, size, lat, 1 - core, [(left, right)])
+
+
+def outer_kernel(own, lon_in, lat_in, diag_in, qkv_weight, proj_weight, grad_so_far, send_first, *refs):
     last = picks(last_rows, HALF, QUARTER)
     both = jnp.concatenate(
         [
@@ -181,17 +182,13 @@
     one_window(both, *project(both, qkv_weight, proj_weight), *refs)
     *_, right, left, _, _ = refs
     lat, core, size = place()
-    for slot in first_order(size):
-        total = grad_so_far[slot] + slot_product(slot, size, lat, 1 - core, [(left, right)])
-        (send_first if slot % 2 else send_rest)[slot // 2] = total.astype(BF)
+    for slot in range(1, size, 2):
+        total = grad_so_far[slot // 2] + slot_product(slot, size, lat, 1 - core, [(left, right)])
+        send_first[slot // 2] = total.astype(BF)
 
 
 def place():
     return lax.axis_index("lat"), lax.rem(lax.axis_index("lon"), 2), lax.axis_size("lat")
-
-
-def first_order(size):
-    return [*range(1, size, 2), *range(0, size, 2)]
 
 
 def one_window(
@@ -259,11 +256,14 @@
         shares(source, left_keep.at[index], lon, core, lon_size)
 
 
-def keep_kernel(inner_left, inner_right, outer_left, outer_right, keep_first):
+def keep_kernel(*refs):
+    *windows, send_rest, keep_first = refs
+    windows = windows[:3], windows[3:]
     lat, core, size = place()
-    windows = [(inner_left, inner_right), (outer_left, outer_right)]
+    for slot in range(0, size, 2):
+        send_rest[slot // 2] = slot_product(slot, size, lat, 1 - core, [(w[2], w[1]) for w in windows]).astype(BF)
     for slot in range(1, size, 2):
-        keep_first[slot // 2] = slot_product(slot, size, lat, core, windows).astype(BF)
+        keep_first[slot // 2] = slot_product(slot, size, lat, core, [(w[0], w[1]) for w in windows]).astype(BF)
 
 
 def output_kernel(_, *refs):
@@ -355,15 +355,21 @@
 
 
 def finish_kernel(_, *refs):
-    *parts, qkv_out, proj_out, shared = refs
-    lat = lax.axis_index("lat")
+    *parts, qkv_out, proj_out = refs
+    lat, _, size = place()
+    width = parts[0].shape[1]
     for step, part in enumerate(parts):
-        shared[lat ^ step] = part[...].astype(F32)
-    width = shared.shape[2]
-    for slot in range(shared.shape[0]):
-        at = slot * width
-        out, at = (qkv_out, at) if at < qkv_out.shape[1] else (proj_out, at - qkv_out.shape[1])
-        out[:, at : at + width] = shared[slot]
+        share = lat ^ step
+        total = part[...].astype(F32)
+        of_qkv = 3 * size // 4
+
+        @pl.when(share < of_qkv)
+        def _():
+            qkv_out[:, pl.ds(pl.multiple_of(share * width, width), width)] = total
+
+        @pl.when(share >= of_qkv)
+        def _():
+            proj_out[:, pl.ds(pl.multiple_of((share - of_qkv) * width, width), width)] = total
 
 
 def call(kernel, outs, *args, name, flops=0, limit=32, scratch=(), unread=()):
@@ -412,15 +418,14 @@
     pick_inner, pick_outer, pick_lon, pick_diag, pick_own, pick_outer_own = picked
     whole, half = ((HALF, 2 * width), F32), ((HALF, 2 * width), BF)
     quarter = ((QUARTER, 2 * width), BF)
-    inner_lat, lon_piece, inner_own = call(
-        pack_kernel, [half, quarter, whole], own_fields, own_grads, pick_inner, pick_lon, pick_own,
-        name="pack", flops=LOAD,
-    )
-    outer_lat, diag_piece, outer_own, *own_parts = call(
+    inner_lat, lon_piece = call(
+        pack_kernel, [half, quarter], own_fields, own_grads, pick_inner, pick_lon, name="pack", flops=LOAD
+    )
+    outer_lat, diag_piece, outer_own, inner_own, *own_parts = call(
         own_kernel,
-        [quarter, quarter, whole, *(((HALF, lanes), F32) for lanes in (width, 3 * width, width))],
-        own_fields, own_grads, pick_outer, pick_diag, pick_outer_own, inner_own, qkv_weight, proj_weight,
-        name="own", flops=5 * 10**8,
+        [quarter, quarter, whole, whole, *(((HALF, lanes), F32) for lanes in (width, 3 * width, width))],
+        lon_piece, own_fields, own_grads, pick_outer, pick_diag, pick_outer_own, pick_own, qkv_weight, proj_weight,
+        name="own", flops=5 * 10**8, unread=(0,),
     )
     inner_in = lax.ppermute(inner_lat, both, lat_route)
     lon_in = lax.ppermute(lon_piece, both, lon_route)
@@ -434,21 +439,22 @@
         ((WIN, width), BF),
         ((2, width // 2, WIN), BF),
         ((WIN, 4 * width), BF),
+        ((2, width // 2, WIN), BF),
     ]
-    scratch = [pltpu.VMEM((2, width // 2, WIN), BF)] + [pltpu.VMEM((width, WIN), BF)] * 2
+    scratch = [pltpu.VMEM((width, WIN), BF)] * 2
     grad_so_far, *inner = call(
-        inner_kernel, [(split, F32), *per_window], inner_own, *own_parts, inner_in, qkv_weight, proj_weight,
+        inner_kernel, [(halves[0], F32), *per_window], inner_own, *own_parts, inner_in, qkv_weight, proj_weight,
         name="inner", flops=10**9, scratch=scratch,
     )
-    send_first, send_rest, *outer = call(
-        outer_kernel, [halves, halves, *per_window],
+    send_first, *outer = call(
+        outer_kernel, [halves, *per_window],
         outer_own, lon_in, outer_in, diag_in, qkv_weight, proj_weight, grad_so_far,
         name="outer", flops=10**9, scratch=scratch,
     )
     sibling = [(j, j ^ 1) for j in range(lon_size)]
     received_first = lax.ppermute(send_first, "lon", sibling)
+    send_rest, keep_first = call(keep_kernel, [halves, halves], *inner[2:], *outer[2:], name="keep", flops=10**9)
     received_rest = lax.ppermute(send_rest, "lon", sibling)
-    (keep_first,) = call(keep_kernel, [halves], *inner[2:], *outer[2:], name="keep", flops=10**9)
 
     def halving(phase, send):
         route = [
@@ -463,7 +469,7 @@
     received = halving(0, send)
     keep_rest, *results = call(
         output_kernel, [halves, ((WIN, 2 * width), BF), ((WIN, 2 * width), BF)],
-        send, *inner, *outer, qkv_weight, proj_weight,
+        send, *inner[:4], *outer[:4], qkv_weight, proj_weight,
         name="outputs", flops=10**9, unread=(0,),
     )
     (lon_back,) = call(pack_lon_kernel, [quarter], results[1], name="pack_lon")
@@ -509,7 +515,7 @@
         finish_kernel,
         [((rows, 3 * width), F32), ((rows, width), F32)],
         done, line_sum, *shared,
-        name="finish", unread=(0,), scratch=[pltpu.VMEM((lat_size, *share[0]), F32)],
+        name="finish", unread=(0,),
     )
     return (field_out.reshape(fields.shape), d_fields.reshape(fields.shape), qkv_grad, jnp.transpose(proj_grad))
 

time: 52.4 us -> 52.4 us (level)
  no operation moved by 1% of the time
where the time goes in v8:
time: 52.4 us; the launch traced here: 52.3 us
  starting transfers between devices  23 us (44%)
  waiting for transfers between devices  16.1 us (31%)
  Pallas kernels  11.4 us (22%)
  local copies, waits for them, and re-layouts  0.94 us (2%)
  between operations  0.76 us (1%)
    pallas_call x16, Pallas kernels, call(): pl.pallas_call(kernel, out_shape=shapes, in_specs=[anywhere if i in unrea...  11.4 us
    ppermute x1, waiting for transfers between devices, per_device(): lon_home = lax.ppermute(lon_back, both, back(lon_route))  5.64 us
    ppermute x2, waiting for transfers between devices, halving(): return lax.ppermute(send, both, route)  5.59 us
    ppermute x3, starting transfers between devices, per_device(): lax.ppermute(parts[step], 'lon', [(j, j ^ 2 * step) for j in range(lon_si...  4.45 us
    ppermute x1, starting transfers between devices, per_device(): inner_in = lax.ppermute(inner_lat, both, lat_route)  3.94 us
    ppermute x3, starting transfers between devices, per_device(): lax.ppermute(line_sum, 'lat', [(i, i ^ step) for i in range(lat_size)])  3.55 us
    ppermute x2, starting transfers between devices, halving(): return lax.ppermute(send, both, route)  3.42 us
    ppermute x3, waiting for transfers between devices, per_device(): lax.ppermute(parts[step], 'lon', [(j, j ^ 2 * step) for j in range(lon_si...  2.13 us
  transfers between devices with their start and end apart: 17, of which 11 were waited for; matrix products, arithmetic and copies ran while one was open for 0% of the time, Pallas kernels for 14%

profile of v8, /device:TPU:0, one launch (start us, length us, event | category | flops | bytes accessed | tf_op | source)
XLA Modules:
  0.0 52.3 jit_solution(1740951047075560371)
XLA Ops:
  0.7 0.1 order.1
  0.8 0.8 %copy-done.3 = bf16[2,6,24,512]{3,2,1,0:T(8,128)(2,1)S(1)} copy-done((bf16[2,6,24,512]{3,2,1,0:T(8,128)(2,1)S(1)}, bf16[2,6,24,512]{3,2,1,0:T(8,128)(2,1)}, u32[]{:S(2)}) %copy-start.3) | copy-done | bytes 294936
  1.6 0.1 copy-done.2
  1.7 0.4 pack.1
  2.0 3.9 %collective-permute-start = (bf16[72,1024]{1,0:T(8,128)(2,1)S(1)}, bf16[72,1024]{1,0:T(8,128)(2,1)S(1)}, u32[]{:S(2)}, u32[]{:S(2)}) collective-permute-start(bf16[72,1024]{1,0:T(8,128)(2,1)S(1)} %get-tuple-element.60), channel_id=1, source_target_pairs={{0,24},{1,9},{2,26},{3,11},{4,28},{5,13},{6,30},{7,15},{8,0},{9,17... | collective-permute-start | bytes 442376 | tf_op jit(solution)/shard_map/ppermute | solution.py:430
  6.0 1.8 %collective-permute-start.1 = (bf16[36,1024]{1,0:T(8,128)(2,1)S(1)}, bf16[36,1024]{1,0:T(8,128)(2,1)S(1)}, u32[]{:S(2)}, u32[]{:S(2)}) collective-permute-start(bf16[36,1024]{1,0:T(8,128)(2,1)S(1)} %get-tuple-element.51._), channel_id=1, source_target_pairs={{0,7},{1,0},{2,1},{3,2},{4,3},{5,4},{6,5},{7,6},{8,15},{9,8},{10,9... | collective-permute-start | bytes 221192 | tf_op jit(solution)/shard_map/ppermute | solution.py:431
  7.8 1.2 %own.1 = (bf16[36,1024]{1,0:T(8,128)(2,1)S(1)}, bf16[36,1024]{1,0:T(8,128)(2,1)S(1)}, f32[72,1024]{1,0:T(8,128)S(1)}, f32[72,1024]{1,0:T(8,128)S(1)}, f32[72,512...) custom-call(bf16[36,1024]{1,0:T(8,128)(2,1)S(1)} %get-tuple-element.51._, ...), custom_call_target="tpu_custom_call" | custom-call | flops 500000000 | bytes 4359680 | tf_op jit(solution)/shard_map/own/pallas_call | solution.py:380
  9.0 1.5 %collective-permute-start.2 = (bf16[36,1024]{1,0:T(8,128)(2,1)S(1)}, bf16[36,1024]{1,0:T(8,128)(2,1)S(1)}, u32[]{:S(2)}, u32[]{:S(2)}) collective-permute-start(bf16[36,1024]{1,0:T(8,128)(2,1)S(1)} %get-tuple-element.65), channel_id=1, source_target_pairs={{0,24},{1,9},{2,26},{3,11},{4,28},{5,13},{6,30},{7,15},{8,0},{9,17... | collective-permute-start | bytes 221192 | tf_op jit(solution)/shard_map/ppermute | solution.py:432
  10.5 1.6 %collective-permute-start.3 = (bf16[36,1024]{1,0:T(8,128)(2,1)S(1)}, bf16[36,1024]{1,0:T(8,128)(2,1)S(1)}, u32[]{:S(2)}, u32[]{:S(2)}) collective-permute-start(bf16[36,1024]{1,0:T(8,128)(2,1)S(1)} %get-tuple-element.66), channel_id=1, source_target_pairs={{0,15},{1,24},{2,9},{3,26},{4,11},{5,28},{6,13},{7,30},{8,23},{9,0... | collective-permute-start | bytes 221192 | tf_op jit(solution)/shard_map/ppermute | solution.py:433
  12.1 0.0 collective-permute-done.lat_in
  12.1 2.1 %inner.1 = (f32[2,256,512]{2,1,0:T(8,128)S(1)}, bf16[144,512]{1,0:T(8,128)(2,1)S(1)}, bf16[144,512]{1,0:T(8,128)(2,1)S(1)}, bf16[2,256,144]{2,1,0:T(8,128)(2,1)S...) custom-call(f32[72,1024]{1,0:T(8,128)S(1)} %get-tuple-element.56.own, ...), custom_call_target="tpu_custom_call" | custom-call | flops 1000000000 | bytes 5505024 | tf_op jit(solution)/shard_map/inner/pallas_call | solution.py:380
  14.3 0.0 collective-permute-done.1.lon_in
  14.3 0.0 collective-permute-done.2.lat_in
  14.3 0.5 collective-permute-done.3.diag_in
  14.8 2.3 %outer.1 = (bf16[2,256,512]{2,1,0:T(8,128)(2,1)S(1)}, bf16[144,512]{1,0:T(8,128)(2,1)S(1)}, bf16[144,512]{1,0:T(8,128)(2,1)S(1)}, bf16[2,256,144]{2,1,0:T(8,128)...) custom-call(f32[72,1024]{1,0:T(8,128)S(1)} %get-tuple-element.64.own, ...), custom_call_target="tpu_custom_call" | custom-call | flops 1000000000 | bytes 5365760 | tf_op jit(solution)/shard_map/outer/pallas_call | solution.py:380
  17.1 0.1 collective-permute-start.4
  17.2 0.7 %keep.1 = (bf16[2,256,512]{2,1,0:T(8,128)(2,1)S(1)}, bf16[2,256,512]{2,1,0:T(8,128)(2,1)S(1)}) custom-call(bf16[2,256,144]{2,1,0:T(8,128)(2,1)S(1)} %get-tuple-element.61.refs_0_.refs_2_, bf16[144,2048]{1,0:T(8,128)(2,1)S(1)} %get-tuple-element.62.refs_1_.refs_3_, bf16[2,256,144]{2,1,0:T(8,128)(2,1)S(1)} %get-tuple-element.63.refs_2_, ...), custom_call_target="tpu_custom_call" | custom-call | flops 1000000000 | bytes 2818048 | tf_op jit(solution)/shard_map/keep/pallas_call | solution.py:380
  17.9 0.5 %collective-permute-start.6 = (bf16[2,256,512]{2,1,0:T(8,128)(2,1)S(1)}, bf16[2,256,512]{2,1,0:T(8,128)(2,1)S(1)}, u32[]{:S(2)}, u32[]{:S(2)}) collective-permute-start(bf16[2,256,512]{2,1,0:T(8,128)(2,1)S(1)} %get-tuple-element.80), channel_id=1, source_target_pairs={{0,1},{1,0},{2,3},{3,2},{4,5},{5,4},{6,7},{7,6},{8,9},{9,8},{10,11... | collective-permute-start | bytes 1572872 | tf_op jit(solution)/shard_map/ppermute | solution.py:457
  18.4 0.6 %collective-permute-done.4.refs_1_ = bf16[2,256,512]{2,1,0:T(8,128)(2,1)S(1)} collective-permute-done((bf16[2,256,512]{2,1,0:T(8,128)(2,1)S(1)}, bf16[2,256,512]{2,1,0:T(8,128)(2,1)S(1)}, u32[]{:S(2)}, u32[]{:S(2)}) %collective-permute-start.4) | collective-permute-done | bytes 524320 | tf_op jit(solution)/shard_map/ppermute | solution.py:455
  19.1 0.1 chip_sum.1._
  19.2 2.5 %collective-permute-start.7 = (bf16[2,256,512]{2,1,0:T(8,128)(2,1)S(1)}, bf16[2,256,512]{2,1,0:T(8,128)(2,1)S(1)}, u32[]{:S(2)}, u32[]{:S(2)}) collective-permute-start(bf16[2,256,512]{2,1,0:T(8,128)(2,1)S(1)} %chip_sum.1._), channel_id=1, source_target_pairs={{0,8},{1,17},{2,10},{3,19},{4,12},{5,21},{6,14},{7,23},{8,0},{9,25... | collective-permute-start | bytes 1572872 | tf_op jit(solution)/shard_map/ppermute | solution.py:465
  21.7 1.2 %outputs.1 = (bf16[2,256,512]{2,1,0:T(8,128)(2,1)S(1)}, bf16[144,1024]{1,0:T(8,128)(2,1)S(1)}, bf16[144,1024]{1,0:T(8,128)(2,1)S(1)}) custom-call(bf16[2,256,512]{2,1,0:T(8,128)(2,1)S(1)} %chip_sum.1._, bf16[144,512]{1,0:T(8,128)(2,1)S(1)} %get-tuple-element.73.refs_0_, bf16[144,512]{1,0:T(8,128)(2,1)S(1)} %get-tuple-element.74.refs_1_, ...), custom_call_target="tpu_custom_call" | custom-call | flops 1000000000 | bytes 5799936 | tf_op jit(solution)/shard_map/outputs/pallas_call | solution.py:380
  22.8 0.1 pack_lon.1
  23.0 0.1 collective-permute-start.5
  23.1 0.0 collective-permute-done.6.refs_1_
  23.1 5.6 %collective-permute-done.5._.lon_in = bf16[36,1024]{1,0:T(8,128)(2,1)S(1)} collective-permute-done((bf16[36,1024]{1,0:T(8,128)(2,1)S(1)}, bf16[36,1024]{1,0:T(8,128)(2,1)S(1)}, u32[]{:S(2)}, u32[]{:S(2)}) %collective-permute-start.5) | collective-permute-done | bytes 73760 | tf_op jit(solution)/shard_map/ppermute | solution.py:476
  28.7 0.1 collective-permute-done.7.refs_2_
  28.8 0.2 halve1.1
  29.0 1.0 %collective-permute-start.8 = (bf16[1,256,512]{2,1,0:T(8,128)(2,1)S(1)}, bf16[1,256,512]{2,1,0:T(8,128)(2,1)S(1)}, u32[]{:S(2)}, u32[]{:S(2)}) collective-permute-start(bf16[1,256,512]{2,1,0:T(8,128)(2,1)S(1)} %get-tuple-element.82), channel_id=1, source_target_pairs={{0,16},{1,9},{2,18},{3,11},{4,20},{5,13},{6,22},{7,15},{8,24},{9,1... | collective-permute-start | bytes 786440 | tf_op jit(solution)/shard_map/ppermute | solution.py:465
  30.0 5.5 %collective-permute-done.8.refs_1_ = bf16[1,256,512]{2,1,0:T(8,128)(2,1)S(1)} collective-permute-done((bf16[1,256,512]{2,1,0:T(8,128)(2,1)S(1)}, bf16[1,256,512]{2,1,0:T(8,128)(2,1)S(1)}, u32[]{:S(2)}, u32[]{:S(2)}) %collective-permute-start.8) | collective-permute-done | bytes 262176 | tf_op jit(solution)/shard_map/ppermute | solution.py:465
  35.4 0.1 line_parts.1
  35.5 3.5 %collective-permute-start.11 = (bf16[64,512]{1,0:T(8,128)(2,1)S(1)}, bf16[64,512]{1,0:T(8,128)(2,1)S(1)}, u32[]{:S(2)}, u32[]{:S(2)}) collective-permute-start(bf16[64,512]{1,0:T(8,128)(2,1)S(1)} %get-tuple-element.90), channel_id=1, source_target_pairs={{0,6},{1,7},{2,4},{3,5},{4,2},{5,3},{6,0},{7,1},{8,14},{9,15},{10,... | collective-permute-start | bytes 196616 | tf_op jit(solution)/shard_map/ppermute | solution.py:491
  39.0 0.0 collective-permute-start.12
  39.0 0.9 %collective-permute-start.13 = (bf16[64,512]{1,0:T(8,128)(2,1)S(1)}, bf16[64,512]{1,0:T(8,128)(2,1)S(1)}, u32[]{:S(2)}, u32[]{:S(2)}) collective-permute-start(bf16[64,512]{1,0:T(8,128)(2,1)S(1)} %get-tuple-element.83._), channel_id=1, source_target_pairs={{0,2},{1,3},{2,0},{3,1},{4,6},{5,7},{6,4},{7,5},{8,10},{9,11},{10,... | collective-permute-start | bytes 196616 | tf_op jit(solution)/shard_map/ppermute | solution.py:491
  40.0 0.2 pack_back.1
  40.2 2.1 %collective-permute-start.9 = (bf16[108,1024]{1,0:T(8,128)(2,1)S(1)}, bf16[108,1024]{1,0:T(8,128)(2,1)S(1)}, u32[]{:S(2)}, u32[]{:S(2)}) collective-permute-start(bf16[108,1024]{1,0:T(8,128)(2,1)S(1)} %get-tuple-element.84), channel_id=1, source_target_pairs={{24,0},{9,1},{26,2},{11,3},{28,4},{13,5},{30,6},{15,7},{0,8},{17,9... | collective-permute-start | bytes 663560 | tf_op jit(solution)/shard_map/ppermute | solution.py:499
  42.2 2.0 %collective-permute-done.12.refs_2_ = bf16[64,512]{1,0:T(8,128)(2,1)S(1)} collective-permute-done((bf16[64,512]{1,0:T(8,128)(2,1)S(1)}, bf16[64,512]{1,0:T(8,128)(2,1)S(1)}, u32[]{:S(2)}, u32[]{:S(2)}) %collective-permute-start.12) | collective-permute-done | bytes 65568 | tf_op jit(solution)/shard_map/ppermute | solution.py:491
  44.3 0.1 collective-permute-done.13.refs_3_
  44.4 1.6 %collective-permute-start.16 = (bf16[64,512]{1,0:T(8,128)(2,1)S(1)}, bf16[64,512]{1,0:T(8,128)(2,1)S(1)}, u32[]{:S(2)}, u32[]{:S(2)}) collective-permute-start(bf16[64,512]{1,0:T(8,128)(2,1)S(1)} %line_sum.1.refs_0_), channel_id=1, source_target_pairs={{0,24},{8,16},{16,8},{24,0},{1,25},{9,17},{17,9},{25,1},{2,26},{10... | collective-permute-start | bytes 196616 | tf_op jit(solution)/shard_map/ppermute | solution.py:503
  46.0 1.2 %collective-permute-start.15 = (bf16[64,512]{1,0:T(8,128)(2,1)S(1)}, bf16[64,512]{1,0:T(8,128)(2,1)S(1)}, u32[]{:S(2)}, u32[]{:S(2)}) collective-permute-start(bf16[64,512]{1,0:T(8,128)(2,1)S(1)} %line_sum.1.refs_0_), channel_id=1, source_target_pairs={{0,16},{8,24},{16,0},{24,8},{1,17},{9,25},{17,1},{25,9},{2,18},{10... | collective-permute-start | bytes 196616 | tf_op jit(solution)/shard_map/ppermute | solution.py:503
  47.2 0.8 %collective-permute-start.14 = (bf16[64,512]{1,0:T(8,128)(2,1)S(1)}, bf16[64,512]{1,0:T(8,128)(2,1)S(1)}, u32[]{:S(2)}, u32[]{:S(2)}) collective-permute-start(bf16[64,512]{1,0:T(8,128)(2,1)S(1)} %line_sum.1.refs_0_), channel_id=1, source_target_pairs={{0,8},{8,0},{16,24},{24,16},{1,9},{9,1},{17,25},{25,17},{2,10},{10... | collective-permute-start | bytes 196616 | tf_op jit(solution)/shard_map/ppermute | solution.py:503
  48.0 0.6 %place.1.placed = f32[288,1024]{1,0:T(8,128)S(1)} custom-call(bf16[144,1024]{1,0:T(8,128)(2,1)S(1)} %get-tuple-element.77.inner_results, bf16[144,1024]{1,0:T(8,128)(2,1)S(1)} %get-tuple-element.78.outer_results, bf16[108,1024]{1,0:T(8,128)(2,1)S(1)} %collective-permute-done.9.lat_in), custom_call_target="tpu_custom_call" | custom-call | bytes 1990656 | tf_op jit(solution)/shard_map/place/pallas_call | solution.py:380
  48.6 0.4 collective-permute-done.10.diag_in
  48.9 1.2 %place_rest.1 = (bf16[288,512]{1,0:T(8,128)(2,1)}, bf16[288,512]{1,0:T(8,128)(2,1)}, f32[8,128]{1,0:T(8,128)S(1)}) custom-call(f32[288,1024]{1,0:T(8,128)S(1)} %place.1.placed, bf16[36,1024]{1,0:T(8,128)(2,1)S(1)} %collective-permute-done.5._.lon_in, bf16[36,1024]{1,0:T(8,128)(2,1)S(1)} %collective-permute-done.10.diag_in), custom_call_target="tpu_custom_call" | custom-call | bytes 1921024 | tf_op jit(solution)/shard_map/place_rest/pallas_call | solution.py:380
  50.1 0.7 %collective-permute-done.16.refs_3_ = bf16[64,512]{1,0:T(8,128)(2,1)S(1)} collective-permute-done((bf16[64,512]{1,0:T(8,128)(2,1)S(1)}, bf16[64,512]{1,0:T(8,128)(2,1)S(1)}, u32[]{:S(2)}, u32[]{:S(2)}) %collective-permute-start.16) | collective-permute-done | bytes 65568 | tf_op jit(solution)/shard_map/ppermute | solution.py:503
  50.8 0.2 collective-permute-done.15.refs_2_
  51.0 0.4 collective-permute-done.14.refs_1_
  51.4 0.9 %finish.1 = (f32[64,1536]{1,0:T(8,128)}, f32[64,512]{1,0:T(8,128)}) custom-call(f32[8,128]{1,0:T(8,128)S(1)} %get-tuple-element.88._, bf16[64,512]{1,0:T(8,128)(2,1)S(1)} %line_sum.1.refs_0_, bf16[64,512]{1,0:T(8,128)(2,1)S(1)} %collective-permute-done.14.refs_1_, bf16[64,512]{1,0:T(8,128)(2,1)S(1)} %collective-permute-done.15.refs_2_, ...), custom_call_target="tpu_custom_call" | custom-call | bytes 790528 | tf_op jit(solution)/shard_map/finish/pallas_call | solution.py:380
  (10 shorter events, 0.1 us)
Async XLA Ops:
  0.6 1.0 %copy-start.3 = (bf16[2,6,24,512]{3,2,1,0:T(8,128)(2,1)S(1)}, bf16[2,6,24,512]{3,2,1,0:T(8,128)(2,1)}, u32[]{:S(2)}) copy-start(bf16[2,6,24,512]{3,2,1,0:T(8,128)(2,1)} %param.5) | copy-start | bytes 884740
  0.6 1.0 %copy-start.2 = (bf16[2,6,24,512]{3,2,1,0:T(8,128)(2,1)S(1)}, bf16[2,6,24,512]{3,2,1,0:T(8,128)(2,1)}, u32[]{:S(2)}) copy-start(bf16[2,6,24,512]{3,2,1,0:T(8,128)(2,1)} %param.4) | copy-start | bytes 884740
  1.7 6.1 %copy-start = (bf16[512,1536]{1,0:T(8,128)(2,1)S(1)}, bf16[512,1536]{1,0:T(8,128)(2,1)}, u32[]{:S(2)}) copy-start(bf16[512,1536]{1,0:T(8,128)(2,1)} %refs_8_.1) | copy-start | bytes 4718596
  1.7 6.1 %copy-start.1 = (bf16[512,512]{1,0:T(8,128)(2,1)S(1)}, bf16[512,512]{1,0:T(8,128)(2,1)}, u32[]{:S(2)}) copy-start(bf16[512,512]{1,0:T(8,128)(2,1)} %refs_9_.1) | copy-start | bytes 1572868
  2.0 10.1 %collective-permute-start = (bf16[72,1024]{1,0:T(8,128)(2,1)S(1)}, bf16[72,1024]{1,0:T(8,128)(2,1)S(1)}, u32[]{:S(2)}, u32[]{:S(2)}) collective-permute-start(bf16[72,1024]{1,0:T(8,128)(2,1)S(1)} %get-tuple-element.60), channel_id=1, source_target_pairs={{0,24},{1,9},{2,26},{3,11},{4,28},{5,13},{6,30},{7,15},{8,0},{9,17... | collective-permute-start | bytes 442376 | tf_op jit(solution)/shard_map/ppermute | solution.py:430
  6.0 8.3 %collective-permute-start.1 = (bf16[36,1024]{1,0:T(8,128)(2,1)S(1)}, bf16[36,1024]{1,0:T(8,128)(2,1)S(1)}, u32[]{:S(2)}, u32[]{:S(2)}) collective-permute-start(bf16[36,1024]{1,0:T(8,128)(2,1)S(1)} %get-tuple-element.51._), channel_id=1, source_target_pairs={{0,7},{1,0},{2,1},{3,2},{4,3},{5,4},{6,5},{7,6},{8,15},{9,8},{10,9... | collective-permute-start | bytes 221192 | tf_op jit(solution)/shard_map/ppermute | solution.py:431
  9.0 5.2 %collective-permute-start.2 = (bf16[36,1024]{1,0:T(8,128)(2,1)S(1)}, bf16[36,1024]{1,0:T(8,128)(2,1)S(1)}, u32[]{:S(2)}, u32[]{:S(2)}) collective-permute-start(bf16[36,1024]{1,0:T(8,128)(2,1)S(1)} %get-tuple-element.65), channel_id=1, source_target_pairs={{0,24},{1,9},{2,26},{3,11},{4,28},{5,13},{6,30},{7,15},{8,0},{9,17... | collective-permute-start | bytes 221192 | tf_op jit(solution)/shard_map/ppermute | solution.py:432
  10.5 4.2 %collective-permute-start.3 = (bf16[36,1024]{1,0:T(8,128)(2,1)S(1)}, bf16[36,1024]{1,0:T(8,128)(2,1)S(1)}, u32[]{:S(2)}, u32[]{:S(2)}) collective-permute-start(bf16[36,1024]{1,0:T(8,128)(2,1)S(1)} %get-tuple-element.66), channel_id=1, source_target_pairs={{0,15},{1,24},{2,9},{3,26},{4,11},{5,28},{6,13},{7,30},{8,23},{9,0... | collective-permute-start | bytes 221192 | tf_op jit(solution)/shard_map/ppermute | solution.py:433
  17.1 2.0 %collective-permute-start.4 = (bf16[2,256,512]{2,1,0:T(8,128)(2,1)S(1)}, bf16[2,256,512]{2,1,0:T(8,128)(2,1)S(1)}, u32[]{:S(2)}, u32[]{:S(2)}) collective-permute-start(bf16[2,256,512]{2,1,0:T(8,128)(2,1)S(1)} %get-tuple-element.72), channel_id=1, source_target_pairs={{0,1},{1,0},{2,3},{3,2},{4,5},{5,4},{6,7},{7,6},{8,9},{9,8},{10,11... | collective-permute-start | bytes 1572872 | tf_op jit(solution)/shard_map/ppermute | solution.py:455
  17.9 5.2 %collective-permute-start.6 = (bf16[2,256,512]{2,1,0:T(8,128)(2,1)S(1)}, bf16[2,256,512]{2,1,0:T(8,128)(2,1)S(1)}, u32[]{:S(2)}, u32[]{:S(2)}) collective-permute-start(bf16[2,256,512]{2,1,0:T(8,128)(2,1)S(1)} %get-tuple-element.80), channel_id=1, source_target_pairs={{0,1},{1,0},{2,3},{3,2},{4,5},{5,4},{6,7},{7,6},{8,9},{9,8},{10,11... | collective-permute-start | bytes 1572872 | tf_op jit(solution)/shard_map/ppermute | solution.py:457
  19.2 9.6 %collective-permute-start.7 = (bf16[2,256,512]{2,1,0:T(8,128)(2,1)S(1)}, bf16[2,256,512]{2,1,0:T(8,128)(2,1)S(1)}, u32[]{:S(2)}, u32[]{:S(2)}) collective-permute-start(bf16[2,256,512]{2,1,0:T(8,128)(2,1)S(1)} %chip_sum.1._), channel_id=1, source_target_pairs={{0,8},{1,17},{2,10},{3,19},{4,12},{5,21},{6,14},{7,23},{8,0},{9,25... | collective-permute-start | bytes 1572872 | tf_op jit(solution)/shard_map/ppermute | solution.py:465
  23.0 5.7 %collective-permute-start.5 = (bf16[36,1024]{1,0:T(8,128)(2,1)S(1)}, bf16[36,1024]{1,0:T(8,128)(2,1)S(1)}, u32[]{:S(2)}, u32[]{:S(2)}) collective-permute-start(bf16[36,1024]{1,0:T(8,128)(2,1)S(1)} %pack_lon.1), channel_id=1, source_target_pairs={{7,0},{0,1},{1,2},{2,3},{3,4},{4,5},{5,6},{6,7},{15,8},{8,9},{9,10... | collective-permute-start | bytes 221192 | tf_op jit(solution)/shard_map/ppermute | solution.py:476
  29.0 6.4 %collective-permute-start.8 = (bf16[1,256,512]{2,1,0:T(8,128)(2,1)S(1)}, bf16[1,256,512]{2,1,0:T(8,128)(2,1)S(1)}, u32[]{:S(2)}, u32[]{:S(2)}) collective-permute-start(bf16[1,256,512]{2,1,0:T(8,128)(2,1)S(1)} %get-tuple-element.82), channel_id=1, source_target_pairs={{0,16},{1,9},{2,18},{3,11},{4,20},{5,13},{6,22},{7,15},{8,24},{9,1... | collective-permute-start | bytes 786440 | tf_op jit(solution)/shard_map/ppermute | solution.py:465
  35.5 6.7 %collective-permute-start.11 = (bf16[64,512]{1,0:T(8,128)(2,1)S(1)}, bf16[64,512]{1,0:T(8,128)(2,1)S(1)}, u32[]{:S(2)}, u32[]{:S(2)}) collective-permute-start(bf16[64,512]{1,0:T(8,128)(2,1)S(1)} %get-tuple-element.90), channel_id=1, source_target_pairs={{0,6},{1,7},{2,4},{3,5},{4,2},{5,3},{6,0},{7,1},{8,14},{9,15},{10,... | collective-permute-start | bytes 196616 | tf_op jit(solution)/shard_map/ppermute | solution.py:491
  39.0 5.2 %collective-permute-start.12 = (bf16[64,512]{1,0:T(8,128)(2,1)S(1)}, bf16[64,512]{1,0:T(8,128)(2,1)S(1)}, u32[]{:S(2)}, u32[]{:S(2)}) collective-permute-start(bf16[64,512]{1,0:T(8,128)(2,1)S(1)} %get-tuple-element.91), channel_id=1, source_target_pairs={{0,4},{1,5},{2,6},{3,7},{4,0},{5,1},{6,2},{7,3},{8,12},{9,13},{10,... | collective-permute-start | bytes 196616 | tf_op jit(solution)/shard_map/ppermute | solution.py:491
  39.0 5.3 %collective-permute-start.13 = (bf16[64,512]{1,0:T(8,128)(2,1)S(1)}, bf16[64,512]{1,0:T(8,128)(2,1)S(1)}, u32[]{:S(2)}, u32[]{:S(2)}) collective-permute-start(bf16[64,512]{1,0:T(8,128)(2,1)S(1)} %get-tuple-element.83._), channel_id=1, source_target_pairs={{0,2},{1,3},{2,0},{3,1},{4,6},{5,7},{6,4},{7,5},{8,10},{9,11},{10,... | collective-permute-start | bytes 196616 | tf_op jit(solution)/shard_map/ppermute | solution.py:491
  40.2 7.8 %collective-permute-start.9 = (bf16[108,1024]{1,0:T(8,128)(2,1)S(1)}, bf16[108,1024]{1,0:T(8,128)(2,1)S(1)}, u32[]{:S(2)}, u32[]{:S(2)}) collective-permute-start(bf16[108,1024]{1,0:T(8,128)(2,1)S(1)} %get-tuple-element.84), channel_id=1, source_target_pairs={{24,0},{9,1},{26,2},{11,3},{28,4},{13,5},{30,6},{15,7},{0,8},{17,9... | collective-permute-start | bytes 663560 | tf_op jit(solution)/shard_map/ppermute | solution.py:499
  42.2 6.7 %collective-permute-start.10 = (bf16[36,1024]{1,0:T(8,128)(2,1)S(1)}, bf16[36,1024]{1,0:T(8,128)(2,1)S(1)}, u32[]{:S(2)}, u32[]{:S(2)}) collective-permute-start(bf16[36,1024]{1,0:T(8,128)(2,1)S(1)} %get-tuple-element.85), channel_id=1, source_target_pairs={{15,0},{24,1},{9,2},{26,3},{11,4},{28,5},{13,6},{30,7},{23,8},{0,9... | collective-permute-start | bytes 221192 | tf_op jit(solution)/shard_map/ppermute | solution.py:500
  44.4 6.4 %collective-permute-start.16 = (bf16[64,512]{1,0:T(8,128)(2,1)S(1)}, bf16[64,512]{1,0:T(8,128)(2,1)S(1)}, u32[]{:S(2)}, u32[]{:S(2)}) collective-permute-start(bf16[64,512]{1,0:T(8,128)(2,1)S(1)} %line_sum.1.refs_0_), channel_id=1, source_target_pairs={{0,24},{8,16},{16,8},{24,0},{1,25},{9,17},{17,9},{25,1},{2,26},{10... | collective-permute-start | bytes 196616 | tf_op jit(solution)/shard_map/ppermute | solution.py:503
  46.0 5.0 %collective-permute-start.15 = (bf16[64,512]{1,0:T(8,128)(2,1)S(1)}, bf16[64,512]{1,0:T(8,128)(2,1)S(1)}, u32[]{:S(2)}, u32[]{:S(2)}) collective-permute-start(bf16[64,512]{1,0:T(8,128)(2,1)S(1)} %line_sum.1.refs_0_), channel_id=1, source_target_pairs={{0,16},{8,24},{16,0},{24,8},{1,17},{9,25},{17,1},{25,9},{2,18},{10... | collective-permute-start | bytes 196616 | tf_op jit(solution)/shard_map/ppermute | solution.py:503
  47.2 4.3 %collective-permute-start.14 = (bf16[64,512]{1,0:T(8,128)(2,1)S(1)}, bf16[64,512]{1,0:T(8,128)(2,1)S(1)}, u32[]{:S(2)}, u32[]{:S(2)}) collective-permute-start(bf16[64,512]{1,0:T(8,128)(2,1)S(1)} %line_sum.1.refs_0_), channel_id=1, source_target_pairs={{0,8},{8,0},{16,24},{24,16},{1,9},{9,1},{17,25},{25,17},{2,10},{10... | collective-permute-start | bytes 196616 | tf_op jit(solution)/shard_map/ppermute | solution.py:503

commit v9 on v8

--- a/solution.py
+++ b/solution.py
@@ -148,12 +148,11 @@
     return normed, projected, dot(both[:, width:].astype(BF), proj_weight[...], NT)
 
 
-def own_kernel(
-    _, fields, cotangent, pick_lat, pick_diag, pick_outer, pick_inner, qkv_weight, proj_weight,
-    outer_lat, diag, outer_own, inner_own, normed, projected, d_mixed,
-):
-    picked = pick_lat, pick_diag, pick_outer, pick_inner
-    pack_kernel(fields, cotangent, *picked, outer_lat, diag, outer_own, inner_own)
+def pack_rest_kernel(_, *refs):
+    pack_kernel(*refs)
+
+
+def own_kernel(inner_own, qkv_weight, proj_weight, normed, projected, d_mixed):
     normed[...], projected[...], d_mixed[...] = project(inner_own[...], qkv_weight, proj_weight)
 
 
@@ -421,11 +420,15 @@
     inner_lat, lon_piece = call(
         pack_kernel, [half, quarter], own_fields, own_grads, pick_inner, pick_lon, name="pack", flops=LOAD
     )
-    outer_lat, diag_piece, outer_own, inner_own, *own_parts = call(
-        own_kernel,
-        [quarter, quarter, whole, whole, *(((HALF, lanes), F32) for lanes in (width, 3 * width, width))],
-        lon_piece, own_fields, own_grads, pick_outer, pick_diag, pick_outer_own, pick_own, qkv_weight, proj_weight,
-        name="own", flops=5 * 10**8, unread=(0,),
+    outer_lat, diag_piece, outer_own, inner_own = call(
+        pack_rest_kernel, [quarter, quarter, whole, whole],
+        lon_piece, own_fields, own_grads, pick_outer, pick_diag, pick_outer_own, pick_own,
+        name="pack_rest", flops=5 * 10**8, unread=(0,),
+    )
+    own_parts = call(
+        own_kernel, [((HALF, lanes), F32) for lanes in (width, 3 * width, width)],
+        inner_own, qkv_weight, proj_weight,
+        name="own", flops=5 * 10**8,
     )
     inner_in = lax.ppermute(inner_lat, both, lat_route)
     lon_in = lax.ppermute(lon_piece, both, lon_route)

time: 52.4 us -> 52.1 us (level)
  waiting for transfers between devices: 16.1 us -> 15.4 us
    pallas_call x16 -> x17, Pallas kernels: 11.4 us -> 11.5 us  [call(): pl.pallas_call(kernel, out_shape=shapes, in_specs=[anywhere if i in unrea...]
  transfers between devices with their start and end apart: 17 -> 17, of which waited for: 11 -> 9; matrix products, arithmetic and copies ran while one was open for 0% -> 0% of each run, Pallas kernels for 14% -> 15%
where the time goes in v9:
time: 52.1 us; the launch traced here: 51.9 us
  starting transfers between devices  23.3 us (45%)
  waiting for transfers between devices  15.4 us (30%)
  Pallas kernels  11.5 us (22%)
  local copies, waits for them, and re-layouts  0.94 us (2%)
  between operations  0.79 us (2%)
    pallas_call x17, Pallas kernels, call(): pl.pallas_call(kernel, out_shape=shapes, in_specs=[anywhere if i in unrea...  11.5 us
    ppermute x1, waiting for transfers between devices, per_device(): lon_home = lax.ppermute(lon_back, both, back(lon_route))  5.64 us
    ppermute x2, waiting for transfers between devices, halving(): return lax.ppermute(send, both, route)  5.08 us
    ppermute x3, starting transfers between devices, per_device(): lax.ppermute(parts[step], 'lon', [(j, j ^ 2 * step) for j in range(lon_si...  4.45 us
    ppermute x1, starting transfers between devices, per_device(): inner_in = lax.ppermute(inner_lat, both, lat_route)  3.94 us
    ppermute x2, starting transfers between devices, halving(): return lax.ppermute(send, both, route)  3.67 us
    ppermute x3, starting transfers between devices, per_device(): lax.ppermute(line_sum, 'lat', [(i, i ^ step) for i in range(lat_size)])  3.55 us
    ppermute x1, starting transfers between devices, per_device(): lat_home = lax.ppermute(lat_back, both, back(lat_route))  2.07 us
  transfers between devices with their start and end apart: 17, of which 9 were waited for; matrix products, arithmetic and copies ran while one was open for 0% of the time, Pallas kernels for 15%

profile of v9, /device:TPU:0, one launch (start us, length us, event | category | flops | bytes accessed | tf_op | source)
XLA Modules:
  0.0 51.9 jit_solution(16748599846326309355)
XLA Ops:
  0.7 0.1 order.1
  0.8 0.8 %copy-done.3 = bf16[2,6,24,512]{3,2,1,0:T(8,128)(2,1)S(1)} copy-done((bf16[2,6,24,512]{3,2,1,0:T(8,128)(2,1)S(1)}, bf16[2,6,24,512]{3,2,1,0:T(8,128)(2,1)}, u32[]{:S(2)}) %copy-start.3) | copy-done | bytes 294936
  1.6 0.1 copy-done.2
  1.7 0.4 pack.1
  2.0 0.0 copy-start
  2.1 3.9 %collective-permute-start = (bf16[72,1024]{1,0:T(8,128)(2,1)S(1)}, bf16[72,1024]{1,0:T(8,128)(2,1)S(1)}, u32[]{:S(2)}, u32[]{:S(2)}) collective-permute-start(bf16[72,1024]{1,0:T(8,128)(2,1)S(1)} %get-tuple-element.60), channel_id=1, source_target_pairs={{0,24},{1,9},{2,26},{3,11},{4,28},{5,13},{6,30},{7,15},{8,0},{9,17... | collective-permute-start | bytes 442376 | tf_op jit(solution)/shard_map/ppermute | solution.py:433
  6.0 1.8 %collective-permute-start.1 = (bf16[36,1024]{1,0:T(8,128)(2,1)S(1)}, bf16[36,1024]{1,0:T(8,128)(2,1)S(1)}, u32[]{:S(2)}, u32[]{:S(2)}) collective-permute-start(bf16[36,1024]{1,0:T(8,128)(2,1)S(1)} %get-tuple-element.51._), channel_id=1, source_target_pairs={{0,7},{1,0},{2,1},{3,2},{4,3},{5,4},{6,5},{7,6},{8,15},{9,8},{10,9... | collective-permute-start | bytes 221192 | tf_op jit(solution)/shard_map/ppermute | solution.py:434
  7.8 0.6 %pack_rest.1 = (bf16[36,1024]{1,0:T(8,128)(2,1)S(1)}, bf16[36,1024]{1,0:T(8,128)(2,1)S(1)}, f32[72,1024]{1,0:T(8,128)S(1)}, f32[72,1024]{1,0:T(8,128)S(1)}) custom-call(bf16[36,1024]{1,0:T(8,128)(2,1)S(1)} %get-tuple-element.51._, bf16[288,512]{1,0:T(8,128)(2,1)S(1)} %bitcast.6, bf16[288,512]{1,0:T(8,128)(2,1)S(1)} %bitcast.8, ...), custom_call_target="tpu_custom_call" | custom-call | flops 500000000 | bytes 1525248 | tf_op jit(solution)/shard_map/pack_rest/pallas_call | solution.py:379
  8.4 1.5 %collective-permute-start.2 = (bf16[36,1024]{1,0:T(8,128)(2,1)S(1)}, bf16[36,1024]{1,0:T(8,128)(2,1)S(1)}, u32[]{:S(2)}, u32[]{:S(2)}) collective-permute-start(bf16[36,1024]{1,0:T(8,128)(2,1)S(1)} %get-tuple-element.65), channel_id=1, source_target_pairs={{0,24},{1,9},{2,26},{3,11},{4,28},{5,13},{6,30},{7,15},{8,0},{9,17... | collective-permute-start | bytes 221192 | tf_op jit(solution)/shard_map/ppermute | solution.py:435
  9.9 1.6 %collective-permute-start.3 = (bf16[36,1024]{1,0:T(8,128)(2,1)S(1)}, bf16[36,1024]{1,0:T(8,128)(2,1)S(1)}, u32[]{:S(2)}, u32[]{:S(2)}) collective-permute-start(bf16[36,1024]{1,0:T(8,128)(2,1)S(1)} %get-tuple-element.66), channel_id=1, source_target_pairs={{0,15},{1,24},{2,9},{3,26},{4,11},{5,28},{6,13},{7,30},{8,23},{9,0... | collective-permute-start | bytes 221192 | tf_op jit(solution)/shard_map/ppermute | solution.py:436
  11.5 0.7 %own.1 = (f32[72,512]{1,0:T(8,128)S(1)}, f32[72,1536]{1,0:T(8,128)S(1)}, f32[72,512]{1,0:T(8,128)S(1)}) custom-call(f32[72,1024]{1,0:T(8,128)S(1)} %get-tuple-element.56.inner_own.own, bf16[512,1536]{1,0:T(8,128)(2,1)S(1)} %copy-done, bf16[512,512]{1,0:T(8,128)(2,1)S(1)} %copy-done.1), custom_call_target="tpu_custom_call" | custom-call | flops 500000000 | bytes 3129344 | tf_op jit(solution)/shard_map/own/pallas_call | solution.py:379
  12.2 0.0 collective-permute-done.lat_in
  12.2 2.1 %inner.1 = (f32[2,256,512]{2,1,0:T(8,128)S(1)}, bf16[144,512]{1,0:T(8,128)(2,1)S(1)}, bf16[144,512]{1,0:T(8,128)(2,1)S(1)}, bf16[2,256,144]{2,1,0:T(8,128)(2,1)S...) custom-call(f32[72,1024]{1,0:T(8,128)S(1)} %get-tuple-element.56.inner_own.own, ...), custom_call_target="tpu_custom_call" | custom-call | flops 1000000000 | bytes 5505024 | tf_op jit(solution)/shard_map/inner/pallas_call | solution.py:379
  14.4 0.0 collective-permute-done.3.diag_in
  14.4 2.4 %outer.1 = (bf16[2,256,512]{2,1,0:T(8,128)(2,1)S(1)}, bf16[144,512]{1,0:T(8,128)(2,1)S(1)}, bf16[144,512]{1,0:T(8,128)(2,1)S(1)}, bf16[2,256,144]{2,1,0:T(8,128)...) custom-call(f32[72,1024]{1,0:T(8,128)S(1)} %get-tuple-element.64.own, ...), custom_call_target="tpu_custom_call" | custom-call | flops 1000000000 | bytes 5365760 | tf_op jit(solution)/shard_map/outer/pallas_call | solution.py:379
  16.8 0.1 collective-permute-start.4
  16.9 0.7 %keep.1 = (bf16[2,256,512]{2,1,0:T(8,128)(2,1)S(1)}, bf16[2,256,512]{2,1,0:T(8,128)(2,1)S(1)}) custom-call(bf16[2,256,144]{2,1,0:T(8,128)(2,1)S(1)} %get-tuple-element.61.refs_0_.refs_2_, bf16[144,2048]{1,0:T(8,128)(2,1)S(1)} %get-tuple-element.62.refs_1_.refs_3_, bf16[2,256,144]{2,1,0:T(8,128)(2,1)S(1)} %get-tuple-element.63.refs_2_, ...), custom_call_target="tpu_custom_call" | custom-call | flops 1000000000 | bytes 2818048 | tf_op jit(solution)/shard_map/keep/pallas_call | solution.py:379
  17.6 0.5 collective-permute-start.6
  18.1 0.6 %collective-permute-done.4.refs_1_ = bf16[2,256,512]{2,1,0:T(8,128)(2,1)S(1)} collective-permute-done((bf16[2,256,512]{2,1,0:T(8,128)(2,1)S(1)}, bf16[2,256,512]{2,1,0:T(8,128)(2,1)S(1)}, u32[]{:S(2)}, u32[]{:S(2)}) %collective-permute-start.4) | collective-permute-done | bytes 524320 | tf_op jit(solution)/shard_map/ppermute | solution.py:458
  18.7 0.1 chip_sum.1._
  18.9 2.2 %collective-permute-start.7 = (bf16[2,256,512]{2,1,0:T(8,128)(2,1)S(1)}, bf16[2,256,512]{2,1,0:T(8,128)(2,1)S(1)}, u32[]{:S(2)}, u32[]{:S(2)}) collective-permute-start(bf16[2,256,512]{2,1,0:T(8,128)(2,1)S(1)} %chip_sum.1._), channel_id=1, source_target_pairs={{0,8},{1,17},{2,10},{3,19},{4,12},{5,21},{6,14},{7,23},{8,0},{9,25... | collective-permute-start | bytes 1572872 | tf_op jit(solution)/shard_map/ppermute | solution.py:468
  21.1 1.2 %outputs.1 = (bf16[2,256,512]{2,1,0:T(8,128)(2,1)S(1)}, bf16[144,1024]{1,0:T(8,128)(2,1)S(1)}, bf16[144,1024]{1,0:T(8,128)(2,1)S(1)}) custom-call(bf16[2,256,512]{2,1,0:T(8,128)(2,1)S(1)} %chip_sum.1._, bf16[144,512]{1,0:T(8,128)(2,1)S(1)} %get-tuple-element.73.refs_0_, bf16[144,512]{1,0:T(8,128)(2,1)S(1)} %get-tuple-element.74.refs_1_, ...), custom_call_target="tpu_custom_call" | custom-call | flops 1000000000 | bytes 5799936 | tf_op jit(solution)/shard_map/outputs/pallas_call | solution.py:379
  22.2 0.1 pack_lon.1
  22.4 0.1 collective-permute-start.5
  22.5 5.6 %collective-permute-done.5._.lon_in = bf16[36,1024]{1,0:T(8,128)(2,1)S(1)} collective-permute-done((bf16[36,1024]{1,0:T(8,128)(2,1)S(1)}, bf16[36,1024]{1,0:T(8,128)(2,1)S(1)}, u32[]{:S(2)}, u32[]{:S(2)}) %collective-permute-start.5) | collective-permute-done | bytes 73760 | tf_op jit(solution)/shard_map/ppermute | solution.py:479
  28.1 0.1 collective-permute-done.7.refs_2_
  28.2 0.2 halve1.1
  28.4 1.5 %collective-permute-start.8 = (bf16[1,256,512]{2,1,0:T(8,128)(2,1)S(1)}, bf16[1,256,512]{2,1,0:T(8,128)(2,1)S(1)}, u32[]{:S(2)}, u32[]{:S(2)}) collective-permute-start(bf16[1,256,512]{2,1,0:T(8,128)(2,1)S(1)} %get-tuple-element.82), channel_id=1, source_target_pairs={{0,16},{1,9},{2,18},{3,11},{4,20},{5,13},{6,22},{7,15},{8,24},{9,1... | collective-permute-start | bytes 786440 | tf_op jit(solution)/shard_map/ppermute | solution.py:468
  29.9 5.0 %collective-permute-done.8.refs_1_ = bf16[1,256,512]{2,1,0:T(8,128)(2,1)S(1)} collective-permute-done((bf16[1,256,512]{2,1,0:T(8,128)(2,1)S(1)}, bf16[1,256,512]{2,1,0:T(8,128)(2,1)S(1)}, u32[]{:S(2)}, u32[]{:S(2)}) %collective-permute-start.8) | collective-permute-done | bytes 262176 | tf_op jit(solution)/shard_map/ppermute | solution.py:468
  34.8 0.1 line_parts.1
  34.9 3.5 %collective-permute-start.11 = (bf16[64,512]{1,0:T(8,128)(2,1)S(1)}, bf16[64,512]{1,0:T(8,128)(2,1)S(1)}, u32[]{:S(2)}, u32[]{:S(2)}) collective-permute-start(bf16[64,512]{1,0:T(8,128)(2,1)S(1)} %get-tuple-element.90), channel_id=1, source_target_pairs={{0,6},{1,7},{2,4},{3,5},{4,2},{5,3},{6,0},{7,1},{8,14},{9,15},{10,... | collective-permute-start | bytes 196616 | tf_op jit(solution)/shard_map/ppermute | solution.py:494
  38.4 0.0 collective-permute-start.12
  38.4 0.9 %collective-permute-start.13 = (bf16[64,512]{1,0:T(8,128)(2,1)S(1)}, bf16[64,512]{1,0:T(8,128)(2,1)S(1)}, u32[]{:S(2)}, u32[]{:S(2)}) collective-permute-start(bf16[64,512]{1,0:T(8,128)(2,1)S(1)} %get-tuple-element.83._), channel_id=1, source_target_pairs={{0,2},{1,3},{2,0},{3,1},{4,6},{5,7},{6,4},{7,5},{8,10},{9,11},{10,... | collective-permute-start | bytes 196616 | tf_op jit(solution)/shard_map/ppermute | solution.py:494
  39.4 0.2 pack_back.1
  39.6 2.1 %collective-permute-start.9 = (bf16[108,1024]{1,0:T(8,128)(2,1)S(1)}, bf16[108,1024]{1,0:T(8,128)(2,1)S(1)}, u32[]{:S(2)}, u32[]{:S(2)}) collective-permute-start(bf16[108,1024]{1,0:T(8,128)(2,1)S(1)} %get-tuple-element.84), channel_id=1, source_target_pairs={{24,0},{9,1},{26,2},{11,3},{28,4},{13,5},{30,6},{15,7},{0,8},{17,9... | collective-permute-start | bytes 663560 | tf_op jit(solution)/shard_map/ppermute | solution.py:502
  41.6 2.0 %collective-permute-done.12.refs_2_ = bf16[64,512]{1,0:T(8,128)(2,1)S(1)} collective-permute-done((bf16[64,512]{1,0:T(8,128)(2,1)S(1)}, bf16[64,512]{1,0:T(8,128)(2,1)S(1)}, u32[]{:S(2)}, u32[]{:S(2)}) %collective-permute-start.12) | collective-permute-done | bytes 65568 | tf_op jit(solution)/shard_map/ppermute | solution.py:494
  43.6 0.0 collective-permute-done.13.refs_3_
  43.7 1.6 %collective-permute-start.16 = (bf16[64,512]{1,0:T(8,128)(2,1)S(1)}, bf16[64,512]{1,0:T(8,128)(2,1)S(1)}, u32[]{:S(2)}, u32[]{:S(2)}) collective-permute-start(bf16[64,512]{1,0:T(8,128)(2,1)S(1)} %line_sum.1.refs_0_), channel_id=1, source_target_pairs={{0,24},{8,16},{16,8},{24,0},{1,25},{9,17},{17,9},{25,1},{2,26},{10... | collective-permute-start | bytes 196616 | tf_op jit(solution)/shard_map/ppermute | solution.py:506
  45.3 1.2 %collective-permute-start.15 = (bf16[64,512]{1,0:T(8,128)(2,1)S(1)}, bf16[64,512]{1,0:T(8,128)(2,1)S(1)}, u32[]{:S(2)}, u32[]{:S(2)}) collective-permute-start(bf16[64,512]{1,0:T(8,128)(2,1)S(1)} %line_sum.1.refs_0_), channel_id=1, source_target_pairs={{0,16},{8,24},{16,0},{24,8},{1,17},{9,25},{17,1},{25,9},{2,18},{10... | collective-permute-start | bytes 196616 | tf_op jit(solution)/shard_map/ppermute | solution.py:506
  46.6 0.7 %collective-permute-start.14 = (bf16[64,512]{1,0:T(8,128)(2,1)S(1)}, bf16[64,512]{1,0:T(8,128)(2,1)S(1)}, u32[]{:S(2)}, u32[]{:S(2)}) collective-permute-start(bf16[64,512]{1,0:T(8,128)(2,1)S(1)} %line_sum.1.refs_0_), channel_id=1, source_target_pairs={{0,8},{8,0},{16,24},{24,16},{1,9},{9,1},{17,25},{25,17},{2,10},{10... | collective-permute-start | bytes 196616 | tf_op jit(solution)/shard_map/ppermute | solution.py:506
  47.3 0.0 collective-permute-done.9.lat_in
  47.3 0.6 %place.1.placed = f32[288,1024]{1,0:T(8,128)S(1)} custom-call(bf16[144,1024]{1,0:T(8,128)(2,1)S(1)} %get-tuple-element.77.inner_results, bf16[144,1024]{1,0:T(8,128)(2,1)S(1)} %get-tuple-element.78.outer_results, bf16[108,1024]{1,0:T(8,128)(2,1)S(1)} %collective-permute-done.9.lat_in), custom_call_target="tpu_custom_call" | custom-call | bytes 1990656 | tf_op jit(solution)/shard_map/place/pallas_call | solution.py:379
  47.9 0.5 collective-permute-done.10.diag_in
  48.3 1.2 %place_rest.1 = (bf16[288,512]{1,0:T(8,128)(2,1)}, bf16[288,512]{1,0:T(8,128)(2,1)}, f32[8,128]{1,0:T(8,128)S(1)}) custom-call(f32[288,1024]{1,0:T(8,128)S(1)} %place.1.placed, bf16[36,1024]{1,0:T(8,128)(2,1)S(1)} %collective-permute-done.5._.lon_in, bf16[36,1024]{1,0:T(8,128)(2,1)S(1)} %collective-permute-done.10.diag_in), custom_call_target="tpu_custom_call" | custom-call | bytes 1921024 | tf_op jit(solution)/shard_map/place_rest/pallas_call | solution.py:379
  49.5 0.7 %collective-permute-done.16.refs_3_ = bf16[64,512]{1,0:T(8,128)(2,1)S(1)} collective-permute-done((bf16[64,512]{1,0:T(8,128)(2,1)S(1)}, bf16[64,512]{1,0:T(8,128)(2,1)S(1)}, u32[]{:S(2)}, u32[]{:S(2)}) %collective-permute-start.16) | collective-permute-done | bytes 65568 | tf_op jit(solution)/shard_map/ppermute | solution.py:506
  50.2 0.2 collective-permute-done.15.refs_2_
  50.4 0.7 %collective-permute-done.14.refs_1_ = bf16[64,512]{1,0:T(8,128)(2,1)S(1)} collective-permute-done((bf16[64,512]{1,0:T(8,128)(2,1)S(1)}, bf16[64,512]{1,0:T(8,128)(2,1)S(1)}, u32[]{:S(2)}, u32[]{:S(2)}) %collective-permute-start.14) | collective-permute-done | bytes 65568 | tf_op jit(solution)/shard_map/ppermute | solution.py:506
  51.1 0.9 %finish.1 = (f32[64,1536]{1,0:T(8,128)}, f32[64,512]{1,0:T(8,128)}) custom-call(f32[8,128]{1,0:T(8,128)S(1)} %get-tuple-element.88._, bf16[64,512]{1,0:T(8,128)(2,1)S(1)} %line_sum.1.refs_0_, bf16[64,512]{1,0:T(8,128)(2,1)S(1)} %collective-permute-done.14.refs_1_, bf16[64,512]{1,0:T(8,128)(2,1)S(1)} %collective-permute-done.15.refs_2_, ...), custom_call_target="tpu_custom_call" | custom-call | bytes 790528 | tf_op jit(solution)/shard_map/finish/pallas_call | solution.py:379
  (11 shorter events, 0.1 us)
Async XLA Ops:
  0.6 1.0 %copy-start.3 = (bf16[2,6,24,512]{3,2,1,0:T(8,128)(2,1)S(1)}, bf16[2,6,24,512]{3,2,1,0:T(8,128)(2,1)}, u32[]{:S(2)}) copy-start(bf16[2,6,24,512]{3,2,1,0:T(8,128)(2,1)} %param.5) | copy-start | bytes 884740
  0.6 1.0 %copy-start.2 = (bf16[2,6,24,512]{3,2,1,0:T(8,128)(2,1)S(1)}, bf16[2,6,24,512]{3,2,1,0:T(8,128)(2,1)}, u32[]{:S(2)}) copy-start(bf16[2,6,24,512]{3,2,1,0:T(8,128)(2,1)} %param.4) | copy-start | bytes 884740
  1.7 9.8 %copy-start.1 = (bf16[512,512]{1,0:T(8,128)(2,1)S(1)}, bf16[512,512]{1,0:T(8,128)(2,1)}, u32[]{:S(2)}) copy-start(bf16[512,512]{1,0:T(8,128)(2,1)} %refs_9_.1) | copy-start | bytes 1572868
  2.0 9.5 %copy-start = (bf16[512,1536]{1,0:T(8,128)(2,1)S(1)}, bf16[512,1536]{1,0:T(8,128)(2,1)}, u32[]{:S(2)}) copy-start(bf16[512,1536]{1,0:T(8,128)(2,1)} %refs_8_.1) | copy-start | bytes 4718596
  2.1 10.2 %collective-permute-start = (bf16[72,1024]{1,0:T(8,128)(2,1)S(1)}, bf16[72,1024]{1,0:T(8,128)(2,1)S(1)}, u32[]{:S(2)}, u32[]{:S(2)}) collective-permute-start(bf16[72,1024]{1,0:T(8,128)(2,1)S(1)} %get-tuple-element.60), channel_id=1, source_target_pairs={{0,24},{1,9},{2,26},{3,11},{4,28},{5,13},{6,30},{7,15},{8,0},{9,17... | collective-permute-start | bytes 442376 | tf_op jit(solution)/shard_map/ppermute | solution.py:433
  6.0 8.4 %collective-permute-start.1 = (bf16[36,1024]{1,0:T(8,128)(2,1)S(1)}, bf16[36,1024]{1,0:T(8,128)(2,1)S(1)}, u32[]{:S(2)}, u32[]{:S(2)}) collective-permute-start(bf16[36,1024]{1,0:T(8,128)(2,1)S(1)} %get-tuple-element.51._), channel_id=1, source_target_pairs={{0,7},{1,0},{2,1},{3,2},{4,3},{5,4},{6,5},{7,6},{8,15},{9,8},{10,9... | collective-permute-start | bytes 221192 | tf_op jit(solution)/shard_map/ppermute | solution.py:434
  8.4 5.9 %collective-permute-start.2 = (bf16[36,1024]{1,0:T(8,128)(2,1)S(1)}, bf16[36,1024]{1,0:T(8,128)(2,1)S(1)}, u32[]{:S(2)}, u32[]{:S(2)}) collective-permute-start(bf16[36,1024]{1,0:T(8,128)(2,1)S(1)} %get-tuple-element.65), channel_id=1, source_target_pairs={{0,24},{1,9},{2,26},{3,11},{4,28},{5,13},{6,30},{7,15},{8,0},{9,17... | collective-permute-start | bytes 221192 | tf_op jit(solution)/shard_map/ppermute | solution.py:435
  9.9 4.5 %collective-permute-start.3 = (bf16[36,1024]{1,0:T(8,128)(2,1)S(1)}, bf16[36,1024]{1,0:T(8,128)(2,1)S(1)}, u32[]{:S(2)}, u32[]{:S(2)}) collective-permute-start(bf16[36,1024]{1,0:T(8,128)(2,1)S(1)} %get-tuple-element.66), channel_id=1, source_target_pairs={{0,15},{1,24},{2,9},{3,26},{4,11},{5,28},{6,13},{7,30},{8,23},{9,0... | collective-permute-start | bytes 221192 | tf_op jit(solution)/shard_map/ppermute | solution.py:436
  16.8 2.0 %collective-permute-start.4 = (bf16[2,256,512]{2,1,0:T(8,128)(2,1)S(1)}, bf16[2,256,512]{2,1,0:T(8,128)(2,1)S(1)}, u32[]{:S(2)}, u32[]{:S(2)}) collective-permute-start(bf16[2,256,512]{2,1,0:T(8,128)(2,1)S(1)} %get-tuple-element.72), channel_id=1, source_target_pairs={{0,1},{1,0},{2,3},{3,2},{4,5},{5,4},{6,7},{7,6},{8,9},{9,8},{10,11... | collective-permute-start | bytes 1572872 | tf_op jit(solution)/shard_map/ppermute | solution.py:458
  17.6 4.9 %collective-permute-start.6 = (bf16[2,256,512]{2,1,0:T(8,128)(2,1)S(1)}, bf16[2,256,512]{2,1,0:T(8,128)(2,1)S(1)}, u32[]{:S(2)}, u32[]{:S(2)}) collective-permute-start(bf16[2,256,512]{2,1,0:T(8,128)(2,1)S(1)} %get-tuple-element.80), channel_id=1, source_target_pairs={{0,1},{1,0},{2,3},{3,2},{4,5},{5,4},{6,7},{7,6},{8,9},{9,8},{10,11... | collective-permute-start | bytes 1572872 | tf_op jit(solution)/shard_map/ppermute | solution.py:460
  18.9 9.4 %collective-permute-start.7 = (bf16[2,256,512]{2,1,0:T(8,128)(2,1)S(1)}, bf16[2,256,512]{2,1,0:T(8,128)(2,1)S(1)}, u32[]{:S(2)}, u32[]{:S(2)}) collective-permute-start(bf16[2,256,512]{2,1,0:T(8,128)(2,1)S(1)} %chip_sum.1._), channel_id=1, source_target_pairs={{0,8},{1,17},{2,10},{3,19},{4,12},{5,21},{6,14},{7,23},{8,0},{9,25... | collective-permute-start | bytes 1572872 | tf_op jit(solution)/shard_map/ppermute | solution.py:468
  22.4 5.7 %collective-permute-start.5 = (bf16[36,1024]{1,0:T(8,128)(2,1)S(1)}, bf16[36,1024]{1,0:T(8,128)(2,1)S(1)}, u32[]{:S(2)}, u32[]{:S(2)}) collective-permute-start(bf16[36,1024]{1,0:T(8,128)(2,1)S(1)} %pack_lon.1), channel_id=1, source_target_pairs={{7,0},{0,1},{1,2},{2,3},{3,4},{4,5},{5,6},{6,7},{15,8},{8,9},{9,10... | collective-permute-start | bytes 221192 | tf_op jit(solution)/shard_map/ppermute | solution.py:479
  28.4 6.4 %collective-permute-start.8 = (bf16[1,256,512]{2,1,0:T(8,128)(2,1)S(1)}, bf16[1,256,512]{2,1,0:T(8,128)(2,1)S(1)}, u32[]{:S(2)}, u32[]{:S(2)}) collective-permute-start(bf16[1,256,512]{2,1,0:T(8,128)(2,1)S(1)} %get-tuple-element.82), channel_id=1, source_target_pairs={{0,16},{1,9},{2,18},{3,11},{4,20},{5,13},{6,22},{7,15},{8,24},{9,1... | collective-permute-start | bytes 786440 | tf_op jit(solution)/shard_map/ppermute | solution.py:468
  34.9 6.7 %collective-permute-start.11 = (bf16[64,512]{1,0:T(8,128)(2,1)S(1)}, bf16[64,512]{1,0:T(8,128)(2,1)S(1)}, u32[]{:S(2)}, u32[]{:S(2)}) collective-permute-start(bf16[64,512]{1,0:T(8,128)(2,1)S(1)} %get-tuple-element.90), channel_id=1, source_target_pairs={{0,6},{1,7},{2,4},{3,5},{4,2},{5,3},{6,0},{7,1},{8,14},{9,15},{10,... | collective-permute-start | bytes 196616 | tf_op jit(solution)/shard_map/ppermute | solution.py:494
  38.4 5.2 %collective-permute-start.12 = (bf16[64,512]{1,0:T(8,128)(2,1)S(1)}, bf16[64,512]{1,0:T(8,128)(2,1)S(1)}, u32[]{:S(2)}, u32[]{:S(2)}) collective-permute-start(bf16[64,512]{1,0:T(8,128)(2,1)S(1)} %get-tuple-element.91), channel_id=1, source_target_pairs={{0,4},{1,5},{2,6},{3,7},{4,0},{5,1},{6,2},{7,3},{8,12},{9,13},{10,... | collective-permute-start | bytes 196616 | tf_op jit(solution)/shard_map/ppermute | solution.py:494
  38.4 5.2 %collective-permute-start.13 = (bf16[64,512]{1,0:T(8,128)(2,1)S(1)}, bf16[64,512]{1,0:T(8,128)(2,1)S(1)}, u32[]{:S(2)}, u32[]{:S(2)}) collective-permute-start(bf16[64,512]{1,0:T(8,128)(2,1)S(1)} %get-tuple-element.83._), channel_id=1, source_target_pairs={{0,2},{1,3},{2,0},{3,1},{4,6},{5,7},{6,4},{7,5},{8,10},{9,11},{10,... | collective-permute-start | bytes 196616 | tf_op jit(solution)/shard_map/ppermute | solution.py:494
  39.6 7.7 %collective-permute-start.9 = (bf16[108,1024]{1,0:T(8,128)(2,1)S(1)}, bf16[108,1024]{1,0:T(8,128)(2,1)S(1)}, u32[]{:S(2)}, u32[]{:S(2)}) collective-permute-start(bf16[108,1024]{1,0:T(8,128)(2,1)S(1)} %get-tuple-element.84), channel_id=1, source_target_pairs={{24,0},{9,1},{26,2},{11,3},{28,4},{13,5},{30,6},{15,7},{0,8},{17,9... | collective-permute-start | bytes 663560 | tf_op jit(solution)/shard_map/ppermute | solution.py:502
  41.6 6.7 %collective-permute-start.10 = (bf16[36,1024]{1,0:T(8,128)(2,1)S(1)}, bf16[36,1024]{1,0:T(8,128)(2,1)S(1)}, u32[]{:S(2)}, u32[]{:S(2)}) collective-permute-start(bf16[36,1024]{1,0:T(8,128)(2,1)S(1)} %get-tuple-element.85), channel_id=1, source_target_pairs={{15,0},{24,1},{9,2},{26,3},{11,4},{28,5},{13,6},{30,7},{23,8},{0,9... | collective-permute-start | bytes 221192 | tf_op jit(solution)/shard_map/ppermute | solution.py:503
  43.7 6.5 %collective-permute-start.16 = (bf16[64,512]{1,0:T(8,128)(2,1)S(1)}, bf16[64,512]{1,0:T(8,128)(2,1)S(1)}, u32[]{:S(2)}, u32[]{:S(2)}) collective-permute-start(bf16[64,512]{1,0:T(8,128)(2,1)S(1)} %line_sum.1.refs_0_), channel_id=1, source_target_pairs={{0,24},{8,16},{16,8},{24,0},{1,25},{9,17},{17,9},{25,1},{2,26},{10... | collective-permute-start | bytes 196616 | tf_op jit(solution)/shard_map/ppermute | solution.py:506
  45.3 5.0 %collective-permute-start.15 = (bf16[64,512]{1,0:T(8,128)(2,1)S(1)}, bf16[64,512]{1,0:T(8,128)(2,1)S(1)}, u32[]{:S(2)}, u32[]{:S(2)}) collective-permute-start(bf16[64,512]{1,0:T(8,128)(2,1)S(1)} %line_sum.1.refs_0_), channel_id=1, source_target_pairs={{0,16},{8,24},{16,0},{24,8},{1,17},{9,25},{17,1},{25,9},{2,18},{10... | collective-permute-start | bytes 196616 | tf_op jit(solution)/shard_map/ppermute | solution.py:506
  46.6 4.5 %collective-permute-start.14 = (bf16[64,512]{1,0:T(8,128)(2,1)S(1)}, bf16[64,512]{1,0:T(8,128)(2,1)S(1)}, u32[]{:S(2)}, u32[]{:S(2)}) collective-permute-start(bf16[64,512]{1,0:T(8,128)(2,1)S(1)} %line_sum.1.refs_0_), channel_id=1, source_target_pairs={{0,8},{8,0},{16,24},{24,16},{1,9},{9,1},{17,25},{25,17},{2,10},{10... | collective-permute-start | bytes 196616 | tf_op jit(solution)/shard_map/ppermute | solution.py:506

commit v10 on v9

--- a/solution.py
+++ b/solution.py
@@ -169,7 +169,7 @@
         send_grad[slot // 2] = slot_product(slot, size, lat, 1 - core, [(left, right)])
 
 
-def outer_kernel(own, lon_in, lat_in, diag_in, qkv_weight, proj_weight, grad_so_far, send_first, *refs):
+def outer_kernel(own, lon_in, diag_in, lat_in, qkv_weight, proj_weight, grad_so_far, send_first, *refs):
     last = picks(last_rows, HALF, QUARTER)
     both = jnp.concatenate(
         [
@@ -353,22 +353,40 @@
     out[...] = total.astype(out.dtype)
 
 
+def at_share(share, size, width, qkv_out, proj_out, write):
+    of_qkv = 3 * size // 4
+
+    @pl.when(share < of_qkv)
+    def _():
+        write(qkv_out.at[:, pl.ds(pl.multiple_of(share * width, width), width)])
+
+    @pl.when(share >= of_qkv)
+    def _():
+        write(proj_out.at[:, pl.ds(pl.multiple_of((share - of_qkv) * width, width), width)])
+
+
 def finish_kernel(_, *refs):
     *parts, qkv_out, proj_out = refs
     lat, _, size = place()
-    width = parts[0].shape[1]
-    for step, part in enumerate(parts):
-        share = lat ^ step
+    for step, part in zip((0, *range(2, size)), parts):
         total = part[...].astype(F32)
-        of_qkv = 3 * size // 4
-
-        @pl.when(share < of_qkv)
-        def _():
-            qkv_out[:, pl.ds(pl.multiple_of(share * width, width), width)] = total
-
-        @pl.when(share >= of_qkv)
-        def _():
-            proj_out[:, pl.ds(pl.multiple_of((share - of_qkv) * width, width), width)] = total
+
+        def write(out):
+            out[...] = total
+
+        at_share(lat ^ step, size, part.shape[1], qkv_out, proj_out, write)
+
+
+def last_share_kernel(part, qkv_in, proj_in, qkv_out, proj_out, total, done):
+    lat, _, size = place()
+    total[...] = part[...].astype(F32)
+
+    def write(out):
+        copy = pltpu.make_async_copy(total, out, done)
+        copy.start()
+        copy.wait()
+
+    at_share(lat ^ 1, size, part.shape[1], qkv_out, proj_out, write)
 
 
 def call(kernel, outs, *args, name, flops=0, limit=32, scratch=(), unread=()):
@@ -451,7 +469,7 @@
     )
     send_first, *outer = call(
         outer_kernel, [halves, *per_window],
-        outer_own, lon_in, outer_in, diag_in, qkv_weight, proj_weight, grad_so_far,
+        outer_own, lon_in, diag_in, outer_in, qkv_weight, proj_weight, grad_so_far,
         name="outer", flops=10**9, scratch=scratch,
     )
     sibling = [(j, j ^ 1) for j in range(lon_size)]
@@ -514,12 +532,22 @@
         placed, lon_home, diag_home,
         name="place_rest",
     )
-    qkv_grad, proj_grad = call(
+    grads_so_far = call(
         finish_kernel,
         [((rows, 3 * width), F32), ((rows, width), F32)],
-        done, line_sum, *shared,
+        done, line_sum, *shared[1:],
         name="finish", unread=(0,),
     )
+    anywhere = pl.BlockSpec(memory_space=pl.ANY)
+    qkv_grad, proj_grad = pl.pallas_call(
+        last_share_kernel,
+        out_shape=[jax.ShapeDtypeStruct(part.shape, part.dtype) for part in grads_so_far],
+        in_specs=[pl.BlockSpec(memory_space=pltpu.VMEM), anywhere, anywhere],
+        out_specs=[anywhere, anywhere],
+        scratch_shapes=[pltpu.VMEM(share[0], F32), pltpu.SemaphoreType.DMA],
+        input_output_aliases={1: 0, 2: 1},
+        name="last_share",
+    )(shared[0], *grads_so_far)
     return (field_out.reshape(fields.shape), d_fields.reshape(fields.shape), qkv_grad, jnp.transpose(proj_grad))
 
 

time: 52.1 us -> 54.8 us (1.052)
  Pallas kernels: 11.5 us -> 13 us
  waiting for transfers between devices: 15.4 us -> 16.3 us
  local copies, waits for them, and re-layouts: 0.94 us -> 1.56 us
    ppermute x1, starting transfers between devices: 1.49 us -> 3.33 us  [per_device(): outer_in = lax.ppermute(outer_lat, both, lat_route)]
    pallas_call x0 -> x1, Pallas kernels: none -> 1.51 us  [per_device(): pl.pallas_call(last_share_kernel, out_shape=[jax.ShapeDtypeStruct(part.sh...]
    ppermute x2, starting transfers between devices: 3.67 us -> 2.62 us  [halving(): return lax.ppermute(send, both, route)]
    ppermute x2, waiting for transfers between devices: 5.08 us -> 6.01 us  [halving(): return lax.ppermute(send, both, route)]
    ppermute x1, waiting for transfers between devices: 0.01 us -> 0.64 us  [per_device(): lat_home = lax.ppermute(lat_back, both, back(lat_route))]
    unnamed x8 -> x10, local copies, waits for them, and re-layouts: 0.94 us -> 1.56 us
    ppermute x1, starting transfers between devices: 1.6 us -> 0.99 us  [per_device(): diag_in = lax.ppermute(diag_piece, both, diag_route)]
  transfers between devices with their start and end apart: 17 -> 17, of which waited for: 9 -> 8; matrix products, arithmetic and copies ran while one was open for 0% -> 0% of each run, Pallas kernels for 15% -> 15%
where the time goes in v10:
time: 54.8 us; the launch traced here: 54.6 us
  starting transfers between devices  22.9 us (42%)
  waiting for transfers between devices  16.3 us (30%)
  Pallas kernels  13 us (24%)
  local copies, waits for them, and re-layouts  1.56 us (3%)
  between operations  0.8 us (1%)
    pallas_call x17, Pallas kernels, call(): pl.pallas_call(kernel, out_shape=shapes, in_specs=[anywhere if i in unrea...  11.5 us
    ppermute x2, waiting for transfers between devices, halving(): return lax.ppermute(send, both, route)  6.01 us
    ppermute x1, waiting for transfers between devices, per_device(): lon_home = lax.ppermute(lon_back, both, back(lon_route))  5.64 us
    ppermute x3, starting transfers between devices, per_device(): lax.ppermute(parts[step], 'lon', [(j, j ^ 2 * step) for j in range(lon_si...  4.45 us
    ppermute x1, starting transfers between devices, per_device(): inner_in = lax.ppermute(inner_lat, both, lat_route)  3.94 us
    ppermute x3, starting transfers between devices, per_device(): lax.ppermute(line_sum, 'lat', [(i, i ^ step) for i in range(lat_size)])  3.55 us
    ppermute x1, starting transfers between devices, per_device(): outer_in = lax.ppermute(outer_lat, both, lat_route)  3.33 us
    ppermute x2, starting transfers between devices, halving(): return lax.ppermute(send, both, route)  2.62 us
  transfers between devices with their start and end apart: 17, of which 8 were waited for; matrix products, arithmetic and copies ran while one was open for 0% of the time, Pallas kernels for 15%

profile of v10, /device:TPU:0, one launch (start us, length us, event | category | flops | bytes accessed | tf_op | source)
XLA Modules:
  0.0 54.6 jit_solution(17279207028219518154)
XLA Ops:
  0.7 0.1 order.1
  0.8 0.8 %copy-done.3 = bf16[2,6,24,512]{3,2,1,0:T(8,128)(2,1)S(1)} copy-done((bf16[2,6,24,512]{3,2,1,0:T(8,128)(2,1)S(1)}, bf16[2,6,24,512]{3,2,1,0:T(8,128)(2,1)}, u32[]{:S(2)}) %copy-start.3) | copy-done | bytes 294936
  1.6 0.1 copy-done.2
  1.7 0.4 pack.1
  2.0 0.0 copy-start
  2.1 3.9 %collective-permute-start = (bf16[72,1024]{1,0:T(8,128)(2,1)S(1)}, bf16[72,1024]{1,0:T(8,128)(2,1)S(1)}, u32[]{:S(2)}, u32[]{:S(2)}) collective-permute-start(bf16[72,1024]{1,0:T(8,128)(2,1)S(1)} %get-tuple-element.62), channel_id=1, source_target_pairs={{0,24},{1,9},{2,26},{3,11},{4,28},{5,13},{6,30},{7,15},{8,0},{9,17... | collective-permute-start | bytes 442376 | tf_op jit(solution)/shard_map/ppermute | solution.py:451
  6.0 1.8 %collective-permute-start.1 = (bf16[36,1024]{1,0:T(8,128)(2,1)S(1)}, bf16[36,1024]{1,0:T(8,128)(2,1)S(1)}, u32[]{:S(2)}, u32[]{:S(2)}) collective-permute-start(bf16[36,1024]{1,0:T(8,128)(2,1)S(1)} %get-tuple-element.53._), channel_id=1, source_target_pairs={{0,7},{1,0},{2,1},{3,2},{4,3},{5,4},{6,5},{7,6},{8,15},{9,8},{10,9... | collective-permute-start | bytes 221192 | tf_op jit(solution)/shard_map/ppermute | solution.py:452
  7.8 0.6 %pack_rest.1 = (bf16[36,1024]{1,0:T(8,128)(2,1)S(1)}, bf16[36,1024]{1,0:T(8,128)(2,1)S(1)}, f32[72,1024]{1,0:T(8,128)S(1)}, f32[72,1024]{1,0:T(8,128)S(1)}) custom-call(bf16[36,1024]{1,0:T(8,128)(2,1)S(1)} %get-tuple-element.53._, bf16[288,512]{1,0:T(8,128)(2,1)S(1)} %bitcast.6, bf16[288,512]{1,0:T(8,128)(2,1)S(1)} %bitcast.8, ...), custom_call_target="tpu_custom_call" | custom-call | flops 500000000 | bytes 1525248 | tf_op jit(solution)/shard_map/pack_rest/pallas_call | solution.py:397
  8.4 1.0 %collective-permute-start.2 = (bf16[36,1024]{1,0:T(8,128)(2,1)S(1)}, bf16[36,1024]{1,0:T(8,128)(2,1)S(1)}, u32[]{:S(2)}, u32[]{:S(2)}) collective-permute-start(bf16[36,1024]{1,0:T(8,128)(2,1)S(1)} %get-tuple-element.67), channel_id=1, source_target_pairs={{0,15},{1,24},{2,9},{3,26},{4,11},{5,28},{6,13},{7,30},{8,23},{9,0... | collective-permute-start | bytes 221192 | tf_op jit(solution)/shard_map/ppermute | solution.py:454
  9.4 3.3 %collective-permute-start.3 = (bf16[36,1024]{1,0:T(8,128)(2,1)S(1)}, bf16[36,1024]{1,0:T(8,128)(2,1)S(1)}, u32[]{:S(2)}, u32[]{:S(2)}) collective-permute-start(bf16[36,1024]{1,0:T(8,128)(2,1)S(1)} %get-tuple-element.68), channel_id=1, source_target_pairs={{0,24},{1,9},{2,26},{3,11},{4,28},{5,13},{6,30},{7,15},{8,0},{9,17... | collective-permute-start | bytes 221192 | tf_op jit(solution)/shard_map/ppermute | solution.py:453
  12.8 0.7 %own.1 = (f32[72,512]{1,0:T(8,128)S(1)}, f32[72,1536]{1,0:T(8,128)S(1)}, f32[72,512]{1,0:T(8,128)S(1)}) custom-call(f32[72,1024]{1,0:T(8,128)S(1)} %get-tuple-element.58.inner_own.own, bf16[512,1536]{1,0:T(8,128)(2,1)S(1)} %copy-done, bf16[512,512]{1,0:T(8,128)(2,1)S(1)} %copy-done.1), custom_call_target="tpu_custom_call" | custom-call | flops 500000000 | bytes 3129344 | tf_op jit(solution)/shard_map/own/pallas_call | solution.py:397
  13.4 0.0 collective-permute-done.lat_in
  13.5 2.1 %inner.1 = (f32[2,256,512]{2,1,0:T(8,128)S(1)}, bf16[144,512]{1,0:T(8,128)(2,1)S(1)}, bf16[144,512]{1,0:T(8,128)(2,1)S(1)}, bf16[2,256,144]{2,1,0:T(8,128)(2,1)S...) custom-call(f32[72,1024]{1,0:T(8,128)S(1)} %get-tuple-element.58.inner_own.own, ...), custom_call_target="tpu_custom_call" | custom-call | flops 1000000000 | bytes 5505024 | tf_op jit(solution)/shard_map/inner/pallas_call | solution.py:397
  15.6 0.0 collective-permute-done.1.lon_in
  15.6 0.0 collective-permute-done.2.diag_in
  15.6 2.4 %outer.1 = (bf16[2,256,512]{2,1,0:T(8,128)(2,1)S(1)}, bf16[144,512]{1,0:T(8,128)(2,1)S(1)}, bf16[144,512]{1,0:T(8,128)(2,1)S(1)}, bf16[2,256,144]{2,1,0:T(8,128)...) custom-call(f32[72,1024]{1,0:T(8,128)S(1)} %get-tuple-element.66.own, ...), custom_call_target="tpu_custom_call" | custom-call | flops 1000000000 | bytes 5365760 | tf_op jit(solution)/shard_map/outer/pallas_call | solution.py:397
  18.0 0.1 collective-permute-start.4
  18.1 0.7 %keep.1 = (bf16[2,256,512]{2,1,0:T(8,128)(2,1)S(1)}, bf16[2,256,512]{2,1,0:T(8,128)(2,1)S(1)}) custom-call(bf16[2,256,144]{2,1,0:T(8,128)(2,1)S(1)} %get-tuple-element.63.refs_0_.refs_2_, bf16[144,2048]{1,0:T(8,128)(2,1)S(1)} %get-tuple-element.64.refs_1_.refs_3_, bf16[2,256,144]{2,1,0:T(8,128)(2,1)S(1)} %get-tuple-element.65.refs_2_, ...), custom_call_target="tpu_custom_call" | custom-call | flops 1000000000 | bytes 2818048 | tf_op jit(solution)/shard_map/keep/pallas_call | solution.py:397
  18.8 0.5 collective-permute-start.6
  19.3 0.6 %collective-permute-done.4.refs_1_ = bf16[2,256,512]{2,1,0:T(8,128)(2,1)S(1)} collective-permute-done((bf16[2,256,512]{2,1,0:T(8,128)(2,1)S(1)}, bf16[2,256,512]{2,1,0:T(8,128)(2,1)S(1)}, u32[]{:S(2)}, u32[]{:S(2)}) %collective-permute-start.4) | collective-permute-done | bytes 524320 | tf_op jit(solution)/shard_map/ppermute | solution.py:476
  20.0 0.1 chip_sum.1._
  20.1 1.6 %collective-permute-start.7 = (bf16[2,256,512]{2,1,0:T(8,128)(2,1)S(1)}, bf16[2,256,512]{2,1,0:T(8,128)(2,1)S(1)}, u32[]{:S(2)}, u32[]{:S(2)}) collective-permute-start(bf16[2,256,512]{2,1,0:T(8,128)(2,1)S(1)} %chip_sum.1._), channel_id=1, source_target_pairs={{0,8},{1,17},{2,10},{3,19},{4,12},{5,21},{6,14},{7,23},{8,0},{9,25... | collective-permute-start | bytes 1572872 | tf_op jit(solution)/shard_map/ppermute | solution.py:486
  21.6 1.2 %outputs.1 = (bf16[2,256,512]{2,1,0:T(8,128)(2,1)S(1)}, bf16[144,1024]{1,0:T(8,128)(2,1)S(1)}, bf16[144,1024]{1,0:T(8,128)(2,1)S(1)}) custom-call(bf16[2,256,512]{2,1,0:T(8,128)(2,1)S(1)} %chip_sum.1._, bf16[144,512]{1,0:T(8,128)(2,1)S(1)} %get-tuple-element.75.refs_0_, bf16[144,512]{1,0:T(8,128)(2,1)S(1)} %get-tuple-element.76.refs_1_, ...), custom_call_target="tpu_custom_call" | custom-call | flops 1000000000 | bytes 5799936 | tf_op jit(solution)/shard_map/outputs/pallas_call | solution.py:397
  22.8 0.1 pack_lon.1
  23.0 0.1 collective-permute-start.5
  23.1 5.6 %collective-permute-done.5._.lon_in = bf16[36,1024]{1,0:T(8,128)(2,1)S(1)} collective-permute-done((bf16[36,1024]{1,0:T(8,128)(2,1)S(1)}, bf16[36,1024]{1,0:T(8,128)(2,1)S(1)}, u32[]{:S(2)}, u32[]{:S(2)}) %collective-permute-start.5) | collective-permute-done | bytes 73760 | tf_op jit(solution)/shard_map/ppermute | solution.py:497
  28.7 0.6 %collective-permute-done.7.refs_2_ = bf16[2,256,512]{2,1,0:T(8,128)(2,1)S(1)} collective-permute-done((bf16[2,256,512]{2,1,0:T(8,128)(2,1)S(1)}, bf16[2,256,512]{2,1,0:T(8,128)(2,1)S(1)}, u32[]{:S(2)}, u32[]{:S(2)}) %collective-permute-start.7) | collective-permute-done | bytes 524320 | tf_op jit(solution)/shard_map/ppermute | solution.py:486
  29.3 0.2 halve1.1
  29.5 1.1 %collective-permute-start.8 = (bf16[1,256,512]{2,1,0:T(8,128)(2,1)S(1)}, bf16[1,256,512]{2,1,0:T(8,128)(2,1)S(1)}, u32[]{:S(2)}, u32[]{:S(2)}) collective-permute-start(bf16[1,256,512]{2,1,0:T(8,128)(2,1)S(1)} %get-tuple-element.84), channel_id=1, source_target_pairs={{0,16},{1,9},{2,18},{3,11},{4,20},{5,13},{6,22},{7,15},{8,24},{9,1... | collective-permute-start | bytes 786440 | tf_op jit(solution)/shard_map/ppermute | solution.py:486
  30.6 5.4 %collective-permute-done.8.refs_1_ = bf16[1,256,512]{2,1,0:T(8,128)(2,1)S(1)} collective-permute-done((bf16[1,256,512]{2,1,0:T(8,128)(2,1)S(1)}, bf16[1,256,512]{2,1,0:T(8,128)(2,1)S(1)}, u32[]{:S(2)}, u32[]{:S(2)}) %collective-permute-start.8) | collective-permute-done | bytes 262176 | tf_op jit(solution)/shard_map/ppermute | solution.py:486
  36.0 0.1 line_parts.1
  36.0 2.3 %collective-permute-start.11 = (bf16[64,512]{1,0:T(8,128)(2,1)S(1)}, bf16[64,512]{1,0:T(8,128)(2,1)S(1)}, u32[]{:S(2)}, u32[]{:S(2)}) collective-permute-start(bf16[64,512]{1,0:T(8,128)(2,1)S(1)} %get-tuple-element.91), channel_id=1, source_target_pairs={{0,6},{1,7},{2,4},{3,5},{4,2},{5,3},{6,0},{7,1},{8,14},{9,15},{10,... | collective-permute-start | bytes 196616 | tf_op jit(solution)/shard_map/ppermute | solution.py:512
  38.3 2.1 %collective-permute-start.13 = (bf16[64,512]{1,0:T(8,128)(2,1)S(1)}, bf16[64,512]{1,0:T(8,128)(2,1)S(1)}, u32[]{:S(2)}, u32[]{:S(2)}) collective-permute-start(bf16[64,512]{1,0:T(8,128)(2,1)S(1)} %get-tuple-element.85._), channel_id=1, source_target_pairs={{0,2},{1,3},{2,0},{3,1},{4,6},{5,7},{6,4},{7,5},{8,10},{9,11},{10,... | collective-permute-start | bytes 196616 | tf_op jit(solution)/shard_map/ppermute | solution.py:512
  40.5 0.2 pack_back.1
  40.7 1.5 %collective-permute-start.9 = (bf16[108,1024]{1,0:T(8,128)(2,1)S(1)}, bf16[108,1024]{1,0:T(8,128)(2,1)S(1)}, u32[]{:S(2)}, u32[]{:S(2)}) collective-permute-start(bf16[108,1024]{1,0:T(8,128)(2,1)S(1)} %get-tuple-element.86), channel_id=1, source_target_pairs={{24,0},{9,1},{26,2},{11,3},{28,4},{13,5},{30,6},{15,7},{0,8},{17,9... | collective-permute-start | bytes 663560 | tf_op jit(solution)/shard_map/ppermute | solution.py:520
  42.2 0.7 %collective-permute-done.11.refs_1_ = bf16[64,512]{1,0:T(8,128)(2,1)S(1)} collective-permute-done((bf16[64,512]{1,0:T(8,128)(2,1)S(1)}, bf16[64,512]{1,0:T(8,128)(2,1)S(1)}, u32[]{:S(2)}, u32[]{:S(2)}) %collective-permute-start.11) | collective-permute-done | bytes 65568 | tf_op jit(solution)/shard_map/ppermute | solution.py:512
  42.9 1.3 %collective-permute-done.12.refs_2_ = bf16[64,512]{1,0:T(8,128)(2,1)S(1)} collective-permute-done((bf16[64,512]{1,0:T(8,128)(2,1)S(1)}, bf16[64,512]{1,0:T(8,128)(2,1)S(1)}, u32[]{:S(2)}, u32[]{:S(2)}) %collective-permute-start.12) | collective-permute-done | bytes 65568 | tf_op jit(solution)/shard_map/ppermute | solution.py:512
  44.3 1.9 %collective-permute-start.16 = (bf16[64,512]{1,0:T(8,128)(2,1)S(1)}, bf16[64,512]{1,0:T(8,128)(2,1)S(1)}, u32[]{:S(2)}, u32[]{:S(2)}) collective-permute-start(bf16[64,512]{1,0:T(8,128)(2,1)S(1)} %line_sum.1.refs_0_), channel_id=1, source_target_pairs={{0,24},{8,16},{16,8},{24,0},{1,25},{9,17},{17,9},{25,1},{2,26},{10... | collective-permute-start | bytes 196616 | tf_op jit(solution)/shard_map/ppermute | solution.py:524
  46.1 0.8 %collective-permute-start.15 = (bf16[64,512]{1,0:T(8,128)(2,1)S(1)}, bf16[64,512]{1,0:T(8,128)(2,1)S(1)}, u32[]{:S(2)}, u32[]{:S(2)}) collective-permute-start(bf16[64,512]{1,0:T(8,128)(2,1)S(1)} %line_sum.1.refs_0_), channel_id=1, source_target_pairs={{0,16},{8,24},{16,0},{24,8},{1,17},{9,25},{17,1},{25,9},{2,18},{10... | collective-permute-start | bytes 196616 | tf_op jit(solution)/shard_map/ppermute | solution.py:524
  46.9 0.9 %collective-permute-start.14 = (bf16[64,512]{1,0:T(8,128)(2,1)S(1)}, bf16[64,512]{1,0:T(8,128)(2,1)S(1)}, u32[]{:S(2)}, u32[]{:S(2)}) collective-permute-start(bf16[64,512]{1,0:T(8,128)(2,1)S(1)} %line_sum.1.refs_0_), channel_id=1, source_target_pairs={{0,8},{8,0},{16,24},{24,16},{1,9},{9,1},{17,25},{25,17},{2,10},{10... | collective-permute-start | bytes 196616 | tf_op jit(solution)/shard_map/ppermute | solution.py:524
  47.8 0.6 %collective-permute-done.9.lat_in = bf16[108,1024]{1,0:T(8,128)(2,1)S(1)} collective-permute-done((bf16[108,1024]{1,0:T(8,128)(2,1)S(1)}, bf16[108,1024]{1,0:T(8,128)(2,1)S(1)}, u32[]{:S(2)}, u32[]{:S(2)}) %collective-permute-start.9) | collective-permute-done | bytes 221216 | tf_op jit(solution)/shard_map/ppermute | solution.py:520
  48.5 0.6 %place.1.placed = f32[288,1024]{1,0:T(8,128)S(1)} custom-call(bf16[144,1024]{1,0:T(8,128)(2,1)S(1)} %get-tuple-element.79.inner_results, bf16[144,1024]{1,0:T(8,128)(2,1)S(1)} %get-tuple-element.80.outer_results, bf16[108,1024]{1,0:T(8,128)(2,1)S(1)} %collective-permute-done.9.lat_in), custom_call_target="tpu_custom_call" | custom-call | bytes 1990656 | tf_op jit(solution)/shard_map/place/pallas_call | solution.py:397
  49.1 1.2 %place_rest.1 = (bf16[288,512]{1,0:T(8,128)(2,1)}, bf16[288,512]{1,0:T(8,128)(2,1)}, f32[8,128]{1,0:T(8,128)S(1)}) custom-call(f32[288,1024]{1,0:T(8,128)S(1)} %place.1.placed, bf16[36,1024]{1,0:T(8,128)(2,1)S(1)} %collective-permute-done.5._.lon_in, bf16[36,1024]{1,0:T(8,128)(2,1)S(1)} %collective-permute-done.10.diag_in), custom_call_target="tpu_custom_call" | custom-call | bytes 1921024 | tf_op jit(solution)/shard_map/place_rest/pallas_call | solution.py:397
  50.3 1.4 %collective-permute-done.16.refs_2_ = bf16[64,512]{1,0:T(8,128)(2,1)S(1)} collective-permute-done((bf16[64,512]{1,0:T(8,128)(2,1)S(1)}, bf16[64,512]{1,0:T(8,128)(2,1)S(1)}, u32[]{:S(2)}, u32[]{:S(2)}) %collective-permute-start.16) | collective-permute-done | bytes 65568 | tf_op jit(solution)/shard_map/ppermute | solution.py:524
  51.6 0.0 collective-permute-done.15.refs_1_
  51.6 0.8 %finish.1 = (f32[64,1536]{1,0:T(8,128)}, f32[64,512]{1,0:T(8,128)}) custom-call(f32[8,128]{1,0:T(8,128)S(1)} %get-tuple-element.93._, bf16[64,512]{1,0:T(8,128)(2,1)S(1)} %line_sum.1.refs_0_, bf16[64,512]{1,0:T(8,128)(2,1)S(1)} %collective-permute-done.15.refs_1_, bf16[64,512]{1,0:T(8,128)(2,1)S(1)} %collective-permute-done.16.refs_2_), custom_call_target="tpu_custom_call" | custom-call | bytes 724992 | tf_op jit(solution)/shard_map/finish/pallas_call | solution.py:397
  52.5 0.6 %copy-done.4 = bf16[64,512]{1,0:T(8,128)(2,1)} copy-done((bf16[64,512]{1,0:T(8,128)(2,1)}, bf16[64,512]{1,0:T(8,128)(2,1)S(1)}, u32[]{:S(2)}) %copy-start.4) | copy-done | bytes 65560
  53.1 1.5 %last_share.1 = (f32[64,1536]{1,0:T(8,128)}, f32[64,512]{1,0:T(8,128)}) custom-call(bf16[64,512]{1,0:T(8,128)(2,1)} %copy-done.4, f32[64,1536]{1,0:T(8,128)} %get-tuple-element.94.qkv_in, f32[64,512]{1,0:T(8,128)} %get-tuple-element.95.proj_in), custom_call_target="tpu_custom_call", output_to_operand_aliasing={{0}: (1, {}), {1}: (2, {})} | custom-call | tf_op jit(solution)/shard_map/last_share/pallas_call | solution.py:542
  (14 shorter events, 0.1 us)
Async XLA Ops:
  0.6 1.0 %copy-start.3 = (bf16[2,6,24,512]{3,2,1,0:T(8,128)(2,1)S(1)}, bf16[2,6,24,512]{3,2,1,0:T(8,128)(2,1)}, u32[]{:S(2)}) copy-start(bf16[2,6,24,512]{3,2,1,0:T(8,128)(2,1)} %param.5) | copy-start | bytes 884740
  0.6 1.0 %copy-start.2 = (bf16[2,6,24,512]{3,2,1,0:T(8,128)(2,1)S(1)}, bf16[2,6,24,512]{3,2,1,0:T(8,128)(2,1)}, u32[]{:S(2)}) copy-start(bf16[2,6,24,512]{3,2,1,0:T(8,128)(2,1)} %param.4) | copy-start | bytes 884740
  1.7 11.1 %copy-start.1 = (bf16[512,512]{1,0:T(8,128)(2,1)S(1)}, bf16[512,512]{1,0:T(8,128)(2,1)}, u32[]{:S(2)}) copy-start(bf16[512,512]{1,0:T(8,128)(2,1)} %refs_9_.1) | copy-start | bytes 1572868
  2.0 10.7 %copy-start = (bf16[512,1536]{1,0:T(8,128)(2,1)S(1)}, bf16[512,1536]{1,0:T(8,128)(2,1)}, u32[]{:S(2)}) copy-start(bf16[512,1536]{1,0:T(8,128)(2,1)} %refs_8_.1) | copy-start | bytes 4718596
  2.1 11.4 %collective-permute-start = (bf16[72,1024]{1,0:T(8,128)(2,1)S(1)}, bf16[72,1024]{1,0:T(8,128)(2,1)S(1)}, u32[]{:S(2)}, u32[]{:S(2)}) collective-permute-start(bf16[72,1024]{1,0:T(8,128)(2,1)S(1)} %get-tuple-element.62), channel_id=1, source_target_pairs={{0,24},{1,9},{2,26},{3,11},{4,28},{5,13},{6,30},{7,15},{8,0},{9,17... | collective-permute-start | bytes 442376 | tf_op jit(solution)/shard_map/ppermute | solution.py:451
  6.0 9.6 %collective-permute-start.1 = (bf16[36,1024]{1,0:T(8,128)(2,1)S(1)}, bf16[36,1024]{1,0:T(8,128)(2,1)S(1)}, u32[]{:S(2)}, u32[]{:S(2)}) collective-permute-start(bf16[36,1024]{1,0:T(8,128)(2,1)S(1)} %get-tuple-element.53._), channel_id=1, source_target_pairs={{0,7},{1,0},{2,1},{3,2},{4,3},{5,4},{6,5},{7,6},{8,15},{9,8},{10,9... | collective-permute-start | bytes 221192 | tf_op jit(solution)/shard_map/ppermute | solution.py:452
  8.4 7.2 %collective-permute-start.2 = (bf16[36,1024]{1,0:T(8,128)(2,1)S(1)}, bf16[36,1024]{1,0:T(8,128)(2,1)S(1)}, u32[]{:S(2)}, u32[]{:S(2)}) collective-permute-start(bf16[36,1024]{1,0:T(8,128)(2,1)S(1)} %get-tuple-element.67), channel_id=1, source_target_pairs={{0,15},{1,24},{2,9},{3,26},{4,11},{5,28},{6,13},{7,30},{8,23},{9,0... | collective-permute-start | bytes 221192 | tf_op jit(solution)/shard_map/ppermute | solution.py:454
  9.4 6.2 %collective-permute-start.3 = (bf16[36,1024]{1,0:T(8,128)(2,1)S(1)}, bf16[36,1024]{1,0:T(8,128)(2,1)S(1)}, u32[]{:S(2)}, u32[]{:S(2)}) collective-permute-start(bf16[36,1024]{1,0:T(8,128)(2,1)S(1)} %get-tuple-element.68), channel_id=1, source_target_pairs={{0,24},{1,9},{2,26},{3,11},{4,28},{5,13},{6,30},{7,15},{8,0},{9,17... | collective-permute-start | bytes 221192 | tf_op jit(solution)/shard_map/ppermute | solution.py:453
  18.0 2.0 %collective-permute-start.4 = (bf16[2,256,512]{2,1,0:T(8,128)(2,1)S(1)}, bf16[2,256,512]{2,1,0:T(8,128)(2,1)S(1)}, u32[]{:S(2)}, u32[]{:S(2)}) collective-permute-start(bf16[2,256,512]{2,1,0:T(8,128)(2,1)S(1)} %get-tuple-element.74), channel_id=1, source_target_pairs={{0,1},{1,0},{2,3},{3,2},{4,5},{5,4},{6,7},{7,6},{8,9},{9,8},{10,11... | collective-permute-start | bytes 1572872 | tf_op jit(solution)/shard_map/ppermute | solution.py:476
  18.8 4.3 %collective-permute-start.6 = (bf16[2,256,512]{2,1,0:T(8,128)(2,1)S(1)}, bf16[2,256,512]{2,1,0:T(8,128)(2,1)S(1)}, u32[]{:S(2)}, u32[]{:S(2)}) collective-permute-start(bf16[2,256,512]{2,1,0:T(8,128)(2,1)S(1)} %get-tuple-element.82), channel_id=1, source_target_pairs={{0,1},{1,0},{2,3},{3,2},{4,5},{5,4},{6,7},{7,6},{8,9},{9,8},{10,11... | collective-permute-start | bytes 1572872 | tf_op jit(solution)/shard_map/ppermute | solution.py:478
  20.1 9.2 %collective-permute-start.7 = (bf16[2,256,512]{2,1,0:T(8,128)(2,1)S(1)}, bf16[2,256,512]{2,1,0:T(8,128)(2,1)S(1)}, u32[]{:S(2)}, u32[]{:S(2)}) collective-permute-start(bf16[2,256,512]{2,1,0:T(8,128)(2,1)S(1)} %chip_sum.1._), channel_id=1, source_target_pairs={{0,8},{1,17},{2,10},{3,19},{4,12},{5,21},{6,14},{7,23},{8,0},{9,25... | collective-permute-start | bytes 1572872 | tf_op jit(solution)/shard_map/ppermute | solution.py:486
  23.0 5.7 %collective-permute-start.5 = (bf16[36,1024]{1,0:T(8,128)(2,1)S(1)}, bf16[36,1024]{1,0:T(8,128)(2,1)S(1)}, u32[]{:S(2)}, u32[]{:S(2)}) collective-permute-start(bf16[36,1024]{1,0:T(8,128)(2,1)S(1)} %pack_lon.1), channel_id=1, source_target_pairs={{7,0},{0,1},{1,2},{2,3},{3,4},{4,5},{5,6},{6,7},{15,8},{8,9},{9,10... | collective-permute-start | bytes 221192 | tf_op jit(solution)/shard_map/ppermute | solution.py:497
  29.5 6.4 %collective-permute-start.8 = (bf16[1,256,512]{2,1,0:T(8,128)(2,1)S(1)}, bf16[1,256,512]{2,1,0:T(8,128)(2,1)S(1)}, u32[]{:S(2)}, u32[]{:S(2)}) collective-permute-start(bf16[1,256,512]{2,1,0:T(8,128)(2,1)S(1)} %get-tuple-element.84), channel_id=1, source_target_pairs={{0,16},{1,9},{2,18},{3,11},{4,20},{5,13},{6,22},{7,15},{8,24},{9,1... | collective-permute-start | bytes 786440 | tf_op jit(solution)/shard_map/ppermute | solution.py:486
  36.0 6.9 %collective-permute-start.11 = (bf16[64,512]{1,0:T(8,128)(2,1)S(1)}, bf16[64,512]{1,0:T(8,128)(2,1)S(1)}, u32[]{:S(2)}, u32[]{:S(2)}) collective-permute-start(bf16[64,512]{1,0:T(8,128)(2,1)S(1)} %get-tuple-element.91), channel_id=1, source_target_pairs={{0,6},{1,7},{2,4},{3,5},{4,2},{5,3},{6,0},{7,1},{8,14},{9,15},{10,... | collective-permute-start | bytes 196616 | tf_op jit(solution)/shard_map/ppermute | solution.py:512
  38.3 5.9 %collective-permute-start.12 = (bf16[64,512]{1,0:T(8,128)(2,1)S(1)}, bf16[64,512]{1,0:T(8,128)(2,1)S(1)}, u32[]{:S(2)}, u32[]{:S(2)}) collective-permute-start(bf16[64,512]{1,0:T(8,128)(2,1)S(1)} %get-tuple-element.92), channel_id=1, source_target_pairs={{0,4},{1,5},{2,6},{3,7},{4,0},{5,1},{6,2},{7,3},{8,12},{9,13},{10,... | collective-permute-start | bytes 196616 | tf_op jit(solution)/shard_map/ppermute | solution.py:512
  38.3 5.9 %collective-permute-start.13 = (bf16[64,512]{1,0:T(8,128)(2,1)S(1)}, bf16[64,512]{1,0:T(8,128)(2,1)S(1)}, u32[]{:S(2)}, u32[]{:S(2)}) collective-permute-start(bf16[64,512]{1,0:T(8,128)(2,1)S(1)} %get-tuple-element.85._), channel_id=1, source_target_pairs={{0,2},{1,3},{2,0},{3,1},{4,6},{5,7},{6,4},{7,5},{8,10},{9,11},{10,... | collective-permute-start | bytes 196616 | tf_op jit(solution)/shard_map/ppermute | solution.py:512
  40.7 7.8 %collective-permute-start.9 = (bf16[108,1024]{1,0:T(8,128)(2,1)S(1)}, bf16[108,1024]{1,0:T(8,128)(2,1)S(1)}, u32[]{:S(2)}, u32[]{:S(2)}) collective-permute-start(bf16[108,1024]{1,0:T(8,128)(2,1)S(1)} %get-tuple-element.86), channel_id=1, source_target_pairs={{24,0},{9,1},{26,2},{11,3},{28,4},{13,5},{30,6},{15,7},{0,8},{17,9... | collective-permute-start | bytes 663560 | tf_op jit(solution)/shard_map/ppermute | solution.py:520
  42.2 6.8 %collective-permute-start.10 = (bf16[36,1024]{1,0:T(8,128)(2,1)S(1)}, bf16[36,1024]{1,0:T(8,128)(2,1)S(1)}, u32[]{:S(2)}, u32[]{:S(2)}) collective-permute-start(bf16[36,1024]{1,0:T(8,128)(2,1)S(1)} %get-tuple-element.87), channel_id=1, source_target_pairs={{15,0},{24,1},{9,2},{26,3},{11,4},{28,5},{13,6},{30,7},{23,8},{0,9... | collective-permute-start | bytes 221192 | tf_op jit(solution)/shard_map/ppermute | solution.py:521
  44.3 7.4 %collective-permute-start.16 = (bf16[64,512]{1,0:T(8,128)(2,1)S(1)}, bf16[64,512]{1,0:T(8,128)(2,1)S(1)}, u32[]{:S(2)}, u32[]{:S(2)}) collective-permute-start(bf16[64,512]{1,0:T(8,128)(2,1)S(1)} %line_sum.1.refs_0_), channel_id=1, source_target_pairs={{0,24},{8,16},{16,8},{24,0},{1,25},{9,17},{17,9},{25,1},{2,26},{10... | collective-permute-start | bytes 196616 | tf_op jit(solution)/shard_map/ppermute | solution.py:524
  46.1 5.5 %collective-permute-start.15 = (bf16[64,512]{1,0:T(8,128)(2,1)S(1)}, bf16[64,512]{1,0:T(8,128)(2,1)S(1)}, u32[]{:S(2)}, u32[]{:S(2)}) collective-permute-start(bf16[64,512]{1,0:T(8,128)(2,1)S(1)} %line_sum.1.refs_0_), channel_id=1, source_target_pairs={{0,16},{8,24},{16,0},{24,8},{1,17},{9,25},{17,1},{25,9},{2,18},{10... | collective-permute-start | bytes 196616 | tf_op jit(solution)/shard_map/ppermute | solution.py:524
  46.9 5.6 %collective-permute-start.14 = (bf16[64,512]{1,0:T(8,128)(2,1)S(1)}, bf16[64,512]{1,0:T(8,128)(2,1)S(1)}, u32[]{:S(2)}, u32[]{:S(2)}) collective-permute-start(bf16[64,512]{1,0:T(8,128)(2,1)S(1)} %line_sum.1.refs_0_), channel_id=1, source_target_pairs={{0,8},{8,0},{16,24},{24,16},{1,9},{9,1},{17,25},{25,17},{2,10},{10... | collective-permute-start | bytes 196616 | tf_op jit(solution)/shard_map/ppermute | solution.py:524
  52.5 0.6 %copy-start.4 = (bf16[64,512]{1,0:T(8,128)(2,1)}, bf16[64,512]{1,0:T(8,128)(2,1)S(1)}, u32[]{:S(2)}) copy-start(bf16[64,512]{1,0:T(8,128)(2,1)S(1)} %collective-permute-done.14.part) | copy-start | bytes 196612

commit v11 on v9

--- a/solution.py
+++ b/solution.py
@@ -21,7 +21,7 @@
 LANES = 128
 
 epsilon = 1e-05
-LONG = 13 * 10**8
+LONG = 5 * 10**9
 LOAD = 5 * 10**9
 BF = jnp.bfloat16
 F32 = jnp.float32
@@ -294,27 +294,32 @@
     lon_out[...] = dot(puts(last_rows, QUARTER, HALF), outer_x, NN).astype(BF)
 
 
-def pack_back_kernel(_, inner_results, outer_results, lat_out, diag_out):
+def place_own_kernel(_, inner_results, outer_results, placed, lat_out):
+    _, _, _, _, inner_own, outer_own = (source for source, _ in sources())
+
+    def only_first(source):
+        return lambda v: jnp.where(v < HALF, source(v), -1)
+
+    placed[...] = dot(puts(only_first(inner_own), TOKENS, WIN), inner_results[...], NN) + dot(
+        puts(only_first(outer_own), TOKENS, WIN), outer_results[...], NN
+    )
     inner_y = inner_results[...].astype(F32)[HALF:]
     outer_y = outer_results[...].astype(F32)[HALF:].astype(BF)
     lat_out[...] = jnp.concatenate([inner_y, dot(puts(first_rows, QUARTER, HALF), outer_y, NN)], axis=0).astype(BF)
+
+
+def pack_diag_kernel(_, outer_results, diag_out):
+    outer_y = outer_results[...].astype(F32)[HALF:].astype(BF)
     diag_out[...] = dot(puts(last_rows, QUARTER, HALF), outer_y, NN).astype(BF)
 
 
-def place_kernel(inner_results, outer_results, lat_in, placed):
-    inner_lat, outer_lat, _, _, inner_own, outer_own = (source for source, _ in sources())
+def place_lat_kernel(so_far, lat_in, placed):
+    inner_lat, outer_lat, _, _, _, _ = (source for source, _ in sources())
 
     def lat(v):
         return jnp.where(v < HALF, inner_lat(v), outer_lat(v - HALF))
 
-    def only_first(source):
-        return lambda v: jnp.where(v < HALF, source(v), -1)
-
-    placed[...] = (
-        dot(puts(only_first(inner_own), TOKENS, WIN), inner_results[...], NN)
-        + dot(puts(only_first(outer_own), TOKENS, WIN), outer_results[...], NN)
-        + dot(puts(lat, TOKENS, HALF + QUARTER), lat_in[...], NN)
-    )
+    placed[...] = so_far[...] + dot(puts(lat, TOKENS, HALF + QUARTER), lat_in[...], NN)
 
 
 def place_rest_kernel(placed, lon_in, diag_in, field_out, d_fields, done):
@@ -343,6 +348,10 @@
     for step, out in enumerate((keep, *sends)):
         at = slice(step * rows, (step + 1) * rows)
         out[...] = sum(part[0, at].astype(F32) for part in parts).astype(out.dtype)
+
+
+def line_sum_kernel(_, *refs):
+    sum_kernel(*refs)
 
 
 def sum_kernel(*refs):
@@ -485,29 +494,30 @@
         send, keep = call(halve_kernel, [stay, stay], lon_home, *kept, name=f"halve{slots}", unread=(0,))
         kept = [keep, halving(phase, send)]
 
+    placed, lat_back = call(
+        place_own_kernel, [((TOKENS, 2 * width), F32), ((HALF + QUARTER, 2 * width), BF)], send, *results,
+        name="place_own", unread=(0,),
+    )
+    lat_home = lax.ppermute(lat_back, both, back(lat_route))
+
     rows = width // lon_size
     share = ((rows, split[2]), BF)
     parts = call(
-        functools.partial(line_parts_kernel, len(kept)), [share] * (lon_size // 2), *kept, name="line_parts"
+        functools.partial(line_parts_kernel, len(kept)), [share] * (lon_size // 2), *kept, name="line_parts", flops=LONG
     )
     arrived = [
         lax.ppermute(parts[step], "lon", [(j, j ^ (2 * step)) for j in range(lon_size)])
         for step in range(lon_size // 2 - 1, 0, -1)
     ]
-    lat_back, diag_back = call(
-        pack_back_kernel, [((HALF + QUARTER, 2 * width), BF), quarter],
-        parts[1], *results,
-        name="pack_back", unread=(0,),
-    )
-    lat_home = lax.ppermute(lat_back, both, back(lat_route))
+    (diag_back,) = call(pack_diag_kernel, [quarter], parts[1], results[1], name="pack_diag", unread=(0,))
     diag_home = lax.ppermute(diag_back, both, back(diag_route))
-    (line_sum,) = call(sum_kernel, [share], parts[0], *arrived, name="line_sum", flops=LONG)
+    (placed,) = call(place_lat_kernel, [((TOKENS, 2 * width), F32)], placed, lat_home, name="place_lat")
+    (line_sum,) = call(
+        line_sum_kernel, [share], placed, parts[0], *arrived, name="line_sum", unread=(0,)
+    )
     shared = [
         lax.ppermute(line_sum, "lat", [(i, i ^ step) for i in range(lat_size)]) for step in range(1, lat_size)
     ]
-    (placed,) = call(
-        place_kernel, [((TOKENS, 2 * width), F32)], *results, lat_home, name="place"
-    )
     field_out, d_fields, done = call(
         place_rest_kernel,
         [((TOKENS, width), BF), ((TOKENS, width), BF), ((8, LANES), F32)],

time: 52.1 us -> 54.4 us (1.044)
  waiting for transfers between devices: 15.4 us -> 16.8 us
  starting transfers between devices: 23.3 us -> 24.1 us
    ppermute x3, waiting for transfers between devices: 2.04 us -> 3.99 us  [per_device(): lax.ppermute(parts[step], 'lon', [(j, j ^ 2 * step) for j in range(lon_si...]
    ppermute x2, waiting for transfers between devices: 5.08 us -> 3.42 us  [halving(): return lax.ppermute(send, both, route)]
    ppermute x3, waiting for transfers between devices: 1.53 us -> 3.07 us  [per_device(): lax.ppermute(line_sum, 'lat', [(i, i ^ step) for i in range(lat_size)])]
    ppermute x3, starting transfers between devices: 3.55 us -> 4.96 us  [per_device(): lax.ppermute(line_sum, 'lat', [(i, i ^ step) for i in range(lat_size)])]
    ppermute x1, starting transfers between devices: 2.07 us -> 1.18 us  [per_device(): lat_home = lax.ppermute(lat_back, both, back(lat_route))]
    pallas_call x17 -> x18, Pallas kernels: 11.5 us -> 11.6 us  [call(): pl.pallas_call(kernel, out_shape=shapes, in_specs=[anywhere if i in unrea...]
  transfers between devices with their start and end apart: 17 -> 17, of which waited for: 9 -> 9; matrix products, arithmetic and copies ran while one was open for 0% -> 0% of each run, Pallas kernels for 15% -> 14%
where the time goes in v11:
time: 54.4 us; the launch traced here: 54.3 us
  starting transfers between devices  24.1 us (44%)
  waiting for transfers between devices  16.8 us (31%)
  Pallas kernels  11.6 us (21%)
  local copies, waits for them, and re-layouts  0.94 us (2%)
  between operations  0.81 us (1%)
    pallas_call x18, Pallas kernels, call(): pl.pallas_call(kernel, out_shape=shapes, in_specs=[anywhere if i in unrea...  11.6 us
    ppermute x1, waiting for transfers between devices, per_device(): lon_home = lax.ppermute(lon_back, both, back(lon_route))  5.64 us
    ppermute x3, starting transfers between devices, per_device(): lax.ppermute(line_sum, 'lat', [(i, i ^ step) for i in range(lat_size)])  4.96 us
    ppermute x3, starting transfers between devices, per_device(): lax.ppermute(parts[step], 'lon', [(j, j ^ 2 * step) for j in range(lon_si...  4.7 us
    ppermute x3, waiting for transfers between devices, per_device(): lax.ppermute(parts[step], 'lon', [(j, j ^ 2 * step) for j in range(lon_si...  3.99 us
    ppermute x1, starting transfers between devices, per_device(): inner_in = lax.ppermute(inner_lat, both, lat_route)  3.94 us
    ppermute x2, starting transfers between devices, halving(): return lax.ppermute(send, both, route)  3.67 us
    ppermute x2, waiting for transfers between devices, halving(): return lax.ppermute(send, both, route)  3.42 us
  transfers between devices with their start and end apart: 17, of which 9 were waited for; matrix products, arithmetic and copies ran while one was open for 0% of the time, Pallas kernels for 14%

profile of v11, /device:TPU:0, one launch (start us, length us, event | category | flops | bytes accessed | tf_op | source)
XLA Modules:
  0.0 54.3 jit_solution(10119193756500730488)
XLA Ops:
  0.7 0.1 order.1
  0.8 0.8 %copy-done.3 = bf16[2,6,24,512]{3,2,1,0:T(8,128)(2,1)S(1)} copy-done((bf16[2,6,24,512]{3,2,1,0:T(8,128)(2,1)S(1)}, bf16[2,6,24,512]{3,2,1,0:T(8,128)(2,1)}, u32[]{:S(2)}) %copy-start.3) | copy-done | bytes 294936
  1.6 0.1 copy-done.2
  1.7 0.4 pack.1
  2.0 0.0 copy-start
  2.1 3.9 %collective-permute-start = (bf16[72,1024]{1,0:T(8,128)(2,1)S(1)}, bf16[72,1024]{1,0:T(8,128)(2,1)S(1)}, u32[]{:S(2)}, u32[]{:S(2)}) collective-permute-start(bf16[72,1024]{1,0:T(8,128)(2,1)S(1)} %get-tuple-element.60), channel_id=1, source_target_pairs={{0,24},{1,9},{2,26},{3,11},{4,28},{5,13},{6,30},{7,15},{8,0},{9,17... | collective-permute-start | bytes 442376 | tf_op jit(solution)/shard_map/ppermute | solution.py:442
  6.0 1.8 %collective-permute-start.1 = (bf16[36,1024]{1,0:T(8,128)(2,1)S(1)}, bf16[36,1024]{1,0:T(8,128)(2,1)S(1)}, u32[]{:S(2)}, u32[]{:S(2)}) collective-permute-start(bf16[36,1024]{1,0:T(8,128)(2,1)S(1)} %get-tuple-element.51._), channel_id=1, source_target_pairs={{0,7},{1,0},{2,1},{3,2},{4,3},{5,4},{6,5},{7,6},{8,15},{9,8},{10,9... | collective-permute-start | bytes 221192 | tf_op jit(solution)/shard_map/ppermute | solution.py:443
  7.8 0.6 %pack_rest.1 = (bf16[36,1024]{1,0:T(8,128)(2,1)S(1)}, bf16[36,1024]{1,0:T(8,128)(2,1)S(1)}, f32[72,1024]{1,0:T(8,128)S(1)}, f32[72,1024]{1,0:T(8,128)S(1)}) custom-call(bf16[36,1024]{1,0:T(8,128)(2,1)S(1)} %get-tuple-element.51._, bf16[288,512]{1,0:T(8,128)(2,1)S(1)} %bitcast.6, bf16[288,512]{1,0:T(8,128)(2,1)S(1)} %bitcast.8, ...), custom_call_target="tpu_custom_call" | custom-call | flops 500000000 | bytes 1525248 | tf_op jit(solution)/shard_map/pack_rest/pallas_call | solution.py:388
  8.4 1.5 %collective-permute-start.2 = (bf16[36,1024]{1,0:T(8,128)(2,1)S(1)}, bf16[36,1024]{1,0:T(8,128)(2,1)S(1)}, u32[]{:S(2)}, u32[]{:S(2)}) collective-permute-start(bf16[36,1024]{1,0:T(8,128)(2,1)S(1)} %get-tuple-element.65), channel_id=1, source_target_pairs={{0,24},{1,9},{2,26},{3,11},{4,28},{5,13},{6,30},{7,15},{8,0},{9,17... | collective-permute-start | bytes 221192 | tf_op jit(solution)/shard_map/ppermute | solution.py:444
  9.9 1.6 %collective-permute-start.3 = (bf16[36,1024]{1,0:T(8,128)(2,1)S(1)}, bf16[36,1024]{1,0:T(8,128)(2,1)S(1)}, u32[]{:S(2)}, u32[]{:S(2)}) collective-permute-start(bf16[36,1024]{1,0:T(8,128)(2,1)S(1)} %get-tuple-element.66), channel_id=1, source_target_pairs={{0,15},{1,24},{2,9},{3,26},{4,11},{5,28},{6,13},{7,30},{8,23},{9,0... | collective-permute-start | bytes 221192 | tf_op jit(solution)/shard_map/ppermute | solution.py:445
  11.5 0.7 %own.1 = (f32[72,512]{1,0:T(8,128)S(1)}, f32[72,1536]{1,0:T(8,128)S(1)}, f32[72,512]{1,0:T(8,128)S(1)}) custom-call(f32[72,1024]{1,0:T(8,128)S(1)} %get-tuple-element.56.inner_own.own, bf16[512,1536]{1,0:T(8,128)(2,1)S(1)} %copy-done, bf16[512,512]{1,0:T(8,128)(2,1)S(1)} %copy-done.1), custom_call_target="tpu_custom_call" | custom-call | flops 500000000 | bytes 3129344 | tf_op jit(solution)/shard_map/own/pallas_call | solution.py:388
  12.2 0.0 collective-permute-done.lat_in
  12.2 2.1 %inner.1 = (f32[2,256,512]{2,1,0:T(8,128)S(1)}, bf16[144,512]{1,0:T(8,128)(2,1)S(1)}, bf16[144,512]{1,0:T(8,128)(2,1)S(1)}, bf16[2,256,144]{2,1,0:T(8,128)(2,1)S...) custom-call(f32[72,1024]{1,0:T(8,128)S(1)} %get-tuple-element.56.inner_own.own, ...), custom_call_target="tpu_custom_call" | custom-call | flops 1000000000 | bytes 5505024 | tf_op jit(solution)/shard_map/inner/pallas_call | solution.py:388
  14.4 0.0 collective-permute-done.2.lat_in
  14.4 2.4 %outer.1 = (bf16[2,256,512]{2,1,0:T(8,128)(2,1)S(1)}, bf16[144,512]{1,0:T(8,128)(2,1)S(1)}, bf16[144,512]{1,0:T(8,128)(2,1)S(1)}, bf16[2,256,144]{2,1,0:T(8,128)...) custom-call(f32[72,1024]{1,0:T(8,128)S(1)} %get-tuple-element.64.own, ...), custom_call_target="tpu_custom_call" | custom-call | flops 1000000000 | bytes 5365760 | tf_op jit(solution)/shard_map/outer/pallas_call | solution.py:388
  16.8 0.1 collective-permute-start.4
  16.9 0.7 %keep.1 = (bf16[2,256,512]{2,1,0:T(8,128)(2,1)S(1)}, bf16[2,256,512]{2,1,0:T(8,128)(2,1)S(1)}) custom-call(bf16[2,256,144]{2,1,0:T(8,128)(2,1)S(1)} %get-tuple-element.61.refs_0_.refs_2_, bf16[144,2048]{1,0:T(8,128)(2,1)S(1)} %get-tuple-element.62.refs_1_.refs_3_, bf16[2,256,144]{2,1,0:T(8,128)(2,1)S(1)} %get-tuple-element.63.refs_2_, ...), custom_call_target="tpu_custom_call" | custom-call | flops 1000000000 | bytes 2818048 | tf_op jit(solution)/shard_map/keep/pallas_call | solution.py:388
  17.6 0.5 collective-permute-start.6
  18.1 0.6 %collective-permute-done.4.refs_1_ = bf16[2,256,512]{2,1,0:T(8,128)(2,1)S(1)} collective-permute-done((bf16[2,256,512]{2,1,0:T(8,128)(2,1)S(1)}, bf16[2,256,512]{2,1,0:T(8,128)(2,1)S(1)}, u32[]{:S(2)}, u32[]{:S(2)}) %collective-permute-start.4) | collective-permute-done | bytes 524320 | tf_op jit(solution)/shard_map/ppermute | solution.py:467
  18.7 0.1 chip_sum.1._
  18.9 2.2 %collective-permute-start.7 = (bf16[2,256,512]{2,1,0:T(8,128)(2,1)S(1)}, bf16[2,256,512]{2,1,0:T(8,128)(2,1)S(1)}, u32[]{:S(2)}, u32[]{:S(2)}) collective-permute-start(bf16[2,256,512]{2,1,0:T(8,128)(2,1)S(1)} %chip_sum.1._), channel_id=1, source_target_pairs={{0,8},{1,17},{2,10},{3,19},{4,12},{5,21},{6,14},{7,23},{8,0},{9,25... | collective-permute-start | bytes 1572872 | tf_op jit(solution)/shard_map/ppermute | solution.py:477
  21.1 1.2 %outputs.1 = (bf16[2,256,512]{2,1,0:T(8,128)(2,1)S(1)}, bf16[144,1024]{1,0:T(8,128)(2,1)S(1)}, bf16[144,1024]{1,0:T(8,128)(2,1)S(1)}) custom-call(bf16[2,256,512]{2,1,0:T(8,128)(2,1)S(1)} %chip_sum.1._, bf16[144,512]{1,0:T(8,128)(2,1)S(1)} %get-tuple-element.73.refs_0_, bf16[144,512]{1,0:T(8,128)(2,1)S(1)} %get-tuple-element.74.refs_1_, ...), custom_call_target="tpu_custom_call" | custom-call | flops 1000000000 | bytes 5799936 | tf_op jit(solution)/shard_map/outputs/pallas_call | solution.py:388
  22.2 0.1 pack_lon.1
  22.4 0.1 collective-permute-start.5
  22.5 5.6 %collective-permute-done.5._.lon_in = bf16[36,1024]{1,0:T(8,128)(2,1)S(1)} collective-permute-done((bf16[36,1024]{1,0:T(8,128)(2,1)S(1)}, bf16[36,1024]{1,0:T(8,128)(2,1)S(1)}, u32[]{:S(2)}, u32[]{:S(2)}) %collective-permute-start.5) | collective-permute-done | bytes 73760 | tf_op jit(solution)/shard_map/ppermute | solution.py:488
  28.1 0.1 collective-permute-done.7.refs_2_
  28.2 0.2 halve1.1
  28.4 1.5 %collective-permute-start.9 = (bf16[1,256,512]{2,1,0:T(8,128)(2,1)S(1)}, bf16[1,256,512]{2,1,0:T(8,128)(2,1)S(1)}, u32[]{:S(2)}, u32[]{:S(2)}) collective-permute-start(bf16[1,256,512]{2,1,0:T(8,128)(2,1)S(1)} %get-tuple-element.80._), channel_id=1, source_target_pairs={{0,16},{1,9},{2,18},{3,11},{4,20},{5,13},{6,22},{7,15},{8,24},{9,1... | collective-permute-start | bytes 786440 | tf_op jit(solution)/shard_map/ppermute | solution.py:477
  29.9 0.5 place_own.1
  30.4 1.2 %collective-permute-start.8 = (bf16[108,1024]{1,0:T(8,128)(2,1)S(1)}, bf16[108,1024]{1,0:T(8,128)(2,1)S(1)}, u32[]{:S(2)}, u32[]{:S(2)}) collective-permute-start(bf16[108,1024]{1,0:T(8,128)(2,1)S(1)} %get-tuple-element.83), channel_id=1, source_target_pairs={{24,0},{9,1},{26,2},{11,3},{28,4},{13,5},{30,6},{15,7},{0,8},{17,9... | collective-permute-start | bytes 663560 | tf_op jit(solution)/shard_map/ppermute | solution.py:501
  31.5 3.3 %collective-permute-done.9.refs_1_ = bf16[1,256,512]{2,1,0:T(8,128)(2,1)S(1)} collective-permute-done((bf16[1,256,512]{2,1,0:T(8,128)(2,1)S(1)}, bf16[1,256,512]{2,1,0:T(8,128)(2,1)S(1)}, u32[]{:S(2)}, u32[]{:S(2)}) %collective-permute-start.9) | collective-permute-done | bytes 262176 | tf_op jit(solution)/shard_map/ppermute | solution.py:477
  34.8 0.1 line_parts.1
  34.9 4.1 %collective-permute-start.11 = (bf16[64,512]{1,0:T(8,128)(2,1)S(1)}, bf16[64,512]{1,0:T(8,128)(2,1)S(1)}, u32[]{:S(2)}, u32[]{:S(2)}) collective-permute-start(bf16[64,512]{1,0:T(8,128)(2,1)S(1)} %get-tuple-element.90), channel_id=1, source_target_pairs={{0,6},{1,7},{2,4},{3,5},{4,2},{5,3},{6,0},{7,1},{8,14},{9,15},{10,... | collective-permute-start | bytes 196616 | tf_op jit(solution)/shard_map/ppermute | solution.py:509
  39.0 0.6 %collective-permute-start.13 = (bf16[64,512]{1,0:T(8,128)(2,1)S(1)}, bf16[64,512]{1,0:T(8,128)(2,1)S(1)}, u32[]{:S(2)}, u32[]{:S(2)}) collective-permute-start(bf16[64,512]{1,0:T(8,128)(2,1)S(1)} %get-tuple-element.85._), channel_id=1, source_target_pairs={{0,2},{1,3},{2,0},{3,1},{4,6},{5,7},{6,4},{7,5},{8,10},{9,11},{10,... | collective-permute-start | bytes 196616 | tf_op jit(solution)/shard_map/ppermute | solution.py:509
  39.6 0.1 pack_diag.1
  39.8 0.1 collective-permute-start.10
  39.8 0.3 place_lat.1.placed._
  40.1 1.2 %collective-permute-done.11.refs_1_ = bf16[64,512]{1,0:T(8,128)(2,1)S(1)} collective-permute-done((bf16[64,512]{1,0:T(8,128)(2,1)S(1)}, bf16[64,512]{1,0:T(8,128)(2,1)S(1)}, u32[]{:S(2)}, u32[]{:S(2)}) %collective-permute-start.11) | collective-permute-done | bytes 65568 | tf_op jit(solution)/shard_map/ppermute | solution.py:509
  41.3 2.8 %collective-permute-done.12.refs_2_ = bf16[64,512]{1,0:T(8,128)(2,1)S(1)} collective-permute-done((bf16[64,512]{1,0:T(8,128)(2,1)S(1)}, bf16[64,512]{1,0:T(8,128)(2,1)S(1)}, u32[]{:S(2)}, u32[]{:S(2)}) %collective-permute-start.12) | collective-permute-done | bytes 65568 | tf_op jit(solution)/shard_map/ppermute | solution.py:509
  44.2 4.3 %collective-permute-start.16 = (bf16[64,512]{1,0:T(8,128)(2,1)S(1)}, bf16[64,512]{1,0:T(8,128)(2,1)S(1)}, u32[]{:S(2)}, u32[]{:S(2)}) collective-permute-start(bf16[64,512]{1,0:T(8,128)(2,1)S(1)} %line_sum.1.refs_0_), channel_id=1, source_target_pairs={{0,24},{8,16},{16,8},{24,0},{1,25},{9,17},{17,9},{25,1},{2,26},{10... | collective-permute-start | bytes 196616 | tf_op jit(solution)/shard_map/ppermute | solution.py:519
  48.5 0.7 %collective-permute-start.15 = (bf16[64,512]{1,0:T(8,128)(2,1)S(1)}, bf16[64,512]{1,0:T(8,128)(2,1)S(1)}, u32[]{:S(2)}, u32[]{:S(2)}) collective-permute-start(bf16[64,512]{1,0:T(8,128)(2,1)S(1)} %line_sum.1.refs_0_), channel_id=1, source_target_pairs={{0,16},{8,24},{16,0},{24,8},{1,17},{9,25},{17,1},{25,9},{2,18},{10... | collective-permute-start | bytes 196616 | tf_op jit(solution)/shard_map/ppermute | solution.py:519
  49.1 0.0 collective-permute-start.14
  49.1 0.0 collective-permute-done.10.diag_in
  49.1 1.2 %place_rest.1 = (bf16[288,512]{1,0:T(8,128)(2,1)}, bf16[288,512]{1,0:T(8,128)(2,1)}, f32[8,128]{1,0:T(8,128)S(1)}) custom-call(f32[288,1024]{1,0:T(8,128)S(1)} %place_lat.1.placed._, bf16[36,1024]{1,0:T(8,128)(2,1)S(1)} %collective-permute-done.5._.lon_in, bf16[36,1024]{1,0:T(8,128)(2,1)S(1)} %collective-permute-done.10.diag_in), custom_call_target="tpu_custom_call" | custom-call | bytes 1921024 | tf_op jit(solution)/shard_map/place_rest/pallas_call | solution.py:388
  50.3 0.4 collective-permute-done.16.refs_3_
  50.7 2.0 %collective-permute-done.15.refs_2_ = bf16[64,512]{1,0:T(8,128)(2,1)S(1)} collective-permute-done((bf16[64,512]{1,0:T(8,128)(2,1)S(1)}, bf16[64,512]{1,0:T(8,128)(2,1)S(1)}, u32[]{:S(2)}, u32[]{:S(2)}) %collective-permute-start.15) | collective-permute-done | bytes 65568 | tf_op jit(solution)/shard_map/ppermute | solution.py:519
  52.7 0.7 %collective-permute-done.14.refs_1_ = bf16[64,512]{1,0:T(8,128)(2,1)S(1)} collective-permute-done((bf16[64,512]{1,0:T(8,128)(2,1)S(1)}, bf16[64,512]{1,0:T(8,128)(2,1)S(1)}, u32[]{:S(2)}, u32[]{:S(2)}) %collective-permute-start.14) | collective-permute-done | bytes 65568 | tf_op jit(solution)/shard_map/ppermute | solution.py:519
  53.4 0.9 %finish.1 = (f32[64,1536]{1,0:T(8,128)}, f32[64,512]{1,0:T(8,128)}) custom-call(f32[8,128]{1,0:T(8,128)S(1)} %get-tuple-element.88._, bf16[64,512]{1,0:T(8,128)(2,1)S(1)} %line_sum.1.refs_0_, bf16[64,512]{1,0:T(8,128)(2,1)S(1)} %collective-permute-done.14.refs_1_, bf16[64,512]{1,0:T(8,128)(2,1)S(1)} %collective-permute-done.15.refs_2_, ...), custom_call_target="tpu_custom_call" | custom-call | bytes 790528 | tf_op jit(solution)/shard_map/finish/pallas_call | solution.py:388
  (12 shorter events, 0.1 us)
Async XLA Ops:
  0.6 1.0 %copy-start.3 = (bf16[2,6,24,512]{3,2,1,0:T(8,128)(2,1)S(1)}, bf16[2,6,24,512]{3,2,1,0:T(8,128)(2,1)}, u32[]{:S(2)}) copy-start(bf16[2,6,24,512]{3,2,1,0:T(8,128)(2,1)} %param.5) | copy-start | bytes 884740
  0.6 1.0 %copy-start.2 = (bf16[2,6,24,512]{3,2,1,0:T(8,128)(2,1)S(1)}, bf16[2,6,24,512]{3,2,1,0:T(8,128)(2,1)}, u32[]{:S(2)}) copy-start(bf16[2,6,24,512]{3,2,1,0:T(8,128)(2,1)} %param.4) | copy-start | bytes 884740
  1.7 9.8 %copy-start.1 = (bf16[512,512]{1,0:T(8,128)(2,1)S(1)}, bf16[512,512]{1,0:T(8,128)(2,1)}, u32[]{:S(2)}) copy-start(bf16[512,512]{1,0:T(8,128)(2,1)} %refs_9_.1) | copy-start | bytes 1572868
  2.0 9.5 %copy-start = (bf16[512,1536]{1,0:T(8,128)(2,1)S(1)}, bf16[512,1536]{1,0:T(8,128)(2,1)}, u32[]{:S(2)}) copy-start(bf16[512,1536]{1,0:T(8,128)(2,1)} %refs_8_.1) | copy-start | bytes 4718596
  2.1 10.2 %collective-permute-start = (bf16[72,1024]{1,0:T(8,128)(2,1)S(1)}, bf16[72,1024]{1,0:T(8,128)(2,1)S(1)}, u32[]{:S(2)}, u32[]{:S(2)}) collective-permute-start(bf16[72,1024]{1,0:T(8,128)(2,1)S(1)} %get-tuple-element.60), channel_id=1, source_target_pairs={{0,24},{1,9},{2,26},{3,11},{4,28},{5,13},{6,30},{7,15},{8,0},{9,17... | collective-permute-start | bytes 442376 | tf_op jit(solution)/shard_map/ppermute | solution.py:442
  6.0 8.4 %collective-permute-start.1 = (bf16[36,1024]{1,0:T(8,128)(2,1)S(1)}, bf16[36,1024]{1,0:T(8,128)(2,1)S(1)}, u32[]{:S(2)}, u32[]{:S(2)}) collective-permute-start(bf16[36,1024]{1,0:T(8,128)(2,1)S(1)} %get-tuple-element.51._), channel_id=1, source_target_pairs={{0,7},{1,0},{2,1},{3,2},{4,3},{5,4},{6,5},{7,6},{8,15},{9,8},{10,9... | collective-permute-start | bytes 221192 | tf_op jit(solution)/shard_map/ppermute | solution.py:443
  8.4 5.9 %collective-permute-start.2 = (bf16[36,1024]{1,0:T(8,128)(2,1)S(1)}, bf16[36,1024]{1,0:T(8,128)(2,1)S(1)}, u32[]{:S(2)}, u32[]{:S(2)}) collective-permute-start(bf16[36,1024]{1,0:T(8,128)(2,1)S(1)} %get-tuple-element.65), channel_id=1, source_target_pairs={{0,24},{1,9},{2,26},{3,11},{4,28},{5,13},{6,30},{7,15},{8,0},{9,17... | collective-permute-start | bytes 221192 | tf_op jit(solution)/shard_map/ppermute | solution.py:444
  9.9 4.5 %collective-permute-start.3 = (bf16[36,1024]{1,0:T(8,128)(2,1)S(1)}, bf16[36,1024]{1,0:T(8,128)(2,1)S(1)}, u32[]{:S(2)}, u32[]{:S(2)}) collective-permute-start(bf16[36,1024]{1,0:T(8,128)(2,1)S(1)} %get-tuple-element.66), channel_id=1, source_target_pairs={{0,15},{1,24},{2,9},{3,26},{4,11},{5,28},{6,13},{7,30},{8,23},{9,0... | collective-permute-start | bytes 221192 | tf_op jit(solution)/shard_map/ppermute | solution.py:445
  16.8 2.0 %collective-permute-start.4 = (bf16[2,256,512]{2,1,0:T(8,128)(2,1)S(1)}, bf16[2,256,512]{2,1,0:T(8,128)(2,1)S(1)}, u32[]{:S(2)}, u32[]{:S(2)}) collective-permute-start(bf16[2,256,512]{2,1,0:T(8,128)(2,1)S(1)} %get-tuple-element.72), channel_id=1, source_target_pairs={{0,1},{1,0},{2,3},{3,2},{4,5},{5,4},{6,7},{7,6},{8,9},{9,8},{10,11... | collective-permute-start | bytes 1572872 | tf_op jit(solution)/shard_map/ppermute | solution.py:467
  17.6 4.9 %collective-permute-start.6 = (bf16[2,256,512]{2,1,0:T(8,128)(2,1)S(1)}, bf16[2,256,512]{2,1,0:T(8,128)(2,1)S(1)}, u32[]{:S(2)}, u32[]{:S(2)}) collective-permute-start(bf16[2,256,512]{2,1,0:T(8,128)(2,1)S(1)} %get-tuple-element.79), channel_id=1, source_target_pairs={{0,1},{1,0},{2,3},{3,2},{4,5},{5,4},{6,7},{7,6},{8,9},{9,8},{10,11... | collective-permute-start | bytes 1572872 | tf_op jit(solution)/shard_map/ppermute | solution.py:469
  18.9 9.4 %collective-permute-start.7 = (bf16[2,256,512]{2,1,0:T(8,128)(2,1)S(1)}, bf16[2,256,512]{2,1,0:T(8,128)(2,1)S(1)}, u32[]{:S(2)}, u32[]{:S(2)}) collective-permute-start(bf16[2,256,512]{2,1,0:T(8,128)(2,1)S(1)} %chip_sum.1._), channel_id=1, source_target_pairs={{0,8},{1,17},{2,10},{3,19},{4,12},{5,21},{6,14},{7,23},{8,0},{9,25... | collective-permute-start | bytes 1572872 | tf_op jit(solution)/shard_map/ppermute | solution.py:477
  22.4 5.7 %collective-permute-start.5 = (bf16[36,1024]{1,0:T(8,128)(2,1)S(1)}, bf16[36,1024]{1,0:T(8,128)(2,1)S(1)}, u32[]{:S(2)}, u32[]{:S(2)}) collective-permute-start(bf16[36,1024]{1,0:T(8,128)(2,1)S(1)} %pack_lon.1), channel_id=1, source_target_pairs={{7,0},{0,1},{1,2},{2,3},{3,4},{4,5},{5,6},{6,7},{15,8},{8,9},{9,10... | collective-permute-start | bytes 221192 | tf_op jit(solution)/shard_map/ppermute | solution.py:488
  28.4 6.4 %collective-permute-start.9 = (bf16[1,256,512]{2,1,0:T(8,128)(2,1)S(1)}, bf16[1,256,512]{2,1,0:T(8,128)(2,1)S(1)}, u32[]{:S(2)}, u32[]{:S(2)}) collective-permute-start(bf16[1,256,512]{2,1,0:T(8,128)(2,1)S(1)} %get-tuple-element.80._), channel_id=1, source_target_pairs={{0,16},{1,9},{2,18},{3,11},{4,20},{5,13},{6,22},{7,15},{8,24},{9,1... | collective-permute-start | bytes 786440 | tf_op jit(solution)/shard_map/ppermute | solution.py:477
  30.4 9.5 %collective-permute-start.8 = (bf16[108,1024]{1,0:T(8,128)(2,1)S(1)}, bf16[108,1024]{1,0:T(8,128)(2,1)S(1)}, u32[]{:S(2)}, u32[]{:S(2)}) collective-permute-start(bf16[108,1024]{1,0:T(8,128)(2,1)S(1)} %get-tuple-element.83), channel_id=1, source_target_pairs={{24,0},{9,1},{26,2},{11,3},{28,4},{13,5},{30,6},{15,7},{0,8},{17,9... | collective-permute-start | bytes 663560 | tf_op jit(solution)/shard_map/ppermute | solution.py:501
  34.9 6.4 %collective-permute-start.11 = (bf16[64,512]{1,0:T(8,128)(2,1)S(1)}, bf16[64,512]{1,0:T(8,128)(2,1)S(1)}, u32[]{:S(2)}, u32[]{:S(2)}) collective-permute-start(bf16[64,512]{1,0:T(8,128)(2,1)S(1)} %get-tuple-element.90), channel_id=1, source_target_pairs={{0,6},{1,7},{2,4},{3,5},{4,2},{5,3},{6,0},{7,1},{8,14},{9,15},{10,... | collective-permute-start | bytes 196616 | tf_op jit(solution)/shard_map/ppermute | solution.py:509
  39.0 5.2 %collective-permute-start.12 = (bf16[64,512]{1,0:T(8,128)(2,1)S(1)}, bf16[64,512]{1,0:T(8,128)(2,1)S(1)}, u32[]{:S(2)}, u32[]{:S(2)}) collective-permute-start(bf16[64,512]{1,0:T(8,128)(2,1)S(1)} %get-tuple-element.91), channel_id=1, source_target_pairs={{0,4},{1,5},{2,6},{3,7},{4,0},{5,1},{6,2},{7,3},{8,12},{9,13},{10,... | collective-permute-start | bytes 196616 | tf_op jit(solution)/shard_map/ppermute | solution.py:509
  39.0 5.2 %collective-permute-start.13 = (bf16[64,512]{1,0:T(8,128)(2,1)S(1)}, bf16[64,512]{1,0:T(8,128)(2,1)S(1)}, u32[]{:S(2)}, u32[]{:S(2)}) collective-permute-start(bf16[64,512]{1,0:T(8,128)(2,1)S(1)} %get-tuple-element.85._), channel_id=1, source_target_pairs={{0,2},{1,3},{2,0},{3,1},{4,6},{5,7},{6,4},{7,5},{8,10},{9,11},{10,... | collective-permute-start | bytes 196616 | tf_op jit(solution)/shard_map/ppermute | solution.py:509
  39.8 9.4 %collective-permute-start.10 = (bf16[36,1024]{1,0:T(8,128)(2,1)S(1)}, bf16[36,1024]{1,0:T(8,128)(2,1)S(1)}, u32[]{:S(2)}, u32[]{:S(2)}) collective-permute-start(bf16[36,1024]{1,0:T(8,128)(2,1)S(1)} %pack_diag.1), channel_id=1, source_target_pairs={{15,0},{24,1},{9,2},{26,3},{11,4},{28,5},{13,6},{30,7},{23,8},{0,9... | collective-permute-start | bytes 221192 | tf_op jit(solution)/shard_map/ppermute | solution.py:513
  44.2 6.5 %collective-permute-start.16 = (bf16[64,512]{1,0:T(8,128)(2,1)S(1)}, bf16[64,512]{1,0:T(8,128)(2,1)S(1)}, u32[]{:S(2)}, u32[]{:S(2)}) collective-permute-start(bf16[64,512]{1,0:T(8,128)(2,1)S(1)} %line_sum.1.refs_0_), channel_id=1, source_target_pairs={{0,24},{8,16},{16,8},{24,0},{1,25},{9,17},{17,9},{25,1},{2,26},{10... | collective-permute-start | bytes 196616 | tf_op jit(solution)/shard_map/ppermute | solution.py:519
  48.5 4.3 %collective-permute-start.15 = (bf16[64,512]{1,0:T(8,128)(2,1)S(1)}, bf16[64,512]{1,0:T(8,128)(2,1)S(1)}, u32[]{:S(2)}, u32[]{:S(2)}) collective-permute-start(bf16[64,512]{1,0:T(8,128)(2,1)S(1)} %line_sum.1.refs_0_), channel_id=1, source_target_pairs={{0,16},{8,24},{16,0},{24,8},{1,17},{9,25},{17,1},{25,9},{2,18},{10... | collective-permute-start | bytes 196616 | tf_op jit(solution)/shard_map/ppermute | solution.py:519
  49.1 4.3 %collective-permute-start.14 = (bf16[64,512]{1,0:T(8,128)(2,1)S(1)}, bf16[64,512]{1,0:T(8,128)(2,1)S(1)}, u32[]{:S(2)}, u32[]{:S(2)}) collective-permute-start(bf16[64,512]{1,0:T(8,128)(2,1)S(1)} %line_sum.1.refs_0_), channel_id=1, source_target_pairs={{0,8},{8,0},{16,24},{24,16},{1,9},{9,1},{17,25},{25,17},{2,10},{10... | collective-permute-start | bytes 196616 | tf_op jit(solution)/shard_map/ppermute | solution.py:519

commit v12 on v9

--- a/solution.py
+++ b/solution.py
@@ -119,16 +119,16 @@
 
 
 def transpose_bf16(block):
-    return jnp.transpose(block.astype(F32)).astype(BF)
+    return jnp.transpose(block.astype(BF))
 
 
 def slot_product(slot, size, lat, core, windows):
     share = lat ^ swap_bits(slot, size, core)
     total = None
     for left, right in windows:
-        lanes = right.shape[1] // size
+        rows = right.shape[0] // size
         of_proj = (share >= 3 * size // 4).astype(jnp.int32)
-        part = dot(left[of_proj], right[:, pl.ds(pl.multiple_of(share * lanes, lanes), lanes)], NN)
+        part = dot(left[of_proj], right[pl.ds(pl.multiple_of(share * rows, rows), rows), :], NT)
         total = part if total is None else total + part
     return total
 
@@ -208,45 +208,50 @@
     head_size = width // HEADS
     factor = head_size ** (-0.5)
     apart = jnp.where(even, lat == lat_size - 1, lat == 0).astype(jnp.int32)
-    half_b = (lax.broadcasted_iota(jnp.int32, (WIN, 2 * WIN), 0) >= HALF).astype(jnp.int32)
-    at_a = lax.broadcasted_iota(jnp.int32, (WIN, 2 * WIN), 1)
-    at_a = jnp.where(at_a >= WIN, at_a - WIN, at_a)
-    half_a = (at_a >= HALF).astype(jnp.int32)
+    half_b = (lax.broadcasted_iota(jnp.int32, (WIN, WIN), 0) >= HALF).astype(jnp.int32)
+    half_a = (lax.broadcasted_iota(jnp.int32, (WIN, WIN), 1) >= HALF).astype(jnp.int32)
     allowed = ((half_a != half_b).astype(jnp.int32) * apart) == 0
     first_head = lax.broadcasted_iota(jnp.int32, (WIN, LANES), 1) < head_size
     zero = jnp.zeros((WIN, LANES), BF)
 
-    def split_heads(block):
-        return jnp.concatenate([jnp.where(first_head, block, zero), jnp.where(first_head, zero, block)], axis=0)
-
-    def join_heads(block):
-        return jnp.where(first_head, block[:WIN], block[WIN:]).astype(BF)
-
     pairs = range(width // LANES)
+    heads = range(HEADS)
 
     def blocks_of(array, lanes_from):
         return [array[:, lanes_from + pair * LANES : lanes_from + (pair + 1) * LANES] for pair in pairs]
 
-    def store(out, lanes_from, blocks):
-        for pair, block in zip(pairs, blocks):
-            out[:, lanes_from + pair * LANES : lanes_from + (pair + 1) * LANES] = block.astype(out.dtype)
-
-    k, v = blocks_of(projected, width), blocks_of(projected, 2 * width)
-    q2 = [split_heads(block) for block in blocks_of(projected, 0)]
-    dm2 = [split_heads(block) for block in blocks_of(d_mixed, 0)]
-    scores = [jnp.where(allowed, dot(k[p], q2[p], NT) * factor, -1e30) for p in pairs]
-    d_probs = [dot(v[p], dm2[p], NT) for p in pairs]
+    def head_lanes(blocks):
+        return [
+            jnp.where(first_head, block, zero) if half == 0 else jnp.where(first_head, zero, block)
+            for block in blocks
+            for half in range(2)
+        ]
+
+    def head_rows(blocks):
+        turned = [jnp.transpose(block) for block in blocks]
+        return [block[half * head_size : (half + 1) * head_size] for block in turned for half in range(2)]
+
+    def store(rows_from, blocks):
+        for head, block in zip(heads, blocks):
+            right[rows_from + head * head_size : rows_from + (head + 1) * head_size, :] = block.astype(BF)
+
+    q, k, v = (blocks_of(projected, at * width) for at in range(3))
+    dm = blocks_of(d_mixed, 0)
+    q_lanes, dm_lanes = head_lanes(q), head_lanes(dm)
+    scores = [jnp.where(allowed, dot(k[h // 2], q_lanes[h], NT) * factor, -1e30) for h in heads]
+    d_probs = [dot(v[h // 2], dm_lanes[h], NT) for h in heads]
+    q_rows, k_rows, v_rows, dm_rows = (head_rows(blocks) for blocks in (q, k, v, dm))
     exponents = [jnp.exp(s - jnp.max(s, 0, keepdims=True)) for s in scores]
     probs = [e * (1.0 / jnp.sum(e, 0, keepdims=True)) for e in exponents]
     probs_b = [p.astype(BF) for p in probs]
-    store(right, 3 * width, [join_heads(dot(probs_b[p], v[p], TN)) for p in pairs])
-    store(right, 2 * width, [dot(probs_b[p], dm2[p], NN) for p in pairs])
+    store(3 * width, [dot(v_rows[h], probs_b[h], NN) for h in heads])
+    store(2 * width, [dot(dm_rows[h], probs_b[h], NT) for h in heads])
     d_scores = [
-        (probs[p] * (d_probs[p] - jnp.sum(d_probs[p] * probs[p], 0, keepdims=True)) * factor).astype(BF)
-        for p in pairs
+        (probs[h] * (d_probs[h] - jnp.sum(d_probs[h] * probs[h], 0, keepdims=True)) * factor).astype(BF)
+        for h in heads
     ]
-    store(right, 0, [join_heads(dot(d_scores[p], k[p], TN)) for p in pairs])
-    store(right, width, [dot(d_scores[p], q2[p], NN) for p in pairs])
+    store(0, [dot(k_rows[h], d_scores[h], NN) for h in heads])
+    store(width, [dot(q_rows[h], d_scores[h], NT) for h in heads])
 
     normed_t[...] = transpose_bf16(normed)
     grads_t[...] = transpose_bf16(grads)
@@ -272,12 +277,15 @@
     width = proj_weight.shape[0]
     for slot in range(0, size, 2):
         keep_rest[slot // 2] = slot_product(slot, size, lat, core, [w[2:] for w in per_window]).astype(BF)
-    x, grads, right = (jnp.concatenate([w[i][...] for w in per_window], axis=0) for i in (0, 1, 3))
-    d_projected, mixed = right[:, : 3 * width], right[:, 3 * width :]
+    x, grads = (jnp.concatenate([w[i][...] for w in per_window], axis=0) for i in (0, 1))
+
+    def times(rows, weight, dims):
+        return jnp.concatenate([dot(w[3][rows, :], weight[...], dims) for w in per_window], axis=0)
+
     x = x.astype(F32)
     normed, inv_std = normalise(x)
-    output = (x + dot(mixed, proj_weight[...], NN)).astype(BF)
-    d_normed = dot(d_projected, qkv_weight[...], NT)
+    output = (x + times(slice(3 * width, 4 * width), proj_weight, TN)).astype(BF)
+    d_normed = times(slice(0, 3 * width), qkv_weight, ((0,), (1,)))
     d_inputs = grads.astype(F32) + inv_std * (
         d_normed
         - jnp.mean(d_normed, -1, keepdims=True)
@@ -441,7 +449,7 @@
         ((WIN, width), BF),
         ((WIN, width), BF),
         ((2, width // 2, WIN), BF),
-        ((WIN, 4 * width), BF),
+        ((4 * width, WIN), BF),
         ((2, width // 2, WIN), BF),
     ]
     scratch = [pltpu.VMEM((width, WIN), BF)] * 2

time: 52.1 us -> 52.4 us (level)
  Pallas kernels: 11.5 us -> 12.5 us
  starting transfers between devices: 23.3 us -> 22.3 us
    pallas_call x17, Pallas kernels: 11.5 us -> 12.5 us  [call(): pl.pallas_call(kernel, out_shape=shapes, in_specs=[anywhere if i in unrea...]
  transfers between devices with their start and end apart: 17 -> 17, of which waited for: 9 -> 8; matrix products, arithmetic and copies ran while one was open for 0% -> 0% of each run, Pallas kernels for 15% -> 16%
where the time goes in v12:
time: 52.4 us; the launch traced here: 52.3 us
  starting transfers between devices  22.3 us (43%)
  waiting for transfers between devices  15.7 us (30%)
  Pallas kernels  12.5 us (24%)
  local copies, waits for them, and re-layouts  0.94 us (2%)
  between operations  0.8 us (2%)
    pallas_call x17, Pallas kernels, call(): pl.pallas_call(kernel, out_shape=shapes, in_specs=[anywhere if i in unrea...  12.5 us
    ppermute x1, waiting for transfers between devices, per_device(): lon_home = lax.ppermute(lon_back, both, back(lon_route))  5.64 us
    ppermute x2, waiting for transfers between devices, halving(): return lax.ppermute(send, both, route)  5.28 us
    ppermute x3, starting transfers between devices, per_device(): lax.ppermute(parts[step], 'lon', [(j, j ^ 2 * step) for j in range(lon_si...  4.45 us
    ppermute x1, starting transfers between devices, per_device(): inner_in = lax.ppermute(inner_lat, both, lat_route)  3.94 us
    ppermute x3, starting transfers between devices, per_device(): lax.ppermute(line_sum, 'lat', [(i, i ^ step) for i in range(lat_size)])  3.55 us
    ppermute x2, starting transfers between devices, halving(): return lax.ppermute(send, both, route)  3.17 us
    ppermute x3, waiting for transfers between devices, per_device(): lax.ppermute(parts[step], 'lon', [(j, j ^ 2 * step) for j in range(lon_si...  2.01 us
  transfers between devices with their start and end apart: 17, of which 8 were waited for; matrix products, arithmetic and copies ran while one was open for 0% of the time, Pallas kernels for 16%

profile of v12, /device:TPU:0, one launch (start us, length us, event | category | flops | bytes accessed | tf_op | source)
XLA Modules:
  0.0 52.3 jit_solution(2926338299602328047)
XLA Ops:
  0.7 0.1 order.1
  0.8 0.8 %copy-done.3 = bf16[2,6,24,512]{3,2,1,0:T(8,128)(2,1)S(1)} copy-done((bf16[2,6,24,512]{3,2,1,0:T(8,128)(2,1)S(1)}, bf16[2,6,24,512]{3,2,1,0:T(8,128)(2,1)}, u32[]{:S(2)}) %copy-start.3) | copy-done | bytes 294936
  1.6 0.1 copy-done.2
  1.7 0.4 pack.1
  2.0 0.0 copy-start
  2.1 3.9 %collective-permute-start = (bf16[72,1024]{1,0:T(8,128)(2,1)S(1)}, bf16[72,1024]{1,0:T(8,128)(2,1)S(1)}, u32[]{:S(2)}, u32[]{:S(2)}) collective-permute-start(bf16[72,1024]{1,0:T(8,128)(2,1)S(1)} %get-tuple-element.60), channel_id=1, source_target_pairs={{0,24},{1,9},{2,26},{3,11},{4,28},{5,13},{6,30},{7,15},{8,0},{9,17... | collective-permute-start | bytes 442376 | tf_op jit(solution)/shard_map/ppermute | solution.py:441
  6.0 1.8 %collective-permute-start.1 = (bf16[36,1024]{1,0:T(8,128)(2,1)S(1)}, bf16[36,1024]{1,0:T(8,128)(2,1)S(1)}, u32[]{:S(2)}, u32[]{:S(2)}) collective-permute-start(bf16[36,1024]{1,0:T(8,128)(2,1)S(1)} %get-tuple-element.51._), channel_id=1, source_target_pairs={{0,7},{1,0},{2,1},{3,2},{4,3},{5,4},{6,5},{7,6},{8,15},{9,8},{10,9... | collective-permute-start | bytes 221192 | tf_op jit(solution)/shard_map/ppermute | solution.py:442
  7.8 0.6 %pack_rest.1 = (bf16[36,1024]{1,0:T(8,128)(2,1)S(1)}, bf16[36,1024]{1,0:T(8,128)(2,1)S(1)}, f32[72,1024]{1,0:T(8,128)S(1)}, f32[72,1024]{1,0:T(8,128)S(1)}) custom-call(bf16[36,1024]{1,0:T(8,128)(2,1)S(1)} %get-tuple-element.51._, bf16[288,512]{1,0:T(8,128)(2,1)S(1)} %bitcast.6, bf16[288,512]{1,0:T(8,128)(2,1)S(1)} %bitcast.8, ...), custom_call_target="tpu_custom_call" | custom-call | flops 500000000 | bytes 1525248 | tf_op jit(solution)/shard_map/pack_rest/pallas_call | solution.py:387
  8.4 1.5 %collective-permute-start.2 = (bf16[36,1024]{1,0:T(8,128)(2,1)S(1)}, bf16[36,1024]{1,0:T(8,128)(2,1)S(1)}, u32[]{:S(2)}, u32[]{:S(2)}) collective-permute-start(bf16[36,1024]{1,0:T(8,128)(2,1)S(1)} %get-tuple-element.65), channel_id=1, source_target_pairs={{0,24},{1,9},{2,26},{3,11},{4,28},{5,13},{6,30},{7,15},{8,0},{9,17... | collective-permute-start | bytes 221192 | tf_op jit(solution)/shard_map/ppermute | solution.py:443
  9.9 1.6 %collective-permute-start.3 = (bf16[36,1024]{1,0:T(8,128)(2,1)S(1)}, bf16[36,1024]{1,0:T(8,128)(2,1)S(1)}, u32[]{:S(2)}, u32[]{:S(2)}) collective-permute-start(bf16[36,1024]{1,0:T(8,128)(2,1)S(1)} %get-tuple-element.66), channel_id=1, source_target_pairs={{0,15},{1,24},{2,9},{3,26},{4,11},{5,28},{6,13},{7,30},{8,23},{9,0... | collective-permute-start | bytes 221192 | tf_op jit(solution)/shard_map/ppermute | solution.py:444
  11.5 0.7 %own.1 = (f32[72,512]{1,0:T(8,128)S(1)}, f32[72,1536]{1,0:T(8,128)S(1)}, f32[72,512]{1,0:T(8,128)S(1)}) custom-call(f32[72,1024]{1,0:T(8,128)S(1)} %get-tuple-element.56.inner_own.own, bf16[512,1536]{1,0:T(8,128)(2,1)S(1)} %copy-done, bf16[512,512]{1,0:T(8,128)(2,1)S(1)} %copy-done.1), custom_call_target="tpu_custom_call" | custom-call | flops 500000000 | bytes 3129344 | tf_op jit(solution)/shard_map/own/pallas_call | solution.py:387
  12.2 0.0 collective-permute-done.lat_in
  12.2 2.3 %inner.1 = (f32[2,256,512]{2,1,0:T(8,128)S(1)}, bf16[144,512]{1,0:T(8,128)(2,1)S(1)}, bf16[144,512]{1,0:T(8,128)(2,1)S(1)}, bf16[2,256,144]{2,1,0:T(8,128)(2,1)S...) custom-call(f32[72,1024]{1,0:T(8,128)S(1)} %get-tuple-element.56.inner_own.own, ...), custom_call_target="tpu_custom_call" | custom-call | flops 1000000000 | bytes 5505024 | tf_op jit(solution)/shard_map/inner/pallas_call | solution.py:387
  14.6 0.0 collective-permute-done.1.lon_in
  14.6 2.5 %outer.1 = (bf16[2,256,512]{2,1,0:T(8,128)(2,1)S(1)}, bf16[144,512]{1,0:T(8,128)(2,1)S(1)}, bf16[144,512]{1,0:T(8,128)(2,1)S(1)}, bf16[2,256,144]{2,1,0:T(8,128)...) custom-call(f32[72,1024]{1,0:T(8,128)S(1)} %get-tuple-element.64.own, ...), custom_call_target="tpu_custom_call" | custom-call | flops 1000000000 | bytes 5365760 | tf_op jit(solution)/shard_map/outer/pallas_call | solution.py:387
  17.1 0.1 collective-permute-start.4
  17.2 0.7 %keep.1 = (bf16[2,256,512]{2,1,0:T(8,128)(2,1)S(1)}, bf16[2,256,512]{2,1,0:T(8,128)(2,1)S(1)}) custom-call(bf16[2,256,144]{2,1,0:T(8,128)(2,1)S(1)} %get-tuple-element.61.refs_0_.refs_2_, bf16[2048,144]{1,0:T(8,128)(2,1)S(1)} %get-tuple-element.62.refs_1_.refs_3_, bf16[2,256,144]{2,1,0:T(8,128)(2,1)S(1)} %get-tuple-element.63.refs_2_, ...), custom_call_target="tpu_custom_call" | custom-call | flops 1000000000 | bytes 2818048 | tf_op jit(solution)/shard_map/keep/pallas_call | solution.py:387
  18.0 0.5 collective-permute-start.6
  18.5 0.6 %collective-permute-done.4.refs_1_ = bf16[2,256,512]{2,1,0:T(8,128)(2,1)S(1)} collective-permute-done((bf16[2,256,512]{2,1,0:T(8,128)(2,1)S(1)}, bf16[2,256,512]{2,1,0:T(8,128)(2,1)S(1)}, u32[]{:S(2)}, u32[]{:S(2)}) %collective-permute-start.4) | collective-permute-done | bytes 524320 | tf_op jit(solution)/shard_map/ppermute | solution.py:466
  19.1 0.1 chip_sum.1._
  19.2 2.0 %collective-permute-start.7 = (bf16[2,256,512]{2,1,0:T(8,128)(2,1)S(1)}, bf16[2,256,512]{2,1,0:T(8,128)(2,1)S(1)}, u32[]{:S(2)}, u32[]{:S(2)}) collective-permute-start(bf16[2,256,512]{2,1,0:T(8,128)(2,1)S(1)} %chip_sum.1._), channel_id=1, source_target_pairs={{0,8},{1,17},{2,10},{3,19},{4,12},{5,21},{6,14},{7,23},{8,0},{9,25... | collective-permute-start | bytes 1572872 | tf_op jit(solution)/shard_map/ppermute | solution.py:476
  21.2 1.8 %outputs.1 = (bf16[2,256,512]{2,1,0:T(8,128)(2,1)S(1)}, bf16[144,1024]{1,0:T(8,128)(2,1)S(1)}, bf16[144,1024]{1,0:T(8,128)(2,1)S(1)}) custom-call(bf16[2,256,512]{2,1,0:T(8,128)(2,1)S(1)} %chip_sum.1._, bf16[144,512]{1,0:T(8,128)(2,1)S(1)} %get-tuple-element.73.refs_0_, bf16[144,512]{1,0:T(8,128)(2,1)S(1)} %get-tuple-element.74.refs_1_, ...), custom_call_target="tpu_custom_call" | custom-call | flops 1000000000 | bytes 5799936 | tf_op jit(solution)/shard_map/outputs/pallas_call | solution.py:387
  23.0 0.1 pack_lon.1
  23.2 0.1 collective-permute-start.5
  23.2 0.0 collective-permute-done.6.refs_1_
  23.2 5.6 %collective-permute-done.5._.lon_in = bf16[36,1024]{1,0:T(8,128)(2,1)S(1)} collective-permute-done((bf16[36,1024]{1,0:T(8,128)(2,1)S(1)}, bf16[36,1024]{1,0:T(8,128)(2,1)S(1)}, u32[]{:S(2)}, u32[]{:S(2)}) %collective-permute-start.5) | collective-permute-done | bytes 73760 | tf_op jit(solution)/shard_map/ppermute | solution.py:487
  28.9 0.2 halve1.1
  29.1 1.2 %collective-permute-start.8 = (bf16[1,256,512]{2,1,0:T(8,128)(2,1)S(1)}, bf16[1,256,512]{2,1,0:T(8,128)(2,1)S(1)}, u32[]{:S(2)}, u32[]{:S(2)}) collective-permute-start(bf16[1,256,512]{2,1,0:T(8,128)(2,1)S(1)} %get-tuple-element.82), channel_id=1, source_target_pairs={{0,16},{1,9},{2,18},{3,11},{4,20},{5,13},{6,22},{7,15},{8,24},{9,1... | collective-permute-start | bytes 786440 | tf_op jit(solution)/shard_map/ppermute | solution.py:476
  30.2 5.3 %collective-permute-done.8.refs_1_ = bf16[1,256,512]{2,1,0:T(8,128)(2,1)S(1)} collective-permute-done((bf16[1,256,512]{2,1,0:T(8,128)(2,1)S(1)}, bf16[1,256,512]{2,1,0:T(8,128)(2,1)S(1)}, u32[]{:S(2)}, u32[]{:S(2)}) %collective-permute-start.8) | collective-permute-done | bytes 262176 | tf_op jit(solution)/shard_map/ppermute | solution.py:476
  35.5 0.1 line_parts.1
  35.6 3.0 %collective-permute-start.11 = (bf16[64,512]{1,0:T(8,128)(2,1)S(1)}, bf16[64,512]{1,0:T(8,128)(2,1)S(1)}, u32[]{:S(2)}, u32[]{:S(2)}) collective-permute-start(bf16[64,512]{1,0:T(8,128)(2,1)S(1)} %get-tuple-element.90), channel_id=1, source_target_pairs={{0,6},{1,7},{2,4},{3,5},{4,2},{5,3},{6,0},{7,1},{8,14},{9,15},{10,... | collective-permute-start | bytes 196616 | tf_op jit(solution)/shard_map/ppermute | solution.py:502
  38.6 0.0 collective-permute-start.12
  38.6 1.5 %collective-permute-start.13 = (bf16[64,512]{1,0:T(8,128)(2,1)S(1)}, bf16[64,512]{1,0:T(8,128)(2,1)S(1)}, u32[]{:S(2)}, u32[]{:S(2)}) collective-permute-start(bf16[64,512]{1,0:T(8,128)(2,1)S(1)} %get-tuple-element.83._), channel_id=1, source_target_pairs={{0,2},{1,3},{2,0},{3,1},{4,6},{5,7},{6,4},{7,5},{8,10},{9,11},{10,... | collective-permute-start | bytes 196616 | tf_op jit(solution)/shard_map/ppermute | solution.py:502
  40.0 0.2 pack_back.1
  40.2 1.6 %collective-permute-start.9 = (bf16[108,1024]{1,0:T(8,128)(2,1)S(1)}, bf16[108,1024]{1,0:T(8,128)(2,1)S(1)}, u32[]{:S(2)}, u32[]{:S(2)}) collective-permute-start(bf16[108,1024]{1,0:T(8,128)(2,1)S(1)} %get-tuple-element.84), channel_id=1, source_target_pairs={{24,0},{9,1},{26,2},{11,3},{28,4},{13,5},{30,6},{15,7},{0,8},{17,9... | collective-permute-start | bytes 663560 | tf_op jit(solution)/shard_map/ppermute | solution.py:510
  41.8 0.0 collective-permute-done.11.refs_1_
  41.8 2.0 %collective-permute-done.12.refs_2_ = bf16[64,512]{1,0:T(8,128)(2,1)S(1)} collective-permute-done((bf16[64,512]{1,0:T(8,128)(2,1)S(1)}, bf16[64,512]{1,0:T(8,128)(2,1)S(1)}, u32[]{:S(2)}, u32[]{:S(2)}) %collective-permute-start.12) | collective-permute-done | bytes 65568 | tf_op jit(solution)/shard_map/ppermute | solution.py:502
  43.8 0.0 collective-permute-done.13.refs_3_
  43.9 1.7 %collective-permute-start.16 = (bf16[64,512]{1,0:T(8,128)(2,1)S(1)}, bf16[64,512]{1,0:T(8,128)(2,1)S(1)}, u32[]{:S(2)}, u32[]{:S(2)}) collective-permute-start(bf16[64,512]{1,0:T(8,128)(2,1)S(1)} %line_sum.1.refs_0_), channel_id=1, source_target_pairs={{0,24},{8,16},{16,8},{24,0},{1,25},{9,17},{17,9},{25,1},{2,26},{10... | collective-permute-start | bytes 196616 | tf_op jit(solution)/shard_map/ppermute | solution.py:514
  45.5 1.2 %collective-permute-start.15 = (bf16[64,512]{1,0:T(8,128)(2,1)S(1)}, bf16[64,512]{1,0:T(8,128)(2,1)S(1)}, u32[]{:S(2)}, u32[]{:S(2)}) collective-permute-start(bf16[64,512]{1,0:T(8,128)(2,1)S(1)} %line_sum.1.refs_0_), channel_id=1, source_target_pairs={{0,16},{8,24},{16,0},{24,8},{1,17},{9,25},{17,1},{25,9},{2,18},{10... | collective-permute-start | bytes 196616 | tf_op jit(solution)/shard_map/ppermute | solution.py:514
  46.7 0.7 %collective-permute-start.14 = (bf16[64,512]{1,0:T(8,128)(2,1)S(1)}, bf16[64,512]{1,0:T(8,128)(2,1)S(1)}, u32[]{:S(2)}, u32[]{:S(2)}) collective-permute-start(bf16[64,512]{1,0:T(8,128)(2,1)S(1)} %line_sum.1.refs_0_), channel_id=1, source_target_pairs={{0,8},{8,0},{16,24},{24,16},{1,9},{9,1},{17,25},{25,17},{2,10},{10... | collective-permute-start | bytes 196616 | tf_op jit(solution)/shard_map/ppermute | solution.py:514
  47.4 0.1 collective-permute-done.9.lat_in
  47.5 0.6 %place.1.placed = f32[288,1024]{1,0:T(8,128)S(1)} custom-call(bf16[144,1024]{1,0:T(8,128)(2,1)S(1)} %get-tuple-element.77.inner_results, bf16[144,1024]{1,0:T(8,128)(2,1)S(1)} %get-tuple-element.78.outer_results, bf16[108,1024]{1,0:T(8,128)(2,1)S(1)} %collective-permute-done.9.lat_in), custom_call_target="tpu_custom_call" | custom-call | bytes 1990656 | tf_op jit(solution)/shard_map/place/pallas_call | solution.py:387
  48.1 0.4 collective-permute-done.10.diag_in
  48.5 1.2 %place_rest.1 = (bf16[288,512]{1,0:T(8,128)(2,1)}, bf16[288,512]{1,0:T(8,128)(2,1)}, f32[8,128]{1,0:T(8,128)S(1)}) custom-call(f32[288,1024]{1,0:T(8,128)S(1)} %place.1.placed, bf16[36,1024]{1,0:T(8,128)(2,1)S(1)} %collective-permute-done.5._.lon_in, bf16[36,1024]{1,0:T(8,128)(2,1)S(1)} %collective-permute-done.10.diag_in), custom_call_target="tpu_custom_call" | custom-call | bytes 1921024 | tf_op jit(solution)/shard_map/place_rest/pallas_call | solution.py:387
  49.7 1.4 %collective-permute-done.16.refs_3_ = bf16[64,512]{1,0:T(8,128)(2,1)S(1)} collective-permute-done((bf16[64,512]{1,0:T(8,128)(2,1)S(1)}, bf16[64,512]{1,0:T(8,128)(2,1)S(1)}, u32[]{:S(2)}, u32[]{:S(2)}) %collective-permute-start.16) | collective-permute-done | bytes 65568 | tf_op jit(solution)/shard_map/ppermute | solution.py:514
  51.1 0.3 collective-permute-done.14.refs_1_
  51.4 0.9 %finish.1 = (f32[64,1536]{1,0:T(8,128)}, f32[64,512]{1,0:T(8,128)}) custom-call(f32[8,128]{1,0:T(8,128)S(1)} %get-tuple-element.88._, bf16[64,512]{1,0:T(8,128)(2,1)S(1)} %line_sum.1.refs_0_, bf16[64,512]{1,0:T(8,128)(2,1)S(1)} %collective-permute-done.14.refs_1_, bf16[64,512]{1,0:T(8,128)(2,1)S(1)} %collective-permute-done.15.refs_2_, ...), custom_call_target="tpu_custom_call" | custom-call | bytes 790528 | tf_op jit(solution)/shard_map/finish/pallas_call | solution.py:387
  (11 shorter events, 0.1 us)
Async XLA Ops:
  0.6 1.0 %copy-start.3 = (bf16[2,6,24,512]{3,2,1,0:T(8,128)(2,1)S(1)}, bf16[2,6,24,512]{3,2,1,0:T(8,128)(2,1)}, u32[]{:S(2)}) copy-start(bf16[2,6,24,512]{3,2,1,0:T(8,128)(2,1)} %param.5) | copy-start | bytes 884740
  0.6 1.0 %copy-start.2 = (bf16[2,6,24,512]{3,2,1,0:T(8,128)(2,1)S(1)}, bf16[2,6,24,512]{3,2,1,0:T(8,128)(2,1)}, u32[]{:S(2)}) copy-start(bf16[2,6,24,512]{3,2,1,0:T(8,128)(2,1)} %param.4) | copy-start | bytes 884740
  1.7 9.8 %copy-start.1 = (bf16[512,512]{1,0:T(8,128)(2,1)S(1)}, bf16[512,512]{1,0:T(8,128)(2,1)}, u32[]{:S(2)}) copy-start(bf16[512,512]{1,0:T(8,128)(2,1)} %refs_9_.1) | copy-start | bytes 1572868
  2.0 9.5 %copy-start = (bf16[512,1536]{1,0:T(8,128)(2,1)S(1)}, bf16[512,1536]{1,0:T(8,128)(2,1)}, u32[]{:S(2)}) copy-start(bf16[512,1536]{1,0:T(8,128)(2,1)} %refs_8_.1) | copy-start | bytes 4718596
  2.1 10.2 %collective-permute-start = (bf16[72,1024]{1,0:T(8,128)(2,1)S(1)}, bf16[72,1024]{1,0:T(8,128)(2,1)S(1)}, u32[]{:S(2)}, u32[]{:S(2)}) collective-permute-start(bf16[72,1024]{1,0:T(8,128)(2,1)S(1)} %get-tuple-element.60), channel_id=1, source_target_pairs={{0,24},{1,9},{2,26},{3,11},{4,28},{5,13},{6,30},{7,15},{8,0},{9,17... | collective-permute-start | bytes 442376 | tf_op jit(solution)/shard_map/ppermute | solution.py:441
  6.0 8.6 %collective-permute-start.1 = (bf16[36,1024]{1,0:T(8,128)(2,1)S(1)}, bf16[36,1024]{1,0:T(8,128)(2,1)S(1)}, u32[]{:S(2)}, u32[]{:S(2)}) collective-permute-start(bf16[36,1024]{1,0:T(8,128)(2,1)S(1)} %get-tuple-element.51._), channel_id=1, source_target_pairs={{0,7},{1,0},{2,1},{3,2},{4,3},{5,4},{6,5},{7,6},{8,15},{9,8},{10,9... | collective-permute-start | bytes 221192 | tf_op jit(solution)/shard_map/ppermute | solution.py:442
  8.4 6.1 %collective-permute-start.2 = (bf16[36,1024]{1,0:T(8,128)(2,1)S(1)}, bf16[36,1024]{1,0:T(8,128)(2,1)S(1)}, u32[]{:S(2)}, u32[]{:S(2)}) collective-permute-start(bf16[36,1024]{1,0:T(8,128)(2,1)S(1)} %get-tuple-element.65), channel_id=1, source_target_pairs={{0,24},{1,9},{2,26},{3,11},{4,28},{5,13},{6,30},{7,15},{8,0},{9,17... | collective-permute-start | bytes 221192 | tf_op jit(solution)/shard_map/ppermute | solution.py:443
  9.9 4.7 %collective-permute-start.3 = (bf16[36,1024]{1,0:T(8,128)(2,1)S(1)}, bf16[36,1024]{1,0:T(8,128)(2,1)S(1)}, u32[]{:S(2)}, u32[]{:S(2)}) collective-permute-start(bf16[36,1024]{1,0:T(8,128)(2,1)S(1)} %get-tuple-element.66), channel_id=1, source_target_pairs={{0,15},{1,24},{2,9},{3,26},{4,11},{5,28},{6,13},{7,30},{8,23},{9,0... | collective-permute-start | bytes 221192 | tf_op jit(solution)/shard_map/ppermute | solution.py:444
  17.1 2.0 %collective-permute-start.4 = (bf16[2,256,512]{2,1,0:T(8,128)(2,1)S(1)}, bf16[2,256,512]{2,1,0:T(8,128)(2,1)S(1)}, u32[]{:S(2)}, u32[]{:S(2)}) collective-permute-start(bf16[2,256,512]{2,1,0:T(8,128)(2,1)S(1)} %get-tuple-element.72), channel_id=1, source_target_pairs={{0,1},{1,0},{2,3},{3,2},{4,5},{5,4},{6,7},{7,6},{8,9},{9,8},{10,11... | collective-permute-start | bytes 1572872 | tf_op jit(solution)/shard_map/ppermute | solution.py:466
  18.0 5.3 %collective-permute-start.6 = (bf16[2,256,512]{2,1,0:T(8,128)(2,1)S(1)}, bf16[2,256,512]{2,1,0:T(8,128)(2,1)S(1)}, u32[]{:S(2)}, u32[]{:S(2)}) collective-permute-start(bf16[2,256,512]{2,1,0:T(8,128)(2,1)S(1)} %get-tuple-element.80), channel_id=1, source_target_pairs={{0,1},{1,0},{2,3},{3,2},{4,5},{5,4},{6,7},{7,6},{8,9},{9,8},{10,11... | collective-permute-start | bytes 1572872 | tf_op jit(solution)/shard_map/ppermute | solution.py:468
  19.2 9.7 %collective-permute-start.7 = (bf16[2,256,512]{2,1,0:T(8,128)(2,1)S(1)}, bf16[2,256,512]{2,1,0:T(8,128)(2,1)S(1)}, u32[]{:S(2)}, u32[]{:S(2)}) collective-permute-start(bf16[2,256,512]{2,1,0:T(8,128)(2,1)S(1)} %chip_sum.1._), channel_id=1, source_target_pairs={{0,8},{1,17},{2,10},{3,19},{4,12},{5,21},{6,14},{7,23},{8,0},{9,25... | collective-permute-start | bytes 1572872 | tf_op jit(solution)/shard_map/ppermute | solution.py:476
  23.2 5.7 %collective-permute-start.5 = (bf16[36,1024]{1,0:T(8,128)(2,1)S(1)}, bf16[36,1024]{1,0:T(8,128)(2,1)S(1)}, u32[]{:S(2)}, u32[]{:S(2)}) collective-permute-start(bf16[36,1024]{1,0:T(8,128)(2,1)S(1)} %pack_lon.1), channel_id=1, source_target_pairs={{7,0},{0,1},{1,2},{2,3},{3,4},{4,5},{5,6},{6,7},{15,8},{8,9},{9,10... | collective-permute-start | bytes 221192 | tf_op jit(solution)/shard_map/ppermute | solution.py:487
  29.1 6.4 %collective-permute-start.8 = (bf16[1,256,512]{2,1,0:T(8,128)(2,1)S(1)}, bf16[1,256,512]{2,1,0:T(8,128)(2,1)S(1)}, u32[]{:S(2)}, u32[]{:S(2)}) collective-permute-start(bf16[1,256,512]{2,1,0:T(8,128)(2,1)S(1)} %get-tuple-element.82), channel_id=1, source_target_pairs={{0,16},{1,9},{2,18},{3,11},{4,20},{5,13},{6,22},{7,15},{8,24},{9,1... | collective-permute-start | bytes 786440 | tf_op jit(solution)/shard_map/ppermute | solution.py:476
  35.6 6.3 %collective-permute-start.11 = (bf16[64,512]{1,0:T(8,128)(2,1)S(1)}, bf16[64,512]{1,0:T(8,128)(2,1)S(1)}, u32[]{:S(2)}, u32[]{:S(2)}) collective-permute-start(bf16[64,512]{1,0:T(8,128)(2,1)S(1)} %get-tuple-element.90), channel_id=1, source_target_pairs={{0,6},{1,7},{2,4},{3,5},{4,2},{5,3},{6,0},{7,1},{8,14},{9,15},{10,... | collective-permute-start | bytes 196616 | tf_op jit(solution)/shard_map/ppermute | solution.py:502
  38.6 5.2 %collective-permute-start.12 = (bf16[64,512]{1,0:T(8,128)(2,1)S(1)}, bf16[64,512]{1,0:T(8,128)(2,1)S(1)}, u32[]{:S(2)}, u32[]{:S(2)}) collective-permute-start(bf16[64,512]{1,0:T(8,128)(2,1)S(1)} %get-tuple-element.91), channel_id=1, source_target_pairs={{0,4},{1,5},{2,6},{3,7},{4,0},{5,1},{6,2},{7,3},{8,12},{9,13},{10,... | collective-permute-start | bytes 196616 | tf_op jit(solution)/shard_map/ppermute | solution.py:502
  38.6 5.2 %collective-permute-start.13 = (bf16[64,512]{1,0:T(8,128)(2,1)S(1)}, bf16[64,512]{1,0:T(8,128)(2,1)S(1)}, u32[]{:S(2)}, u32[]{:S(2)}) collective-permute-start(bf16[64,512]{1,0:T(8,128)(2,1)S(1)} %get-tuple-element.83._), channel_id=1, source_target_pairs={{0,2},{1,3},{2,0},{3,1},{4,6},{5,7},{6,4},{7,5},{8,10},{9,11},{10,... | collective-permute-start | bytes 196616 | tf_op jit(solution)/shard_map/ppermute | solution.py:502
  40.2 7.2 %collective-permute-start.9 = (bf16[108,1024]{1,0:T(8,128)(2,1)S(1)}, bf16[108,1024]{1,0:T(8,128)(2,1)S(1)}, u32[]{:S(2)}, u32[]{:S(2)}) collective-permute-start(bf16[108,1024]{1,0:T(8,128)(2,1)S(1)} %get-tuple-element.84), channel_id=1, source_target_pairs={{24,0},{9,1},{26,2},{11,3},{28,4},{13,5},{30,6},{15,7},{0,8},{17,9... | collective-permute-start | bytes 663560 | tf_op jit(solution)/shard_map/ppermute | solution.py:510
  41.8 6.7 %collective-permute-start.10 = (bf16[36,1024]{1,0:T(8,128)(2,1)S(1)}, bf16[36,1024]{1,0:T(8,128)(2,1)S(1)}, u32[]{:S(2)}, u32[]{:S(2)}) collective-permute-start(bf16[36,1024]{1,0:T(8,128)(2,1)S(1)} %get-tuple-element.85), channel_id=1, source_target_pairs={{15,0},{24,1},{9,2},{26,3},{11,4},{28,5},{13,6},{30,7},{23,8},{0,9... | collective-permute-start | bytes 221192 | tf_op jit(solution)/shard_map/ppermute | solution.py:511
  43.9 7.2 %collective-permute-start.16 = (bf16[64,512]{1,0:T(8,128)(2,1)S(1)}, bf16[64,512]{1,0:T(8,128)(2,1)S(1)}, u32[]{:S(2)}, u32[]{:S(2)}) collective-permute-start(bf16[64,512]{1,0:T(8,128)(2,1)S(1)} %line_sum.1.refs_0_), channel_id=1, source_target_pairs={{0,24},{8,16},{16,8},{24,0},{1,25},{9,17},{17,9},{25,1},{2,26},{10... | collective-permute-start | bytes 196616 | tf_op jit(solution)/shard_map/ppermute | solution.py:514
  45.5 5.5 %collective-permute-start.15 = (bf16[64,512]{1,0:T(8,128)(2,1)S(1)}, bf16[64,512]{1,0:T(8,128)(2,1)S(1)}, u32[]{:S(2)}, u32[]{:S(2)}) collective-permute-start(bf16[64,512]{1,0:T(8,128)(2,1)S(1)} %line_sum.1.refs_0_), channel_id=1, source_target_pairs={{0,16},{8,24},{16,0},{24,8},{1,17},{9,25},{17,1},{25,9},{2,18},{10... | collective-permute-start | bytes 196616 | tf_op jit(solution)/shard_map/ppermute | solution.py:514
  46.7 4.7 %collective-permute-start.14 = (bf16[64,512]{1,0:T(8,128)(2,1)S(1)}, bf16[64,512]{1,0:T(8,128)(2,1)S(1)}, u32[]{:S(2)}, u32[]{:S(2)}) collective-permute-start(bf16[64,512]{1,0:T(8,128)(2,1)S(1)} %line_sum.1.refs_0_), channel_id=1, source_target_pairs={{0,8},{8,0},{16,24},{24,16},{1,9},{9,1},{17,25},{25,17},{2,10},{10... | collective-permute-start | bytes 196616 | tf_op jit(solution)/shard_map/ppermute | solution.py:514

commit v13 on v9

--- a/solution.py
+++ b/solution.py
@@ -1,4 +1,5 @@
 import functools
+import math
 
 import jax
 import jax.numpy as jnp
@@ -119,7 +120,7 @@
 
 
 def transpose_bf16(block):
-    return jnp.transpose(block.astype(F32)).astype(BF)
+    return jnp.transpose(block.astype(BF))
 
 
 def slot_product(slot, size, lat, core, windows):
@@ -234,15 +235,16 @@
     k, v = blocks_of(projected, width), blocks_of(projected, 2 * width)
     q2 = [split_heads(block) for block in blocks_of(projected, 0)]
     dm2 = [split_heads(block) for block in blocks_of(d_mixed, 0)]
-    scores = [jnp.where(allowed, dot(k[p], q2[p], NT) * factor, -1e30) for p in pairs]
-    d_probs = [dot(v[p], dm2[p], NT) for p in pairs]
-    exponents = [jnp.exp(s - jnp.max(s, 0, keepdims=True)) for s in scores]
+    to_power = factor * math.log2(math.e)
+    scores = [jnp.where(allowed, dot(k[p], q2[p], NT), -1e30) for p in pairs]
+    d_probs = [dot(v[p], dm2[p] * jnp.asarray(factor, BF), NT) for p in pairs]
+    exponents = [jnp.exp2((s - jnp.max(s, 0, keepdims=True)) * to_power) for s in scores]
     probs = [e * (1.0 / jnp.sum(e, 0, keepdims=True)) for e in exponents]
     probs_b = [p.astype(BF) for p in probs]
     store(right, 3 * width, [join_heads(dot(probs_b[p], v[p], TN)) for p in pairs])
     store(right, 2 * width, [dot(probs_b[p], dm2[p], NN) for p in pairs])
     d_scores = [
-        (probs[p] * (d_probs[p] - jnp.sum(d_probs[p] * probs[p], 0, keepdims=True)) * factor).astype(BF)
+        (probs[p] * (d_probs[p] - jnp.sum(d_probs[p] * probs[p], 0, keepdims=True))).astype(BF)
         for p in pairs
     ]
     store(right, 0, [join_heads(dot(d_scores[p], k[p], TN)) for p in pairs])

time: 52.1 us -> 52 us (level)
  no operation moved by 1% of the time
where the time goes in v13:
time: 52 us; the launch traced here: 51.9 us
  starting transfers between devices  23.3 us (45%)
  waiting for transfers between devices  15.4 us (30%)
  Pallas kernels  11.5 us (22%)
  local copies, waits for them, and re-layouts  0.94 us (2%)
  between operations  0.79 us (2%)
    pallas_call x17, Pallas kernels, call(): pl.pallas_call(kernel, out_shape=shapes, in_specs=[anywhere if i in unrea...  11.5 us
    ppermute x1, waiting for transfers between devices, per_device(): lon_home = lax.ppermute(lon_back, both, back(lon_route))  5.64 us
    ppermute x2, waiting for transfers between devices, halving(): return lax.ppermute(send, both, route)  5.1 us
    ppermute x3, starting transfers between devices, per_device(): lax.ppermute(parts[step], 'lon', [(j, j ^ 2 * step) for j in range(lon_si...  4.45 us
    ppermute x1, starting transfers between devices, per_device(): inner_in = lax.ppermute(inner_lat, both, lat_route)  3.94 us
    ppermute x2, starting transfers between devices, halving(): return lax.ppermute(send, both, route)  3.67 us
    ppermute x3, starting transfers between devices, per_device(): lax.ppermute(line_sum, 'lat', [(i, i ^ step) for i in range(lat_size)])  3.55 us
    ppermute x1, starting transfers between devices, per_device(): lat_home = lax.ppermute(lat_back, both, back(lat_route))  2.07 us
  transfers between devices with their start and end apart: 17, of which 9 were waited for; matrix products, arithmetic and copies ran while one was open for 0% of the time, Pallas kernels for 15%

profile of v13, /device:TPU:0, one launch (start us, length us, event | category | flops | bytes accessed | tf_op | source)
XLA Modules:
  0.0 51.9 jit_solution(2152634780031841564)
XLA Ops:
  0.7 0.1 order.1
  0.8 0.8 %copy-done.3 = bf16[2,6,24,512]{3,2,1,0:T(8,128)(2,1)S(1)} copy-done((bf16[2,6,24,512]{3,2,1,0:T(8,128)(2,1)S(1)}, bf16[2,6,24,512]{3,2,1,0:T(8,128)(2,1)}, u32[]{:S(2)}) %copy-start.3) | copy-done | bytes 294936
  1.6 0.1 copy-done.2
  1.7 0.4 pack.1
  2.0 0.0 copy-start
  2.1 3.9 %collective-permute-start = (bf16[72,1024]{1,0:T(8,128)(2,1)S(1)}, bf16[72,1024]{1,0:T(8,128)(2,1)S(1)}, u32[]{:S(2)}, u32[]{:S(2)}) collective-permute-start(bf16[72,1024]{1,0:T(8,128)(2,1)S(1)} %get-tuple-element.60), channel_id=1, source_target_pairs={{0,24},{1,9},{2,26},{3,11},{4,28},{5,13},{6,30},{7,15},{8,0},{9,17... | collective-permute-start | bytes 442376 | tf_op jit(solution)/shard_map/ppermute | solution.py:435
  6.0 1.8 %collective-permute-start.1 = (bf16[36,1024]{1,0:T(8,128)(2,1)S(1)}, bf16[36,1024]{1,0:T(8,128)(2,1)S(1)}, u32[]{:S(2)}, u32[]{:S(2)}) collective-permute-start(bf16[36,1024]{1,0:T(8,128)(2,1)S(1)} %get-tuple-element.51._), channel_id=1, source_target_pairs={{0,7},{1,0},{2,1},{3,2},{4,3},{5,4},{6,5},{7,6},{8,15},{9,8},{10,9... | collective-permute-start | bytes 221192 | tf_op jit(solution)/shard_map/ppermute | solution.py:436
  7.8 0.6 %pack_rest.1 = (bf16[36,1024]{1,0:T(8,128)(2,1)S(1)}, bf16[36,1024]{1,0:T(8,128)(2,1)S(1)}, f32[72,1024]{1,0:T(8,128)S(1)}, f32[72,1024]{1,0:T(8,128)S(1)}) custom-call(bf16[36,1024]{1,0:T(8,128)(2,1)S(1)} %get-tuple-element.51._, bf16[288,512]{1,0:T(8,128)(2,1)S(1)} %bitcast.6, bf16[288,512]{1,0:T(8,128)(2,1)S(1)} %bitcast.8, ...), custom_call_target="tpu_custom_call" | custom-call | flops 500000000 | bytes 1525248 | tf_op jit(solution)/shard_map/pack_rest/pallas_call | solution.py:381
  8.4 1.5 %collective-permute-start.2 = (bf16[36,1024]{1,0:T(8,128)(2,1)S(1)}, bf16[36,1024]{1,0:T(8,128)(2,1)S(1)}, u32[]{:S(2)}, u32[]{:S(2)}) collective-permute-start(bf16[36,1024]{1,0:T(8,128)(2,1)S(1)} %get-tuple-element.65), channel_id=1, source_target_pairs={{0,24},{1,9},{2,26},{3,11},{4,28},{5,13},{6,30},{7,15},{8,0},{9,17... | collective-permute-start | bytes 221192 | tf_op jit(solution)/shard_map/ppermute | solution.py:437
  9.9 1.6 %collective-permute-start.3 = (bf16[36,1024]{1,0:T(8,128)(2,1)S(1)}, bf16[36,1024]{1,0:T(8,128)(2,1)S(1)}, u32[]{:S(2)}, u32[]{:S(2)}) collective-permute-start(bf16[36,1024]{1,0:T(8,128)(2,1)S(1)} %get-tuple-element.66), channel_id=1, source_target_pairs={{0,15},{1,24},{2,9},{3,26},{4,11},{5,28},{6,13},{7,30},{8,23},{9,0... | collective-permute-start | bytes 221192 | tf_op jit(solution)/shard_map/ppermute | solution.py:438
  11.5 0.7 %own.1 = (f32[72,512]{1,0:T(8,128)S(1)}, f32[72,1536]{1,0:T(8,128)S(1)}, f32[72,512]{1,0:T(8,128)S(1)}) custom-call(f32[72,1024]{1,0:T(8,128)S(1)} %get-tuple-element.56.inner_own.own, bf16[512,1536]{1,0:T(8,128)(2,1)S(1)} %copy-done, bf16[512,512]{1,0:T(8,128)(2,1)S(1)} %copy-done.1), custom_call_target="tpu_custom_call" | custom-call | flops 500000000 | bytes 3129344 | tf_op jit(solution)/shard_map/own/pallas_call | solution.py:381
  12.2 0.0 collective-permute-done.lat_in
  12.2 2.1 %inner.1 = (f32[2,256,512]{2,1,0:T(8,128)S(1)}, bf16[144,512]{1,0:T(8,128)(2,1)S(1)}, bf16[144,512]{1,0:T(8,128)(2,1)S(1)}, bf16[2,256,144]{2,1,0:T(8,128)(2,1)S...) custom-call(f32[72,1024]{1,0:T(8,128)S(1)} %get-tuple-element.56.inner_own.own, ...), custom_call_target="tpu_custom_call" | custom-call | flops 1000000000 | bytes 5505024 | tf_op jit(solution)/shard_map/inner/pallas_call | solution.py:381
  14.3 0.0 collective-permute-done.1.lon_in
  14.4 0.0 collective-permute-done.2.lat_in
  14.4 2.3 %outer.1 = (bf16[2,256,512]{2,1,0:T(8,128)(2,1)S(1)}, bf16[144,512]{1,0:T(8,128)(2,1)S(1)}, bf16[144,512]{1,0:T(8,128)(2,1)S(1)}, bf16[2,256,144]{2,1,0:T(8,128)...) custom-call(f32[72,1024]{1,0:T(8,128)S(1)} %get-tuple-element.64.own, ...), custom_call_target="tpu_custom_call" | custom-call | flops 1000000000 | bytes 5365760 | tf_op jit(solution)/shard_map/outer/pallas_call | solution.py:381
  16.7 0.1 collective-permute-start.4
  16.8 0.7 %keep.1 = (bf16[2,256,512]{2,1,0:T(8,128)(2,1)S(1)}, bf16[2,256,512]{2,1,0:T(8,128)(2,1)S(1)}) custom-call(bf16[2,256,144]{2,1,0:T(8,128)(2,1)S(1)} %get-tuple-element.61.refs_0_.refs_2_, bf16[144,2048]{1,0:T(8,128)(2,1)S(1)} %get-tuple-element.62.refs_1_.refs_3_, bf16[2,256,144]{2,1,0:T(8,128)(2,1)S(1)} %get-tuple-element.63.refs_2_, ...), custom_call_target="tpu_custom_call" | custom-call | flops 1000000000 | bytes 2818048 | tf_op jit(solution)/shard_map/keep/pallas_call | solution.py:381
  17.5 0.5 %collective-permute-start.6 = (bf16[2,256,512]{2,1,0:T(8,128)(2,1)S(1)}, bf16[2,256,512]{2,1,0:T(8,128)(2,1)S(1)}, u32[]{:S(2)}, u32[]{:S(2)}) collective-permute-start(bf16[2,256,512]{2,1,0:T(8,128)(2,1)S(1)} %get-tuple-element.80), channel_id=1, source_target_pairs={{0,1},{1,0},{2,3},{3,2},{4,5},{5,4},{6,7},{7,6},{8,9},{9,8},{10,11... | collective-permute-start | bytes 1572872 | tf_op jit(solution)/shard_map/ppermute | solution.py:462
  18.1 0.6 %collective-permute-done.4.refs_1_ = bf16[2,256,512]{2,1,0:T(8,128)(2,1)S(1)} collective-permute-done((bf16[2,256,512]{2,1,0:T(8,128)(2,1)S(1)}, bf16[2,256,512]{2,1,0:T(8,128)(2,1)S(1)}, u32[]{:S(2)}, u32[]{:S(2)}) %collective-permute-start.4) | collective-permute-done | bytes 524320 | tf_op jit(solution)/shard_map/ppermute | solution.py:460
  18.7 0.1 chip_sum.1._
  18.8 2.2 %collective-permute-start.7 = (bf16[2,256,512]{2,1,0:T(8,128)(2,1)S(1)}, bf16[2,256,512]{2,1,0:T(8,128)(2,1)S(1)}, u32[]{:S(2)}, u32[]{:S(2)}) collective-permute-start(bf16[2,256,512]{2,1,0:T(8,128)(2,1)S(1)} %chip_sum.1._), channel_id=1, source_target_pairs={{0,8},{1,17},{2,10},{3,19},{4,12},{5,21},{6,14},{7,23},{8,0},{9,25... | collective-permute-start | bytes 1572872 | tf_op jit(solution)/shard_map/ppermute | solution.py:470
  21.0 1.2 %outputs.1 = (bf16[2,256,512]{2,1,0:T(8,128)(2,1)S(1)}, bf16[144,1024]{1,0:T(8,128)(2,1)S(1)}, bf16[144,1024]{1,0:T(8,128)(2,1)S(1)}) custom-call(bf16[2,256,512]{2,1,0:T(8,128)(2,1)S(1)} %chip_sum.1._, bf16[144,512]{1,0:T(8,128)(2,1)S(1)} %get-tuple-element.73.refs_0_, bf16[144,512]{1,0:T(8,128)(2,1)S(1)} %get-tuple-element.74.refs_1_, ...), custom_call_target="tpu_custom_call" | custom-call | flops 1000000000 | bytes 5799936 | tf_op jit(solution)/shard_map/outputs/pallas_call | solution.py:381
  22.2 0.1 pack_lon.1
  22.4 0.1 collective-permute-start.5
  22.4 0.0 collective-permute-done.6.refs_1_
  22.4 5.6 %collective-permute-done.5._.lon_in = bf16[36,1024]{1,0:T(8,128)(2,1)S(1)} collective-permute-done((bf16[36,1024]{1,0:T(8,128)(2,1)S(1)}, bf16[36,1024]{1,0:T(8,128)(2,1)S(1)}, u32[]{:S(2)}, u32[]{:S(2)}) %collective-permute-start.5) | collective-permute-done | bytes 73760 | tf_op jit(solution)/shard_map/ppermute | solution.py:481
  28.1 0.1 collective-permute-done.7.refs_2_
  28.2 0.2 halve1.1
  28.4 1.5 %collective-permute-start.8 = (bf16[1,256,512]{2,1,0:T(8,128)(2,1)S(1)}, bf16[1,256,512]{2,1,0:T(8,128)(2,1)S(1)}, u32[]{:S(2)}, u32[]{:S(2)}) collective-permute-start(bf16[1,256,512]{2,1,0:T(8,128)(2,1)S(1)} %get-tuple-element.82), channel_id=1, source_target_pairs={{0,16},{1,9},{2,18},{3,11},{4,20},{5,13},{6,22},{7,15},{8,24},{9,1... | collective-permute-start | bytes 786440 | tf_op jit(solution)/shard_map/ppermute | solution.py:470
  29.8 5.0 %collective-permute-done.8.refs_1_ = bf16[1,256,512]{2,1,0:T(8,128)(2,1)S(1)} collective-permute-done((bf16[1,256,512]{2,1,0:T(8,128)(2,1)S(1)}, bf16[1,256,512]{2,1,0:T(8,128)(2,1)S(1)}, u32[]{:S(2)}, u32[]{:S(2)}) %collective-permute-start.8) | collective-permute-done | bytes 262176 | tf_op jit(solution)/shard_map/ppermute | solution.py:470
  34.8 0.1 line_parts.1
  34.9 3.5 %collective-permute-start.11 = (bf16[64,512]{1,0:T(8,128)(2,1)S(1)}, bf16[64,512]{1,0:T(8,128)(2,1)S(1)}, u32[]{:S(2)}, u32[]{:S(2)}) collective-permute-start(bf16[64,512]{1,0:T(8,128)(2,1)S(1)} %get-tuple-element.90), channel_id=1, source_target_pairs={{0,6},{1,7},{2,4},{3,5},{4,2},{5,3},{6,0},{7,1},{8,14},{9,15},{10,... | collective-permute-start | bytes 196616 | tf_op jit(solution)/shard_map/ppermute | solution.py:496
  38.4 0.9 %collective-permute-start.13 = (bf16[64,512]{1,0:T(8,128)(2,1)S(1)}, bf16[64,512]{1,0:T(8,128)(2,1)S(1)}, u32[]{:S(2)}, u32[]{:S(2)}) collective-permute-start(bf16[64,512]{1,0:T(8,128)(2,1)S(1)} %get-tuple-element.83._), channel_id=1, source_target_pairs={{0,2},{1,3},{2,0},{3,1},{4,6},{5,7},{6,4},{7,5},{8,10},{9,11},{10,... | collective-permute-start | bytes 196616 | tf_op jit(solution)/shard_map/ppermute | solution.py:496
  39.4 0.2 pack_back.1
  39.5 2.1 %collective-permute-start.9 = (bf16[108,1024]{1,0:T(8,128)(2,1)S(1)}, bf16[108,1024]{1,0:T(8,128)(2,1)S(1)}, u32[]{:S(2)}, u32[]{:S(2)}) collective-permute-start(bf16[108,1024]{1,0:T(8,128)(2,1)S(1)} %get-tuple-element.84), channel_id=1, source_target_pairs={{24,0},{9,1},{26,2},{11,3},{28,4},{13,5},{30,6},{15,7},{0,8},{17,9... | collective-permute-start | bytes 663560 | tf_op jit(solution)/shard_map/ppermute | solution.py:504
  41.6 2.0 %collective-permute-done.12.refs_2_ = bf16[64,512]{1,0:T(8,128)(2,1)S(1)} collective-permute-done((bf16[64,512]{1,0:T(8,128)(2,1)S(1)}, bf16[64,512]{1,0:T(8,128)(2,1)S(1)}, u32[]{:S(2)}, u32[]{:S(2)}) %collective-permute-start.12) | collective-permute-done | bytes 65568 | tf_op jit(solution)/shard_map/ppermute | solution.py:496
  43.6 0.0 collective-permute-done.13.refs_3_
  43.7 1.6 %collective-permute-start.16 = (bf16[64,512]{1,0:T(8,128)(2,1)S(1)}, bf16[64,512]{1,0:T(8,128)(2,1)S(1)}, u32[]{:S(2)}, u32[]{:S(2)}) collective-permute-start(bf16[64,512]{1,0:T(8,128)(2,1)S(1)} %line_sum.1.refs_0_), channel_id=1, source_target_pairs={{0,24},{8,16},{16,8},{24,0},{1,25},{9,17},{17,9},{25,1},{2,26},{10... | collective-permute-start | bytes 196616 | tf_op jit(solution)/shard_map/ppermute | solution.py:508
  45.3 1.2 %collective-permute-start.15 = (bf16[64,512]{1,0:T(8,128)(2,1)S(1)}, bf16[64,512]{1,0:T(8,128)(2,1)S(1)}, u32[]{:S(2)}, u32[]{:S(2)}) collective-permute-start(bf16[64,512]{1,0:T(8,128)(2,1)S(1)} %line_sum.1.refs_0_), channel_id=1, source_target_pairs={{0,16},{8,24},{16,0},{24,8},{1,17},{9,25},{17,1},{25,9},{2,18},{10... | collective-permute-start | bytes 196616 | tf_op jit(solution)/shard_map/ppermute | solution.py:508
  46.5 0.7 %collective-permute-start.14 = (bf16[64,512]{1,0:T(8,128)(2,1)S(1)}, bf16[64,512]{1,0:T(8,128)(2,1)S(1)}, u32[]{:S(2)}, u32[]{:S(2)}) collective-permute-start(bf16[64,512]{1,0:T(8,128)(2,1)S(1)} %line_sum.1.refs_0_), channel_id=1, source_target_pairs={{0,8},{8,0},{16,24},{24,16},{1,9},{9,1},{17,25},{25,17},{2,10},{10... | collective-permute-start | bytes 196616 | tf_op jit(solution)/shard_map/ppermute | solution.py:508
  47.3 0.6 %place.1.placed = f32[288,1024]{1,0:T(8,128)S(1)} custom-call(bf16[144,1024]{1,0:T(8,128)(2,1)S(1)} %get-tuple-element.77.inner_results, bf16[144,1024]{1,0:T(8,128)(2,1)S(1)} %get-tuple-element.78.outer_results, bf16[108,1024]{1,0:T(8,128)(2,1)S(1)} %collective-permute-done.9.lat_in), custom_call_target="tpu_custom_call" | custom-call | bytes 1990656 | tf_op jit(solution)/shard_map/place/pallas_call | solution.py:381
  47.9 0.5 collective-permute-done.10.diag_in
  48.3 1.2 %place_rest.1 = (bf16[288,512]{1,0:T(8,128)(2,1)}, bf16[288,512]{1,0:T(8,128)(2,1)}, f32[8,128]{1,0:T(8,128)S(1)}) custom-call(f32[288,1024]{1,0:T(8,128)S(1)} %place.1.placed, bf16[36,1024]{1,0:T(8,128)(2,1)S(1)} %collective-permute-done.5._.lon_in, bf16[36,1024]{1,0:T(8,128)(2,1)S(1)} %collective-permute-done.10.diag_in), custom_call_target="tpu_custom_call" | custom-call | bytes 1921024 | tf_op jit(solution)/shard_map/place_rest/pallas_call | solution.py:381
  49.5 0.7 %collective-permute-done.16.refs_3_ = bf16[64,512]{1,0:T(8,128)(2,1)S(1)} collective-permute-done((bf16[64,512]{1,0:T(8,128)(2,1)S(1)}, bf16[64,512]{1,0:T(8,128)(2,1)S(1)}, u32[]{:S(2)}, u32[]{:S(2)}) %collective-permute-start.16) | collective-permute-done | bytes 65568 | tf_op jit(solution)/shard_map/ppermute | solution.py:508
  50.2 0.1 collective-permute-done.15.refs_2_
  50.4 0.6 %collective-permute-done.14.refs_1_ = bf16[64,512]{1,0:T(8,128)(2,1)S(1)} collective-permute-done((bf16[64,512]{1,0:T(8,128)(2,1)S(1)}, bf16[64,512]{1,0:T(8,128)(2,1)S(1)}, u32[]{:S(2)}, u32[]{:S(2)}) %collective-permute-start.14) | collective-permute-done | bytes 65568 | tf_op jit(solution)/shard_map/ppermute | solution.py:508
  51.0 0.9 %finish.1 = (f32[64,1536]{1,0:T(8,128)}, f32[64,512]{1,0:T(8,128)}) custom-call(f32[8,128]{1,0:T(8,128)S(1)} %get-tuple-element.88._, bf16[64,512]{1,0:T(8,128)(2,1)S(1)} %line_sum.1.refs_0_, bf16[64,512]{1,0:T(8,128)(2,1)S(1)} %collective-permute-done.14.refs_1_, bf16[64,512]{1,0:T(8,128)(2,1)S(1)} %collective-permute-done.15.refs_2_, ...), custom_call_target="tpu_custom_call" | custom-call | bytes 790528 | tf_op jit(solution)/shard_map/finish/pallas_call | solution.py:381
  (11 shorter events, 0.1 us)
Async XLA Ops:
  0.6 1.0 %copy-start.3 = (bf16[2,6,24,512]{3,2,1,0:T(8,128)(2,1)S(1)}, bf16[2,6,24,512]{3,2,1,0:T(8,128)(2,1)}, u32[]{:S(2)}) copy-start(bf16[2,6,24,512]{3,2,1,0:T(8,128)(2,1)} %param.5) | copy-start | bytes 884740
  0.6 1.0 %copy-start.2 = (bf16[2,6,24,512]{3,2,1,0:T(8,128)(2,1)S(1)}, bf16[2,6,24,512]{3,2,1,0:T(8,128)(2,1)}, u32[]{:S(2)}) copy-start(bf16[2,6,24,512]{3,2,1,0:T(8,128)(2,1)} %param.4) | copy-start | bytes 884740
  1.7 9.8 %copy-start.1 = (bf16[512,512]{1,0:T(8,128)(2,1)S(1)}, bf16[512,512]{1,0:T(8,128)(2,1)}, u32[]{:S(2)}) copy-start(bf16[512,512]{1,0:T(8,128)(2,1)} %refs_9_.1) | copy-start | bytes 1572868
  2.0 9.5 %copy-start = (bf16[512,1536]{1,0:T(8,128)(2,1)S(1)}, bf16[512,1536]{1,0:T(8,128)(2,1)}, u32[]{:S(2)}) copy-start(bf16[512,1536]{1,0:T(8,128)(2,1)} %refs_8_.1) | copy-start | bytes 4718596
  2.1 10.2 %collective-permute-start = (bf16[72,1024]{1,0:T(8,128)(2,1)S(1)}, bf16[72,1024]{1,0:T(8,128)(2,1)S(1)}, u32[]{:S(2)}, u32[]{:S(2)}) collective-permute-start(bf16[72,1024]{1,0:T(8,128)(2,1)S(1)} %get-tuple-element.60), channel_id=1, source_target_pairs={{0,24},{1,9},{2,26},{3,11},{4,28},{5,13},{6,30},{7,15},{8,0},{9,17... | collective-permute-start | bytes 442376 | tf_op jit(solution)/shard_map/ppermute | solution.py:435
  6.0 8.3 %collective-permute-start.1 = (bf16[36,1024]{1,0:T(8,128)(2,1)S(1)}, bf16[36,1024]{1,0:T(8,128)(2,1)S(1)}, u32[]{:S(2)}, u32[]{:S(2)}) collective-permute-start(bf16[36,1024]{1,0:T(8,128)(2,1)S(1)} %get-tuple-element.51._), channel_id=1, source_target_pairs={{0,7},{1,0},{2,1},{3,2},{4,3},{5,4},{6,5},{7,6},{8,15},{9,8},{10,9... | collective-permute-start | bytes 221192 | tf_op jit(solution)/shard_map/ppermute | solution.py:436
  8.4 5.9 %collective-permute-start.2 = (bf16[36,1024]{1,0:T(8,128)(2,1)S(1)}, bf16[36,1024]{1,0:T(8,128)(2,1)S(1)}, u32[]{:S(2)}, u32[]{:S(2)}) collective-permute-start(bf16[36,1024]{1,0:T(8,128)(2,1)S(1)} %get-tuple-element.65), channel_id=1, source_target_pairs={{0,24},{1,9},{2,26},{3,11},{4,28},{5,13},{6,30},{7,15},{8,0},{9,17... | collective-permute-start | bytes 221192 | tf_op jit(solution)/shard_map/ppermute | solution.py:437
  9.9 4.4 %collective-permute-start.3 = (bf16[36,1024]{1,0:T(8,128)(2,1)S(1)}, bf16[36,1024]{1,0:T(8,128)(2,1)S(1)}, u32[]{:S(2)}, u32[]{:S(2)}) collective-permute-start(bf16[36,1024]{1,0:T(8,128)(2,1)S(1)} %get-tuple-element.66), channel_id=1, source_target_pairs={{0,15},{1,24},{2,9},{3,26},{4,11},{5,28},{6,13},{7,30},{8,23},{9,0... | collective-permute-start | bytes 221192 | tf_op jit(solution)/shard_map/ppermute | solution.py:438
  16.7 2.0 %collective-permute-start.4 = (bf16[2,256,512]{2,1,0:T(8,128)(2,1)S(1)}, bf16[2,256,512]{2,1,0:T(8,128)(2,1)S(1)}, u32[]{:S(2)}, u32[]{:S(2)}) collective-permute-start(bf16[2,256,512]{2,1,0:T(8,128)(2,1)S(1)} %get-tuple-element.72), channel_id=1, source_target_pairs={{0,1},{1,0},{2,3},{3,2},{4,5},{5,4},{6,7},{7,6},{8,9},{9,8},{10,11... | collective-permute-start | bytes 1572872 | tf_op jit(solution)/shard_map/ppermute | solution.py:460
  17.5 4.9 %collective-permute-start.6 = (bf16[2,256,512]{2,1,0:T(8,128)(2,1)S(1)}, bf16[2,256,512]{2,1,0:T(8,128)(2,1)S(1)}, u32[]{:S(2)}, u32[]{:S(2)}) collective-permute-start(bf16[2,256,512]{2,1,0:T(8,128)(2,1)S(1)} %get-tuple-element.80), channel_id=1, source_target_pairs={{0,1},{1,0},{2,3},{3,2},{4,5},{5,4},{6,7},{7,6},{8,9},{9,8},{10,11... | collective-permute-start | bytes 1572872 | tf_op jit(solution)/shard_map/ppermute | solution.py:462
  18.8 9.4 %collective-permute-start.7 = (bf16[2,256,512]{2,1,0:T(8,128)(2,1)S(1)}, bf16[2,256,512]{2,1,0:T(8,128)(2,1)S(1)}, u32[]{:S(2)}, u32[]{:S(2)}) collective-permute-start(bf16[2,256,512]{2,1,0:T(8,128)(2,1)S(1)} %chip_sum.1._), channel_id=1, source_target_pairs={{0,8},{1,17},{2,10},{3,19},{4,12},{5,21},{6,14},{7,23},{8,0},{9,25... | collective-permute-start | bytes 1572872 | tf_op jit(solution)/shard_map/ppermute | solution.py:470
  22.4 5.7 %collective-permute-start.5 = (bf16[36,1024]{1,0:T(8,128)(2,1)S(1)}, bf16[36,1024]{1,0:T(8,128)(2,1)S(1)}, u32[]{:S(2)}, u32[]{:S(2)}) collective-permute-start(bf16[36,1024]{1,0:T(8,128)(2,1)S(1)} %pack_lon.1), channel_id=1, source_target_pairs={{7,0},{0,1},{1,2},{2,3},{3,4},{4,5},{5,6},{6,7},{15,8},{8,9},{9,10... | collective-permute-start | bytes 221192 | tf_op jit(solution)/shard_map/ppermute | solution.py:481
  28.4 6.4 %collective-permute-start.8 = (bf16[1,256,512]{2,1,0:T(8,128)(2,1)S(1)}, bf16[1,256,512]{2,1,0:T(8,128)(2,1)S(1)}, u32[]{:S(2)}, u32[]{:S(2)}) collective-permute-start(bf16[1,256,512]{2,1,0:T(8,128)(2,1)S(1)} %get-tuple-element.82), channel_id=1, source_target_pairs={{0,16},{1,9},{2,18},{3,11},{4,20},{5,13},{6,22},{7,15},{8,24},{9,1... | collective-permute-start | bytes 786440 | tf_op jit(solution)/shard_map/ppermute | solution.py:470
  34.9 6.7 %collective-permute-start.11 = (bf16[64,512]{1,0:T(8,128)(2,1)S(1)}, bf16[64,512]{1,0:T(8,128)(2,1)S(1)}, u32[]{:S(2)}, u32[]{:S(2)}) collective-permute-start(bf16[64,512]{1,0:T(8,128)(2,1)S(1)} %get-tuple-element.90), channel_id=1, source_target_pairs={{0,6},{1,7},{2,4},{3,5},{4,2},{5,3},{6,0},{7,1},{8,14},{9,15},{10,... | collective-permute-start | bytes 196616 | tf_op jit(solution)/shard_map/ppermute | solution.py:496
  38.4 5.2 %collective-permute-start.12 = (bf16[64,512]{1,0:T(8,128)(2,1)S(1)}, bf16[64,512]{1,0:T(8,128)(2,1)S(1)}, u32[]{:S(2)}, u32[]{:S(2)}) collective-permute-start(bf16[64,512]{1,0:T(8,128)(2,1)S(1)} %get-tuple-element.91), channel_id=1, source_target_pairs={{0,4},{1,5},{2,6},{3,7},{4,0},{5,1},{6,2},{7,3},{8,12},{9,13},{10,... | collective-permute-start | bytes 196616 | tf_op jit(solution)/shard_map/ppermute | solution.py:496
  38.4 5.2 %collective-permute-start.13 = (bf16[64,512]{1,0:T(8,128)(2,1)S(1)}, bf16[64,512]{1,0:T(8,128)(2,1)S(1)}, u32[]{:S(2)}, u32[]{:S(2)}) collective-permute-start(bf16[64,512]{1,0:T(8,128)(2,1)S(1)} %get-tuple-element.83._), channel_id=1, source_target_pairs={{0,2},{1,3},{2,0},{3,1},{4,6},{5,7},{6,4},{7,5},{8,10},{9,11},{10,... | collective-permute-start | bytes 196616 | tf_op jit(solution)/shard_map/ppermute | solution.py:496
  39.5 7.7 %collective-permute-start.9 = (bf16[108,1024]{1,0:T(8,128)(2,1)S(1)}, bf16[108,1024]{1,0:T(8,128)(2,1)S(1)}, u32[]{:S(2)}, u32[]{:S(2)}) collective-permute-start(bf16[108,1024]{1,0:T(8,128)(2,1)S(1)} %get-tuple-element.84), channel_id=1, source_target_pairs={{24,0},{9,1},{26,2},{11,3},{28,4},{13,5},{30,6},{15,7},{0,8},{17,9... | collective-permute-start | bytes 663560 | tf_op jit(solution)/shard_map/ppermute | solution.py:504
  41.6 6.7 %collective-permute-start.10 = (bf16[36,1024]{1,0:T(8,128)(2,1)S(1)}, bf16[36,1024]{1,0:T(8,128)(2,1)S(1)}, u32[]{:S(2)}, u32[]{:S(2)}) collective-permute-start(bf16[36,1024]{1,0:T(8,128)(2,1)S(1)} %get-tuple-element.85), channel_id=1, source_target_pairs={{15,0},{24,1},{9,2},{26,3},{11,4},{28,5},{13,6},{30,7},{23,8},{0,9... | collective-permute-start | bytes 221192 | tf_op jit(solution)/shard_map/ppermute | solution.py:505
  43.7 6.5 %collective-permute-start.16 = (bf16[64,512]{1,0:T(8,128)(2,1)S(1)}, bf16[64,512]{1,0:T(8,128)(2,1)S(1)}, u32[]{:S(2)}, u32[]{:S(2)}) collective-permute-start(bf16[64,512]{1,0:T(8,128)(2,1)S(1)} %line_sum.1.refs_0_), channel_id=1, source_target_pairs={{0,24},{8,16},{16,8},{24,0},{1,25},{9,17},{17,9},{25,1},{2,26},{10... | collective-permute-start | bytes 196616 | tf_op jit(solution)/shard_map/ppermute | solution.py:508
  45.3 5.0 %collective-permute-start.15 = (bf16[64,512]{1,0:T(8,128)(2,1)S(1)}, bf16[64,512]{1,0:T(8,128)(2,1)S(1)}, u32[]{:S(2)}, u32[]{:S(2)}) collective-permute-start(bf16[64,512]{1,0:T(8,128)(2,1)S(1)} %line_sum.1.refs_0_), channel_id=1, source_target_pairs={{0,16},{8,24},{16,0},{24,8},{1,17},{9,25},{17,1},{25,9},{2,18},{10... | collective-permute-start | bytes 196616 | tf_op jit(solution)/shard_map/ppermute | solution.py:508
  46.5 4.5 %collective-permute-start.14 = (bf16[64,512]{1,0:T(8,128)(2,1)S(1)}, bf16[64,512]{1,0:T(8,128)(2,1)S(1)}, u32[]{:S(2)}, u32[]{:S(2)}) collective-permute-start(bf16[64,512]{1,0:T(8,128)(2,1)S(1)} %line_sum.1.refs_0_), channel_id=1, source_target_pairs={{0,8},{8,0},{16,24},{24,16},{1,9},{9,1},{17,25},{25,17},{2,10},{10... | collective-permute-start | bytes 196616 | tf_op jit(solution)/shard_map/ppermute | solution.py:508

commit v14 on v9

--- a/solution.py
+++ b/solution.py
@@ -169,7 +169,7 @@
         send_grad[slot // 2] = slot_product(slot, size, lat, 1 - core, [(left, right)])
 
 
-def outer_kernel(own, lon_in, lat_in, diag_in, qkv_weight, proj_weight, grad_so_far, send_first, *refs):
+def outer_kernel(own, lon_in, lat_in, diag_in, qkv_weight, proj_weight, grad_so_far, send_a, send_b, *refs):
     last = picks(last_rows, HALF, QUARTER)
     both = jnp.concatenate(
         [
@@ -183,7 +183,13 @@
     lat, core, size = place()
     for slot in range(1, size, 2):
         total = grad_so_far[slot // 2] + slot_product(slot, size, lat, 1 - core, [(left, right)])
-        send_first[slot // 2] = total.astype(BF)
+        put_chunks((send_a, send_b), slot // 2, total)
+
+
+def put_chunks(outs, slot, total):
+    width = outs[0].shape[2]
+    for chunk, out in enumerate(outs):
+        out[slot] = total[:, chunk * width : (chunk + 1) * width].astype(BF)
 
 
 def place():
@@ -256,23 +262,28 @@
 
 
 def keep_kernel(*refs):
-    *windows, send_rest, keep_first = refs
+    *windows, keep_a, keep_b = refs
+    windows = [windows[:2], windows[2:]]
+    lat, core, size = place()
+    for slot in range(1, size, 2):
+        put_chunks((keep_a, keep_b), slot // 2, slot_product(slot, size, lat, core, windows))
+
+
+def rest_kernel(_, __, *refs):
+    *windows, send_rest, keep_rest = refs
     windows = windows[:3], windows[3:]
     lat, core, size = place()
     for slot in range(0, size, 2):
         send_rest[slot // 2] = slot_product(slot, size, lat, 1 - core, [(w[2], w[1]) for w in windows]).astype(BF)
-    for slot in range(1, size, 2):
-        keep_first[slot // 2] = slot_product(slot, size, lat, core, [(w[0], w[1]) for w in windows]).astype(BF)
+    for slot in range(0, size, 2):
+        keep_rest[slot // 2] = slot_product(slot, size, lat, core, [(w[0], w[1]) for w in windows]).astype(BF)
 
 
 def output_kernel(_, *refs):
-    (*windows, qkv_weight, proj_weight, keep_rest, inner_results, outer_results) = refs
-    per_window = windows[:4], windows[4:]
-    lat, core, size = place()
+    (*windows, qkv_weight, proj_weight, inner_results, outer_results) = refs
+    per_window = windows[:3], windows[3:]
     width = proj_weight.shape[0]
-    for slot in range(0, size, 2):
-        keep_rest[slot // 2] = slot_product(slot, size, lat, core, [w[2:] for w in per_window]).astype(BF)
-    x, grads, right = (jnp.concatenate([w[i][...] for w in per_window], axis=0) for i in (0, 1, 3))
+    x, grads, right = (jnp.concatenate([w[i][...] for w in per_window], axis=0) for i in range(3))
     d_projected, mixed = right[:, : 3 * width], right[:, 3 * width :]
     x = x.astype(F32)
     normed, inv_std = normalise(x)
@@ -330,19 +341,25 @@
     d_fields[...] = total[:, width:]
 
 
-def halve_kernel(_, *refs):
+def halve_kernel(chunk, _, *refs):
     *parts, send, keep = refs
+    width = send.shape[2]
+
+    def lanes(part):
+        return slice(None) if part.shape[2] == width else slice(chunk * width, (chunk + 1) * width)
+
     for slot in range(send.shape[0]):
         for out, source in ((send, 2 * slot + 1), (keep, 2 * slot)):
-            out[slot] = sum(part[source].astype(F32) for part in parts).astype(BF)
+            out[slot] = sum(part[source, :, lanes(part)].astype(F32) for part in parts).astype(BF)
 
 
 def line_parts_kernel(count, *refs):
-    parts, (keep, *sends) = refs[:count], refs[count:]
+    chunks, (keep, *sends) = (refs[:count], refs[count : 2 * count]), refs[2 * count :]
     rows = keep.shape[0]
     for step, out in enumerate((keep, *sends)):
         at = slice(step * rows, (step + 1) * rows)
-        out[...] = sum(part[0, at].astype(F32) for part in parts).astype(out.dtype)
+        totals = [sum(part[0, at].astype(F32) for part in parts) for parts in chunks]
+        out[...] = jnp.concatenate(totals, axis=1).astype(out.dtype)
 
 
 def sum_kernel(*refs):
@@ -371,11 +388,11 @@
             proj_out[:, pl.ds(pl.multiple_of((share - of_qkv) * width, width), width)] = total
 
 
-def call(kernel, outs, *args, name, flops=0, limit=32, scratch=(), unread=()):
+def call(kernel, outs, *args, name, flops=0, limit=32, scratch=(), unread=(), beside=False):
     vmem = pl.BlockSpec(memory_space=pltpu.VMEM)
     anywhere = pl.BlockSpec(memory_space=pl.ANY)
     shapes = [jax.ShapeDtypeStruct(shape, dtype) for shape, dtype in outs]
-    nbytes = sum(a.size * a.dtype.itemsize for a in (*args, *shapes))
+    nbytes = 0 if beside else sum(a.size * a.dtype.itemsize for a in (*args, *shapes))
     return pl.pallas_call(
         kernel,
         out_shape=shapes,
@@ -437,6 +454,7 @@
 
     split = (lat_size, width // 2, 4 * width // lat_size)
     halves = ((lat_size // 2, *split[1:]), BF)
+    chunk = ((lat_size // 2, split[1], split[2] // 2), BF)
     per_window = [
         ((WIN, width), BF),
         ((WIN, width), BF),
@@ -449,15 +467,14 @@
         inner_kernel, [(halves[0], F32), *per_window], inner_own, *own_parts, inner_in, qkv_weight, proj_weight,
         name="inner", flops=10**9, scratch=scratch,
     )
-    send_first, *outer = call(
-        outer_kernel, [halves, *per_window],
+    send_a, send_b, *outer = call(
+        outer_kernel, [chunk, chunk, *per_window],
         outer_own, lon_in, outer_in, diag_in, qkv_weight, proj_weight, grad_so_far,
         name="outer", flops=10**9, scratch=scratch,
     )
     sibling = [(j, j ^ 1) for j in range(lon_size)]
-    received_first = lax.ppermute(send_first, "lon", sibling)
-    send_rest, keep_first = call(keep_kernel, [halves, halves], *inner[2:], *outer[2:], name="keep", flops=10**9)
-    received_rest = lax.ppermute(send_rest, "lon", sibling)
+    arrived = [lax.ppermute(send, "lon", sibling) for send in (send_a, send_b)]
+    keep = call(keep_kernel, [chunk, chunk], *inner[2:4], *outer[2:4], name="keep", flops=10**9)
 
     def halving(phase, send):
         route = [
@@ -468,27 +485,38 @@
         return lax.ppermute(send, both, route)
 
     bits = lat_size.bit_length() - 1
-    (send,) = call(sum_kernel, [halves], keep_first, received_first, name="chip_sum")
-    received = halving(0, send)
-    keep_rest, *results = call(
-        output_kernel, [halves, ((WIN, 2 * width), BF), ((WIN, 2 * width), BF)],
-        send, *inner[:4], *outer[:4], qkv_weight, proj_weight,
-        name="outputs", flops=10**9, unread=(0,),
-    )
-    (lon_back,) = call(pack_lon_kernel, [quarter], results[1], name="pack_lon")
+    sends = [
+        call(sum_kernel, [chunk], mine, theirs, name="chip_sum")[0] for mine, theirs in zip(keep, arrived)
+    ]
+    received = [halving(0, send) for send in sends]
+    send_rest, keep_rest = call(
+        rest_kernel, [halves, halves], *sends, *inner[2:], *outer[2:], name="rest", unread=(0, 1), beside=True
+    )
+    received_rest = lax.ppermute(send_rest, "lon", sibling)
+    results = call(
+        output_kernel, [((WIN, 2 * width), BF)] * 2,
+        keep_rest, *inner[:2], inner[3], *outer[:2], outer[3], qkv_weight, proj_weight,
+        name="outputs", unread=(0,), flops=10**10,
+    )
+    (lon_back,) = call(pack_lon_kernel, [quarter], results[1], name="pack_lon", beside=True)
     lon_home = lax.ppermute(lon_back, both, back(lon_route))
-    kept = [keep_rest, received_rest, received]
+    kept = [[keep_rest, received_rest, part] for part in received]
     slots = lat_size // 2
     for phase in range(1, bits):
         slots //= 2
-        stay = ((slots, *split[1:]), BF)
-        send, keep = call(halve_kernel, [stay, stay], lon_home, *kept, name=f"halve{slots}", unread=(0,))
-        kept = [keep, halving(phase, send)]
+        stay = ((slots, *chunk[0][1:]), BF)
+        for index, after in enumerate((lon_home, sends[1])):
+            send, keep = call(
+                functools.partial(halve_kernel, index), [stay, stay], after, *kept[index],
+                name=f"halve{slots}", unread=(0,),
+            )
+            kept[index] = [keep, halving(phase, send)]
 
     rows = width // lon_size
     share = ((rows, split[2]), BF)
     parts = call(
-        functools.partial(line_parts_kernel, len(kept)), [share] * (lon_size // 2), *kept, name="line_parts"
+        functools.partial(line_parts_kernel, len(kept[0])), [share] * (lon_size // 2), *kept[0], *kept[1],
+        name="line_parts",
     )
     arrived = [
         lax.ppermute(parts[step], "lon", [(j, j ^ (2 * step)) for j in range(lon_size)])

time: 52.1 us -> 50.8 us (0.975)
  waiting for transfers between devices: 15.4 us -> 11.9 us
  starting transfers between devices: 23.3 us -> 25.4 us
    ppermute x1, waiting for transfers between devices: 5.64 us -> 2.02 us  [per_device(): lon_home = lax.ppermute(lon_back, both, back(lon_route))]
    ppermute x2 -> x4, starting transfers between devices: 3.67 us -> 5.35 us  [halving(): return lax.ppermute(send, both, route)]
    pallas_call x17 -> x20, Pallas kernels: 11.5 us -> 11.7 us  [call(): pl.pallas_call(kernel, out_shape=shapes, in_specs=[anywhere if i in unrea...]
    ppermute x2 -> x4, waiting for transfers between devices: 5.08 us -> 5.23 us  [halving(): return lax.ppermute(send, both, route)]
  transfers between devices with their start and end apart: 17 -> 20, of which waited for: 9 -> 10; matrix products, arithmetic and copies ran while one was open for 0% -> 0% of each run, Pallas kernels for 15% -> 16%
where the time goes in v14:
time: 50.8 us; the launch traced here: 50.7 us
  starting transfers between devices  25.4 us (50%)
  waiting for transfers between devices  11.9 us (23%)
  Pallas kernels  11.7 us (23%)
  local copies, waits for them, and re-layouts  0.94 us (2%)
  between operations  0.8 us (2%)
    pallas_call x20, Pallas kernels, call(): pl.pallas_call(kernel, out_shape=shapes, in_specs=[anywhere if i in unrea...  11.7 us
    ppermute x4, starting transfers between devices, halving(): return lax.ppermute(send, both, route)  5.35 us
    ppermute x4, waiting for transfers between devices, halving(): return lax.ppermute(send, both, route)  5.23 us
    ppermute x3, starting transfers between devices, per_device(): lax.ppermute(parts[step], 'lon', [(j, j ^ 2 * step) for j in range(lon_si...  4.45 us
    ppermute x1, starting transfers between devices, per_device(): inner_in = lax.ppermute(inner_lat, both, lat_route)  3.94 us
    ppermute x3, starting transfers between devices, per_device(): lax.ppermute(line_sum, 'lat', [(i, i ^ step) for i in range(lat_size)])  3.55 us
    ppermute x1, waiting for transfers between devices, per_device(): lon_home = lax.ppermute(lon_back, both, back(lon_route))  2.02 us
    ppermute x1, starting transfers between devices, per_device(): lat_home = lax.ppermute(lat_back, both, back(lat_route))  1.98 us
  transfers between devices with their start and end apart: 20, of which 10 were waited for; matrix products, arithmetic and copies ran while one was open for 0% of the time, Pallas kernels for 16%

profile of v14, /device:TPU:0, one launch (start us, length us, event | category | flops | bytes accessed | tf_op | source)
XLA Modules:
  0.0 50.7 jit_solution(11327197581515270871)
XLA Ops:
  0.7 0.1 order.1
  0.8 0.8 %copy-done.3 = bf16[2,6,24,512]{3,2,1,0:T(8,128)(2,1)S(1)} copy-done((bf16[2,6,24,512]{3,2,1,0:T(8,128)(2,1)S(1)}, bf16[2,6,24,512]{3,2,1,0:T(8,128)(2,1)}, u32[]{:S(2)}) %copy-start.3) | copy-done | bytes 294936
  1.6 0.1 copy-done.2
  1.7 0.4 pack.1
  2.1 3.9 %collective-permute-start = (bf16[72,1024]{1,0:T(8,128)(2,1)S(1)}, bf16[72,1024]{1,0:T(8,128)(2,1)S(1)}, u32[]{:S(2)}, u32[]{:S(2)}) collective-permute-start(bf16[72,1024]{1,0:T(8,128)(2,1)S(1)} %get-tuple-element.64), channel_id=1, source_target_pairs={{0,24},{1,9},{2,26},{3,11},{4,28},{5,13},{6,30},{7,15},{8,0},{9,17... | collective-permute-start | bytes 442376 | tf_op jit(solution)/shard_map/ppermute | solution.py:450
  6.0 1.8 %collective-permute-start.1 = (bf16[36,1024]{1,0:T(8,128)(2,1)S(1)}, bf16[36,1024]{1,0:T(8,128)(2,1)S(1)}, u32[]{:S(2)}, u32[]{:S(2)}) collective-permute-start(bf16[36,1024]{1,0:T(8,128)(2,1)S(1)} %get-tuple-element.55._), channel_id=1, source_target_pairs={{0,7},{1,0},{2,1},{3,2},{4,3},{5,4},{6,5},{7,6},{8,15},{9,8},{10,9... | collective-permute-start | bytes 221192 | tf_op jit(solution)/shard_map/ppermute | solution.py:451
  7.8 0.6 %pack_rest.1 = (bf16[36,1024]{1,0:T(8,128)(2,1)S(1)}, bf16[36,1024]{1,0:T(8,128)(2,1)S(1)}, f32[72,1024]{1,0:T(8,128)S(1)}, f32[72,1024]{1,0:T(8,128)S(1)}) custom-call(bf16[36,1024]{1,0:T(8,128)(2,1)S(1)} %get-tuple-element.55._, bf16[288,512]{1,0:T(8,128)(2,1)S(1)} %bitcast.6, bf16[288,512]{1,0:T(8,128)(2,1)S(1)} %bitcast.8, ...), custom_call_target="tpu_custom_call" | custom-call | flops 500000000 | bytes 1525248 | tf_op jit(solution)/shard_map/pack_rest/pallas_call | solution.py:396
  8.4 1.5 %collective-permute-start.2 = (bf16[36,1024]{1,0:T(8,128)(2,1)S(1)}, bf16[36,1024]{1,0:T(8,128)(2,1)S(1)}, u32[]{:S(2)}, u32[]{:S(2)}) collective-permute-start(bf16[36,1024]{1,0:T(8,128)(2,1)S(1)} %get-tuple-element.68), channel_id=1, source_target_pairs={{0,24},{1,9},{2,26},{3,11},{4,28},{5,13},{6,30},{7,15},{8,0},{9,17... | collective-permute-start | bytes 221192 | tf_op jit(solution)/shard_map/ppermute | solution.py:452
  9.9 1.6 %collective-permute-start.3 = (bf16[36,1024]{1,0:T(8,128)(2,1)S(1)}, bf16[36,1024]{1,0:T(8,128)(2,1)S(1)}, u32[]{:S(2)}, u32[]{:S(2)}) collective-permute-start(bf16[36,1024]{1,0:T(8,128)(2,1)S(1)} %get-tuple-element.69), channel_id=1, source_target_pairs={{0,15},{1,24},{2,9},{3,26},{4,11},{5,28},{6,13},{7,30},{8,23},{9,0... | collective-permute-start | bytes 221192 | tf_op jit(solution)/shard_map/ppermute | solution.py:453
  11.5 0.7 %own.1 = (f32[72,512]{1,0:T(8,128)S(1)}, f32[72,1536]{1,0:T(8,128)S(1)}, f32[72,512]{1,0:T(8,128)S(1)}) custom-call(f32[72,1024]{1,0:T(8,128)S(1)} %get-tuple-element.60.inner_own.own, bf16[512,1536]{1,0:T(8,128)(2,1)S(1)} %copy-done, bf16[512,512]{1,0:T(8,128)(2,1)S(1)} %copy-done.1), custom_call_target="tpu_custom_call" | custom-call | flops 500000000 | bytes 3129344 | tf_op jit(solution)/shard_map/own/pallas_call | solution.py:396
  12.2 2.1 %inner.1 = (f32[2,256,512]{2,1,0:T(8,128)S(1)}, bf16[144,512]{1,0:T(8,128)(2,1)S(1)}, bf16[144,512]{1,0:T(8,128)(2,1)S(1)}, bf16[2,256,144]{2,1,0:T(8,128)(2,1)S...) custom-call(f32[72,1024]{1,0:T(8,128)S(1)} %get-tuple-element.60.inner_own.own, ...), custom_call_target="tpu_custom_call" | custom-call | flops 1000000000 | bytes 5505024 | tf_op jit(solution)/shard_map/inner/pallas_call | solution.py:396
  14.4 2.4 %outer.1 = (bf16[2,256,256]{2,1,0:T(8,128)(2,1)S(1)}, bf16[2,256,256]{2,1,0:T(8,128)(2,1)S(1)}, bf16[144,512]{1,0:T(8,128)(2,1)S(1)}, bf16[144,512]{1,0:T(8,128)...) custom-call(f32[72,1024]{1,0:T(8,128)S(1)} %get-tuple-element.67.own, ...), custom_call_target="tpu_custom_call" | custom-call | flops 1000000000 | bytes 5365760 | tf_op jit(solution)/shard_map/outer/pallas_call | solution.py:396
  16.8 0.1 collective-permute-start.5
  16.9 0.4 collective-permute-start.4
  17.3 0.4 keep.1
  17.8 0.6 %collective-permute-done.5.refs_1_ = bf16[2,256,256]{2,1,0:T(8,128)(2,1)S(1)} collective-permute-done((bf16[2,256,256]{2,1,0:T(8,128)(2,1)S(1)}, bf16[2,256,256]{2,1,0:T(8,128)(2,1)S(1)}, u32[]{:S(2)}, u32[]{:S(2)}) %collective-permute-start.5) | collective-permute-done | bytes 262176 | tf_op jit(solution)/shard_map/ppermute | solution.py:476
  18.4 0.1 chip_sum.3.__._
  18.4 2.2 %collective-permute-start.10 = (bf16[2,256,256]{2,1,0:T(8,128)(2,1)S(1)}, bf16[2,256,256]{2,1,0:T(8,128)(2,1)S(1)}, u32[]{:S(2)}, u32[]{:S(2)}) collective-permute-start(bf16[2,256,256]{2,1,0:T(8,128)(2,1)S(1)} %chip_sum.3.__._), channel_id=1, source_target_pairs={{0,8},{1,17},{2,10},{3,19},{4,12},{5,21},{6,14},{7,23},{8,0},{9,25... | collective-permute-start | bytes 786440 | tf_op jit(solution)/shard_map/ppermute | solution.py:485
  20.6 0.1 chip_sum.2._
  20.7 0.3 collective-permute-start.8
  21.0 0.7 %rest.1 = (bf16[2,256,512]{2,1,0:T(8,128)(2,1)S(1)}, bf16[2,256,512]{2,1,0:T(8,128)(2,1)S(1)}) custom-call(bf16[2,256,256]{2,1,0:T(8,128)(2,1)S(1)} %chip_sum.2._, bf16[2,256,256]{2,1,0:T(8,128)(2,1)S(1)} %chip_sum.3.__._, bf16[2,256,144]{2,1,0:T(8,128)(2,1)S(1)} %get-tuple-element.65.refs_0_, bf16[144,2048]{1,0:T(8,128)(2,1)S(1)} %get-tuple-element.66.refs_1_.refs_2_, ...), custom_call_target="tpu_custom_call" | custom-call | tf_op jit(solution)/shard_map/rest/pallas_call | solution.py:396
  21.7 0.1 collective-permute-start.7
  21.8 0.9 %outputs.1 = (bf16[144,1024]{1,0:T(8,128)(2,1)S(1)}, bf16[144,1024]{1,0:T(8,128)(2,1)S(1)}) custom-call(bf16[2,256,512]{2,1,0:T(8,128)(2,1)S(1)} %get-tuple-element.79._.refs_0_, bf16[144,512]{1,0:T(8,128)(2,1)S(1)} %get-tuple-element.80.refs_0_, bf16[144,512]{1,0:T(8,128)(2,1)S(1)} %get-tuple-element.81.refs_1_, ...), custom_call_target="tpu_custom_call" | custom-call | flops 10000000000 | bytes 4980736 | tf_op jit(solution)/shard_map/outputs/pallas_call | solution.py:396
  22.7 0.2 pack_lon.1
  22.8 0.5 %collective-permute-start.6 = (bf16[36,1024]{1,0:T(8,128)(2,1)S(1)}, bf16[36,1024]{1,0:T(8,128)(2,1)S(1)}, u32[]{:S(2)}, u32[]{:S(2)}) collective-permute-start(bf16[36,1024]{1,0:T(8,128)(2,1)S(1)} %pack_lon.1), channel_id=1, source_target_pairs={{7,0},{0,1},{1,2},{2,3},{3,4},{4,5},{5,6},{6,7},{15,8},{8,9},{9,10... | collective-permute-start | bytes 221192 | tf_op jit(solution)/shard_map/ppermute | solution.py:502
  23.4 1.6 %collective-permute-done.10.refs_2_ = bf16[2,256,256]{2,1,0:T(8,128)(2,1)S(1)} collective-permute-done((bf16[2,256,256]{2,1,0:T(8,128)(2,1)S(1)}, bf16[2,256,256]{2,1,0:T(8,128)(2,1)S(1)}, u32[]{:S(2)}, u32[]{:S(2)}) %collective-permute-start.10) | collective-permute-done | bytes 262176 | tf_op jit(solution)/shard_map/ppermute | solution.py:485
  25.0 0.1 halve1.3
  25.1 1.5 %collective-permute-start.11 = (bf16[1,256,256]{2,1,0:T(8,128)(2,1)S(1)}, bf16[1,256,256]{2,1,0:T(8,128)(2,1)S(1)}, u32[]{:S(2)}, u32[]{:S(2)}) collective-permute-start(bf16[1,256,256]{2,1,0:T(8,128)(2,1)S(1)} %get-tuple-element.90), channel_id=1, source_target_pairs={{0,16},{1,9},{2,18},{3,11},{4,20},{5,13},{6,22},{7,15},{8,24},{9,1... | collective-permute-start | bytes 393224 | tf_op jit(solution)/shard_map/ppermute | solution.py:485
  26.5 2.0 %collective-permute-done.6._.lon_in = bf16[36,1024]{1,0:T(8,128)(2,1)S(1)} collective-permute-done((bf16[36,1024]{1,0:T(8,128)(2,1)S(1)}, bf16[36,1024]{1,0:T(8,128)(2,1)S(1)}, u32[]{:S(2)}, u32[]{:S(2)}) %collective-permute-start.6) | collective-permute-done | bytes 73760 | tf_op jit(solution)/shard_map/ppermute | solution.py:502
  28.6 0.1 halve1.2
  28.7 1.4 %collective-permute-start.9 = (bf16[1,256,256]{2,1,0:T(8,128)(2,1)S(1)}, bf16[1,256,256]{2,1,0:T(8,128)(2,1)S(1)}, u32[]{:S(2)}, u32[]{:S(2)}) collective-permute-start(bf16[1,256,256]{2,1,0:T(8,128)(2,1)S(1)} %get-tuple-element.88), channel_id=1, source_target_pairs={{0,16},{1,9},{2,18},{3,11},{4,20},{5,13},{6,22},{7,15},{8,24},{9,1... | collective-permute-start | bytes 393224 | tf_op jit(solution)/shard_map/ppermute | solution.py:485
  30.1 3.6 %collective-permute-done.9.refs_1_ = bf16[1,256,256]{2,1,0:T(8,128)(2,1)S(1)} collective-permute-done((bf16[1,256,256]{2,1,0:T(8,128)(2,1)S(1)}, bf16[1,256,256]{2,1,0:T(8,128)(2,1)S(1)}, u32[]{:S(2)}, u32[]{:S(2)}) %collective-permute-start.9) | collective-permute-done | bytes 131104 | tf_op jit(solution)/shard_map/ppermute | solution.py:485
  33.7 0.1 line_parts.1
  33.8 3.2 %collective-permute-start.14 = (bf16[64,512]{1,0:T(8,128)(2,1)S(1)}, bf16[64,512]{1,0:T(8,128)(2,1)S(1)}, u32[]{:S(2)}, u32[]{:S(2)}) collective-permute-start(bf16[64,512]{1,0:T(8,128)(2,1)S(1)} %get-tuple-element.98), channel_id=1, source_target_pairs={{0,6},{1,7},{2,4},{3,5},{4,2},{5,3},{6,0},{7,1},{8,14},{9,15},{10,... | collective-permute-start | bytes 196616 | tf_op jit(solution)/shard_map/ppermute | solution.py:522
  36.9 1.3 %collective-permute-start.16 = (bf16[64,512]{1,0:T(8,128)(2,1)S(1)}, bf16[64,512]{1,0:T(8,128)(2,1)S(1)}, u32[]{:S(2)}, u32[]{:S(2)}) collective-permute-start(bf16[64,512]{1,0:T(8,128)(2,1)S(1)} %get-tuple-element.91._), channel_id=1, source_target_pairs={{0,2},{1,3},{2,0},{3,1},{4,6},{5,7},{6,4},{7,5},{8,10},{9,11},{10,... | collective-permute-start | bytes 196616 | tf_op jit(solution)/shard_map/ppermute | solution.py:522
  38.2 0.2 pack_back.1
  38.4 2.0 %collective-permute-start.12 = (bf16[108,1024]{1,0:T(8,128)(2,1)S(1)}, bf16[108,1024]{1,0:T(8,128)(2,1)S(1)}, u32[]{:S(2)}, u32[]{:S(2)}) collective-permute-start(bf16[108,1024]{1,0:T(8,128)(2,1)S(1)} %get-tuple-element.92), channel_id=1, source_target_pairs={{24,0},{9,1},{26,2},{11,3},{28,4},{13,5},{30,6},{15,7},{0,8},{17,9... | collective-permute-start | bytes 663560 | tf_op jit(solution)/shard_map/ppermute | solution.py:530
  40.4 0.1 collective-permute-done.14.refs_1_
  40.5 1.6 %collective-permute-done.15.refs_2_ = bf16[64,512]{1,0:T(8,128)(2,1)S(1)} collective-permute-done((bf16[64,512]{1,0:T(8,128)(2,1)S(1)}, bf16[64,512]{1,0:T(8,128)(2,1)S(1)}, u32[]{:S(2)}, u32[]{:S(2)}) %collective-permute-start.15) | collective-permute-done | bytes 65568 | tf_op jit(solution)/shard_map/ppermute | solution.py:522
  42.2 1.7 %collective-permute-start.19 = (bf16[64,512]{1,0:T(8,128)(2,1)S(1)}, bf16[64,512]{1,0:T(8,128)(2,1)S(1)}, u32[]{:S(2)}, u32[]{:S(2)}) collective-permute-start(bf16[64,512]{1,0:T(8,128)(2,1)S(1)} %line_sum.1.refs_0_), channel_id=1, source_target_pairs={{0,24},{8,16},{16,8},{24,0},{1,25},{9,17},{17,9},{25,1},{2,26},{10... | collective-permute-start | bytes 196616 | tf_op jit(solution)/shard_map/ppermute | solution.py:534
  43.9 0.9 %collective-permute-start.18 = (bf16[64,512]{1,0:T(8,128)(2,1)S(1)}, bf16[64,512]{1,0:T(8,128)(2,1)S(1)}, u32[]{:S(2)}, u32[]{:S(2)}) collective-permute-start(bf16[64,512]{1,0:T(8,128)(2,1)S(1)} %line_sum.1.refs_0_), channel_id=1, source_target_pairs={{0,16},{8,24},{16,0},{24,8},{1,17},{9,25},{17,1},{25,9},{2,18},{10... | collective-permute-start | bytes 196616 | tf_op jit(solution)/shard_map/ppermute | solution.py:534
  44.8 0.9 %collective-permute-start.17 = (bf16[64,512]{1,0:T(8,128)(2,1)S(1)}, bf16[64,512]{1,0:T(8,128)(2,1)S(1)}, u32[]{:S(2)}, u32[]{:S(2)}) collective-permute-start(bf16[64,512]{1,0:T(8,128)(2,1)S(1)} %line_sum.1.refs_0_), channel_id=1, source_target_pairs={{0,8},{8,0},{16,24},{24,16},{1,9},{9,1},{17,25},{25,17},{2,10},{10... | collective-permute-start | bytes 196616 | tf_op jit(solution)/shard_map/ppermute | solution.py:534
  45.7 0.6 %place.1.placed = f32[288,1024]{1,0:T(8,128)S(1)} custom-call(bf16[144,1024]{1,0:T(8,128)(2,1)S(1)} %get-tuple-element.84.inner_results, bf16[144,1024]{1,0:T(8,128)(2,1)S(1)} %get-tuple-element.85.outer_results, bf16[108,1024]{1,0:T(8,128)(2,1)S(1)} %collective-permute-done.12.lat_in), custom_call_target="tpu_custom_call" | custom-call | bytes 1990656 | tf_op jit(solution)/shard_map/place/pallas_call | solution.py:396
  46.3 0.8 %collective-permute-done.13.diag_in = bf16[36,1024]{1,0:T(8,128)(2,1)S(1)} collective-permute-done((bf16[36,1024]{1,0:T(8,128)(2,1)S(1)}, bf16[36,1024]{1,0:T(8,128)(2,1)S(1)}, u32[]{:S(2)}, u32[]{:S(2)}) %collective-permute-start.13) | collective-permute-done | bytes 73760 | tf_op jit(solution)/shard_map/ppermute | solution.py:531
  47.1 1.2 %place_rest.1 = (bf16[288,512]{1,0:T(8,128)(2,1)}, bf16[288,512]{1,0:T(8,128)(2,1)}, f32[8,128]{1,0:T(8,128)S(1)}) custom-call(f32[288,1024]{1,0:T(8,128)S(1)} %place.1.placed, bf16[36,1024]{1,0:T(8,128)(2,1)S(1)} %collective-permute-done.6._.lon_in, bf16[36,1024]{1,0:T(8,128)(2,1)S(1)} %collective-permute-done.13.diag_in), custom_call_target="tpu_custom_call" | custom-call | bytes 1921024 | tf_op jit(solution)/shard_map/place_rest/pallas_call | solution.py:396
  48.3 0.9 %collective-permute-done.19.refs_3_ = bf16[64,512]{1,0:T(8,128)(2,1)S(1)} collective-permute-done((bf16[64,512]{1,0:T(8,128)(2,1)S(1)}, bf16[64,512]{1,0:T(8,128)(2,1)S(1)}, u32[]{:S(2)}, u32[]{:S(2)}) %collective-permute-start.19) | collective-permute-done | bytes 65568 | tf_op jit(solution)/shard_map/ppermute | solution.py:534
  49.3 0.6 %collective-permute-done.17.refs_1_ = bf16[64,512]{1,0:T(8,128)(2,1)S(1)} collective-permute-done((bf16[64,512]{1,0:T(8,128)(2,1)S(1)}, bf16[64,512]{1,0:T(8,128)(2,1)S(1)}, u32[]{:S(2)}, u32[]{:S(2)}) %collective-permute-start.17) | collective-permute-done | bytes 65568 | tf_op jit(solution)/shard_map/ppermute | solution.py:534
  49.8 0.9 %finish.1 = (f32[64,1536]{1,0:T(8,128)}, f32[64,512]{1,0:T(8,128)}) custom-call(f32[8,128]{1,0:T(8,128)S(1)} %get-tuple-element.96._, bf16[64,512]{1,0:T(8,128)(2,1)S(1)} %line_sum.1.refs_0_, bf16[64,512]{1,0:T(8,128)(2,1)S(1)} %collective-permute-done.17.refs_1_, bf16[64,512]{1,0:T(8,128)(2,1)S(1)} %collective-permute-done.18.refs_2_, ...), custom_call_target="tpu_custom_call" | custom-call | bytes 790528 | tf_op jit(solution)/shard_map/finish/pallas_call | solution.py:396
  (20 shorter events, 0.1 us)
Async XLA Ops:
  0.6 1.0 %copy-start.3 = (bf16[2,6,24,512]{3,2,1,0:T(8,128)(2,1)S(1)}, bf16[2,6,24,512]{3,2,1,0:T(8,128)(2,1)}, u32[]{:S(2)}) copy-start(bf16[2,6,24,512]{3,2,1,0:T(8,128)(2,1)} %param.5) | copy-start | bytes 884740
  0.6 1.0 %copy-start.2 = (bf16[2,6,24,512]{3,2,1,0:T(8,128)(2,1)S(1)}, bf16[2,6,24,512]{3,2,1,0:T(8,128)(2,1)}, u32[]{:S(2)}) copy-start(bf16[2,6,24,512]{3,2,1,0:T(8,128)(2,1)} %param.4) | copy-start | bytes 884740
  1.7 9.8 %copy-start.1 = (bf16[512,512]{1,0:T(8,128)(2,1)S(1)}, bf16[512,512]{1,0:T(8,128)(2,1)}, u32[]{:S(2)}) copy-start(bf16[512,512]{1,0:T(8,128)(2,1)} %refs_7_.1) | copy-start | bytes 1572868
  2.0 9.5 %copy-start = (bf16[512,1536]{1,0:T(8,128)(2,1)S(1)}, bf16[512,1536]{1,0:T(8,128)(2,1)}, u32[]{:S(2)}) copy-start(bf16[512,1536]{1,0:T(8,128)(2,1)} %refs_6_.1) | copy-start | bytes 4718596
  2.1 10.2 %collective-permute-start = (bf16[72,1024]{1,0:T(8,128)(2,1)S(1)}, bf16[72,1024]{1,0:T(8,128)(2,1)S(1)}, u32[]{:S(2)}, u32[]{:S(2)}) collective-permute-start(bf16[72,1024]{1,0:T(8,128)(2,1)S(1)} %get-tuple-element.64), channel_id=1, source_target_pairs={{0,24},{1,9},{2,26},{3,11},{4,28},{5,13},{6,30},{7,15},{8,0},{9,17... | collective-permute-start | bytes 442376 | tf_op jit(solution)/shard_map/ppermute | solution.py:450
  6.0 8.4 %collective-permute-start.1 = (bf16[36,1024]{1,0:T(8,128)(2,1)S(1)}, bf16[36,1024]{1,0:T(8,128)(2,1)S(1)}, u32[]{:S(2)}, u32[]{:S(2)}) collective-permute-start(bf16[36,1024]{1,0:T(8,128)(2,1)S(1)} %get-tuple-element.55._), channel_id=1, source_target_pairs={{0,7},{1,0},{2,1},{3,2},{4,3},{5,4},{6,5},{7,6},{8,15},{9,8},{10,9... | collective-permute-start | bytes 221192 | tf_op jit(solution)/shard_map/ppermute | solution.py:451
  8.4 5.9 %collective-permute-start.2 = (bf16[36,1024]{1,0:T(8,128)(2,1)S(1)}, bf16[36,1024]{1,0:T(8,128)(2,1)S(1)}, u32[]{:S(2)}, u32[]{:S(2)}) collective-permute-start(bf16[36,1024]{1,0:T(8,128)(2,1)S(1)} %get-tuple-element.68), channel_id=1, source_target_pairs={{0,24},{1,9},{2,26},{3,11},{4,28},{5,13},{6,30},{7,15},{8,0},{9,17... | collective-permute-start | bytes 221192 | tf_op jit(solution)/shard_map/ppermute | solution.py:452
  9.9 4.5 %collective-permute-start.3 = (bf16[36,1024]{1,0:T(8,128)(2,1)S(1)}, bf16[36,1024]{1,0:T(8,128)(2,1)S(1)}, u32[]{:S(2)}, u32[]{:S(2)}) collective-permute-start(bf16[36,1024]{1,0:T(8,128)(2,1)S(1)} %get-tuple-element.69), channel_id=1, source_target_pairs={{0,15},{1,24},{2,9},{3,26},{4,11},{5,28},{6,13},{7,30},{8,23},{9,0... | collective-permute-start | bytes 221192 | tf_op jit(solution)/shard_map/ppermute | solution.py:453
  16.8 1.6 %collective-permute-start.5 = (bf16[2,256,256]{2,1,0:T(8,128)(2,1)S(1)}, bf16[2,256,256]{2,1,0:T(8,128)(2,1)S(1)}, u32[]{:S(2)}, u32[]{:S(2)}) collective-permute-start(bf16[2,256,256]{2,1,0:T(8,128)(2,1)S(1)} %get-tuple-element.76), channel_id=1, source_target_pairs={{0,1},{1,0},{2,3},{3,2},{4,5},{5,4},{6,7},{7,6},{8,9},{9,8},{10,11... | collective-permute-start | bytes 786440 | tf_op jit(solution)/shard_map/ppermute | solution.py:476
  16.9 3.7 %collective-permute-start.4 = (bf16[2,256,256]{2,1,0:T(8,128)(2,1)S(1)}, bf16[2,256,256]{2,1,0:T(8,128)(2,1)S(1)}, u32[]{:S(2)}, u32[]{:S(2)}) collective-permute-start(bf16[2,256,256]{2,1,0:T(8,128)(2,1)S(1)} %get-tuple-element.74), channel_id=1, source_target_pairs={{0,1},{1,0},{2,3},{3,2},{4,5},{5,4},{6,7},{7,6},{8,9},{9,8},{10,11... | collective-permute-start | bytes 786440 | tf_op jit(solution)/shard_map/ppermute | solution.py:476
  18.4 6.6 %collective-permute-start.10 = (bf16[2,256,256]{2,1,0:T(8,128)(2,1)S(1)}, bf16[2,256,256]{2,1,0:T(8,128)(2,1)S(1)}, u32[]{:S(2)}, u32[]{:S(2)}) collective-permute-start(bf16[2,256,256]{2,1,0:T(8,128)(2,1)S(1)} %chip_sum.3.__._), channel_id=1, source_target_pairs={{0,8},{1,17},{2,10},{3,19},{4,12},{5,21},{6,14},{7,23},{8,0},{9,25... | collective-permute-start | bytes 786440 | tf_op jit(solution)/shard_map/ppermute | solution.py:485
  20.7 7.9 %collective-permute-start.8 = (bf16[2,256,256]{2,1,0:T(8,128)(2,1)S(1)}, bf16[2,256,256]{2,1,0:T(8,128)(2,1)S(1)}, u32[]{:S(2)}, u32[]{:S(2)}) collective-permute-start(bf16[2,256,256]{2,1,0:T(8,128)(2,1)S(1)} %chip_sum.2._), channel_id=1, source_target_pairs={{0,8},{1,17},{2,10},{3,19},{4,12},{5,21},{6,14},{7,23},{8,0},{9,25... | collective-permute-start | bytes 786440 | tf_op jit(solution)/shard_map/ppermute | solution.py:485
  21.7 3.3 %collective-permute-start.7 = (bf16[2,256,512]{2,1,0:T(8,128)(2,1)S(1)}, bf16[2,256,512]{2,1,0:T(8,128)(2,1)S(1)}, u32[]{:S(2)}, u32[]{:S(2)}) collective-permute-start(bf16[2,256,512]{2,1,0:T(8,128)(2,1)S(1)} %get-tuple-element.86), channel_id=1, source_target_pairs={{0,1},{1,0},{2,3},{3,2},{4,5},{5,4},{6,7},{7,6},{8,9},{9,8},{10,11... | collective-permute-start | bytes 1572872 | tf_op jit(solution)/shard_map/ppermute | solution.py:495
  22.8 5.7 %collective-permute-start.6 = (bf16[36,1024]{1,0:T(8,128)(2,1)S(1)}, bf16[36,1024]{1,0:T(8,128)(2,1)S(1)}, u32[]{:S(2)}, u32[]{:S(2)}) collective-permute-start(bf16[36,1024]{1,0:T(8,128)(2,1)S(1)} %pack_lon.1), channel_id=1, source_target_pairs={{7,0},{0,1},{1,2},{2,3},{3,4},{4,5},{5,6},{6,7},{15,8},{8,9},{9,10... | collective-permute-start | bytes 221192 | tf_op jit(solution)/shard_map/ppermute | solution.py:502
  25.1 5.0 %collective-permute-start.11 = (bf16[1,256,256]{2,1,0:T(8,128)(2,1)S(1)}, bf16[1,256,256]{2,1,0:T(8,128)(2,1)S(1)}, u32[]{:S(2)}, u32[]{:S(2)}) collective-permute-start(bf16[1,256,256]{2,1,0:T(8,128)(2,1)S(1)} %get-tuple-element.90), channel_id=1, source_target_pairs={{0,16},{1,9},{2,18},{3,11},{4,20},{5,13},{6,22},{7,15},{8,24},{9,1... | collective-permute-start | bytes 393224 | tf_op jit(solution)/shard_map/ppermute | solution.py:485
  28.7 5.0 %collective-permute-start.9 = (bf16[1,256,256]{2,1,0:T(8,128)(2,1)S(1)}, bf16[1,256,256]{2,1,0:T(8,128)(2,1)S(1)}, u32[]{:S(2)}, u32[]{:S(2)}) collective-permute-start(bf16[1,256,256]{2,1,0:T(8,128)(2,1)S(1)} %get-tuple-element.88), channel_id=1, source_target_pairs={{0,16},{1,9},{2,18},{3,11},{4,20},{5,13},{6,22},{7,15},{8,24},{9,1... | collective-permute-start | bytes 393224 | tf_op jit(solution)/shard_map/ppermute | solution.py:485
  33.8 6.8 %collective-permute-start.14 = (bf16[64,512]{1,0:T(8,128)(2,1)S(1)}, bf16[64,512]{1,0:T(8,128)(2,1)S(1)}, u32[]{:S(2)}, u32[]{:S(2)}) collective-permute-start(bf16[64,512]{1,0:T(8,128)(2,1)S(1)} %get-tuple-element.98), channel_id=1, source_target_pairs={{0,6},{1,7},{2,4},{3,5},{4,2},{5,3},{6,0},{7,1},{8,14},{9,15},{10,... | collective-permute-start | bytes 196616 | tf_op jit(solution)/shard_map/ppermute | solution.py:522
  36.9 5.2 %collective-permute-start.15 = (bf16[64,512]{1,0:T(8,128)(2,1)S(1)}, bf16[64,512]{1,0:T(8,128)(2,1)S(1)}, u32[]{:S(2)}, u32[]{:S(2)}) collective-permute-start(bf16[64,512]{1,0:T(8,128)(2,1)S(1)} %get-tuple-element.99), channel_id=1, source_target_pairs={{0,4},{1,5},{2,6},{3,7},{4,0},{5,1},{6,2},{7,3},{8,12},{9,13},{10,... | collective-permute-start | bytes 196616 | tf_op jit(solution)/shard_map/ppermute | solution.py:522
  36.9 5.2 %collective-permute-start.16 = (bf16[64,512]{1,0:T(8,128)(2,1)S(1)}, bf16[64,512]{1,0:T(8,128)(2,1)S(1)}, u32[]{:S(2)}, u32[]{:S(2)}) collective-permute-start(bf16[64,512]{1,0:T(8,128)(2,1)S(1)} %get-tuple-element.91._), channel_id=1, source_target_pairs={{0,2},{1,3},{2,0},{3,1},{4,6},{5,7},{6,4},{7,5},{8,10},{9,11},{10,... | collective-permute-start | bytes 196616 | tf_op jit(solution)/shard_map/ppermute | solution.py:522
  38.4 7.3 %collective-permute-start.12 = (bf16[108,1024]{1,0:T(8,128)(2,1)S(1)}, bf16[108,1024]{1,0:T(8,128)(2,1)S(1)}, u32[]{:S(2)}, u32[]{:S(2)}) collective-permute-start(bf16[108,1024]{1,0:T(8,128)(2,1)S(1)} %get-tuple-element.92), channel_id=1, source_target_pairs={{24,0},{9,1},{26,2},{11,3},{28,4},{13,5},{30,6},{15,7},{0,8},{17,9... | collective-permute-start | bytes 663560 | tf_op jit(solution)/shard_map/ppermute | solution.py:530
  40.4 6.7 %collective-permute-start.13 = (bf16[36,1024]{1,0:T(8,128)(2,1)S(1)}, bf16[36,1024]{1,0:T(8,128)(2,1)S(1)}, u32[]{:S(2)}, u32[]{:S(2)}) collective-permute-start(bf16[36,1024]{1,0:T(8,128)(2,1)S(1)} %get-tuple-element.93), channel_id=1, source_target_pairs={{15,0},{24,1},{9,2},{26,3},{11,4},{28,5},{13,6},{30,7},{23,8},{0,9... | collective-permute-start | bytes 221192 | tf_op jit(solution)/shard_map/ppermute | solution.py:531
  42.2 7.1 %collective-permute-start.19 = (bf16[64,512]{1,0:T(8,128)(2,1)S(1)}, bf16[64,512]{1,0:T(8,128)(2,1)S(1)}, u32[]{:S(2)}, u32[]{:S(2)}) collective-permute-start(bf16[64,512]{1,0:T(8,128)(2,1)S(1)} %line_sum.1.refs_0_), channel_id=1, source_target_pairs={{0,24},{8,16},{16,8},{24,0},{1,25},{9,17},{17,9},{25,1},{2,26},{10... | collective-permute-start | bytes 196616 | tf_op jit(solution)/shard_map/ppermute | solution.py:534
  43.9 5.4 %collective-permute-start.18 = (bf16[64,512]{1,0:T(8,128)(2,1)S(1)}, bf16[64,512]{1,0:T(8,128)(2,1)S(1)}, u32[]{:S(2)}, u32[]{:S(2)}) collective-permute-start(bf16[64,512]{1,0:T(8,128)(2,1)S(1)} %line_sum.1.refs_0_), channel_id=1, source_target_pairs={{0,16},{8,24},{16,0},{24,8},{1,17},{9,25},{17,1},{25,9},{2,18},{10... | collective-permute-start | bytes 196616 | tf_op jit(solution)/shard_map/ppermute | solution.py:534
  44.8 5.0 %collective-permute-start.17 = (bf16[64,512]{1,0:T(8,128)(2,1)S(1)}, bf16[64,512]{1,0:T(8,128)(2,1)S(1)}, u32[]{:S(2)}, u32[]{:S(2)}) collective-permute-start(bf16[64,512]{1,0:T(8,128)(2,1)S(1)} %line_sum.1.refs_0_), channel_id=1, source_target_pairs={{0,8},{8,0},{16,24},{24,16},{1,9},{9,1},{17,25},{25,17},{2,10},{10... | collective-permute-start | bytes 196616 | tf_op jit(solution)/shard_map/ppermute | solution.py:534

commit v15 on v14

--- a/solution.py
+++ b/solution.py
@@ -169,7 +169,9 @@
         send_grad[slot // 2] = slot_product(slot, size, lat, 1 - core, [(left, right)])
 
 
-def outer_kernel(own, lon_in, lat_in, diag_in, qkv_weight, proj_weight, grad_so_far, send_a, send_b, *refs):
+def outer_kernel(own, lon_in, lat_in, diag_in, qkv_weight, proj_weight, grad_so_far, *refs):
+    count = len(chunk_widths(proj_weight.shape[0] * 4 // lax.axis_size("lat")))
+    sends, refs = refs[:count], refs[count:]
     last = picks(last_rows, HALF, QUARTER)
     both = jnp.concatenate(
         [
@@ -183,13 +185,18 @@
     lat, core, size = place()
     for slot in range(1, size, 2):
         total = grad_so_far[slot // 2] + slot_product(slot, size, lat, 1 - core, [(left, right)])
-        put_chunks((send_a, send_b), slot // 2, total)
+        put_chunks(sends, slot // 2, total)
+
+
+def chunk_widths(lanes):
+    return (lanes // 2, lanes // 4, lanes // 4) if lanes % 512 == 0 else (lanes // 2,) * 2
 
 
 def put_chunks(outs, slot, total):
-    width = outs[0].shape[2]
-    for chunk, out in enumerate(outs):
-        out[slot] = total[:, chunk * width : (chunk + 1) * width].astype(BF)
+    at = 0
+    for out in outs:
+        out[slot] = total[:, at : at + out.shape[2]].astype(BF)
+        at += out.shape[2]
 
 
 def place():
@@ -262,15 +269,14 @@
 
 
 def keep_kernel(*refs):
-    *windows, keep_a, keep_b = refs
-    windows = [windows[:2], windows[2:]]
+    windows, keeps = [refs[:2], refs[2:4]], refs[4:]
     lat, core, size = place()
     for slot in range(1, size, 2):
-        put_chunks((keep_a, keep_b), slot // 2, slot_product(slot, size, lat, core, windows))
-
-
-def rest_kernel(_, __, *refs):
-    *windows, send_rest, keep_rest = refs
+        put_chunks(keeps, slot // 2, slot_product(slot, size, lat, core, windows))
+
+
+def rest_kernel(count, *refs):
+    *windows, send_rest, keep_rest = refs[count:]
     windows = windows[:3], windows[3:]
     lat, core, size = place()
     for slot in range(0, size, 2):
@@ -341,22 +347,25 @@
     d_fields[...] = total[:, width:]
 
 
-def halve_kernel(chunk, _, *refs):
+def halve_kernel(first_lane, _, *refs):
     *parts, send, keep = refs
     width = send.shape[2]
 
     def lanes(part):
-        return slice(None) if part.shape[2] == width else slice(chunk * width, (chunk + 1) * width)
+        return slice(None) if part.shape[2] == width else slice(first_lane, first_lane + width)
 
     for slot in range(send.shape[0]):
         for out, source in ((send, 2 * slot + 1), (keep, 2 * slot)):
             out[slot] = sum(part[source, :, lanes(part)].astype(F32) for part in parts).astype(BF)
 
 
-def line_parts_kernel(count, *refs):
-    chunks, (keep, *sends) = (refs[:count], refs[count : 2 * count]), refs[2 * count :]
-    rows = keep.shape[0]
-    for step, out in enumerate((keep, *sends)):
+def line_parts_kernel(counts, *refs):
+    chunks = []
+    for count in counts:
+        chunks.append(refs[:count])
+        refs = refs[count:]
+    rows = refs[0].shape[0]
+    for step, out in enumerate(refs):
         at = slice(step * rows, (step + 1) * rows)
         totals = [sum(part[0, at].astype(F32) for part in parts) for parts in chunks]
         out[...] = jnp.concatenate(totals, axis=1).astype(out.dtype)
@@ -368,6 +377,10 @@
     for part in parts[1:]:
         total = total + part[...].astype(F32)
     out[...] = total.astype(out.dtype)
+
+
+def next_sum_kernel(_, *refs):
+    sum_kernel(*refs)
 
 
 def finish_kernel(_, *refs):
@@ -454,7 +467,8 @@
 
     split = (lat_size, width // 2, 4 * width // lat_size)
     halves = ((lat_size // 2, *split[1:]), BF)
-    chunk = ((lat_size // 2, split[1], split[2] // 2), BF)
+    widths = chunk_widths(split[2])
+    chunks = [((lat_size // 2, split[1], lanes), BF) for lanes in widths]
     per_window = [
         ((WIN, width), BF),
         ((WIN, width), BF),
@@ -467,14 +481,15 @@
         inner_kernel, [(halves[0], F32), *per_window], inner_own, *own_parts, inner_in, qkv_weight, proj_weight,
         name="inner", flops=10**9, scratch=scratch,
     )
-    send_a, send_b, *outer = call(
-        outer_kernel, [chunk, chunk, *per_window],
+    outer = call(
+        outer_kernel, [*chunks, *per_window],
         outer_own, lon_in, outer_in, diag_in, qkv_weight, proj_weight, grad_so_far,
         name="outer", flops=10**9, scratch=scratch,
     )
     sibling = [(j, j ^ 1) for j in range(lon_size)]
-    arrived = [lax.ppermute(send, "lon", sibling) for send in (send_a, send_b)]
-    keep = call(keep_kernel, [chunk, chunk], *inner[2:4], *outer[2:4], name="keep", flops=10**9)
+    first, outer = outer[: len(widths)], outer[len(widths) :]
+    arrived = [lax.ppermute(send, "lon", sibling) for send in first]
+    keep = call(keep_kernel, chunks, *inner[2:4], *outer[2:4], name="keep", flops=10**9)
 
     def halving(phase, send):
         route = [
@@ -485,12 +500,14 @@
         return lax.ppermute(send, both, route)
 
     bits = lat_size.bit_length() - 1
-    sends = [
-        call(sum_kernel, [chunk], mine, theirs, name="chip_sum")[0] for mine, theirs in zip(keep, arrived)
-    ]
+    sends = [keep[0]]
+    for part, mine, theirs in zip(chunks, keep, arrived):
+        sends += call(next_sum_kernel, [part], sends[-1], mine, theirs, name="chip_sum", unread=(0,))
+    sends = sends[1:]
     received = [halving(0, send) for send in sends]
     send_rest, keep_rest = call(
-        rest_kernel, [halves, halves], *sends, *inner[2:], *outer[2:], name="rest", unread=(0, 1), beside=True
+        functools.partial(rest_kernel, len(sends)), [halves, halves], *sends, *inner[2:], *outer[2:],
+        name="rest", unread=range(len(sends)), beside=True,
     )
     received_rest = lax.ppermute(send_rest, "lon", sibling)
     results = call(
@@ -504,19 +521,21 @@
     slots = lat_size // 2
     for phase in range(1, bits):
         slots //= 2
-        stay = ((slots, *chunk[0][1:]), BF)
-        for index, after in enumerate((lon_home, sends[1])):
+        after = sends[-1]
+        for index, lanes in enumerate(widths):
+            stay = ((slots, split[1], lanes), BF)
             send, keep = call(
-                functools.partial(halve_kernel, index), [stay, stay], after, *kept[index],
+                functools.partial(halve_kernel, sum(widths[:index])), [stay, stay], lon_home if index == len(widths) - 1 else after, *kept[index],
                 name=f"halve{slots}", unread=(0,),
             )
             kept[index] = [keep, halving(phase, send)]
+            after = send
 
     rows = width // lon_size
     share = ((rows, split[2]), BF)
     parts = call(
-        functools.partial(line_parts_kernel, len(kept[0])), [share] * (lon_size // 2), *kept[0], *kept[1],
-        name="line_parts",
+        functools.partial(line_parts_kernel, [len(parts) for parts in kept]), [share] * (lon_size // 2),
+        *sum(kept, []), name="line_parts",
     )
     arrived = [
         lax.ppermute(parts[step], "lon", [(j, j ^ (2 * step)) for j in range(lon_size)])

time: 50.8 us -> 51.4 us (1.012)
    ppermute x1, waiting for transfers between devices: 0.01 us -> 2.28 us  [per_device(): lat_home = lax.ppermute(lat_back, both, back(lat_route))]
    ppermute x1, starting transfers between devices: 1.98 us -> 0.11 us  [per_device(): lat_home = lax.ppermute(lat_back, both, back(lat_route))]
    ppermute x4 -> x6, starting transfers between devices: 5.35 us -> 7.14 us  [halving(): return lax.ppermute(send, both, route)]
    ppermute x4 -> x6, waiting for transfers between devices: 5.23 us -> 3.77 us  [halving(): return lax.ppermute(send, both, route)]
    ppermute x3, waiting for transfers between devices: 1.5 us -> 0.38 us  [per_device(): lax.ppermute(line_sum, 'lat', [(i, i ^ step) for i in range(lat_size)])]
    ppermute x3, waiting for transfers between devices: 1.71 us -> 2.65 us  [per_device(): lax.ppermute(parts[step], 'lon', [(j, j ^ 2 * step) for j in range(lon_si...]
    ppermute x1, waiting for transfers between devices: 0.81 us -> 0.01 us  [per_device(): diag_home = lax.ppermute(diag_back, both, back(diag_route))]
    ppermute x1, waiting for transfers between devices: 2.02 us -> 2.54 us  [per_device(): lon_home = lax.ppermute(lon_back, both, back(lon_route))]
  transfers between devices with their start and end apart: 20 -> 23, of which waited for: 10 -> 9; matrix products, arithmetic and copies ran while one was open for 0% -> 0% of each run, Pallas kernels for 16% -> 16%
where the time goes in v15:
time: 51.4 us; the launch traced here: 51.3 us
  starting transfers between devices  25.4 us (49%)
  waiting for transfers between devices  12.4 us (24%)
  Pallas kernels  11.7 us (23%)
  local copies, waits for them, and re-layouts  0.94 us (2%)
  between operations  0.84 us (2%)
    pallas_call x22, Pallas kernels, call(): pl.pallas_call(kernel, out_shape=shapes, in_specs=[anywhere if i in unrea...  11.7 us
    ppermute x6, starting transfers between devices, halving(): return lax.ppermute(send, both, route)  7.14 us
    ppermute x3, starting transfers between devices, per_device(): lax.ppermute(parts[step], 'lon', [(j, j ^ 2 * step) for j in range(lon_si...  4.45 us
    ppermute x1, starting transfers between devices, per_device(): inner_in = lax.ppermute(inner_lat, both, lat_route)  3.94 us
    ppermute x6, waiting for transfers between devices, halving(): return lax.ppermute(send, both, route)  3.77 us
    ppermute x3, starting transfers between devices, per_device(): lax.ppermute(line_sum, 'lat', [(i, i ^ step) for i in range(lat_size)])  3.55 us
    ppermute x3, waiting for transfers between devices, per_device(): lax.ppermute(parts[step], 'lon', [(j, j ^ 2 * step) for j in range(lon_si...  2.65 us
    ppermute x1, waiting for transfers between devices, per_device(): lon_home = lax.ppermute(lon_back, both, back(lon_route))  2.54 us
  transfers between devices with their start and end apart: 23, of which 9 were waited for; matrix products, arithmetic and copies ran while one was open for 0% of the time, Pallas kernels for 16%

profile of v15, /device:TPU:0, one launch (start us, length us, event | category | flops | bytes accessed | tf_op | source)
XLA Modules:
  0.0 51.3 jit_solution(12011796204311168344)
XLA Ops:
  0.7 0.1 order.1
  0.8 0.8 %copy-done.3 = bf16[2,6,24,512]{3,2,1,0:T(8,128)(2,1)S(1)} copy-done((bf16[2,6,24,512]{3,2,1,0:T(8,128)(2,1)S(1)}, bf16[2,6,24,512]{3,2,1,0:T(8,128)(2,1)}, u32[]{:S(2)}) %copy-start.3) | copy-done | bytes 294936
  1.6 0.1 copy-done.2
  1.7 0.4 pack.1
  2.1 3.9 %collective-permute-start = (bf16[72,1024]{1,0:T(8,128)(2,1)S(1)}, bf16[72,1024]{1,0:T(8,128)(2,1)S(1)}, u32[]{:S(2)}, u32[]{:S(2)}) collective-permute-start(bf16[72,1024]{1,0:T(8,128)(2,1)S(1)} %get-tuple-element.68), channel_id=1, source_target_pairs={{0,24},{1,9},{2,26},{3,11},{4,28},{5,13},{6,30},{7,15},{8,0},{9,17... | collective-permute-start | bytes 442376 | tf_op jit(solution)/shard_map/ppermute | solution.py:463
  6.0 1.8 %collective-permute-start.1 = (bf16[36,1024]{1,0:T(8,128)(2,1)S(1)}, bf16[36,1024]{1,0:T(8,128)(2,1)S(1)}, u32[]{:S(2)}, u32[]{:S(2)}) collective-permute-start(bf16[36,1024]{1,0:T(8,128)(2,1)S(1)} %get-tuple-element.59._), channel_id=1, source_target_pairs={{0,7},{1,0},{2,1},{3,2},{4,3},{5,4},{6,5},{7,6},{8,15},{9,8},{10,9... | collective-permute-start | bytes 221192 | tf_op jit(solution)/shard_map/ppermute | solution.py:464
  7.8 0.6 %pack_rest.1 = (bf16[36,1024]{1,0:T(8,128)(2,1)S(1)}, bf16[36,1024]{1,0:T(8,128)(2,1)S(1)}, f32[72,1024]{1,0:T(8,128)S(1)}, f32[72,1024]{1,0:T(8,128)S(1)}) custom-call(bf16[36,1024]{1,0:T(8,128)(2,1)S(1)} %get-tuple-element.59._, bf16[288,512]{1,0:T(8,128)(2,1)S(1)} %bitcast.6, bf16[288,512]{1,0:T(8,128)(2,1)S(1)} %bitcast.8, ...), custom_call_target="tpu_custom_call" | custom-call | flops 500000000 | bytes 1525248 | tf_op jit(solution)/shard_map/pack_rest/pallas_call | solution.py:409
  8.4 1.5 %collective-permute-start.2 = (bf16[36,1024]{1,0:T(8,128)(2,1)S(1)}, bf16[36,1024]{1,0:T(8,128)(2,1)S(1)}, u32[]{:S(2)}, u32[]{:S(2)}) collective-permute-start(bf16[36,1024]{1,0:T(8,128)(2,1)S(1)} %get-tuple-element.72), channel_id=1, source_target_pairs={{0,24},{1,9},{2,26},{3,11},{4,28},{5,13},{6,30},{7,15},{8,0},{9,17... | collective-permute-start | bytes 221192 | tf_op jit(solution)/shard_map/ppermute | solution.py:465
  9.9 1.6 %collective-permute-start.3 = (bf16[36,1024]{1,0:T(8,128)(2,1)S(1)}, bf16[36,1024]{1,0:T(8,128)(2,1)S(1)}, u32[]{:S(2)}, u32[]{:S(2)}) collective-permute-start(bf16[36,1024]{1,0:T(8,128)(2,1)S(1)} %get-tuple-element.73), channel_id=1, source_target_pairs={{0,15},{1,24},{2,9},{3,26},{4,11},{5,28},{6,13},{7,30},{8,23},{9,0... | collective-permute-start | bytes 221192 | tf_op jit(solution)/shard_map/ppermute | solution.py:466
  11.5 0.7 %own.1 = (f32[72,512]{1,0:T(8,128)S(1)}, f32[72,1536]{1,0:T(8,128)S(1)}, f32[72,512]{1,0:T(8,128)S(1)}) custom-call(f32[72,1024]{1,0:T(8,128)S(1)} %get-tuple-element.64.inner_own.own, bf16[512,1536]{1,0:T(8,128)(2,1)S(1)} %copy-done, bf16[512,512]{1,0:T(8,128)(2,1)S(1)} %copy-done.1), custom_call_target="tpu_custom_call" | custom-call | flops 500000000 | bytes 3129344 | tf_op jit(solution)/shard_map/own/pallas_call | solution.py:409
  12.2 2.1 %inner.1 = (f32[2,256,512]{2,1,0:T(8,128)S(1)}, bf16[144,512]{1,0:T(8,128)(2,1)S(1)}, bf16[144,512]{1,0:T(8,128)(2,1)S(1)}, bf16[2,256,144]{2,1,0:T(8,128)(2,1)S...) custom-call(f32[72,1024]{1,0:T(8,128)S(1)} %get-tuple-element.64.inner_own.own, ...), custom_call_target="tpu_custom_call" | custom-call | flops 1000000000 | bytes 5505024 | tf_op jit(solution)/shard_map/inner/pallas_call | solution.py:409
  14.4 2.3 %outer.1 = (bf16[2,256,256]{2,1,0:T(8,128)(2,1)S(1)}, bf16[2,256,128]{2,1,0:T(8,128)(2,1)S(1)}, bf16[2,256,128]{2,1,0:T(8,128)(2,1)S(1)}, bf16[144,512]{1,0:T(8,...) custom-call(f32[72,1024]{1,0:T(8,128)S(1)} %get-tuple-element.71.own, ...), custom_call_target="tpu_custom_call" | custom-call | flops 1000000000 | bytes 5365760 | tf_op jit(solution)/shard_map/outer/pallas_call | solution.py:409
  16.8 0.1 collective-permute-start.4
  16.9 0.4 collective-permute-start.5
  17.3 0.1 collective-permute-start.6
  17.4 0.4 keep.1
  17.8 0.5 %collective-permute-done.4.refs_1_ = bf16[2,256,256]{2,1,0:T(8,128)(2,1)S(1)} collective-permute-done((bf16[2,256,256]{2,1,0:T(8,128)(2,1)S(1)}, bf16[2,256,256]{2,1,0:T(8,128)(2,1)S(1)}, u32[]{:S(2)}, u32[]{:S(2)}) %collective-permute-start.4) | collective-permute-done | bytes 262176 | tf_op jit(solution)/shard_map/ppermute | solution.py:491
  18.4 0.1 chip_sum.3._.refs_0_
  18.4 2.2 %collective-permute-start.8 = (bf16[2,256,256]{2,1,0:T(8,128)(2,1)S(1)}, bf16[2,256,256]{2,1,0:T(8,128)(2,1)S(1)}, u32[]{:S(2)}, u32[]{:S(2)}) collective-permute-start(bf16[2,256,256]{2,1,0:T(8,128)(2,1)S(1)} %chip_sum.3._.refs_0_), channel_id=1, source_target_pairs={{0,8},{1,17},{2,10},{3,19},{4,12},{5,21},{6,14},{7,23},{8,0},{9,25... | collective-permute-start | bytes 786440 | tf_op jit(solution)/shard_map/ppermute | solution.py:500
  20.7 0.1 collective-permute-start.10
  20.8 2.0 %collective-permute-start.13 = (bf16[2,256,128]{2,1,0:T(8,128)(2,1)S(1)}, bf16[2,256,128]{2,1,0:T(8,128)(2,1)S(1)}, u32[]{:S(2)}, u32[]{:S(2)}) collective-permute-start(bf16[2,256,128]{2,1,0:T(8,128)(2,1)S(1)} %chip_sum.5.refs_2_._), channel_id=1, source_target_pairs={{0,8},{1,17},{2,10},{3,19},{4,12},{5,21},{6,14},{7,23},{8,0},{9,25... | collective-permute-start | bytes 393224 | tf_op jit(solution)/shard_map/ppermute | solution.py:500
  22.9 0.7 %rest.1 = (bf16[2,256,512]{2,1,0:T(8,128)(2,1)S(1)}, bf16[2,256,512]{2,1,0:T(8,128)(2,1)S(1)}) custom-call(bf16[2,256,256]{2,1,0:T(8,128)(2,1)S(1)} %chip_sum.3._.refs_0_, bf16[2,256,128]{2,1,0:T(8,128)(2,1)S(1)} %chip_sum.4._.refs_1_, bf16[2,256,128]{2,1,0:T(8,128)(2,1)S(1)} %chip_sum.5.refs_2_._, ...), custom_call_target="tpu_custom_call" | custom-call | tf_op jit(solution)/shard_map/rest/pallas_call | solution.py:409
  23.6 0.1 collective-permute-start.7
  23.6 0.9 %outputs.1 = (bf16[144,1024]{1,0:T(8,128)(2,1)S(1)}, bf16[144,1024]{1,0:T(8,128)(2,1)S(1)}) custom-call(bf16[2,256,512]{2,1,0:T(8,128)(2,1)S(1)} %get-tuple-element.85._.refs_0_, bf16[144,512]{1,0:T(8,128)(2,1)S(1)} %get-tuple-element.86.refs_0_, bf16[144,512]{1,0:T(8,128)(2,1)S(1)} %get-tuple-element.87.refs_1_, ...), custom_call_target="tpu_custom_call" | custom-call | flops 10000000000 | bytes 4980736 | tf_op jit(solution)/shard_map/outputs/pallas_call | solution.py:409
  24.6 0.1 pack_lon.1
  24.7 0.5 %collective-permute-start.12 = (bf16[36,1024]{1,0:T(8,128)(2,1)S(1)}, bf16[36,1024]{1,0:T(8,128)(2,1)S(1)}, u32[]{:S(2)}, u32[]{:S(2)}) collective-permute-start(bf16[36,1024]{1,0:T(8,128)(2,1)S(1)} %pack_lon.1), channel_id=1, source_target_pairs={{7,0},{0,1},{1,2},{2,3},{3,4},{4,5},{5,6},{6,7},{15,8},{8,9},{9,10... | collective-permute-start | bytes 221192 | tf_op jit(solution)/shard_map/ppermute | solution.py:519
  25.3 0.3 collective-permute-done.7.refs_1_
  25.5 0.1 halve1.3
  25.6 0.9 %collective-permute-start.9 = (bf16[1,256,256]{2,1,0:T(8,128)(2,1)S(1)}, bf16[1,256,256]{2,1,0:T(8,128)(2,1)S(1)}, u32[]{:S(2)}, u32[]{:S(2)}) collective-permute-start(bf16[1,256,256]{2,1,0:T(8,128)(2,1)S(1)} %get-tuple-element.94._), channel_id=1, source_target_pairs={{0,16},{1,9},{2,18},{3,11},{4,20},{5,13},{6,22},{7,15},{8,24},{9,1... | collective-permute-start | bytes 393224 | tf_op jit(solution)/shard_map/ppermute | solution.py:500
  26.6 1.3 %collective-permute-start.11 = (bf16[1,256,128]{2,1,0:T(8,128)(2,1)S(1)}, bf16[1,256,128]{2,1,0:T(8,128)(2,1)S(1)}, u32[]{:S(2)}, u32[]{:S(2)}) collective-permute-start(bf16[1,256,128]{2,1,0:T(8,128)(2,1)S(1)} %get-tuple-element.96), channel_id=1, source_target_pairs={{0,16},{1,9},{2,18},{3,11},{4,20},{5,13},{6,22},{7,15},{8,24},{9,1... | collective-permute-start | bytes 196616 | tf_op jit(solution)/shard_map/ppermute | solution.py:500
  27.9 2.5 %collective-permute-done.12._.lon_in = bf16[36,1024]{1,0:T(8,128)(2,1)S(1)} collective-permute-done((bf16[36,1024]{1,0:T(8,128)(2,1)S(1)}, bf16[36,1024]{1,0:T(8,128)(2,1)S(1)}, u32[]{:S(2)}, u32[]{:S(2)}) %collective-permute-start.12) | collective-permute-done | bytes 73760 | tf_op jit(solution)/shard_map/ppermute | solution.py:519
  30.5 0.6 %collective-permute-start.14 = (bf16[1,256,128]{2,1,0:T(8,128)(2,1)S(1)}, bf16[1,256,128]{2,1,0:T(8,128)(2,1)S(1)}, u32[]{:S(2)}, u32[]{:S(2)}) collective-permute-start(bf16[1,256,128]{2,1,0:T(8,128)(2,1)S(1)} %get-tuple-element.98), channel_id=1, source_target_pairs={{0,16},{1,9},{2,18},{3,11},{4,20},{5,13},{6,22},{7,15},{8,24},{9,1... | collective-permute-start | bytes 196616 | tf_op jit(solution)/shard_map/ppermute | solution.py:500
  31.1 0.3 collective-permute-done.11.refs_3_
  31.4 3.5 %collective-permute-done.14.refs_5_ = bf16[1,256,128]{2,1,0:T(8,128)(2,1)S(1)} collective-permute-done((bf16[1,256,128]{2,1,0:T(8,128)(2,1)S(1)}, bf16[1,256,128]{2,1,0:T(8,128)(2,1)S(1)}, u32[]{:S(2)}, u32[]{:S(2)}) %collective-permute-start.14) | collective-permute-done | bytes 65568 | tf_op jit(solution)/shard_map/ppermute | solution.py:500
  34.9 0.9 %collective-permute-start.17 = (bf16[64,512]{1,0:T(8,128)(2,1)S(1)}, bf16[64,512]{1,0:T(8,128)(2,1)S(1)}, u32[]{:S(2)}, u32[]{:S(2)}) collective-permute-start(bf16[64,512]{1,0:T(8,128)(2,1)S(1)} %get-tuple-element.106), channel_id=1, source_target_pairs={{0,6},{1,7},{2,4},{3,5},{4,2},{5,3},{6,0},{7,1},{8,14},{9,15},{10,... | collective-permute-start | bytes 196616 | tf_op jit(solution)/shard_map/ppermute | solution.py:541
  35.8 3.6 %collective-permute-start.19 = (bf16[64,512]{1,0:T(8,128)(2,1)S(1)}, bf16[64,512]{1,0:T(8,128)(2,1)S(1)}, u32[]{:S(2)}, u32[]{:S(2)}) collective-permute-start(bf16[64,512]{1,0:T(8,128)(2,1)S(1)} %get-tuple-element.99._), channel_id=1, source_target_pairs={{0,2},{1,3},{2,0},{3,1},{4,6},{5,7},{6,4},{7,5},{8,10},{9,11},{10,... | collective-permute-start | bytes 196616 | tf_op jit(solution)/shard_map/ppermute | solution.py:541
  39.3 0.2 pack_back.1
  39.5 0.1 collective-permute-start.15
  39.7 1.5 %collective-permute-done.17.refs_1_ = bf16[64,512]{1,0:T(8,128)(2,1)S(1)} collective-permute-done((bf16[64,512]{1,0:T(8,128)(2,1)S(1)}, bf16[64,512]{1,0:T(8,128)(2,1)S(1)}, u32[]{:S(2)}, u32[]{:S(2)}) %collective-permute-start.17) | collective-permute-done | bytes 65568 | tf_op jit(solution)/shard_map/ppermute | solution.py:541
  41.1 1.2 %collective-permute-done.18.refs_2_ = bf16[64,512]{1,0:T(8,128)(2,1)S(1)} collective-permute-done((bf16[64,512]{1,0:T(8,128)(2,1)S(1)}, bf16[64,512]{1,0:T(8,128)(2,1)S(1)}, u32[]{:S(2)}, u32[]{:S(2)}) %collective-permute-start.18) | collective-permute-done | bytes 65568 | tf_op jit(solution)/shard_map/ppermute | solution.py:541
  42.4 1.0 %collective-permute-start.22 = (bf16[64,512]{1,0:T(8,128)(2,1)S(1)}, bf16[64,512]{1,0:T(8,128)(2,1)S(1)}, u32[]{:S(2)}, u32[]{:S(2)}) collective-permute-start(bf16[64,512]{1,0:T(8,128)(2,1)S(1)} %line_sum.1.refs_0_), channel_id=1, source_target_pairs={{0,24},{8,16},{16,8},{24,0},{1,25},{9,17},{17,9},{25,1},{2,26},{10... | collective-permute-start | bytes 196616 | tf_op jit(solution)/shard_map/ppermute | solution.py:553
  43.4 0.7 %collective-permute-start.21 = (bf16[64,512]{1,0:T(8,128)(2,1)S(1)}, bf16[64,512]{1,0:T(8,128)(2,1)S(1)}, u32[]{:S(2)}, u32[]{:S(2)}) collective-permute-start(bf16[64,512]{1,0:T(8,128)(2,1)S(1)} %line_sum.1.refs_0_), channel_id=1, source_target_pairs={{0,16},{8,24},{16,0},{24,8},{1,17},{9,25},{17,1},{25,9},{2,18},{10... | collective-permute-start | bytes 196616 | tf_op jit(solution)/shard_map/ppermute | solution.py:553
  44.1 1.9 %collective-permute-start.20 = (bf16[64,512]{1,0:T(8,128)(2,1)S(1)}, bf16[64,512]{1,0:T(8,128)(2,1)S(1)}, u32[]{:S(2)}, u32[]{:S(2)}) collective-permute-start(bf16[64,512]{1,0:T(8,128)(2,1)S(1)} %line_sum.1.refs_0_), channel_id=1, source_target_pairs={{0,8},{8,0},{16,24},{24,16},{1,9},{9,1},{17,25},{25,17},{2,10},{10... | collective-permute-start | bytes 196616 | tf_op jit(solution)/shard_map/ppermute | solution.py:553
  45.9 2.3 %collective-permute-done.15.lat_in = bf16[108,1024]{1,0:T(8,128)(2,1)S(1)} collective-permute-done((bf16[108,1024]{1,0:T(8,128)(2,1)S(1)}, bf16[108,1024]{1,0:T(8,128)(2,1)S(1)}, u32[]{:S(2)}, u32[]{:S(2)}) %collective-permute-start.15) | collective-permute-done | bytes 221216 | tf_op jit(solution)/shard_map/ppermute | solution.py:549
  48.2 0.6 %place.1.placed = f32[288,1024]{1,0:T(8,128)S(1)} custom-call(bf16[144,1024]{1,0:T(8,128)(2,1)S(1)} %get-tuple-element.90.inner_results, bf16[144,1024]{1,0:T(8,128)(2,1)S(1)} %get-tuple-element.91.outer_results, bf16[108,1024]{1,0:T(8,128)(2,1)S(1)} %collective-permute-done.15.lat_in), custom_call_target="tpu_custom_call" | custom-call | bytes 1990656 | tf_op jit(solution)/shard_map/place/pallas_call | solution.py:409
  48.8 1.2 %place_rest.1 = (bf16[288,512]{1,0:T(8,128)(2,1)}, bf16[288,512]{1,0:T(8,128)(2,1)}, f32[8,128]{1,0:T(8,128)S(1)}) custom-call(f32[288,1024]{1,0:T(8,128)S(1)} %place.1.placed, bf16[36,1024]{1,0:T(8,128)(2,1)S(1)} %collective-permute-done.12._.lon_in, bf16[36,1024]{1,0:T(8,128)(2,1)S(1)} %collective-permute-done.16.diag_in), custom_call_target="tpu_custom_call" | custom-call | bytes 1921024 | tf_op jit(solution)/shard_map/place_rest/pallas_call | solution.py:409
  50.0 0.4 collective-permute-done.22.refs_3_
  50.4 0.9 %finish.1 = (f32[64,1536]{1,0:T(8,128)}, f32[64,512]{1,0:T(8,128)}) custom-call(f32[8,128]{1,0:T(8,128)S(1)} %get-tuple-element.104._, bf16[64,512]{1,0:T(8,128)(2,1)S(1)} %line_sum.1.refs_0_, bf16[64,512]{1,0:T(8,128)(2,1)S(1)} %collective-permute-done.20.refs_1_, bf16[64,512]{1,0:T(8,128)(2,1)S(1)} %collective-permute-done.21.refs_2_, ...), custom_call_target="tpu_custom_call" | custom-call | bytes 790528 | tf_op jit(solution)/shard_map/finish/pallas_call | solution.py:409
  (28 shorter events, 0.3 us)
Async XLA Ops:
  0.6 1.0 %copy-start.3 = (bf16[2,6,24,512]{3,2,1,0:T(8,128)(2,1)S(1)}, bf16[2,6,24,512]{3,2,1,0:T(8,128)(2,1)}, u32[]{:S(2)}) copy-start(bf16[2,6,24,512]{3,2,1,0:T(8,128)(2,1)} %param.5) | copy-start | bytes 884740
  0.6 1.0 %copy-start.2 = (bf16[2,6,24,512]{3,2,1,0:T(8,128)(2,1)S(1)}, bf16[2,6,24,512]{3,2,1,0:T(8,128)(2,1)}, u32[]{:S(2)}) copy-start(bf16[2,6,24,512]{3,2,1,0:T(8,128)(2,1)} %param.4) | copy-start | bytes 884740
  1.7 9.8 %copy-start.1 = (bf16[512,512]{1,0:T(8,128)(2,1)S(1)}, bf16[512,512]{1,0:T(8,128)(2,1)}, u32[]{:S(2)}) copy-start(bf16[512,512]{1,0:T(8,128)(2,1)} %refs_7_.1) | copy-start | bytes 1572868
  2.0 9.5 %copy-start = (bf16[512,1536]{1,0:T(8,128)(2,1)S(1)}, bf16[512,1536]{1,0:T(8,128)(2,1)}, u32[]{:S(2)}) copy-start(bf16[512,1536]{1,0:T(8,128)(2,1)} %refs_6_.1) | copy-start | bytes 4718596
  2.1 10.2 %collective-permute-start = (bf16[72,1024]{1,0:T(8,128)(2,1)S(1)}, bf16[72,1024]{1,0:T(8,128)(2,1)S(1)}, u32[]{:S(2)}, u32[]{:S(2)}) collective-permute-start(bf16[72,1024]{1,0:T(8,128)(2,1)S(1)} %get-tuple-element.68), channel_id=1, source_target_pairs={{0,24},{1,9},{2,26},{3,11},{4,28},{5,13},{6,30},{7,15},{8,0},{9,17... | collective-permute-start | bytes 442376 | tf_op jit(solution)/shard_map/ppermute | solution.py:463
  6.0 8.4 %collective-permute-start.1 = (bf16[36,1024]{1,0:T(8,128)(2,1)S(1)}, bf16[36,1024]{1,0:T(8,128)(2,1)S(1)}, u32[]{:S(2)}, u32[]{:S(2)}) collective-permute-start(bf16[36,1024]{1,0:T(8,128)(2,1)S(1)} %get-tuple-element.59._), channel_id=1, source_target_pairs={{0,7},{1,0},{2,1},{3,2},{4,3},{5,4},{6,5},{7,6},{8,15},{9,8},{10,9... | collective-permute-start | bytes 221192 | tf_op jit(solution)/shard_map/ppermute | solution.py:464
  8.4 5.9 %collective-permute-start.2 = (bf16[36,1024]{1,0:T(8,128)(2,1)S(1)}, bf16[36,1024]{1,0:T(8,128)(2,1)S(1)}, u32[]{:S(2)}, u32[]{:S(2)}) collective-permute-start(bf16[36,1024]{1,0:T(8,128)(2,1)S(1)} %get-tuple-element.72), channel_id=1, source_target_pairs={{0,24},{1,9},{2,26},{3,11},{4,28},{5,13},{6,30},{7,15},{8,0},{9,17... | collective-permute-start | bytes 221192 | tf_op jit(solution)/shard_map/ppermute | solution.py:465
  9.9 4.5 %collective-permute-start.3 = (bf16[36,1024]{1,0:T(8,128)(2,1)S(1)}, bf16[36,1024]{1,0:T(8,128)(2,1)S(1)}, u32[]{:S(2)}, u32[]{:S(2)}) collective-permute-start(bf16[36,1024]{1,0:T(8,128)(2,1)S(1)} %get-tuple-element.73), channel_id=1, source_target_pairs={{0,15},{1,24},{2,9},{3,26},{4,11},{5,28},{6,13},{7,30},{8,23},{9,0... | collective-permute-start | bytes 221192 | tf_op jit(solution)/shard_map/ppermute | solution.py:466
  16.8 1.6 %collective-permute-start.4 = (bf16[2,256,256]{2,1,0:T(8,128)(2,1)S(1)}, bf16[2,256,256]{2,1,0:T(8,128)(2,1)S(1)}, u32[]{:S(2)}, u32[]{:S(2)}) collective-permute-start(bf16[2,256,256]{2,1,0:T(8,128)(2,1)S(1)} %get-tuple-element.78), channel_id=1, source_target_pairs={{0,1},{1,0},{2,3},{3,2},{4,5},{5,4},{6,7},{7,6},{8,9},{9,8},{10,11... | collective-permute-start | bytes 786440 | tf_op jit(solution)/shard_map/ppermute | solution.py:491
  16.9 3.7 %collective-permute-start.5 = (bf16[2,256,128]{2,1,0:T(8,128)(2,1)S(1)}, bf16[2,256,128]{2,1,0:T(8,128)(2,1)S(1)}, u32[]{:S(2)}, u32[]{:S(2)}) collective-permute-start(bf16[2,256,128]{2,1,0:T(8,128)(2,1)S(1)} %get-tuple-element.80), channel_id=1, source_target_pairs={{0,1},{1,0},{2,3},{3,2},{4,5},{5,4},{6,7},{7,6},{8,9},{9,8},{10,11... | collective-permute-start | bytes 393224 | tf_op jit(solution)/shard_map/ppermute | solution.py:491
  17.3 3.5 %collective-permute-start.6 = (bf16[2,256,128]{2,1,0:T(8,128)(2,1)S(1)}, bf16[2,256,128]{2,1,0:T(8,128)(2,1)S(1)}, u32[]{:S(2)}, u32[]{:S(2)}) collective-permute-start(bf16[2,256,128]{2,1,0:T(8,128)(2,1)S(1)} %get-tuple-element.82), channel_id=1, source_target_pairs={{0,1},{1,0},{2,3},{3,2},{4,5},{5,4},{6,7},{7,6},{8,9},{9,8},{10,11... | collective-permute-start | bytes 393224 | tf_op jit(solution)/shard_map/ppermute | solution.py:491
  18.4 6.8 %collective-permute-start.8 = (bf16[2,256,256]{2,1,0:T(8,128)(2,1)S(1)}, bf16[2,256,256]{2,1,0:T(8,128)(2,1)S(1)}, u32[]{:S(2)}, u32[]{:S(2)}) collective-permute-start(bf16[2,256,256]{2,1,0:T(8,128)(2,1)S(1)} %chip_sum.3._.refs_0_), channel_id=1, source_target_pairs={{0,8},{1,17},{2,10},{3,19},{4,12},{5,21},{6,14},{7,23},{8,0},{9,25... | collective-permute-start | bytes 786440 | tf_op jit(solution)/shard_map/ppermute | solution.py:500
  20.7 5.9 %collective-permute-start.10 = (bf16[2,256,128]{2,1,0:T(8,128)(2,1)S(1)}, bf16[2,256,128]{2,1,0:T(8,128)(2,1)S(1)}, u32[]{:S(2)}, u32[]{:S(2)}) collective-permute-start(bf16[2,256,128]{2,1,0:T(8,128)(2,1)S(1)} %chip_sum.4._.refs_1_), channel_id=1, source_target_pairs={{0,8},{1,17},{2,10},{3,19},{4,12},{5,21},{6,14},{7,23},{8,0},{9,25... | collective-permute-start | bytes 393224 | tf_op jit(solution)/shard_map/ppermute | solution.py:500
  20.8 9.6 %collective-permute-start.13 = (bf16[2,256,128]{2,1,0:T(8,128)(2,1)S(1)}, bf16[2,256,128]{2,1,0:T(8,128)(2,1)S(1)}, u32[]{:S(2)}, u32[]{:S(2)}) collective-permute-start(bf16[2,256,128]{2,1,0:T(8,128)(2,1)S(1)} %chip_sum.5.refs_2_._), channel_id=1, source_target_pairs={{0,8},{1,17},{2,10},{3,19},{4,12},{5,21},{6,14},{7,23},{8,0},{9,25... | collective-permute-start | bytes 393224 | tf_op jit(solution)/shard_map/ppermute | solution.py:500
  23.6 2.0 %collective-permute-start.7 = (bf16[2,256,512]{2,1,0:T(8,128)(2,1)S(1)}, bf16[2,256,512]{2,1,0:T(8,128)(2,1)S(1)}, u32[]{:S(2)}, u32[]{:S(2)}) collective-permute-start(bf16[2,256,512]{2,1,0:T(8,128)(2,1)S(1)} %get-tuple-element.92), channel_id=1, source_target_pairs={{0,1},{1,0},{2,3},{3,2},{4,5},{5,4},{6,7},{7,6},{8,9},{9,8},{10,11... | collective-permute-start | bytes 1572872 | tf_op jit(solution)/shard_map/ppermute | solution.py:512
  24.7 5.7 %collective-permute-start.12 = (bf16[36,1024]{1,0:T(8,128)(2,1)S(1)}, bf16[36,1024]{1,0:T(8,128)(2,1)S(1)}, u32[]{:S(2)}, u32[]{:S(2)}) collective-permute-start(bf16[36,1024]{1,0:T(8,128)(2,1)S(1)} %pack_lon.1), channel_id=1, source_target_pairs={{7,0},{0,1},{1,2},{2,3},{3,4},{4,5},{5,6},{6,7},{15,8},{8,9},{9,10... | collective-permute-start | bytes 221192 | tf_op jit(solution)/shard_map/ppermute | solution.py:519
  25.6 9.2 %collective-permute-start.9 = (bf16[1,256,256]{2,1,0:T(8,128)(2,1)S(1)}, bf16[1,256,256]{2,1,0:T(8,128)(2,1)S(1)}, u32[]{:S(2)}, u32[]{:S(2)}) collective-permute-start(bf16[1,256,256]{2,1,0:T(8,128)(2,1)S(1)} %get-tuple-element.94._), channel_id=1, source_target_pairs={{0,16},{1,9},{2,18},{3,11},{4,20},{5,13},{6,22},{7,15},{8,24},{9,1... | collective-permute-start | bytes 393224 | tf_op jit(solution)/shard_map/ppermute | solution.py:500
  26.6 4.8 %collective-permute-start.11 = (bf16[1,256,128]{2,1,0:T(8,128)(2,1)S(1)}, bf16[1,256,128]{2,1,0:T(8,128)(2,1)S(1)}, u32[]{:S(2)}, u32[]{:S(2)}) collective-permute-start(bf16[1,256,128]{2,1,0:T(8,128)(2,1)S(1)} %get-tuple-element.96), channel_id=1, source_target_pairs={{0,16},{1,9},{2,18},{3,11},{4,20},{5,13},{6,22},{7,15},{8,24},{9,1... | collective-permute-start | bytes 196616 | tf_op jit(solution)/shard_map/ppermute | solution.py:500
  30.5 4.3 %collective-permute-start.14 = (bf16[1,256,128]{2,1,0:T(8,128)(2,1)S(1)}, bf16[1,256,128]{2,1,0:T(8,128)(2,1)S(1)}, u32[]{:S(2)}, u32[]{:S(2)}) collective-permute-start(bf16[1,256,128]{2,1,0:T(8,128)(2,1)S(1)} %get-tuple-element.98), channel_id=1, source_target_pairs={{0,16},{1,9},{2,18},{3,11},{4,20},{5,13},{6,22},{7,15},{8,24},{9,1... | collective-permute-start | bytes 196616 | tf_op jit(solution)/shard_map/ppermute | solution.py:500
  34.9 6.3 %collective-permute-start.17 = (bf16[64,512]{1,0:T(8,128)(2,1)S(1)}, bf16[64,512]{1,0:T(8,128)(2,1)S(1)}, u32[]{:S(2)}, u32[]{:S(2)}) collective-permute-start(bf16[64,512]{1,0:T(8,128)(2,1)S(1)} %get-tuple-element.106), channel_id=1, source_target_pairs={{0,6},{1,7},{2,4},{3,5},{4,2},{5,3},{6,0},{7,1},{8,14},{9,15},{10,... | collective-permute-start | bytes 196616 | tf_op jit(solution)/shard_map/ppermute | solution.py:541
  35.7 6.6 %collective-permute-start.18 = (bf16[64,512]{1,0:T(8,128)(2,1)S(1)}, bf16[64,512]{1,0:T(8,128)(2,1)S(1)}, u32[]{:S(2)}, u32[]{:S(2)}) collective-permute-start(bf16[64,512]{1,0:T(8,128)(2,1)S(1)} %get-tuple-element.107), channel_id=1, source_target_pairs={{0,4},{1,5},{2,6},{3,7},{4,0},{5,1},{6,2},{7,3},{8,12},{9,13},{10,... | collective-permute-start | bytes 196616 | tf_op jit(solution)/shard_map/ppermute | solution.py:541
  35.8 6.6 %collective-permute-start.19 = (bf16[64,512]{1,0:T(8,128)(2,1)S(1)}, bf16[64,512]{1,0:T(8,128)(2,1)S(1)}, u32[]{:S(2)}, u32[]{:S(2)}) collective-permute-start(bf16[64,512]{1,0:T(8,128)(2,1)S(1)} %get-tuple-element.99._), channel_id=1, source_target_pairs={{0,2},{1,3},{2,0},{3,1},{4,6},{5,7},{6,4},{7,5},{8,10},{9,11},{10,... | collective-permute-start | bytes 196616 | tf_op jit(solution)/shard_map/ppermute | solution.py:541
  39.5 8.7 %collective-permute-start.15 = (bf16[108,1024]{1,0:T(8,128)(2,1)S(1)}, bf16[108,1024]{1,0:T(8,128)(2,1)S(1)}, u32[]{:S(2)}, u32[]{:S(2)}) collective-permute-start(bf16[108,1024]{1,0:T(8,128)(2,1)S(1)} %get-tuple-element.100), channel_id=1, source_target_pairs={{24,0},{9,1},{26,2},{11,3},{28,4},{13,5},{30,6},{15,7},{0,8},{17,9... | collective-permute-start | bytes 663560 | tf_op jit(solution)/shard_map/ppermute | solution.py:549
  39.7 9.2 %collective-permute-start.16 = (bf16[36,1024]{1,0:T(8,128)(2,1)S(1)}, bf16[36,1024]{1,0:T(8,128)(2,1)S(1)}, u32[]{:S(2)}, u32[]{:S(2)}) collective-permute-start(bf16[36,1024]{1,0:T(8,128)(2,1)S(1)} %get-tuple-element.101), channel_id=1, source_target_pairs={{15,0},{24,1},{9,2},{26,3},{11,4},{28,5},{13,6},{30,7},{23,8},{0,9... | collective-permute-start | bytes 221192 | tf_op jit(solution)/shard_map/ppermute | solution.py:550
  42.4 8.0 %collective-permute-start.22 = (bf16[64,512]{1,0:T(8,128)(2,1)S(1)}, bf16[64,512]{1,0:T(8,128)(2,1)S(1)}, u32[]{:S(2)}, u32[]{:S(2)}) collective-permute-start(bf16[64,512]{1,0:T(8,128)(2,1)S(1)} %line_sum.1.refs_0_), channel_id=1, source_target_pairs={{0,24},{8,16},{16,8},{24,0},{1,25},{9,17},{17,9},{25,1},{2,26},{10... | collective-permute-start | bytes 196616 | tf_op jit(solution)/shard_map/ppermute | solution.py:553
  43.4 7.0 %collective-permute-start.21 = (bf16[64,512]{1,0:T(8,128)(2,1)S(1)}, bf16[64,512]{1,0:T(8,128)(2,1)S(1)}, u32[]{:S(2)}, u32[]{:S(2)}) collective-permute-start(bf16[64,512]{1,0:T(8,128)(2,1)S(1)} %line_sum.1.refs_0_), channel_id=1, source_target_pairs={{0,16},{8,24},{16,0},{24,8},{1,17},{9,25},{17,1},{25,9},{2,18},{10... | collective-permute-start | bytes 196616 | tf_op jit(solution)/shard_map/ppermute | solution.py:553
  44.1 6.3 %collective-permute-start.20 = (bf16[64,512]{1,0:T(8,128)(2,1)S(1)}, bf16[64,512]{1,0:T(8,128)(2,1)S(1)}, u32[]{:S(2)}, u32[]{:S(2)}) collective-permute-start(bf16[64,512]{1,0:T(8,128)(2,1)S(1)} %line_sum.1.refs_0_), channel_id=1, source_target_pairs={{0,8},{8,0},{16,24},{24,16},{1,9},{9,1},{17,25},{25,17},{2,10},{10... | collective-permute-start | bytes 196616 | tf_op jit(solution)/shard_map/ppermute | solution.py:553

commit v16 on v15

--- a/solution.py
+++ b/solution.py
@@ -21,8 +21,9 @@
 LANES = 128
 
 epsilon = 1e-05
-LONG = 13 * 10**8
+LONG = 8 * 10**8
 LOAD = 5 * 10**9
+LATER = 10**9
 BF = jnp.bfloat16
 F32 = jnp.float32
 
@@ -359,13 +360,13 @@
             out[slot] = sum(part[source, :, lanes(part)].astype(F32) for part in parts).astype(BF)
 
 
-def line_parts_kernel(counts, *refs):
-    chunks = []
+def line_parts_kernel(counts, first_step, after, *refs):
+    chunks, refs = [], refs[after:]
     for count in counts:
         chunks.append(refs[:count])
         refs = refs[count:]
     rows = refs[0].shape[0]
-    for step, out in enumerate(refs):
+    for step, out in enumerate(refs, first_step):
         at = slice(step * rows, (step + 1) * rows)
         totals = [sum(part[0, at].astype(F32) for part in parts) for parts in chunks]
         out[...] = jnp.concatenate(totals, axis=1).astype(out.dtype)
@@ -533,22 +534,30 @@
 
     rows = width // lon_size
     share = ((rows, split[2]), BF)
-    parts = call(
-        functools.partial(line_parts_kernel, [len(parts) for parts in kept]), [share] * (lon_size // 2),
-        *sum(kept, []), name="line_parts",
-    )
-    arrived = [
-        lax.ppermute(parts[step], "lon", [(j, j ^ (2 * step)) for j in range(lon_size)])
-        for step in range(lon_size // 2 - 1, 0, -1)
-    ]
+    counts, chips = [len(parts) for parts in kept], lon_size // 2
+
+    def line_parts(first, last, *after):
+        return call(
+            functools.partial(line_parts_kernel, counts, first, len(after)), [share] * (last - first),
+            *after, *sum(kept, []), name="line_parts", unread=range(len(after)),
+        )
+
+    def along(part, step):
+        return lax.ppermute(part, "lon", [(j, j ^ (2 * step)) for j in range(lon_size)])
+
+    (farthest,) = line_parts(chips - 1, chips)
+    arrived = [along(farthest, chips - 1)]
     lat_back, diag_back = call(
         pack_back_kernel, [((HALF + QUARTER, 2 * width), BF), quarter],
-        parts[1], *results,
+        farthest, *results,
         name="pack_back", unread=(0,),
     )
     lat_home = lax.ppermute(lat_back, both, back(lat_route))
     diag_home = lax.ppermute(diag_back, both, back(diag_route))
-    (line_sum,) = call(sum_kernel, [share], parts[0], *arrived, name="line_sum", flops=LONG)
+    parts = line_parts(0, chips - 1, lat_back)
+    arrived += [along(parts[step], step) for step in range(chips - 2, 0, -1)]
+    (far_sum,) = call(sum_kernel, [((rows, split[2]), F32)], parts[0], arrived[0], name="far_sum", flops=LATER)
+    (line_sum,) = call(sum_kernel, [share], far_sum, *arrived[1:], name="line_sum", flops=LONG)
     shared = [
         lax.ppermute(line_sum, "lat", [(i, i ^ step) for i in range(lat_size)]) for step in range(1, lat_size)
     ]

time: 51.4 us -> 51.4 us (level)
    ppermute x1, waiting for transfers between devices: 2.28 us -> 0.01 us  [per_device(): lat_home = lax.ppermute(lat_back, both, back(lat_route))]
    ppermute x3, waiting for transfers between devices: 0.38 us -> 2.13 us  [per_device(): lax.ppermute(line_sum, 'lat', [(i, i ^ step) for i in range(lat_size)])]
    ppermute x1, starting transfers between devices: 0.11 us -> 0.99 us  [per_device(): lat_home = lax.ppermute(lat_back, both, back(lat_route))]
    ppermute x3, starting transfers between devices: 4.45 us -> 3.63 us  [along(): lax.ppermute(part, 'lon', [(j, j ^ 2 * step) for j in range(lon_size)])]
    pallas_call x22 -> x24, Pallas kernels: 11.7 us -> 11.7 us  [call(): pl.pallas_call(kernel, out_shape=shapes, in_specs=[anywhere if i in unrea...]
  transfers between devices with their start and end apart: 23 -> 23, of which waited for: 9 -> 10; matrix products, arithmetic and copies ran while one was open for 0% -> 0% of each run, Pallas kernels for 16% -> 16%
where the time goes in v16:
time: 51.4 us; the launch traced here: 51.2 us
  starting transfers between devices  25.4 us (49%)
  waiting for transfers between devices  12.4 us (24%)
  Pallas kernels  11.7 us (23%)
  local copies, waits for them, and re-layouts  0.94 us (2%)
  between operations  0.84 us (2%)
    pallas_call x24, Pallas kernels, call(): pl.pallas_call(kernel, out_shape=shapes, in_specs=[anywhere if i in unrea...  11.7 us
    ppermute x6, starting transfers between devices, halving(): return lax.ppermute(send, both, route)  7.14 us
    ppermute x1, starting transfers between devices, per_device(): inner_in = lax.ppermute(inner_lat, both, lat_route)  3.94 us
    ppermute x6, waiting for transfers between devices, halving(): return lax.ppermute(send, both, route)  3.77 us
    ppermute x3, starting transfers between devices, along(): lax.ppermute(part, 'lon', [(j, j ^ 2 * step) for j in range(lon_size)])  3.63 us
    ppermute x3, starting transfers between devices, per_device(): lax.ppermute(line_sum, 'lat', [(i, i ^ step) for i in range(lat_size)])  3.55 us
    ppermute x3, waiting for transfers between devices, along(): lax.ppermute(part, 'lon', [(j, j ^ 2 * step) for j in range(lon_size)])  3.12 us
    ppermute x1, waiting for transfers between devices, per_device(): lon_home = lax.ppermute(lon_back, both, back(lon_route))  2.54 us
  transfers between devices with their start and end apart: 23, of which 10 were waited for; matrix products, arithmetic and copies ran while one was open for 0% of the time, Pallas kernels for 16%

profile of v16, /device:TPU:0, one launch (start us, length us, event | category | flops | bytes accessed | tf_op | source)
XLA Modules:
  0.0 51.2 jit_solution(6861451403012804106)
XLA Ops:
  0.7 0.1 order.1
  0.8 0.8 %copy-done.3 = bf16[2,6,24,512]{3,2,1,0:T(8,128)(2,1)S(1)} copy-done((bf16[2,6,24,512]{3,2,1,0:T(8,128)(2,1)S(1)}, bf16[2,6,24,512]{3,2,1,0:T(8,128)(2,1)}, u32[]{:S(2)}) %copy-start.3) | copy-done | bytes 294936
  1.6 0.1 copy-done.2
  1.7 0.4 pack.1
  2.1 3.9 %collective-permute-start = (bf16[72,1024]{1,0:T(8,128)(2,1)S(1)}, bf16[72,1024]{1,0:T(8,128)(2,1)S(1)}, u32[]{:S(2)}, u32[]{:S(2)}) collective-permute-start(bf16[72,1024]{1,0:T(8,128)(2,1)S(1)} %get-tuple-element.67), channel_id=1, source_target_pairs={{0,24},{1,9},{2,26},{3,11},{4,28},{5,13},{6,30},{7,15},{8,0},{9,17... | collective-permute-start | bytes 442376 | tf_op jit(solution)/shard_map/ppermute | solution.py:464
  6.0 1.8 %collective-permute-start.1 = (bf16[36,1024]{1,0:T(8,128)(2,1)S(1)}, bf16[36,1024]{1,0:T(8,128)(2,1)S(1)}, u32[]{:S(2)}, u32[]{:S(2)}) collective-permute-start(bf16[36,1024]{1,0:T(8,128)(2,1)S(1)} %get-tuple-element.58._), channel_id=1, source_target_pairs={{0,7},{1,0},{2,1},{3,2},{4,3},{5,4},{6,5},{7,6},{8,15},{9,8},{10,9... | collective-permute-start | bytes 221192 | tf_op jit(solution)/shard_map/ppermute | solution.py:465
  7.8 0.6 %pack_rest.1 = (bf16[36,1024]{1,0:T(8,128)(2,1)S(1)}, bf16[36,1024]{1,0:T(8,128)(2,1)S(1)}, f32[72,1024]{1,0:T(8,128)S(1)}, f32[72,1024]{1,0:T(8,128)S(1)}) custom-call(bf16[36,1024]{1,0:T(8,128)(2,1)S(1)} %get-tuple-element.58._, bf16[288,512]{1,0:T(8,128)(2,1)S(1)} %bitcast.6, bf16[288,512]{1,0:T(8,128)(2,1)S(1)} %bitcast.8, ...), custom_call_target="tpu_custom_call" | custom-call | flops 500000000 | bytes 1525248 | tf_op jit(solution)/shard_map/pack_rest/pallas_call | solution.py:410
  8.4 1.5 %collective-permute-start.2 = (bf16[36,1024]{1,0:T(8,128)(2,1)S(1)}, bf16[36,1024]{1,0:T(8,128)(2,1)S(1)}, u32[]{:S(2)}, u32[]{:S(2)}) collective-permute-start(bf16[36,1024]{1,0:T(8,128)(2,1)S(1)} %get-tuple-element.71), channel_id=1, source_target_pairs={{0,24},{1,9},{2,26},{3,11},{4,28},{5,13},{6,30},{7,15},{8,0},{9,17... | collective-permute-start | bytes 221192 | tf_op jit(solution)/shard_map/ppermute | solution.py:466
  9.9 1.6 %collective-permute-start.3 = (bf16[36,1024]{1,0:T(8,128)(2,1)S(1)}, bf16[36,1024]{1,0:T(8,128)(2,1)S(1)}, u32[]{:S(2)}, u32[]{:S(2)}) collective-permute-start(bf16[36,1024]{1,0:T(8,128)(2,1)S(1)} %get-tuple-element.72), channel_id=1, source_target_pairs={{0,15},{1,24},{2,9},{3,26},{4,11},{5,28},{6,13},{7,30},{8,23},{9,0... | collective-permute-start | bytes 221192 | tf_op jit(solution)/shard_map/ppermute | solution.py:467
  11.5 0.7 %own.1 = (f32[72,512]{1,0:T(8,128)S(1)}, f32[72,1536]{1,0:T(8,128)S(1)}, f32[72,512]{1,0:T(8,128)S(1)}) custom-call(f32[72,1024]{1,0:T(8,128)S(1)} %get-tuple-element.63.inner_own.own, bf16[512,1536]{1,0:T(8,128)(2,1)S(1)} %copy-done, bf16[512,512]{1,0:T(8,128)(2,1)S(1)} %copy-done.1), custom_call_target="tpu_custom_call" | custom-call | flops 500000000 | bytes 3129344 | tf_op jit(solution)/shard_map/own/pallas_call | solution.py:410
  12.2 2.1 %inner.1 = (f32[2,256,512]{2,1,0:T(8,128)S(1)}, bf16[144,512]{1,0:T(8,128)(2,1)S(1)}, bf16[144,512]{1,0:T(8,128)(2,1)S(1)}, bf16[2,256,144]{2,1,0:T(8,128)(2,1)S...) custom-call(f32[72,1024]{1,0:T(8,128)S(1)} %get-tuple-element.63.inner_own.own, ...), custom_call_target="tpu_custom_call" | custom-call | flops 1000000000 | bytes 5505024 | tf_op jit(solution)/shard_map/inner/pallas_call | solution.py:410
  14.4 2.3 %outer.1 = (bf16[2,256,256]{2,1,0:T(8,128)(2,1)S(1)}, bf16[2,256,128]{2,1,0:T(8,128)(2,1)S(1)}, bf16[2,256,128]{2,1,0:T(8,128)(2,1)S(1)}, bf16[144,512]{1,0:T(8,...) custom-call(f32[72,1024]{1,0:T(8,128)S(1)} %get-tuple-element.70.own, ...), custom_call_target="tpu_custom_call" | custom-call | flops 1000000000 | bytes 5365760 | tf_op jit(solution)/shard_map/outer/pallas_call | solution.py:410
  16.8 0.1 collective-permute-start.4
  16.9 0.4 collective-permute-start.5
  17.3 0.1 collective-permute-start.6
  17.4 0.4 keep.1
  17.8 0.5 %collective-permute-done.4.refs_1_ = bf16[2,256,256]{2,1,0:T(8,128)(2,1)S(1)} collective-permute-done((bf16[2,256,256]{2,1,0:T(8,128)(2,1)S(1)}, bf16[2,256,256]{2,1,0:T(8,128)(2,1)S(1)}, u32[]{:S(2)}, u32[]{:S(2)}) %collective-permute-start.4) | collective-permute-done | bytes 262176 | tf_op jit(solution)/shard_map/ppermute | solution.py:492
  18.4 2.2 %collective-permute-start.8 = (bf16[2,256,256]{2,1,0:T(8,128)(2,1)S(1)}, bf16[2,256,256]{2,1,0:T(8,128)(2,1)S(1)}, u32[]{:S(2)}, u32[]{:S(2)}) collective-permute-start(bf16[2,256,256]{2,1,0:T(8,128)(2,1)S(1)} %chip_sum.3._.refs_0_), channel_id=1, source_target_pairs={{0,8},{1,17},{2,10},{3,19},{4,12},{5,21},{6,14},{7,23},{8,0},{9,25... | collective-permute-start | bytes 786440 | tf_op jit(solution)/shard_map/ppermute | solution.py:501
  20.7 0.1 collective-permute-start.10
  20.8 2.0 %collective-permute-start.13 = (bf16[2,256,128]{2,1,0:T(8,128)(2,1)S(1)}, bf16[2,256,128]{2,1,0:T(8,128)(2,1)S(1)}, u32[]{:S(2)}, u32[]{:S(2)}) collective-permute-start(bf16[2,256,128]{2,1,0:T(8,128)(2,1)S(1)} %chip_sum.5.refs_2_._), channel_id=1, source_target_pairs={{0,8},{1,17},{2,10},{3,19},{4,12},{5,21},{6,14},{7,23},{8,0},{9,25... | collective-permute-start | bytes 393224 | tf_op jit(solution)/shard_map/ppermute | solution.py:501
  22.9 0.7 %rest.1 = (bf16[2,256,512]{2,1,0:T(8,128)(2,1)S(1)}, bf16[2,256,512]{2,1,0:T(8,128)(2,1)S(1)}) custom-call(bf16[2,256,256]{2,1,0:T(8,128)(2,1)S(1)} %chip_sum.3._.refs_0_, bf16[2,256,128]{2,1,0:T(8,128)(2,1)S(1)} %chip_sum.4._.refs_1_, bf16[2,256,128]{2,1,0:T(8,128)(2,1)S(1)} %chip_sum.5.refs_2_._, ...), custom_call_target="tpu_custom_call" | custom-call | tf_op jit(solution)/shard_map/rest/pallas_call | solution.py:410
  23.6 0.1 collective-permute-start.7
  23.6 0.9 %outputs.1 = (bf16[144,1024]{1,0:T(8,128)(2,1)S(1)}, bf16[144,1024]{1,0:T(8,128)(2,1)S(1)}) custom-call(bf16[2,256,512]{2,1,0:T(8,128)(2,1)S(1)} %get-tuple-element.84._.refs_0_, bf16[144,512]{1,0:T(8,128)(2,1)S(1)} %get-tuple-element.85.refs_0_, bf16[144,512]{1,0:T(8,128)(2,1)S(1)} %get-tuple-element.86.refs_1_, ...), custom_call_target="tpu_custom_call" | custom-call | flops 10000000000 | bytes 4980736 | tf_op jit(solution)/shard_map/outputs/pallas_call | solution.py:410
  24.6 0.1 pack_lon.1
  24.7 0.5 %collective-permute-start.12 = (bf16[36,1024]{1,0:T(8,128)(2,1)S(1)}, bf16[36,1024]{1,0:T(8,128)(2,1)S(1)}, u32[]{:S(2)}, u32[]{:S(2)}) collective-permute-start(bf16[36,1024]{1,0:T(8,128)(2,1)S(1)} %pack_lon.1), channel_id=1, source_target_pairs={{7,0},{0,1},{1,2},{2,3},{3,4},{4,5},{5,6},{6,7},{15,8},{8,9},{9,10... | collective-permute-start | bytes 221192 | tf_op jit(solution)/shard_map/ppermute | solution.py:520
  25.3 0.3 collective-permute-done.7.refs_1_
  25.5 0.1 halve1.3
  25.6 0.9 %collective-permute-start.9 = (bf16[1,256,256]{2,1,0:T(8,128)(2,1)S(1)}, bf16[1,256,256]{2,1,0:T(8,128)(2,1)S(1)}, u32[]{:S(2)}, u32[]{:S(2)}) collective-permute-start(bf16[1,256,256]{2,1,0:T(8,128)(2,1)S(1)} %get-tuple-element.93._), channel_id=1, source_target_pairs={{0,16},{1,9},{2,18},{3,11},{4,20},{5,13},{6,22},{7,15},{8,24},{9,1... | collective-permute-start | bytes 393224 | tf_op jit(solution)/shard_map/ppermute | solution.py:501
  26.6 1.3 %collective-permute-start.11 = (bf16[1,256,128]{2,1,0:T(8,128)(2,1)S(1)}, bf16[1,256,128]{2,1,0:T(8,128)(2,1)S(1)}, u32[]{:S(2)}, u32[]{:S(2)}) collective-permute-start(bf16[1,256,128]{2,1,0:T(8,128)(2,1)S(1)} %get-tuple-element.95), channel_id=1, source_target_pairs={{0,16},{1,9},{2,18},{3,11},{4,20},{5,13},{6,22},{7,15},{8,24},{9,1... | collective-permute-start | bytes 196616 | tf_op jit(solution)/shard_map/ppermute | solution.py:501
  27.9 2.5 %collective-permute-done.12._.lon_in = bf16[36,1024]{1,0:T(8,128)(2,1)S(1)} collective-permute-done((bf16[36,1024]{1,0:T(8,128)(2,1)S(1)}, bf16[36,1024]{1,0:T(8,128)(2,1)S(1)}, u32[]{:S(2)}, u32[]{:S(2)}) %collective-permute-start.12) | collective-permute-done | bytes 73760 | tf_op jit(solution)/shard_map/ppermute | solution.py:520
  30.5 0.6 %collective-permute-start.14 = (bf16[1,256,128]{2,1,0:T(8,128)(2,1)S(1)}, bf16[1,256,128]{2,1,0:T(8,128)(2,1)S(1)}, u32[]{:S(2)}, u32[]{:S(2)}) collective-permute-start(bf16[1,256,128]{2,1,0:T(8,128)(2,1)S(1)} %get-tuple-element.97), channel_id=1, source_target_pairs={{0,16},{1,9},{2,18},{3,11},{4,20},{5,13},{6,22},{7,15},{8,24},{9,1... | collective-permute-start | bytes 196616 | tf_op jit(solution)/shard_map/ppermute | solution.py:501
  31.1 0.3 collective-permute-done.11.refs_3_.refs_4_
  31.4 3.5 %collective-permute-done.14.refs_5_.refs_6_ = bf16[1,256,128]{2,1,0:T(8,128)(2,1)S(1)} collective-permute-done((bf16[1,256,128]{2,1,0:T(8,128)(2,1)S(1)}, bf16[1,256,128]{2,1,0:T(8,128)(2,1)S(1)}, u32[]{:S(2)}, u32[]{:S(2)}) %collective-permute-start.14) | collective-permute-done | bytes 65568 | tf_op jit(solution)/shard_map/ppermute | solution.py:501
  34.8 0.9 %collective-permute-start.17 = (bf16[64,512]{1,0:T(8,128)(2,1)S(1)}, bf16[64,512]{1,0:T(8,128)(2,1)S(1)}, u32[]{:S(2)}, u32[]{:S(2)}) collective-permute-start(bf16[64,512]{1,0:T(8,128)(2,1)S(1)} %line_parts.2._), channel_id=1, source_target_pairs={{0,6},{1,7},{2,4},{3,5},{4,2},{5,3},{6,0},{7,1},{8,14},{9,15},{10,... | collective-permute-start | bytes 196616 | tf_op jit(solution)/shard_map/ppermute | solution.py:546
  35.7 0.2 pack_back.1
  35.9 1.0 %collective-permute-start.15 = (bf16[108,1024]{1,0:T(8,128)(2,1)S(1)}, bf16[108,1024]{1,0:T(8,128)(2,1)S(1)}, u32[]{:S(2)}, u32[]{:S(2)}) collective-permute-start(bf16[108,1024]{1,0:T(8,128)(2,1)S(1)} %get-tuple-element.98.refs_0_), channel_id=1, source_target_pairs={{24,0},{9,1},{26,2},{11,3},{28,4},{13,5},{30,6},{15,7},{0,8},{17,9... | collective-permute-start | bytes 663560 | tf_op jit(solution)/shard_map/ppermute | solution.py:555
  37.0 2.7 %collective-permute-start.19 = (bf16[64,512]{1,0:T(8,128)(2,1)S(1)}, bf16[64,512]{1,0:T(8,128)(2,1)S(1)}, u32[]{:S(2)}, u32[]{:S(2)}) collective-permute-start(bf16[64,512]{1,0:T(8,128)(2,1)S(1)} %get-tuple-element.105), channel_id=1, source_target_pairs={{0,2},{1,3},{2,0},{3,1},{4,6},{5,7},{6,4},{7,5},{8,10},{9,11},{10,... | collective-permute-start | bytes 196616 | tf_op jit(solution)/shard_map/ppermute | solution.py:546
  39.7 1.7 %collective-permute-done.17.refs_1_ = bf16[64,512]{1,0:T(8,128)(2,1)S(1)} collective-permute-done((bf16[64,512]{1,0:T(8,128)(2,1)S(1)}, bf16[64,512]{1,0:T(8,128)(2,1)S(1)}, u32[]{:S(2)}, u32[]{:S(2)}) %collective-permute-start.17) | collective-permute-done | bytes 65568 | tf_op jit(solution)/shard_map/ppermute | solution.py:546
  41.5 1.4 %collective-permute-done.18.refs_1_ = bf16[64,512]{1,0:T(8,128)(2,1)S(1)} collective-permute-done((bf16[64,512]{1,0:T(8,128)(2,1)S(1)}, bf16[64,512]{1,0:T(8,128)(2,1)S(1)}, u32[]{:S(2)}, u32[]{:S(2)}) %collective-permute-start.18) | collective-permute-done | bytes 65568 | tf_op jit(solution)/shard_map/ppermute | solution.py:546
  42.9 2.5 %collective-permute-start.22 = (bf16[64,512]{1,0:T(8,128)(2,1)S(1)}, bf16[64,512]{1,0:T(8,128)(2,1)S(1)}, u32[]{:S(2)}, u32[]{:S(2)}) collective-permute-start(bf16[64,512]{1,0:T(8,128)(2,1)S(1)} %line_sum.1.refs_0_), channel_id=1, source_target_pairs={{0,24},{8,16},{16,8},{24,0},{1,25},{9,17},{17,9},{25,1},{2,26},{10... | collective-permute-start | bytes 196616 | tf_op jit(solution)/shard_map/ppermute | solution.py:562
  45.4 0.7 %collective-permute-start.21 = (bf16[64,512]{1,0:T(8,128)(2,1)S(1)}, bf16[64,512]{1,0:T(8,128)(2,1)S(1)}, u32[]{:S(2)}, u32[]{:S(2)}) collective-permute-start(bf16[64,512]{1,0:T(8,128)(2,1)S(1)} %line_sum.1.refs_0_), channel_id=1, source_target_pairs={{0,16},{8,24},{16,0},{24,8},{1,17},{9,25},{17,1},{25,9},{2,18},{10... | collective-permute-start | bytes 196616 | tf_op jit(solution)/shard_map/ppermute | solution.py:562
  46.1 0.3 collective-permute-start.20
  46.5 0.6 %place.1.placed = f32[288,1024]{1,0:T(8,128)S(1)} custom-call(bf16[144,1024]{1,0:T(8,128)(2,1)S(1)} %get-tuple-element.89.inner_results, bf16[144,1024]{1,0:T(8,128)(2,1)S(1)} %get-tuple-element.90.outer_results, bf16[108,1024]{1,0:T(8,128)(2,1)S(1)} %collective-permute-done.15.lat_in), custom_call_target="tpu_custom_call" | custom-call | bytes 1990656 | tf_op jit(solution)/shard_map/place/pallas_call | solution.py:410
  47.1 1.2 %place_rest.1 = (bf16[288,512]{1,0:T(8,128)(2,1)}, bf16[288,512]{1,0:T(8,128)(2,1)}, f32[8,128]{1,0:T(8,128)S(1)}) custom-call(f32[288,1024]{1,0:T(8,128)S(1)} %place.1.placed, bf16[36,1024]{1,0:T(8,128)(2,1)S(1)} %collective-permute-done.12._.lon_in, bf16[36,1024]{1,0:T(8,128)(2,1)S(1)} %collective-permute-done.16.diag_in), custom_call_target="tpu_custom_call" | custom-call | bytes 1921024 | tf_op jit(solution)/shard_map/place_rest/pallas_call | solution.py:410
  48.3 0.5 collective-permute-done.22.refs_3_
  48.8 0.9 %collective-permute-done.21.refs_2_ = bf16[64,512]{1,0:T(8,128)(2,1)S(1)} collective-permute-done((bf16[64,512]{1,0:T(8,128)(2,1)S(1)}, bf16[64,512]{1,0:T(8,128)(2,1)S(1)}, u32[]{:S(2)}, u32[]{:S(2)}) %collective-permute-start.21) | collective-permute-done | bytes 65568 | tf_op jit(solution)/shard_map/ppermute | solution.py:562
  49.7 0.7 %collective-permute-done.20.refs_1_ = bf16[64,512]{1,0:T(8,128)(2,1)S(1)} collective-permute-done((bf16[64,512]{1,0:T(8,128)(2,1)S(1)}, bf16[64,512]{1,0:T(8,128)(2,1)S(1)}, u32[]{:S(2)}, u32[]{:S(2)}) %collective-permute-start.20) | collective-permute-done | bytes 65568 | tf_op jit(solution)/shard_map/ppermute | solution.py:562
  50.4 0.9 %finish.1 = (f32[64,1536]{1,0:T(8,128)}, f32[64,512]{1,0:T(8,128)}) custom-call(f32[8,128]{1,0:T(8,128)S(1)} %get-tuple-element.102._, bf16[64,512]{1,0:T(8,128)(2,1)S(1)} %line_sum.1.refs_0_, bf16[64,512]{1,0:T(8,128)(2,1)S(1)} %collective-permute-done.20.refs_1_, bf16[64,512]{1,0:T(8,128)(2,1)S(1)} %collective-permute-done.21.refs_2_, ...), custom_call_target="tpu_custom_call" | custom-call | bytes 790528 | tf_op jit(solution)/shard_map/finish/pallas_call | solution.py:410
  (30 shorter events, 0.5 us)
Async XLA Ops:
  0.6 1.0 %copy-start.3 = (bf16[2,6,24,512]{3,2,1,0:T(8,128)(2,1)S(1)}, bf16[2,6,24,512]{3,2,1,0:T(8,128)(2,1)}, u32[]{:S(2)}) copy-start(bf16[2,6,24,512]{3,2,1,0:T(8,128)(2,1)} %param.5) | copy-start | bytes 884740
  0.6 1.0 %copy-start.2 = (bf16[2,6,24,512]{3,2,1,0:T(8,128)(2,1)S(1)}, bf16[2,6,24,512]{3,2,1,0:T(8,128)(2,1)}, u32[]{:S(2)}) copy-start(bf16[2,6,24,512]{3,2,1,0:T(8,128)(2,1)} %param.4) | copy-start | bytes 884740
  1.7 9.8 %copy-start.1 = (bf16[512,512]{1,0:T(8,128)(2,1)S(1)}, bf16[512,512]{1,0:T(8,128)(2,1)}, u32[]{:S(2)}) copy-start(bf16[512,512]{1,0:T(8,128)(2,1)} %refs_7_.1) | copy-start | bytes 1572868
  2.0 9.5 %copy-start = (bf16[512,1536]{1,0:T(8,128)(2,1)S(1)}, bf16[512,1536]{1,0:T(8,128)(2,1)}, u32[]{:S(2)}) copy-start(bf16[512,1536]{1,0:T(8,128)(2,1)} %refs_6_.1) | copy-start | bytes 4718596
  2.1 10.2 %collective-permute-start = (bf16[72,1024]{1,0:T(8,128)(2,1)S(1)}, bf16[72,1024]{1,0:T(8,128)(2,1)S(1)}, u32[]{:S(2)}, u32[]{:S(2)}) collective-permute-start(bf16[72,1024]{1,0:T(8,128)(2,1)S(1)} %get-tuple-element.67), channel_id=1, source_target_pairs={{0,24},{1,9},{2,26},{3,11},{4,28},{5,13},{6,30},{7,15},{8,0},{9,17... | collective-permute-start | bytes 442376 | tf_op jit(solution)/shard_map/ppermute | solution.py:464
  6.0 8.4 %collective-permute-start.1 = (bf16[36,1024]{1,0:T(8,128)(2,1)S(1)}, bf16[36,1024]{1,0:T(8,128)(2,1)S(1)}, u32[]{:S(2)}, u32[]{:S(2)}) collective-permute-start(bf16[36,1024]{1,0:T(8,128)(2,1)S(1)} %get-tuple-element.58._), channel_id=1, source_target_pairs={{0,7},{1,0},{2,1},{3,2},{4,3},{5,4},{6,5},{7,6},{8,15},{9,8},{10,9... | collective-permute-start | bytes 221192 | tf_op jit(solution)/shard_map/ppermute | solution.py:465
  8.4 5.9 %collective-permute-start.2 = (bf16[36,1024]{1,0:T(8,128)(2,1)S(1)}, bf16[36,1024]{1,0:T(8,128)(2,1)S(1)}, u32[]{:S(2)}, u32[]{:S(2)}) collective-permute-start(bf16[36,1024]{1,0:T(8,128)(2,1)S(1)} %get-tuple-element.71), channel_id=1, source_target_pairs={{0,24},{1,9},{2,26},{3,11},{4,28},{5,13},{6,30},{7,15},{8,0},{9,17... | collective-permute-start | bytes 221192 | tf_op jit(solution)/shard_map/ppermute | solution.py:466
  9.9 4.5 %collective-permute-start.3 = (bf16[36,1024]{1,0:T(8,128)(2,1)S(1)}, bf16[36,1024]{1,0:T(8,128)(2,1)S(1)}, u32[]{:S(2)}, u32[]{:S(2)}) collective-permute-start(bf16[36,1024]{1,0:T(8,128)(2,1)S(1)} %get-tuple-element.72), channel_id=1, source_target_pairs={{0,15},{1,24},{2,9},{3,26},{4,11},{5,28},{6,13},{7,30},{8,23},{9,0... | collective-permute-start | bytes 221192 | tf_op jit(solution)/shard_map/ppermute | solution.py:467
  16.8 1.6 %collective-permute-start.4 = (bf16[2,256,256]{2,1,0:T(8,128)(2,1)S(1)}, bf16[2,256,256]{2,1,0:T(8,128)(2,1)S(1)}, u32[]{:S(2)}, u32[]{:S(2)}) collective-permute-start(bf16[2,256,256]{2,1,0:T(8,128)(2,1)S(1)} %get-tuple-element.77), channel_id=1, source_target_pairs={{0,1},{1,0},{2,3},{3,2},{4,5},{5,4},{6,7},{7,6},{8,9},{9,8},{10,11... | collective-permute-start | bytes 786440 | tf_op jit(solution)/shard_map/ppermute | solution.py:492
  16.9 3.7 %collective-permute-start.5 = (bf16[2,256,128]{2,1,0:T(8,128)(2,1)S(1)}, bf16[2,256,128]{2,1,0:T(8,128)(2,1)S(1)}, u32[]{:S(2)}, u32[]{:S(2)}) collective-permute-start(bf16[2,256,128]{2,1,0:T(8,128)(2,1)S(1)} %get-tuple-element.79), channel_id=1, source_target_pairs={{0,1},{1,0},{2,3},{3,2},{4,5},{5,4},{6,7},{7,6},{8,9},{9,8},{10,11... | collective-permute-start | bytes 393224 | tf_op jit(solution)/shard_map/ppermute | solution.py:492
  17.3 3.5 %collective-permute-start.6 = (bf16[2,256,128]{2,1,0:T(8,128)(2,1)S(1)}, bf16[2,256,128]{2,1,0:T(8,128)(2,1)S(1)}, u32[]{:S(2)}, u32[]{:S(2)}) collective-permute-start(bf16[2,256,128]{2,1,0:T(8,128)(2,1)S(1)} %get-tuple-element.81), channel_id=1, source_target_pairs={{0,1},{1,0},{2,3},{3,2},{4,5},{5,4},{6,7},{7,6},{8,9},{9,8},{10,11... | collective-permute-start | bytes 393224 | tf_op jit(solution)/shard_map/ppermute | solution.py:492
  18.4 6.8 %collective-permute-start.8 = (bf16[2,256,256]{2,1,0:T(8,128)(2,1)S(1)}, bf16[2,256,256]{2,1,0:T(8,128)(2,1)S(1)}, u32[]{:S(2)}, u32[]{:S(2)}) collective-permute-start(bf16[2,256,256]{2,1,0:T(8,128)(2,1)S(1)} %chip_sum.3._.refs_0_), channel_id=1, source_target_pairs={{0,8},{1,17},{2,10},{3,19},{4,12},{5,21},{6,14},{7,23},{8,0},{9,25... | collective-permute-start | bytes 786440 | tf_op jit(solution)/shard_map/ppermute | solution.py:501
  20.7 5.9 %collective-permute-start.10 = (bf16[2,256,128]{2,1,0:T(8,128)(2,1)S(1)}, bf16[2,256,128]{2,1,0:T(8,128)(2,1)S(1)}, u32[]{:S(2)}, u32[]{:S(2)}) collective-permute-start(bf16[2,256,128]{2,1,0:T(8,128)(2,1)S(1)} %chip_sum.4._.refs_1_), channel_id=1, source_target_pairs={{0,8},{1,17},{2,10},{3,19},{4,12},{5,21},{6,14},{7,23},{8,0},{9,25... | collective-permute-start | bytes 393224 | tf_op jit(solution)/shard_map/ppermute | solution.py:501
  20.8 9.6 %collective-permute-start.13 = (bf16[2,256,128]{2,1,0:T(8,128)(2,1)S(1)}, bf16[2,256,128]{2,1,0:T(8,128)(2,1)S(1)}, u32[]{:S(2)}, u32[]{:S(2)}) collective-permute-start(bf16[2,256,128]{2,1,0:T(8,128)(2,1)S(1)} %chip_sum.5.refs_2_._), channel_id=1, source_target_pairs={{0,8},{1,17},{2,10},{3,19},{4,12},{5,21},{6,14},{7,23},{8,0},{9,25... | collective-permute-start | bytes 393224 | tf_op jit(solution)/shard_map/ppermute | solution.py:501
  23.6 2.0 %collective-permute-start.7 = (bf16[2,256,512]{2,1,0:T(8,128)(2,1)S(1)}, bf16[2,256,512]{2,1,0:T(8,128)(2,1)S(1)}, u32[]{:S(2)}, u32[]{:S(2)}) collective-permute-start(bf16[2,256,512]{2,1,0:T(8,128)(2,1)S(1)} %get-tuple-element.91), channel_id=1, source_target_pairs={{0,1},{1,0},{2,3},{3,2},{4,5},{5,4},{6,7},{7,6},{8,9},{9,8},{10,11... | collective-permute-start | bytes 1572872 | tf_op jit(solution)/shard_map/ppermute | solution.py:513
  24.7 5.7 %collective-permute-start.12 = (bf16[36,1024]{1,0:T(8,128)(2,1)S(1)}, bf16[36,1024]{1,0:T(8,128)(2,1)S(1)}, u32[]{:S(2)}, u32[]{:S(2)}) collective-permute-start(bf16[36,1024]{1,0:T(8,128)(2,1)S(1)} %pack_lon.1), channel_id=1, source_target_pairs={{7,0},{0,1},{1,2},{2,3},{3,4},{4,5},{5,6},{6,7},{15,8},{8,9},{9,10... | collective-permute-start | bytes 221192 | tf_op jit(solution)/shard_map/ppermute | solution.py:520
  25.6 9.2 %collective-permute-start.9 = (bf16[1,256,256]{2,1,0:T(8,128)(2,1)S(1)}, bf16[1,256,256]{2,1,0:T(8,128)(2,1)S(1)}, u32[]{:S(2)}, u32[]{:S(2)}) collective-permute-start(bf16[1,256,256]{2,1,0:T(8,128)(2,1)S(1)} %get-tuple-element.93._), channel_id=1, source_target_pairs={{0,16},{1,9},{2,18},{3,11},{4,20},{5,13},{6,22},{7,15},{8,24},{9,1... | collective-permute-start | bytes 393224 | tf_op jit(solution)/shard_map/ppermute | solution.py:501
  26.6 4.8 %collective-permute-start.11 = (bf16[1,256,128]{2,1,0:T(8,128)(2,1)S(1)}, bf16[1,256,128]{2,1,0:T(8,128)(2,1)S(1)}, u32[]{:S(2)}, u32[]{:S(2)}) collective-permute-start(bf16[1,256,128]{2,1,0:T(8,128)(2,1)S(1)} %get-tuple-element.95), channel_id=1, source_target_pairs={{0,16},{1,9},{2,18},{3,11},{4,20},{5,13},{6,22},{7,15},{8,24},{9,1... | collective-permute-start | bytes 196616 | tf_op jit(solution)/shard_map/ppermute | solution.py:501
  30.5 4.3 %collective-permute-start.14 = (bf16[1,256,128]{2,1,0:T(8,128)(2,1)S(1)}, bf16[1,256,128]{2,1,0:T(8,128)(2,1)S(1)}, u32[]{:S(2)}, u32[]{:S(2)}) collective-permute-start(bf16[1,256,128]{2,1,0:T(8,128)(2,1)S(1)} %get-tuple-element.97), channel_id=1, source_target_pairs={{0,16},{1,9},{2,18},{3,11},{4,20},{5,13},{6,22},{7,15},{8,24},{9,1... | collective-permute-start | bytes 196616 | tf_op jit(solution)/shard_map/ppermute | solution.py:501
  34.8 6.6 %collective-permute-start.17 = (bf16[64,512]{1,0:T(8,128)(2,1)S(1)}, bf16[64,512]{1,0:T(8,128)(2,1)S(1)}, u32[]{:S(2)}, u32[]{:S(2)}) collective-permute-start(bf16[64,512]{1,0:T(8,128)(2,1)S(1)} %line_parts.2._), channel_id=1, source_target_pairs={{0,6},{1,7},{2,4},{3,5},{4,2},{5,3},{6,0},{7,1},{8,14},{9,15},{10,... | collective-permute-start | bytes 196616 | tf_op jit(solution)/shard_map/ppermute | solution.py:546
  35.9 10.6 %collective-permute-start.15 = (bf16[108,1024]{1,0:T(8,128)(2,1)S(1)}, bf16[108,1024]{1,0:T(8,128)(2,1)S(1)}, u32[]{:S(2)}, u32[]{:S(2)}) collective-permute-start(bf16[108,1024]{1,0:T(8,128)(2,1)S(1)} %get-tuple-element.98.refs_0_), channel_id=1, source_target_pairs={{24,0},{9,1},{26,2},{11,3},{28,4},{13,5},{30,6},{15,7},{0,8},{17,9... | collective-permute-start | bytes 663560 | tf_op jit(solution)/shard_map/ppermute | solution.py:555
  36.9 5.9 %collective-permute-start.18 = (bf16[64,512]{1,0:T(8,128)(2,1)S(1)}, bf16[64,512]{1,0:T(8,128)(2,1)S(1)}, u32[]{:S(2)}, u32[]{:S(2)}) collective-permute-start(bf16[64,512]{1,0:T(8,128)(2,1)S(1)} %get-tuple-element.104), channel_id=1, source_target_pairs={{0,4},{1,5},{2,6},{3,7},{4,0},{5,1},{6,2},{7,3},{8,12},{9,13},{10,... | collective-permute-start | bytes 196616 | tf_op jit(solution)/shard_map/ppermute | solution.py:546
  37.0 5.9 %collective-permute-start.19 = (bf16[64,512]{1,0:T(8,128)(2,1)S(1)}, bf16[64,512]{1,0:T(8,128)(2,1)S(1)}, u32[]{:S(2)}, u32[]{:S(2)}) collective-permute-start(bf16[64,512]{1,0:T(8,128)(2,1)S(1)} %get-tuple-element.105), channel_id=1, source_target_pairs={{0,2},{1,3},{2,0},{3,1},{4,6},{5,7},{6,4},{7,5},{8,10},{9,11},{10,... | collective-permute-start | bytes 196616 | tf_op jit(solution)/shard_map/ppermute | solution.py:546
  39.7 7.3 %collective-permute-start.16 = (bf16[36,1024]{1,0:T(8,128)(2,1)S(1)}, bf16[36,1024]{1,0:T(8,128)(2,1)S(1)}, u32[]{:S(2)}, u32[]{:S(2)}) collective-permute-start(bf16[36,1024]{1,0:T(8,128)(2,1)S(1)} %get-tuple-element.99), channel_id=1, source_target_pairs={{15,0},{24,1},{9,2},{26,3},{11,4},{28,5},{13,6},{30,7},{23,8},{0,9... | collective-permute-start | bytes 221192 | tf_op jit(solution)/shard_map/ppermute | solution.py:556
  42.9 5.9 %collective-permute-start.22 = (bf16[64,512]{1,0:T(8,128)(2,1)S(1)}, bf16[64,512]{1,0:T(8,128)(2,1)S(1)}, u32[]{:S(2)}, u32[]{:S(2)}) collective-permute-start(bf16[64,512]{1,0:T(8,128)(2,1)S(1)} %line_sum.1.refs_0_), channel_id=1, source_target_pairs={{0,24},{8,16},{16,8},{24,0},{1,25},{9,17},{17,9},{25,1},{2,26},{10... | collective-permute-start | bytes 196616 | tf_op jit(solution)/shard_map/ppermute | solution.py:562
  45.4 4.3 %collective-permute-start.21 = (bf16[64,512]{1,0:T(8,128)(2,1)S(1)}, bf16[64,512]{1,0:T(8,128)(2,1)S(1)}, u32[]{:S(2)}, u32[]{:S(2)}) collective-permute-start(bf16[64,512]{1,0:T(8,128)(2,1)S(1)} %line_sum.1.refs_0_), channel_id=1, source_target_pairs={{0,16},{8,24},{16,0},{24,8},{1,17},{9,25},{17,1},{25,9},{2,18},{10... | collective-permute-start | bytes 196616 | tf_op jit(solution)/shard_map/ppermute | solution.py:562
  46.1 4.3 %collective-permute-start.20 = (bf16[64,512]{1,0:T(8,128)(2,1)S(1)}, bf16[64,512]{1,0:T(8,128)(2,1)S(1)}, u32[]{:S(2)}, u32[]{:S(2)}) collective-permute-start(bf16[64,512]{1,0:T(8,128)(2,1)S(1)} %line_sum.1.refs_0_), channel_id=1, source_target_pairs={{0,8},{8,0},{16,24},{24,16},{1,9},{9,1},{17,25},{25,17},{2,10},{10... | collective-permute-start | bytes 196616 | tf_op jit(solution)/shard_map/ppermute | solution.py:562

commit v17 on v14

--- a/solution.py
+++ b/solution.py
@@ -23,6 +23,7 @@
 epsilon = 1e-05
 LONG = 13 * 10**8
 LOAD = 5 * 10**9
+PARTS = 5 * 10**9
 BF = jnp.bfloat16
 F32 = jnp.float32
 
@@ -305,18 +306,19 @@
     lon_out[...] = dot(puts(last_rows, QUARTER, HALF), outer_x, NN).astype(BF)
 
 
-def pack_back_kernel(_, inner_results, outer_results, lat_out, diag_out):
+def pack_diag_kernel(_, outer_results, diag_out):
+    outer_y = outer_results[...].astype(F32)[HALF:].astype(BF)
+    diag_out[...] = dot(puts(last_rows, QUARTER, HALF), outer_y, NN).astype(BF)
+
+
+def pack_lat_kernel(_, inner_results, outer_results, lat_out):
     inner_y = inner_results[...].astype(F32)[HALF:]
     outer_y = outer_results[...].astype(F32)[HALF:].astype(BF)
     lat_out[...] = jnp.concatenate([inner_y, dot(puts(first_rows, QUARTER, HALF), outer_y, NN)], axis=0).astype(BF)
-    diag_out[...] = dot(puts(last_rows, QUARTER, HALF), outer_y, NN).astype(BF)
-
-
-def place_kernel(inner_results, outer_results, lat_in, placed):
-    inner_lat, outer_lat, _, _, inner_own, outer_own = (source for source, _ in sources())
-
-    def lat(v):
-        return jnp.where(v < HALF, inner_lat(v), outer_lat(v - HALF))
+
+
+def place_kernel(inner_results, outer_results, lon_in, diag_in, placed):
+    _, _, lon, diag, inner_own, outer_own = (source for source, _ in sources())
 
     def only_first(source):
         return lambda v: jnp.where(v < HALF, source(v), -1)
@@ -324,19 +326,20 @@
     placed[...] = (
         dot(puts(only_first(inner_own), TOKENS, WIN), inner_results[...], NN)
         + dot(puts(only_first(outer_own), TOKENS, WIN), outer_results[...], NN)
-        + dot(puts(lat, TOKENS, HALF + QUARTER), lat_in[...], NN)
-    )
-
-
-def place_rest_kernel(placed, lon_in, diag_in, field_out, d_fields, done):
+        + dot(puts(lon, TOKENS, QUARTER), lon_in[...], NN)
+        + dot(puts(diag, TOKENS, QUARTER), diag_in[...], NN)
+    )
+
+
+def place_rest_kernel(placed, lat_in, field_out, d_fields, done):
     done[...] = jnp.zeros_like(done)
     width = field_out.shape[1]
-    _, _, lon, diag, _, _ = (source for source, _ in sources())
-    total = (
-        placed[...]
-        + dot(puts(lon, TOKENS, QUARTER), lon_in[...], NN)
-        + dot(puts(diag, TOKENS, QUARTER), diag_in[...], NN)
-    ).astype(BF)
+    inner_lat, outer_lat, *_ = (source for source, _ in sources())
+
+    def lat(v):
+        return jnp.where(v < HALF, inner_lat(v), outer_lat(v - HALF))
+
+    total = (placed[...] + dot(puts(lat, TOKENS, HALF + QUARTER), lat_in[...], NN)).astype(BF)
     field_out[...] = total[:, :width]
     d_fields[...] = total[:, width:]
 
@@ -360,6 +363,10 @@
         at = slice(step * rows, (step + 1) * rows)
         totals = [sum(part[0, at].astype(F32) for part in parts) for parts in chunks]
         out[...] = jnp.concatenate(totals, axis=1).astype(out.dtype)
+
+
+def line_sum_kernel(_, *refs):
+    sum_kernel(*refs)
 
 
 def sum_kernel(*refs):
@@ -512,34 +519,36 @@
             )
             kept[index] = [keep, halving(phase, send)]
 
+    (diag_back,) = call(pack_diag_kernel, [quarter], send, results[1], name="pack_diag", unread=(0,))
+    diag_home = lax.ppermute(diag_back, both, back(diag_route))
+
     rows = width // lon_size
     share = ((rows, split[2]), BF)
     parts = call(
         functools.partial(line_parts_kernel, len(kept[0])), [share] * (lon_size // 2), *kept[0], *kept[1],
-        name="line_parts",
+        name="line_parts", flops=PARTS,
     )
     arrived = [
         lax.ppermute(parts[step], "lon", [(j, j ^ (2 * step)) for j in range(lon_size)])
         for step in range(lon_size // 2 - 1, 0, -1)
     ]
-    lat_back, diag_back = call(
-        pack_back_kernel, [((HALF + QUARTER, 2 * width), BF), quarter],
-        parts[1], *results,
-        name="pack_back", unread=(0,),
+    (lat_back,) = call(
+        pack_lat_kernel, [((HALF + QUARTER, 2 * width), BF)], parts[1], *results, name="pack_lat", unread=(0,)
     )
     lat_home = lax.ppermute(lat_back, both, back(lat_route))
-    diag_home = lax.ppermute(diag_back, both, back(diag_route))
-    (line_sum,) = call(sum_kernel, [share], parts[0], *arrived, name="line_sum", flops=LONG)
+    (placed,) = call(
+        place_kernel, [((TOKENS, 2 * width), F32)], *results, lon_home, diag_home, name="place"
+    )
+    (line_sum,) = call(
+        line_sum_kernel, [share], placed, parts[0], *arrived, name="line_sum", flops=LONG, unread=(0,)
+    )
     shared = [
         lax.ppermute(line_sum, "lat", [(i, i ^ step) for i in range(lat_size)]) for step in range(1, lat_size)
     ]
-    (placed,) = call(
-        place_kernel, [((TOKENS, 2 * width), F32)], *results, lat_home, name="place"
-    )
     field_out, d_fields, done = call(
         place_rest_kernel,
         [((TOKENS, width), BF), ((TOKENS, width), BF), ((8, LANES), F32)],
-        placed, lon_home, diag_home,
+        placed, lat_home,
         name="place_rest",
     )
     qkv_grad, proj_grad = call(

time: 50.8 us -> 51.3 us (level)
  waiting for transfers between devices: 11.9 us -> 13.9 us
  starting transfers between devices: 25.4 us -> 23.7 us
    ppermute x1, waiting for transfers between devices: 2.02 us -> 5.17 us  [per_device(): lon_home = lax.ppermute(lon_back, both, back(lon_route))]
    ppermute x1, starting transfers between devices: 1.98 us -> 0.97 us  [per_device(): lat_home = lax.ppermute(lat_back, both, back(lat_route))]
    ppermute x1, waiting for transfers between devices: 0.81 us -> 0.01 us  [per_device(): diag_home = lax.ppermute(diag_back, both, back(diag_route))]
    ppermute x1, waiting for transfers between devices: 0.01 us -> 0.79 us  [per_device(): lat_home = lax.ppermute(lat_back, both, back(lat_route))]
    ppermute x4, starting transfers between devices: 5.35 us -> 4.66 us  [halving(): return lax.ppermute(send, both, route)]
    ppermute x3, waiting for transfers between devices: 1.5 us -> 0.97 us  [per_device(): lax.ppermute(line_sum, 'lat', [(i, i ^ step) for i in range(lat_size)])]
    pallas_call x20 -> x21, Pallas kernels: 11.7 us -> 11.8 us  [call(): pl.pallas_call(kernel, out_shape=shapes, in_specs=[anywhere if i in unrea...]
  transfers between devices with their start and end apart: 20 -> 20, of which waited for: 10 -> 9; matrix products, arithmetic and copies ran while one was open for 0% -> 0% of each run, Pallas kernels for 16% -> 16%
where the time goes in v17:
time: 51.3 us; the launch traced here: 51.2 us
  starting transfers between devices  23.7 us (46%)
  waiting for transfers between devices  13.9 us (27%)
  Pallas kernels  11.8 us (23%)
  local copies, waits for them, and re-layouts  0.94 us (2%)
  between operations  0.8 us (2%)
    pallas_call x21, Pallas kernels, call(): pl.pallas_call(kernel, out_shape=shapes, in_specs=[anywhere if i in unrea...  11.8 us
    ppermute x1, waiting for transfers between devices, per_device(): lon_home = lax.ppermute(lon_back, both, back(lon_route))  5.17 us
    ppermute x4, waiting for transfers between devices, halving(): return lax.ppermute(send, both, route)  4.84 us
    ppermute x4, starting transfers between devices, halving(): return lax.ppermute(send, both, route)  4.66 us
    ppermute x3, starting transfers between devices, per_device(): lax.ppermute(parts[step], 'lon', [(j, j ^ 2 * step) for j in range(lon_si...  4.45 us
    ppermute x1, starting transfers between devices, per_device(): inner_in = lax.ppermute(inner_lat, both, lat_route)  3.94 us
    ppermute x3, starting transfers between devices, per_device(): lax.ppermute(line_sum, 'lat', [(i, i ^ step) for i in range(lat_size)])  3.55 us
    ppermute x1, starting transfers between devices, per_device(): lon_in = lax.ppermute(lon_piece, both, lon_route)  1.8 us
  transfers between devices with their start and end apart: 20, of which 9 were waited for; matrix products, arithmetic and copies ran while one was open for 0% of the time, Pallas kernels for 16%

profile of v17, /device:TPU:0, one launch (start us, length us, event | category | flops | bytes accessed | tf_op | source)
XLA Modules:
  0.0 51.2 jit_solution(13335408431415164164)
XLA Ops:
  0.7 0.1 order.1
  0.8 0.8 %copy-done.3 = bf16[2,6,24,512]{3,2,1,0:T(8,128)(2,1)S(1)} copy-done((bf16[2,6,24,512]{3,2,1,0:T(8,128)(2,1)S(1)}, bf16[2,6,24,512]{3,2,1,0:T(8,128)(2,1)}, u32[]{:S(2)}) %copy-start.3) | copy-done | bytes 294936
  1.6 0.1 copy-done.2
  1.7 0.4 pack.1
  2.1 3.9 %collective-permute-start = (bf16[72,1024]{1,0:T(8,128)(2,1)S(1)}, bf16[72,1024]{1,0:T(8,128)(2,1)S(1)}, u32[]{:S(2)}, u32[]{:S(2)}) collective-permute-start(bf16[72,1024]{1,0:T(8,128)(2,1)S(1)} %get-tuple-element.62), channel_id=1, source_target_pairs={{0,24},{1,9},{2,26},{3,11},{4,28},{5,13},{6,30},{7,15},{8,0},{9,17... | collective-permute-start | bytes 442376 | tf_op jit(solution)/shard_map/ppermute | solution.py:457
  6.0 1.8 %collective-permute-start.1 = (bf16[36,1024]{1,0:T(8,128)(2,1)S(1)}, bf16[36,1024]{1,0:T(8,128)(2,1)S(1)}, u32[]{:S(2)}, u32[]{:S(2)}) collective-permute-start(bf16[36,1024]{1,0:T(8,128)(2,1)S(1)} %get-tuple-element.53._), channel_id=1, source_target_pairs={{0,7},{1,0},{2,1},{3,2},{4,3},{5,4},{6,5},{7,6},{8,15},{9,8},{10,9... | collective-permute-start | bytes 221192 | tf_op jit(solution)/shard_map/ppermute | solution.py:458
  7.8 0.6 %pack_rest.1 = (bf16[36,1024]{1,0:T(8,128)(2,1)S(1)}, bf16[36,1024]{1,0:T(8,128)(2,1)S(1)}, f32[72,1024]{1,0:T(8,128)S(1)}, f32[72,1024]{1,0:T(8,128)S(1)}) custom-call(bf16[36,1024]{1,0:T(8,128)(2,1)S(1)} %get-tuple-element.53._, bf16[288,512]{1,0:T(8,128)(2,1)S(1)} %bitcast.6, bf16[288,512]{1,0:T(8,128)(2,1)S(1)} %bitcast.8, ...), custom_call_target="tpu_custom_call" | custom-call | flops 500000000 | bytes 1525248 | tf_op jit(solution)/shard_map/pack_rest/pallas_call | solution.py:403
  8.4 1.5 %collective-permute-start.2 = (bf16[36,1024]{1,0:T(8,128)(2,1)S(1)}, bf16[36,1024]{1,0:T(8,128)(2,1)S(1)}, u32[]{:S(2)}, u32[]{:S(2)}) collective-permute-start(bf16[36,1024]{1,0:T(8,128)(2,1)S(1)} %get-tuple-element.66), channel_id=1, source_target_pairs={{0,24},{1,9},{2,26},{3,11},{4,28},{5,13},{6,30},{7,15},{8,0},{9,17... | collective-permute-start | bytes 221192 | tf_op jit(solution)/shard_map/ppermute | solution.py:459
  9.9 1.6 %collective-permute-start.3 = (bf16[36,1024]{1,0:T(8,128)(2,1)S(1)}, bf16[36,1024]{1,0:T(8,128)(2,1)S(1)}, u32[]{:S(2)}, u32[]{:S(2)}) collective-permute-start(bf16[36,1024]{1,0:T(8,128)(2,1)S(1)} %get-tuple-element.67), channel_id=1, source_target_pairs={{0,15},{1,24},{2,9},{3,26},{4,11},{5,28},{6,13},{7,30},{8,23},{9,0... | collective-permute-start | bytes 221192 | tf_op jit(solution)/shard_map/ppermute | solution.py:460
  11.5 0.7 %own.1 = (f32[72,512]{1,0:T(8,128)S(1)}, f32[72,1536]{1,0:T(8,128)S(1)}, f32[72,512]{1,0:T(8,128)S(1)}) custom-call(f32[72,1024]{1,0:T(8,128)S(1)} %get-tuple-element.58.inner_own.own, bf16[512,1536]{1,0:T(8,128)(2,1)S(1)} %copy-done, bf16[512,512]{1,0:T(8,128)(2,1)S(1)} %copy-done.1), custom_call_target="tpu_custom_call" | custom-call | flops 500000000 | bytes 3129344 | tf_op jit(solution)/shard_map/own/pallas_call | solution.py:403
  12.2 2.1 %inner.1 = (f32[2,256,512]{2,1,0:T(8,128)S(1)}, bf16[144,512]{1,0:T(8,128)(2,1)S(1)}, bf16[144,512]{1,0:T(8,128)(2,1)S(1)}, bf16[2,256,144]{2,1,0:T(8,128)(2,1)S...) custom-call(f32[72,1024]{1,0:T(8,128)S(1)} %get-tuple-element.58.inner_own.own, ...), custom_call_target="tpu_custom_call" | custom-call | flops 1000000000 | bytes 5505024 | tf_op jit(solution)/shard_map/inner/pallas_call | solution.py:403
  14.4 2.4 %outer.1 = (bf16[2,256,256]{2,1,0:T(8,128)(2,1)S(1)}, bf16[2,256,256]{2,1,0:T(8,128)(2,1)S(1)}, bf16[144,512]{1,0:T(8,128)(2,1)S(1)}, bf16[144,512]{1,0:T(8,128)...) custom-call(f32[72,1024]{1,0:T(8,128)S(1)} %get-tuple-element.65.own, ...), custom_call_target="tpu_custom_call" | custom-call | flops 1000000000 | bytes 5365760 | tf_op jit(solution)/shard_map/outer/pallas_call | solution.py:403
  16.8 0.1 collective-permute-start.5
  16.9 0.4 collective-permute-start.4
  17.3 0.4 keep.1
  17.8 0.6 %collective-permute-done.5.refs_1_ = bf16[2,256,256]{2,1,0:T(8,128)(2,1)S(1)} collective-permute-done((bf16[2,256,256]{2,1,0:T(8,128)(2,1)S(1)}, bf16[2,256,256]{2,1,0:T(8,128)(2,1)S(1)}, u32[]{:S(2)}, u32[]{:S(2)}) %collective-permute-start.5) | collective-permute-done | bytes 262176 | tf_op jit(solution)/shard_map/ppermute | solution.py:483
  18.4 0.1 chip_sum.3.__._
  18.4 2.2 %collective-permute-start.8 = (bf16[2,256,256]{2,1,0:T(8,128)(2,1)S(1)}, bf16[2,256,256]{2,1,0:T(8,128)(2,1)S(1)}, u32[]{:S(2)}, u32[]{:S(2)}) collective-permute-start(bf16[2,256,256]{2,1,0:T(8,128)(2,1)S(1)} %chip_sum.3.__._), channel_id=1, source_target_pairs={{0,8},{1,17},{2,10},{3,19},{4,12},{5,21},{6,14},{7,23},{8,0},{9,25... | collective-permute-start | bytes 786440 | tf_op jit(solution)/shard_map/ppermute | solution.py:492
  20.7 0.3 collective-permute-start.10
  21.0 0.7 %rest.1 = (bf16[2,256,512]{2,1,0:T(8,128)(2,1)S(1)}, bf16[2,256,512]{2,1,0:T(8,128)(2,1)S(1)}) custom-call(bf16[2,256,256]{2,1,0:T(8,128)(2,1)S(1)} %chip_sum.2._, bf16[2,256,256]{2,1,0:T(8,128)(2,1)S(1)} %chip_sum.3.__._, bf16[2,256,144]{2,1,0:T(8,128)(2,1)S(1)} %get-tuple-element.63.refs_0_, bf16[144,2048]{1,0:T(8,128)(2,1)S(1)} %get-tuple-element.64.refs_1_.refs_2_, ...), custom_call_target="tpu_custom_call" | custom-call | tf_op jit(solution)/shard_map/rest/pallas_call | solution.py:403
  21.7 0.1 collective-permute-start.7
  21.8 0.9 %outputs.1 = (bf16[144,1024]{1,0:T(8,128)(2,1)S(1)}, bf16[144,1024]{1,0:T(8,128)(2,1)S(1)}) custom-call(bf16[2,256,512]{2,1,0:T(8,128)(2,1)S(1)} %get-tuple-element.77._.refs_0_, bf16[144,512]{1,0:T(8,128)(2,1)S(1)} %get-tuple-element.78.refs_0_, bf16[144,512]{1,0:T(8,128)(2,1)S(1)} %get-tuple-element.79.refs_1_, ...), custom_call_target="tpu_custom_call" | custom-call | flops 10000000000 | bytes 4980736 | tf_op jit(solution)/shard_map/outputs/pallas_call | solution.py:403
  22.7 0.2 pack_lon.1
  22.8 0.5 %collective-permute-start.6 = (bf16[36,1024]{1,0:T(8,128)(2,1)S(1)}, bf16[36,1024]{1,0:T(8,128)(2,1)S(1)}, u32[]{:S(2)}, u32[]{:S(2)}) collective-permute-start(bf16[36,1024]{1,0:T(8,128)(2,1)S(1)} %pack_lon.1), channel_id=1, source_target_pairs={{7,0},{0,1},{1,2},{2,3},{3,4},{4,5},{5,6},{6,7},{15,8},{8,9},{9,10... | collective-permute-start | bytes 221192 | tf_op jit(solution)/shard_map/ppermute | solution.py:509
  23.4 5.2 %collective-permute-done.6.lon_in._ = bf16[36,1024]{1,0:T(8,128)(2,1)S(1)} collective-permute-done((bf16[36,1024]{1,0:T(8,128)(2,1)S(1)}, bf16[36,1024]{1,0:T(8,128)(2,1)S(1)}, u32[]{:S(2)}, u32[]{:S(2)}) %collective-permute-start.6) | collective-permute-done | bytes 73760 | tf_op jit(solution)/shard_map/ppermute | solution.py:509
  28.6 0.1 halve1.3
  28.7 1.2 %collective-permute-start.11 = (bf16[1,256,256]{2,1,0:T(8,128)(2,1)S(1)}, bf16[1,256,256]{2,1,0:T(8,128)(2,1)S(1)}, u32[]{:S(2)}, u32[]{:S(2)}) collective-permute-start(bf16[1,256,256]{2,1,0:T(8,128)(2,1)S(1)} %get-tuple-element.87), channel_id=1, source_target_pairs={{0,16},{1,9},{2,18},{3,11},{4,20},{5,13},{6,22},{7,15},{8,24},{9,1... | collective-permute-start | bytes 393224 | tf_op jit(solution)/shard_map/ppermute | solution.py:492
  29.9 0.1 halve1.2
  30.0 0.9 %collective-permute-start.12 = (bf16[1,256,256]{2,1,0:T(8,128)(2,1)S(1)}, bf16[1,256,256]{2,1,0:T(8,128)(2,1)S(1)}, u32[]{:S(2)}, u32[]{:S(2)}) collective-permute-start(bf16[1,256,256]{2,1,0:T(8,128)(2,1)S(1)} %get-tuple-element.85._), channel_id=1, source_target_pairs={{0,16},{1,9},{2,18},{3,11},{4,20},{5,13},{6,22},{7,15},{8,24},{9,1... | collective-permute-start | bytes 393224 | tf_op jit(solution)/shard_map/ppermute | solution.py:492
  30.9 0.1 pack_diag.1
  31.1 2.6 %collective-permute-done.11.refs_1_ = bf16[1,256,256]{2,1,0:T(8,128)(2,1)S(1)} collective-permute-done((bf16[1,256,256]{2,1,0:T(8,128)(2,1)S(1)}, bf16[1,256,256]{2,1,0:T(8,128)(2,1)S(1)}, u32[]{:S(2)}, u32[]{:S(2)}) %collective-permute-start.11) | collective-permute-done | bytes 131104 | tf_op jit(solution)/shard_map/ppermute | solution.py:492
  33.7 2.3 %collective-permute-done.12.refs_3_ = bf16[1,256,256]{2,1,0:T(8,128)(2,1)S(1)} collective-permute-done((bf16[1,256,256]{2,1,0:T(8,128)(2,1)S(1)}, bf16[1,256,256]{2,1,0:T(8,128)(2,1)S(1)}, u32[]{:S(2)}, u32[]{:S(2)}) %collective-permute-start.12) | collective-permute-done | bytes 131104 | tf_op jit(solution)/shard_map/ppermute | solution.py:492
  36.0 0.1 line_parts.1
  36.1 2.7 %collective-permute-start.14 = (bf16[64,512]{1,0:T(8,128)(2,1)S(1)}, bf16[64,512]{1,0:T(8,128)(2,1)S(1)}, u32[]{:S(2)}, u32[]{:S(2)}) collective-permute-start(bf16[64,512]{1,0:T(8,128)(2,1)S(1)} %get-tuple-element.94), channel_id=1, source_target_pairs={{0,6},{1,7},{2,4},{3,5},{4,2},{5,3},{6,0},{7,1},{8,14},{9,15},{10,... | collective-permute-start | bytes 196616 | tf_op jit(solution)/shard_map/ppermute | solution.py:532
  38.8 1.7 %collective-permute-start.16 = (bf16[64,512]{1,0:T(8,128)(2,1)S(1)}, bf16[64,512]{1,0:T(8,128)(2,1)S(1)}, u32[]{:S(2)}, u32[]{:S(2)}) collective-permute-start(bf16[64,512]{1,0:T(8,128)(2,1)S(1)} %get-tuple-element.89._), channel_id=1, source_target_pairs={{0,2},{1,3},{2,0},{3,1},{4,6},{5,7},{6,4},{7,5},{8,10},{9,11},{10,... | collective-permute-start | bytes 196616 | tf_op jit(solution)/shard_map/ppermute | solution.py:532
  40.5 0.1 pack_lat.1
  40.7 1.0 %collective-permute-start.13 = (bf16[108,1024]{1,0:T(8,128)(2,1)S(1)}, bf16[108,1024]{1,0:T(8,128)(2,1)S(1)}, u32[]{:S(2)}, u32[]{:S(2)}) collective-permute-start(bf16[108,1024]{1,0:T(8,128)(2,1)S(1)} %pack_lat.1), channel_id=1, source_target_pairs={{24,0},{9,1},{26,2},{11,3},{28,4},{13,5},{30,6},{15,7},{0,8},{17,9... | collective-permute-start | bytes 663560 | tf_op jit(solution)/shard_map/ppermute | solution.py:538
  41.6 0.8 %place.1.placed._ = f32[288,1024]{1,0:T(8,128)S(1)} custom-call(bf16[144,1024]{1,0:T(8,128)(2,1)S(1)} %get-tuple-element.82.inner_results, bf16[144,1024]{1,0:T(8,128)(2,1)S(1)} %get-tuple-element.83.outer_results, bf16[36,1024]{1,0:T(8,128)(2,1)S(1)} %collective-permute-done.6.lon_in._, bf16[36,1024]{1,0:T(8,128)(2,1)S(1)} %collective-permute-done.9.diag_in), custom_call_target="tpu_custom_call" | custom-call | bytes 1916928 | tf_op jit(solution)/shard_map/place/pallas_call | solution.py:403
  42.4 0.1 collective-permute-done.14.refs_1_
  42.5 1.4 %collective-permute-done.15.refs_2_ = bf16[64,512]{1,0:T(8,128)(2,1)S(1)} collective-permute-done((bf16[64,512]{1,0:T(8,128)(2,1)S(1)}, bf16[64,512]{1,0:T(8,128)(2,1)S(1)}, u32[]{:S(2)}, u32[]{:S(2)}) %collective-permute-start.15) | collective-permute-done | bytes 65568 | tf_op jit(solution)/shard_map/ppermute | solution.py:532
  44.0 1.4 %collective-permute-start.19 = (bf16[64,512]{1,0:T(8,128)(2,1)S(1)}, bf16[64,512]{1,0:T(8,128)(2,1)S(1)}, u32[]{:S(2)}, u32[]{:S(2)}) collective-permute-start(bf16[64,512]{1,0:T(8,128)(2,1)S(1)} %line_sum.1.refs_0_), channel_id=1, source_target_pairs={{0,24},{8,16},{16,8},{24,0},{1,25},{9,17},{17,9},{25,1},{2,26},{10... | collective-permute-start | bytes 196616 | tf_op jit(solution)/shard_map/ppermute | solution.py:546
  45.4 0.7 %collective-permute-start.18 = (bf16[64,512]{1,0:T(8,128)(2,1)S(1)}, bf16[64,512]{1,0:T(8,128)(2,1)S(1)}, u32[]{:S(2)}, u32[]{:S(2)}) collective-permute-start(bf16[64,512]{1,0:T(8,128)(2,1)S(1)} %line_sum.1.refs_0_), channel_id=1, source_target_pairs={{0,16},{8,24},{16,0},{24,8},{1,17},{9,25},{17,1},{25,9},{2,18},{10... | collective-permute-start | bytes 196616 | tf_op jit(solution)/shard_map/ppermute | solution.py:546
  46.1 1.5 %collective-permute-start.17 = (bf16[64,512]{1,0:T(8,128)(2,1)S(1)}, bf16[64,512]{1,0:T(8,128)(2,1)S(1)}, u32[]{:S(2)}, u32[]{:S(2)}) collective-permute-start(bf16[64,512]{1,0:T(8,128)(2,1)S(1)} %line_sum.1.refs_0_), channel_id=1, source_target_pairs={{0,8},{8,0},{16,24},{24,16},{1,9},{9,1},{17,25},{25,17},{2,10},{10... | collective-permute-start | bytes 196616 | tf_op jit(solution)/shard_map/ppermute | solution.py:546
  47.5 0.8 %collective-permute-done.13.lat_in = bf16[108,1024]{1,0:T(8,128)(2,1)S(1)} collective-permute-done((bf16[108,1024]{1,0:T(8,128)(2,1)S(1)}, bf16[108,1024]{1,0:T(8,128)(2,1)S(1)}, u32[]{:S(2)}, u32[]{:S(2)}) %collective-permute-start.13) | collective-permute-done | bytes 221216 | tf_op jit(solution)/shard_map/ppermute | solution.py:538
  48.3 1.0 %place_rest.1 = (bf16[288,512]{1,0:T(8,128)(2,1)}, bf16[288,512]{1,0:T(8,128)(2,1)}, f32[8,128]{1,0:T(8,128)S(1)}) custom-call(f32[288,1024]{1,0:T(8,128)S(1)} %place.1.placed._, bf16[108,1024]{1,0:T(8,128)(2,1)S(1)} %collective-permute-done.13.lat_in), custom_call_target="tpu_custom_call" | custom-call | bytes 1994752 | tf_op jit(solution)/shard_map/place_rest/pallas_call | solution.py:403
  49.4 0.5 %collective-permute-done.18.refs_2_ = bf16[64,512]{1,0:T(8,128)(2,1)S(1)} collective-permute-done((bf16[64,512]{1,0:T(8,128)(2,1)S(1)}, bf16[64,512]{1,0:T(8,128)(2,1)S(1)}, u32[]{:S(2)}, u32[]{:S(2)}) %collective-permute-start.18) | collective-permute-done | bytes 65568 | tf_op jit(solution)/shard_map/ppermute | solution.py:546
  49.9 0.4 collective-permute-done.17.refs_1_
  50.3 0.9 %finish.1 = (f32[64,1536]{1,0:T(8,128)}, f32[64,512]{1,0:T(8,128)}) custom-call(f32[8,128]{1,0:T(8,128)S(1)} %get-tuple-element.92._, bf16[64,512]{1,0:T(8,128)(2,1)S(1)} %line_sum.1.refs_0_, bf16[64,512]{1,0:T(8,128)(2,1)S(1)} %collective-permute-done.17.refs_1_, bf16[64,512]{1,0:T(8,128)(2,1)S(1)} %collective-permute-done.18.refs_2_, ...), custom_call_target="tpu_custom_call" | custom-call | bytes 790528 | tf_op jit(solution)/shard_map/finish/pallas_call | solution.py:403
  (21 shorter events, 0.2 us)
Async XLA Ops:
  0.6 1.0 %copy-start.3 = (bf16[2,6,24,512]{3,2,1,0:T(8,128)(2,1)S(1)}, bf16[2,6,24,512]{3,2,1,0:T(8,128)(2,1)}, u32[]{:S(2)}) copy-start(bf16[2,6,24,512]{3,2,1,0:T(8,128)(2,1)} %param.5) | copy-start | bytes 884740
  0.6 1.0 %copy-start.2 = (bf16[2,6,24,512]{3,2,1,0:T(8,128)(2,1)S(1)}, bf16[2,6,24,512]{3,2,1,0:T(8,128)(2,1)}, u32[]{:S(2)}) copy-start(bf16[2,6,24,512]{3,2,1,0:T(8,128)(2,1)} %param.4) | copy-start | bytes 884740
  1.7 9.8 %copy-start.1 = (bf16[512,512]{1,0:T(8,128)(2,1)S(1)}, bf16[512,512]{1,0:T(8,128)(2,1)}, u32[]{:S(2)}) copy-start(bf16[512,512]{1,0:T(8,128)(2,1)} %refs_7_.1) | copy-start | bytes 1572868
  2.0 9.5 %copy-start = (bf16[512,1536]{1,0:T(8,128)(2,1)S(1)}, bf16[512,1536]{1,0:T(8,128)(2,1)}, u32[]{:S(2)}) copy-start(bf16[512,1536]{1,0:T(8,128)(2,1)} %refs_6_.1) | copy-start | bytes 4718596
  2.1 10.2 %collective-permute-start = (bf16[72,1024]{1,0:T(8,128)(2,1)S(1)}, bf16[72,1024]{1,0:T(8,128)(2,1)S(1)}, u32[]{:S(2)}, u32[]{:S(2)}) collective-permute-start(bf16[72,1024]{1,0:T(8,128)(2,1)S(1)} %get-tuple-element.62), channel_id=1, source_target_pairs={{0,24},{1,9},{2,26},{3,11},{4,28},{5,13},{6,30},{7,15},{8,0},{9,17... | collective-permute-start | bytes 442376 | tf_op jit(solution)/shard_map/ppermute | solution.py:457
  6.0 8.4 %collective-permute-start.1 = (bf16[36,1024]{1,0:T(8,128)(2,1)S(1)}, bf16[36,1024]{1,0:T(8,128)(2,1)S(1)}, u32[]{:S(2)}, u32[]{:S(2)}) collective-permute-start(bf16[36,1024]{1,0:T(8,128)(2,1)S(1)} %get-tuple-element.53._), channel_id=1, source_target_pairs={{0,7},{1,0},{2,1},{3,2},{4,3},{5,4},{6,5},{7,6},{8,15},{9,8},{10,9... | collective-permute-start | bytes 221192 | tf_op jit(solution)/shard_map/ppermute | solution.py:458
  8.4 5.9 %collective-permute-start.2 = (bf16[36,1024]{1,0:T(8,128)(2,1)S(1)}, bf16[36,1024]{1,0:T(8,128)(2,1)S(1)}, u32[]{:S(2)}, u32[]{:S(2)}) collective-permute-start(bf16[36,1024]{1,0:T(8,128)(2,1)S(1)} %get-tuple-element.66), channel_id=1, source_target_pairs={{0,24},{1,9},{2,26},{3,11},{4,28},{5,13},{6,30},{7,15},{8,0},{9,17... | collective-permute-start | bytes 221192 | tf_op jit(solution)/shard_map/ppermute | solution.py:459
  9.9 4.5 %collective-permute-start.3 = (bf16[36,1024]{1,0:T(8,128)(2,1)S(1)}, bf16[36,1024]{1,0:T(8,128)(2,1)S(1)}, u32[]{:S(2)}, u32[]{:S(2)}) collective-permute-start(bf16[36,1024]{1,0:T(8,128)(2,1)S(1)} %get-tuple-element.67), channel_id=1, source_target_pairs={{0,15},{1,24},{2,9},{3,26},{4,11},{5,28},{6,13},{7,30},{8,23},{9,0... | collective-permute-start | bytes 221192 | tf_op jit(solution)/shard_map/ppermute | solution.py:460
  16.8 1.6 %collective-permute-start.5 = (bf16[2,256,256]{2,1,0:T(8,128)(2,1)S(1)}, bf16[2,256,256]{2,1,0:T(8,128)(2,1)S(1)}, u32[]{:S(2)}, u32[]{:S(2)}) collective-permute-start(bf16[2,256,256]{2,1,0:T(8,128)(2,1)S(1)} %get-tuple-element.74), channel_id=1, source_target_pairs={{0,1},{1,0},{2,3},{3,2},{4,5},{5,4},{6,7},{7,6},{8,9},{9,8},{10,11... | collective-permute-start | bytes 786440 | tf_op jit(solution)/shard_map/ppermute | solution.py:483
  16.9 3.7 %collective-permute-start.4 = (bf16[2,256,256]{2,1,0:T(8,128)(2,1)S(1)}, bf16[2,256,256]{2,1,0:T(8,128)(2,1)S(1)}, u32[]{:S(2)}, u32[]{:S(2)}) collective-permute-start(bf16[2,256,256]{2,1,0:T(8,128)(2,1)S(1)} %get-tuple-element.72), channel_id=1, source_target_pairs={{0,1},{1,0},{2,3},{3,2},{4,5},{5,4},{6,7},{7,6},{8,9},{9,8},{10,11... | collective-permute-start | bytes 786440 | tf_op jit(solution)/shard_map/ppermute | solution.py:483
  18.4 11.5 %collective-permute-start.8 = (bf16[2,256,256]{2,1,0:T(8,128)(2,1)S(1)}, bf16[2,256,256]{2,1,0:T(8,128)(2,1)S(1)}, u32[]{:S(2)}, u32[]{:S(2)}) collective-permute-start(bf16[2,256,256]{2,1,0:T(8,128)(2,1)S(1)} %chip_sum.3.__._), channel_id=1, source_target_pairs={{0,8},{1,17},{2,10},{3,19},{4,12},{5,21},{6,14},{7,23},{8,0},{9,25... | collective-permute-start | bytes 786440 | tf_op jit(solution)/shard_map/ppermute | solution.py:492
  20.7 7.9 %collective-permute-start.10 = (bf16[2,256,256]{2,1,0:T(8,128)(2,1)S(1)}, bf16[2,256,256]{2,1,0:T(8,128)(2,1)S(1)}, u32[]{:S(2)}, u32[]{:S(2)}) collective-permute-start(bf16[2,256,256]{2,1,0:T(8,128)(2,1)S(1)} %chip_sum.2._), channel_id=1, source_target_pairs={{0,8},{1,17},{2,10},{3,19},{4,12},{5,21},{6,14},{7,23},{8,0},{9,25... | collective-permute-start | bytes 786440 | tf_op jit(solution)/shard_map/ppermute | solution.py:492
  21.7 6.9 %collective-permute-start.7 = (bf16[2,256,512]{2,1,0:T(8,128)(2,1)S(1)}, bf16[2,256,512]{2,1,0:T(8,128)(2,1)S(1)}, u32[]{:S(2)}, u32[]{:S(2)}) collective-permute-start(bf16[2,256,512]{2,1,0:T(8,128)(2,1)S(1)} %get-tuple-element.84), channel_id=1, source_target_pairs={{0,1},{1,0},{2,3},{3,2},{4,5},{5,4},{6,7},{7,6},{8,9},{9,8},{10,11... | collective-permute-start | bytes 1572872 | tf_op jit(solution)/shard_map/ppermute | solution.py:502
  22.8 5.7 %collective-permute-start.6 = (bf16[36,1024]{1,0:T(8,128)(2,1)S(1)}, bf16[36,1024]{1,0:T(8,128)(2,1)S(1)}, u32[]{:S(2)}, u32[]{:S(2)}) collective-permute-start(bf16[36,1024]{1,0:T(8,128)(2,1)S(1)} %pack_lon.1), channel_id=1, source_target_pairs={{7,0},{0,1},{1,2},{2,3},{3,4},{4,5},{5,6},{6,7},{15,8},{8,9},{9,10... | collective-permute-start | bytes 221192 | tf_op jit(solution)/shard_map/ppermute | solution.py:509
  28.7 5.0 %collective-permute-start.11 = (bf16[1,256,256]{2,1,0:T(8,128)(2,1)S(1)}, bf16[1,256,256]{2,1,0:T(8,128)(2,1)S(1)}, u32[]{:S(2)}, u32[]{:S(2)}) collective-permute-start(bf16[1,256,256]{2,1,0:T(8,128)(2,1)S(1)} %get-tuple-element.87), channel_id=1, source_target_pairs={{0,16},{1,9},{2,18},{3,11},{4,20},{5,13},{6,22},{7,15},{8,24},{9,1... | collective-permute-start | bytes 393224 | tf_op jit(solution)/shard_map/ppermute | solution.py:492
  30.0 6.0 %collective-permute-start.12 = (bf16[1,256,256]{2,1,0:T(8,128)(2,1)S(1)}, bf16[1,256,256]{2,1,0:T(8,128)(2,1)S(1)}, u32[]{:S(2)}, u32[]{:S(2)}) collective-permute-start(bf16[1,256,256]{2,1,0:T(8,128)(2,1)S(1)} %get-tuple-element.85._), channel_id=1, source_target_pairs={{0,16},{1,9},{2,18},{3,11},{4,20},{5,13},{6,22},{7,15},{8,24},{9,1... | collective-permute-start | bytes 393224 | tf_op jit(solution)/shard_map/ppermute | solution.py:492
  31.1 10.5 %collective-permute-start.9 = (bf16[36,1024]{1,0:T(8,128)(2,1)S(1)}, bf16[36,1024]{1,0:T(8,128)(2,1)S(1)}, u32[]{:S(2)}, u32[]{:S(2)}) collective-permute-start(bf16[36,1024]{1,0:T(8,128)(2,1)S(1)} %pack_diag.1), channel_id=1, source_target_pairs={{15,0},{24,1},{9,2},{26,3},{11,4},{28,5},{13,6},{30,7},{23,8},{0,9... | collective-permute-start | bytes 221192 | tf_op jit(solution)/shard_map/ppermute | solution.py:523
  36.1 6.5 %collective-permute-start.14 = (bf16[64,512]{1,0:T(8,128)(2,1)S(1)}, bf16[64,512]{1,0:T(8,128)(2,1)S(1)}, u32[]{:S(2)}, u32[]{:S(2)}) collective-permute-start(bf16[64,512]{1,0:T(8,128)(2,1)S(1)} %get-tuple-element.94), channel_id=1, source_target_pairs={{0,6},{1,7},{2,4},{3,5},{4,2},{5,3},{6,0},{7,1},{8,14},{9,15},{10,... | collective-permute-start | bytes 196616 | tf_op jit(solution)/shard_map/ppermute | solution.py:532
  38.8 5.2 %collective-permute-start.15 = (bf16[64,512]{1,0:T(8,128)(2,1)S(1)}, bf16[64,512]{1,0:T(8,128)(2,1)S(1)}, u32[]{:S(2)}, u32[]{:S(2)}) collective-permute-start(bf16[64,512]{1,0:T(8,128)(2,1)S(1)} %get-tuple-element.95), channel_id=1, source_target_pairs={{0,4},{1,5},{2,6},{3,7},{4,0},{5,1},{6,2},{7,3},{8,12},{9,13},{10,... | collective-permute-start | bytes 196616 | tf_op jit(solution)/shard_map/ppermute | solution.py:532
  38.8 5.2 %collective-permute-start.16 = (bf16[64,512]{1,0:T(8,128)(2,1)S(1)}, bf16[64,512]{1,0:T(8,128)(2,1)S(1)}, u32[]{:S(2)}, u32[]{:S(2)}) collective-permute-start(bf16[64,512]{1,0:T(8,128)(2,1)S(1)} %get-tuple-element.89._), channel_id=1, source_target_pairs={{0,2},{1,3},{2,0},{3,1},{4,6},{5,7},{6,4},{7,5},{8,10},{9,11},{10,... | collective-permute-start | bytes 196616 | tf_op jit(solution)/shard_map/ppermute | solution.py:532
  40.7 7.7 %collective-permute-start.13 = (bf16[108,1024]{1,0:T(8,128)(2,1)S(1)}, bf16[108,1024]{1,0:T(8,128)(2,1)S(1)}, u32[]{:S(2)}, u32[]{:S(2)}) collective-permute-start(bf16[108,1024]{1,0:T(8,128)(2,1)S(1)} %pack_lat.1), channel_id=1, source_target_pairs={{24,0},{9,1},{26,2},{11,3},{28,4},{13,5},{30,6},{15,7},{0,8},{17,9... | collective-permute-start | bytes 663560 | tf_op jit(solution)/shard_map/ppermute | solution.py:538
  44.0 5.4 %collective-permute-start.19 = (bf16[64,512]{1,0:T(8,128)(2,1)S(1)}, bf16[64,512]{1,0:T(8,128)(2,1)S(1)}, u32[]{:S(2)}, u32[]{:S(2)}) collective-permute-start(bf16[64,512]{1,0:T(8,128)(2,1)S(1)} %line_sum.1.refs_0_), channel_id=1, source_target_pairs={{0,24},{8,16},{16,8},{24,0},{1,25},{9,17},{17,9},{25,1},{2,26},{10... | collective-permute-start | bytes 196616 | tf_op jit(solution)/shard_map/ppermute | solution.py:546
  45.4 4.5 %collective-permute-start.18 = (bf16[64,512]{1,0:T(8,128)(2,1)S(1)}, bf16[64,512]{1,0:T(8,128)(2,1)S(1)}, u32[]{:S(2)}, u32[]{:S(2)}) collective-permute-start(bf16[64,512]{1,0:T(8,128)(2,1)S(1)} %line_sum.1.refs_0_), channel_id=1, source_target_pairs={{0,16},{8,24},{16,0},{24,8},{1,17},{9,25},{17,1},{25,9},{2,18},{10... | collective-permute-start | bytes 196616 | tf_op jit(solution)/shard_map/ppermute | solution.py:546
  46.1 4.3 %collective-permute-start.17 = (bf16[64,512]{1,0:T(8,128)(2,1)S(1)}, bf16[64,512]{1,0:T(8,128)(2,1)S(1)}, u32[]{:S(2)}, u32[]{:S(2)}) collective-permute-start(bf16[64,512]{1,0:T(8,128)(2,1)S(1)} %line_sum.1.refs_0_), channel_id=1, source_target_pairs={{0,8},{8,0},{16,24},{24,16},{1,9},{9,1},{17,25},{25,17},{2,10},{10... | collective-permute-start | bytes 196616 | tf_op jit(solution)/shard_map/ppermute | solution.py:546

commit v18 on v17

--- a/solution.py
+++ b/solution.py
@@ -23,6 +23,7 @@
 epsilon = 1e-05
 LONG = 13 * 10**8
 LOAD = 5 * 10**9
+LATER = 10**9
 PARTS = 5 * 10**9
 BF = jnp.bfloat16
 F32 = jnp.float32
@@ -345,7 +346,7 @@
 
 
 def halve_kernel(chunk, _, *refs):
-    *parts, send, keep = refs
+    *parts, _, send, keep = refs
     width = send.shape[2]
 
     def lanes(part):
@@ -356,8 +357,8 @@
             out[slot] = sum(part[source, :, lanes(part)].astype(F32) for part in parts).astype(BF)
 
 
-def line_parts_kernel(count, *refs):
-    chunks, (keep, *sends) = (refs[:count], refs[count : 2 * count]), refs[2 * count :]
+def line_parts_kernel(*refs):
+    chunks, (keep, *sends) = (refs[:1], refs[1:3]), refs[3:]
     rows = keep.shape[0]
     for step, out in enumerate((keep, *sends)):
         at = slice(step * rows, (step + 1) * rows)
@@ -365,7 +366,7 @@
         out[...] = jnp.concatenate(totals, axis=1).astype(out.dtype)
 
 
-def line_sum_kernel(_, *refs):
+def next_sum_kernel(_, *refs):
     sum_kernel(*refs)
 
 
@@ -492,9 +493,10 @@
         return lax.ppermute(send, both, route)
 
     bits = lat_size.bit_length() - 1
-    sends = [
-        call(sum_kernel, [chunk], mine, theirs, name="chip_sum")[0] for mine, theirs in zip(keep, arrived)
-    ]
+    sends = [keep[0]]
+    for mine, theirs in zip(keep, arrived):
+        sends += call(next_sum_kernel, [chunk], sends[-1], mine, theirs, name="chip_sum", unread=(0,))
+    sends = sends[1:]
     received = [halving(0, send) for send in sends]
     send_rest, keep_rest = call(
         rest_kernel, [halves, halves], *sends, *inner[2:], *outer[2:], name="rest", unread=(0, 1), beside=True
@@ -512,21 +514,26 @@
     for phase in range(1, bits):
         slots //= 2
         stay = ((slots, *chunk[0][1:]), BF)
-        for index, after in enumerate((lon_home, sends[1])):
+        after = results[0]
+        for index in range(2):
             send, keep = call(
                 functools.partial(halve_kernel, index), [stay, stay], after, *kept[index],
-                name=f"halve{slots}", unread=(0,),
+                after, name=f"halve{slots}", unread=(0, 1 + len(kept[index])),
             )
             kept[index] = [keep, halving(phase, send)]
+            after = send
 
     (diag_back,) = call(pack_diag_kernel, [quarter], send, results[1], name="pack_diag", unread=(0,))
     diag_home = lax.ppermute(diag_back, both, back(diag_route))
 
     rows = width // lon_size
     share = ((rows, split[2]), BF)
+    (first_chunk,) = call(
+        next_sum_kernel, [((1, split[1], split[2] // 2), F32)], lon_home, *kept[0],
+        name="first_chunk", flops=LATER, unread=(0,),
+    )
     parts = call(
-        functools.partial(line_parts_kernel, len(kept[0])), [share] * (lon_size // 2), *kept[0], *kept[1],
-        name="line_parts", flops=PARTS,
+        line_parts_kernel, [share] * (lon_size // 2), first_chunk, *kept[1], name="line_parts", flops=PARTS
     )
     arrived = [
         lax.ppermute(parts[step], "lon", [(j, j ^ (2 * step)) for j in range(lon_size)])
@@ -540,7 +547,7 @@
         place_kernel, [((TOKENS, 2 * width), F32)], *results, lon_home, diag_home, name="place"
     )
     (line_sum,) = call(
-        line_sum_kernel, [share], placed, parts[0], *arrived, name="line_sum", flops=LONG, unread=(0,)
+        next_sum_kernel, [share], placed, parts[0], *arrived, name="line_sum", flops=LONG, unread=(0,)
     )
     shared = [
         lax.ppermute(line_sum, "lat", [(i, i ^ step) for i in range(lat_size)]) for step in range(1, lat_size)

time: 51.3 us -> 50 us (0.975)
  waiting for transfers between devices: 13.9 us -> 10.8 us
  starting transfers between devices: 23.7 us -> 25.6 us
    ppermute x1, waiting for transfers between devices: 5.17 us -> 2.15 us  [per_device(): lon_home = lax.ppermute(lon_back, both, back(lon_route))]
    ppermute x4, starting transfers between devices: 4.66 us -> 5.72 us  [halving(): return lax.ppermute(send, both, route)]
    ppermute x1, waiting for transfers between devices: 0.79 us -> 0.01 us  [per_device(): lat_home = lax.ppermute(lat_back, both, back(lat_route))]
    ppermute x1, starting transfers between devices: 0.97 us -> 1.73 us  [per_device(): lat_home = lax.ppermute(lat_back, both, back(lat_route))]
    pallas_call x21 -> x22, Pallas kernels: 11.8 us -> 11.8 us  [call(): pl.pallas_call(kernel, out_shape=shapes, in_specs=[anywhere if i in unrea...]
where the time goes in v18:
time: 50 us; the launch traced here: 49.9 us
  starting transfers between devices  25.6 us (51%)
  Pallas kernels  11.8 us (24%)
  waiting for transfers between devices  10.8 us (22%)
  local copies, waits for them, and re-layouts  0.94 us (2%)
  between operations  0.82 us (2%)
    pallas_call x22, Pallas kernels, call(): pl.pallas_call(kernel, out_shape=shapes, in_specs=[anywhere if i in unrea...  11.8 us
    ppermute x4, starting transfers between devices, halving(): return lax.ppermute(send, both, route)  5.72 us
    ppermute x3, starting transfers between devices, per_device(): lax.ppermute(parts[step], 'lon', [(j, j ^ 2 * step) for j in range(lon_si...  4.96 us
    ppermute x4, waiting for transfers between devices, halving(): return lax.ppermute(send, both, route)  4.71 us
    ppermute x1, starting transfers between devices, per_device(): inner_in = lax.ppermute(inner_lat, both, lat_route)  3.94 us
    ppermute x3, starting transfers between devices, per_device(): lax.ppermute(line_sum, 'lat', [(i, i ^ step) for i in range(lat_size)])  3.55 us
    ppermute x1, waiting for transfers between devices, per_device(): lon_home = lax.ppermute(lon_back, both, back(lon_route))  2.15 us
    ppermute x3, waiting for transfers between devices, per_device(): lax.ppermute(parts[step], 'lon', [(j, j ^ 2 * step) for j in range(lon_si...  1.94 us
  transfers between devices with their start and end apart: 20, of which 9 were waited for; matrix products, arithmetic and copies ran while one was open for 0% of the time, Pallas kernels for 16%

profile of v18, /device:TPU:0, one launch (start us, length us, event | category | flops | bytes accessed | tf_op | source)
XLA Modules:
  0.0 49.9 jit_solution(806381163145356295)
XLA Ops:
  0.7 0.1 order.1
  0.8 0.8 %copy-done.3 = bf16[2,6,24,512]{3,2,1,0:T(8,128)(2,1)S(1)} copy-done((bf16[2,6,24,512]{3,2,1,0:T(8,128)(2,1)S(1)}, bf16[2,6,24,512]{3,2,1,0:T(8,128)(2,1)}, u32[]{:S(2)}) %copy-start.3) | copy-done | bytes 294936
  1.6 0.1 copy-done.2
  1.7 0.4 pack.1
  2.1 3.9 %collective-permute-start = (bf16[72,1024]{1,0:T(8,128)(2,1)S(1)}, bf16[72,1024]{1,0:T(8,128)(2,1)S(1)}, u32[]{:S(2)}, u32[]{:S(2)}) collective-permute-start(bf16[72,1024]{1,0:T(8,128)(2,1)S(1)} %get-tuple-element.62), channel_id=1, source_target_pairs={{0,24},{1,9},{2,26},{3,11},{4,28},{5,13},{6,30},{7,15},{8,0},{9,17... | collective-permute-start | bytes 442376 | tf_op jit(solution)/shard_map/ppermute | solution.py:458
  6.0 1.8 %collective-permute-start.1 = (bf16[36,1024]{1,0:T(8,128)(2,1)S(1)}, bf16[36,1024]{1,0:T(8,128)(2,1)S(1)}, u32[]{:S(2)}, u32[]{:S(2)}) collective-permute-start(bf16[36,1024]{1,0:T(8,128)(2,1)S(1)} %get-tuple-element.53._), channel_id=1, source_target_pairs={{0,7},{1,0},{2,1},{3,2},{4,3},{5,4},{6,5},{7,6},{8,15},{9,8},{10,9... | collective-permute-start | bytes 221192 | tf_op jit(solution)/shard_map/ppermute | solution.py:459
  7.8 0.6 %pack_rest.1 = (bf16[36,1024]{1,0:T(8,128)(2,1)S(1)}, bf16[36,1024]{1,0:T(8,128)(2,1)S(1)}, f32[72,1024]{1,0:T(8,128)S(1)}, f32[72,1024]{1,0:T(8,128)S(1)}) custom-call(bf16[36,1024]{1,0:T(8,128)(2,1)S(1)} %get-tuple-element.53._, bf16[288,512]{1,0:T(8,128)(2,1)S(1)} %bitcast.6, bf16[288,512]{1,0:T(8,128)(2,1)S(1)} %bitcast.8, ...), custom_call_target="tpu_custom_call" | custom-call | flops 500000000 | bytes 1525248 | tf_op jit(solution)/shard_map/pack_rest/pallas_call | solution.py:404
  8.4 1.5 %collective-permute-start.2 = (bf16[36,1024]{1,0:T(8,128)(2,1)S(1)}, bf16[36,1024]{1,0:T(8,128)(2,1)S(1)}, u32[]{:S(2)}, u32[]{:S(2)}) collective-permute-start(bf16[36,1024]{1,0:T(8,128)(2,1)S(1)} %get-tuple-element.66), channel_id=1, source_target_pairs={{0,24},{1,9},{2,26},{3,11},{4,28},{5,13},{6,30},{7,15},{8,0},{9,17... | collective-permute-start | bytes 221192 | tf_op jit(solution)/shard_map/ppermute | solution.py:460
  9.9 1.6 %collective-permute-start.3 = (bf16[36,1024]{1,0:T(8,128)(2,1)S(1)}, bf16[36,1024]{1,0:T(8,128)(2,1)S(1)}, u32[]{:S(2)}, u32[]{:S(2)}) collective-permute-start(bf16[36,1024]{1,0:T(8,128)(2,1)S(1)} %get-tuple-element.67), channel_id=1, source_target_pairs={{0,15},{1,24},{2,9},{3,26},{4,11},{5,28},{6,13},{7,30},{8,23},{9,0... | collective-permute-start | bytes 221192 | tf_op jit(solution)/shard_map/ppermute | solution.py:461
  11.5 0.7 %own.1 = (f32[72,512]{1,0:T(8,128)S(1)}, f32[72,1536]{1,0:T(8,128)S(1)}, f32[72,512]{1,0:T(8,128)S(1)}) custom-call(f32[72,1024]{1,0:T(8,128)S(1)} %get-tuple-element.58.inner_own.own, bf16[512,1536]{1,0:T(8,128)(2,1)S(1)} %copy-done, bf16[512,512]{1,0:T(8,128)(2,1)S(1)} %copy-done.1), custom_call_target="tpu_custom_call" | custom-call | flops 500000000 | bytes 3129344 | tf_op jit(solution)/shard_map/own/pallas_call | solution.py:404
  12.2 2.1 %inner.1 = (f32[2,256,512]{2,1,0:T(8,128)S(1)}, bf16[144,512]{1,0:T(8,128)(2,1)S(1)}, bf16[144,512]{1,0:T(8,128)(2,1)S(1)}, bf16[2,256,144]{2,1,0:T(8,128)(2,1)S...) custom-call(f32[72,1024]{1,0:T(8,128)S(1)} %get-tuple-element.58.inner_own.own, ...), custom_call_target="tpu_custom_call" | custom-call | flops 1000000000 | bytes 5505024 | tf_op jit(solution)/shard_map/inner/pallas_call | solution.py:404
  14.4 2.4 %outer.1 = (bf16[2,256,256]{2,1,0:T(8,128)(2,1)S(1)}, bf16[2,256,256]{2,1,0:T(8,128)(2,1)S(1)}, bf16[144,512]{1,0:T(8,128)(2,1)S(1)}, bf16[144,512]{1,0:T(8,128)...) custom-call(f32[72,1024]{1,0:T(8,128)S(1)} %get-tuple-element.65.own, ...), custom_call_target="tpu_custom_call" | custom-call | flops 1000000000 | bytes 5365760 | tf_op jit(solution)/shard_map/outer/pallas_call | solution.py:404
  16.8 0.1 collective-permute-start.4
  16.9 0.4 collective-permute-start.5
  17.3 0.4 keep.1
  17.8 0.6 %collective-permute-done.4.refs_1_ = bf16[2,256,256]{2,1,0:T(8,128)(2,1)S(1)} collective-permute-done((bf16[2,256,256]{2,1,0:T(8,128)(2,1)S(1)}, bf16[2,256,256]{2,1,0:T(8,128)(2,1)S(1)}, u32[]{:S(2)}, u32[]{:S(2)}) %collective-permute-start.4) | collective-permute-done | bytes 262176 | tf_op jit(solution)/shard_map/ppermute | solution.py:484
  18.4 0.1 chip_sum.2._
  18.4 2.2 %collective-permute-start.8 = (bf16[2,256,256]{2,1,0:T(8,128)(2,1)S(1)}, bf16[2,256,256]{2,1,0:T(8,128)(2,1)S(1)}, u32[]{:S(2)}, u32[]{:S(2)}) collective-permute-start(bf16[2,256,256]{2,1,0:T(8,128)(2,1)S(1)} %chip_sum.2._), channel_id=1, source_target_pairs={{0,8},{1,17},{2,10},{3,19},{4,12},{5,21},{6,14},{7,23},{8,0},{9,25... | collective-permute-start | bytes 786440 | tf_op jit(solution)/shard_map/ppermute | solution.py:493
  20.6 0.1 chip_sum.3.__
  20.7 0.3 collective-permute-start.9
  21.0 0.7 %rest.1 = (bf16[2,256,512]{2,1,0:T(8,128)(2,1)S(1)}, bf16[2,256,512]{2,1,0:T(8,128)(2,1)S(1)}) custom-call(bf16[2,256,256]{2,1,0:T(8,128)(2,1)S(1)} %chip_sum.2._, bf16[2,256,256]{2,1,0:T(8,128)(2,1)S(1)} %chip_sum.3.__, bf16[2,256,144]{2,1,0:T(8,128)(2,1)S(1)} %get-tuple-element.63.refs_0_, bf16[144,2048]{1,0:T(8,128)(2,1)S(1)} %get-tuple-element.64.refs_1_.refs_2_, ...), custom_call_target="tpu_custom_call" | custom-call | tf_op jit(solution)/shard_map/rest/pallas_call | solution.py:404
  21.7 0.1 collective-permute-start.7
  21.8 0.9 %outputs.1 = (bf16[144,1024]{1,0:T(8,128)(2,1)S(1)}, bf16[144,1024]{1,0:T(8,128)(2,1)S(1)}) custom-call(bf16[2,256,512]{2,1,0:T(8,128)(2,1)S(1)} %get-tuple-element.77._.refs_0_, bf16[144,512]{1,0:T(8,128)(2,1)S(1)} %get-tuple-element.78.refs_0_, bf16[144,512]{1,0:T(8,128)(2,1)S(1)} %get-tuple-element.79.refs_1_, ...), custom_call_target="tpu_custom_call" | custom-call | flops 10000000000 | bytes 4980736 | tf_op jit(solution)/shard_map/outputs/pallas_call | solution.py:404
  22.7 2.3 %collective-permute-done.8.refs_2_ = bf16[2,256,256]{2,1,0:T(8,128)(2,1)S(1)} collective-permute-done((bf16[2,256,256]{2,1,0:T(8,128)(2,1)S(1)}, bf16[2,256,256]{2,1,0:T(8,128)(2,1)S(1)}, u32[]{:S(2)}, u32[]{:S(2)}) %collective-permute-start.8) | collective-permute-done | bytes 262176 | tf_op jit(solution)/shard_map/ppermute | solution.py:493
  25.0 0.1 halve1.2
  25.1 1.5 %collective-permute-start.11 = (bf16[1,256,256]{2,1,0:T(8,128)(2,1)S(1)}, bf16[1,256,256]{2,1,0:T(8,128)(2,1)S(1)}, u32[]{:S(2)}, u32[]{:S(2)}) collective-permute-start(bf16[1,256,256]{2,1,0:T(8,128)(2,1)S(1)} %get-tuple-element.85._.refs_3_), channel_id=1, source_target_pairs={{0,16},{1,9},{2,18},{3,11},{4,20},{5,13},{6,22},{7,15},{8,24},{9,1... | collective-permute-start | bytes 393224 | tf_op jit(solution)/shard_map/ppermute | solution.py:493
  26.5 0.1 pack_lon.1
  26.8 1.4 %collective-permute-done.9.refs_2_ = bf16[2,256,256]{2,1,0:T(8,128)(2,1)S(1)} collective-permute-done((bf16[2,256,256]{2,1,0:T(8,128)(2,1)S(1)}, bf16[2,256,256]{2,1,0:T(8,128)(2,1)S(1)}, u32[]{:S(2)}, u32[]{:S(2)}) %collective-permute-start.9) | collective-permute-done | bytes 262176 | tf_op jit(solution)/shard_map/ppermute | solution.py:493
  28.2 0.1 halve1.3
  28.3 1.8 %collective-permute-start.12 = (bf16[1,256,256]{2,1,0:T(8,128)(2,1)S(1)}, bf16[1,256,256]{2,1,0:T(8,128)(2,1)S(1)}, u32[]{:S(2)}, u32[]{:S(2)}) collective-permute-start(bf16[1,256,256]{2,1,0:T(8,128)(2,1)S(1)} %get-tuple-element.86._), channel_id=1, source_target_pairs={{0,16},{1,9},{2,18},{3,11},{4,20},{5,13},{6,22},{7,15},{8,24},{9,1... | collective-permute-start | bytes 393224 | tf_op jit(solution)/shard_map/ppermute | solution.py:493
  30.0 0.1 pack_diag.1
  30.2 0.1 collective-permute-start.10
  30.3 2.1 %collective-permute-done.6.lon_in._ = bf16[36,1024]{1,0:T(8,128)(2,1)S(1)} collective-permute-done((bf16[36,1024]{1,0:T(8,128)(2,1)S(1)}, bf16[36,1024]{1,0:T(8,128)(2,1)S(1)}, u32[]{:S(2)}, u32[]{:S(2)}) %collective-permute-start.6) | collective-permute-done | bytes 73760 | tf_op jit(solution)/shard_map/ppermute | solution.py:511
  32.4 1.0 %collective-permute-done.12.refs_2_ = bf16[1,256,256]{2,1,0:T(8,128)(2,1)S(1)} collective-permute-done((bf16[1,256,256]{2,1,0:T(8,128)(2,1)S(1)}, bf16[1,256,256]{2,1,0:T(8,128)(2,1)S(1)}, u32[]{:S(2)}, u32[]{:S(2)}) %collective-permute-start.12) | collective-permute-done | bytes 131104 | tf_op jit(solution)/shard_map/ppermute | solution.py:493
  33.5 4.3 %collective-permute-start.14 = (bf16[64,512]{1,0:T(8,128)(2,1)S(1)}, bf16[64,512]{1,0:T(8,128)(2,1)S(1)}, u32[]{:S(2)}, u32[]{:S(2)}) collective-permute-start(bf16[64,512]{1,0:T(8,128)(2,1)S(1)} %get-tuple-element.94), channel_id=1, source_target_pairs={{0,6},{1,7},{2,4},{3,5},{4,2},{5,3},{6,0},{7,1},{8,14},{9,15},{10,... | collective-permute-start | bytes 196616 | tf_op jit(solution)/shard_map/ppermute | solution.py:539
  37.8 0.6 %collective-permute-start.16 = (bf16[64,512]{1,0:T(8,128)(2,1)S(1)}, bf16[64,512]{1,0:T(8,128)(2,1)S(1)}, u32[]{:S(2)}, u32[]{:S(2)}) collective-permute-start(bf16[64,512]{1,0:T(8,128)(2,1)S(1)} %get-tuple-element.89._), channel_id=1, source_target_pairs={{0,2},{1,3},{2,0},{3,1},{4,6},{5,7},{6,4},{7,5},{8,10},{9,11},{10,... | collective-permute-start | bytes 196616 | tf_op jit(solution)/shard_map/ppermute | solution.py:539
  38.4 0.1 pack_lat.1
  38.6 1.7 %collective-permute-start.13 = (bf16[108,1024]{1,0:T(8,128)(2,1)S(1)}, bf16[108,1024]{1,0:T(8,128)(2,1)S(1)}, u32[]{:S(2)}, u32[]{:S(2)}) collective-permute-start(bf16[108,1024]{1,0:T(8,128)(2,1)S(1)} %pack_lat.1), channel_id=1, source_target_pairs={{24,0},{9,1},{26,2},{11,3},{28,4},{13,5},{30,6},{15,7},{0,8},{17,9... | collective-permute-start | bytes 663560 | tf_op jit(solution)/shard_map/ppermute | solution.py:545
  40.3 0.8 %place.1.placed._ = f32[288,1024]{1,0:T(8,128)S(1)} custom-call(bf16[144,1024]{1,0:T(8,128)(2,1)S(1)} %get-tuple-element.82._.refs_3_.inner_results, bf16[144,1024]{1,0:T(8,128)(2,1)S(1)} %get-tuple-element.83.outer_results, bf16[36,1024]{1,0:T(8,128)(2,1)S(1)} %collective-permute-done.6.lon_in._, bf16[36,1024]{1,0:T(8,128)(2,1)S(1)} %collective-permute-done.10.diag_in), custom_call_target="tpu_custom_call" | custom-call | bytes 1916928 | tf_op jit(solution)/shard_map/place/pallas_call | solution.py:404
  41.1 1.9 %collective-permute-done.15.refs_2_ = bf16[64,512]{1,0:T(8,128)(2,1)S(1)} collective-permute-done((bf16[64,512]{1,0:T(8,128)(2,1)S(1)}, bf16[64,512]{1,0:T(8,128)(2,1)S(1)}, u32[]{:S(2)}, u32[]{:S(2)}) %collective-permute-start.15) | collective-permute-done | bytes 65568 | tf_op jit(solution)/shard_map/ppermute | solution.py:539
  43.1 0.9 %collective-permute-start.19 = (bf16[64,512]{1,0:T(8,128)(2,1)S(1)}, bf16[64,512]{1,0:T(8,128)(2,1)S(1)}, u32[]{:S(2)}, u32[]{:S(2)}) collective-permute-start(bf16[64,512]{1,0:T(8,128)(2,1)S(1)} %line_sum.1.refs_0_), channel_id=1, source_target_pairs={{0,24},{8,16},{16,8},{24,0},{1,25},{9,17},{17,9},{25,1},{2,26},{10... | collective-permute-start | bytes 196616 | tf_op jit(solution)/shard_map/ppermute | solution.py:553
  44.0 0.8 %collective-permute-start.18 = (bf16[64,512]{1,0:T(8,128)(2,1)S(1)}, bf16[64,512]{1,0:T(8,128)(2,1)S(1)}, u32[]{:S(2)}, u32[]{:S(2)}) collective-permute-start(bf16[64,512]{1,0:T(8,128)(2,1)S(1)} %line_sum.1.refs_0_), channel_id=1, source_target_pairs={{0,16},{8,24},{16,0},{24,8},{1,17},{9,25},{17,1},{25,9},{2,18},{10... | collective-permute-start | bytes 196616 | tf_op jit(solution)/shard_map/ppermute | solution.py:553
  44.8 1.9 %collective-permute-start.17 = (bf16[64,512]{1,0:T(8,128)(2,1)S(1)}, bf16[64,512]{1,0:T(8,128)(2,1)S(1)}, u32[]{:S(2)}, u32[]{:S(2)}) collective-permute-start(bf16[64,512]{1,0:T(8,128)(2,1)S(1)} %line_sum.1.refs_0_), channel_id=1, source_target_pairs={{0,8},{8,0},{16,24},{24,16},{1,9},{9,1},{17,25},{25,17},{2,10},{10... | collective-permute-start | bytes 196616 | tf_op jit(solution)/shard_map/ppermute | solution.py:553
  46.6 1.0 %place_rest.1 = (bf16[288,512]{1,0:T(8,128)(2,1)}, bf16[288,512]{1,0:T(8,128)(2,1)}, f32[8,128]{1,0:T(8,128)S(1)}) custom-call(f32[288,1024]{1,0:T(8,128)S(1)} %place.1.placed._, bf16[108,1024]{1,0:T(8,128)(2,1)S(1)} %collective-permute-done.13.lat_in), custom_call_target="tpu_custom_call" | custom-call | bytes 1994752 | tf_op jit(solution)/shard_map/place_rest/pallas_call | solution.py:404
  47.7 0.7 %collective-permute-done.19.refs_3_ = bf16[64,512]{1,0:T(8,128)(2,1)S(1)} collective-permute-done((bf16[64,512]{1,0:T(8,128)(2,1)S(1)}, bf16[64,512]{1,0:T(8,128)(2,1)S(1)}, u32[]{:S(2)}, u32[]{:S(2)}) %collective-permute-start.19) | collective-permute-done | bytes 65568 | tf_op jit(solution)/shard_map/ppermute | solution.py:553
  48.4 0.5 %collective-permute-done.18.refs_2_ = bf16[64,512]{1,0:T(8,128)(2,1)S(1)} collective-permute-done((bf16[64,512]{1,0:T(8,128)(2,1)S(1)}, bf16[64,512]{1,0:T(8,128)(2,1)S(1)}, u32[]{:S(2)}, u32[]{:S(2)}) %collective-permute-start.18) | collective-permute-done | bytes 65568 | tf_op jit(solution)/shard_map/ppermute | solution.py:553
  48.9 0.1 collective-permute-done.17.refs_1_
  49.0 0.9 %finish.1 = (f32[64,1536]{1,0:T(8,128)}, f32[64,512]{1,0:T(8,128)}) custom-call(f32[8,128]{1,0:T(8,128)S(1)} %get-tuple-element.92._, bf16[64,512]{1,0:T(8,128)(2,1)S(1)} %line_sum.1.refs_0_, bf16[64,512]{1,0:T(8,128)(2,1)S(1)} %collective-permute-done.17.refs_1_, bf16[64,512]{1,0:T(8,128)(2,1)S(1)} %collective-permute-done.18.refs_2_, ...), custom_call_target="tpu_custom_call" | custom-call | bytes 790528 | tf_op jit(solution)/shard_map/finish/pallas_call | solution.py:404
  (22 shorter events, 0.2 us)
Async XLA Ops:
  0.6 1.0 %copy-start.3 = (bf16[2,6,24,512]{3,2,1,0:T(8,128)(2,1)S(1)}, bf16[2,6,24,512]{3,2,1,0:T(8,128)(2,1)}, u32[]{:S(2)}) copy-start(bf16[2,6,24,512]{3,2,1,0:T(8,128)(2,1)} %param.5) | copy-start | bytes 884740
  0.6 1.0 %copy-start.2 = (bf16[2,6,24,512]{3,2,1,0:T(8,128)(2,1)S(1)}, bf16[2,6,24,512]{3,2,1,0:T(8,128)(2,1)}, u32[]{:S(2)}) copy-start(bf16[2,6,24,512]{3,2,1,0:T(8,128)(2,1)} %param.4) | copy-start | bytes 884740
  1.7 9.8 %copy-start.1 = (bf16[512,512]{1,0:T(8,128)(2,1)S(1)}, bf16[512,512]{1,0:T(8,128)(2,1)}, u32[]{:S(2)}) copy-start(bf16[512,512]{1,0:T(8,128)(2,1)} %refs_7_.1) | copy-start | bytes 1572868
  2.0 9.5 %copy-start = (bf16[512,1536]{1,0:T(8,128)(2,1)S(1)}, bf16[512,1536]{1,0:T(8,128)(2,1)}, u32[]{:S(2)}) copy-start(bf16[512,1536]{1,0:T(8,128)(2,1)} %refs_6_.1) | copy-start | bytes 4718596
  2.1 10.2 %collective-permute-start = (bf16[72,1024]{1,0:T(8,128)(2,1)S(1)}, bf16[72,1024]{1,0:T(8,128)(2,1)S(1)}, u32[]{:S(2)}, u32[]{:S(2)}) collective-permute-start(bf16[72,1024]{1,0:T(8,128)(2,1)S(1)} %get-tuple-element.62), channel_id=1, source_target_pairs={{0,24},{1,9},{2,26},{3,11},{4,28},{5,13},{6,30},{7,15},{8,0},{9,17... | collective-permute-start | bytes 442376 | tf_op jit(solution)/shard_map/ppermute | solution.py:458
  6.0 8.4 %collective-permute-start.1 = (bf16[36,1024]{1,0:T(8,128)(2,1)S(1)}, bf16[36,1024]{1,0:T(8,128)(2,1)S(1)}, u32[]{:S(2)}, u32[]{:S(2)}) collective-permute-start(bf16[36,1024]{1,0:T(8,128)(2,1)S(1)} %get-tuple-element.53._), channel_id=1, source_target_pairs={{0,7},{1,0},{2,1},{3,2},{4,3},{5,4},{6,5},{7,6},{8,15},{9,8},{10,9... | collective-permute-start | bytes 221192 | tf_op jit(solution)/shard_map/ppermute | solution.py:459
  8.4 5.9 %collective-permute-start.2 = (bf16[36,1024]{1,0:T(8,128)(2,1)S(1)}, bf16[36,1024]{1,0:T(8,128)(2,1)S(1)}, u32[]{:S(2)}, u32[]{:S(2)}) collective-permute-start(bf16[36,1024]{1,0:T(8,128)(2,1)S(1)} %get-tuple-element.66), channel_id=1, source_target_pairs={{0,24},{1,9},{2,26},{3,11},{4,28},{5,13},{6,30},{7,15},{8,0},{9,17... | collective-permute-start | bytes 221192 | tf_op jit(solution)/shard_map/ppermute | solution.py:460
  9.9 4.5 %collective-permute-start.3 = (bf16[36,1024]{1,0:T(8,128)(2,1)S(1)}, bf16[36,1024]{1,0:T(8,128)(2,1)S(1)}, u32[]{:S(2)}, u32[]{:S(2)}) collective-permute-start(bf16[36,1024]{1,0:T(8,128)(2,1)S(1)} %get-tuple-element.67), channel_id=1, source_target_pairs={{0,15},{1,24},{2,9},{3,26},{4,11},{5,28},{6,13},{7,30},{8,23},{9,0... | collective-permute-start | bytes 221192 | tf_op jit(solution)/shard_map/ppermute | solution.py:461
  16.8 1.6 %collective-permute-start.4 = (bf16[2,256,256]{2,1,0:T(8,128)(2,1)S(1)}, bf16[2,256,256]{2,1,0:T(8,128)(2,1)S(1)}, u32[]{:S(2)}, u32[]{:S(2)}) collective-permute-start(bf16[2,256,256]{2,1,0:T(8,128)(2,1)S(1)} %get-tuple-element.72), channel_id=1, source_target_pairs={{0,1},{1,0},{2,3},{3,2},{4,5},{5,4},{6,7},{7,6},{8,9},{9,8},{10,11... | collective-permute-start | bytes 786440 | tf_op jit(solution)/shard_map/ppermute | solution.py:484
  16.9 3.7 %collective-permute-start.5 = (bf16[2,256,256]{2,1,0:T(8,128)(2,1)S(1)}, bf16[2,256,256]{2,1,0:T(8,128)(2,1)S(1)}, u32[]{:S(2)}, u32[]{:S(2)}) collective-permute-start(bf16[2,256,256]{2,1,0:T(8,128)(2,1)S(1)} %get-tuple-element.74), channel_id=1, source_target_pairs={{0,1},{1,0},{2,3},{3,2},{4,5},{5,4},{6,7},{7,6},{8,9},{9,8},{10,11... | collective-permute-start | bytes 786440 | tf_op jit(solution)/shard_map/ppermute | solution.py:484
  18.4 6.6 %collective-permute-start.8 = (bf16[2,256,256]{2,1,0:T(8,128)(2,1)S(1)}, bf16[2,256,256]{2,1,0:T(8,128)(2,1)S(1)}, u32[]{:S(2)}, u32[]{:S(2)}) collective-permute-start(bf16[2,256,256]{2,1,0:T(8,128)(2,1)S(1)} %chip_sum.2._), channel_id=1, source_target_pairs={{0,8},{1,17},{2,10},{3,19},{4,12},{5,21},{6,14},{7,23},{8,0},{9,25... | collective-permute-start | bytes 786440 | tf_op jit(solution)/shard_map/ppermute | solution.py:493
  20.7 7.5 %collective-permute-start.9 = (bf16[2,256,256]{2,1,0:T(8,128)(2,1)S(1)}, bf16[2,256,256]{2,1,0:T(8,128)(2,1)S(1)}, u32[]{:S(2)}, u32[]{:S(2)}) collective-permute-start(bf16[2,256,256]{2,1,0:T(8,128)(2,1)S(1)} %chip_sum.3.__), channel_id=1, source_target_pairs={{0,8},{1,17},{2,10},{3,19},{4,12},{5,21},{6,14},{7,23},{8,0},{9,25... | collective-permute-start | bytes 786440 | tf_op jit(solution)/shard_map/ppermute | solution.py:493
  21.7 3.3 %collective-permute-start.7 = (bf16[2,256,512]{2,1,0:T(8,128)(2,1)S(1)}, bf16[2,256,512]{2,1,0:T(8,128)(2,1)S(1)}, u32[]{:S(2)}, u32[]{:S(2)}) collective-permute-start(bf16[2,256,512]{2,1,0:T(8,128)(2,1)S(1)} %get-tuple-element.84), channel_id=1, source_target_pairs={{0,1},{1,0},{2,3},{3,2},{4,5},{5,4},{6,7},{7,6},{8,9},{9,8},{10,11... | collective-permute-start | bytes 1572872 | tf_op jit(solution)/shard_map/ppermute | solution.py:504
  25.1 7.3 %collective-permute-start.11 = (bf16[1,256,256]{2,1,0:T(8,128)(2,1)S(1)}, bf16[1,256,256]{2,1,0:T(8,128)(2,1)S(1)}, u32[]{:S(2)}, u32[]{:S(2)}) collective-permute-start(bf16[1,256,256]{2,1,0:T(8,128)(2,1)S(1)} %get-tuple-element.85._.refs_3_), channel_id=1, source_target_pairs={{0,16},{1,9},{2,18},{3,11},{4,20},{5,13},{6,22},{7,15},{8,24},{9,1... | collective-permute-start | bytes 393224 | tf_op jit(solution)/shard_map/ppermute | solution.py:493
  26.7 5.7 %collective-permute-start.6 = (bf16[36,1024]{1,0:T(8,128)(2,1)S(1)}, bf16[36,1024]{1,0:T(8,128)(2,1)S(1)}, u32[]{:S(2)}, u32[]{:S(2)}) collective-permute-start(bf16[36,1024]{1,0:T(8,128)(2,1)S(1)} %pack_lon.1), channel_id=1, source_target_pairs={{7,0},{0,1},{1,2},{2,3},{3,4},{4,5},{5,6},{6,7},{15,8},{8,9},{9,10... | collective-permute-start | bytes 221192 | tf_op jit(solution)/shard_map/ppermute | solution.py:511
  28.3 5.1 %collective-permute-start.12 = (bf16[1,256,256]{2,1,0:T(8,128)(2,1)S(1)}, bf16[1,256,256]{2,1,0:T(8,128)(2,1)S(1)}, u32[]{:S(2)}, u32[]{:S(2)}) collective-permute-start(bf16[1,256,256]{2,1,0:T(8,128)(2,1)S(1)} %get-tuple-element.86._), channel_id=1, source_target_pairs={{0,16},{1,9},{2,18},{3,11},{4,20},{5,13},{6,22},{7,15},{8,24},{9,1... | collective-permute-start | bytes 393224 | tf_op jit(solution)/shard_map/ppermute | solution.py:493
  30.2 10.1 %collective-permute-start.10 = (bf16[36,1024]{1,0:T(8,128)(2,1)S(1)}, bf16[36,1024]{1,0:T(8,128)(2,1)S(1)}, u32[]{:S(2)}, u32[]{:S(2)}) collective-permute-start(bf16[36,1024]{1,0:T(8,128)(2,1)S(1)} %pack_diag.1), channel_id=1, source_target_pairs={{15,0},{24,1},{9,2},{26,3},{11,4},{28,5},{13,6},{30,7},{23,8},{0,9... | collective-permute-start | bytes 221192 | tf_op jit(solution)/shard_map/ppermute | solution.py:527
  33.5 7.6 %collective-permute-start.14 = (bf16[64,512]{1,0:T(8,128)(2,1)S(1)}, bf16[64,512]{1,0:T(8,128)(2,1)S(1)}, u32[]{:S(2)}, u32[]{:S(2)}) collective-permute-start(bf16[64,512]{1,0:T(8,128)(2,1)S(1)} %get-tuple-element.94), channel_id=1, source_target_pairs={{0,6},{1,7},{2,4},{3,5},{4,2},{5,3},{6,0},{7,1},{8,14},{9,15},{10,... | collective-permute-start | bytes 196616 | tf_op jit(solution)/shard_map/ppermute | solution.py:539
  37.8 5.2 %collective-permute-start.15 = (bf16[64,512]{1,0:T(8,128)(2,1)S(1)}, bf16[64,512]{1,0:T(8,128)(2,1)S(1)}, u32[]{:S(2)}, u32[]{:S(2)}) collective-permute-start(bf16[64,512]{1,0:T(8,128)(2,1)S(1)} %get-tuple-element.95), channel_id=1, source_target_pairs={{0,4},{1,5},{2,6},{3,7},{4,0},{5,1},{6,2},{7,3},{8,12},{9,13},{10,... | collective-permute-start | bytes 196616 | tf_op jit(solution)/shard_map/ppermute | solution.py:539
  37.8 5.2 %collective-permute-start.16 = (bf16[64,512]{1,0:T(8,128)(2,1)S(1)}, bf16[64,512]{1,0:T(8,128)(2,1)S(1)}, u32[]{:S(2)}, u32[]{:S(2)}) collective-permute-start(bf16[64,512]{1,0:T(8,128)(2,1)S(1)} %get-tuple-element.89._), channel_id=1, source_target_pairs={{0,2},{1,3},{2,0},{3,1},{4,6},{5,7},{6,4},{7,5},{8,10},{9,11},{10,... | collective-permute-start | bytes 196616 | tf_op jit(solution)/shard_map/ppermute | solution.py:539
  38.6 8.0 %collective-permute-start.13 = (bf16[108,1024]{1,0:T(8,128)(2,1)S(1)}, bf16[108,1024]{1,0:T(8,128)(2,1)S(1)}, u32[]{:S(2)}, u32[]{:S(2)}) collective-permute-start(bf16[108,1024]{1,0:T(8,128)(2,1)S(1)} %pack_lat.1), channel_id=1, source_target_pairs={{24,0},{9,1},{26,2},{11,3},{28,4},{13,5},{30,6},{15,7},{0,8},{17,9... | collective-permute-start | bytes 663560 | tf_op jit(solution)/shard_map/ppermute | solution.py:545
  43.1 5.3 %collective-permute-start.19 = (bf16[64,512]{1,0:T(8,128)(2,1)S(1)}, bf16[64,512]{1,0:T(8,128)(2,1)S(1)}, u32[]{:S(2)}, u32[]{:S(2)}) collective-permute-start(bf16[64,512]{1,0:T(8,128)(2,1)S(1)} %line_sum.1.refs_0_), channel_id=1, source_target_pairs={{0,24},{8,16},{16,8},{24,0},{1,25},{9,17},{17,9},{25,1},{2,26},{10... | collective-permute-start | bytes 196616 | tf_op jit(solution)/shard_map/ppermute | solution.py:553
  44.0 5.0 %collective-permute-start.18 = (bf16[64,512]{1,0:T(8,128)(2,1)S(1)}, bf16[64,512]{1,0:T(8,128)(2,1)S(1)}, u32[]{:S(2)}, u32[]{:S(2)}) collective-permute-start(bf16[64,512]{1,0:T(8,128)(2,1)S(1)} %line_sum.1.refs_0_), channel_id=1, source_target_pairs={{0,16},{8,24},{16,0},{24,8},{1,17},{9,25},{17,1},{25,9},{2,18},{10... | collective-permute-start | bytes 196616 | tf_op jit(solution)/shard_map/ppermute | solution.py:553
  44.8 4.3 %collective-permute-start.17 = (bf16[64,512]{1,0:T(8,128)(2,1)S(1)}, bf16[64,512]{1,0:T(8,128)(2,1)S(1)}, u32[]{:S(2)}, u32[]{:S(2)}) collective-permute-start(bf16[64,512]{1,0:T(8,128)(2,1)S(1)} %line_sum.1.refs_0_), channel_id=1, source_target_pairs={{0,8},{8,0},{16,24},{24,16},{1,9},{9,1},{17,25},{25,17},{2,10},{10... | collective-permute-start | bytes 196616 | tf_op jit(solution)/shard_map/ppermute | solution.py:553

commit v19 on v18

--- a/solution.py
+++ b/solution.py
@@ -109,7 +109,7 @@
 def swap_bits(index, size, core):
     bits = size.bit_length() - 1
     turned = sum(((index >> b) & 1) << (bits - 1 - b) for b in range(bits))
-    return jnp.where(core == 0, index, turned)
+    return jnp.where(core == 0, turned, index)
 
 
 def shares(transposed, out, lon, core_of, lon_size):
@@ -486,7 +486,7 @@
 
     def halving(phase, send):
         route = [
-            (i * lon_size + j, (i ^ (1 << (phase if j % 2 == 0 else bits - 1 - phase))) * lon_size + j)
+            (i * lon_size + j, (i ^ (1 << (phase if j % 2 else bits - 1 - phase))) * lon_size + j)
             for i in range(lat_size)
             for j in range(lon_size)
         ]

time: 50 us -> 50.5 us (1.010)
  starting transfers between devices: 25.6 us -> 26.7 us
  waiting for transfers between devices: 10.8 us -> 10 us
    ppermute x4, waiting for transfers between devices: 4.71 us -> 3.53 us  [halving(): return lax.ppermute(send, both, route)]
    ppermute x4, starting transfers between devices: 5.72 us -> 6.88 us  [halving(): return lax.ppermute(send, both, route)]
where the time goes in v19:
time: 50.5 us; the launch traced here: 50.3 us
  starting transfers between devices  26.7 us (53%)
  Pallas kernels  11.8 us (23%)
  waiting for transfers between devices  10 us (20%)
  local copies, waits for them, and re-layouts  0.94 us (2%)
  between operations  0.81 us (2%)
    pallas_call x22, Pallas kernels, call(): pl.pallas_call(kernel, out_shape=shapes, in_specs=[anywhere if i in unrea...  11.8 us
    ppermute x4, starting transfers between devices, halving(): return lax.ppermute(send, both, route)  6.88 us
    ppermute x3, starting transfers between devices, per_device(): lax.ppermute(parts[step], 'lon', [(j, j ^ 2 * step) for j in range(lon_si...  4.79 us
    ppermute x1, starting transfers between devices, per_device(): inner_in = lax.ppermute(inner_lat, both, lat_route)  3.94 us
    ppermute x3, starting transfers between devices, per_device(): lax.ppermute(line_sum, 'lat', [(i, i ^ step) for i in range(lat_size)])  3.55 us
    ppermute x4, waiting for transfers between devices, halving(): return lax.ppermute(send, both, route)  3.53 us
    ppermute x1, waiting for transfers between devices, per_device(): lon_home = lax.ppermute(lon_back, both, back(lon_route))  2.15 us
    ppermute x3, waiting for transfers between devices, per_device(): lax.ppermute(parts[step], 'lon', [(j, j ^ 2 * step) for j in range(lon_si...  1.88 us
  transfers between devices with their start and end apart: 20, of which 9 were waited for; matrix products, arithmetic and copies ran while one was open for 0% of the time, Pallas kernels for 16%

profile of v19, /device:TPU:0, one launch (start us, length us, event | category | flops | bytes accessed | tf_op | source)
XLA Modules:
  0.0 50.3 jit_solution(15363036656688812989)
XLA Ops:
  0.7 0.1 order.1
  0.8 0.8 %copy-done.3 = bf16[2,6,24,512]{3,2,1,0:T(8,128)(2,1)S(1)} copy-done((bf16[2,6,24,512]{3,2,1,0:T(8,128)(2,1)S(1)}, bf16[2,6,24,512]{3,2,1,0:T(8,128)(2,1)}, u32[]{:S(2)}) %copy-start.3) | copy-done | bytes 294936
  1.6 0.1 copy-done.2
  1.7 0.4 pack.1
  2.1 3.9 %collective-permute-start = (bf16[72,1024]{1,0:T(8,128)(2,1)S(1)}, bf16[72,1024]{1,0:T(8,128)(2,1)S(1)}, u32[]{:S(2)}, u32[]{:S(2)}) collective-permute-start(bf16[72,1024]{1,0:T(8,128)(2,1)S(1)} %get-tuple-element.62), channel_id=1, source_target_pairs={{0,24},{1,9},{2,26},{3,11},{4,28},{5,13},{6,30},{7,15},{8,0},{9,17... | collective-permute-start | bytes 442376 | tf_op jit(solution)/shard_map/ppermute | solution.py:458
  6.0 1.8 %collective-permute-start.1 = (bf16[36,1024]{1,0:T(8,128)(2,1)S(1)}, bf16[36,1024]{1,0:T(8,128)(2,1)S(1)}, u32[]{:S(2)}, u32[]{:S(2)}) collective-permute-start(bf16[36,1024]{1,0:T(8,128)(2,1)S(1)} %get-tuple-element.53._), channel_id=1, source_target_pairs={{0,7},{1,0},{2,1},{3,2},{4,3},{5,4},{6,5},{7,6},{8,15},{9,8},{10,9... | collective-permute-start | bytes 221192 | tf_op jit(solution)/shard_map/ppermute | solution.py:459
  7.8 0.6 %pack_rest.1 = (bf16[36,1024]{1,0:T(8,128)(2,1)S(1)}, bf16[36,1024]{1,0:T(8,128)(2,1)S(1)}, f32[72,1024]{1,0:T(8,128)S(1)}, f32[72,1024]{1,0:T(8,128)S(1)}) custom-call(bf16[36,1024]{1,0:T(8,128)(2,1)S(1)} %get-tuple-element.53._, bf16[288,512]{1,0:T(8,128)(2,1)S(1)} %bitcast.6, bf16[288,512]{1,0:T(8,128)(2,1)S(1)} %bitcast.8, ...), custom_call_target="tpu_custom_call" | custom-call | flops 500000000 | bytes 1525248 | tf_op jit(solution)/shard_map/pack_rest/pallas_call | solution.py:404
  8.4 1.5 %collective-permute-start.2 = (bf16[36,1024]{1,0:T(8,128)(2,1)S(1)}, bf16[36,1024]{1,0:T(8,128)(2,1)S(1)}, u32[]{:S(2)}, u32[]{:S(2)}) collective-permute-start(bf16[36,1024]{1,0:T(8,128)(2,1)S(1)} %get-tuple-element.66), channel_id=1, source_target_pairs={{0,24},{1,9},{2,26},{3,11},{4,28},{5,13},{6,30},{7,15},{8,0},{9,17... | collective-permute-start | bytes 221192 | tf_op jit(solution)/shard_map/ppermute | solution.py:460
  9.9 1.6 %collective-permute-start.3 = (bf16[36,1024]{1,0:T(8,128)(2,1)S(1)}, bf16[36,1024]{1,0:T(8,128)(2,1)S(1)}, u32[]{:S(2)}, u32[]{:S(2)}) collective-permute-start(bf16[36,1024]{1,0:T(8,128)(2,1)S(1)} %get-tuple-element.67), channel_id=1, source_target_pairs={{0,15},{1,24},{2,9},{3,26},{4,11},{5,28},{6,13},{7,30},{8,23},{9,0... | collective-permute-start | bytes 221192 | tf_op jit(solution)/shard_map/ppermute | solution.py:461
  11.5 0.7 %own.1 = (f32[72,512]{1,0:T(8,128)S(1)}, f32[72,1536]{1,0:T(8,128)S(1)}, f32[72,512]{1,0:T(8,128)S(1)}) custom-call(f32[72,1024]{1,0:T(8,128)S(1)} %get-tuple-element.58.inner_own.own, bf16[512,1536]{1,0:T(8,128)(2,1)S(1)} %copy-done, bf16[512,512]{1,0:T(8,128)(2,1)S(1)} %copy-done.1), custom_call_target="tpu_custom_call" | custom-call | flops 500000000 | bytes 3129344 | tf_op jit(solution)/shard_map/own/pallas_call | solution.py:404
  12.2 2.1 %inner.1 = (f32[2,256,512]{2,1,0:T(8,128)S(1)}, bf16[144,512]{1,0:T(8,128)(2,1)S(1)}, bf16[144,512]{1,0:T(8,128)(2,1)S(1)}, bf16[2,256,144]{2,1,0:T(8,128)(2,1)S...) custom-call(f32[72,1024]{1,0:T(8,128)S(1)} %get-tuple-element.58.inner_own.own, ...), custom_call_target="tpu_custom_call" | custom-call | flops 1000000000 | bytes 5505024 | tf_op jit(solution)/shard_map/inner/pallas_call | solution.py:404
  14.4 2.4 %outer.1 = (bf16[2,256,256]{2,1,0:T(8,128)(2,1)S(1)}, bf16[2,256,256]{2,1,0:T(8,128)(2,1)S(1)}, bf16[144,512]{1,0:T(8,128)(2,1)S(1)}, bf16[144,512]{1,0:T(8,128)...) custom-call(f32[72,1024]{1,0:T(8,128)S(1)} %get-tuple-element.65.own, ...), custom_call_target="tpu_custom_call" | custom-call | flops 1000000000 | bytes 5365760 | tf_op jit(solution)/shard_map/outer/pallas_call | solution.py:404
  16.8 0.1 collective-permute-start.4
  16.9 0.5 collective-permute-start.5
  17.3 0.4 keep.1
  17.8 0.6 %collective-permute-done.4.refs_1_ = bf16[2,256,256]{2,1,0:T(8,128)(2,1)S(1)} collective-permute-done((bf16[2,256,256]{2,1,0:T(8,128)(2,1)S(1)}, bf16[2,256,256]{2,1,0:T(8,128)(2,1)S(1)}, u32[]{:S(2)}, u32[]{:S(2)}) %collective-permute-start.4) | collective-permute-done | bytes 262176 | tf_op jit(solution)/shard_map/ppermute | solution.py:484
  18.4 0.1 chip_sum.2._
  18.4 1.6 %collective-permute-start.8 = (bf16[2,256,256]{2,1,0:T(8,128)(2,1)S(1)}, bf16[2,256,256]{2,1,0:T(8,128)(2,1)S(1)}, u32[]{:S(2)}, u32[]{:S(2)}) collective-permute-start(bf16[2,256,256]{2,1,0:T(8,128)(2,1)S(1)} %chip_sum.2._), channel_id=1, source_target_pairs={{0,16},{1,9},{2,18},{3,11},{4,20},{5,13},{6,22},{7,15},{8,24},{9,1... | collective-permute-start | bytes 786440 | tf_op jit(solution)/shard_map/ppermute | solution.py:493
  20.0 0.1 chip_sum.3.__
  20.1 0.6 %collective-permute-start.9 = (bf16[2,256,256]{2,1,0:T(8,128)(2,1)S(1)}, bf16[2,256,256]{2,1,0:T(8,128)(2,1)S(1)}, u32[]{:S(2)}, u32[]{:S(2)}) collective-permute-start(bf16[2,256,256]{2,1,0:T(8,128)(2,1)S(1)} %chip_sum.3.__), channel_id=1, source_target_pairs={{0,16},{1,9},{2,18},{3,11},{4,20},{5,13},{6,22},{7,15},{8,24},{9,1... | collective-permute-start | bytes 786440 | tf_op jit(solution)/shard_map/ppermute | solution.py:493
  20.7 0.7 %rest.1 = (bf16[2,256,512]{2,1,0:T(8,128)(2,1)S(1)}, bf16[2,256,512]{2,1,0:T(8,128)(2,1)S(1)}) custom-call(bf16[2,256,256]{2,1,0:T(8,128)(2,1)S(1)} %chip_sum.2._, bf16[2,256,256]{2,1,0:T(8,128)(2,1)S(1)} %chip_sum.3.__, bf16[2,256,144]{2,1,0:T(8,128)(2,1)S(1)} %get-tuple-element.63.refs_0_, bf16[144,2048]{1,0:T(8,128)(2,1)S(1)} %get-tuple-element.64.refs_1_.refs_2_, ...), custom_call_target="tpu_custom_call" | custom-call | tf_op jit(solution)/shard_map/rest/pallas_call | solution.py:404
  21.4 0.2 collective-permute-start.7
  21.6 0.9 %outputs.1 = (bf16[144,1024]{1,0:T(8,128)(2,1)S(1)}, bf16[144,1024]{1,0:T(8,128)(2,1)S(1)}) custom-call(bf16[2,256,512]{2,1,0:T(8,128)(2,1)S(1)} %get-tuple-element.77._.refs_0_, bf16[144,512]{1,0:T(8,128)(2,1)S(1)} %get-tuple-element.78.refs_0_, bf16[144,512]{1,0:T(8,128)(2,1)S(1)} %get-tuple-element.79.refs_1_, ...), custom_call_target="tpu_custom_call" | custom-call | flops 10000000000 | bytes 4980736 | tf_op jit(solution)/shard_map/outputs/pallas_call | solution.py:404
  22.5 2.3 %collective-permute-done.8.refs_2_ = bf16[2,256,256]{2,1,0:T(8,128)(2,1)S(1)} collective-permute-done((bf16[2,256,256]{2,1,0:T(8,128)(2,1)S(1)}, bf16[2,256,256]{2,1,0:T(8,128)(2,1)S(1)}, u32[]{:S(2)}, u32[]{:S(2)}) %collective-permute-start.8) | collective-permute-done | bytes 262176 | tf_op jit(solution)/shard_map/ppermute | solution.py:493
  24.9 0.1 halve1.2
  25.0 2.2 %collective-permute-start.11 = (bf16[1,256,256]{2,1,0:T(8,128)(2,1)S(1)}, bf16[1,256,256]{2,1,0:T(8,128)(2,1)S(1)}, u32[]{:S(2)}, u32[]{:S(2)}) collective-permute-start(bf16[1,256,256]{2,1,0:T(8,128)(2,1)S(1)} %get-tuple-element.85._.refs_3_), channel_id=1, source_target_pairs={{0,8},{1,17},{2,10},{3,19},{4,12},{5,21},{6,14},{7,23},{8,0},{9,25... | collective-permute-start | bytes 393224 | tf_op jit(solution)/shard_map/ppermute | solution.py:493
  27.2 0.1 pack_lon.1
  27.4 0.6 %collective-permute-done.9.refs_2_ = bf16[2,256,256]{2,1,0:T(8,128)(2,1)S(1)} collective-permute-done((bf16[2,256,256]{2,1,0:T(8,128)(2,1)S(1)}, bf16[2,256,256]{2,1,0:T(8,128)(2,1)S(1)}, u32[]{:S(2)}, u32[]{:S(2)}) %collective-permute-start.9) | collective-permute-done | bytes 262176 | tf_op jit(solution)/shard_map/ppermute | solution.py:493
  28.0 0.1 halve1.3
  28.1 2.6 %collective-permute-start.12 = (bf16[1,256,256]{2,1,0:T(8,128)(2,1)S(1)}, bf16[1,256,256]{2,1,0:T(8,128)(2,1)S(1)}, u32[]{:S(2)}, u32[]{:S(2)}) collective-permute-start(bf16[1,256,256]{2,1,0:T(8,128)(2,1)S(1)} %get-tuple-element.86._), channel_id=1, source_target_pairs={{0,8},{1,17},{2,10},{3,19},{4,12},{5,21},{6,14},{7,23},{8,0},{9,25... | collective-permute-start | bytes 393224 | tf_op jit(solution)/shard_map/ppermute | solution.py:493
  30.7 0.1 pack_diag.1
  30.8 0.1 collective-permute-start.10
  30.9 2.1 %collective-permute-done.6.lon_in._ = bf16[36,1024]{1,0:T(8,128)(2,1)S(1)} collective-permute-done((bf16[36,1024]{1,0:T(8,128)(2,1)S(1)}, bf16[36,1024]{1,0:T(8,128)(2,1)S(1)}, u32[]{:S(2)}, u32[]{:S(2)}) %collective-permute-start.6) | collective-permute-done | bytes 73760 | tf_op jit(solution)/shard_map/ppermute | solution.py:511
  33.1 0.5 %collective-permute-done.12.refs_2_ = bf16[1,256,256]{2,1,0:T(8,128)(2,1)S(1)} collective-permute-done((bf16[1,256,256]{2,1,0:T(8,128)(2,1)S(1)}, bf16[1,256,256]{2,1,0:T(8,128)(2,1)S(1)}, u32[]{:S(2)}, u32[]{:S(2)}) %collective-permute-start.12) | collective-permute-done | bytes 131104 | tf_op jit(solution)/shard_map/ppermute | solution.py:493
  33.6 4.2 %collective-permute-start.14 = (bf16[64,512]{1,0:T(8,128)(2,1)S(1)}, bf16[64,512]{1,0:T(8,128)(2,1)S(1)}, u32[]{:S(2)}, u32[]{:S(2)}) collective-permute-start(bf16[64,512]{1,0:T(8,128)(2,1)S(1)} %get-tuple-element.94), channel_id=1, source_target_pairs={{0,6},{1,7},{2,4},{3,5},{4,2},{5,3},{6,0},{7,1},{8,14},{9,15},{10,... | collective-permute-start | bytes 196616 | tf_op jit(solution)/shard_map/ppermute | solution.py:539
  37.8 0.6 %collective-permute-start.16 = (bf16[64,512]{1,0:T(8,128)(2,1)S(1)}, bf16[64,512]{1,0:T(8,128)(2,1)S(1)}, u32[]{:S(2)}, u32[]{:S(2)}) collective-permute-start(bf16[64,512]{1,0:T(8,128)(2,1)S(1)} %get-tuple-element.89._), channel_id=1, source_target_pairs={{0,2},{1,3},{2,0},{3,1},{4,6},{5,7},{6,4},{7,5},{8,10},{9,11},{10,... | collective-permute-start | bytes 196616 | tf_op jit(solution)/shard_map/ppermute | solution.py:539
  38.4 0.1 pack_lat.1
  38.6 1.7 %collective-permute-start.13 = (bf16[108,1024]{1,0:T(8,128)(2,1)S(1)}, bf16[108,1024]{1,0:T(8,128)(2,1)S(1)}, u32[]{:S(2)}, u32[]{:S(2)}) collective-permute-start(bf16[108,1024]{1,0:T(8,128)(2,1)S(1)} %pack_lat.1), channel_id=1, source_target_pairs={{24,0},{9,1},{26,2},{11,3},{28,4},{13,5},{30,6},{15,7},{0,8},{17,9... | collective-permute-start | bytes 663560 | tf_op jit(solution)/shard_map/ppermute | solution.py:545
  40.3 0.8 %place.1.placed._ = f32[288,1024]{1,0:T(8,128)S(1)} custom-call(bf16[144,1024]{1,0:T(8,128)(2,1)S(1)} %get-tuple-element.82._.refs_3_.inner_results, bf16[144,1024]{1,0:T(8,128)(2,1)S(1)} %get-tuple-element.83.outer_results, bf16[36,1024]{1,0:T(8,128)(2,1)S(1)} %collective-permute-done.6.lon_in._, bf16[36,1024]{1,0:T(8,128)(2,1)S(1)} %collective-permute-done.10.diag_in), custom_call_target="tpu_custom_call" | custom-call | bytes 1916928 | tf_op jit(solution)/shard_map/place/pallas_call | solution.py:404
  41.1 1.9 %collective-permute-done.15.refs_2_ = bf16[64,512]{1,0:T(8,128)(2,1)S(1)} collective-permute-done((bf16[64,512]{1,0:T(8,128)(2,1)S(1)}, bf16[64,512]{1,0:T(8,128)(2,1)S(1)}, u32[]{:S(2)}, u32[]{:S(2)}) %collective-permute-start.15) | collective-permute-done | bytes 65568 | tf_op jit(solution)/shard_map/ppermute | solution.py:539
  43.0 0.8 %collective-permute-start.19 = (bf16[64,512]{1,0:T(8,128)(2,1)S(1)}, bf16[64,512]{1,0:T(8,128)(2,1)S(1)}, u32[]{:S(2)}, u32[]{:S(2)}) collective-permute-start(bf16[64,512]{1,0:T(8,128)(2,1)S(1)} %line_sum.1.refs_0_), channel_id=1, source_target_pairs={{0,24},{8,16},{16,8},{24,0},{1,25},{9,17},{17,9},{25,1},{2,26},{10... | collective-permute-start | bytes 196616 | tf_op jit(solution)/shard_map/ppermute | solution.py:553
  43.8 1.4 %collective-permute-start.18 = (bf16[64,512]{1,0:T(8,128)(2,1)S(1)}, bf16[64,512]{1,0:T(8,128)(2,1)S(1)}, u32[]{:S(2)}, u32[]{:S(2)}) collective-permute-start(bf16[64,512]{1,0:T(8,128)(2,1)S(1)} %line_sum.1.refs_0_), channel_id=1, source_target_pairs={{0,16},{8,24},{16,0},{24,8},{1,17},{9,25},{17,1},{25,9},{2,18},{10... | collective-permute-start | bytes 196616 | tf_op jit(solution)/shard_map/ppermute | solution.py:553
  45.2 1.4 %collective-permute-start.17 = (bf16[64,512]{1,0:T(8,128)(2,1)S(1)}, bf16[64,512]{1,0:T(8,128)(2,1)S(1)}, u32[]{:S(2)}, u32[]{:S(2)}) collective-permute-start(bf16[64,512]{1,0:T(8,128)(2,1)S(1)} %line_sum.1.refs_0_), channel_id=1, source_target_pairs={{0,8},{8,0},{16,24},{24,16},{1,9},{9,1},{17,25},{25,17},{2,10},{10... | collective-permute-start | bytes 196616 | tf_op jit(solution)/shard_map/ppermute | solution.py:553
  46.6 1.0 %place_rest.1 = (bf16[288,512]{1,0:T(8,128)(2,1)}, bf16[288,512]{1,0:T(8,128)(2,1)}, f32[8,128]{1,0:T(8,128)S(1)}) custom-call(f32[288,1024]{1,0:T(8,128)S(1)} %place.1.placed._, bf16[108,1024]{1,0:T(8,128)(2,1)S(1)} %collective-permute-done.13.lat_in), custom_call_target="tpu_custom_call" | custom-call | bytes 1994752 | tf_op jit(solution)/shard_map/place_rest/pallas_call | solution.py:404
  47.6 0.7 %collective-permute-done.19.refs_3_ = bf16[64,512]{1,0:T(8,128)(2,1)S(1)} collective-permute-done((bf16[64,512]{1,0:T(8,128)(2,1)S(1)}, bf16[64,512]{1,0:T(8,128)(2,1)S(1)}, u32[]{:S(2)}, u32[]{:S(2)}) %collective-permute-start.19) | collective-permute-done | bytes 65568 | tf_op jit(solution)/shard_map/ppermute | solution.py:553
  48.3 0.5 collective-permute-done.18.refs_2_
  48.8 0.7 %collective-permute-done.17.refs_1_ = bf16[64,512]{1,0:T(8,128)(2,1)S(1)} collective-permute-done((bf16[64,512]{1,0:T(8,128)(2,1)S(1)}, bf16[64,512]{1,0:T(8,128)(2,1)S(1)}, u32[]{:S(2)}, u32[]{:S(2)}) %collective-permute-start.17) | collective-permute-done | bytes 65568 | tf_op jit(solution)/shard_map/ppermute | solution.py:553
  49.5 0.9 %finish.1 = (f32[64,1536]{1,0:T(8,128)}, f32[64,512]{1,0:T(8,128)}) custom-call(f32[8,128]{1,0:T(8,128)S(1)} %get-tuple-element.92._, bf16[64,512]{1,0:T(8,128)(2,1)S(1)} %line_sum.1.refs_0_, bf16[64,512]{1,0:T(8,128)(2,1)S(1)} %collective-permute-done.17.refs_1_, bf16[64,512]{1,0:T(8,128)(2,1)S(1)} %collective-permute-done.18.refs_2_, ...), custom_call_target="tpu_custom_call" | custom-call | bytes 790528 | tf_op jit(solution)/shard_map/finish/pallas_call | solution.py:404
  (22 shorter events, 0.2 us)
Async XLA Ops:
  0.6 1.0 %copy-start.3 = (bf16[2,6,24,512]{3,2,1,0:T(8,128)(2,1)S(1)}, bf16[2,6,24,512]{3,2,1,0:T(8,128)(2,1)}, u32[]{:S(2)}) copy-start(bf16[2,6,24,512]{3,2,1,0:T(8,128)(2,1)} %param.5) | copy-start | bytes 884740
  0.6 1.0 %copy-start.2 = (bf16[2,6,24,512]{3,2,1,0:T(8,128)(2,1)S(1)}, bf16[2,6,24,512]{3,2,1,0:T(8,128)(2,1)}, u32[]{:S(2)}) copy-start(bf16[2,6,24,512]{3,2,1,0:T(8,128)(2,1)} %param.4) | copy-start | bytes 884740
  1.7 9.8 %copy-start.1 = (bf16[512,512]{1,0:T(8,128)(2,1)S(1)}, bf16[512,512]{1,0:T(8,128)(2,1)}, u32[]{:S(2)}) copy-start(bf16[512,512]{1,0:T(8,128)(2,1)} %refs_7_.1) | copy-start | bytes 1572868
  2.0 9.5 %copy-start = (bf16[512,1536]{1,0:T(8,128)(2,1)S(1)}, bf16[512,1536]{1,0:T(8,128)(2,1)}, u32[]{:S(2)}) copy-start(bf16[512,1536]{1,0:T(8,128)(2,1)} %refs_6_.1) | copy-start | bytes 4718596
  2.1 10.2 %collective-permute-start = (bf16[72,1024]{1,0:T(8,128)(2,1)S(1)}, bf16[72,1024]{1,0:T(8,128)(2,1)S(1)}, u32[]{:S(2)}, u32[]{:S(2)}) collective-permute-start(bf16[72,1024]{1,0:T(8,128)(2,1)S(1)} %get-tuple-element.62), channel_id=1, source_target_pairs={{0,24},{1,9},{2,26},{3,11},{4,28},{5,13},{6,30},{7,15},{8,0},{9,17... | collective-permute-start | bytes 442376 | tf_op jit(solution)/shard_map/ppermute | solution.py:458
  6.0 8.4 %collective-permute-start.1 = (bf16[36,1024]{1,0:T(8,128)(2,1)S(1)}, bf16[36,1024]{1,0:T(8,128)(2,1)S(1)}, u32[]{:S(2)}, u32[]{:S(2)}) collective-permute-start(bf16[36,1024]{1,0:T(8,128)(2,1)S(1)} %get-tuple-element.53._), channel_id=1, source_target_pairs={{0,7},{1,0},{2,1},{3,2},{4,3},{5,4},{6,5},{7,6},{8,15},{9,8},{10,9... | collective-permute-start | bytes 221192 | tf_op jit(solution)/shard_map/ppermute | solution.py:459
  8.4 6.0 %collective-permute-start.2 = (bf16[36,1024]{1,0:T(8,128)(2,1)S(1)}, bf16[36,1024]{1,0:T(8,128)(2,1)S(1)}, u32[]{:S(2)}, u32[]{:S(2)}) collective-permute-start(bf16[36,1024]{1,0:T(8,128)(2,1)S(1)} %get-tuple-element.66), channel_id=1, source_target_pairs={{0,24},{1,9},{2,26},{3,11},{4,28},{5,13},{6,30},{7,15},{8,0},{9,17... | collective-permute-start | bytes 221192 | tf_op jit(solution)/shard_map/ppermute | solution.py:460
  9.9 4.5 %collective-permute-start.3 = (bf16[36,1024]{1,0:T(8,128)(2,1)S(1)}, bf16[36,1024]{1,0:T(8,128)(2,1)S(1)}, u32[]{:S(2)}, u32[]{:S(2)}) collective-permute-start(bf16[36,1024]{1,0:T(8,128)(2,1)S(1)} %get-tuple-element.67), channel_id=1, source_target_pairs={{0,15},{1,24},{2,9},{3,26},{4,11},{5,28},{6,13},{7,30},{8,23},{9,0... | collective-permute-start | bytes 221192 | tf_op jit(solution)/shard_map/ppermute | solution.py:461
  16.8 1.6 %collective-permute-start.4 = (bf16[2,256,256]{2,1,0:T(8,128)(2,1)S(1)}, bf16[2,256,256]{2,1,0:T(8,128)(2,1)S(1)}, u32[]{:S(2)}, u32[]{:S(2)}) collective-permute-start(bf16[2,256,256]{2,1,0:T(8,128)(2,1)S(1)} %get-tuple-element.72), channel_id=1, source_target_pairs={{0,1},{1,0},{2,3},{3,2},{4,5},{5,4},{6,7},{7,6},{8,9},{9,8},{10,11... | collective-permute-start | bytes 786440 | tf_op jit(solution)/shard_map/ppermute | solution.py:484
  16.9 3.1 %collective-permute-start.5 = (bf16[2,256,256]{2,1,0:T(8,128)(2,1)S(1)}, bf16[2,256,256]{2,1,0:T(8,128)(2,1)S(1)}, u32[]{:S(2)}, u32[]{:S(2)}) collective-permute-start(bf16[2,256,256]{2,1,0:T(8,128)(2,1)S(1)} %get-tuple-element.74), channel_id=1, source_target_pairs={{0,1},{1,0},{2,3},{3,2},{4,5},{5,4},{6,7},{7,6},{8,9},{9,8},{10,11... | collective-permute-start | bytes 786440 | tf_op jit(solution)/shard_map/ppermute | solution.py:484
  18.4 6.4 %collective-permute-start.8 = (bf16[2,256,256]{2,1,0:T(8,128)(2,1)S(1)}, bf16[2,256,256]{2,1,0:T(8,128)(2,1)S(1)}, u32[]{:S(2)}, u32[]{:S(2)}) collective-permute-start(bf16[2,256,256]{2,1,0:T(8,128)(2,1)S(1)} %chip_sum.2._), channel_id=1, source_target_pairs={{0,16},{1,9},{2,18},{3,11},{4,20},{5,13},{6,22},{7,15},{8,24},{9,1... | collective-permute-start | bytes 786440 | tf_op jit(solution)/shard_map/ppermute | solution.py:493
  20.1 7.9 %collective-permute-start.9 = (bf16[2,256,256]{2,1,0:T(8,128)(2,1)S(1)}, bf16[2,256,256]{2,1,0:T(8,128)(2,1)S(1)}, u32[]{:S(2)}, u32[]{:S(2)}) collective-permute-start(bf16[2,256,256]{2,1,0:T(8,128)(2,1)S(1)} %chip_sum.3.__), channel_id=1, source_target_pairs={{0,16},{1,9},{2,18},{3,11},{4,20},{5,13},{6,22},{7,15},{8,24},{9,1... | collective-permute-start | bytes 786440 | tf_op jit(solution)/shard_map/ppermute | solution.py:493
  21.4 3.5 %collective-permute-start.7 = (bf16[2,256,512]{2,1,0:T(8,128)(2,1)S(1)}, bf16[2,256,512]{2,1,0:T(8,128)(2,1)S(1)}, u32[]{:S(2)}, u32[]{:S(2)}) collective-permute-start(bf16[2,256,512]{2,1,0:T(8,128)(2,1)S(1)} %get-tuple-element.84), channel_id=1, source_target_pairs={{0,1},{1,0},{2,3},{3,2},{4,5},{5,4},{6,7},{7,6},{8,9},{9,8},{10,11... | collective-permute-start | bytes 1572872 | tf_op jit(solution)/shard_map/ppermute | solution.py:504
  25.0 8.0 %collective-permute-start.11 = (bf16[1,256,256]{2,1,0:T(8,128)(2,1)S(1)}, bf16[1,256,256]{2,1,0:T(8,128)(2,1)S(1)}, u32[]{:S(2)}, u32[]{:S(2)}) collective-permute-start(bf16[1,256,256]{2,1,0:T(8,128)(2,1)S(1)} %get-tuple-element.85._.refs_3_), channel_id=1, source_target_pairs={{0,8},{1,17},{2,10},{3,19},{4,12},{5,21},{6,14},{7,23},{8,0},{9,25... | collective-permute-start | bytes 393224 | tf_op jit(solution)/shard_map/ppermute | solution.py:493
  27.3 5.7 %collective-permute-start.6 = (bf16[36,1024]{1,0:T(8,128)(2,1)S(1)}, bf16[36,1024]{1,0:T(8,128)(2,1)S(1)}, u32[]{:S(2)}, u32[]{:S(2)}) collective-permute-start(bf16[36,1024]{1,0:T(8,128)(2,1)S(1)} %pack_lon.1), channel_id=1, source_target_pairs={{7,0},{0,1},{1,2},{2,3},{3,4},{4,5},{5,6},{6,7},{15,8},{8,9},{9,10... | collective-permute-start | bytes 221192 | tf_op jit(solution)/shard_map/ppermute | solution.py:511
  28.1 5.5 %collective-permute-start.12 = (bf16[1,256,256]{2,1,0:T(8,128)(2,1)S(1)}, bf16[1,256,256]{2,1,0:T(8,128)(2,1)S(1)}, u32[]{:S(2)}, u32[]{:S(2)}) collective-permute-start(bf16[1,256,256]{2,1,0:T(8,128)(2,1)S(1)} %get-tuple-element.86._), channel_id=1, source_target_pairs={{0,8},{1,17},{2,10},{3,19},{4,12},{5,21},{6,14},{7,23},{8,0},{9,25... | collective-permute-start | bytes 393224 | tf_op jit(solution)/shard_map/ppermute | solution.py:493
  30.8 9.5 %collective-permute-start.10 = (bf16[36,1024]{1,0:T(8,128)(2,1)S(1)}, bf16[36,1024]{1,0:T(8,128)(2,1)S(1)}, u32[]{:S(2)}, u32[]{:S(2)}) collective-permute-start(bf16[36,1024]{1,0:T(8,128)(2,1)S(1)} %pack_diag.1), channel_id=1, source_target_pairs={{15,0},{24,1},{9,2},{26,3},{11,4},{28,5},{13,6},{30,7},{23,8},{0,9... | collective-permute-start | bytes 221192 | tf_op jit(solution)/shard_map/ppermute | solution.py:527
  33.6 7.4 %collective-permute-start.14 = (bf16[64,512]{1,0:T(8,128)(2,1)S(1)}, bf16[64,512]{1,0:T(8,128)(2,1)S(1)}, u32[]{:S(2)}, u32[]{:S(2)}) collective-permute-start(bf16[64,512]{1,0:T(8,128)(2,1)S(1)} %get-tuple-element.94), channel_id=1, source_target_pairs={{0,6},{1,7},{2,4},{3,5},{4,2},{5,3},{6,0},{7,1},{8,14},{9,15},{10,... | collective-permute-start | bytes 196616 | tf_op jit(solution)/shard_map/ppermute | solution.py:539
  37.8 5.2 %collective-permute-start.15 = (bf16[64,512]{1,0:T(8,128)(2,1)S(1)}, bf16[64,512]{1,0:T(8,128)(2,1)S(1)}, u32[]{:S(2)}, u32[]{:S(2)}) collective-permute-start(bf16[64,512]{1,0:T(8,128)(2,1)S(1)} %get-tuple-element.95), channel_id=1, source_target_pairs={{0,4},{1,5},{2,6},{3,7},{4,0},{5,1},{6,2},{7,3},{8,12},{9,13},{10,... | collective-permute-start | bytes 196616 | tf_op jit(solution)/shard_map/ppermute | solution.py:539
  37.8 5.2 %collective-permute-start.16 = (bf16[64,512]{1,0:T(8,128)(2,1)S(1)}, bf16[64,512]{1,0:T(8,128)(2,1)S(1)}, u32[]{:S(2)}, u32[]{:S(2)}) collective-permute-start(bf16[64,512]{1,0:T(8,128)(2,1)S(1)} %get-tuple-element.89._), channel_id=1, source_target_pairs={{0,2},{1,3},{2,0},{3,1},{4,6},{5,7},{6,4},{7,5},{8,10},{9,11},{10,... | collective-permute-start | bytes 196616 | tf_op jit(solution)/shard_map/ppermute | solution.py:539
  38.6 8.0 %collective-permute-start.13 = (bf16[108,1024]{1,0:T(8,128)(2,1)S(1)}, bf16[108,1024]{1,0:T(8,128)(2,1)S(1)}, u32[]{:S(2)}, u32[]{:S(2)}) collective-permute-start(bf16[108,1024]{1,0:T(8,128)(2,1)S(1)} %pack_lat.1), channel_id=1, source_target_pairs={{24,0},{9,1},{26,2},{11,3},{28,4},{13,5},{30,6},{15,7},{0,8},{17,9... | collective-permute-start | bytes 663560 | tf_op jit(solution)/shard_map/ppermute | solution.py:545
  43.0 5.3 %collective-permute-start.19 = (bf16[64,512]{1,0:T(8,128)(2,1)S(1)}, bf16[64,512]{1,0:T(8,128)(2,1)S(1)}, u32[]{:S(2)}, u32[]{:S(2)}) collective-permute-start(bf16[64,512]{1,0:T(8,128)(2,1)S(1)} %line_sum.1.refs_0_), channel_id=1, source_target_pairs={{0,24},{8,16},{16,8},{24,0},{1,25},{9,17},{17,9},{25,1},{2,26},{10... | collective-permute-start | bytes 196616 | tf_op jit(solution)/shard_map/ppermute | solution.py:553
  43.8 5.0 %collective-permute-start.18 = (bf16[64,512]{1,0:T(8,128)(2,1)S(1)}, bf16[64,512]{1,0:T(8,128)(2,1)S(1)}, u32[]{:S(2)}, u32[]{:S(2)}) collective-permute-start(bf16[64,512]{1,0:T(8,128)(2,1)S(1)} %line_sum.1.refs_0_), channel_id=1, source_target_pairs={{0,16},{8,24},{16,0},{24,8},{1,17},{9,25},{17,1},{25,9},{2,18},{10... | collective-permute-start | bytes 196616 | tf_op jit(solution)/shard_map/ppermute | solution.py:553
  45.2 4.3 %collective-permute-start.17 = (bf16[64,512]{1,0:T(8,128)(2,1)S(1)}, bf16[64,512]{1,0:T(8,128)(2,1)S(1)}, u32[]{:S(2)}, u32[]{:S(2)}) collective-permute-start(bf16[64,512]{1,0:T(8,128)(2,1)S(1)} %line_sum.1.refs_0_), channel_id=1, source_target_pairs={{0,8},{8,0},{16,24},{24,16},{1,9},{9,1},{17,25},{25,17},{2,10},{10... | collective-permute-start | bytes 196616 | tf_op jit(solution)/shard_map/ppermute | solution.py:553

commit v20 on v18

--- a/solution.py
+++ b/solution.py
@@ -523,15 +523,14 @@
             kept[index] = [keep, halving(phase, send)]
             after = send
 
-    (diag_back,) = call(pack_diag_kernel, [quarter], send, results[1], name="pack_diag", unread=(0,))
-    diag_home = lax.ppermute(diag_back, both, back(diag_route))
-
     rows = width // lon_size
     share = ((rows, split[2]), BF)
     (first_chunk,) = call(
         next_sum_kernel, [((1, split[1], split[2] // 2), F32)], lon_home, *kept[0],
         name="first_chunk", flops=LATER, unread=(0,),
     )
+    (diag_back,) = call(pack_diag_kernel, [quarter], first_chunk, results[1], name="pack_diag", unread=(0,))
+    diag_home = lax.ppermute(diag_back, both, back(diag_route))
     parts = call(
         line_parts_kernel, [share] * (lon_size // 2), first_chunk, *kept[1], name="line_parts", flops=PARTS
     )

time: 50 us -> 51.5 us (1.030)
  waiting for transfers between devices: 10.8 us -> 12.1 us
    ppermute x3, waiting for transfers between devices: 1.94 us -> 2.99 us  [per_device(): lax.ppermute(parts[step], 'lon', [(j, j ^ 2 * step) for j in range(lon_si...]
    ppermute x1, starting transfers between devices: 1.73 us -> 2.35 us  [per_device(): lat_home = lax.ppermute(lat_back, both, back(lat_route))]
where the time goes in v20:
time: 51.5 us; the launch traced here: 51.4 us
  starting transfers between devices  25.7 us (50%)
  waiting for transfers between devices  12.1 us (23%)
  Pallas kernels  11.8 us (23%)
  local copies, waits for them, and re-layouts  0.94 us (2%)
  between operations  0.83 us (2%)
    pallas_call x22, Pallas kernels, call(): pl.pallas_call(kernel, out_shape=shapes, in_specs=[anywhere if i in unrea...  11.8 us
    ppermute x4, starting transfers between devices, halving(): return lax.ppermute(send, both, route)  5.72 us
    ppermute x3, starting transfers between devices, per_device(): lax.ppermute(parts[step], 'lon', [(j, j ^ 2 * step) for j in range(lon_si...  4.45 us
    ppermute x4, waiting for transfers between devices, halving(): return lax.ppermute(send, both, route)  4.37 us
    ppermute x1, starting transfers between devices, per_device(): inner_in = lax.ppermute(inner_lat, both, lat_route)  3.94 us
    ppermute x3, starting transfers between devices, per_device(): lax.ppermute(line_sum, 'lat', [(i, i ^ step) for i in range(lat_size)])  3.55 us
    ppermute x3, waiting for transfers between devices, per_device(): lax.ppermute(parts[step], 'lon', [(j, j ^ 2 * step) for j in range(lon_si...  2.99 us
    ppermute x1, waiting for transfers between devices, per_device(): lon_home = lax.ppermute(lon_back, both, back(lon_route))  2.36 us
  transfers between devices with their start and end apart: 20, of which 9 were waited for; matrix products, arithmetic and copies ran while one was open for 0% of the time, Pallas kernels for 16%

profile of v20, /device:TPU:0, one launch (start us, length us, event | category | flops | bytes accessed | tf_op | source)
XLA Modules:
  0.0 51.4 jit_solution(4240482519546607198)
XLA Ops:
  0.7 0.1 order.1
  0.8 0.8 %copy-done.3 = bf16[2,6,24,512]{3,2,1,0:T(8,128)(2,1)S(1)} copy-done((bf16[2,6,24,512]{3,2,1,0:T(8,128)(2,1)S(1)}, bf16[2,6,24,512]{3,2,1,0:T(8,128)(2,1)}, u32[]{:S(2)}) %copy-start.3) | copy-done | bytes 294936
  1.6 0.1 copy-done.2
  1.7 0.4 pack.1
  2.1 3.9 %collective-permute-start = (bf16[72,1024]{1,0:T(8,128)(2,1)S(1)}, bf16[72,1024]{1,0:T(8,128)(2,1)S(1)}, u32[]{:S(2)}, u32[]{:S(2)}) collective-permute-start(bf16[72,1024]{1,0:T(8,128)(2,1)S(1)} %get-tuple-element.62), channel_id=1, source_target_pairs={{0,24},{1,9},{2,26},{3,11},{4,28},{5,13},{6,30},{7,15},{8,0},{9,17... | collective-permute-start | bytes 442376 | tf_op jit(solution)/shard_map/ppermute | solution.py:458
  6.0 1.8 %collective-permute-start.1 = (bf16[36,1024]{1,0:T(8,128)(2,1)S(1)}, bf16[36,1024]{1,0:T(8,128)(2,1)S(1)}, u32[]{:S(2)}, u32[]{:S(2)}) collective-permute-start(bf16[36,1024]{1,0:T(8,128)(2,1)S(1)} %get-tuple-element.53._), channel_id=1, source_target_pairs={{0,7},{1,0},{2,1},{3,2},{4,3},{5,4},{6,5},{7,6},{8,15},{9,8},{10,9... | collective-permute-start | bytes 221192 | tf_op jit(solution)/shard_map/ppermute | solution.py:459
  7.8 0.6 %pack_rest.1 = (bf16[36,1024]{1,0:T(8,128)(2,1)S(1)}, bf16[36,1024]{1,0:T(8,128)(2,1)S(1)}, f32[72,1024]{1,0:T(8,128)S(1)}, f32[72,1024]{1,0:T(8,128)S(1)}) custom-call(bf16[36,1024]{1,0:T(8,128)(2,1)S(1)} %get-tuple-element.53._, bf16[288,512]{1,0:T(8,128)(2,1)S(1)} %bitcast.6, bf16[288,512]{1,0:T(8,128)(2,1)S(1)} %bitcast.8, ...), custom_call_target="tpu_custom_call" | custom-call | flops 500000000 | bytes 1525248 | tf_op jit(solution)/shard_map/pack_rest/pallas_call | solution.py:404
  8.4 1.5 %collective-permute-start.2 = (bf16[36,1024]{1,0:T(8,128)(2,1)S(1)}, bf16[36,1024]{1,0:T(8,128)(2,1)S(1)}, u32[]{:S(2)}, u32[]{:S(2)}) collective-permute-start(bf16[36,1024]{1,0:T(8,128)(2,1)S(1)} %get-tuple-element.66), channel_id=1, source_target_pairs={{0,24},{1,9},{2,26},{3,11},{4,28},{5,13},{6,30},{7,15},{8,0},{9,17... | collective-permute-start | bytes 221192 | tf_op jit(solution)/shard_map/ppermute | solution.py:460
  9.9 1.6 %collective-permute-start.3 = (bf16[36,1024]{1,0:T(8,128)(2,1)S(1)}, bf16[36,1024]{1,0:T(8,128)(2,1)S(1)}, u32[]{:S(2)}, u32[]{:S(2)}) collective-permute-start(bf16[36,1024]{1,0:T(8,128)(2,1)S(1)} %get-tuple-element.67), channel_id=1, source_target_pairs={{0,15},{1,24},{2,9},{3,26},{4,11},{5,28},{6,13},{7,30},{8,23},{9,0... | collective-permute-start | bytes 221192 | tf_op jit(solution)/shard_map/ppermute | solution.py:461
  11.5 0.7 %own.1 = (f32[72,512]{1,0:T(8,128)S(1)}, f32[72,1536]{1,0:T(8,128)S(1)}, f32[72,512]{1,0:T(8,128)S(1)}) custom-call(f32[72,1024]{1,0:T(8,128)S(1)} %get-tuple-element.58.inner_own.own, bf16[512,1536]{1,0:T(8,128)(2,1)S(1)} %copy-done, bf16[512,512]{1,0:T(8,128)(2,1)S(1)} %copy-done.1), custom_call_target="tpu_custom_call" | custom-call | flops 500000000 | bytes 3129344 | tf_op jit(solution)/shard_map/own/pallas_call | solution.py:404
  12.2 2.1 %inner.1 = (f32[2,256,512]{2,1,0:T(8,128)S(1)}, bf16[144,512]{1,0:T(8,128)(2,1)S(1)}, bf16[144,512]{1,0:T(8,128)(2,1)S(1)}, bf16[2,256,144]{2,1,0:T(8,128)(2,1)S...) custom-call(f32[72,1024]{1,0:T(8,128)S(1)} %get-tuple-element.58.inner_own.own, ...), custom_call_target="tpu_custom_call" | custom-call | flops 1000000000 | bytes 5505024 | tf_op jit(solution)/shard_map/inner/pallas_call | solution.py:404
  14.4 2.4 %outer.1 = (bf16[2,256,256]{2,1,0:T(8,128)(2,1)S(1)}, bf16[2,256,256]{2,1,0:T(8,128)(2,1)S(1)}, bf16[144,512]{1,0:T(8,128)(2,1)S(1)}, bf16[144,512]{1,0:T(8,128)...) custom-call(f32[72,1024]{1,0:T(8,128)S(1)} %get-tuple-element.65.own, ...), custom_call_target="tpu_custom_call" | custom-call | flops 1000000000 | bytes 5365760 | tf_op jit(solution)/shard_map/outer/pallas_call | solution.py:404
  16.8 0.1 collective-permute-start.4
  16.9 0.4 collective-permute-start.5
  17.3 0.4 keep.1
  17.8 0.6 %collective-permute-done.4.refs_1_ = bf16[2,256,256]{2,1,0:T(8,128)(2,1)S(1)} collective-permute-done((bf16[2,256,256]{2,1,0:T(8,128)(2,1)S(1)}, bf16[2,256,256]{2,1,0:T(8,128)(2,1)S(1)}, u32[]{:S(2)}, u32[]{:S(2)}) %collective-permute-start.4) | collective-permute-done | bytes 262176 | tf_op jit(solution)/shard_map/ppermute | solution.py:484
  18.4 0.1 chip_sum.2._
  18.4 2.2 %collective-permute-start.8 = (bf16[2,256,256]{2,1,0:T(8,128)(2,1)S(1)}, bf16[2,256,256]{2,1,0:T(8,128)(2,1)S(1)}, u32[]{:S(2)}, u32[]{:S(2)}) collective-permute-start(bf16[2,256,256]{2,1,0:T(8,128)(2,1)S(1)} %chip_sum.2._), channel_id=1, source_target_pairs={{0,8},{1,17},{2,10},{3,19},{4,12},{5,21},{6,14},{7,23},{8,0},{9,25... | collective-permute-start | bytes 786440 | tf_op jit(solution)/shard_map/ppermute | solution.py:493
  20.6 0.1 chip_sum.3.__
  20.7 0.3 collective-permute-start.11
  21.0 0.7 %rest.1 = (bf16[2,256,512]{2,1,0:T(8,128)(2,1)S(1)}, bf16[2,256,512]{2,1,0:T(8,128)(2,1)S(1)}) custom-call(bf16[2,256,256]{2,1,0:T(8,128)(2,1)S(1)} %chip_sum.2._, bf16[2,256,256]{2,1,0:T(8,128)(2,1)S(1)} %chip_sum.3.__, bf16[2,256,144]{2,1,0:T(8,128)(2,1)S(1)} %get-tuple-element.63.refs_0_, bf16[144,2048]{1,0:T(8,128)(2,1)S(1)} %get-tuple-element.64.refs_1_.refs_2_, ...), custom_call_target="tpu_custom_call" | custom-call | tf_op jit(solution)/shard_map/rest/pallas_call | solution.py:404
  21.7 0.1 collective-permute-start.7
  21.8 0.9 %outputs.1 = (bf16[144,1024]{1,0:T(8,128)(2,1)S(1)}, bf16[144,1024]{1,0:T(8,128)(2,1)S(1)}) custom-call(bf16[2,256,512]{2,1,0:T(8,128)(2,1)S(1)} %get-tuple-element.77._.refs_0_, bf16[144,512]{1,0:T(8,128)(2,1)S(1)} %get-tuple-element.78.refs_0_, bf16[144,512]{1,0:T(8,128)(2,1)S(1)} %get-tuple-element.79.refs_1_, ...), custom_call_target="tpu_custom_call" | custom-call | flops 10000000000 | bytes 4980736 | tf_op jit(solution)/shard_map/outputs/pallas_call | solution.py:404
  22.7 2.3 %collective-permute-done.8.refs_2_ = bf16[2,256,256]{2,1,0:T(8,128)(2,1)S(1)} collective-permute-done((bf16[2,256,256]{2,1,0:T(8,128)(2,1)S(1)}, bf16[2,256,256]{2,1,0:T(8,128)(2,1)S(1)}, u32[]{:S(2)}, u32[]{:S(2)}) %collective-permute-start.8) | collective-permute-done | bytes 262176 | tf_op jit(solution)/shard_map/ppermute | solution.py:493
  25.0 0.1 halve1.2
  25.1 1.5 %collective-permute-start.9 = (bf16[1,256,256]{2,1,0:T(8,128)(2,1)S(1)}, bf16[1,256,256]{2,1,0:T(8,128)(2,1)S(1)}, u32[]{:S(2)}, u32[]{:S(2)}) collective-permute-start(bf16[1,256,256]{2,1,0:T(8,128)(2,1)S(1)} %get-tuple-element.86._.refs_3_), channel_id=1, source_target_pairs={{0,16},{1,9},{2,18},{3,11},{4,20},{5,13},{6,22},{7,15},{8,24},{9,1... | collective-permute-start | bytes 393224 | tf_op jit(solution)/shard_map/ppermute | solution.py:493
  26.5 0.1 pack_lon.1
  26.8 1.4 %collective-permute-done.11.refs_2_ = bf16[2,256,256]{2,1,0:T(8,128)(2,1)S(1)} collective-permute-done((bf16[2,256,256]{2,1,0:T(8,128)(2,1)S(1)}, bf16[2,256,256]{2,1,0:T(8,128)(2,1)S(1)}, u32[]{:S(2)}, u32[]{:S(2)}) %collective-permute-start.11) | collective-permute-done | bytes 262176 | tf_op jit(solution)/shard_map/ppermute | solution.py:493
  28.2 0.1 halve1.3
  28.3 1.8 %collective-permute-start.12 = (bf16[1,256,256]{2,1,0:T(8,128)(2,1)S(1)}, bf16[1,256,256]{2,1,0:T(8,128)(2,1)S(1)}, u32[]{:S(2)}, u32[]{:S(2)}) collective-permute-start(bf16[1,256,256]{2,1,0:T(8,128)(2,1)S(1)} %get-tuple-element.88), channel_id=1, source_target_pairs={{0,16},{1,9},{2,18},{3,11},{4,20},{5,13},{6,22},{7,15},{8,24},{9,1... | collective-permute-start | bytes 393224 | tf_op jit(solution)/shard_map/ppermute | solution.py:493
  30.0 2.4 %collective-permute-done.6._.lon_in = bf16[36,1024]{1,0:T(8,128)(2,1)S(1)} collective-permute-done((bf16[36,1024]{1,0:T(8,128)(2,1)S(1)}, bf16[36,1024]{1,0:T(8,128)(2,1)S(1)}, u32[]{:S(2)}, u32[]{:S(2)}) %collective-permute-start.6) | collective-permute-done | bytes 73760 | tf_op jit(solution)/shard_map/ppermute | solution.py:511
  32.4 0.1 pack_diag.1
  32.6 0.1 collective-permute-start.10
  32.7 0.7 %collective-permute-done.12.refs_2_ = bf16[1,256,256]{2,1,0:T(8,128)(2,1)S(1)} collective-permute-done((bf16[1,256,256]{2,1,0:T(8,128)(2,1)S(1)}, bf16[1,256,256]{2,1,0:T(8,128)(2,1)S(1)}, u32[]{:S(2)}, u32[]{:S(2)}) %collective-permute-start.12) | collective-permute-done | bytes 131104 | tf_op jit(solution)/shard_map/ppermute | solution.py:493
  33.4 3.6 %collective-permute-start.14 = (bf16[64,512]{1,0:T(8,128)(2,1)S(1)}, bf16[64,512]{1,0:T(8,128)(2,1)S(1)}, u32[]{:S(2)}, u32[]{:S(2)}) collective-permute-start(bf16[64,512]{1,0:T(8,128)(2,1)S(1)} %get-tuple-element.94), channel_id=1, source_target_pairs={{0,6},{1,7},{2,4},{3,5},{4,2},{5,3},{6,0},{7,1},{8,14},{9,15},{10,... | collective-permute-start | bytes 196616 | tf_op jit(solution)/shard_map/ppermute | solution.py:538
  36.9 0.9 %collective-permute-start.16 = (bf16[64,512]{1,0:T(8,128)(2,1)S(1)}, bf16[64,512]{1,0:T(8,128)(2,1)S(1)}, u32[]{:S(2)}, u32[]{:S(2)}) collective-permute-start(bf16[64,512]{1,0:T(8,128)(2,1)S(1)} %get-tuple-element.89._), channel_id=1, source_target_pairs={{0,2},{1,3},{2,0},{3,1},{4,6},{5,7},{6,4},{7,5},{8,10},{9,11},{10,... | collective-permute-start | bytes 196616 | tf_op jit(solution)/shard_map/ppermute | solution.py:538
  37.8 0.1 pack_lat.1
  38.0 2.4 %collective-permute-start.13 = (bf16[108,1024]{1,0:T(8,128)(2,1)S(1)}, bf16[108,1024]{1,0:T(8,128)(2,1)S(1)}, u32[]{:S(2)}, u32[]{:S(2)}) collective-permute-start(bf16[108,1024]{1,0:T(8,128)(2,1)S(1)} %pack_lat.1), channel_id=1, source_target_pairs={{24,0},{9,1},{26,2},{11,3},{28,4},{13,5},{30,6},{15,7},{0,8},{17,9... | collective-permute-start | bytes 663560 | tf_op jit(solution)/shard_map/ppermute | solution.py:544
  40.3 0.8 %place.1.placed._ = f32[288,1024]{1,0:T(8,128)S(1)} custom-call(bf16[144,1024]{1,0:T(8,128)(2,1)S(1)} %get-tuple-element.82._.refs_3_.inner_results, bf16[144,1024]{1,0:T(8,128)(2,1)S(1)} %get-tuple-element.83.outer_results, bf16[36,1024]{1,0:T(8,128)(2,1)S(1)} %collective-permute-done.6._.lon_in, bf16[36,1024]{1,0:T(8,128)(2,1)S(1)} %collective-permute-done.10.diag_in), custom_call_target="tpu_custom_call" | custom-call | bytes 1916928 | tf_op jit(solution)/shard_map/place/pallas_call | solution.py:404
  41.1 2.8 %collective-permute-done.15.refs_2_ = bf16[64,512]{1,0:T(8,128)(2,1)S(1)} collective-permute-done((bf16[64,512]{1,0:T(8,128)(2,1)S(1)}, bf16[64,512]{1,0:T(8,128)(2,1)S(1)}, u32[]{:S(2)}, u32[]{:S(2)}) %collective-permute-start.15) | collective-permute-done | bytes 65568 | tf_op jit(solution)/shard_map/ppermute | solution.py:538
  43.9 0.2 collective-permute-done.16.refs_3_
  44.1 0.7 %collective-permute-start.19 = (bf16[64,512]{1,0:T(8,128)(2,1)S(1)}, bf16[64,512]{1,0:T(8,128)(2,1)S(1)}, u32[]{:S(2)}, u32[]{:S(2)}) collective-permute-start(bf16[64,512]{1,0:T(8,128)(2,1)S(1)} %line_sum.1.refs_0_), channel_id=1, source_target_pairs={{0,24},{8,16},{16,8},{24,0},{1,25},{9,17},{17,9},{25,1},{2,26},{10... | collective-permute-start | bytes 196616 | tf_op jit(solution)/shard_map/ppermute | solution.py:552
  44.9 1.4 %collective-permute-start.18 = (bf16[64,512]{1,0:T(8,128)(2,1)S(1)}, bf16[64,512]{1,0:T(8,128)(2,1)S(1)}, u32[]{:S(2)}, u32[]{:S(2)}) collective-permute-start(bf16[64,512]{1,0:T(8,128)(2,1)S(1)} %line_sum.1.refs_0_), channel_id=1, source_target_pairs={{0,16},{8,24},{16,0},{24,8},{1,17},{9,25},{17,1},{25,9},{2,18},{10... | collective-permute-start | bytes 196616 | tf_op jit(solution)/shard_map/ppermute | solution.py:552
  46.2 1.4 %collective-permute-start.17 = (bf16[64,512]{1,0:T(8,128)(2,1)S(1)}, bf16[64,512]{1,0:T(8,128)(2,1)S(1)}, u32[]{:S(2)}, u32[]{:S(2)}) collective-permute-start(bf16[64,512]{1,0:T(8,128)(2,1)S(1)} %line_sum.1.refs_0_), channel_id=1, source_target_pairs={{0,8},{8,0},{16,24},{24,16},{1,9},{9,1},{17,25},{25,17},{2,10},{10... | collective-permute-start | bytes 196616 | tf_op jit(solution)/shard_map/ppermute | solution.py:552
  47.7 1.0 %place_rest.1 = (bf16[288,512]{1,0:T(8,128)(2,1)}, bf16[288,512]{1,0:T(8,128)(2,1)}, f32[8,128]{1,0:T(8,128)S(1)}) custom-call(f32[288,1024]{1,0:T(8,128)S(1)} %place.1.placed._, bf16[108,1024]{1,0:T(8,128)(2,1)S(1)} %collective-permute-done.13.lat_in), custom_call_target="tpu_custom_call" | custom-call | bytes 1994752 | tf_op jit(solution)/shard_map/place_rest/pallas_call | solution.py:404
  48.7 1.2 %collective-permute-done.19.refs_3_ = bf16[64,512]{1,0:T(8,128)(2,1)S(1)} collective-permute-done((bf16[64,512]{1,0:T(8,128)(2,1)S(1)}, bf16[64,512]{1,0:T(8,128)(2,1)S(1)}, u32[]{:S(2)}, u32[]{:S(2)}) %collective-permute-start.19) | collective-permute-done | bytes 65568 | tf_op jit(solution)/shard_map/ppermute | solution.py:552
  49.9 0.6 %collective-permute-done.17.refs_1_ = bf16[64,512]{1,0:T(8,128)(2,1)S(1)} collective-permute-done((bf16[64,512]{1,0:T(8,128)(2,1)S(1)}, bf16[64,512]{1,0:T(8,128)(2,1)S(1)}, u32[]{:S(2)}, u32[]{:S(2)}) %collective-permute-start.17) | collective-permute-done | bytes 65568 | tf_op jit(solution)/shard_map/ppermute | solution.py:552
  50.5 0.9 %finish.1 = (f32[64,1536]{1,0:T(8,128)}, f32[64,512]{1,0:T(8,128)}) custom-call(f32[8,128]{1,0:T(8,128)S(1)} %get-tuple-element.92._, bf16[64,512]{1,0:T(8,128)(2,1)S(1)} %line_sum.1.refs_0_, bf16[64,512]{1,0:T(8,128)(2,1)S(1)} %collective-permute-done.17.refs_1_, bf16[64,512]{1,0:T(8,128)(2,1)S(1)} %collective-permute-done.18.refs_2_, ...), custom_call_target="tpu_custom_call" | custom-call | bytes 790528 | tf_op jit(solution)/shard_map/finish/pallas_call | solution.py:404
  (22 shorter events, 0.2 us)
Async XLA Ops:
  0.6 1.0 %copy-start.3 = (bf16[2,6,24,512]{3,2,1,0:T(8,128)(2,1)S(1)}, bf16[2,6,24,512]{3,2,1,0:T(8,128)(2,1)}, u32[]{:S(2)}) copy-start(bf16[2,6,24,512]{3,2,1,0:T(8,128)(2,1)} %param.5) | copy-start | bytes 884740
  0.6 1.0 %copy-start.2 = (bf16[2,6,24,512]{3,2,1,0:T(8,128)(2,1)S(1)}, bf16[2,6,24,512]{3,2,1,0:T(8,128)(2,1)}, u32[]{:S(2)}) copy-start(bf16[2,6,24,512]{3,2,1,0:T(8,128)(2,1)} %param.4) | copy-start | bytes 884740
  1.7 9.8 %copy-start.1 = (bf16[512,512]{1,0:T(8,128)(2,1)S(1)}, bf16[512,512]{1,0:T(8,128)(2,1)}, u32[]{:S(2)}) copy-start(bf16[512,512]{1,0:T(8,128)(2,1)} %refs_7_.1) | copy-start | bytes 1572868
  2.0 9.5 %copy-start = (bf16[512,1536]{1,0:T(8,128)(2,1)S(1)}, bf16[512,1536]{1,0:T(8,128)(2,1)}, u32[]{:S(2)}) copy-start(bf16[512,1536]{1,0:T(8,128)(2,1)} %refs_6_.1) | copy-start | bytes 4718596
  2.1 10.2 %collective-permute-start = (bf16[72,1024]{1,0:T(8,128)(2,1)S(1)}, bf16[72,1024]{1,0:T(8,128)(2,1)S(1)}, u32[]{:S(2)}, u32[]{:S(2)}) collective-permute-start(bf16[72,1024]{1,0:T(8,128)(2,1)S(1)} %get-tuple-element.62), channel_id=1, source_target_pairs={{0,24},{1,9},{2,26},{3,11},{4,28},{5,13},{6,30},{7,15},{8,0},{9,17... | collective-permute-start | bytes 442376 | tf_op jit(solution)/shard_map/ppermute | solution.py:458
  6.0 8.4 %collective-permute-start.1 = (bf16[36,1024]{1,0:T(8,128)(2,1)S(1)}, bf16[36,1024]{1,0:T(8,128)(2,1)S(1)}, u32[]{:S(2)}, u32[]{:S(2)}) collective-permute-start(bf16[36,1024]{1,0:T(8,128)(2,1)S(1)} %get-tuple-element.53._), channel_id=1, source_target_pairs={{0,7},{1,0},{2,1},{3,2},{4,3},{5,4},{6,5},{7,6},{8,15},{9,8},{10,9... | collective-permute-start | bytes 221192 | tf_op jit(solution)/shard_map/ppermute | solution.py:459
  8.4 5.9 %collective-permute-start.2 = (bf16[36,1024]{1,0:T(8,128)(2,1)S(1)}, bf16[36,1024]{1,0:T(8,128)(2,1)S(1)}, u32[]{:S(2)}, u32[]{:S(2)}) collective-permute-start(bf16[36,1024]{1,0:T(8,128)(2,1)S(1)} %get-tuple-element.66), channel_id=1, source_target_pairs={{0,24},{1,9},{2,26},{3,11},{4,28},{5,13},{6,30},{7,15},{8,0},{9,17... | collective-permute-start | bytes 221192 | tf_op jit(solution)/shard_map/ppermute | solution.py:460
  9.9 4.5 %collective-permute-start.3 = (bf16[36,1024]{1,0:T(8,128)(2,1)S(1)}, bf16[36,1024]{1,0:T(8,128)(2,1)S(1)}, u32[]{:S(2)}, u32[]{:S(2)}) collective-permute-start(bf16[36,1024]{1,0:T(8,128)(2,1)S(1)} %get-tuple-element.67), channel_id=1, source_target_pairs={{0,15},{1,24},{2,9},{3,26},{4,11},{5,28},{6,13},{7,30},{8,23},{9,0... | collective-permute-start | bytes 221192 | tf_op jit(solution)/shard_map/ppermute | solution.py:461
  16.8 1.6 %collective-permute-start.4 = (bf16[2,256,256]{2,1,0:T(8,128)(2,1)S(1)}, bf16[2,256,256]{2,1,0:T(8,128)(2,1)S(1)}, u32[]{:S(2)}, u32[]{:S(2)}) collective-permute-start(bf16[2,256,256]{2,1,0:T(8,128)(2,1)S(1)} %get-tuple-element.72), channel_id=1, source_target_pairs={{0,1},{1,0},{2,3},{3,2},{4,5},{5,4},{6,7},{7,6},{8,9},{9,8},{10,11... | collective-permute-start | bytes 786440 | tf_op jit(solution)/shard_map/ppermute | solution.py:484
  16.9 3.7 %collective-permute-start.5 = (bf16[2,256,256]{2,1,0:T(8,128)(2,1)S(1)}, bf16[2,256,256]{2,1,0:T(8,128)(2,1)S(1)}, u32[]{:S(2)}, u32[]{:S(2)}) collective-permute-start(bf16[2,256,256]{2,1,0:T(8,128)(2,1)S(1)} %get-tuple-element.74), channel_id=1, source_target_pairs={{0,1},{1,0},{2,3},{3,2},{4,5},{5,4},{6,7},{7,6},{8,9},{9,8},{10,11... | collective-permute-start | bytes 786440 | tf_op jit(solution)/shard_map/ppermute | solution.py:484
  18.4 6.6 %collective-permute-start.8 = (bf16[2,256,256]{2,1,0:T(8,128)(2,1)S(1)}, bf16[2,256,256]{2,1,0:T(8,128)(2,1)S(1)}, u32[]{:S(2)}, u32[]{:S(2)}) collective-permute-start(bf16[2,256,256]{2,1,0:T(8,128)(2,1)S(1)} %chip_sum.2._), channel_id=1, source_target_pairs={{0,8},{1,17},{2,10},{3,19},{4,12},{5,21},{6,14},{7,23},{8,0},{9,25... | collective-permute-start | bytes 786440 | tf_op jit(solution)/shard_map/ppermute | solution.py:493
  20.7 7.5 %collective-permute-start.11 = (bf16[2,256,256]{2,1,0:T(8,128)(2,1)S(1)}, bf16[2,256,256]{2,1,0:T(8,128)(2,1)S(1)}, u32[]{:S(2)}, u32[]{:S(2)}) collective-permute-start(bf16[2,256,256]{2,1,0:T(8,128)(2,1)S(1)} %chip_sum.3.__), channel_id=1, source_target_pairs={{0,8},{1,17},{2,10},{3,19},{4,12},{5,21},{6,14},{7,23},{8,0},{9,25... | collective-permute-start | bytes 786440 | tf_op jit(solution)/shard_map/ppermute | solution.py:493
  21.7 3.3 %collective-permute-start.7 = (bf16[2,256,512]{2,1,0:T(8,128)(2,1)S(1)}, bf16[2,256,512]{2,1,0:T(8,128)(2,1)S(1)}, u32[]{:S(2)}, u32[]{:S(2)}) collective-permute-start(bf16[2,256,512]{2,1,0:T(8,128)(2,1)S(1)} %get-tuple-element.84), channel_id=1, source_target_pairs={{0,1},{1,0},{2,3},{3,2},{4,5},{5,4},{6,7},{7,6},{8,9},{9,8},{10,11... | collective-permute-start | bytes 1572872 | tf_op jit(solution)/shard_map/ppermute | solution.py:504
  25.1 7.3 %collective-permute-start.9 = (bf16[1,256,256]{2,1,0:T(8,128)(2,1)S(1)}, bf16[1,256,256]{2,1,0:T(8,128)(2,1)S(1)}, u32[]{:S(2)}, u32[]{:S(2)}) collective-permute-start(bf16[1,256,256]{2,1,0:T(8,128)(2,1)S(1)} %get-tuple-element.86._.refs_3_), channel_id=1, source_target_pairs={{0,16},{1,9},{2,18},{3,11},{4,20},{5,13},{6,22},{7,15},{8,24},{9,1... | collective-permute-start | bytes 393224 | tf_op jit(solution)/shard_map/ppermute | solution.py:493
  26.7 5.7 %collective-permute-start.6 = (bf16[36,1024]{1,0:T(8,128)(2,1)S(1)}, bf16[36,1024]{1,0:T(8,128)(2,1)S(1)}, u32[]{:S(2)}, u32[]{:S(2)}) collective-permute-start(bf16[36,1024]{1,0:T(8,128)(2,1)S(1)} %pack_lon.1), channel_id=1, source_target_pairs={{7,0},{0,1},{1,2},{2,3},{3,4},{4,5},{5,6},{6,7},{15,8},{8,9},{9,10... | collective-permute-start | bytes 221192 | tf_op jit(solution)/shard_map/ppermute | solution.py:511
  28.3 5.0 %collective-permute-start.12 = (bf16[1,256,256]{2,1,0:T(8,128)(2,1)S(1)}, bf16[1,256,256]{2,1,0:T(8,128)(2,1)S(1)}, u32[]{:S(2)}, u32[]{:S(2)}) collective-permute-start(bf16[1,256,256]{2,1,0:T(8,128)(2,1)S(1)} %get-tuple-element.88), channel_id=1, source_target_pairs={{0,16},{1,9},{2,18},{3,11},{4,20},{5,13},{6,22},{7,15},{8,24},{9,1... | collective-permute-start | bytes 393224 | tf_op jit(solution)/shard_map/ppermute | solution.py:493
  32.6 7.7 %collective-permute-start.10 = (bf16[36,1024]{1,0:T(8,128)(2,1)S(1)}, bf16[36,1024]{1,0:T(8,128)(2,1)S(1)}, u32[]{:S(2)}, u32[]{:S(2)}) collective-permute-start(bf16[36,1024]{1,0:T(8,128)(2,1)S(1)} %pack_diag.1), channel_id=1, source_target_pairs={{15,0},{24,1},{9,2},{26,3},{11,4},{28,5},{13,6},{30,7},{23,8},{0,9... | collective-permute-start | bytes 221192 | tf_op jit(solution)/shard_map/ppermute | solution.py:533
  33.4 7.7 %collective-permute-start.14 = (bf16[64,512]{1,0:T(8,128)(2,1)S(1)}, bf16[64,512]{1,0:T(8,128)(2,1)S(1)}, u32[]{:S(2)}, u32[]{:S(2)}) collective-permute-start(bf16[64,512]{1,0:T(8,128)(2,1)S(1)} %get-tuple-element.94), channel_id=1, source_target_pairs={{0,6},{1,7},{2,4},{3,5},{4,2},{5,3},{6,0},{7,1},{8,14},{9,15},{10,... | collective-permute-start | bytes 196616 | tf_op jit(solution)/shard_map/ppermute | solution.py:538
  36.9 7.0 %collective-permute-start.15 = (bf16[64,512]{1,0:T(8,128)(2,1)S(1)}, bf16[64,512]{1,0:T(8,128)(2,1)S(1)}, u32[]{:S(2)}, u32[]{:S(2)}) collective-permute-start(bf16[64,512]{1,0:T(8,128)(2,1)S(1)} %get-tuple-element.95), channel_id=1, source_target_pairs={{0,4},{1,5},{2,6},{3,7},{4,0},{5,1},{6,2},{7,3},{8,12},{9,13},{10,... | collective-permute-start | bytes 196616 | tf_op jit(solution)/shard_map/ppermute | solution.py:538
  36.9 7.2 %collective-permute-start.16 = (bf16[64,512]{1,0:T(8,128)(2,1)S(1)}, bf16[64,512]{1,0:T(8,128)(2,1)S(1)}, u32[]{:S(2)}, u32[]{:S(2)}) collective-permute-start(bf16[64,512]{1,0:T(8,128)(2,1)S(1)} %get-tuple-element.89._), channel_id=1, source_target_pairs={{0,2},{1,3},{2,0},{3,1},{4,6},{5,7},{6,4},{7,5},{8,10},{9,11},{10,... | collective-permute-start | bytes 196616 | tf_op jit(solution)/shard_map/ppermute | solution.py:538
  38.0 9.7 %collective-permute-start.13 = (bf16[108,1024]{1,0:T(8,128)(2,1)S(1)}, bf16[108,1024]{1,0:T(8,128)(2,1)S(1)}, u32[]{:S(2)}, u32[]{:S(2)}) collective-permute-start(bf16[108,1024]{1,0:T(8,128)(2,1)S(1)} %pack_lat.1), channel_id=1, source_target_pairs={{24,0},{9,1},{26,2},{11,3},{28,4},{13,5},{30,6},{15,7},{0,8},{17,9... | collective-permute-start | bytes 663560 | tf_op jit(solution)/shard_map/ppermute | solution.py:544
  44.1 5.8 %collective-permute-start.19 = (bf16[64,512]{1,0:T(8,128)(2,1)S(1)}, bf16[64,512]{1,0:T(8,128)(2,1)S(1)}, u32[]{:S(2)}, u32[]{:S(2)}) collective-permute-start(bf16[64,512]{1,0:T(8,128)(2,1)S(1)} %line_sum.1.refs_0_), channel_id=1, source_target_pairs={{0,24},{8,16},{16,8},{24,0},{1,25},{9,17},{17,9},{25,1},{2,26},{10... | collective-permute-start | bytes 196616 | tf_op jit(solution)/shard_map/ppermute | solution.py:552
  44.9 5.1 %collective-permute-start.18 = (bf16[64,512]{1,0:T(8,128)(2,1)S(1)}, bf16[64,512]{1,0:T(8,128)(2,1)S(1)}, u32[]{:S(2)}, u32[]{:S(2)}) collective-permute-start(bf16[64,512]{1,0:T(8,128)(2,1)S(1)} %line_sum.1.refs_0_), channel_id=1, source_target_pairs={{0,16},{8,24},{16,0},{24,8},{1,17},{9,25},{17,1},{25,9},{2,18},{10... | collective-permute-start | bytes 196616 | tf_op jit(solution)/shard_map/ppermute | solution.py:552
  46.2 4.3 %collective-permute-start.17 = (bf16[64,512]{1,0:T(8,128)(2,1)S(1)}, bf16[64,512]{1,0:T(8,128)(2,1)S(1)}, u32[]{:S(2)}, u32[]{:S(2)}) collective-permute-start(bf16[64,512]{1,0:T(8,128)(2,1)S(1)} %line_sum.1.refs_0_), channel_id=1, source_target_pairs={{0,8},{8,0},{16,24},{24,16},{1,9},{9,1},{17,25},{25,17},{2,10},{10... | collective-permute-start | bytes 196616 | tf_op jit(solution)/shard_map/ppermute | solution.py:552

commit v21 on v18

--- a/solution.py
+++ b/solution.py
@@ -171,7 +171,7 @@
         send_grad[slot // 2] = slot_product(slot, size, lat, 1 - core, [(left, right)])
 
 
-def outer_kernel(own, lon_in, lat_in, diag_in, qkv_weight, proj_weight, grad_so_far, send_a, send_b, *refs):
+def outer_kernel(own, lon_in, diag_in, lat_in, qkv_weight, proj_weight, grad_so_far, send_a, send_b, *refs):
     last = picks(last_rows, HALF, QUARTER)
     both = jnp.concatenate(
         [
@@ -477,7 +477,7 @@
     )
     send_a, send_b, *outer = call(
         outer_kernel, [chunk, chunk, *per_window],
-        outer_own, lon_in, outer_in, diag_in, qkv_weight, proj_weight, grad_so_far,
+        outer_own, lon_in, diag_in, outer_in, qkv_weight, proj_weight, grad_so_far,
         name="outer", flops=10**9, scratch=scratch,
     )
     sibling = [(j, j ^ 1) for j in range(lon_size)]

time: 50 us -> 51 us (1.020)
  waiting for transfers between devices: 10.8 us -> 13.8 us
  starting transfers between devices: 25.6 us -> 23.5 us
    ppermute x4, waiting for transfers between devices: 4.71 us -> 7.07 us  [halving(): return lax.ppermute(send, both, route)]
    ppermute x1, starting transfers between devices: 1.49 us -> 3.33 us  [per_device(): outer_in = lax.ppermute(outer_lat, both, lat_route)]
    ppermute x4, starting transfers between devices: 5.72 us -> 4.01 us  [halving(): return lax.ppermute(send, both, route)]
    ppermute x1, starting transfers between devices: 1.73 us -> 0.67 us  [per_device(): lat_home = lax.ppermute(lat_back, both, back(lat_route))]
    ppermute x1, starting transfers between devices: 1.6 us -> 0.99 us  [per_device(): diag_in = lax.ppermute(diag_piece, both, diag_route)]
  transfers between devices with their start and end apart: 20 -> 20, of which waited for: 9 -> 11; matrix products, arithmetic and copies ran while one was open for 0% -> 0% of each run, Pallas kernels for 16% -> 16%
where the time goes in v21:
time: 51 us; the launch traced here: 50.9 us
  starting transfers between devices  23.5 us (46%)
  waiting for transfers between devices  13.8 us (27%)
  Pallas kernels  11.8 us (23%)
  local copies, waits for them, and re-layouts  0.94 us (2%)
  between operations  0.83 us (2%)
    pallas_call x22, Pallas kernels, call(): pl.pallas_call(kernel, out_shape=shapes, in_specs=[anywhere if i in unrea...  11.8 us
    ppermute x4, waiting for transfers between devices, halving(): return lax.ppermute(send, both, route)  7.07 us
    ppermute x3, starting transfers between devices, per_device(): lax.ppermute(parts[step], 'lon', [(j, j ^ 2 * step) for j in range(lon_si...  4.45 us
    ppermute x4, starting transfers between devices, halving(): return lax.ppermute(send, both, route)  4.01 us
    ppermute x1, starting transfers between devices, per_device(): inner_in = lax.ppermute(inner_lat, both, lat_route)  3.94 us
    ppermute x3, starting transfers between devices, per_device(): lax.ppermute(line_sum, 'lat', [(i, i ^ step) for i in range(lat_size)])  3.55 us
    ppermute x1, starting transfers between devices, per_device(): outer_in = lax.ppermute(outer_lat, both, lat_route)  3.33 us
    ppermute x1, waiting for transfers between devices, per_device(): lon_home = lax.ppermute(lon_back, both, back(lon_route))  2.43 us
  transfers between devices with their start and end apart: 20, of which 11 were waited for; matrix products, arithmetic and copies ran while one was open for 0% of the time, Pallas kernels for 16%

profile of v21, /device:TPU:0, one launch (start us, length us, event | category | flops | bytes accessed | tf_op | source)
XLA Modules:
  0.0 50.9 jit_solution(5664906684448740566)
XLA Ops:
  0.7 0.1 order.1
  0.8 0.8 %copy-done.3 = bf16[2,6,24,512]{3,2,1,0:T(8,128)(2,1)S(1)} copy-done((bf16[2,6,24,512]{3,2,1,0:T(8,128)(2,1)S(1)}, bf16[2,6,24,512]{3,2,1,0:T(8,128)(2,1)}, u32[]{:S(2)}) %copy-start.3) | copy-done | bytes 294936
  1.6 0.1 copy-done.2
  1.7 0.4 pack.1
  2.1 3.9 %collective-permute-start = (bf16[72,1024]{1,0:T(8,128)(2,1)S(1)}, bf16[72,1024]{1,0:T(8,128)(2,1)S(1)}, u32[]{:S(2)}, u32[]{:S(2)}) collective-permute-start(bf16[72,1024]{1,0:T(8,128)(2,1)S(1)} %get-tuple-element.62), channel_id=1, source_target_pairs={{0,24},{1,9},{2,26},{3,11},{4,28},{5,13},{6,30},{7,15},{8,0},{9,17... | collective-permute-start | bytes 442376 | tf_op jit(solution)/shard_map/ppermute | solution.py:458
  6.0 1.8 %collective-permute-start.1 = (bf16[36,1024]{1,0:T(8,128)(2,1)S(1)}, bf16[36,1024]{1,0:T(8,128)(2,1)S(1)}, u32[]{:S(2)}, u32[]{:S(2)}) collective-permute-start(bf16[36,1024]{1,0:T(8,128)(2,1)S(1)} %get-tuple-element.53._), channel_id=1, source_target_pairs={{0,7},{1,0},{2,1},{3,2},{4,3},{5,4},{6,5},{7,6},{8,15},{9,8},{10,9... | collective-permute-start | bytes 221192 | tf_op jit(solution)/shard_map/ppermute | solution.py:459
  7.8 0.6 %pack_rest.1 = (bf16[36,1024]{1,0:T(8,128)(2,1)S(1)}, bf16[36,1024]{1,0:T(8,128)(2,1)S(1)}, f32[72,1024]{1,0:T(8,128)S(1)}, f32[72,1024]{1,0:T(8,128)S(1)}) custom-call(bf16[36,1024]{1,0:T(8,128)(2,1)S(1)} %get-tuple-element.53._, bf16[288,512]{1,0:T(8,128)(2,1)S(1)} %bitcast.6, bf16[288,512]{1,0:T(8,128)(2,1)S(1)} %bitcast.8, ...), custom_call_target="tpu_custom_call" | custom-call | flops 500000000 | bytes 1525248 | tf_op jit(solution)/shard_map/pack_rest/pallas_call | solution.py:404
  8.4 1.0 %collective-permute-start.2 = (bf16[36,1024]{1,0:T(8,128)(2,1)S(1)}, bf16[36,1024]{1,0:T(8,128)(2,1)S(1)}, u32[]{:S(2)}, u32[]{:S(2)}) collective-permute-start(bf16[36,1024]{1,0:T(8,128)(2,1)S(1)} %get-tuple-element.66), channel_id=1, source_target_pairs={{0,15},{1,24},{2,9},{3,26},{4,11},{5,28},{6,13},{7,30},{8,23},{9,0... | collective-permute-start | bytes 221192 | tf_op jit(solution)/shard_map/ppermute | solution.py:461
  9.4 3.3 %collective-permute-start.3 = (bf16[36,1024]{1,0:T(8,128)(2,1)S(1)}, bf16[36,1024]{1,0:T(8,128)(2,1)S(1)}, u32[]{:S(2)}, u32[]{:S(2)}) collective-permute-start(bf16[36,1024]{1,0:T(8,128)(2,1)S(1)} %get-tuple-element.67), channel_id=1, source_target_pairs={{0,24},{1,9},{2,26},{3,11},{4,28},{5,13},{6,30},{7,15},{8,0},{9,17... | collective-permute-start | bytes 221192 | tf_op jit(solution)/shard_map/ppermute | solution.py:460
  12.8 0.7 %own.1 = (f32[72,512]{1,0:T(8,128)S(1)}, f32[72,1536]{1,0:T(8,128)S(1)}, f32[72,512]{1,0:T(8,128)S(1)}) custom-call(f32[72,1024]{1,0:T(8,128)S(1)} %get-tuple-element.58.inner_own.own, bf16[512,1536]{1,0:T(8,128)(2,1)S(1)} %copy-done, bf16[512,512]{1,0:T(8,128)(2,1)S(1)} %copy-done.1), custom_call_target="tpu_custom_call" | custom-call | flops 500000000 | bytes 3129344 | tf_op jit(solution)/shard_map/own/pallas_call | solution.py:404
  13.5 2.1 %inner.1 = (f32[2,256,512]{2,1,0:T(8,128)S(1)}, bf16[144,512]{1,0:T(8,128)(2,1)S(1)}, bf16[144,512]{1,0:T(8,128)(2,1)S(1)}, bf16[2,256,144]{2,1,0:T(8,128)(2,1)S...) custom-call(f32[72,1024]{1,0:T(8,128)S(1)} %get-tuple-element.58.inner_own.own, ...), custom_call_target="tpu_custom_call" | custom-call | flops 1000000000 | bytes 5505024 | tf_op jit(solution)/shard_map/inner/pallas_call | solution.py:404
  15.6 2.4 %outer.1 = (bf16[2,256,256]{2,1,0:T(8,128)(2,1)S(1)}, bf16[2,256,256]{2,1,0:T(8,128)(2,1)S(1)}, bf16[144,512]{1,0:T(8,128)(2,1)S(1)}, bf16[144,512]{1,0:T(8,128)...) custom-call(f32[72,1024]{1,0:T(8,128)S(1)} %get-tuple-element.65.own, ...), custom_call_target="tpu_custom_call" | custom-call | flops 1000000000 | bytes 5365760 | tf_op jit(solution)/shard_map/outer/pallas_call | solution.py:404
  18.0 0.1 collective-permute-start.4
  18.1 0.5 collective-permute-start.5
  18.6 0.4 keep.1
  19.0 0.6 %collective-permute-done.4.refs_1_ = bf16[2,256,256]{2,1,0:T(8,128)(2,1)S(1)} collective-permute-done((bf16[2,256,256]{2,1,0:T(8,128)(2,1)S(1)}, bf16[2,256,256]{2,1,0:T(8,128)(2,1)S(1)}, u32[]{:S(2)}, u32[]{:S(2)}) %collective-permute-start.4) | collective-permute-done | bytes 262176 | tf_op jit(solution)/shard_map/ppermute | solution.py:484
  19.7 1.6 %collective-permute-start.8 = (bf16[2,256,256]{2,1,0:T(8,128)(2,1)S(1)}, bf16[2,256,256]{2,1,0:T(8,128)(2,1)S(1)}, u32[]{:S(2)}, u32[]{:S(2)}) collective-permute-start(bf16[2,256,256]{2,1,0:T(8,128)(2,1)S(1)} %chip_sum.2._), channel_id=1, source_target_pairs={{0,8},{1,17},{2,10},{3,19},{4,12},{5,21},{6,14},{7,23},{8,0},{9,25... | collective-permute-start | bytes 786440 | tf_op jit(solution)/shard_map/ppermute | solution.py:493
  21.2 0.1 chip_sum.3.__
  21.3 0.6 %collective-permute-start.9 = (bf16[2,256,256]{2,1,0:T(8,128)(2,1)S(1)}, bf16[2,256,256]{2,1,0:T(8,128)(2,1)S(1)}, u32[]{:S(2)}, u32[]{:S(2)}) collective-permute-start(bf16[2,256,256]{2,1,0:T(8,128)(2,1)S(1)} %chip_sum.3.__), channel_id=1, source_target_pairs={{0,8},{1,17},{2,10},{3,19},{4,12},{5,21},{6,14},{7,23},{8,0},{9,25... | collective-permute-start | bytes 786440 | tf_op jit(solution)/shard_map/ppermute | solution.py:493
  21.9 0.7 %rest.1 = (bf16[2,256,512]{2,1,0:T(8,128)(2,1)S(1)}, bf16[2,256,512]{2,1,0:T(8,128)(2,1)S(1)}) custom-call(bf16[2,256,256]{2,1,0:T(8,128)(2,1)S(1)} %chip_sum.2._, bf16[2,256,256]{2,1,0:T(8,128)(2,1)S(1)} %chip_sum.3.__, bf16[2,256,144]{2,1,0:T(8,128)(2,1)S(1)} %get-tuple-element.63.refs_0_, bf16[144,2048]{1,0:T(8,128)(2,1)S(1)} %get-tuple-element.64.refs_1_.refs_2_, ...), custom_call_target="tpu_custom_call" | custom-call | tf_op jit(solution)/shard_map/rest/pallas_call | solution.py:404
  22.6 0.1 collective-permute-start.7
  22.7 0.9 %outputs.1 = (bf16[144,1024]{1,0:T(8,128)(2,1)S(1)}, bf16[144,1024]{1,0:T(8,128)(2,1)S(1)}) custom-call(bf16[2,256,512]{2,1,0:T(8,128)(2,1)S(1)} %get-tuple-element.77._.refs_0_, bf16[144,512]{1,0:T(8,128)(2,1)S(1)} %get-tuple-element.78.refs_0_, bf16[144,512]{1,0:T(8,128)(2,1)S(1)} %get-tuple-element.79.refs_1_, ...), custom_call_target="tpu_custom_call" | custom-call | flops 10000000000 | bytes 4980736 | tf_op jit(solution)/shard_map/outputs/pallas_call | solution.py:404
  23.6 2.5 %collective-permute-done.8.refs_2_ = bf16[2,256,256]{2,1,0:T(8,128)(2,1)S(1)} collective-permute-done((bf16[2,256,256]{2,1,0:T(8,128)(2,1)S(1)}, bf16[2,256,256]{2,1,0:T(8,128)(2,1)S(1)}, u32[]{:S(2)}, u32[]{:S(2)}) %collective-permute-start.8) | collective-permute-done | bytes 262176 | tf_op jit(solution)/shard_map/ppermute | solution.py:493
  26.1 0.1 halve1.2
  26.2 1.1 %collective-permute-start.11 = (bf16[1,256,256]{2,1,0:T(8,128)(2,1)S(1)}, bf16[1,256,256]{2,1,0:T(8,128)(2,1)S(1)}, u32[]{:S(2)}, u32[]{:S(2)}) collective-permute-start(bf16[1,256,256]{2,1,0:T(8,128)(2,1)S(1)} %get-tuple-element.85._.refs_3_), channel_id=1, source_target_pairs={{0,16},{1,9},{2,18},{3,11},{4,20},{5,13},{6,22},{7,15},{8,24},{9,1... | collective-permute-start | bytes 393224 | tf_op jit(solution)/shard_map/ppermute | solution.py:493
  27.3 0.1 pack_lon.1
  27.5 2.1 %collective-permute-done.9.refs_2_ = bf16[2,256,256]{2,1,0:T(8,128)(2,1)S(1)} collective-permute-done((bf16[2,256,256]{2,1,0:T(8,128)(2,1)S(1)}, bf16[2,256,256]{2,1,0:T(8,128)(2,1)S(1)}, u32[]{:S(2)}, u32[]{:S(2)}) %collective-permute-start.9) | collective-permute-done | bytes 262176 | tf_op jit(solution)/shard_map/ppermute | solution.py:493
  29.6 0.1 halve1.3
  29.7 0.8 %collective-permute-start.12 = (bf16[1,256,256]{2,1,0:T(8,128)(2,1)S(1)}, bf16[1,256,256]{2,1,0:T(8,128)(2,1)S(1)}, u32[]{:S(2)}, u32[]{:S(2)}) collective-permute-start(bf16[1,256,256]{2,1,0:T(8,128)(2,1)S(1)} %get-tuple-element.86._), channel_id=1, source_target_pairs={{0,16},{1,9},{2,18},{3,11},{4,20},{5,13},{6,22},{7,15},{8,24},{9,1... | collective-permute-start | bytes 393224 | tf_op jit(solution)/shard_map/ppermute | solution.py:493
  30.5 0.1 pack_diag.1
  30.7 2.4 %collective-permute-done.6.lon_in._ = bf16[36,1024]{1,0:T(8,128)(2,1)S(1)} collective-permute-done((bf16[36,1024]{1,0:T(8,128)(2,1)S(1)}, bf16[36,1024]{1,0:T(8,128)(2,1)S(1)}, u32[]{:S(2)}, u32[]{:S(2)}) %collective-permute-start.6) | collective-permute-done | bytes 73760 | tf_op jit(solution)/shard_map/ppermute | solution.py:511
  33.2 2.4 %collective-permute-done.12.refs_2_ = bf16[1,256,256]{2,1,0:T(8,128)(2,1)S(1)} collective-permute-done((bf16[1,256,256]{2,1,0:T(8,128)(2,1)S(1)}, bf16[1,256,256]{2,1,0:T(8,128)(2,1)S(1)}, u32[]{:S(2)}, u32[]{:S(2)}) %collective-permute-start.12) | collective-permute-done | bytes 131104 | tf_op jit(solution)/shard_map/ppermute | solution.py:493
  35.7 1.2 %collective-permute-start.14 = (bf16[64,512]{1,0:T(8,128)(2,1)S(1)}, bf16[64,512]{1,0:T(8,128)(2,1)S(1)}, u32[]{:S(2)}, u32[]{:S(2)}) collective-permute-start(bf16[64,512]{1,0:T(8,128)(2,1)S(1)} %get-tuple-element.94), channel_id=1, source_target_pairs={{0,6},{1,7},{2,4},{3,5},{4,2},{5,3},{6,0},{7,1},{8,14},{9,15},{10,... | collective-permute-start | bytes 196616 | tf_op jit(solution)/shard_map/ppermute | solution.py:539
  36.8 3.3 %collective-permute-start.16 = (bf16[64,512]{1,0:T(8,128)(2,1)S(1)}, bf16[64,512]{1,0:T(8,128)(2,1)S(1)}, u32[]{:S(2)}, u32[]{:S(2)}) collective-permute-start(bf16[64,512]{1,0:T(8,128)(2,1)S(1)} %get-tuple-element.89._), channel_id=1, source_target_pairs={{0,2},{1,3},{2,0},{3,1},{4,6},{5,7},{6,4},{7,5},{8,10},{9,11},{10,... | collective-permute-start | bytes 196616 | tf_op jit(solution)/shard_map/ppermute | solution.py:539
  40.1 0.1 pack_lat.1
  40.3 0.7 %collective-permute-start.13 = (bf16[108,1024]{1,0:T(8,128)(2,1)S(1)}, bf16[108,1024]{1,0:T(8,128)(2,1)S(1)}, u32[]{:S(2)}, u32[]{:S(2)}) collective-permute-start(bf16[108,1024]{1,0:T(8,128)(2,1)S(1)} %pack_lat.1), channel_id=1, source_target_pairs={{24,0},{9,1},{26,2},{11,3},{28,4},{13,5},{30,6},{15,7},{0,8},{17,9... | collective-permute-start | bytes 663560 | tf_op jit(solution)/shard_map/ppermute | solution.py:545
  40.9 0.8 %place.1.placed._ = f32[288,1024]{1,0:T(8,128)S(1)} custom-call(bf16[144,1024]{1,0:T(8,128)(2,1)S(1)} %get-tuple-element.82._.refs_3_.inner_results, bf16[144,1024]{1,0:T(8,128)(2,1)S(1)} %get-tuple-element.83.outer_results, bf16[36,1024]{1,0:T(8,128)(2,1)S(1)} %collective-permute-done.6.lon_in._, bf16[36,1024]{1,0:T(8,128)(2,1)S(1)} %collective-permute-done.10.diag_in), custom_call_target="tpu_custom_call" | custom-call | bytes 1916928 | tf_op jit(solution)/shard_map/place/pallas_call | solution.py:404
  41.7 0.8 %collective-permute-done.14.refs_1_ = bf16[64,512]{1,0:T(8,128)(2,1)S(1)} collective-permute-done((bf16[64,512]{1,0:T(8,128)(2,1)S(1)}, bf16[64,512]{1,0:T(8,128)(2,1)S(1)}, u32[]{:S(2)}, u32[]{:S(2)}) %collective-permute-start.14) | collective-permute-done | bytes 65568 | tf_op jit(solution)/shard_map/ppermute | solution.py:539
  42.4 0.9 %collective-permute-done.15.refs_2_ = bf16[64,512]{1,0:T(8,128)(2,1)S(1)} collective-permute-done((bf16[64,512]{1,0:T(8,128)(2,1)S(1)}, bf16[64,512]{1,0:T(8,128)(2,1)S(1)}, u32[]{:S(2)}, u32[]{:S(2)}) %collective-permute-start.15) | collective-permute-done | bytes 65568 | tf_op jit(solution)/shard_map/ppermute | solution.py:539
  43.3 1.6 %collective-permute-start.19 = (bf16[64,512]{1,0:T(8,128)(2,1)S(1)}, bf16[64,512]{1,0:T(8,128)(2,1)S(1)}, u32[]{:S(2)}, u32[]{:S(2)}) collective-permute-start(bf16[64,512]{1,0:T(8,128)(2,1)S(1)} %line_sum.1.refs_0_), channel_id=1, source_target_pairs={{0,24},{8,16},{16,8},{24,0},{1,25},{9,17},{17,9},{25,1},{2,26},{10... | collective-permute-start | bytes 196616 | tf_op jit(solution)/shard_map/ppermute | solution.py:553
  45.0 0.8 %collective-permute-start.18 = (bf16[64,512]{1,0:T(8,128)(2,1)S(1)}, bf16[64,512]{1,0:T(8,128)(2,1)S(1)}, u32[]{:S(2)}, u32[]{:S(2)}) collective-permute-start(bf16[64,512]{1,0:T(8,128)(2,1)S(1)} %line_sum.1.refs_0_), channel_id=1, source_target_pairs={{0,16},{8,24},{16,0},{24,8},{1,17},{9,25},{17,1},{25,9},{2,18},{10... | collective-permute-start | bytes 196616 | tf_op jit(solution)/shard_map/ppermute | solution.py:553
  45.8 1.1 %collective-permute-start.17 = (bf16[64,512]{1,0:T(8,128)(2,1)S(1)}, bf16[64,512]{1,0:T(8,128)(2,1)S(1)}, u32[]{:S(2)}, u32[]{:S(2)}) collective-permute-start(bf16[64,512]{1,0:T(8,128)(2,1)S(1)} %line_sum.1.refs_0_), channel_id=1, source_target_pairs={{0,8},{8,0},{16,24},{24,16},{1,9},{9,1},{17,25},{25,17},{2,10},{10... | collective-permute-start | bytes 196616 | tf_op jit(solution)/shard_map/ppermute | solution.py:553
  46.9 0.5 collective-permute-done.13.lat_in
  47.4 1.0 %place_rest.1 = (bf16[288,512]{1,0:T(8,128)(2,1)}, bf16[288,512]{1,0:T(8,128)(2,1)}, f32[8,128]{1,0:T(8,128)S(1)}) custom-call(f32[288,1024]{1,0:T(8,128)S(1)} %place.1.placed._, bf16[108,1024]{1,0:T(8,128)(2,1)S(1)} %collective-permute-done.13.lat_in), custom_call_target="tpu_custom_call" | custom-call | bytes 1994752 | tf_op jit(solution)/shard_map/place_rest/pallas_call | solution.py:404
  48.4 0.4 collective-permute-done.19.refs_3_
  48.8 0.7 %collective-permute-done.18.refs_2_ = bf16[64,512]{1,0:T(8,128)(2,1)S(1)} collective-permute-done((bf16[64,512]{1,0:T(8,128)(2,1)S(1)}, bf16[64,512]{1,0:T(8,128)(2,1)S(1)}, u32[]{:S(2)}, u32[]{:S(2)}) %collective-permute-start.18) | collective-permute-done | bytes 65568 | tf_op jit(solution)/shard_map/ppermute | solution.py:553
  49.4 0.6 %collective-permute-done.17.refs_1_ = bf16[64,512]{1,0:T(8,128)(2,1)S(1)} collective-permute-done((bf16[64,512]{1,0:T(8,128)(2,1)S(1)}, bf16[64,512]{1,0:T(8,128)(2,1)S(1)}, u32[]{:S(2)}, u32[]{:S(2)}) %collective-permute-start.17) | collective-permute-done | bytes 65568 | tf_op jit(solution)/shard_map/ppermute | solution.py:553
  50.0 0.9 %finish.1 = (f32[64,1536]{1,0:T(8,128)}, f32[64,512]{1,0:T(8,128)}) custom-call(f32[8,128]{1,0:T(8,128)S(1)} %get-tuple-element.92._, bf16[64,512]{1,0:T(8,128)(2,1)S(1)} %line_sum.1.refs_0_, bf16[64,512]{1,0:T(8,128)(2,1)S(1)} %collective-permute-done.17.refs_1_, bf16[64,512]{1,0:T(8,128)(2,1)S(1)} %collective-permute-done.18.refs_2_, ...), custom_call_target="tpu_custom_call" | custom-call | bytes 790528 | tf_op jit(solution)/shard_map/finish/pallas_call | solution.py:404
  (22 shorter events, 0.3 us)
Async XLA Ops:
  0.6 1.0 %copy-start.3 = (bf16[2,6,24,512]{3,2,1,0:T(8,128)(2,1)S(1)}, bf16[2,6,24,512]{3,2,1,0:T(8,128)(2,1)}, u32[]{:S(2)}) copy-start(bf16[2,6,24,512]{3,2,1,0:T(8,128)(2,1)} %param.5) | copy-start | bytes 884740
  0.6 1.0 %copy-start.2 = (bf16[2,6,24,512]{3,2,1,0:T(8,128)(2,1)S(1)}, bf16[2,6,24,512]{3,2,1,0:T(8,128)(2,1)}, u32[]{:S(2)}) copy-start(bf16[2,6,24,512]{3,2,1,0:T(8,128)(2,1)} %param.4) | copy-start | bytes 884740
  1.7 11.1 %copy-start.1 = (bf16[512,512]{1,0:T(8,128)(2,1)S(1)}, bf16[512,512]{1,0:T(8,128)(2,1)}, u32[]{:S(2)}) copy-start(bf16[512,512]{1,0:T(8,128)(2,1)} %refs_7_.1) | copy-start | bytes 1572868
  2.0 10.7 %copy-start = (bf16[512,1536]{1,0:T(8,128)(2,1)S(1)}, bf16[512,1536]{1,0:T(8,128)(2,1)}, u32[]{:S(2)}) copy-start(bf16[512,1536]{1,0:T(8,128)(2,1)} %refs_6_.1) | copy-start | bytes 4718596
  2.1 11.4 %collective-permute-start = (bf16[72,1024]{1,0:T(8,128)(2,1)S(1)}, bf16[72,1024]{1,0:T(8,128)(2,1)S(1)}, u32[]{:S(2)}, u32[]{:S(2)}) collective-permute-start(bf16[72,1024]{1,0:T(8,128)(2,1)S(1)} %get-tuple-element.62), channel_id=1, source_target_pairs={{0,24},{1,9},{2,26},{3,11},{4,28},{5,13},{6,30},{7,15},{8,0},{9,17... | collective-permute-start | bytes 442376 | tf_op jit(solution)/shard_map/ppermute | solution.py:458
  6.0 9.6 %collective-permute-start.1 = (bf16[36,1024]{1,0:T(8,128)(2,1)S(1)}, bf16[36,1024]{1,0:T(8,128)(2,1)S(1)}, u32[]{:S(2)}, u32[]{:S(2)}) collective-permute-start(bf16[36,1024]{1,0:T(8,128)(2,1)S(1)} %get-tuple-element.53._), channel_id=1, source_target_pairs={{0,7},{1,0},{2,1},{3,2},{4,3},{5,4},{6,5},{7,6},{8,15},{9,8},{10,9... | collective-permute-start | bytes 221192 | tf_op jit(solution)/shard_map/ppermute | solution.py:459
  8.4 7.2 %collective-permute-start.2 = (bf16[36,1024]{1,0:T(8,128)(2,1)S(1)}, bf16[36,1024]{1,0:T(8,128)(2,1)S(1)}, u32[]{:S(2)}, u32[]{:S(2)}) collective-permute-start(bf16[36,1024]{1,0:T(8,128)(2,1)S(1)} %get-tuple-element.66), channel_id=1, source_target_pairs={{0,15},{1,24},{2,9},{3,26},{4,11},{5,28},{6,13},{7,30},{8,23},{9,0... | collective-permute-start | bytes 221192 | tf_op jit(solution)/shard_map/ppermute | solution.py:461
  9.4 6.2 %collective-permute-start.3 = (bf16[36,1024]{1,0:T(8,128)(2,1)S(1)}, bf16[36,1024]{1,0:T(8,128)(2,1)S(1)}, u32[]{:S(2)}, u32[]{:S(2)}) collective-permute-start(bf16[36,1024]{1,0:T(8,128)(2,1)S(1)} %get-tuple-element.67), channel_id=1, source_target_pairs={{0,24},{1,9},{2,26},{3,11},{4,28},{5,13},{6,30},{7,15},{8,0},{9,17... | collective-permute-start | bytes 221192 | tf_op jit(solution)/shard_map/ppermute | solution.py:460
  18.0 1.6 %collective-permute-start.4 = (bf16[2,256,256]{2,1,0:T(8,128)(2,1)S(1)}, bf16[2,256,256]{2,1,0:T(8,128)(2,1)S(1)}, u32[]{:S(2)}, u32[]{:S(2)}) collective-permute-start(bf16[2,256,256]{2,1,0:T(8,128)(2,1)S(1)} %get-tuple-element.72), channel_id=1, source_target_pairs={{0,1},{1,0},{2,3},{3,2},{4,5},{5,4},{6,7},{7,6},{8,9},{9,8},{10,11... | collective-permute-start | bytes 786440 | tf_op jit(solution)/shard_map/ppermute | solution.py:484
  18.1 3.1 %collective-permute-start.5 = (bf16[2,256,256]{2,1,0:T(8,128)(2,1)S(1)}, bf16[2,256,256]{2,1,0:T(8,128)(2,1)S(1)}, u32[]{:S(2)}, u32[]{:S(2)}) collective-permute-start(bf16[2,256,256]{2,1,0:T(8,128)(2,1)S(1)} %get-tuple-element.74), channel_id=1, source_target_pairs={{0,1},{1,0},{2,3},{3,2},{4,5},{5,4},{6,7},{7,6},{8,9},{9,8},{10,11... | collective-permute-start | bytes 786440 | tf_op jit(solution)/shard_map/ppermute | solution.py:484
  19.7 6.4 %collective-permute-start.8 = (bf16[2,256,256]{2,1,0:T(8,128)(2,1)S(1)}, bf16[2,256,256]{2,1,0:T(8,128)(2,1)S(1)}, u32[]{:S(2)}, u32[]{:S(2)}) collective-permute-start(bf16[2,256,256]{2,1,0:T(8,128)(2,1)S(1)} %chip_sum.2._), channel_id=1, source_target_pairs={{0,8},{1,17},{2,10},{3,19},{4,12},{5,21},{6,14},{7,23},{8,0},{9,25... | collective-permute-start | bytes 786440 | tf_op jit(solution)/shard_map/ppermute | solution.py:493
  21.3 8.3 %collective-permute-start.9 = (bf16[2,256,256]{2,1,0:T(8,128)(2,1)S(1)}, bf16[2,256,256]{2,1,0:T(8,128)(2,1)S(1)}, u32[]{:S(2)}, u32[]{:S(2)}) collective-permute-start(bf16[2,256,256]{2,1,0:T(8,128)(2,1)S(1)} %chip_sum.3.__), channel_id=1, source_target_pairs={{0,8},{1,17},{2,10},{3,19},{4,12},{5,21},{6,14},{7,23},{8,0},{9,25... | collective-permute-start | bytes 786440 | tf_op jit(solution)/shard_map/ppermute | solution.py:493
  22.6 3.5 %collective-permute-start.7 = (bf16[2,256,512]{2,1,0:T(8,128)(2,1)S(1)}, bf16[2,256,512]{2,1,0:T(8,128)(2,1)S(1)}, u32[]{:S(2)}, u32[]{:S(2)}) collective-permute-start(bf16[2,256,512]{2,1,0:T(8,128)(2,1)S(1)} %get-tuple-element.84), channel_id=1, source_target_pairs={{0,1},{1,0},{2,3},{3,2},{4,5},{5,4},{6,7},{7,6},{8,9},{9,8},{10,11... | collective-permute-start | bytes 1572872 | tf_op jit(solution)/shard_map/ppermute | solution.py:504
  26.2 6.9 %collective-permute-start.11 = (bf16[1,256,256]{2,1,0:T(8,128)(2,1)S(1)}, bf16[1,256,256]{2,1,0:T(8,128)(2,1)S(1)}, u32[]{:S(2)}, u32[]{:S(2)}) collective-permute-start(bf16[1,256,256]{2,1,0:T(8,128)(2,1)S(1)} %get-tuple-element.85._.refs_3_), channel_id=1, source_target_pairs={{0,16},{1,9},{2,18},{3,11},{4,20},{5,13},{6,22},{7,15},{8,24},{9,1... | collective-permute-start | bytes 393224 | tf_op jit(solution)/shard_map/ppermute | solution.py:493
  27.4 5.7 %collective-permute-start.6 = (bf16[36,1024]{1,0:T(8,128)(2,1)S(1)}, bf16[36,1024]{1,0:T(8,128)(2,1)S(1)}, u32[]{:S(2)}, u32[]{:S(2)}) collective-permute-start(bf16[36,1024]{1,0:T(8,128)(2,1)S(1)} %pack_lon.1), channel_id=1, source_target_pairs={{7,0},{0,1},{1,2},{2,3},{3,4},{4,5},{5,6},{6,7},{15,8},{8,9},{9,10... | collective-permute-start | bytes 221192 | tf_op jit(solution)/shard_map/ppermute | solution.py:511
  29.7 5.9 %collective-permute-start.12 = (bf16[1,256,256]{2,1,0:T(8,128)(2,1)S(1)}, bf16[1,256,256]{2,1,0:T(8,128)(2,1)S(1)}, u32[]{:S(2)}, u32[]{:S(2)}) collective-permute-start(bf16[1,256,256]{2,1,0:T(8,128)(2,1)S(1)} %get-tuple-element.86._), channel_id=1, source_target_pairs={{0,16},{1,9},{2,18},{3,11},{4,20},{5,13},{6,22},{7,15},{8,24},{9,1... | collective-permute-start | bytes 393224 | tf_op jit(solution)/shard_map/ppermute | solution.py:493
  30.6 10.3 %collective-permute-start.10 = (bf16[36,1024]{1,0:T(8,128)(2,1)S(1)}, bf16[36,1024]{1,0:T(8,128)(2,1)S(1)}, u32[]{:S(2)}, u32[]{:S(2)}) collective-permute-start(bf16[36,1024]{1,0:T(8,128)(2,1)S(1)} %pack_diag.1), channel_id=1, source_target_pairs={{15,0},{24,1},{9,2},{26,3},{11,4},{28,5},{13,6},{30,7},{23,8},{0,9... | collective-permute-start | bytes 221192 | tf_op jit(solution)/shard_map/ppermute | solution.py:527
  35.7 6.8 %collective-permute-start.14 = (bf16[64,512]{1,0:T(8,128)(2,1)S(1)}, bf16[64,512]{1,0:T(8,128)(2,1)S(1)}, u32[]{:S(2)}, u32[]{:S(2)}) collective-permute-start(bf16[64,512]{1,0:T(8,128)(2,1)S(1)} %get-tuple-element.94), channel_id=1, source_target_pairs={{0,6},{1,7},{2,4},{3,5},{4,2},{5,3},{6,0},{7,1},{8,14},{9,15},{10,... | collective-permute-start | bytes 196616 | tf_op jit(solution)/shard_map/ppermute | solution.py:539
  36.8 6.5 %collective-permute-start.15 = (bf16[64,512]{1,0:T(8,128)(2,1)S(1)}, bf16[64,512]{1,0:T(8,128)(2,1)S(1)}, u32[]{:S(2)}, u32[]{:S(2)}) collective-permute-start(bf16[64,512]{1,0:T(8,128)(2,1)S(1)} %get-tuple-element.95), channel_id=1, source_target_pairs={{0,4},{1,5},{2,6},{3,7},{4,0},{5,1},{6,2},{7,3},{8,12},{9,13},{10,... | collective-permute-start | bytes 196616 | tf_op jit(solution)/shard_map/ppermute | solution.py:539
  36.8 6.5 %collective-permute-start.16 = (bf16[64,512]{1,0:T(8,128)(2,1)S(1)}, bf16[64,512]{1,0:T(8,128)(2,1)S(1)}, u32[]{:S(2)}, u32[]{:S(2)}) collective-permute-start(bf16[64,512]{1,0:T(8,128)(2,1)S(1)} %get-tuple-element.89._), channel_id=1, source_target_pairs={{0,2},{1,3},{2,0},{3,1},{4,6},{5,7},{6,4},{7,5},{8,10},{9,11},{10,... | collective-permute-start | bytes 196616 | tf_op jit(solution)/shard_map/ppermute | solution.py:539
  40.3 7.1 %collective-permute-start.13 = (bf16[108,1024]{1,0:T(8,128)(2,1)S(1)}, bf16[108,1024]{1,0:T(8,128)(2,1)S(1)}, u32[]{:S(2)}, u32[]{:S(2)}) collective-permute-start(bf16[108,1024]{1,0:T(8,128)(2,1)S(1)} %pack_lat.1), channel_id=1, source_target_pairs={{24,0},{9,1},{26,2},{11,3},{28,4},{13,5},{30,6},{15,7},{0,8},{17,9... | collective-permute-start | bytes 663560 | tf_op jit(solution)/shard_map/ppermute | solution.py:545
  43.3 5.4 %collective-permute-start.19 = (bf16[64,512]{1,0:T(8,128)(2,1)S(1)}, bf16[64,512]{1,0:T(8,128)(2,1)S(1)}, u32[]{:S(2)}, u32[]{:S(2)}) collective-permute-start(bf16[64,512]{1,0:T(8,128)(2,1)S(1)} %line_sum.1.refs_0_), channel_id=1, source_target_pairs={{0,24},{8,16},{16,8},{24,0},{1,25},{9,17},{17,9},{25,1},{2,26},{10... | collective-permute-start | bytes 196616 | tf_op jit(solution)/shard_map/ppermute | solution.py:553
  45.0 4.5 %collective-permute-start.18 = (bf16[64,512]{1,0:T(8,128)(2,1)S(1)}, bf16[64,512]{1,0:T(8,128)(2,1)S(1)}, u32[]{:S(2)}, u32[]{:S(2)}) collective-permute-start(bf16[64,512]{1,0:T(8,128)(2,1)S(1)} %line_sum.1.refs_0_), channel_id=1, source_target_pairs={{0,16},{8,24},{16,0},{24,8},{1,17},{9,25},{17,1},{25,9},{2,18},{10... | collective-permute-start | bytes 196616 | tf_op jit(solution)/shard_map/ppermute | solution.py:553
  45.8 4.3 %collective-permute-start.17 = (bf16[64,512]{1,0:T(8,128)(2,1)S(1)}, bf16[64,512]{1,0:T(8,128)(2,1)S(1)}, u32[]{:S(2)}, u32[]{:S(2)}) collective-permute-start(bf16[64,512]{1,0:T(8,128)(2,1)S(1)} %line_sum.1.refs_0_), channel_id=1, source_target_pairs={{0,8},{8,0},{16,24},{24,16},{1,9},{9,1},{17,25},{25,17},{2,10},{10... | collective-permute-start | bytes 196616 | tf_op jit(solution)/shard_map/ppermute | solution.py:553

commit v22 on v18

--- a/solution.py
+++ b/solution.py
@@ -19,6 +19,7 @@
 TOKENS = 2 * WIN
 QUARTER = HALF // 2
 LANES = 128
+FINISH_ROWS = 16
 
 epsilon = 1e-05
 LONG = 13 * 10**8
@@ -379,21 +380,19 @@
 
 
 def finish_kernel(_, *refs):
-    *parts, qkv_out, proj_out = refs
-    lat, _, size = place()
-    width = parts[0].shape[1]
-    for step, part in enumerate(parts):
-        share = lat ^ step
-        total = part[...].astype(F32)
-        of_qkv = 3 * size // 4
-
-        @pl.when(share < of_qkv)
-        def _():
-            qkv_out[:, pl.ds(pl.multiple_of(share * width, width), width)] = total
-
-        @pl.when(share >= of_qkv)
-        def _():
-            proj_out[:, pl.ds(pl.multiple_of((share - of_qkv) * width, width), width)] = total
+    *parts, qkv_out, proj_out, total, done = refs
+    lat = lax.axis_index("lat")
+    width, split = parts[0].shape[1], qkv_out.shape[1]
+    copies = []
+    for block in range(total.shape[0] // FINISH_ROWS):
+        rows = slice(block * FINISH_ROWS, (block + 1) * FINISH_ROWS)
+        for step, part in enumerate(parts):
+            total[rows, pl.ds(pl.multiple_of((lat ^ step) * width, width), width)] = part[rows, :].astype(F32)
+        for index, (out, lanes) in enumerate(((qkv_out, slice(0, split)), (proj_out, slice(split, total.shape[1])))):
+            copies.append(pltpu.make_async_copy(total.at[rows, lanes], out.at[rows, :], done.at[block, index]))
+            copies[-1].start()
+    for copy in copies:
+        copy.wait()
 
 
 def call(kernel, outs, *args, name, flops=0, limit=32, scratch=(), unread=(), beside=False):
@@ -558,12 +557,20 @@
         placed, lat_home,
         name="place_rest",
     )
-    qkv_grad, proj_grad = call(
+    vmem, anywhere = pl.BlockSpec(memory_space=pltpu.VMEM), pl.BlockSpec(memory_space=pl.ANY)
+    qkv_grad, proj_grad = pl.pallas_call(
         finish_kernel,
-        [((rows, 3 * width), F32), ((rows, width), F32)],
-        done, line_sum, *shared,
-        name="finish", unread=(0,),
-    )
+        out_shape=[jax.ShapeDtypeStruct((rows, lanes * width), F32) for lanes in (3, 1)],
+        in_specs=[anywhere, *[vmem] * lat_size],
+        out_specs=[anywhere, anywhere],
+        scratch_shapes=[
+            pltpu.VMEM((rows, 4 * width), F32),
+            pltpu.SemaphoreType.DMA((rows // FINISH_ROWS, 2)),
+        ],
+        compiler_params=pltpu.CompilerParams(vmem_limit_bytes=32 * 2**20),
+        cost_estimate=pl.CostEstimate(flops=0, bytes_accessed=10**6, transcendentals=0),
+        name="finish",
+    )(done, line_sum, *shared)
     return (field_out.reshape(fields.shape), d_fields.reshape(fields.shape), qkv_grad, jnp.transpose(proj_grad))
 
 

time: 50 us -> 50 us (level)
    pallas_call x0 -> x1, Pallas kernels: none -> 0.86 us  [per_device(): pl.pallas_call(finish_kernel, out_shape=[jax.ShapeDtypeStruct((rows, lane...]
    pallas_call x22 -> x21, Pallas kernels: 11.8 us -> 10.9 us  [call(): pl.pallas_call(kernel, out_shape=shapes, in_specs=[anywhere if i in unrea...]
where the time goes in v22:
time: 50 us; the launch traced here: 49.9 us
  starting transfers between devices  25.6 us (51%)
  Pallas kernels  11.8 us (24%)
  waiting for transfers between devices  10.8 us (22%)
  local copies, waits for them, and re-layouts  0.94 us (2%)
  between operations  0.82 us (2%)
    pallas_call x21, Pallas kernels, call(): pl.pallas_call(kernel, out_shape=shapes, in_specs=[anywhere if i in unrea...  10.9 us
    ppermute x4, starting transfers between devices, halving(): return lax.ppermute(send, both, route)  5.72 us
    ppermute x3, starting transfers between devices, per_device(): lax.ppermute(parts[step], 'lon', [(j, j ^ 2 * step) for j in range(lon_si...  4.96 us
    ppermute x4, waiting for transfers between devices, halving(): return lax.ppermute(send, both, route)  4.71 us
    ppermute x1, starting transfers between devices, per_device(): inner_in = lax.ppermute(inner_lat, both, lat_route)  3.94 us
    ppermute x3, starting transfers between devices, per_device(): lax.ppermute(line_sum, 'lat', [(i, i ^ step) for i in range(lat_size)])  3.55 us
    ppermute x1, waiting for transfers between devices, per_device(): lon_home = lax.ppermute(lon_back, both, back(lon_route))  2.15 us
    ppermute x3, waiting for transfers between devices, per_device(): lax.ppermute(parts[step], 'lon', [(j, j ^ 2 * step) for j in range(lon_si...  1.94 us
  transfers between devices with their start and end apart: 20, of which 9 were waited for; matrix products, arithmetic and copies ran while one was open for 0% of the time, Pallas kernels for 16%

profile of v22, /device:TPU:0, one launch (start us, length us, event | category | flops | bytes accessed | tf_op | source)
XLA Modules:
  0.0 49.9 jit_solution(1540974817435060749)
XLA Ops:
  0.7 0.1 order.1
  0.8 0.8 %copy-done.3 = bf16[2,6,24,512]{3,2,1,0:T(8,128)(2,1)S(1)} copy-done((bf16[2,6,24,512]{3,2,1,0:T(8,128)(2,1)S(1)}, bf16[2,6,24,512]{3,2,1,0:T(8,128)(2,1)}, u32[]{:S(2)}) %copy-start.3) | copy-done | bytes 294936
  1.6 0.1 copy-done.2
  1.7 0.4 pack.1
  2.1 3.9 %collective-permute-start = (bf16[72,1024]{1,0:T(8,128)(2,1)S(1)}, bf16[72,1024]{1,0:T(8,128)(2,1)S(1)}, u32[]{:S(2)}, u32[]{:S(2)}) collective-permute-start(bf16[72,1024]{1,0:T(8,128)(2,1)S(1)} %get-tuple-element.62), channel_id=1, source_target_pairs={{0,24},{1,9},{2,26},{3,11},{4,28},{5,13},{6,30},{7,15},{8,0},{9,17... | collective-permute-start | bytes 442376 | tf_op jit(solution)/shard_map/ppermute | solution.py:457
  6.0 1.8 %collective-permute-start.1 = (bf16[36,1024]{1,0:T(8,128)(2,1)S(1)}, bf16[36,1024]{1,0:T(8,128)(2,1)S(1)}, u32[]{:S(2)}, u32[]{:S(2)}) collective-permute-start(bf16[36,1024]{1,0:T(8,128)(2,1)S(1)} %get-tuple-element.53._), channel_id=1, source_target_pairs={{0,7},{1,0},{2,1},{3,2},{4,3},{5,4},{6,5},{7,6},{8,15},{9,8},{10,9... | collective-permute-start | bytes 221192 | tf_op jit(solution)/shard_map/ppermute | solution.py:458
  7.8 0.6 %pack_rest.1 = (bf16[36,1024]{1,0:T(8,128)(2,1)S(1)}, bf16[36,1024]{1,0:T(8,128)(2,1)S(1)}, f32[72,1024]{1,0:T(8,128)S(1)}, f32[72,1024]{1,0:T(8,128)S(1)}) custom-call(bf16[36,1024]{1,0:T(8,128)(2,1)S(1)} %get-tuple-element.53._, bf16[288,512]{1,0:T(8,128)(2,1)S(1)} %bitcast.6, bf16[288,512]{1,0:T(8,128)(2,1)S(1)} %bitcast.8, ...), custom_call_target="tpu_custom_call" | custom-call | flops 500000000 | bytes 1525248 | tf_op jit(solution)/shard_map/pack_rest/pallas_call | solution.py:403
  8.4 1.5 %collective-permute-start.2 = (bf16[36,1024]{1,0:T(8,128)(2,1)S(1)}, bf16[36,1024]{1,0:T(8,128)(2,1)S(1)}, u32[]{:S(2)}, u32[]{:S(2)}) collective-permute-start(bf16[36,1024]{1,0:T(8,128)(2,1)S(1)} %get-tuple-element.66), channel_id=1, source_target_pairs={{0,24},{1,9},{2,26},{3,11},{4,28},{5,13},{6,30},{7,15},{8,0},{9,17... | collective-permute-start | bytes 221192 | tf_op jit(solution)/shard_map/ppermute | solution.py:459
  9.9 1.6 %collective-permute-start.3 = (bf16[36,1024]{1,0:T(8,128)(2,1)S(1)}, bf16[36,1024]{1,0:T(8,128)(2,1)S(1)}, u32[]{:S(2)}, u32[]{:S(2)}) collective-permute-start(bf16[36,1024]{1,0:T(8,128)(2,1)S(1)} %get-tuple-element.67), channel_id=1, source_target_pairs={{0,15},{1,24},{2,9},{3,26},{4,11},{5,28},{6,13},{7,30},{8,23},{9,0... | collective-permute-start | bytes 221192 | tf_op jit(solution)/shard_map/ppermute | solution.py:460
  11.5 0.7 %own.1 = (f32[72,512]{1,0:T(8,128)S(1)}, f32[72,1536]{1,0:T(8,128)S(1)}, f32[72,512]{1,0:T(8,128)S(1)}) custom-call(f32[72,1024]{1,0:T(8,128)S(1)} %get-tuple-element.58.inner_own.own, bf16[512,1536]{1,0:T(8,128)(2,1)S(1)} %copy-done, bf16[512,512]{1,0:T(8,128)(2,1)S(1)} %copy-done.1), custom_call_target="tpu_custom_call" | custom-call | flops 500000000 | bytes 3129344 | tf_op jit(solution)/shard_map/own/pallas_call | solution.py:403
  12.2 2.1 %inner.1 = (f32[2,256,512]{2,1,0:T(8,128)S(1)}, bf16[144,512]{1,0:T(8,128)(2,1)S(1)}, bf16[144,512]{1,0:T(8,128)(2,1)S(1)}, bf16[2,256,144]{2,1,0:T(8,128)(2,1)S...) custom-call(f32[72,1024]{1,0:T(8,128)S(1)} %get-tuple-element.58.inner_own.own, ...), custom_call_target="tpu_custom_call" | custom-call | flops 1000000000 | bytes 5505024 | tf_op jit(solution)/shard_map/inner/pallas_call | solution.py:403
  14.4 2.4 %outer.1 = (bf16[2,256,256]{2,1,0:T(8,128)(2,1)S(1)}, bf16[2,256,256]{2,1,0:T(8,128)(2,1)S(1)}, bf16[144,512]{1,0:T(8,128)(2,1)S(1)}, bf16[144,512]{1,0:T(8,128)...) custom-call(f32[72,1024]{1,0:T(8,128)S(1)} %get-tuple-element.65.own, ...), custom_call_target="tpu_custom_call" | custom-call | flops 1000000000 | bytes 5365760 | tf_op jit(solution)/shard_map/outer/pallas_call | solution.py:403
  16.8 0.1 collective-permute-start.4
  16.9 0.4 collective-permute-start.5
  17.3 0.4 keep.1
  17.8 0.6 %collective-permute-done.4.refs_1_ = bf16[2,256,256]{2,1,0:T(8,128)(2,1)S(1)} collective-permute-done((bf16[2,256,256]{2,1,0:T(8,128)(2,1)S(1)}, bf16[2,256,256]{2,1,0:T(8,128)(2,1)S(1)}, u32[]{:S(2)}, u32[]{:S(2)}) %collective-permute-start.4) | collective-permute-done | bytes 262176 | tf_op jit(solution)/shard_map/ppermute | solution.py:483
  18.4 0.1 chip_sum.2._
  18.4 2.2 %collective-permute-start.8 = (bf16[2,256,256]{2,1,0:T(8,128)(2,1)S(1)}, bf16[2,256,256]{2,1,0:T(8,128)(2,1)S(1)}, u32[]{:S(2)}, u32[]{:S(2)}) collective-permute-start(bf16[2,256,256]{2,1,0:T(8,128)(2,1)S(1)} %chip_sum.2._), channel_id=1, source_target_pairs={{0,8},{1,17},{2,10},{3,19},{4,12},{5,21},{6,14},{7,23},{8,0},{9,25... | collective-permute-start | bytes 786440 | tf_op jit(solution)/shard_map/ppermute | solution.py:492
  20.6 0.1 chip_sum.3.__
  20.7 0.3 collective-permute-start.9
  21.0 0.7 %rest.1 = (bf16[2,256,512]{2,1,0:T(8,128)(2,1)S(1)}, bf16[2,256,512]{2,1,0:T(8,128)(2,1)S(1)}) custom-call(bf16[2,256,256]{2,1,0:T(8,128)(2,1)S(1)} %chip_sum.2._, bf16[2,256,256]{2,1,0:T(8,128)(2,1)S(1)} %chip_sum.3.__, bf16[2,256,144]{2,1,0:T(8,128)(2,1)S(1)} %get-tuple-element.63.refs_0_, bf16[144,2048]{1,0:T(8,128)(2,1)S(1)} %get-tuple-element.64.refs_1_.refs_2_, ...), custom_call_target="tpu_custom_call" | custom-call | tf_op jit(solution)/shard_map/rest/pallas_call | solution.py:403
  21.7 0.1 collective-permute-start.7
  21.8 0.9 %outputs.1 = (bf16[144,1024]{1,0:T(8,128)(2,1)S(1)}, bf16[144,1024]{1,0:T(8,128)(2,1)S(1)}) custom-call(bf16[2,256,512]{2,1,0:T(8,128)(2,1)S(1)} %get-tuple-element.77._.refs_0_, bf16[144,512]{1,0:T(8,128)(2,1)S(1)} %get-tuple-element.78.refs_0_, bf16[144,512]{1,0:T(8,128)(2,1)S(1)} %get-tuple-element.79.refs_1_, ...), custom_call_target="tpu_custom_call" | custom-call | flops 10000000000 | bytes 4980736 | tf_op jit(solution)/shard_map/outputs/pallas_call | solution.py:403
  22.7 2.3 %collective-permute-done.8.refs_2_ = bf16[2,256,256]{2,1,0:T(8,128)(2,1)S(1)} collective-permute-done((bf16[2,256,256]{2,1,0:T(8,128)(2,1)S(1)}, bf16[2,256,256]{2,1,0:T(8,128)(2,1)S(1)}, u32[]{:S(2)}, u32[]{:S(2)}) %collective-permute-start.8) | collective-permute-done | bytes 262176 | tf_op jit(solution)/shard_map/ppermute | solution.py:492
  25.0 0.1 halve1.2
  25.1 1.5 %collective-permute-start.11 = (bf16[1,256,256]{2,1,0:T(8,128)(2,1)S(1)}, bf16[1,256,256]{2,1,0:T(8,128)(2,1)S(1)}, u32[]{:S(2)}, u32[]{:S(2)}) collective-permute-start(bf16[1,256,256]{2,1,0:T(8,128)(2,1)S(1)} %get-tuple-element.85._.refs_3_), channel_id=1, source_target_pairs={{0,16},{1,9},{2,18},{3,11},{4,20},{5,13},{6,22},{7,15},{8,24},{9,1... | collective-permute-start | bytes 393224 | tf_op jit(solution)/shard_map/ppermute | solution.py:492
  26.5 0.1 pack_lon.1
  26.8 1.4 %collective-permute-done.9.refs_2_ = bf16[2,256,256]{2,1,0:T(8,128)(2,1)S(1)} collective-permute-done((bf16[2,256,256]{2,1,0:T(8,128)(2,1)S(1)}, bf16[2,256,256]{2,1,0:T(8,128)(2,1)S(1)}, u32[]{:S(2)}, u32[]{:S(2)}) %collective-permute-start.9) | collective-permute-done | bytes 262176 | tf_op jit(solution)/shard_map/ppermute | solution.py:492
  28.2 0.1 halve1.3
  28.3 1.8 %collective-permute-start.12 = (bf16[1,256,256]{2,1,0:T(8,128)(2,1)S(1)}, bf16[1,256,256]{2,1,0:T(8,128)(2,1)S(1)}, u32[]{:S(2)}, u32[]{:S(2)}) collective-permute-start(bf16[1,256,256]{2,1,0:T(8,128)(2,1)S(1)} %get-tuple-element.86._), channel_id=1, source_target_pairs={{0,16},{1,9},{2,18},{3,11},{4,20},{5,13},{6,22},{7,15},{8,24},{9,1... | collective-permute-start | bytes 393224 | tf_op jit(solution)/shard_map/ppermute | solution.py:492
  30.0 0.1 pack_diag.1
  30.2 0.1 collective-permute-start.10
  30.3 2.1 %collective-permute-done.6.lon_in._ = bf16[36,1024]{1,0:T(8,128)(2,1)S(1)} collective-permute-done((bf16[36,1024]{1,0:T(8,128)(2,1)S(1)}, bf16[36,1024]{1,0:T(8,128)(2,1)S(1)}, u32[]{:S(2)}, u32[]{:S(2)}) %collective-permute-start.6) | collective-permute-done | bytes 73760 | tf_op jit(solution)/shard_map/ppermute | solution.py:510
  32.4 1.0 %collective-permute-done.12.refs_2_ = bf16[1,256,256]{2,1,0:T(8,128)(2,1)S(1)} collective-permute-done((bf16[1,256,256]{2,1,0:T(8,128)(2,1)S(1)}, bf16[1,256,256]{2,1,0:T(8,128)(2,1)S(1)}, u32[]{:S(2)}, u32[]{:S(2)}) %collective-permute-start.12) | collective-permute-done | bytes 131104 | tf_op jit(solution)/shard_map/ppermute | solution.py:492
  33.5 4.3 %collective-permute-start.14 = (bf16[64,512]{1,0:T(8,128)(2,1)S(1)}, bf16[64,512]{1,0:T(8,128)(2,1)S(1)}, u32[]{:S(2)}, u32[]{:S(2)}) collective-permute-start(bf16[64,512]{1,0:T(8,128)(2,1)S(1)} %get-tuple-element.94), channel_id=1, source_target_pairs={{0,6},{1,7},{2,4},{3,5},{4,2},{5,3},{6,0},{7,1},{8,14},{9,15},{10,... | collective-permute-start | bytes 196616 | tf_op jit(solution)/shard_map/ppermute | solution.py:538
  37.8 0.6 %collective-permute-start.16 = (bf16[64,512]{1,0:T(8,128)(2,1)S(1)}, bf16[64,512]{1,0:T(8,128)(2,1)S(1)}, u32[]{:S(2)}, u32[]{:S(2)}) collective-permute-start(bf16[64,512]{1,0:T(8,128)(2,1)S(1)} %get-tuple-element.89._), channel_id=1, source_target_pairs={{0,2},{1,3},{2,0},{3,1},{4,6},{5,7},{6,4},{7,5},{8,10},{9,11},{10,... | collective-permute-start | bytes 196616 | tf_op jit(solution)/shard_map/ppermute | solution.py:538
  38.4 0.1 pack_lat.1
  38.6 1.7 %collective-permute-start.13 = (bf16[108,1024]{1,0:T(8,128)(2,1)S(1)}, bf16[108,1024]{1,0:T(8,128)(2,1)S(1)}, u32[]{:S(2)}, u32[]{:S(2)}) collective-permute-start(bf16[108,1024]{1,0:T(8,128)(2,1)S(1)} %pack_lat.1), channel_id=1, source_target_pairs={{24,0},{9,1},{26,2},{11,3},{28,4},{13,5},{30,6},{15,7},{0,8},{17,9... | collective-permute-start | bytes 663560 | tf_op jit(solution)/shard_map/ppermute | solution.py:544
  40.3 0.8 %place.1.placed._ = f32[288,1024]{1,0:T(8,128)S(1)} custom-call(bf16[144,1024]{1,0:T(8,128)(2,1)S(1)} %get-tuple-element.82._.refs_3_.inner_results, bf16[144,1024]{1,0:T(8,128)(2,1)S(1)} %get-tuple-element.83.outer_results, bf16[36,1024]{1,0:T(8,128)(2,1)S(1)} %collective-permute-done.6.lon_in._, bf16[36,1024]{1,0:T(8,128)(2,1)S(1)} %collective-permute-done.10.diag_in), custom_call_target="tpu_custom_call" | custom-call | bytes 1916928 | tf_op jit(solution)/shard_map/place/pallas_call | solution.py:403
  41.1 1.9 %collective-permute-done.15.refs_2_ = bf16[64,512]{1,0:T(8,128)(2,1)S(1)} collective-permute-done((bf16[64,512]{1,0:T(8,128)(2,1)S(1)}, bf16[64,512]{1,0:T(8,128)(2,1)S(1)}, u32[]{:S(2)}, u32[]{:S(2)}) %collective-permute-start.15) | collective-permute-done | bytes 65568 | tf_op jit(solution)/shard_map/ppermute | solution.py:538
  43.1 0.9 %collective-permute-start.19 = (bf16[64,512]{1,0:T(8,128)(2,1)S(1)}, bf16[64,512]{1,0:T(8,128)(2,1)S(1)}, u32[]{:S(2)}, u32[]{:S(2)}) collective-permute-start(bf16[64,512]{1,0:T(8,128)(2,1)S(1)} %line_sum.1.refs_0_), channel_id=1, source_target_pairs={{0,24},{8,16},{16,8},{24,0},{1,25},{9,17},{17,9},{25,1},{2,26},{10... | collective-permute-start | bytes 196616 | tf_op jit(solution)/shard_map/ppermute | solution.py:552
  44.0 0.8 %collective-permute-start.18 = (bf16[64,512]{1,0:T(8,128)(2,1)S(1)}, bf16[64,512]{1,0:T(8,128)(2,1)S(1)}, u32[]{:S(2)}, u32[]{:S(2)}) collective-permute-start(bf16[64,512]{1,0:T(8,128)(2,1)S(1)} %line_sum.1.refs_0_), channel_id=1, source_target_pairs={{0,16},{8,24},{16,0},{24,8},{1,17},{9,25},{17,1},{25,9},{2,18},{10... | collective-permute-start | bytes 196616 | tf_op jit(solution)/shard_map/ppermute | solution.py:552
  44.8 1.9 %collective-permute-start.17 = (bf16[64,512]{1,0:T(8,128)(2,1)S(1)}, bf16[64,512]{1,0:T(8,128)(2,1)S(1)}, u32[]{:S(2)}, u32[]{:S(2)}) collective-permute-start(bf16[64,512]{1,0:T(8,128)(2,1)S(1)} %line_sum.1.refs_0_), channel_id=1, source_target_pairs={{0,8},{8,0},{16,24},{24,16},{1,9},{9,1},{17,25},{25,17},{2,10},{10... | collective-permute-start | bytes 196616 | tf_op jit(solution)/shard_map/ppermute | solution.py:552
  46.6 1.0 %place_rest.1 = (bf16[288,512]{1,0:T(8,128)(2,1)}, bf16[288,512]{1,0:T(8,128)(2,1)}, f32[8,128]{1,0:T(8,128)S(1)}) custom-call(f32[288,1024]{1,0:T(8,128)S(1)} %place.1.placed._, bf16[108,1024]{1,0:T(8,128)(2,1)S(1)} %collective-permute-done.13.lat_in), custom_call_target="tpu_custom_call" | custom-call | bytes 1994752 | tf_op jit(solution)/shard_map/place_rest/pallas_call | solution.py:403
  47.7 0.7 %collective-permute-done.19.refs_3_ = bf16[64,512]{1,0:T(8,128)(2,1)S(1)} collective-permute-done((bf16[64,512]{1,0:T(8,128)(2,1)S(1)}, bf16[64,512]{1,0:T(8,128)(2,1)S(1)}, u32[]{:S(2)}, u32[]{:S(2)}) %collective-permute-start.19) | collective-permute-done | bytes 65568 | tf_op jit(solution)/shard_map/ppermute | solution.py:552
  48.4 0.5 %collective-permute-done.18.refs_2_ = bf16[64,512]{1,0:T(8,128)(2,1)S(1)} collective-permute-done((bf16[64,512]{1,0:T(8,128)(2,1)S(1)}, bf16[64,512]{1,0:T(8,128)(2,1)S(1)}, u32[]{:S(2)}, u32[]{:S(2)}) %collective-permute-start.18) | collective-permute-done | bytes 65568 | tf_op jit(solution)/shard_map/ppermute | solution.py:552
  48.9 0.1 collective-permute-done.17.refs_1_
  49.0 0.9 %finish.1 = (f32[64,1536]{1,0:T(8,128)}, f32[64,512]{1,0:T(8,128)}) custom-call(f32[8,128]{1,0:T(8,128)S(1)} %get-tuple-element.92._, bf16[64,512]{1,0:T(8,128)(2,1)S(1)} %line_sum.1.refs_0_, bf16[64,512]{1,0:T(8,128)(2,1)S(1)} %collective-permute-done.17.refs_1_, bf16[64,512]{1,0:T(8,128)(2,1)S(1)} %collective-permute-done.18.refs_2_, ...), custom_call_target="tpu_custom_call" | custom-call | bytes 1000000 | tf_op jit(solution)/shard_map/finish/pallas_call | solution.py:561
  (22 shorter events, 0.2 us)
Async XLA Ops:
  0.6 1.0 %copy-start.3 = (bf16[2,6,24,512]{3,2,1,0:T(8,128)(2,1)S(1)}, bf16[2,6,24,512]{3,2,1,0:T(8,128)(2,1)}, u32[]{:S(2)}) copy-start(bf16[2,6,24,512]{3,2,1,0:T(8,128)(2,1)} %param.5) | copy-start | bytes 884740
  0.6 1.0 %copy-start.2 = (bf16[2,6,24,512]{3,2,1,0:T(8,128)(2,1)S(1)}, bf16[2,6,24,512]{3,2,1,0:T(8,128)(2,1)}, u32[]{:S(2)}) copy-start(bf16[2,6,24,512]{3,2,1,0:T(8,128)(2,1)} %param.4) | copy-start | bytes 884740
  1.7 9.8 %copy-start.1 = (bf16[512,512]{1,0:T(8,128)(2,1)S(1)}, bf16[512,512]{1,0:T(8,128)(2,1)}, u32[]{:S(2)}) copy-start(bf16[512,512]{1,0:T(8,128)(2,1)} %refs_7_.1) | copy-start | bytes 1572868
  2.0 9.5 %copy-start = (bf16[512,1536]{1,0:T(8,128)(2,1)S(1)}, bf16[512,1536]{1,0:T(8,128)(2,1)}, u32[]{:S(2)}) copy-start(bf16[512,1536]{1,0:T(8,128)(2,1)} %refs_6_.1) | copy-start | bytes 4718596
  2.1 10.2 %collective-permute-start = (bf16[72,1024]{1,0:T(8,128)(2,1)S(1)}, bf16[72,1024]{1,0:T(8,128)(2,1)S(1)}, u32[]{:S(2)}, u32[]{:S(2)}) collective-permute-start(bf16[72,1024]{1,0:T(8,128)(2,1)S(1)} %get-tuple-element.62), channel_id=1, source_target_pairs={{0,24},{1,9},{2,26},{3,11},{4,28},{5,13},{6,30},{7,15},{8,0},{9,17... | collective-permute-start | bytes 442376 | tf_op jit(solution)/shard_map/ppermute | solution.py:457
  6.0 8.4 %collective-permute-start.1 = (bf16[36,1024]{1,0:T(8,128)(2,1)S(1)}, bf16[36,1024]{1,0:T(8,128)(2,1)S(1)}, u32[]{:S(2)}, u32[]{:S(2)}) collective-permute-start(bf16[36,1024]{1,0:T(8,128)(2,1)S(1)} %get-tuple-element.53._), channel_id=1, source_target_pairs={{0,7},{1,0},{2,1},{3,2},{4,3},{5,4},{6,5},{7,6},{8,15},{9,8},{10,9... | collective-permute-start | bytes 221192 | tf_op jit(solution)/shard_map/ppermute | solution.py:458
  8.4 5.9 %collective-permute-start.2 = (bf16[36,1024]{1,0:T(8,128)(2,1)S(1)}, bf16[36,1024]{1,0:T(8,128)(2,1)S(1)}, u32[]{:S(2)}, u32[]{:S(2)}) collective-permute-start(bf16[36,1024]{1,0:T(8,128)(2,1)S(1)} %get-tuple-element.66), channel_id=1, source_target_pairs={{0,24},{1,9},{2,26},{3,11},{4,28},{5,13},{6,30},{7,15},{8,0},{9,17... | collective-permute-start | bytes 221192 | tf_op jit(solution)/shard_map/ppermute | solution.py:459
  9.9 4.5 %collective-permute-start.3 = (bf16[36,1024]{1,0:T(8,128)(2,1)S(1)}, bf16[36,1024]{1,0:T(8,128)(2,1)S(1)}, u32[]{:S(2)}, u32[]{:S(2)}) collective-permute-start(bf16[36,1024]{1,0:T(8,128)(2,1)S(1)} %get-tuple-element.67), channel_id=1, source_target_pairs={{0,15},{1,24},{2,9},{3,26},{4,11},{5,28},{6,13},{7,30},{8,23},{9,0... | collective-permute-start | bytes 221192 | tf_op jit(solution)/shard_map/ppermute | solution.py:460
  16.8 1.6 %collective-permute-start.4 = (bf16[2,256,256]{2,1,0:T(8,128)(2,1)S(1)}, bf16[2,256,256]{2,1,0:T(8,128)(2,1)S(1)}, u32[]{:S(2)}, u32[]{:S(2)}) collective-permute-start(bf16[2,256,256]{2,1,0:T(8,128)(2,1)S(1)} %get-tuple-element.72), channel_id=1, source_target_pairs={{0,1},{1,0},{2,3},{3,2},{4,5},{5,4},{6,7},{7,6},{8,9},{9,8},{10,11... | collective-permute-start | bytes 786440 | tf_op jit(solution)/shard_map/ppermute | solution.py:483
  16.9 3.7 %collective-permute-start.5 = (bf16[2,256,256]{2,1,0:T(8,128)(2,1)S(1)}, bf16[2,256,256]{2,1,0:T(8,128)(2,1)S(1)}, u32[]{:S(2)}, u32[]{:S(2)}) collective-permute-start(bf16[2,256,256]{2,1,0:T(8,128)(2,1)S(1)} %get-tuple-element.74), channel_id=1, source_target_pairs={{0,1},{1,0},{2,3},{3,2},{4,5},{5,4},{6,7},{7,6},{8,9},{9,8},{10,11... | collective-permute-start | bytes 786440 | tf_op jit(solution)/shard_map/ppermute | solution.py:483
  18.4 6.6 %collective-permute-start.8 = (bf16[2,256,256]{2,1,0:T(8,128)(2,1)S(1)}, bf16[2,256,256]{2,1,0:T(8,128)(2,1)S(1)}, u32[]{:S(2)}, u32[]{:S(2)}) collective-permute-start(bf16[2,256,256]{2,1,0:T(8,128)(2,1)S(1)} %chip_sum.2._), channel_id=1, source_target_pairs={{0,8},{1,17},{2,10},{3,19},{4,12},{5,21},{6,14},{7,23},{8,0},{9,25... | collective-permute-start | bytes 786440 | tf_op jit(solution)/shard_map/ppermute | solution.py:492
  20.7 7.5 %collective-permute-start.9 = (bf16[2,256,256]{2,1,0:T(8,128)(2,1)S(1)}, bf16[2,256,256]{2,1,0:T(8,128)(2,1)S(1)}, u32[]{:S(2)}, u32[]{:S(2)}) collective-permute-start(bf16[2,256,256]{2,1,0:T(8,128)(2,1)S(1)} %chip_sum.3.__), channel_id=1, source_target_pairs={{0,8},{1,17},{2,10},{3,19},{4,12},{5,21},{6,14},{7,23},{8,0},{9,25... | collective-permute-start | bytes 786440 | tf_op jit(solution)/shard_map/ppermute | solution.py:492
  21.7 3.3 %collective-permute-start.7 = (bf16[2,256,512]{2,1,0:T(8,128)(2,1)S(1)}, bf16[2,256,512]{2,1,0:T(8,128)(2,1)S(1)}, u32[]{:S(2)}, u32[]{:S(2)}) collective-permute-start(bf16[2,256,512]{2,1,0:T(8,128)(2,1)S(1)} %get-tuple-element.84), channel_id=1, source_target_pairs={{0,1},{1,0},{2,3},{3,2},{4,5},{5,4},{6,7},{7,6},{8,9},{9,8},{10,11... | collective-permute-start | bytes 1572872 | tf_op jit(solution)/shard_map/ppermute | solution.py:503
  25.1 7.3 %collective-permute-start.11 = (bf16[1,256,256]{2,1,0:T(8,128)(2,1)S(1)}, bf16[1,256,256]{2,1,0:T(8,128)(2,1)S(1)}, u32[]{:S(2)}, u32[]{:S(2)}) collective-permute-start(bf16[1,256,256]{2,1,0:T(8,128)(2,1)S(1)} %get-tuple-element.85._.refs_3_), channel_id=1, source_target_pairs={{0,16},{1,9},{2,18},{3,11},{4,20},{5,13},{6,22},{7,15},{8,24},{9,1... | collective-permute-start | bytes 393224 | tf_op jit(solution)/shard_map/ppermute | solution.py:492
  26.7 5.7 %collective-permute-start.6 = (bf16[36,1024]{1,0:T(8,128)(2,1)S(1)}, bf16[36,1024]{1,0:T(8,128)(2,1)S(1)}, u32[]{:S(2)}, u32[]{:S(2)}) collective-permute-start(bf16[36,1024]{1,0:T(8,128)(2,1)S(1)} %pack_lon.1), channel_id=1, source_target_pairs={{7,0},{0,1},{1,2},{2,3},{3,4},{4,5},{5,6},{6,7},{15,8},{8,9},{9,10... | collective-permute-start | bytes 221192 | tf_op jit(solution)/shard_map/ppermute | solution.py:510
  28.3 5.1 %collective-permute-start.12 = (bf16[1,256,256]{2,1,0:T(8,128)(2,1)S(1)}, bf16[1,256,256]{2,1,0:T(8,128)(2,1)S(1)}, u32[]{:S(2)}, u32[]{:S(2)}) collective-permute-start(bf16[1,256,256]{2,1,0:T(8,128)(2,1)S(1)} %get-tuple-element.86._), channel_id=1, source_target_pairs={{0,16},{1,9},{2,18},{3,11},{4,20},{5,13},{6,22},{7,15},{8,24},{9,1... | collective-permute-start | bytes 393224 | tf_op jit(solution)/shard_map/ppermute | solution.py:492
  30.2 10.1 %collective-permute-start.10 = (bf16[36,1024]{1,0:T(8,128)(2,1)S(1)}, bf16[36,1024]{1,0:T(8,128)(2,1)S(1)}, u32[]{:S(2)}, u32[]{:S(2)}) collective-permute-start(bf16[36,1024]{1,0:T(8,128)(2,1)S(1)} %pack_diag.1), channel_id=1, source_target_pairs={{15,0},{24,1},{9,2},{26,3},{11,4},{28,5},{13,6},{30,7},{23,8},{0,9... | collective-permute-start | bytes 221192 | tf_op jit(solution)/shard_map/ppermute | solution.py:526
  33.5 7.6 %collective-permute-start.14 = (bf16[64,512]{1,0:T(8,128)(2,1)S(1)}, bf16[64,512]{1,0:T(8,128)(2,1)S(1)}, u32[]{:S(2)}, u32[]{:S(2)}) collective-permute-start(bf16[64,512]{1,0:T(8,128)(2,1)S(1)} %get-tuple-element.94), channel_id=1, source_target_pairs={{0,6},{1,7},{2,4},{3,5},{4,2},{5,3},{6,0},{7,1},{8,14},{9,15},{10,... | collective-permute-start | bytes 196616 | tf_op jit(solution)/shard_map/ppermute | solution.py:538
  37.8 5.2 %collective-permute-start.15 = (bf16[64,512]{1,0:T(8,128)(2,1)S(1)}, bf16[64,512]{1,0:T(8,128)(2,1)S(1)}, u32[]{:S(2)}, u32[]{:S(2)}) collective-permute-start(bf16[64,512]{1,0:T(8,128)(2,1)S(1)} %get-tuple-element.95), channel_id=1, source_target_pairs={{0,4},{1,5},{2,6},{3,7},{4,0},{5,1},{6,2},{7,3},{8,12},{9,13},{10,... | collective-permute-start | bytes 196616 | tf_op jit(solution)/shard_map/ppermute | solution.py:538
  37.8 5.2 %collective-permute-start.16 = (bf16[64,512]{1,0:T(8,128)(2,1)S(1)}, bf16[64,512]{1,0:T(8,128)(2,1)S(1)}, u32[]{:S(2)}, u32[]{:S(2)}) collective-permute-start(bf16[64,512]{1,0:T(8,128)(2,1)S(1)} %get-tuple-element.89._), channel_id=1, source_target_pairs={{0,2},{1,3},{2,0},{3,1},{4,6},{5,7},{6,4},{7,5},{8,10},{9,11},{10,... | collective-permute-start | bytes 196616 | tf_op jit(solution)/shard_map/ppermute | solution.py:538
  38.6 8.0 %collective-permute-start.13 = (bf16[108,1024]{1,0:T(8,128)(2,1)S(1)}, bf16[108,1024]{1,0:T(8,128)(2,1)S(1)}, u32[]{:S(2)}, u32[]{:S(2)}) collective-permute-start(bf16[108,1024]{1,0:T(8,128)(2,1)S(1)} %pack_lat.1), channel_id=1, source_target_pairs={{24,0},{9,1},{26,2},{11,3},{28,4},{13,5},{30,6},{15,7},{0,8},{17,9... | collective-permute-start | bytes 663560 | tf_op jit(solution)/shard_map/ppermute | solution.py:544
  43.1 5.3 %collective-permute-start.19 = (bf16[64,512]{1,0:T(8,128)(2,1)S(1)}, bf16[64,512]{1,0:T(8,128)(2,1)S(1)}, u32[]{:S(2)}, u32[]{:S(2)}) collective-permute-start(bf16[64,512]{1,0:T(8,128)(2,1)S(1)} %line_sum.1.refs_0_), channel_id=1, source_target_pairs={{0,24},{8,16},{16,8},{24,0},{1,25},{9,17},{17,9},{25,1},{2,26},{10... | collective-permute-start | bytes 196616 | tf_op jit(solution)/shard_map/ppermute | solution.py:552
  44.0 5.0 %collective-permute-start.18 = (bf16[64,512]{1,0:T(8,128)(2,1)S(1)}, bf16[64,512]{1,0:T(8,128)(2,1)S(1)}, u32[]{:S(2)}, u32[]{:S(2)}) collective-permute-start(bf16[64,512]{1,0:T(8,128)(2,1)S(1)} %line_sum.1.refs_0_), channel_id=1, source_target_pairs={{0,16},{8,24},{16,0},{24,8},{1,17},{9,25},{17,1},{25,9},{2,18},{10... | collective-permute-start | bytes 196616 | tf_op jit(solution)/shard_map/ppermute | solution.py:552
  44.8 4.3 %collective-permute-start.17 = (bf16[64,512]{1,0:T(8,128)(2,1)S(1)}, bf16[64,512]{1,0:T(8,128)(2,1)S(1)}, u32[]{:S(2)}, u32[]{:S(2)}) collective-permute-start(bf16[64,512]{1,0:T(8,128)(2,1)S(1)} %line_sum.1.refs_0_), channel_id=1, source_target_pairs={{0,8},{8,0},{16,24},{24,16},{1,9},{9,1},{17,25},{25,17},{2,10},{10... | collective-permute-start | bytes 196616 | tf_op jit(solution)/shard_map/ppermute | solution.py:552

commit v23 on v18

--- a/solution.py
+++ b/solution.py
@@ -124,13 +124,15 @@
     return jnp.transpose(block.astype(F32)).astype(BF)
 
 
-def slot_product(slot, size, lat, core, windows):
+def slot_product(slot, size, lat, core, windows, chunk=None):
     share = lat ^ swap_bits(slot, size, core)
     total = None
     for left, right in windows:
         lanes = right.shape[1] // size
         of_proj = (share >= 3 * size // 4).astype(jnp.int32)
-        part = dot(left[of_proj], right[:, pl.ds(pl.multiple_of(share * lanes, lanes), lanes)], NN)
+        half = lanes // 2
+        start, width = (share * lanes, lanes) if chunk is None else (share * lanes + chunk * half, half)
+        part = dot(left[of_proj], right[:, pl.ds(pl.multiple_of(start, half), width)], NN)
         total = part if total is None else total + part
     return total
 
@@ -168,10 +170,10 @@
     *_, right, left, _, _ = refs
     lat, core, size = place()
     for slot in range(1, size, 2):
-        send_grad[slot // 2] = slot_product(slot, size, lat, 1 - core, [(left, right)])
-
-
-def outer_kernel(own, lon_in, lat_in, diag_in, qkv_weight, proj_weight, grad_so_far, send_a, send_b, *refs):
+        send_grad[slot // 2] = slot_product(slot, size, lat, 1 - core, [(left, right)], 0)
+
+
+def outer_kernel(own, lon_in, lat_in, diag_in, qkv_weight, proj_weight, grad_so_far, send_a, *refs):
     last = picks(last_rows, HALF, QUARTER)
     both = jnp.concatenate(
         [
@@ -184,8 +186,8 @@
     *_, right, left, _, _ = refs
     lat, core, size = place()
     for slot in range(1, size, 2):
-        total = grad_so_far[slot // 2] + slot_product(slot, size, lat, 1 - core, [(left, right)])
-        put_chunks((send_a, send_b), slot // 2, total)
+        total = grad_so_far[slot // 2] + slot_product(slot, size, lat, 1 - core, [(left, right)], 0)
+        send_a[slot // 2] = total.astype(BF)
 
 
 def put_chunks(outs, slot, total):
@@ -264,11 +266,14 @@
 
 
 def keep_kernel(*refs):
-    *windows, keep_a, keep_b = refs
-    windows = [windows[:2], windows[2:]]
+    *windows, send_b, keep_a, keep_b = refs
+    windows = windows[:3], windows[3:]
     lat, core, size = place()
     for slot in range(1, size, 2):
-        put_chunks((keep_a, keep_b), slot // 2, slot_product(slot, size, lat, core, windows))
+        total = slot_product(slot, size, lat, 1 - core, [(w[2], w[1]) for w in windows], 1)
+        send_b[slot // 2] = total.astype(BF)
+    for slot in range(1, size, 2):
+        put_chunks((keep_a, keep_b), slot // 2, slot_product(slot, size, lat, core, [w[:2] for w in windows]))
 
 
 def rest_kernel(_, __, *refs):
@@ -472,17 +477,17 @@
     ]
     scratch = [pltpu.VMEM((width, WIN), BF)] * 2
     grad_so_far, *inner = call(
-        inner_kernel, [(halves[0], F32), *per_window], inner_own, *own_parts, inner_in, qkv_weight, proj_weight,
+        inner_kernel, [(chunk[0], F32), *per_window], inner_own, *own_parts, inner_in, qkv_weight, proj_weight,
         name="inner", flops=10**9, scratch=scratch,
     )
-    send_a, send_b, *outer = call(
-        outer_kernel, [chunk, chunk, *per_window],
+    send_a, *outer = call(
+        outer_kernel, [chunk, *per_window],
         outer_own, lon_in, outer_in, diag_in, qkv_weight, proj_weight, grad_so_far,
         name="outer", flops=10**9, scratch=scratch,
     )
     sibling = [(j, j ^ 1) for j in range(lon_size)]
+    send_b, *keep = call(keep_kernel, [chunk] * 3, *inner[2:], *outer[2:], name="keep", flops=10**9)
     arrived = [lax.ppermute(send, "lon", sibling) for send in (send_a, send_b)]
-    keep = call(keep_kernel, [chunk, chunk], *inner[2:4], *outer[2:4], name="keep", flops=10**9)
 
     def halving(phase, send):
         route = [

time: 50 us -> 50.6 us (1.012)
  no operation moved by 1% of the time
where the time goes in v23:
time: 50.6 us; the launch traced here: 50.5 us
  starting transfers between devices  25.8 us (51%)
  Pallas kernels  11.8 us (23%)
  waiting for transfers between devices  11.2 us (22%)
  local copies, waits for them, and re-layouts  0.94 us (2%)
  between operations  0.82 us (2%)
    pallas_call x22, Pallas kernels, call(): pl.pallas_call(kernel, out_shape=shapes, in_specs=[anywhere if i in unrea...  11.8 us
    ppermute x4, starting transfers between devices, halving(): return lax.ppermute(send, both, route)  5.92 us
    ppermute x3, starting transfers between devices, per_device(): lax.ppermute(parts[step], 'lon', [(j, j ^ 2 * step) for j in range(lon_si...  4.93 us
    ppermute x4, waiting for transfers between devices, halving(): return lax.ppermute(send, both, route)  4.65 us
    ppermute x1, starting transfers between devices, per_device(): inner_in = lax.ppermute(inner_lat, both, lat_route)  3.94 us
    ppermute x3, starting transfers between devices, per_device(): lax.ppermute(line_sum, 'lat', [(i, i ^ step) for i in range(lat_size)])  3.55 us
    ppermute x1, waiting for transfers between devices, per_device(): lon_home = lax.ppermute(lon_back, both, back(lon_route))  2.15 us
    ppermute x3, waiting for transfers between devices, per_device(): lax.ppermute(parts[step], 'lon', [(j, j ^ 2 * step) for j in range(lon_si...  1.93 us
  transfers between devices with their start and end apart: 20, of which 9 were waited for; matrix products, arithmetic and copies ran while one was open for 0% of the time, Pallas kernels for 16%

profile of v23, /device:TPU:0, one launch (start us, length us, event | category | flops | bytes accessed | tf_op | source)
XLA Modules:
  0.0 50.5 jit_solution(15813039672554908316)
XLA Ops:
  0.7 0.1 order.1
  0.8 0.8 %copy-done.2 = bf16[2,6,24,512]{3,2,1,0:T(8,128)(2,1)S(1)} copy-done((bf16[2,6,24,512]{3,2,1,0:T(8,128)(2,1)S(1)}, bf16[2,6,24,512]{3,2,1,0:T(8,128)(2,1)}, u32[]{:S(2)}) %copy-start.2) | copy-done | bytes 294936
  1.6 0.1 copy-done.3
  1.7 0.4 pack.1
  2.1 3.9 %collective-permute-start = (bf16[72,1024]{1,0:T(8,128)(2,1)S(1)}, bf16[72,1024]{1,0:T(8,128)(2,1)S(1)}, u32[]{:S(2)}, u32[]{:S(2)}) collective-permute-start(bf16[72,1024]{1,0:T(8,128)(2,1)S(1)} %get-tuple-element.62), channel_id=1, source_target_pairs={{0,24},{1,9},{2,26},{3,11},{4,28},{5,13},{6,30},{7,15},{8,0},{9,17... | collective-permute-start | bytes 442376 | tf_op jit(solution)/shard_map/ppermute | solution.py:463
  6.0 1.8 %collective-permute-start.1 = (bf16[36,1024]{1,0:T(8,128)(2,1)S(1)}, bf16[36,1024]{1,0:T(8,128)(2,1)S(1)}, u32[]{:S(2)}, u32[]{:S(2)}) collective-permute-start(bf16[36,1024]{1,0:T(8,128)(2,1)S(1)} %get-tuple-element.53._), channel_id=1, source_target_pairs={{0,7},{1,0},{2,1},{3,2},{4,3},{5,4},{6,5},{7,6},{8,15},{9,8},{10,9... | collective-permute-start | bytes 221192 | tf_op jit(solution)/shard_map/ppermute | solution.py:464
  7.8 0.6 %pack_rest.1 = (bf16[36,1024]{1,0:T(8,128)(2,1)S(1)}, bf16[36,1024]{1,0:T(8,128)(2,1)S(1)}, f32[72,1024]{1,0:T(8,128)S(1)}, f32[72,1024]{1,0:T(8,128)S(1)}) custom-call(bf16[36,1024]{1,0:T(8,128)(2,1)S(1)} %get-tuple-element.53._, bf16[288,512]{1,0:T(8,128)(2,1)S(1)} %bitcast.6, bf16[288,512]{1,0:T(8,128)(2,1)S(1)} %bitcast.8, ...), custom_call_target="tpu_custom_call" | custom-call | flops 500000000 | bytes 1525248 | tf_op jit(solution)/shard_map/pack_rest/pallas_call | solution.py:409
  8.4 1.5 %collective-permute-start.2 = (bf16[36,1024]{1,0:T(8,128)(2,1)S(1)}, bf16[36,1024]{1,0:T(8,128)(2,1)S(1)}, u32[]{:S(2)}, u32[]{:S(2)}) collective-permute-start(bf16[36,1024]{1,0:T(8,128)(2,1)S(1)} %get-tuple-element.67), channel_id=1, source_target_pairs={{0,24},{1,9},{2,26},{3,11},{4,28},{5,13},{6,30},{7,15},{8,0},{9,17... | collective-permute-start | bytes 221192 | tf_op jit(solution)/shard_map/ppermute | solution.py:465
  9.9 1.6 %collective-permute-start.3 = (bf16[36,1024]{1,0:T(8,128)(2,1)S(1)}, bf16[36,1024]{1,0:T(8,128)(2,1)S(1)}, u32[]{:S(2)}, u32[]{:S(2)}) collective-permute-start(bf16[36,1024]{1,0:T(8,128)(2,1)S(1)} %get-tuple-element.68), channel_id=1, source_target_pairs={{0,15},{1,24},{2,9},{3,26},{4,11},{5,28},{6,13},{7,30},{8,23},{9,0... | collective-permute-start | bytes 221192 | tf_op jit(solution)/shard_map/ppermute | solution.py:466
  11.5 0.7 %own.1 = (f32[72,512]{1,0:T(8,128)S(1)}, f32[72,1536]{1,0:T(8,128)S(1)}, f32[72,512]{1,0:T(8,128)S(1)}) custom-call(f32[72,1024]{1,0:T(8,128)S(1)} %get-tuple-element.58.inner_own.own, bf16[512,1536]{1,0:T(8,128)(2,1)S(1)} %copy-done, bf16[512,512]{1,0:T(8,128)(2,1)S(1)} %copy-done.1), custom_call_target="tpu_custom_call" | custom-call | flops 500000000 | bytes 3129344 | tf_op jit(solution)/shard_map/own/pallas_call | solution.py:409
  12.2 2.1 %inner.1 = (f32[2,256,256]{2,1,0:T(8,128)S(1)}, bf16[144,512]{1,0:T(8,128)(2,1)S(1)}, bf16[144,512]{1,0:T(8,128)(2,1)S(1)}, bf16[2,256,144]{2,1,0:T(8,128)(2,1)S...) custom-call(f32[72,1024]{1,0:T(8,128)S(1)} %get-tuple-element.58.inner_own.own, ...), custom_call_target="tpu_custom_call" | custom-call | flops 1000000000 | bytes 4980736 | tf_op jit(solution)/shard_map/inner/pallas_call | solution.py:409
  14.3 2.3 %outer.1 = (bf16[2,256,256]{2,1,0:T(8,128)(2,1)S(1)}, bf16[144,512]{1,0:T(8,128)(2,1)S(1)}, bf16[144,512]{1,0:T(8,128)(2,1)S(1)}, bf16[2,256,144]{2,1,0:T(8,128)...) custom-call(f32[72,1024]{1,0:T(8,128)S(1)} %get-tuple-element.66.own, ...), custom_call_target="tpu_custom_call" | custom-call | flops 1000000000 | bytes 4579328 | tf_op jit(solution)/shard_map/outer/pallas_call | solution.py:409
  16.6 0.1 collective-permute-start.4
  16.8 0.6 %keep.1 = (bf16[2,256,256]{2,1,0:T(8,128)(2,1)S(1)}, bf16[2,256,256]{2,1,0:T(8,128)(2,1)S(1)}, bf16[2,256,256]{2,1,0:T(8,128)(2,1)S(1)}) custom-call(bf16[2,256,144]{2,1,0:T(8,128)(2,1)S(1)} %get-tuple-element.63.refs_0_, bf16[144,2048]{1,0:T(8,128)(2,1)S(1)} %get-tuple-element.64.refs_1_.refs_2_, bf16[2,256,144]{2,1,0:T(8,128)(2,1)S(1)} %get-tuple-element.65.refs_2_, ...), custom_call_target="tpu_custom_call" | custom-call | flops 1000000000 | bytes 2555904 | tf_op jit(solution)/shard_map/keep/pallas_call | solution.py:409
  17.3 0.5 collective-permute-start.5
  17.8 0.4 collective-permute-done.4.refs_1_
  18.2 0.1 chip_sum.2._
  18.3 2.3 %collective-permute-start.8 = (bf16[2,256,256]{2,1,0:T(8,128)(2,1)S(1)}, bf16[2,256,256]{2,1,0:T(8,128)(2,1)S(1)}, u32[]{:S(2)}, u32[]{:S(2)}) collective-permute-start(bf16[2,256,256]{2,1,0:T(8,128)(2,1)S(1)} %chip_sum.2._), channel_id=1, source_target_pairs={{0,8},{1,17},{2,10},{3,19},{4,12},{5,21},{6,14},{7,23},{8,0},{9,25... | collective-permute-start | bytes 786440 | tf_op jit(solution)/shard_map/ppermute | solution.py:498
  20.6 0.1 chip_sum.3.__
  20.6 0.7 %rest.1 = (bf16[2,256,512]{2,1,0:T(8,128)(2,1)S(1)}, bf16[2,256,512]{2,1,0:T(8,128)(2,1)S(1)}) custom-call(bf16[2,256,256]{2,1,0:T(8,128)(2,1)S(1)} %chip_sum.2._, bf16[2,256,256]{2,1,0:T(8,128)(2,1)S(1)} %chip_sum.3.__, bf16[2,256,144]{2,1,0:T(8,128)(2,1)S(1)} %get-tuple-element.63.refs_0_, bf16[144,2048]{1,0:T(8,128)(2,1)S(1)} %get-tuple-element.64.refs_1_.refs_2_, ...), custom_call_target="tpu_custom_call" | custom-call | tf_op jit(solution)/shard_map/rest/pallas_call | solution.py:409
  21.4 0.7 %collective-permute-start.9 = (bf16[2,256,256]{2,1,0:T(8,128)(2,1)S(1)}, bf16[2,256,256]{2,1,0:T(8,128)(2,1)S(1)}, u32[]{:S(2)}, u32[]{:S(2)}) collective-permute-start(bf16[2,256,256]{2,1,0:T(8,128)(2,1)S(1)} %chip_sum.3.__), channel_id=1, source_target_pairs={{0,8},{1,17},{2,10},{3,19},{4,12},{5,21},{6,14},{7,23},{8,0},{9,25... | collective-permute-start | bytes 786440 | tf_op jit(solution)/shard_map/ppermute | solution.py:498
  22.1 0.9 %outputs.1 = (bf16[144,1024]{1,0:T(8,128)(2,1)S(1)}, bf16[144,1024]{1,0:T(8,128)(2,1)S(1)}) custom-call(bf16[2,256,512]{2,1,0:T(8,128)(2,1)S(1)} %get-tuple-element.77._.refs_0_, bf16[144,512]{1,0:T(8,128)(2,1)S(1)} %get-tuple-element.78.refs_0_, bf16[144,512]{1,0:T(8,128)(2,1)S(1)} %get-tuple-element.79.refs_1_, ...), custom_call_target="tpu_custom_call" | custom-call | flops 10000000000 | bytes 4980736 | tf_op jit(solution)/shard_map/outputs/pallas_call | solution.py:409
  23.0 1.9 %collective-permute-done.8.refs_2_ = bf16[2,256,256]{2,1,0:T(8,128)(2,1)S(1)} collective-permute-done((bf16[2,256,256]{2,1,0:T(8,128)(2,1)S(1)}, bf16[2,256,256]{2,1,0:T(8,128)(2,1)S(1)}, u32[]{:S(2)}, u32[]{:S(2)}) %collective-permute-start.8) | collective-permute-done | bytes 262176 | tf_op jit(solution)/shard_map/ppermute | solution.py:498
  24.9 0.1 halve1.2
  25.0 1.4 %collective-permute-start.11 = (bf16[1,256,256]{2,1,0:T(8,128)(2,1)S(1)}, bf16[1,256,256]{2,1,0:T(8,128)(2,1)S(1)}, u32[]{:S(2)}, u32[]{:S(2)}) collective-permute-start(bf16[1,256,256]{2,1,0:T(8,128)(2,1)S(1)} %get-tuple-element.85._.refs_3_), channel_id=1, source_target_pairs={{0,16},{1,9},{2,18},{3,11},{4,20},{5,13},{6,22},{7,15},{8,24},{9,1... | collective-permute-start | bytes 393224 | tf_op jit(solution)/shard_map/ppermute | solution.py:498
  26.4 0.1 pack_lon.1
  26.6 0.1 collective-permute-start.6
  26.6 1.6 %collective-permute-done.9.refs_2_ = bf16[2,256,256]{2,1,0:T(8,128)(2,1)S(1)} collective-permute-done((bf16[2,256,256]{2,1,0:T(8,128)(2,1)S(1)}, bf16[2,256,256]{2,1,0:T(8,128)(2,1)S(1)}, u32[]{:S(2)}, u32[]{:S(2)}) %collective-permute-start.9) | collective-permute-done | bytes 262176 | tf_op jit(solution)/shard_map/ppermute | solution.py:498
  28.3 0.1 halve1.3
  28.4 1.5 %collective-permute-start.12 = (bf16[1,256,256]{2,1,0:T(8,128)(2,1)S(1)}, bf16[1,256,256]{2,1,0:T(8,128)(2,1)S(1)}, u32[]{:S(2)}, u32[]{:S(2)}) collective-permute-start(bf16[1,256,256]{2,1,0:T(8,128)(2,1)S(1)} %get-tuple-element.86._), channel_id=1, source_target_pairs={{0,16},{1,9},{2,18},{3,11},{4,20},{5,13},{6,22},{7,15},{8,24},{9,1... | collective-permute-start | bytes 393224 | tf_op jit(solution)/shard_map/ppermute | solution.py:498
  29.9 0.1 pack_diag.1
  30.1 0.1 collective-permute-start.10
  30.1 2.1 %collective-permute-done.6.lon_in._ = bf16[36,1024]{1,0:T(8,128)(2,1)S(1)} collective-permute-done((bf16[36,1024]{1,0:T(8,128)(2,1)S(1)}, bf16[36,1024]{1,0:T(8,128)(2,1)S(1)}, u32[]{:S(2)}, u32[]{:S(2)}) %collective-permute-start.6) | collective-permute-done | bytes 73760 | tf_op jit(solution)/shard_map/ppermute | solution.py:516
  32.3 1.1 %collective-permute-done.12.refs_2_ = bf16[1,256,256]{2,1,0:T(8,128)(2,1)S(1)} collective-permute-done((bf16[1,256,256]{2,1,0:T(8,128)(2,1)S(1)}, bf16[1,256,256]{2,1,0:T(8,128)(2,1)S(1)}, u32[]{:S(2)}, u32[]{:S(2)}) %collective-permute-start.12) | collective-permute-done | bytes 131104 | tf_op jit(solution)/shard_map/ppermute | solution.py:498
  33.4 4.3 %collective-permute-start.14 = (bf16[64,512]{1,0:T(8,128)(2,1)S(1)}, bf16[64,512]{1,0:T(8,128)(2,1)S(1)}, u32[]{:S(2)}, u32[]{:S(2)}) collective-permute-start(bf16[64,512]{1,0:T(8,128)(2,1)S(1)} %get-tuple-element.94), channel_id=1, source_target_pairs={{0,6},{1,7},{2,4},{3,5},{4,2},{5,3},{6,0},{7,1},{8,14},{9,15},{10,... | collective-permute-start | bytes 196616 | tf_op jit(solution)/shard_map/ppermute | solution.py:544
  37.7 0.6 %collective-permute-start.16 = (bf16[64,512]{1,0:T(8,128)(2,1)S(1)}, bf16[64,512]{1,0:T(8,128)(2,1)S(1)}, u32[]{:S(2)}, u32[]{:S(2)}) collective-permute-start(bf16[64,512]{1,0:T(8,128)(2,1)S(1)} %get-tuple-element.89._), channel_id=1, source_target_pairs={{0,2},{1,3},{2,0},{3,1},{4,6},{5,7},{6,4},{7,5},{8,10},{9,11},{10,... | collective-permute-start | bytes 196616 | tf_op jit(solution)/shard_map/ppermute | solution.py:544
  38.4 0.1 pack_lat.1
  38.5 1.8 %collective-permute-start.13 = (bf16[108,1024]{1,0:T(8,128)(2,1)S(1)}, bf16[108,1024]{1,0:T(8,128)(2,1)S(1)}, u32[]{:S(2)}, u32[]{:S(2)}) collective-permute-start(bf16[108,1024]{1,0:T(8,128)(2,1)S(1)} %pack_lat.1), channel_id=1, source_target_pairs={{24,0},{9,1},{26,2},{11,3},{28,4},{13,5},{30,6},{15,7},{0,8},{17,9... | collective-permute-start | bytes 663560 | tf_op jit(solution)/shard_map/ppermute | solution.py:550
  40.3 0.8 %place.1.placed._ = f32[288,1024]{1,0:T(8,128)S(1)} custom-call(bf16[144,1024]{1,0:T(8,128)(2,1)S(1)} %get-tuple-element.82._.refs_3_.inner_results, bf16[144,1024]{1,0:T(8,128)(2,1)S(1)} %get-tuple-element.83.outer_results, bf16[36,1024]{1,0:T(8,128)(2,1)S(1)} %collective-permute-done.6.lon_in._, bf16[36,1024]{1,0:T(8,128)(2,1)S(1)} %collective-permute-done.10.diag_in), custom_call_target="tpu_custom_call" | custom-call | bytes 1916928 | tf_op jit(solution)/shard_map/place/pallas_call | solution.py:409
  41.1 1.9 %collective-permute-done.15.refs_2_ = bf16[64,512]{1,0:T(8,128)(2,1)S(1)} collective-permute-done((bf16[64,512]{1,0:T(8,128)(2,1)S(1)}, bf16[64,512]{1,0:T(8,128)(2,1)S(1)}, u32[]{:S(2)}, u32[]{:S(2)}) %collective-permute-start.15) | collective-permute-done | bytes 65568 | tf_op jit(solution)/shard_map/ppermute | solution.py:544
  43.0 0.2 collective-permute-start.17
  43.3 1.2 %collective-permute-start.18 = (bf16[64,512]{1,0:T(8,128)(2,1)S(1)}, bf16[64,512]{1,0:T(8,128)(2,1)S(1)}, u32[]{:S(2)}, u32[]{:S(2)}) collective-permute-start(bf16[64,512]{1,0:T(8,128)(2,1)S(1)} %line_sum.1.refs_0_), channel_id=1, source_target_pairs={{0,16},{8,24},{16,0},{24,8},{1,17},{9,25},{17,1},{25,9},{2,18},{10... | collective-permute-start | bytes 196616 | tf_op jit(solution)/shard_map/ppermute | solution.py:558
  44.5 2.1 %collective-permute-start.19 = (bf16[64,512]{1,0:T(8,128)(2,1)S(1)}, bf16[64,512]{1,0:T(8,128)(2,1)S(1)}, u32[]{:S(2)}, u32[]{:S(2)}) collective-permute-start(bf16[64,512]{1,0:T(8,128)(2,1)S(1)} %line_sum.1.refs_0_), channel_id=1, source_target_pairs={{0,24},{8,16},{16,8},{24,0},{1,25},{9,17},{17,9},{25,1},{2,26},{10... | collective-permute-start | bytes 196616 | tf_op jit(solution)/shard_map/ppermute | solution.py:558
  46.6 0.4 collective-permute-done.13.lat_in
  47.0 1.0 %place_rest.1 = (bf16[288,512]{1,0:T(8,128)(2,1)}, bf16[288,512]{1,0:T(8,128)(2,1)}, f32[8,128]{1,0:T(8,128)S(1)}) custom-call(f32[288,1024]{1,0:T(8,128)S(1)} %place.1.placed._, bf16[108,1024]{1,0:T(8,128)(2,1)S(1)} %collective-permute-done.13.lat_in), custom_call_target="tpu_custom_call" | custom-call | bytes 1994752 | tf_op jit(solution)/shard_map/place_rest/pallas_call | solution.py:409
  48.0 0.1 collective-permute-done.18.refs_2_
  48.2 1.5 %collective-permute-done.19.refs_3_ = bf16[64,512]{1,0:T(8,128)(2,1)S(1)} collective-permute-done((bf16[64,512]{1,0:T(8,128)(2,1)S(1)}, bf16[64,512]{1,0:T(8,128)(2,1)S(1)}, u32[]{:S(2)}, u32[]{:S(2)}) %collective-permute-start.19) | collective-permute-done | bytes 65568 | tf_op jit(solution)/shard_map/ppermute | solution.py:558
  49.6 0.9 %finish.1 = (f32[64,1536]{1,0:T(8,128)}, f32[64,512]{1,0:T(8,128)}) custom-call(f32[8,128]{1,0:T(8,128)S(1)} %get-tuple-element.92._, bf16[64,512]{1,0:T(8,128)(2,1)S(1)} %line_sum.1.refs_0_, bf16[64,512]{1,0:T(8,128)(2,1)S(1)} %collective-permute-done.17.refs_1_, bf16[64,512]{1,0:T(8,128)(2,1)S(1)} %collective-permute-done.18.refs_2_, ...), custom_call_target="tpu_custom_call" | custom-call | bytes 790528 | tf_op jit(solution)/shard_map/finish/pallas_call | solution.py:409
  (22 shorter events, 0.1 us)
Async XLA Ops:
  0.6 1.0 %copy-start.2 = (bf16[2,6,24,512]{3,2,1,0:T(8,128)(2,1)S(1)}, bf16[2,6,24,512]{3,2,1,0:T(8,128)(2,1)}, u32[]{:S(2)}) copy-start(bf16[2,6,24,512]{3,2,1,0:T(8,128)(2,1)} %param.4) | copy-start | bytes 884740
  0.6 1.0 %copy-start.3 = (bf16[2,6,24,512]{3,2,1,0:T(8,128)(2,1)S(1)}, bf16[2,6,24,512]{3,2,1,0:T(8,128)(2,1)}, u32[]{:S(2)}) copy-start(bf16[2,6,24,512]{3,2,1,0:T(8,128)(2,1)} %param.5) | copy-start | bytes 884740
  1.7 9.8 %copy-start.1 = (bf16[512,512]{1,0:T(8,128)(2,1)S(1)}, bf16[512,512]{1,0:T(8,128)(2,1)}, u32[]{:S(2)}) copy-start(bf16[512,512]{1,0:T(8,128)(2,1)} %refs_7_.1) | copy-start | bytes 1572868
  2.0 9.5 %copy-start = (bf16[512,1536]{1,0:T(8,128)(2,1)S(1)}, bf16[512,1536]{1,0:T(8,128)(2,1)}, u32[]{:S(2)}) copy-start(bf16[512,1536]{1,0:T(8,128)(2,1)} %refs_6_.1) | copy-start | bytes 4718596
  2.1 10.2 %collective-permute-start = (bf16[72,1024]{1,0:T(8,128)(2,1)S(1)}, bf16[72,1024]{1,0:T(8,128)(2,1)S(1)}, u32[]{:S(2)}, u32[]{:S(2)}) collective-permute-start(bf16[72,1024]{1,0:T(8,128)(2,1)S(1)} %get-tuple-element.62), channel_id=1, source_target_pairs={{0,24},{1,9},{2,26},{3,11},{4,28},{5,13},{6,30},{7,15},{8,0},{9,17... | collective-permute-start | bytes 442376 | tf_op jit(solution)/shard_map/ppermute | solution.py:463
  6.0 8.3 %collective-permute-start.1 = (bf16[36,1024]{1,0:T(8,128)(2,1)S(1)}, bf16[36,1024]{1,0:T(8,128)(2,1)S(1)}, u32[]{:S(2)}, u32[]{:S(2)}) collective-permute-start(bf16[36,1024]{1,0:T(8,128)(2,1)S(1)} %get-tuple-element.53._), channel_id=1, source_target_pairs={{0,7},{1,0},{2,1},{3,2},{4,3},{5,4},{6,5},{7,6},{8,15},{9,8},{10,9... | collective-permute-start | bytes 221192 | tf_op jit(solution)/shard_map/ppermute | solution.py:464
  8.4 5.9 %collective-permute-start.2 = (bf16[36,1024]{1,0:T(8,128)(2,1)S(1)}, bf16[36,1024]{1,0:T(8,128)(2,1)S(1)}, u32[]{:S(2)}, u32[]{:S(2)}) collective-permute-start(bf16[36,1024]{1,0:T(8,128)(2,1)S(1)} %get-tuple-element.67), channel_id=1, source_target_pairs={{0,24},{1,9},{2,26},{3,11},{4,28},{5,13},{6,30},{7,15},{8,0},{9,17... | collective-permute-start | bytes 221192 | tf_op jit(solution)/shard_map/ppermute | solution.py:465
  9.9 4.4 %collective-permute-start.3 = (bf16[36,1024]{1,0:T(8,128)(2,1)S(1)}, bf16[36,1024]{1,0:T(8,128)(2,1)S(1)}, u32[]{:S(2)}, u32[]{:S(2)}) collective-permute-start(bf16[36,1024]{1,0:T(8,128)(2,1)S(1)} %get-tuple-element.68), channel_id=1, source_target_pairs={{0,15},{1,24},{2,9},{3,26},{4,11},{5,28},{6,13},{7,30},{8,23},{9,0... | collective-permute-start | bytes 221192 | tf_op jit(solution)/shard_map/ppermute | solution.py:466
  16.6 1.6 %collective-permute-start.4 = (bf16[2,256,256]{2,1,0:T(8,128)(2,1)S(1)}, bf16[2,256,256]{2,1,0:T(8,128)(2,1)S(1)}, u32[]{:S(2)}, u32[]{:S(2)}) collective-permute-start(bf16[2,256,256]{2,1,0:T(8,128)(2,1)S(1)} %get-tuple-element.74), channel_id=1, source_target_pairs={{0,1},{1,0},{2,3},{3,2},{4,5},{5,4},{6,7},{7,6},{8,9},{9,8},{10,11... | collective-permute-start | bytes 786440 | tf_op jit(solution)/shard_map/ppermute | solution.py:490
  17.3 3.2 %collective-permute-start.5 = (bf16[2,256,256]{2,1,0:T(8,128)(2,1)S(1)}, bf16[2,256,256]{2,1,0:T(8,128)(2,1)S(1)}, u32[]{:S(2)}, u32[]{:S(2)}) collective-permute-start(bf16[2,256,256]{2,1,0:T(8,128)(2,1)S(1)} %get-tuple-element.76), channel_id=1, source_target_pairs={{0,1},{1,0},{2,3},{3,2},{4,5},{5,4},{6,7},{7,6},{8,9},{9,8},{10,11... | collective-permute-start | bytes 786440 | tf_op jit(solution)/shard_map/ppermute | solution.py:490
  18.3 6.6 %collective-permute-start.8 = (bf16[2,256,256]{2,1,0:T(8,128)(2,1)S(1)}, bf16[2,256,256]{2,1,0:T(8,128)(2,1)S(1)}, u32[]{:S(2)}, u32[]{:S(2)}) collective-permute-start(bf16[2,256,256]{2,1,0:T(8,128)(2,1)S(1)} %chip_sum.2._), channel_id=1, source_target_pairs={{0,8},{1,17},{2,10},{3,19},{4,12},{5,21},{6,14},{7,23},{8,0},{9,25... | collective-permute-start | bytes 786440 | tf_op jit(solution)/shard_map/ppermute | solution.py:498
  21.4 6.9 %collective-permute-start.9 = (bf16[2,256,256]{2,1,0:T(8,128)(2,1)S(1)}, bf16[2,256,256]{2,1,0:T(8,128)(2,1)S(1)}, u32[]{:S(2)}, u32[]{:S(2)}) collective-permute-start(bf16[2,256,256]{2,1,0:T(8,128)(2,1)S(1)} %chip_sum.3.__), channel_id=1, source_target_pairs={{0,8},{1,17},{2,10},{3,19},{4,12},{5,21},{6,14},{7,23},{8,0},{9,25... | collective-permute-start | bytes 786440 | tf_op jit(solution)/shard_map/ppermute | solution.py:498
  22.1 2.9 %collective-permute-start.7 = (bf16[2,256,512]{2,1,0:T(8,128)(2,1)S(1)}, bf16[2,256,512]{2,1,0:T(8,128)(2,1)S(1)}, u32[]{:S(2)}, u32[]{:S(2)}) collective-permute-start(bf16[2,256,512]{2,1,0:T(8,128)(2,1)S(1)} %get-tuple-element.84), channel_id=1, source_target_pairs={{0,1},{1,0},{2,3},{3,2},{4,5},{5,4},{6,7},{7,6},{8,9},{9,8},{10,11... | collective-permute-start | bytes 1572872 | tf_op jit(solution)/shard_map/ppermute | solution.py:509
  25.0 7.3 %collective-permute-start.11 = (bf16[1,256,256]{2,1,0:T(8,128)(2,1)S(1)}, bf16[1,256,256]{2,1,0:T(8,128)(2,1)S(1)}, u32[]{:S(2)}, u32[]{:S(2)}) collective-permute-start(bf16[1,256,256]{2,1,0:T(8,128)(2,1)S(1)} %get-tuple-element.85._.refs_3_), channel_id=1, source_target_pairs={{0,16},{1,9},{2,18},{3,11},{4,20},{5,13},{6,22},{7,15},{8,24},{9,1... | collective-permute-start | bytes 393224 | tf_op jit(solution)/shard_map/ppermute | solution.py:498
  26.6 5.7 %collective-permute-start.6 = (bf16[36,1024]{1,0:T(8,128)(2,1)S(1)}, bf16[36,1024]{1,0:T(8,128)(2,1)S(1)}, u32[]{:S(2)}, u32[]{:S(2)}) collective-permute-start(bf16[36,1024]{1,0:T(8,128)(2,1)S(1)} %pack_lon.1), channel_id=1, source_target_pairs={{7,0},{0,1},{1,2},{2,3},{3,4},{4,5},{5,6},{6,7},{15,8},{8,9},{9,10... | collective-permute-start | bytes 221192 | tf_op jit(solution)/shard_map/ppermute | solution.py:516
  28.4 5.0 %collective-permute-start.12 = (bf16[1,256,256]{2,1,0:T(8,128)(2,1)S(1)}, bf16[1,256,256]{2,1,0:T(8,128)(2,1)S(1)}, u32[]{:S(2)}, u32[]{:S(2)}) collective-permute-start(bf16[1,256,256]{2,1,0:T(8,128)(2,1)S(1)} %get-tuple-element.86._), channel_id=1, source_target_pairs={{0,16},{1,9},{2,18},{3,11},{4,20},{5,13},{6,22},{7,15},{8,24},{9,1... | collective-permute-start | bytes 393224 | tf_op jit(solution)/shard_map/ppermute | solution.py:498
  30.1 10.2 %collective-permute-start.10 = (bf16[36,1024]{1,0:T(8,128)(2,1)S(1)}, bf16[36,1024]{1,0:T(8,128)(2,1)S(1)}, u32[]{:S(2)}, u32[]{:S(2)}) collective-permute-start(bf16[36,1024]{1,0:T(8,128)(2,1)S(1)} %pack_diag.1), channel_id=1, source_target_pairs={{15,0},{24,1},{9,2},{26,3},{11,4},{28,5},{13,6},{30,7},{23,8},{0,9... | collective-permute-start | bytes 221192 | tf_op jit(solution)/shard_map/ppermute | solution.py:532
  33.4 7.6 %collective-permute-start.14 = (bf16[64,512]{1,0:T(8,128)(2,1)S(1)}, bf16[64,512]{1,0:T(8,128)(2,1)S(1)}, u32[]{:S(2)}, u32[]{:S(2)}) collective-permute-start(bf16[64,512]{1,0:T(8,128)(2,1)S(1)} %get-tuple-element.94), channel_id=1, source_target_pairs={{0,6},{1,7},{2,4},{3,5},{4,2},{5,3},{6,0},{7,1},{8,14},{9,15},{10,... | collective-permute-start | bytes 196616 | tf_op jit(solution)/shard_map/ppermute | solution.py:544
  37.7 5.2 %collective-permute-start.15 = (bf16[64,512]{1,0:T(8,128)(2,1)S(1)}, bf16[64,512]{1,0:T(8,128)(2,1)S(1)}, u32[]{:S(2)}, u32[]{:S(2)}) collective-permute-start(bf16[64,512]{1,0:T(8,128)(2,1)S(1)} %get-tuple-element.95), channel_id=1, source_target_pairs={{0,4},{1,5},{2,6},{3,7},{4,0},{5,1},{6,2},{7,3},{8,12},{9,13},{10,... | collective-permute-start | bytes 196616 | tf_op jit(solution)/shard_map/ppermute | solution.py:544
  37.7 5.2 %collective-permute-start.16 = (bf16[64,512]{1,0:T(8,128)(2,1)S(1)}, bf16[64,512]{1,0:T(8,128)(2,1)S(1)}, u32[]{:S(2)}, u32[]{:S(2)}) collective-permute-start(bf16[64,512]{1,0:T(8,128)(2,1)S(1)} %get-tuple-element.89._), channel_id=1, source_target_pairs={{0,2},{1,3},{2,0},{3,1},{4,6},{5,7},{6,4},{7,5},{8,10},{9,11},{10,... | collective-permute-start | bytes 196616 | tf_op jit(solution)/shard_map/ppermute | solution.py:544
  38.5 8.5 %collective-permute-start.13 = (bf16[108,1024]{1,0:T(8,128)(2,1)S(1)}, bf16[108,1024]{1,0:T(8,128)(2,1)S(1)}, u32[]{:S(2)}, u32[]{:S(2)}) collective-permute-start(bf16[108,1024]{1,0:T(8,128)(2,1)S(1)} %pack_lat.1), channel_id=1, source_target_pairs={{24,0},{9,1},{26,2},{11,3},{28,4},{13,5},{30,6},{15,7},{0,8},{17,9... | collective-permute-start | bytes 663560 | tf_op jit(solution)/shard_map/ppermute | solution.py:550
  43.0 5.0 %collective-permute-start.17 = (bf16[64,512]{1,0:T(8,128)(2,1)S(1)}, bf16[64,512]{1,0:T(8,128)(2,1)S(1)}, u32[]{:S(2)}, u32[]{:S(2)}) collective-permute-start(bf16[64,512]{1,0:T(8,128)(2,1)S(1)} %line_sum.1.refs_0_), channel_id=1, source_target_pairs={{0,8},{8,0},{16,24},{24,16},{1,9},{9,1},{17,25},{25,17},{2,10},{10... | collective-permute-start | bytes 196616 | tf_op jit(solution)/shard_map/ppermute | solution.py:558
  43.3 4.9 %collective-permute-start.18 = (bf16[64,512]{1,0:T(8,128)(2,1)S(1)}, bf16[64,512]{1,0:T(8,128)(2,1)S(1)}, u32[]{:S(2)}, u32[]{:S(2)}) collective-permute-start(bf16[64,512]{1,0:T(8,128)(2,1)S(1)} %line_sum.1.refs_0_), channel_id=1, source_target_pairs={{0,16},{8,24},{16,0},{24,8},{1,17},{9,25},{17,1},{25,9},{2,18},{10... | collective-permute-start | bytes 196616 | tf_op jit(solution)/shard_map/ppermute | solution.py:558
  44.5 5.2 %collective-permute-start.19 = (bf16[64,512]{1,0:T(8,128)(2,1)S(1)}, bf16[64,512]{1,0:T(8,128)(2,1)S(1)}, u32[]{:S(2)}, u32[]{:S(2)}) collective-permute-start(bf16[64,512]{1,0:T(8,128)(2,1)S(1)} %line_sum.1.refs_0_), channel_id=1, source_target_pairs={{0,24},{8,16},{16,8},{24,0},{1,25},{9,17},{17,9},{25,1},{2,26},{10... | collective-permute-start | bytes 196616 | tf_op jit(solution)/shard_map/ppermute | solution.py:558

commit v24 on v18

--- a/solution.py
+++ b/solution.py
@@ -154,7 +154,11 @@
     pack_kernel(*refs)
 
 
-def own_kernel(inner_own, qkv_weight, proj_weight, normed, projected, d_mixed):
+def own_kernel(
+    fields, cotangent, pick_outer, pick_inner, qkv_weight, proj_weight,
+    outer_own, inner_own, normed, projected, d_mixed,
+):
+    pack_kernel(fields, cotangent, pick_outer, pick_inner, outer_own, inner_own)
     normed[...], projected[...], d_mixed[...] = project(inner_own[...], qkv_weight, proj_weight)
 
 
@@ -445,14 +449,13 @@
     inner_lat, lon_piece = call(
         pack_kernel, [half, quarter], own_fields, own_grads, pick_inner, pick_lon, name="pack", flops=LOAD
     )
-    outer_lat, diag_piece, outer_own, inner_own = call(
-        pack_rest_kernel, [quarter, quarter, whole, whole],
-        lon_piece, own_fields, own_grads, pick_outer, pick_diag, pick_outer_own, pick_own,
+    outer_lat, diag_piece = call(
+        pack_rest_kernel, [quarter, quarter], lon_piece, own_fields, own_grads, pick_outer, pick_diag,
         name="pack_rest", flops=5 * 10**8, unread=(0,),
     )
-    own_parts = call(
-        own_kernel, [((HALF, lanes), F32) for lanes in (width, 3 * width, width)],
-        inner_own, qkv_weight, proj_weight,
+    outer_own, inner_own, *own_parts = call(
+        own_kernel, [whole, whole, *(((HALF, lanes), F32) for lanes in (width, 3 * width, width))],
+        own_fields, own_grads, pick_outer_own, pick_own, qkv_weight, proj_weight,
         name="own", flops=5 * 10**8,
     )
     inner_in = lax.ppermute(inner_lat, both, lat_route)

time: 50 us -> 49.9 us (level)
  starting transfers between devices: 25.6 us -> 25 us
where the time goes in v24:
time: 49.9 us; the launch traced here: 49.8 us
  starting transfers between devices  25 us (50%)
  Pallas kernels  11.8 us (24%)
  waiting for transfers between devices  11.2 us (22%)
  local copies, waits for them, and re-layouts  0.94 us (2%)
  between operations  0.81 us (2%)
    pallas_call x22, Pallas kernels, call(): pl.pallas_call(kernel, out_shape=shapes, in_specs=[anywhere if i in unrea...  11.8 us
    ppermute x4, starting transfers between devices, halving(): return lax.ppermute(send, both, route)  5.44 us
    ppermute x4, waiting for transfers between devices, halving(): return lax.ppermute(send, both, route)  4.96 us
    ppermute x3, starting transfers between devices, per_device(): lax.ppermute(parts[step], 'lon', [(j, j ^ 2 * step) for j in range(lon_si...  4.64 us
    ppermute x1, starting transfers between devices, per_device(): inner_in = lax.ppermute(inner_lat, both, lat_route)  3.94 us
    ppermute x3, starting transfers between devices, per_device(): lax.ppermute(line_sum, 'lat', [(i, i ^ step) for i in range(lat_size)])  3.55 us
    ppermute x1, waiting for transfers between devices, per_device(): lon_home = lax.ppermute(lon_back, both, back(lon_route))  2.15 us
    ppermute x3, waiting for transfers between devices, per_device(): lax.ppermute(parts[step], 'lon', [(j, j ^ 2 * step) for j in range(lon_si...  1.95 us
  transfers between devices with their start and end apart: 20, of which 9 were waited for; matrix products, arithmetic and copies ran while one was open for 0% of the time, Pallas kernels for 16%

profile of v24, /device:TPU:0, one launch (start us, length us, event | category | flops | bytes accessed | tf_op | source)
XLA Modules:
  0.0 49.8 jit_solution(15390909276293404529)
XLA Ops:
  0.7 0.1 order.1
  0.8 0.8 %copy-done.3 = bf16[2,6,24,512]{3,2,1,0:T(8,128)(2,1)S(1)} copy-done((bf16[2,6,24,512]{3,2,1,0:T(8,128)(2,1)S(1)}, bf16[2,6,24,512]{3,2,1,0:T(8,128)(2,1)}, u32[]{:S(2)}) %copy-start.3) | copy-done | bytes 294936
  1.6 0.1 copy-done.2
  1.7 0.4 pack.1
  2.1 3.9 %collective-permute-start = (bf16[72,1024]{1,0:T(8,128)(2,1)S(1)}, bf16[72,1024]{1,0:T(8,128)(2,1)S(1)}, u32[]{:S(2)}, u32[]{:S(2)}) collective-permute-start(bf16[72,1024]{1,0:T(8,128)(2,1)S(1)} %get-tuple-element.59), channel_id=1, source_target_pairs={{0,24},{1,9},{2,26},{3,11},{4,28},{5,13},{6,30},{7,15},{8,0},{9,17... | collective-permute-start | bytes 442376 | tf_op jit(solution)/shard_map/ppermute | solution.py:461
  6.0 1.8 %collective-permute-start.1 = (bf16[36,1024]{1,0:T(8,128)(2,1)S(1)}, bf16[36,1024]{1,0:T(8,128)(2,1)S(1)}, u32[]{:S(2)}, u32[]{:S(2)}) collective-permute-start(bf16[36,1024]{1,0:T(8,128)(2,1)S(1)} %get-tuple-element.63._), channel_id=1, source_target_pairs={{0,7},{1,0},{2,1},{3,2},{4,3},{5,4},{6,5},{7,6},{8,15},{9,8},{10,9... | collective-permute-start | bytes 221192 | tf_op jit(solution)/shard_map/ppermute | solution.py:462
  7.8 0.3 pack_rest.1
  8.1 1.5 %collective-permute-start.2 = (bf16[36,1024]{1,0:T(8,128)(2,1)S(1)}, bf16[36,1024]{1,0:T(8,128)(2,1)S(1)}, u32[]{:S(2)}, u32[]{:S(2)}) collective-permute-start(bf16[36,1024]{1,0:T(8,128)(2,1)S(1)} %get-tuple-element.66), channel_id=1, source_target_pairs={{0,24},{1,9},{2,26},{3,11},{4,28},{5,13},{6,30},{7,15},{8,0},{9,17... | collective-permute-start | bytes 221192 | tf_op jit(solution)/shard_map/ppermute | solution.py:463
  9.6 1.6 %collective-permute-start.3 = (bf16[36,1024]{1,0:T(8,128)(2,1)S(1)}, bf16[36,1024]{1,0:T(8,128)(2,1)S(1)}, u32[]{:S(2)}, u32[]{:S(2)}) collective-permute-start(bf16[36,1024]{1,0:T(8,128)(2,1)S(1)} %get-tuple-element.67), channel_id=1, source_target_pairs={{0,15},{1,24},{2,9},{3,26},{4,11},{5,28},{6,13},{7,30},{8,23},{9,0... | collective-permute-start | bytes 221192 | tf_op jit(solution)/shard_map/ppermute | solution.py:464
  11.2 1.0 %own.1 = (f32[72,1024]{1,0:T(8,128)S(1)}, f32[72,1024]{1,0:T(8,128)S(1)}, f32[72,512]{1,0:T(8,128)S(1)}, f32[72,1536]{1,0:T(8,128)S(1)}, f32[72,512]{1,0:T(8,128)S(1)}) custom-call(bf16[288,512]{1,0:T(8,128)(2,1)S(1)} %bitcast.7, bf16[288,512]{1,0:T(8,128)(2,1)S(1)} %bitcast.10, bf16[72,288]{1,0:T(8,128)(2,1)S(1)} %get-tuple-element.51.pick_outer, ...), custom_call_target="tpu_custom_call" | custom-call | flops 500000000 | bytes 4097024 | tf_op jit(solution)/shard_map/own/pallas_call | solution.py:408
  12.2 2.1 %inner.1 = (f32[2,256,512]{2,1,0:T(8,128)S(1)}, bf16[144,512]{1,0:T(8,128)(2,1)S(1)}, bf16[144,512]{1,0:T(8,128)(2,1)S(1)}, bf16[2,256,144]{2,1,0:T(8,128)(2,1)S...) custom-call(f32[72,1024]{1,0:T(8,128)S(1)} %get-tuple-element.53.own, ...), custom_call_target="tpu_custom_call" | custom-call | flops 1000000000 | bytes 5505024 | tf_op jit(solution)/shard_map/inner/pallas_call | solution.py:408
  14.4 2.4 %outer.1 = (bf16[2,256,256]{2,1,0:T(8,128)(2,1)S(1)}, bf16[2,256,256]{2,1,0:T(8,128)(2,1)S(1)}, bf16[144,512]{1,0:T(8,128)(2,1)S(1)}, bf16[144,512]{1,0:T(8,128)...) custom-call(f32[72,1024]{1,0:T(8,128)S(1)} %get-tuple-element.62.own, ...), custom_call_target="tpu_custom_call" | custom-call | flops 1000000000 | bytes 5365760 | tf_op jit(solution)/shard_map/outer/pallas_call | solution.py:408
  16.8 0.2 collective-permute-start.4
  16.9 0.4 collective-permute-start.5
  17.4 0.4 keep.1
  17.8 0.6 %collective-permute-done.4.refs_1_ = bf16[2,256,256]{2,1,0:T(8,128)(2,1)S(1)} collective-permute-done((bf16[2,256,256]{2,1,0:T(8,128)(2,1)S(1)}, bf16[2,256,256]{2,1,0:T(8,128)(2,1)S(1)}, u32[]{:S(2)}, u32[]{:S(2)}) %collective-permute-start.4) | collective-permute-done | bytes 262176 | tf_op jit(solution)/shard_map/ppermute | solution.py:487
  18.4 0.1 chip_sum.2._
  18.4 1.9 %collective-permute-start.8 = (bf16[2,256,256]{2,1,0:T(8,128)(2,1)S(1)}, bf16[2,256,256]{2,1,0:T(8,128)(2,1)S(1)}, u32[]{:S(2)}, u32[]{:S(2)}) collective-permute-start(bf16[2,256,256]{2,1,0:T(8,128)(2,1)S(1)} %chip_sum.2._), channel_id=1, source_target_pairs={{0,8},{1,17},{2,10},{3,19},{4,12},{5,21},{6,14},{7,23},{8,0},{9,25... | collective-permute-start | bytes 786440 | tf_op jit(solution)/shard_map/ppermute | solution.py:496
  20.3 0.1 chip_sum.3.__
  20.4 0.3 collective-permute-start.9
  20.7 0.7 %rest.1 = (bf16[2,256,512]{2,1,0:T(8,128)(2,1)S(1)}, bf16[2,256,512]{2,1,0:T(8,128)(2,1)S(1)}) custom-call(bf16[2,256,256]{2,1,0:T(8,128)(2,1)S(1)} %chip_sum.2._, bf16[2,256,256]{2,1,0:T(8,128)(2,1)S(1)} %chip_sum.3.__, bf16[2,256,144]{2,1,0:T(8,128)(2,1)S(1)} %get-tuple-element.60.refs_0_, bf16[144,2048]{1,0:T(8,128)(2,1)S(1)} %get-tuple-element.61.refs_1_.refs_2_, ...), custom_call_target="tpu_custom_call" | custom-call | tf_op jit(solution)/shard_map/rest/pallas_call | solution.py:408
  21.4 0.1 collective-permute-start.7
  21.5 0.9 %outputs.1 = (bf16[144,1024]{1,0:T(8,128)(2,1)S(1)}, bf16[144,1024]{1,0:T(8,128)(2,1)S(1)}) custom-call(bf16[2,256,512]{2,1,0:T(8,128)(2,1)S(1)} %get-tuple-element.77._.refs_0_, bf16[144,512]{1,0:T(8,128)(2,1)S(1)} %get-tuple-element.78.refs_0_, bf16[144,512]{1,0:T(8,128)(2,1)S(1)} %get-tuple-element.79.refs_1_, ...), custom_call_target="tpu_custom_call" | custom-call | flops 10000000000 | bytes 4980736 | tf_op jit(solution)/shard_map/outputs/pallas_call | solution.py:408
  22.4 2.5 %collective-permute-done.8.refs_2_ = bf16[2,256,256]{2,1,0:T(8,128)(2,1)S(1)} collective-permute-done((bf16[2,256,256]{2,1,0:T(8,128)(2,1)S(1)}, bf16[2,256,256]{2,1,0:T(8,128)(2,1)S(1)}, u32[]{:S(2)}, u32[]{:S(2)}) %collective-permute-start.8) | collective-permute-done | bytes 262176 | tf_op jit(solution)/shard_map/ppermute | solution.py:496
  24.9 0.1 halve1.2
  25.0 1.6 %collective-permute-start.11 = (bf16[1,256,256]{2,1,0:T(8,128)(2,1)S(1)}, bf16[1,256,256]{2,1,0:T(8,128)(2,1)S(1)}, u32[]{:S(2)}, u32[]{:S(2)}) collective-permute-start(bf16[1,256,256]{2,1,0:T(8,128)(2,1)S(1)} %get-tuple-element.85._.refs_3_), channel_id=1, source_target_pairs={{0,16},{1,9},{2,18},{3,11},{4,20},{5,13},{6,22},{7,15},{8,24},{9,1... | collective-permute-start | bytes 393224 | tf_op jit(solution)/shard_map/ppermute | solution.py:496
  26.6 0.1 pack_lon.1
  26.8 1.5 %collective-permute-done.9.refs_2_ = bf16[2,256,256]{2,1,0:T(8,128)(2,1)S(1)} collective-permute-done((bf16[2,256,256]{2,1,0:T(8,128)(2,1)S(1)}, bf16[2,256,256]{2,1,0:T(8,128)(2,1)S(1)}, u32[]{:S(2)}, u32[]{:S(2)}) %collective-permute-start.9) | collective-permute-done | bytes 262176 | tf_op jit(solution)/shard_map/ppermute | solution.py:496
  28.3 0.1 halve1.3
  28.4 1.7 %collective-permute-start.12 = (bf16[1,256,256]{2,1,0:T(8,128)(2,1)S(1)}, bf16[1,256,256]{2,1,0:T(8,128)(2,1)S(1)}, u32[]{:S(2)}, u32[]{:S(2)}) collective-permute-start(bf16[1,256,256]{2,1,0:T(8,128)(2,1)S(1)} %get-tuple-element.86._), channel_id=1, source_target_pairs={{0,16},{1,9},{2,18},{3,11},{4,20},{5,13},{6,22},{7,15},{8,24},{9,1... | collective-permute-start | bytes 393224 | tf_op jit(solution)/shard_map/ppermute | solution.py:496
  30.1 0.1 pack_diag.1
  30.2 0.1 collective-permute-start.10
  30.3 2.1 %collective-permute-done.6.lon_in._ = bf16[36,1024]{1,0:T(8,128)(2,1)S(1)} collective-permute-done((bf16[36,1024]{1,0:T(8,128)(2,1)S(1)}, bf16[36,1024]{1,0:T(8,128)(2,1)S(1)}, u32[]{:S(2)}, u32[]{:S(2)}) %collective-permute-start.6) | collective-permute-done | bytes 73760 | tf_op jit(solution)/shard_map/ppermute | solution.py:514
  32.5 1.0 %collective-permute-done.12.refs_2_ = bf16[1,256,256]{2,1,0:T(8,128)(2,1)S(1)} collective-permute-done((bf16[1,256,256]{2,1,0:T(8,128)(2,1)S(1)}, bf16[1,256,256]{2,1,0:T(8,128)(2,1)S(1)}, u32[]{:S(2)}, u32[]{:S(2)}) %collective-permute-start.12) | collective-permute-done | bytes 131104 | tf_op jit(solution)/shard_map/ppermute | solution.py:496
  33.5 4.0 %collective-permute-start.14 = (bf16[64,512]{1,0:T(8,128)(2,1)S(1)}, bf16[64,512]{1,0:T(8,128)(2,1)S(1)}, u32[]{:S(2)}, u32[]{:S(2)}) collective-permute-start(bf16[64,512]{1,0:T(8,128)(2,1)S(1)} %get-tuple-element.94), channel_id=1, source_target_pairs={{0,6},{1,7},{2,4},{3,5},{4,2},{5,3},{6,0},{7,1},{8,14},{9,15},{10,... | collective-permute-start | bytes 196616 | tf_op jit(solution)/shard_map/ppermute | solution.py:542
  37.5 0.6 %collective-permute-start.16 = (bf16[64,512]{1,0:T(8,128)(2,1)S(1)}, bf16[64,512]{1,0:T(8,128)(2,1)S(1)}, u32[]{:S(2)}, u32[]{:S(2)}) collective-permute-start(bf16[64,512]{1,0:T(8,128)(2,1)S(1)} %get-tuple-element.89._), channel_id=1, source_target_pairs={{0,2},{1,3},{2,0},{3,1},{4,6},{5,7},{6,4},{7,5},{8,10},{9,11},{10,... | collective-permute-start | bytes 196616 | tf_op jit(solution)/shard_map/ppermute | solution.py:542
  38.1 0.1 pack_lat.1
  38.3 1.8 %collective-permute-start.13 = (bf16[108,1024]{1,0:T(8,128)(2,1)S(1)}, bf16[108,1024]{1,0:T(8,128)(2,1)S(1)}, u32[]{:S(2)}, u32[]{:S(2)}) collective-permute-start(bf16[108,1024]{1,0:T(8,128)(2,1)S(1)} %pack_lat.1), channel_id=1, source_target_pairs={{24,0},{9,1},{26,2},{11,3},{28,4},{13,5},{30,6},{15,7},{0,8},{17,9... | collective-permute-start | bytes 663560 | tf_op jit(solution)/shard_map/ppermute | solution.py:548
  40.0 0.8 %place.1.placed._ = f32[288,1024]{1,0:T(8,128)S(1)} custom-call(bf16[144,1024]{1,0:T(8,128)(2,1)S(1)} %get-tuple-element.82._.refs_3_.inner_results, bf16[144,1024]{1,0:T(8,128)(2,1)S(1)} %get-tuple-element.83.outer_results, bf16[36,1024]{1,0:T(8,128)(2,1)S(1)} %collective-permute-done.6.lon_in._, bf16[36,1024]{1,0:T(8,128)(2,1)S(1)} %collective-permute-done.10.diag_in), custom_call_target="tpu_custom_call" | custom-call | bytes 1916928 | tf_op jit(solution)/shard_map/place/pallas_call | solution.py:408
  40.8 1.9 %collective-permute-done.15.refs_2_ = bf16[64,512]{1,0:T(8,128)(2,1)S(1)} collective-permute-done((bf16[64,512]{1,0:T(8,128)(2,1)S(1)}, bf16[64,512]{1,0:T(8,128)(2,1)S(1)}, u32[]{:S(2)}, u32[]{:S(2)}) %collective-permute-start.15) | collective-permute-done | bytes 65568 | tf_op jit(solution)/shard_map/ppermute | solution.py:542
  42.8 0.9 %collective-permute-start.19 = (bf16[64,512]{1,0:T(8,128)(2,1)S(1)}, bf16[64,512]{1,0:T(8,128)(2,1)S(1)}, u32[]{:S(2)}, u32[]{:S(2)}) collective-permute-start(bf16[64,512]{1,0:T(8,128)(2,1)S(1)} %line_sum.1.refs_0_), channel_id=1, source_target_pairs={{0,24},{8,16},{16,8},{24,0},{1,25},{9,17},{17,9},{25,1},{2,26},{10... | collective-permute-start | bytes 196616 | tf_op jit(solution)/shard_map/ppermute | solution.py:556
  43.7 1.0 %collective-permute-start.18 = (bf16[64,512]{1,0:T(8,128)(2,1)S(1)}, bf16[64,512]{1,0:T(8,128)(2,1)S(1)}, u32[]{:S(2)}, u32[]{:S(2)}) collective-permute-start(bf16[64,512]{1,0:T(8,128)(2,1)S(1)} %line_sum.1.refs_0_), channel_id=1, source_target_pairs={{0,16},{8,24},{16,0},{24,8},{1,17},{9,25},{17,1},{25,9},{2,18},{10... | collective-permute-start | bytes 196616 | tf_op jit(solution)/shard_map/ppermute | solution.py:556
  44.7 1.7 %collective-permute-start.17 = (bf16[64,512]{1,0:T(8,128)(2,1)S(1)}, bf16[64,512]{1,0:T(8,128)(2,1)S(1)}, u32[]{:S(2)}, u32[]{:S(2)}) collective-permute-start(bf16[64,512]{1,0:T(8,128)(2,1)S(1)} %line_sum.1.refs_0_), channel_id=1, source_target_pairs={{0,8},{8,0},{16,24},{24,16},{1,9},{9,1},{17,25},{25,17},{2,10},{10... | collective-permute-start | bytes 196616 | tf_op jit(solution)/shard_map/ppermute | solution.py:556
  46.3 1.0 %place_rest.1 = (bf16[288,512]{1,0:T(8,128)(2,1)}, bf16[288,512]{1,0:T(8,128)(2,1)}, f32[8,128]{1,0:T(8,128)S(1)}) custom-call(f32[288,1024]{1,0:T(8,128)S(1)} %place.1.placed._, bf16[108,1024]{1,0:T(8,128)(2,1)S(1)} %collective-permute-done.13.lat_in), custom_call_target="tpu_custom_call" | custom-call | bytes 1994752 | tf_op jit(solution)/shard_map/place_rest/pallas_call | solution.py:408
  47.4 0.7 %collective-permute-done.19.refs_3_ = bf16[64,512]{1,0:T(8,128)(2,1)S(1)} collective-permute-done((bf16[64,512]{1,0:T(8,128)(2,1)S(1)}, bf16[64,512]{1,0:T(8,128)(2,1)S(1)}, u32[]{:S(2)}, u32[]{:S(2)}) %collective-permute-start.19) | collective-permute-done | bytes 65568 | tf_op jit(solution)/shard_map/ppermute | solution.py:556
  48.1 0.5 %collective-permute-done.18.refs_2_ = bf16[64,512]{1,0:T(8,128)(2,1)S(1)} collective-permute-done((bf16[64,512]{1,0:T(8,128)(2,1)S(1)}, bf16[64,512]{1,0:T(8,128)(2,1)S(1)}, u32[]{:S(2)}, u32[]{:S(2)}) %collective-permute-start.18) | collective-permute-done | bytes 65568 | tf_op jit(solution)/shard_map/ppermute | solution.py:556
  48.6 0.3 collective-permute-done.17.refs_1_
  48.9 0.9 %finish.1 = (f32[64,1536]{1,0:T(8,128)}, f32[64,512]{1,0:T(8,128)}) custom-call(f32[8,128]{1,0:T(8,128)S(1)} %get-tuple-element.92._, bf16[64,512]{1,0:T(8,128)(2,1)S(1)} %line_sum.1.refs_0_, bf16[64,512]{1,0:T(8,128)(2,1)S(1)} %collective-permute-done.17.refs_1_, bf16[64,512]{1,0:T(8,128)(2,1)S(1)} %collective-permute-done.18.refs_2_, ...), custom_call_target="tpu_custom_call" | custom-call | bytes 790528 | tf_op jit(solution)/shard_map/finish/pallas_call | solution.py:408
  (22 shorter events, 0.2 us)
Async XLA Ops:
  0.6 1.0 %copy-start.3 = (bf16[2,6,24,512]{3,2,1,0:T(8,128)(2,1)S(1)}, bf16[2,6,24,512]{3,2,1,0:T(8,128)(2,1)}, u32[]{:S(2)}) copy-start(bf16[2,6,24,512]{3,2,1,0:T(8,128)(2,1)} %param.5) | copy-start | bytes 884740
  0.6 1.0 %copy-start.2 = (bf16[2,6,24,512]{3,2,1,0:T(8,128)(2,1)S(1)}, bf16[2,6,24,512]{3,2,1,0:T(8,128)(2,1)}, u32[]{:S(2)}) copy-start(bf16[2,6,24,512]{3,2,1,0:T(8,128)(2,1)} %param.4) | copy-start | bytes 884740
  1.7 9.5 %copy-start.1 = (bf16[512,512]{1,0:T(8,128)(2,1)S(1)}, bf16[512,512]{1,0:T(8,128)(2,1)}, u32[]{:S(2)}) copy-start(bf16[512,512]{1,0:T(8,128)(2,1)} %refs_7_.1) | copy-start | bytes 1572868
  2.0 9.2 %copy-start = (bf16[512,1536]{1,0:T(8,128)(2,1)S(1)}, bf16[512,1536]{1,0:T(8,128)(2,1)}, u32[]{:S(2)}) copy-start(bf16[512,1536]{1,0:T(8,128)(2,1)} %refs_6_.1) | copy-start | bytes 4718596
  2.1 10.2 %collective-permute-start = (bf16[72,1024]{1,0:T(8,128)(2,1)S(1)}, bf16[72,1024]{1,0:T(8,128)(2,1)S(1)}, u32[]{:S(2)}, u32[]{:S(2)}) collective-permute-start(bf16[72,1024]{1,0:T(8,128)(2,1)S(1)} %get-tuple-element.59), channel_id=1, source_target_pairs={{0,24},{1,9},{2,26},{3,11},{4,28},{5,13},{6,30},{7,15},{8,0},{9,17... | collective-permute-start | bytes 442376 | tf_op jit(solution)/shard_map/ppermute | solution.py:461
  6.0 8.4 %collective-permute-start.1 = (bf16[36,1024]{1,0:T(8,128)(2,1)S(1)}, bf16[36,1024]{1,0:T(8,128)(2,1)S(1)}, u32[]{:S(2)}, u32[]{:S(2)}) collective-permute-start(bf16[36,1024]{1,0:T(8,128)(2,1)S(1)} %get-tuple-element.63._), channel_id=1, source_target_pairs={{0,7},{1,0},{2,1},{3,2},{4,3},{5,4},{6,5},{7,6},{8,15},{9,8},{10,9... | collective-permute-start | bytes 221192 | tf_op jit(solution)/shard_map/ppermute | solution.py:462
  8.1 6.3 %collective-permute-start.2 = (bf16[36,1024]{1,0:T(8,128)(2,1)S(1)}, bf16[36,1024]{1,0:T(8,128)(2,1)S(1)}, u32[]{:S(2)}, u32[]{:S(2)}) collective-permute-start(bf16[36,1024]{1,0:T(8,128)(2,1)S(1)} %get-tuple-element.66), channel_id=1, source_target_pairs={{0,24},{1,9},{2,26},{3,11},{4,28},{5,13},{6,30},{7,15},{8,0},{9,17... | collective-permute-start | bytes 221192 | tf_op jit(solution)/shard_map/ppermute | solution.py:463
  9.6 4.8 %collective-permute-start.3 = (bf16[36,1024]{1,0:T(8,128)(2,1)S(1)}, bf16[36,1024]{1,0:T(8,128)(2,1)S(1)}, u32[]{:S(2)}, u32[]{:S(2)}) collective-permute-start(bf16[36,1024]{1,0:T(8,128)(2,1)S(1)} %get-tuple-element.67), channel_id=1, source_target_pairs={{0,15},{1,24},{2,9},{3,26},{4,11},{5,28},{6,13},{7,30},{8,23},{9,0... | collective-permute-start | bytes 221192 | tf_op jit(solution)/shard_map/ppermute | solution.py:464
  16.8 1.6 %collective-permute-start.4 = (bf16[2,256,256]{2,1,0:T(8,128)(2,1)S(1)}, bf16[2,256,256]{2,1,0:T(8,128)(2,1)S(1)}, u32[]{:S(2)}, u32[]{:S(2)}) collective-permute-start(bf16[2,256,256]{2,1,0:T(8,128)(2,1)S(1)} %get-tuple-element.72), channel_id=1, source_target_pairs={{0,1},{1,0},{2,3},{3,2},{4,5},{5,4},{6,7},{7,6},{8,9},{9,8},{10,11... | collective-permute-start | bytes 786440 | tf_op jit(solution)/shard_map/ppermute | solution.py:487
  16.9 3.4 %collective-permute-start.5 = (bf16[2,256,256]{2,1,0:T(8,128)(2,1)S(1)}, bf16[2,256,256]{2,1,0:T(8,128)(2,1)S(1)}, u32[]{:S(2)}, u32[]{:S(2)}) collective-permute-start(bf16[2,256,256]{2,1,0:T(8,128)(2,1)S(1)} %get-tuple-element.74), channel_id=1, source_target_pairs={{0,1},{1,0},{2,3},{3,2},{4,5},{5,4},{6,7},{7,6},{8,9},{9,8},{10,11... | collective-permute-start | bytes 786440 | tf_op jit(solution)/shard_map/ppermute | solution.py:487
  18.4 6.4 %collective-permute-start.8 = (bf16[2,256,256]{2,1,0:T(8,128)(2,1)S(1)}, bf16[2,256,256]{2,1,0:T(8,128)(2,1)S(1)}, u32[]{:S(2)}, u32[]{:S(2)}) collective-permute-start(bf16[2,256,256]{2,1,0:T(8,128)(2,1)S(1)} %chip_sum.2._), channel_id=1, source_target_pairs={{0,8},{1,17},{2,10},{3,19},{4,12},{5,21},{6,14},{7,23},{8,0},{9,25... | collective-permute-start | bytes 786440 | tf_op jit(solution)/shard_map/ppermute | solution.py:496
  20.4 7.9 %collective-permute-start.9 = (bf16[2,256,256]{2,1,0:T(8,128)(2,1)S(1)}, bf16[2,256,256]{2,1,0:T(8,128)(2,1)S(1)}, u32[]{:S(2)}, u32[]{:S(2)}) collective-permute-start(bf16[2,256,256]{2,1,0:T(8,128)(2,1)S(1)} %chip_sum.3.__), channel_id=1, source_target_pairs={{0,8},{1,17},{2,10},{3,19},{4,12},{5,21},{6,14},{7,23},{8,0},{9,25... | collective-permute-start | bytes 786440 | tf_op jit(solution)/shard_map/ppermute | solution.py:496
  21.4 3.5 %collective-permute-start.7 = (bf16[2,256,512]{2,1,0:T(8,128)(2,1)S(1)}, bf16[2,256,512]{2,1,0:T(8,128)(2,1)S(1)}, u32[]{:S(2)}, u32[]{:S(2)}) collective-permute-start(bf16[2,256,512]{2,1,0:T(8,128)(2,1)S(1)} %get-tuple-element.84), channel_id=1, source_target_pairs={{0,1},{1,0},{2,3},{3,2},{4,5},{5,4},{6,7},{7,6},{8,9},{9,8},{10,11... | collective-permute-start | bytes 1572872 | tf_op jit(solution)/shard_map/ppermute | solution.py:507
  25.0 7.5 %collective-permute-start.11 = (bf16[1,256,256]{2,1,0:T(8,128)(2,1)S(1)}, bf16[1,256,256]{2,1,0:T(8,128)(2,1)S(1)}, u32[]{:S(2)}, u32[]{:S(2)}) collective-permute-start(bf16[1,256,256]{2,1,0:T(8,128)(2,1)S(1)} %get-tuple-element.85._.refs_3_), channel_id=1, source_target_pairs={{0,16},{1,9},{2,18},{3,11},{4,20},{5,13},{6,22},{7,15},{8,24},{9,1... | collective-permute-start | bytes 393224 | tf_op jit(solution)/shard_map/ppermute | solution.py:496
  26.7 5.7 %collective-permute-start.6 = (bf16[36,1024]{1,0:T(8,128)(2,1)S(1)}, bf16[36,1024]{1,0:T(8,128)(2,1)S(1)}, u32[]{:S(2)}, u32[]{:S(2)}) collective-permute-start(bf16[36,1024]{1,0:T(8,128)(2,1)S(1)} %pack_lon.1), channel_id=1, source_target_pairs={{7,0},{0,1},{1,2},{2,3},{3,4},{4,5},{5,6},{6,7},{15,8},{8,9},{9,10... | collective-permute-start | bytes 221192 | tf_op jit(solution)/shard_map/ppermute | solution.py:514
  28.4 5.0 %collective-permute-start.12 = (bf16[1,256,256]{2,1,0:T(8,128)(2,1)S(1)}, bf16[1,256,256]{2,1,0:T(8,128)(2,1)S(1)}, u32[]{:S(2)}, u32[]{:S(2)}) collective-permute-start(bf16[1,256,256]{2,1,0:T(8,128)(2,1)S(1)} %get-tuple-element.86._), channel_id=1, source_target_pairs={{0,16},{1,9},{2,18},{3,11},{4,20},{5,13},{6,22},{7,15},{8,24},{9,1... | collective-permute-start | bytes 393224 | tf_op jit(solution)/shard_map/ppermute | solution.py:496
  30.2 9.8 %collective-permute-start.10 = (bf16[36,1024]{1,0:T(8,128)(2,1)S(1)}, bf16[36,1024]{1,0:T(8,128)(2,1)S(1)}, u32[]{:S(2)}, u32[]{:S(2)}) collective-permute-start(bf16[36,1024]{1,0:T(8,128)(2,1)S(1)} %pack_diag.1), channel_id=1, source_target_pairs={{15,0},{24,1},{9,2},{26,3},{11,4},{28,5},{13,6},{30,7},{23,8},{0,9... | collective-permute-start | bytes 221192 | tf_op jit(solution)/shard_map/ppermute | solution.py:530
  33.5 7.3 %collective-permute-start.14 = (bf16[64,512]{1,0:T(8,128)(2,1)S(1)}, bf16[64,512]{1,0:T(8,128)(2,1)S(1)}, u32[]{:S(2)}, u32[]{:S(2)}) collective-permute-start(bf16[64,512]{1,0:T(8,128)(2,1)S(1)} %get-tuple-element.94), channel_id=1, source_target_pairs={{0,6},{1,7},{2,4},{3,5},{4,2},{5,3},{6,0},{7,1},{8,14},{9,15},{10,... | collective-permute-start | bytes 196616 | tf_op jit(solution)/shard_map/ppermute | solution.py:542
  37.5 5.2 %collective-permute-start.15 = (bf16[64,512]{1,0:T(8,128)(2,1)S(1)}, bf16[64,512]{1,0:T(8,128)(2,1)S(1)}, u32[]{:S(2)}, u32[]{:S(2)}) collective-permute-start(bf16[64,512]{1,0:T(8,128)(2,1)S(1)} %get-tuple-element.95), channel_id=1, source_target_pairs={{0,4},{1,5},{2,6},{3,7},{4,0},{5,1},{6,2},{7,3},{8,12},{9,13},{10,... | collective-permute-start | bytes 196616 | tf_op jit(solution)/shard_map/ppermute | solution.py:542
  37.5 5.3 %collective-permute-start.16 = (bf16[64,512]{1,0:T(8,128)(2,1)S(1)}, bf16[64,512]{1,0:T(8,128)(2,1)S(1)}, u32[]{:S(2)}, u32[]{:S(2)}) collective-permute-start(bf16[64,512]{1,0:T(8,128)(2,1)S(1)} %get-tuple-element.89._), channel_id=1, source_target_pairs={{0,2},{1,3},{2,0},{3,1},{4,6},{5,7},{6,4},{7,5},{8,10},{9,11},{10,... | collective-permute-start | bytes 196616 | tf_op jit(solution)/shard_map/ppermute | solution.py:542
  38.3 8.1 %collective-permute-start.13 = (bf16[108,1024]{1,0:T(8,128)(2,1)S(1)}, bf16[108,1024]{1,0:T(8,128)(2,1)S(1)}, u32[]{:S(2)}, u32[]{:S(2)}) collective-permute-start(bf16[108,1024]{1,0:T(8,128)(2,1)S(1)} %pack_lat.1), channel_id=1, source_target_pairs={{24,0},{9,1},{26,2},{11,3},{28,4},{13,5},{30,6},{15,7},{0,8},{17,9... | collective-permute-start | bytes 663560 | tf_op jit(solution)/shard_map/ppermute | solution.py:548
  42.8 5.3 %collective-permute-start.19 = (bf16[64,512]{1,0:T(8,128)(2,1)S(1)}, bf16[64,512]{1,0:T(8,128)(2,1)S(1)}, u32[]{:S(2)}, u32[]{:S(2)}) collective-permute-start(bf16[64,512]{1,0:T(8,128)(2,1)S(1)} %line_sum.1.refs_0_), channel_id=1, source_target_pairs={{0,24},{8,16},{16,8},{24,0},{1,25},{9,17},{17,9},{25,1},{2,26},{10... | collective-permute-start | bytes 196616 | tf_op jit(solution)/shard_map/ppermute | solution.py:556
  43.7 5.0 %collective-permute-start.18 = (bf16[64,512]{1,0:T(8,128)(2,1)S(1)}, bf16[64,512]{1,0:T(8,128)(2,1)S(1)}, u32[]{:S(2)}, u32[]{:S(2)}) collective-permute-start(bf16[64,512]{1,0:T(8,128)(2,1)S(1)} %line_sum.1.refs_0_), channel_id=1, source_target_pairs={{0,16},{8,24},{16,0},{24,8},{1,17},{9,25},{17,1},{25,9},{2,18},{10... | collective-permute-start | bytes 196616 | tf_op jit(solution)/shard_map/ppermute | solution.py:556
  44.7 4.3 %collective-permute-start.17 = (bf16[64,512]{1,0:T(8,128)(2,1)S(1)}, bf16[64,512]{1,0:T(8,128)(2,1)S(1)}, u32[]{:S(2)}, u32[]{:S(2)}) collective-permute-start(bf16[64,512]{1,0:T(8,128)(2,1)S(1)} %line_sum.1.refs_0_), channel_id=1, source_target_pairs={{0,8},{8,0},{16,24},{24,16},{1,9},{9,1},{17,25},{25,17},{2,10},{10... | collective-permute-start | bytes 196616 | tf_op jit(solution)/shard_map/ppermute | solution.py:556

commit v25 on v24

--- a/solution.py
+++ b/solution.py
@@ -446,8 +446,9 @@
     pick_inner, pick_outer, pick_lon, pick_diag, pick_own, pick_outer_own = picked
     whole, half = ((HALF, 2 * width), F32), ((HALF, 2 * width), BF)
     quarter = ((QUARTER, 2 * width), BF)
-    inner_lat, lon_piece = call(
-        pack_kernel, [half, quarter], own_fields, own_grads, pick_inner, pick_lon, name="pack", flops=LOAD
+    (inner_lat,) = call(pack_kernel, [half], own_fields, own_grads, pick_inner, name="pack", flops=LOAD)
+    (lon_piece,) = call(
+        pack_rest_kernel, [quarter], inner_lat, own_fields, own_grads, pick_lon, name="pack_piece", unread=(0,)
     )
     outer_lat, diag_piece = call(
         pack_rest_kernel, [quarter, quarter], lon_piece, own_fields, own_grads, pick_outer, pick_diag,

time: 49.9 us -> 50.1 us (level)
    pallas_call x22 -> x23, Pallas kernels: 11.8 us -> 11.9 us  [call(): pl.pallas_call(kernel, out_shape=shapes, in_specs=[anywhere if i in unrea...]
  transfers between devices with their start and end apart: 20 -> 20, of which waited for: 9 -> 9; matrix products, arithmetic and copies ran while one was open for 0% -> 0% of each run, Pallas kernels for 16% -> 17%
where the time goes in v25:
time: 50.1 us; the launch traced here: 49.9 us
  starting transfers between devices  25 us (50%)
  Pallas kernels  11.9 us (24%)
  waiting for transfers between devices  11.2 us (22%)
  local copies, waits for them, and re-layouts  0.95 us (2%)
  between operations  0.83 us (2%)
    pallas_call x23, Pallas kernels, call(): pl.pallas_call(kernel, out_shape=shapes, in_specs=[anywhere if i in unrea...  11.9 us
    ppermute x4, starting transfers between devices, halving(): return lax.ppermute(send, both, route)  5.43 us
    ppermute x4, waiting for transfers between devices, halving(): return lax.ppermute(send, both, route)  4.98 us
    ppermute x3, starting transfers between devices, per_device(): lax.ppermute(parts[step], 'lon', [(j, j ^ 2 * step) for j in range(lon_si...  4.65 us
    ppermute x1, starting transfers between devices, per_device(): inner_in = lax.ppermute(inner_lat, both, lat_route)  3.95 us
    ppermute x3, starting transfers between devices, per_device(): lax.ppermute(line_sum, 'lat', [(i, i ^ step) for i in range(lat_size)])  3.55 us
    ppermute x1, waiting for transfers between devices, per_device(): lon_home = lax.ppermute(lon_back, both, back(lon_route))  2.15 us
    ppermute x3, waiting for transfers between devices, per_device(): lax.ppermute(parts[step], 'lon', [(j, j ^ 2 * step) for j in range(lon_si...  1.94 us
  transfers between devices with their start and end apart: 20, of which 9 were waited for; matrix products, arithmetic and copies ran while one was open for 0% of the time, Pallas kernels for 17%

profile of v25, /device:TPU:0, one launch (start us, length us, event | category | flops | bytes accessed | tf_op | source)
XLA Modules:
  0.0 49.9 jit_solution(14690147624909544654)
XLA Ops:
  0.7 0.1 order.1
  0.8 0.8 %copy-done.2 = bf16[2,6,24,512]{3,2,1,0:T(8,128)(2,1)S(1)} copy-done((bf16[2,6,24,512]{3,2,1,0:T(8,128)(2,1)S(1)}, bf16[2,6,24,512]{3,2,1,0:T(8,128)(2,1)}, u32[]{:S(2)}) %copy-start.2) | copy-done | bytes 294936
  1.6 0.1 copy-done.1
  1.7 0.3 pack.1._
  2.0 4.0 %collective-permute-start = (bf16[72,1024]{1,0:T(8,128)(2,1)S(1)}, bf16[72,1024]{1,0:T(8,128)(2,1)S(1)}, u32[]{:S(2)}, u32[]{:S(2)}) collective-permute-start(bf16[72,1024]{1,0:T(8,128)(2,1)S(1)} %pack.1._), channel_id=1, source_target_pairs={{0,24},{1,9},{2,26},{3,11},{4,28},{5,13},{6,30},{7,15},{8,0},{9,17... | collective-permute-start | bytes 442376 | tf_op jit(solution)/shard_map/ppermute | solution.py:462
  5.9 0.2 pack_piece.1._
  6.1 1.9 %collective-permute-start.1 = (bf16[36,1024]{1,0:T(8,128)(2,1)S(1)}, bf16[36,1024]{1,0:T(8,128)(2,1)S(1)}, u32[]{:S(2)}, u32[]{:S(2)}) collective-permute-start(bf16[36,1024]{1,0:T(8,128)(2,1)S(1)} %pack_piece.1._), channel_id=1, source_target_pairs={{0,7},{1,0},{2,1},{3,2},{4,3},{5,4},{6,5},{7,6},{8,15},{9,8},{10,9... | collective-permute-start | bytes 221192 | tf_op jit(solution)/shard_map/ppermute | solution.py:463
  8.0 0.3 pack_rest.1
  8.3 1.5 %collective-permute-start.2 = (bf16[36,1024]{1,0:T(8,128)(2,1)S(1)}, bf16[36,1024]{1,0:T(8,128)(2,1)S(1)}, u32[]{:S(2)}, u32[]{:S(2)}) collective-permute-start(bf16[36,1024]{1,0:T(8,128)(2,1)S(1)} %get-tuple-element.62), channel_id=1, source_target_pairs={{0,24},{1,9},{2,26},{3,11},{4,28},{5,13},{6,30},{7,15},{8,0},{9,17... | collective-permute-start | bytes 221192 | tf_op jit(solution)/shard_map/ppermute | solution.py:464
  9.8 1.6 %collective-permute-start.3 = (bf16[36,1024]{1,0:T(8,128)(2,1)S(1)}, bf16[36,1024]{1,0:T(8,128)(2,1)S(1)}, u32[]{:S(2)}, u32[]{:S(2)}) collective-permute-start(bf16[36,1024]{1,0:T(8,128)(2,1)S(1)} %get-tuple-element.63), channel_id=1, source_target_pairs={{0,15},{1,24},{2,9},{3,26},{4,11},{5,28},{6,13},{7,30},{8,23},{9,0... | collective-permute-start | bytes 221192 | tf_op jit(solution)/shard_map/ppermute | solution.py:465
  11.4 1.0 %own.1 = (f32[72,1024]{1,0:T(8,128)S(1)}, f32[72,1024]{1,0:T(8,128)S(1)}, f32[72,512]{1,0:T(8,128)S(1)}, f32[72,1536]{1,0:T(8,128)S(1)}, f32[72,512]{1,0:T(8,128)S(1)}) custom-call(bf16[288,512]{1,0:T(8,128)(2,1)S(1)} %bitcast.8, bf16[288,512]{1,0:T(8,128)(2,1)S(1)} %bitcast.12, bf16[72,288]{1,0:T(8,128)(2,1)S(1)} %get-tuple-element.49.pick_outer, ...), custom_call_target="tpu_custom_call" | custom-call | flops 500000000 | bytes 4097024 | tf_op jit(solution)/shard_map/own/pallas_call | solution.py:408
  12.4 2.1 %inner.1 = (f32[2,256,512]{2,1,0:T(8,128)S(1)}, bf16[144,512]{1,0:T(8,128)(2,1)S(1)}, bf16[144,512]{1,0:T(8,128)(2,1)S(1)}, bf16[2,256,144]{2,1,0:T(8,128)(2,1)S...) custom-call(f32[72,1024]{1,0:T(8,128)S(1)} %get-tuple-element.51.own, ...), custom_call_target="tpu_custom_call" | custom-call | flops 1000000000 | bytes 5505024 | tf_op jit(solution)/shard_map/inner/pallas_call | solution.py:408
  14.6 2.4 %outer.1 = (bf16[2,256,256]{2,1,0:T(8,128)(2,1)S(1)}, bf16[2,256,256]{2,1,0:T(8,128)(2,1)S(1)}, bf16[144,512]{1,0:T(8,128)(2,1)S(1)}, bf16[144,512]{1,0:T(8,128)...) custom-call(f32[72,1024]{1,0:T(8,128)S(1)} %get-tuple-element.58.own, ...), custom_call_target="tpu_custom_call" | custom-call | flops 1000000000 | bytes 5365760 | tf_op jit(solution)/shard_map/outer/pallas_call | solution.py:408
  17.0 0.1 collective-permute-start.4
  17.1 0.4 collective-permute-start.5
  17.5 0.4 keep.1
  18.0 0.6 %collective-permute-done.4.refs_1_ = bf16[2,256,256]{2,1,0:T(8,128)(2,1)S(1)} collective-permute-done((bf16[2,256,256]{2,1,0:T(8,128)(2,1)S(1)}, bf16[2,256,256]{2,1,0:T(8,128)(2,1)S(1)}, u32[]{:S(2)}, u32[]{:S(2)}) %collective-permute-start.4) | collective-permute-done | bytes 262176 | tf_op jit(solution)/shard_map/ppermute | solution.py:488
  18.6 0.1 chip_sum.2._
  18.6 1.9 %collective-permute-start.8 = (bf16[2,256,256]{2,1,0:T(8,128)(2,1)S(1)}, bf16[2,256,256]{2,1,0:T(8,128)(2,1)S(1)}, u32[]{:S(2)}, u32[]{:S(2)}) collective-permute-start(bf16[2,256,256]{2,1,0:T(8,128)(2,1)S(1)} %chip_sum.2._), channel_id=1, source_target_pairs={{0,8},{1,17},{2,10},{3,19},{4,12},{5,21},{6,14},{7,23},{8,0},{9,25... | collective-permute-start | bytes 786440 | tf_op jit(solution)/shard_map/ppermute | solution.py:497
  20.5 0.1 chip_sum.3.__
  20.6 0.3 collective-permute-start.9
  20.9 0.7 %rest.1 = (bf16[2,256,512]{2,1,0:T(8,128)(2,1)S(1)}, bf16[2,256,512]{2,1,0:T(8,128)(2,1)S(1)}) custom-call(bf16[2,256,256]{2,1,0:T(8,128)(2,1)S(1)} %chip_sum.2._, bf16[2,256,256]{2,1,0:T(8,128)(2,1)S(1)} %chip_sum.3.__, bf16[2,256,144]{2,1,0:T(8,128)(2,1)S(1)} %get-tuple-element.56.refs_0_, bf16[144,2048]{1,0:T(8,128)(2,1)S(1)} %get-tuple-element.57.refs_1_.refs_2_, ...), custom_call_target="tpu_custom_call" | custom-call | tf_op jit(solution)/shard_map/rest/pallas_call | solution.py:408
  21.6 0.1 collective-permute-start.7
  21.7 0.9 %outputs.1 = (bf16[144,1024]{1,0:T(8,128)(2,1)S(1)}, bf16[144,1024]{1,0:T(8,128)(2,1)S(1)}) custom-call(bf16[2,256,512]{2,1,0:T(8,128)(2,1)S(1)} %get-tuple-element.73._.refs_0_, bf16[144,512]{1,0:T(8,128)(2,1)S(1)} %get-tuple-element.74.refs_0_, bf16[144,512]{1,0:T(8,128)(2,1)S(1)} %get-tuple-element.75.refs_1_, ...), custom_call_target="tpu_custom_call" | custom-call | flops 10000000000 | bytes 4980736 | tf_op jit(solution)/shard_map/outputs/pallas_call | solution.py:408
  22.6 2.5 %collective-permute-done.8.refs_2_ = bf16[2,256,256]{2,1,0:T(8,128)(2,1)S(1)} collective-permute-done((bf16[2,256,256]{2,1,0:T(8,128)(2,1)S(1)}, bf16[2,256,256]{2,1,0:T(8,128)(2,1)S(1)}, u32[]{:S(2)}, u32[]{:S(2)}) %collective-permute-start.8) | collective-permute-done | bytes 262176 | tf_op jit(solution)/shard_map/ppermute | solution.py:497
  25.1 0.1 halve1.2
  25.2 1.6 %collective-permute-start.11 = (bf16[1,256,256]{2,1,0:T(8,128)(2,1)S(1)}, bf16[1,256,256]{2,1,0:T(8,128)(2,1)S(1)}, u32[]{:S(2)}, u32[]{:S(2)}) collective-permute-start(bf16[1,256,256]{2,1,0:T(8,128)(2,1)S(1)} %get-tuple-element.81._.refs_3_), channel_id=1, source_target_pairs={{0,16},{1,9},{2,18},{3,11},{4,20},{5,13},{6,22},{7,15},{8,24},{9,1... | collective-permute-start | bytes 393224 | tf_op jit(solution)/shard_map/ppermute | solution.py:497
  26.8 0.1 pack_lon.1
  27.0 1.5 %collective-permute-done.9.refs_2_ = bf16[2,256,256]{2,1,0:T(8,128)(2,1)S(1)} collective-permute-done((bf16[2,256,256]{2,1,0:T(8,128)(2,1)S(1)}, bf16[2,256,256]{2,1,0:T(8,128)(2,1)S(1)}, u32[]{:S(2)}, u32[]{:S(2)}) %collective-permute-start.9) | collective-permute-done | bytes 262176 | tf_op jit(solution)/shard_map/ppermute | solution.py:497
  28.5 0.1 halve1.3
  28.6 1.7 %collective-permute-start.12 = (bf16[1,256,256]{2,1,0:T(8,128)(2,1)S(1)}, bf16[1,256,256]{2,1,0:T(8,128)(2,1)S(1)}, u32[]{:S(2)}, u32[]{:S(2)}) collective-permute-start(bf16[1,256,256]{2,1,0:T(8,128)(2,1)S(1)} %get-tuple-element.82._), channel_id=1, source_target_pairs={{0,16},{1,9},{2,18},{3,11},{4,20},{5,13},{6,22},{7,15},{8,24},{9,1... | collective-permute-start | bytes 393224 | tf_op jit(solution)/shard_map/ppermute | solution.py:497
  30.3 0.1 pack_diag.1
  30.5 2.1 %collective-permute-done.6.lon_in._ = bf16[36,1024]{1,0:T(8,128)(2,1)S(1)} collective-permute-done((bf16[36,1024]{1,0:T(8,128)(2,1)S(1)}, bf16[36,1024]{1,0:T(8,128)(2,1)S(1)}, u32[]{:S(2)}, u32[]{:S(2)}) %collective-permute-start.6) | collective-permute-done | bytes 73760 | tf_op jit(solution)/shard_map/ppermute | solution.py:515
  32.7 1.0 %collective-permute-done.12.refs_2_ = bf16[1,256,256]{2,1,0:T(8,128)(2,1)S(1)} collective-permute-done((bf16[1,256,256]{2,1,0:T(8,128)(2,1)S(1)}, bf16[1,256,256]{2,1,0:T(8,128)(2,1)S(1)}, u32[]{:S(2)}, u32[]{:S(2)}) %collective-permute-start.12) | collective-permute-done | bytes 131104 | tf_op jit(solution)/shard_map/ppermute | solution.py:497
  33.7 4.0 %collective-permute-start.14 = (bf16[64,512]{1,0:T(8,128)(2,1)S(1)}, bf16[64,512]{1,0:T(8,128)(2,1)S(1)}, u32[]{:S(2)}, u32[]{:S(2)}) collective-permute-start(bf16[64,512]{1,0:T(8,128)(2,1)S(1)} %get-tuple-element.90), channel_id=1, source_target_pairs={{0,6},{1,7},{2,4},{3,5},{4,2},{5,3},{6,0},{7,1},{8,14},{9,15},{10,... | collective-permute-start | bytes 196616 | tf_op jit(solution)/shard_map/ppermute | solution.py:543
  37.7 0.6 %collective-permute-start.16 = (bf16[64,512]{1,0:T(8,128)(2,1)S(1)}, bf16[64,512]{1,0:T(8,128)(2,1)S(1)}, u32[]{:S(2)}, u32[]{:S(2)}) collective-permute-start(bf16[64,512]{1,0:T(8,128)(2,1)S(1)} %get-tuple-element.85._), channel_id=1, source_target_pairs={{0,2},{1,3},{2,0},{3,1},{4,6},{5,7},{6,4},{7,5},{8,10},{9,11},{10,... | collective-permute-start | bytes 196616 | tf_op jit(solution)/shard_map/ppermute | solution.py:543
  38.3 0.1 pack_lat.1
  38.5 1.7 %collective-permute-start.13 = (bf16[108,1024]{1,0:T(8,128)(2,1)S(1)}, bf16[108,1024]{1,0:T(8,128)(2,1)S(1)}, u32[]{:S(2)}, u32[]{:S(2)}) collective-permute-start(bf16[108,1024]{1,0:T(8,128)(2,1)S(1)} %pack_lat.1), channel_id=1, source_target_pairs={{24,0},{9,1},{26,2},{11,3},{28,4},{13,5},{30,6},{15,7},{0,8},{17,9... | collective-permute-start | bytes 663560 | tf_op jit(solution)/shard_map/ppermute | solution.py:549
  40.2 0.8 %place.1.placed._ = f32[288,1024]{1,0:T(8,128)S(1)} custom-call(bf16[144,1024]{1,0:T(8,128)(2,1)S(1)} %get-tuple-element.78._.refs_3_.inner_results, bf16[144,1024]{1,0:T(8,128)(2,1)S(1)} %get-tuple-element.79.outer_results, bf16[36,1024]{1,0:T(8,128)(2,1)S(1)} %collective-permute-done.6.lon_in._, bf16[36,1024]{1,0:T(8,128)(2,1)S(1)} %collective-permute-done.10.diag_in), custom_call_target="tpu_custom_call" | custom-call | bytes 1916928 | tf_op jit(solution)/shard_map/place/pallas_call | solution.py:408
  41.0 1.9 %collective-permute-done.15.refs_2_ = bf16[64,512]{1,0:T(8,128)(2,1)S(1)} collective-permute-done((bf16[64,512]{1,0:T(8,128)(2,1)S(1)}, bf16[64,512]{1,0:T(8,128)(2,1)S(1)}, u32[]{:S(2)}, u32[]{:S(2)}) %collective-permute-start.15) | collective-permute-done | bytes 65568 | tf_op jit(solution)/shard_map/ppermute | solution.py:543
  43.0 0.9 %collective-permute-start.19 = (bf16[64,512]{1,0:T(8,128)(2,1)S(1)}, bf16[64,512]{1,0:T(8,128)(2,1)S(1)}, u32[]{:S(2)}, u32[]{:S(2)}) collective-permute-start(bf16[64,512]{1,0:T(8,128)(2,1)S(1)} %line_sum.1.refs_0_), channel_id=1, source_target_pairs={{0,24},{8,16},{16,8},{24,0},{1,25},{9,17},{17,9},{25,1},{2,26},{10... | collective-permute-start | bytes 196616 | tf_op jit(solution)/shard_map/ppermute | solution.py:557
  43.8 1.0 %collective-permute-start.18 = (bf16[64,512]{1,0:T(8,128)(2,1)S(1)}, bf16[64,512]{1,0:T(8,128)(2,1)S(1)}, u32[]{:S(2)}, u32[]{:S(2)}) collective-permute-start(bf16[64,512]{1,0:T(8,128)(2,1)S(1)} %line_sum.1.refs_0_), channel_id=1, source_target_pairs={{0,16},{8,24},{16,0},{24,8},{1,17},{9,25},{17,1},{25,9},{2,18},{10... | collective-permute-start | bytes 196616 | tf_op jit(solution)/shard_map/ppermute | solution.py:557
  44.8 1.7 %collective-permute-start.17 = (bf16[64,512]{1,0:T(8,128)(2,1)S(1)}, bf16[64,512]{1,0:T(8,128)(2,1)S(1)}, u32[]{:S(2)}, u32[]{:S(2)}) collective-permute-start(bf16[64,512]{1,0:T(8,128)(2,1)S(1)} %line_sum.1.refs_0_), channel_id=1, source_target_pairs={{0,8},{8,0},{16,24},{24,16},{1,9},{9,1},{17,25},{25,17},{2,10},{10... | collective-permute-start | bytes 196616 | tf_op jit(solution)/shard_map/ppermute | solution.py:557
  46.5 1.0 %place_rest.1 = (bf16[288,512]{1,0:T(8,128)(2,1)}, bf16[288,512]{1,0:T(8,128)(2,1)}, f32[8,128]{1,0:T(8,128)S(1)}) custom-call(f32[288,1024]{1,0:T(8,128)S(1)} %place.1.placed._, bf16[108,1024]{1,0:T(8,128)(2,1)S(1)} %collective-permute-done.13.lat_in), custom_call_target="tpu_custom_call" | custom-call | bytes 1994752 | tf_op jit(solution)/shard_map/place_rest/pallas_call | solution.py:408
  47.6 0.7 %collective-permute-done.19.refs_3_ = bf16[64,512]{1,0:T(8,128)(2,1)S(1)} collective-permute-done((bf16[64,512]{1,0:T(8,128)(2,1)S(1)}, bf16[64,512]{1,0:T(8,128)(2,1)S(1)}, u32[]{:S(2)}, u32[]{:S(2)}) %collective-permute-start.19) | collective-permute-done | bytes 65568 | tf_op jit(solution)/shard_map/ppermute | solution.py:557
  48.3 0.5 %collective-permute-done.18.refs_2_ = bf16[64,512]{1,0:T(8,128)(2,1)S(1)} collective-permute-done((bf16[64,512]{1,0:T(8,128)(2,1)S(1)}, bf16[64,512]{1,0:T(8,128)(2,1)S(1)}, u32[]{:S(2)}, u32[]{:S(2)}) %collective-permute-start.18) | collective-permute-done | bytes 65568 | tf_op jit(solution)/shard_map/ppermute | solution.py:557
  48.8 0.3 collective-permute-done.17.refs_1_
  49.1 0.9 %finish.1 = (f32[64,1536]{1,0:T(8,128)}, f32[64,512]{1,0:T(8,128)}) custom-call(f32[8,128]{1,0:T(8,128)S(1)} %get-tuple-element.88._, bf16[64,512]{1,0:T(8,128)(2,1)S(1)} %line_sum.1.refs_0_, bf16[64,512]{1,0:T(8,128)(2,1)S(1)} %collective-permute-done.17.refs_1_, bf16[64,512]{1,0:T(8,128)(2,1)S(1)} %collective-permute-done.18.refs_2_, ...), custom_call_target="tpu_custom_call" | custom-call | bytes 790528 | tf_op jit(solution)/shard_map/finish/pallas_call | solution.py:408
  (23 shorter events, 0.3 us)
Async XLA Ops:
  0.6 1.0 %copy-start.2 = (bf16[2,6,24,512]{3,2,1,0:T(8,128)(2,1)S(1)}, bf16[2,6,24,512]{3,2,1,0:T(8,128)(2,1)}, u32[]{:S(2)}) copy-start(bf16[2,6,24,512]{3,2,1,0:T(8,128)(2,1)} %param.5) | copy-start | bytes 884740
  0.6 1.0 %copy-start.1 = (bf16[2,6,24,512]{3,2,1,0:T(8,128)(2,1)S(1)}, bf16[2,6,24,512]{3,2,1,0:T(8,128)(2,1)}, u32[]{:S(2)}) copy-start(bf16[2,6,24,512]{3,2,1,0:T(8,128)(2,1)} %param.4) | copy-start | bytes 884740
  1.9 9.5 %copy-start = (bf16[512,1536]{1,0:T(8,128)(2,1)S(1)}, bf16[512,1536]{1,0:T(8,128)(2,1)}, u32[]{:S(2)}) copy-start(bf16[512,1536]{1,0:T(8,128)(2,1)} %refs_6_.1) | copy-start | bytes 4718596
  2.0 9.5 %copy-start.3 = (bf16[512,512]{1,0:T(8,128)(2,1)S(1)}, bf16[512,512]{1,0:T(8,128)(2,1)}, u32[]{:S(2)}) copy-start(bf16[512,512]{1,0:T(8,128)(2,1)} %refs_7_.1) | copy-start | bytes 1572868
  2.0 10.5 %collective-permute-start = (bf16[72,1024]{1,0:T(8,128)(2,1)S(1)}, bf16[72,1024]{1,0:T(8,128)(2,1)S(1)}, u32[]{:S(2)}, u32[]{:S(2)}) collective-permute-start(bf16[72,1024]{1,0:T(8,128)(2,1)S(1)} %pack.1._), channel_id=1, source_target_pairs={{0,24},{1,9},{2,26},{3,11},{4,28},{5,13},{6,30},{7,15},{8,0},{9,17... | collective-permute-start | bytes 442376 | tf_op jit(solution)/shard_map/ppermute | solution.py:462
  6.1 8.5 %collective-permute-start.1 = (bf16[36,1024]{1,0:T(8,128)(2,1)S(1)}, bf16[36,1024]{1,0:T(8,128)(2,1)S(1)}, u32[]{:S(2)}, u32[]{:S(2)}) collective-permute-start(bf16[36,1024]{1,0:T(8,128)(2,1)S(1)} %pack_piece.1._), channel_id=1, source_target_pairs={{0,7},{1,0},{2,1},{3,2},{4,3},{5,4},{6,5},{7,6},{8,15},{9,8},{10,9... | collective-permute-start | bytes 221192 | tf_op jit(solution)/shard_map/ppermute | solution.py:463
  8.3 6.3 %collective-permute-start.2 = (bf16[36,1024]{1,0:T(8,128)(2,1)S(1)}, bf16[36,1024]{1,0:T(8,128)(2,1)S(1)}, u32[]{:S(2)}, u32[]{:S(2)}) collective-permute-start(bf16[36,1024]{1,0:T(8,128)(2,1)S(1)} %get-tuple-element.62), channel_id=1, source_target_pairs={{0,24},{1,9},{2,26},{3,11},{4,28},{5,13},{6,30},{7,15},{8,0},{9,17... | collective-permute-start | bytes 221192 | tf_op jit(solution)/shard_map/ppermute | solution.py:464
  9.8 4.8 %collective-permute-start.3 = (bf16[36,1024]{1,0:T(8,128)(2,1)S(1)}, bf16[36,1024]{1,0:T(8,128)(2,1)S(1)}, u32[]{:S(2)}, u32[]{:S(2)}) collective-permute-start(bf16[36,1024]{1,0:T(8,128)(2,1)S(1)} %get-tuple-element.63), channel_id=1, source_target_pairs={{0,15},{1,24},{2,9},{3,26},{4,11},{5,28},{6,13},{7,30},{8,23},{9,0... | collective-permute-start | bytes 221192 | tf_op jit(solution)/shard_map/ppermute | solution.py:465
  17.0 1.6 %collective-permute-start.4 = (bf16[2,256,256]{2,1,0:T(8,128)(2,1)S(1)}, bf16[2,256,256]{2,1,0:T(8,128)(2,1)S(1)}, u32[]{:S(2)}, u32[]{:S(2)}) collective-permute-start(bf16[2,256,256]{2,1,0:T(8,128)(2,1)S(1)} %get-tuple-element.68), channel_id=1, source_target_pairs={{0,1},{1,0},{2,3},{3,2},{4,5},{5,4},{6,7},{7,6},{8,9},{9,8},{10,11... | collective-permute-start | bytes 786440 | tf_op jit(solution)/shard_map/ppermute | solution.py:488
  17.1 3.4 %collective-permute-start.5 = (bf16[2,256,256]{2,1,0:T(8,128)(2,1)S(1)}, bf16[2,256,256]{2,1,0:T(8,128)(2,1)S(1)}, u32[]{:S(2)}, u32[]{:S(2)}) collective-permute-start(bf16[2,256,256]{2,1,0:T(8,128)(2,1)S(1)} %get-tuple-element.70), channel_id=1, source_target_pairs={{0,1},{1,0},{2,3},{3,2},{4,5},{5,4},{6,7},{7,6},{8,9},{9,8},{10,11... | collective-permute-start | bytes 786440 | tf_op jit(solution)/shard_map/ppermute | solution.py:488
  18.6 6.4 %collective-permute-start.8 = (bf16[2,256,256]{2,1,0:T(8,128)(2,1)S(1)}, bf16[2,256,256]{2,1,0:T(8,128)(2,1)S(1)}, u32[]{:S(2)}, u32[]{:S(2)}) collective-permute-start(bf16[2,256,256]{2,1,0:T(8,128)(2,1)S(1)} %chip_sum.2._), channel_id=1, source_target_pairs={{0,8},{1,17},{2,10},{3,19},{4,12},{5,21},{6,14},{7,23},{8,0},{9,25... | collective-permute-start | bytes 786440 | tf_op jit(solution)/shard_map/ppermute | solution.py:497
  20.6 7.9 %collective-permute-start.9 = (bf16[2,256,256]{2,1,0:T(8,128)(2,1)S(1)}, bf16[2,256,256]{2,1,0:T(8,128)(2,1)S(1)}, u32[]{:S(2)}, u32[]{:S(2)}) collective-permute-start(bf16[2,256,256]{2,1,0:T(8,128)(2,1)S(1)} %chip_sum.3.__), channel_id=1, source_target_pairs={{0,8},{1,17},{2,10},{3,19},{4,12},{5,21},{6,14},{7,23},{8,0},{9,25... | collective-permute-start | bytes 786440 | tf_op jit(solution)/shard_map/ppermute | solution.py:497
  21.6 3.5 %collective-permute-start.7 = (bf16[2,256,512]{2,1,0:T(8,128)(2,1)S(1)}, bf16[2,256,512]{2,1,0:T(8,128)(2,1)S(1)}, u32[]{:S(2)}, u32[]{:S(2)}) collective-permute-start(bf16[2,256,512]{2,1,0:T(8,128)(2,1)S(1)} %get-tuple-element.80), channel_id=1, source_target_pairs={{0,1},{1,0},{2,3},{3,2},{4,5},{5,4},{6,7},{7,6},{8,9},{9,8},{10,11... | collective-permute-start | bytes 1572872 | tf_op jit(solution)/shard_map/ppermute | solution.py:508
  25.2 7.5 %collective-permute-start.11 = (bf16[1,256,256]{2,1,0:T(8,128)(2,1)S(1)}, bf16[1,256,256]{2,1,0:T(8,128)(2,1)S(1)}, u32[]{:S(2)}, u32[]{:S(2)}) collective-permute-start(bf16[1,256,256]{2,1,0:T(8,128)(2,1)S(1)} %get-tuple-element.81._.refs_3_), channel_id=1, source_target_pairs={{0,16},{1,9},{2,18},{3,11},{4,20},{5,13},{6,22},{7,15},{8,24},{9,1... | collective-permute-start | bytes 393224 | tf_op jit(solution)/shard_map/ppermute | solution.py:497
  26.9 5.7 %collective-permute-start.6 = (bf16[36,1024]{1,0:T(8,128)(2,1)S(1)}, bf16[36,1024]{1,0:T(8,128)(2,1)S(1)}, u32[]{:S(2)}, u32[]{:S(2)}) collective-permute-start(bf16[36,1024]{1,0:T(8,128)(2,1)S(1)} %pack_lon.1), channel_id=1, source_target_pairs={{7,0},{0,1},{1,2},{2,3},{3,4},{4,5},{5,6},{6,7},{15,8},{8,9},{9,10... | collective-permute-start | bytes 221192 | tf_op jit(solution)/shard_map/ppermute | solution.py:515
  28.6 5.0 %collective-permute-start.12 = (bf16[1,256,256]{2,1,0:T(8,128)(2,1)S(1)}, bf16[1,256,256]{2,1,0:T(8,128)(2,1)S(1)}, u32[]{:S(2)}, u32[]{:S(2)}) collective-permute-start(bf16[1,256,256]{2,1,0:T(8,128)(2,1)S(1)} %get-tuple-element.82._), channel_id=1, source_target_pairs={{0,16},{1,9},{2,18},{3,11},{4,20},{5,13},{6,22},{7,15},{8,24},{9,1... | collective-permute-start | bytes 393224 | tf_op jit(solution)/shard_map/ppermute | solution.py:497
  30.4 9.8 %collective-permute-start.10 = (bf16[36,1024]{1,0:T(8,128)(2,1)S(1)}, bf16[36,1024]{1,0:T(8,128)(2,1)S(1)}, u32[]{:S(2)}, u32[]{:S(2)}) collective-permute-start(bf16[36,1024]{1,0:T(8,128)(2,1)S(1)} %pack_diag.1), channel_id=1, source_target_pairs={{15,0},{24,1},{9,2},{26,3},{11,4},{28,5},{13,6},{30,7},{23,8},{0,9... | collective-permute-start | bytes 221192 | tf_op jit(solution)/shard_map/ppermute | solution.py:531
  33.7 7.3 %collective-permute-start.14 = (bf16[64,512]{1,0:T(8,128)(2,1)S(1)}, bf16[64,512]{1,0:T(8,128)(2,1)S(1)}, u32[]{:S(2)}, u32[]{:S(2)}) collective-permute-start(bf16[64,512]{1,0:T(8,128)(2,1)S(1)} %get-tuple-element.90), channel_id=1, source_target_pairs={{0,6},{1,7},{2,4},{3,5},{4,2},{5,3},{6,0},{7,1},{8,14},{9,15},{10,... | collective-permute-start | bytes 196616 | tf_op jit(solution)/shard_map/ppermute | solution.py:543
  37.7 5.2 %collective-permute-start.15 = (bf16[64,512]{1,0:T(8,128)(2,1)S(1)}, bf16[64,512]{1,0:T(8,128)(2,1)S(1)}, u32[]{:S(2)}, u32[]{:S(2)}) collective-permute-start(bf16[64,512]{1,0:T(8,128)(2,1)S(1)} %get-tuple-element.91), channel_id=1, source_target_pairs={{0,4},{1,5},{2,6},{3,7},{4,0},{5,1},{6,2},{7,3},{8,12},{9,13},{10,... | collective-permute-start | bytes 196616 | tf_op jit(solution)/shard_map/ppermute | solution.py:543
  37.7 5.2 %collective-permute-start.16 = (bf16[64,512]{1,0:T(8,128)(2,1)S(1)}, bf16[64,512]{1,0:T(8,128)(2,1)S(1)}, u32[]{:S(2)}, u32[]{:S(2)}) collective-permute-start(bf16[64,512]{1,0:T(8,128)(2,1)S(1)} %get-tuple-element.85._), channel_id=1, source_target_pairs={{0,2},{1,3},{2,0},{3,1},{4,6},{5,7},{6,4},{7,5},{8,10},{9,11},{10,... | collective-permute-start | bytes 196616 | tf_op jit(solution)/shard_map/ppermute | solution.py:543
  38.5 8.0 %collective-permute-start.13 = (bf16[108,1024]{1,0:T(8,128)(2,1)S(1)}, bf16[108,1024]{1,0:T(8,128)(2,1)S(1)}, u32[]{:S(2)}, u32[]{:S(2)}) collective-permute-start(bf16[108,1024]{1,0:T(8,128)(2,1)S(1)} %pack_lat.1), channel_id=1, source_target_pairs={{24,0},{9,1},{26,2},{11,3},{28,4},{13,5},{30,6},{15,7},{0,8},{17,9... | collective-permute-start | bytes 663560 | tf_op jit(solution)/shard_map/ppermute | solution.py:549
  43.0 5.3 %collective-permute-start.19 = (bf16[64,512]{1,0:T(8,128)(2,1)S(1)}, bf16[64,512]{1,0:T(8,128)(2,1)S(1)}, u32[]{:S(2)}, u32[]{:S(2)}) collective-permute-start(bf16[64,512]{1,0:T(8,128)(2,1)S(1)} %line_sum.1.refs_0_), channel_id=1, source_target_pairs={{0,24},{8,16},{16,8},{24,0},{1,25},{9,17},{17,9},{25,1},{2,26},{10... | collective-permute-start | bytes 196616 | tf_op jit(solution)/shard_map/ppermute | solution.py:557
  43.8 5.0 %collective-permute-start.18 = (bf16[64,512]{1,0:T(8,128)(2,1)S(1)}, bf16[64,512]{1,0:T(8,128)(2,1)S(1)}, u32[]{:S(2)}, u32[]{:S(2)}) collective-permute-start(bf16[64,512]{1,0:T(8,128)(2,1)S(1)} %line_sum.1.refs_0_), channel_id=1, source_target_pairs={{0,16},{8,24},{16,0},{24,8},{1,17},{9,25},{17,1},{25,9},{2,18},{10... | collective-permute-start | bytes 196616 | tf_op jit(solution)/shard_map/ppermute | solution.py:557
  44.8 4.3 %collective-permute-start.17 = (bf16[64,512]{1,0:T(8,128)(2,1)S(1)}, bf16[64,512]{1,0:T(8,128)(2,1)S(1)}, u32[]{:S(2)}, u32[]{:S(2)}) collective-permute-start(bf16[64,512]{1,0:T(8,128)(2,1)S(1)} %line_sum.1.refs_0_), channel_id=1, source_target_pairs={{0,8},{8,0},{16,24},{24,16},{1,9},{9,1},{17,25},{25,17},{2,10},{10... | collective-permute-start | bytes 196616 | tf_op jit(solution)/shard_map/ppermute | solution.py:557
